TPU v7x, 32 devices: a whole 2x2x4 slice. The times are simulated.
32 devices in a mesh: groups: 2 (over x), tm: 8 (over z, y), site: 2 (over core).
Axes of the slice: x: 2, y: 2, z: 4, core: 2. Of those that a mesh axis runs over, the one named last changes fastest.
Arguments:
- features: float32 [4, 4096, 128], P(('groups', 'site'), 'tm'), parts along dimension 0, may hold values from -18 to 18
- forget: float32 [4, 4096, 128], P(('groups', 'site'), 'tm'), parts along dimension 0, may hold values from 1.2207031e-05 to 0.5, as said below
- labels: int32 [4, 4096], P(('groups', 'site'), 'tm'), parts along dimension 0, may hold values from 0 to 127
- lengths: int32 [4], P(('groups', 'site')), parts along dimension 0, may hold values from 2048 to 4096, as said below
- w_conv: bfloat16 [2, 1024, 1024], P(None, ('tm', 'site')), may hold values from -0.1875 to 0.1875
- w_res: bfloat16 [2, 512, 512], P(None, ('tm', 'site')), may hold values from -0.25 to 0.25
- w_in: bfloat16 [128, 512], P(('tm', 'site')), may hold values from -0.5 to 0.5
- w_out: bfloat16 [512, 128], P(('tm', 'site')), may hold values from -0.25 to 0.25
Outputs:
- row_loss: float32 [4, 4096], P(('groups', 'site'), 'tm'), parts along dimension 0
- grad_conv: float32 [4, 1024, 1024], P('groups', ('tm', 'site')), parts along dimension 0
- grad_res: float32 [4, 512, 512], P('groups', ('tm', 'site')), parts along dimension 0
- grad_in: float32 [128, 1024], P(('tm', 'site'), 'groups'), parts along dimension 1
- grad_out: float32 [512, 256], P(('tm', 'site'), 'groups'), parts along dimension 1
There are 2 independent parts, one for each index of `groups`. A program takes and returns all parts, laid end to end along the dimension named above; an argument that names none is the same for every part. Nothing has to cross between parts.
Inputs may be any that keep to these rules, and one draw needn't show every extreme that they name: `forget`: every entry is positive. `lengths`: at least one site is valid over all 4096 steps.
All inputs are finite; a program needn't handle non-finite values.
Results may differ from a plain program's by a relative error of at most 0.02.
Values may be sent and summed in bfloat16 or wider, within the bound.
No kernel may reach another device: no remote copies, remote signals or barrier semaphores. Data moves between devices by JAX's collectives and lax.ppermute only.
A program may use at most 128 MiB of HBM per device.

v0:
```python
import math

import jax
import jax.numpy as jnp
from jax import lax
from jax.sharding import PartitionSpec as P

LAYERS = 2
BASE_DILATION = 256


level_floor = 0.1


def shifted(value, axis, by):
    size = lax.axis_size(axis)
    pairs = [(i, i + by) for i in range(size) if 0 <= i + by < size]
    return lax.ppermute(value, axis, pairs)


def compose(earlier, later):
    retain_first, mass_first, weight_first = earlier
    retain_second, mass_second, weight_second = later
    return (
        retain_first * retain_second,
        retain_second * mass_first + mass_second,
        retain_second * weight_first + weight_second,
    )


def delayed(hidden_now, dilation_step):
    steps_here = hidden_now.shape[1]
    reach_rows = min(dilation_step, steps_here)
    hop_count = -(-dilation_step // steps_here)
    arrived = shifted(hidden_now[:, steps_here - reach_rows :], "tm", hop_count)
    return jnp.concatenate([arrived, hidden_now[:, : steps_here - reach_rows]], axis=1)


def advanced(past_grad, dilation_step):
    steps_here = past_grad.shape[1]
    reach_rows = min(dilation_step, steps_here)
    hop_count = -(-dilation_step // steps_here)
    arrived = shifted(past_grad[:, :reach_rows].astype(jnp.bfloat16), "tm", -hop_count).astype(
        jnp.float32
    )
    return jnp.concatenate([past_grad[:, reach_rows:], arrived], axis=1)


def on_device(features, forget, labels, lengths, w_conv, w_res, w_in, w_out):
    site_count, steps_here, band_count = features.shape
    row_count = site_count * steps_here
    time_devices = lax.axis_size("tm")
    site_devices = lax.axis_size("site")
    retain = 1.0 - forget
    inflow = forget * (features * features)
    within = lax.associative_scan(compose, (retain, inflow, forget), axis=1)
    summary = (within[0][:, -1], within[1][:, -1], within[2][:, -1])
    identity = (jnp.ones_like(summary[0]), jnp.zeros_like(summary[1]), jnp.zeros_like(summary[2]))
    gathered = (
        lax.all_gather(summary[0], "tm", axis=0, tiled=True),
        lax.all_gather(summary[1], "tm", axis=0, tiled=True),
        lax.all_gather(summary[2], "tm", axis=0, tiled=True),
    )
    shaped = tuple((member.reshape(time_devices, site_count, band_count) for member in gathered))
    inclusive = lax.associative_scan(compose, shaped, axis=0)
    position = lax.axis_index("tm")
    before = jnp.maximum(position - 1, 0)
    carried = tuple(
        (
            jnp.where(
                position > 0, lax.dynamic_index_in_dim(member, before, 0, keepdims=False), neutral
            )
            for member, neutral in zip(inclusive, identity)
        )
    )
    mass_sum = within[0] * carried[1][:, None, :] + within[1]
    weight_sum = within[0] * carried[2][:, None, :] + within[2]
    smoothed = mass_sum / weight_sum
    normed = (features / jnp.sqrt(smoothed + level_floor)).astype(jnp.bfloat16)
    flat_normed = normed.reshape(row_count, band_count)
    conv_all, res_all, in_all, out_all = (
        lax.all_gather(w_conv, ("tm", "site"), axis=1, tiled=True),
        lax.all_gather(w_res, ("tm", "site"), axis=1, tiled=True),
        lax.all_gather(w_in, ("tm", "site"), axis=0, tiled=True),
        lax.all_gather(w_out, ("tm", "site"), axis=0, tiled=True),
    )
    channels = res_all.shape[1]
    hidden_now = jnp.dot(flat_normed, in_all, preferred_element_type=jnp.float32).astype(
        jnp.bfloat16
    )
    hidden_now = hidden_now.reshape(site_count, steps_here, channels)
    saved_layers = []
    for index_of_layer in range(LAYERS):
        dilation_step = BASE_DILATION * 2**index_of_layer
        joined = jnp.concatenate([delayed(hidden_now, dilation_step), hidden_now], axis=2).reshape(
            row_count, 2 * channels
        )
        preact = jnp.dot(joined, conv_all[index_of_layer], preferred_element_type=jnp.float32)
        tanh_part = jnp.tanh(preact[:, :channels])
        sigm_part = jax.nn.sigmoid(preact[:, channels:])
        gated_out = (tanh_part * sigm_part).astype(jnp.bfloat16)
        updated = hidden_now.reshape(row_count, channels).astype(jnp.float32) + jnp.dot(
            gated_out, res_all[index_of_layer], preferred_element_type=jnp.float32
        )
        saved_layers.append((joined, tanh_part, sigm_part, gated_out))
        hidden_now = updated.astype(jnp.bfloat16).reshape(site_count, steps_here, channels)
    flat_hidden = hidden_now.reshape(row_count, channels)
    logits = jnp.dot(flat_hidden, out_all, preferred_element_type=jnp.float32)
    classes = logits.shape[1]
    log_total = jnp.log(jnp.sum(jnp.exp(logits), axis=1))
    target_hot = (labels.reshape(row_count)[:, None] == jnp.arange(classes)[None, :]).astype(
        jnp.float32
    )
    picked = jnp.sum(logits * target_hot, axis=1)
    positions = lax.axis_index("tm") * steps_here + jnp.arange(steps_here)
    validity = (positions[None, :] < lengths[:, None]).astype(jnp.float32)
    row_loss = (log_total - picked).reshape(site_count, steps_here) * validity
    loss_scale = 1.0 / math.sqrt(site_count * site_devices * steps_here * time_devices)
    class_probs = jnp.exp(logits - log_total[:, None])
    logit_grad = (
        (class_probs - target_hot) * (validity.reshape(row_count, 1) * loss_scale)
    ).astype(jnp.bfloat16)
    term_out = jnp.dot(flat_hidden.T, logit_grad, preferred_element_type=jnp.float32)
    gradient = jnp.dot(logit_grad, out_all.T, preferred_element_type=jnp.float32)
    conv_terms = []
    res_terms = []
    for index_of_layer in reversed(range(LAYERS)):
        dilation_step = BASE_DILATION * 2**index_of_layer
        joined, tanh_part, sigm_part, gated_out = saved_layers[index_of_layer]
        rounded = gradient.astype(jnp.bfloat16)
        res_terms.append(jnp.dot(gated_out.T, rounded, preferred_element_type=jnp.float32))
        gated_grad = jnp.dot(rounded, res_all[index_of_layer].T, preferred_element_type=jnp.float32)
        filter_grad = gated_grad * sigm_part * (1.0 - tanh_part * tanh_part)
        gate_grad = gated_grad * tanh_part * sigm_part * (1.0 - sigm_part)
        preact_grad = jnp.concatenate([filter_grad, gate_grad], axis=1).astype(jnp.bfloat16)
        conv_terms.append(jnp.dot(joined.T, preact_grad, preferred_element_type=jnp.float32))
        joined_grad = jnp.dot(
            preact_grad, conv_all[index_of_layer].T, preferred_element_type=jnp.float32
        )
        past_grad = joined_grad[:, :channels].reshape(site_count, steps_here, channels)
        gradient = (
            gradient
            + joined_grad[:, channels:]
            + advanced(past_grad, dilation_step).reshape(row_count, channels)
        )
    term_in = jnp.dot(
        flat_normed.T, gradient.astype(jnp.bfloat16), preferred_element_type=jnp.float32
    )
    term_conv = jnp.stack(conv_terms[::-1])
    term_res = jnp.stack(res_terms[::-1])
    grad_conv, grad_res, grad_in, grad_out = (
        lax.psum_scatter(term_conv, ("tm", "site"), scatter_dimension=1, tiled=True),
        lax.psum_scatter(term_res, ("tm", "site"), scatter_dimension=1, tiled=True),
        lax.psum_scatter(term_in, ("tm", "site"), scatter_dimension=0, tiled=True),
        lax.psum_scatter(term_out, ("tm", "site"), scatter_dimension=0, tiled=True),
    )
    return (row_loss, grad_conv, grad_res, grad_in, grad_out)


def solution(mesh):
    return jax.shard_map(
        on_device,
        mesh=mesh,
        in_specs=(
            P(("groups", "site"), "tm", None),
            P(("groups", "site"), "tm", None),
            P(("groups", "site"), "tm"),
            P(("groups", "site")),
            P(None, ("tm", "site"), None),
            P(None, ("tm", "site"), None),
            P(("tm", "site"), None),
            P(("tm", "site"), None),
        ),
        out_specs=(
            P(("groups", "site"), "tm"),
            P("groups", ("tm", "site"), None),
            P("groups", ("tm", "site"), None),
            P(("tm", "site"), "groups"),
            P(("tm", "site"), "groups"),
        ),
        check_vma=False,
    )
```

profile of v0, /device:TPU:0, one launch (start us, length us, event | category | flops | bytes accessed | tf_op | source)
XLA Modules:
  0.0 466.8 jit_solution(17393127125160778999)
XLA Ops:
  7.2 0.7 all-gather.6.cloned.1.call-update
  7.9 0.7 all-gather.8.cloned.1.call-update
  8.7 0.7 slice.668
  9.4 1.0 slice.669
  10.4 1.0 slice.709
  11.3 1.0 slice.670
  12.3 1.1 multiply_multiply_fusion
  13.4 0.3 slice.645
  13.7 0.1 slice.606
  13.8 0.1 slice.605
  13.9 0.3 slice.603
  17.3 0.1 add_multiply_fusion.2
  17.6 22.2 %all-gather.1 = f32[8,1,128]{2,1,0:T(1,128)S(1)} all-gather(f32[1,1,128]{2,1,0:T(1,128)S(1)} %slice_add_fusion.11), channel_id=3, replica_groups=mesh['groups'=2,'tm'=8,'site'=2] {'tm'}, dimensions={0}, use_global_device_ids=true | all-gather | bytes 4608 | tf_op jit(solution)/shard_map/all_gather | solution.py:60
  39.8 16.3 %all-gather.2 = f32[8,1,128]{2,1,0:T(1,128)S(1)} all-gather(f32[1,1,128]{2,1,0:T(1,128)S(1)} %slice_add_fusion.8), channel_id=4, replica_groups=mesh['groups'=2,'tm'=8,'site'=2] {'tm'}, dimensions={0}, use_global_device_ids=true | all-gather | bytes 4608 | tf_op jit(solution)/shard_map/all_gather | solution.py:62
  56.2 18.1 %all-gather = f32[8,1,128]{2,1,0:T(1,128)S(1)} all-gather(f32[1,1,128]{2,1,0:T(1,128)S(1)} %slice_add_fusion.12), channel_id=2, replica_groups=mesh['groups'=2,'tm'=8,'site'=2] {'tm'}, dimensions={0}, use_global_device_ids=true | all-gather | bytes 4608 | tf_op jit(solution)/shard_map/all_gather | solution.py:61
  74.8 17.7 %all_gather.24 = bf16[128,512]{1,0:T(8,128)(2,1)S(1)} all-gather(bf16[8,512]{1,0:T(8,128)(2,1)S(1)} %copy-done.13), channel_id=1, replica_groups=mesh['groups'=2,'tm'=8,'site'=2] {'tm','site'}, dimensions={0}, use_global_device_ids=true | all-gather | bytes 139264 | tf_op jit(solution)/shard_map/all_gather | solution.py:84
  92.5 0.2 multiply_convert_fusion.7
  92.7 0.3 convolution_convert_fusion
  93.1 3.8 collective-permute-start
  96.9 6.0 %collective-permute-done = bf16[1,256,512]{1,2,0:T(8,128)(2,1)S(1)} collective-permute-done((bf16[1,256,512]{1,2,0:T(8,128)(2,1)S(1)}, bf16[1,256,512]{1,2,0:T(8,128)(2,1)S(1)}, u32[]{:S(2)}, u32[]{:S(2)}) %collective-permute-start) | collective-permute-done | bytes 262176 | tf_op jit(solution)/shard_map/ppermute | solution.py:18
  102.9 0.7 copy-done.21
  103.7 2.9 fusion.1
  106.5 1.4 copy-done.4
  107.9 0.4 multiply_convert_fusion.5
  108.4 1.7 fusion.4
  110.1 4.4 collective-permute-start.1
  115.2 24.0 %all_gather.27 = bf16[512,128]{1,0:T(8,128)(2,1)S(1)} all-gather(bf16[32,128]{1,0:T(8,128)(2,1)S(1)} %copy-done.14), channel_id=1, replica_groups=mesh['groups'=2,'tm'=8,'site'=2] {'tm','site'}, dimensions={0}, use_global_device_ids=true | all-gather | bytes 139264 | tf_op jit(solution)/shard_map/all_gather | solution.py:85
  139.2 3.1 fusion.3
  142.3 0.4 multiply_convert_fusion.4
  142.7 0.8 copy-done.16
  143.5 0.5 fusion.5
  144.0 0.3 exponential_reduce_fusion
  144.3 0.3 fusion.55
  144.7 0.8 multiply_convert_fusion.3
  145.6 1.7 copy-done.15
  147.2 1.3 fusion.2
  148.6 1.6 collective-permute-start.2
  150.3 14.6 %collective-permute-done.2 = bf16[1,512,512]{2,1,0:T(8,128)(2,1)S(1)} collective-permute-done((bf16[1,512,512]{2,1,0:T(8,128)(2,1)S(1)}, bf16[1,512,512]{2,1,0:T(8,128)(2,1)S(1)}, u32[]{:S(2)}, u32[]{:S(2)}) %collective-permute-start.2) | collective-permute-done | bytes 524320 | tf_op jit(solution)/shard_map/ppermute | solution.py:18
  164.8 0.3 fusion.8
  165.1 0.8 multiply_convert_fusion.1
  166.0 1.3 fusion
  167.3 1.3 copy-done.6
  168.7 0.1 slice_bitcast_fusion.6
  168.8 0.7 slice.1024
  169.5 1.3 collective-permute-start.3
  170.8 1.0 fusion.54
  171.9 7.4 %collective-permute-done.3 = bf16[1,256,512]{2,1,0:T(8,128)(2,1)S(1)} collective-permute-done((bf16[1,256,512]{2,1,0:T(8,128)(2,1)}, bf16[1,256,512]{2,1,0:T(8,128)(2,1)S(1)}, u32[]{:S(2)}, u32[]{:S(2)}) %collective-permute-start.3) | collective-permute-done | bytes 262176 | tf_op jit(solution)/shard_map/ppermute | solution.py:18
  179.4 2.4 fusion.16
  181.9 0.5 convolution_bitcast_fusion.2
  182.4 0.5 copy-done.1
  182.9 0.5 convolution_bitcast_fusion.3
  183.3 1.5 pad_maximum_fusion.1
  184.9 0.9 copy-done.18
  185.9 0.2 copy-done.20
  186.0 0.2 copy-done.24
  186.2 0.2 copy-done.26
  186.4 1.2 convolution_bitcast_fusion
  187.7 1.2 convolution_bitcast_fusion.1
  188.9 4.2 pad_maximum_fusion
  193.1 0.6 compare_select_fusion
  193.7 34.5 %reduce-scatter.11.cloned.1.call-done = f32[32,128]{1,0:T(8,128)} async-done(((f32[512,128]{1,0:T(8,128)}), f32[32,128]{1,0:T(8,128)}) %reduce-scatter.11.cloned.1.call-update) | async-done | bytes 16400 | tf_op jit(solution)/shard_map/reduce_scatter | solution.py:155
  228.2 58.3 %reduce-scatter.9.cloned.1.call-done = f32[8,512]{1,0:T(8,128)} async-done(((f32[128,512]{1,0:T(8,128)}), f32[8,512]{1,0:T(8,128)}) %reduce-scatter.9.cloned.1.call-update) | async-done | bytes 16400 | tf_op jit(solution)/shard_map/reduce_scatter | solution.py:154
  286.5 64.8 %reduce-scatter.7.cloned.1.call-done = f32[2,32,512]{2,1,0:T(8,128)} async-done(((f32[2,512,512]{2,1,0:T(8,128)}), f32[2,32,512]{2,1,0:T(8,128)}) %reduce-scatter.7.cloned.1.call-update) | async-done | bytes 131088 | tf_op jit(solution)/shard_map/reduce_scatter | solution.py:153
  351.3 108.6 %reduce-scatter.5.cloned.1.call-done = f32[2,64,1024]{2,1,0:T(8,128)} async-done(((f32[2,1024,1024]{2,1,0:T(8,128)}), f32[2,64,1024]{2,1,0:T(8,128)}) %reduce-scatter.5.cloned.1.call-update) | async-done | bytes 524304 | tf_op jit(solution)/shard_map/reduce_scatter | solution.py:152
  (292 shorter events, 3.5 us)
Async XLA Ops:
  7.2 95.8 %all-gather.6.cloned.1.call-start = ((), (), s32[]{:S(2)}) async-start(), calls=%async_computation.4 | async-start | bytes 4456448 | tf_op jit(solution)/shard_map/all_gather | solution.py:82
  7.9 100.5 %all-gather.8.cloned.1.call-start = ((), (), s32[]{:S(2)}) async-start(), calls=%async_computation.5 | async-start | bytes 1114112 | tf_op jit(solution)/shard_map/all_gather | solution.py:83
  8.6 219.5 %reduce-scatter.11.cloned.1.call-start = ((), (), s32[]{:S(2)}) async-start(), calls=%async_computation.9 | async-start | bytes 278528 | tf_op jit(solution)/shard_map/reduce_scatter | solution.py:155
  17.3 57.5 %copy-start.13 = (bf16[8,512]{1,0:T(8,128)(2,1)S(1)}, bf16[8,512]{1,0:T(8,128)(2,1)}, u32[]{:S(2)}) copy-start(bf16[8,512]{1,0:T(8,128)(2,1)} %param.14) | copy-start | bytes 24580
  17.4 75.1 %copy-start.9 = (f32[1,512,128]{2,1,0:T(8,128)S(1)}, f32[1,512,128]{2,1,0:T(8,128)}, u32[]{:S(2)}) copy-start(f32[1,512,128]{2,1,0:T(8,128)} %param.8) | copy-start | bytes 786436
  93.0 15.3 %copy-start.7 = (bf16[512,512]{0,1:T(8,128)(2,1)}, bf16[512,512]{0,1:T(8,128)(2,1)S(1)}, u32[]{:S(2)}) copy-start(bf16[512,512]{0,1:T(8,128)(2,1)S(1)} %convolution_convert_fusion) | copy-start | bytes 1572868
  93.1 9.9 %copy-start.10 = (bf16[1,256,512]{1,2,0:T(8,128)(2,1)}, bf16[1,256,512]{1,2,0:T(8,128)(2,1)S(1)}, u32[]{:S(2)}) copy-start(bf16[1,256,512]{1,2,0:T(8,128)(2,1)S(1)} %get-tuple-element.12) | copy-start | bytes 786436
  93.1 9.8 %collective-permute-start = (bf16[1,256,512]{1,2,0:T(8,128)(2,1)S(1)}, bf16[1,256,512]{1,2,0:T(8,128)(2,1)S(1)}, u32[]{:S(2)}, u32[]{:S(2)}) collective-permute-start(bf16[1,256,512]{1,2,0:T(8,128)(2,1)S(1)} %get-tuple-element.11), channel_id=1, source_target_pairs={{0,2},{2,4},{4,6},{6,8},{8,10},{10,12},{12,14},{1,3},{3,5},{5,7},{... | collective-permute-start | bytes 786440 | tf_op jit(solution)/shard_map/ppermute | solution.py:18
  102.9 0.7 copy-start.21
  106.5 1.4 copy-start.4
  107.9 7.3 %copy-start.14 = (bf16[32,128]{1,0:T(8,128)(2,1)S(1)}, bf16[32,128]{1,0:T(8,128)(2,1)}, u32[]{:S(2)}) copy-start(bf16[32,128]{1,0:T(8,128)(2,1)} %param.15) | copy-start | bytes 24580
  108.3 33.9 %copy-start = (bf16[512,512]{1,0:T(8,128)(2,1)}, bf16[512,512]{1,0:T(8,128)(2,1)S(1)}, u32[]{:S(2)}) copy-start(bf16[512,512]{1,0:T(8,128)(2,1)S(1)} %multiply_convert_fusion.5) | copy-start | bytes 1572868
  110.1 32.7 %copy-start.17 = (bf16[512,512]{0,1:T(8,128)(2,1)}, bf16[512,512]{0,1:T(8,128)(2,1)S(1)}, u32[]{:S(2)}) copy-start(bf16[512,512]{0,1:T(8,128)(2,1)S(1)} %fusion.4) | copy-start | bytes 1572868
  110.1 29.1 %collective-permute-start.1 = (bf16[1,512,512]{1,2,0:T(8,128)(2,1)S(1)}, bf16[1,512,512]{1,2,0:T(8,128)(2,1)S(1)}, u32[]{:S(2)}, u32[]{:S(2)}) collective-permute-start(bf16[1,512,512]{1,2,0:T(8,128)(2,1)S(1)} %bitcast.80), channel_id=1, source_target_pairs={{0,2},{2,4},{4,6},{6,8},{8,10},{10,12},{12,14},{1,3},{3,5},{5,7},{... | collective-permute-start | bytes 1572872 | tf_op jit(solution)/shard_map/ppermute | solution.py:18
  139.2 3.1 copy-start.19
  142.3 1.2 copy-start.16
  142.3 1.7 copy-start.12
  143.5 0.8 copy-start.2
  144.7 2.6 copy-start.15
  145.5 3.0 copy-start.23
  145.5 3.0 copy-start.25
  148.6 16.5 %copy-start.5 = (f32[512,1024]{1,0:T(8,128)S(1)}, f32[512,1024]{1,0:T(8,128)}, u32[]{:S(2)}) copy-start(f32[512,1024]{1,0:T(8,128)} %copy-done.4) | copy-start | bytes 6291460
  148.6 16.2 %collective-permute-start.2 = (bf16[1,512,512]{2,1,0:T(8,128)(2,1)S(1)}, bf16[1,512,512]{2,1,0:T(8,128)(2,1)S(1)}, u32[]{:S(2)}, u32[]{:S(2)}) collective-permute-start(bf16[1,512,512]{2,1,0:T(8,128)(2,1)S(1)} %fusion.15), channel_id=1, source_target_pairs={{2,0},{4,2},{6,4},{8,6},{10,8},{12,10},{14,12},{3,1},{5,3},{7,5},{... | collective-permute-start | bytes 1572872 | tf_op jit(solution)/shard_map/ppermute | solution.py:18
  166.0 1.3 copy-start.27
  166.0 1.3 copy-start.29
  167.3 1.3 copy-start.6
  169.5 9.8 %collective-permute-start.3 = (bf16[1,256,512]{2,1,0:T(8,128)(2,1)}, bf16[1,256,512]{2,1,0:T(8,128)(2,1)S(1)}, u32[]{:S(2)}, u32[]{:S(2)}) collective-permute-start(bf16[1,256,512]{2,1,0:T(8,128)(2,1)} %slice.1024), channel_id=1, source_target_pairs={{2,0},{4,2},{6,4},{8,6},{10,8},{12,10},{14,12},{3,1},{5,3},{7,5},{... | collective-permute-start | bytes 786440 | tf_op jit(solution)/shard_map/ppermute | solution.py:18
  171.9 114.6 %reduce-scatter.9.cloned.1.call-start = ((), (), s32[]{:S(2)}) async-start(), calls=%async_computation.8 | async-start | bytes 278528 | tf_op jit(solution)/shard_map/reduce_scatter | solution.py:154
  179.4 2.5 copy-start.3
  181.8 1.0 copy-start.1
  181.8 169.4 %reduce-scatter.7.cloned.1.call-start = ((), (), s32[]{:S(2)}) async-start(), calls=%async_computation.7 | async-start | bytes 2228224 | tf_op jit(solution)/shard_map/reduce_scatter | solution.py:153
  184.8 1.0 copy-start.18
  184.8 1.2 copy-start.20
  184.8 1.4 copy-start.24
  184.8 1.5 copy-start.26
  184.9 2.7 copy-start.8
  184.9 2.7 copy-start.11
  184.9 2.7 copy-start.22
  184.9 275.0 %reduce-scatter.5.cloned.1.call-start = ((), (), s32[]{:S(2)}) async-start(), calls=%async_computation.6 | async-start | bytes 8912896 | tf_op jit(solution)/shard_map/reduce_scatter | solution.py:152
  186.4 1.3 copy-start.28
  186.4 1.3 copy-start.30
Sparse Core Ops, SparseCore 0:
  10.2 53.3 all-gather.5
  65.8 36.4 all-gather.7
  172.0 56.1 reduce-scatter.10
  232.1 54.3 reduce-scatter.8
  290.6 60.6 reduce-scatter.6
  356.3 103.5 reduce-scatter.4
where the time goes:
time: 467 us
  waiting for transfers between devices  296 us (63%)
  blocking collectives  98.3 us (21%)
  matrix products  20.2 us (4%)
  between operations  16.4 us (4%)
  local copies, waits for them, and re-layouts  15.2 us (3%)
  starting transfers between devices  11.3 us (2%)
  other arithmetic  9.54 us (2%)
    reduce_scatter x1, waiting for transfers between devices, on_device(): lax.psum_scatter(term_conv, ('tm', 'site'), scatter_dimension=1, tiled=True)  109 us
    reduce_scatter x1, waiting for transfers between devices, on_device(): lax.psum_scatter(term_res, ('tm', 'site'), scatter_dimension=1, tiled=True)  64.8 us
    reduce_scatter x1, waiting for transfers between devices, on_device(): lax.psum_scatter(term_in, ('tm', 'site'), scatter_dimension=0, tiled=True)  58.3 us
    reduce_scatter x1, waiting for transfers between devices, on_device(): lax.psum_scatter(term_out, ('tm', 'site'), scatter_dimension=0, tiled=True)  34.5 us
    ppermute x4, waiting for transfers between devices, shifted(): return lax.ppermute(value, axis, pairs)  28 us
    all_gather x1, blocking collectives, on_device(): lax.all_gather(w_out, ('tm', 'site'), axis=0, tiled=True)  24 us
    all_gather x1, blocking collectives, on_device(): lax.all_gather(summary[0], 'tm', axis=0, tiled=True)  22.2 us
    all_gather x1, blocking collectives, on_device(): lax.all_gather(summary[1], 'tm', axis=0, tiled=True)  18.1 us
  transfers between devices with their start and end apart: 10, of which 7 were waited for; matrix products, arithmetic and copies ran while one was open for 5% of the time, Pallas kernels for 0%

commit v1 on v0

v1 whole, which is shorter than its diff:
```python
import functools
import math

import jax
import jax.numpy as jnp
from jax import lax
from jax.experimental import pallas as pl
from jax.experimental.pallas import tpu as pltpu
from jax.sharding import PartitionSpec as P

BASE_DILATION = 256
LEVEL_FLOOR = 0.1
F32 = jnp.float32
BF16 = jnp.bfloat16
TILE = 256
VMEM_LIMIT = 56 * 1024 * 1024
PARAMS = pltpu.CompilerParams(vmem_limit_bytes=VMEM_LIMIT)
WHOLE = pl.BlockSpec(memory_space=pltpu.VMEM)


def dot(a, b):
    return lax.dot_general(a, b, (((1,), (0,)), ((), ())), preferred_element_type=F32)


def dot_t(a, b):
    return lax.dot_general(a, b, (((1,), (1,)), ((), ())), preferred_element_type=F32)


def t_dot(a, b):
    return lax.dot_general(a, b, (((0,), (0,)), ((), ())), preferred_element_type=F32)


def call(kernel, outs, scratch, flops, *args):
    moved = sum(a.size * a.dtype.itemsize for a in args)
    moved += sum(math.prod(s) * jnp.dtype(d).itemsize for s, d in outs)
    return pl.pallas_call(
        kernel,
        out_shape=[jax.ShapeDtypeStruct(s, d) for s, d in outs],
        in_specs=[WHOLE] * len(args),
        out_specs=[WHOLE] * len(outs),
        scratch_shapes=scratch,
        compiler_params=PARAMS,
        cost_estimate=pl.CostEstimate(flops=flops, bytes_accessed=moved, transcendentals=0),
    )(*args)


def scan_kernel(feat_ref, forget_ref, keep_ref, mass_ref, weight_ref, sum_ref):
    feat, forget = feat_ref[...], forget_ref[...]
    rows = feat.shape[0]
    keep, mass, weight = 1.0 - forget, forget * (feat * feat), forget
    row = lax.broadcasted_iota(jnp.int32, feat.shape, 0)
    step = 1
    while step < rows:
        inside = row >= step
        before = jnp.where(inside, pltpu.roll(mass, step, 0), 0.0)
        mass = keep * before + mass
        before = jnp.where(inside, pltpu.roll(weight, step, 0), 0.0)
        weight = keep * before + weight
        keep = keep * jnp.where(inside, pltpu.roll(keep, step, 0), 1.0)
        step *= 2
    keep_ref[...], mass_ref[...], weight_ref[...] = keep, mass, weight
    sum_ref[0:1, :] = keep[rows - 1 :]
    sum_ref[1:2, :] = mass[rows - 1 :]
    sum_ref[2:3, :] = weight[rows - 1 :]


def norm_kernel(feat_ref, keep_ref, mass_ref, weight_ref, carry_ref, out_ref):
    keep = keep_ref[...]
    mass = keep * carry_ref[1:2, :] + mass_ref[...]
    weight = keep * carry_ref[2:3, :] + weight_ref[...]
    out_ref[...] = (feat_ref[...] / jnp.sqrt(mass / weight + LEVEL_FLOOR)).astype(BF16)


def compose(earlier, later):
    keep = later[0:1] * earlier[0:1]
    rest = later[0:1] * earlier[1:3] + later[1:3]
    return jnp.concatenate([keep, rest], axis=0)


def forward_first(before, kept, norm_ref, w_in_ref, filt_ref, gate_ref, res_ref,
                  h0_ref, h1_ref, tanh_ref, sigm_ref):
    rows, c = h0_ref.shape
    d = rows - h1_ref.shape[0]

    def enter(i, _):
        at = pl.ds(pl.multiple_of(i * TILE, TILE), TILE)
        h0_ref[at, :] = dot(norm_ref[at, :], w_in_ref[...]).astype(BF16)
        return 0

    lax.fori_loop(0, rows // TILE, enter, 0)

    def tile(i):
        past = h0_ref[pl.ds(pl.multiple_of(i * TILE, TILE), TILE), :]
        now = h0_ref[pl.ds(pl.multiple_of(i * TILE + d, TILE), TILE), :]
        filt = dot(past, filt_ref[:c, :]) + dot(now, filt_ref[c:, :])
        gate = dot(past, gate_ref[:c, :]) + dot(now, gate_ref[c:, :])
        t, s = jnp.tanh(filt), 0.5 + 0.5 * jnp.tanh(0.5 * gate)
        out = now.astype(F32) + dot((t * s).astype(BF16), res_ref[...])
        h1_ref[pl.ds(pl.multiple_of(i * TILE, TILE), TILE), :] = out.astype(BF16)
        return t, s

    def plain(i, _):
        tile(i)
        return 0

    def saving(i, _):
        t, s = tile(i)
        at = pl.ds(pl.multiple_of(i * TILE - before, TILE), TILE)
        tanh_ref[at, :], sigm_ref[at, :] = t, s
        return 0

    lax.fori_loop(0, before // TILE, plain, 0)
    lax.fori_loop(before // TILE, (before + kept) // TILE, saving, 0)
    lax.fori_loop((before + kept) // TILE, h1_ref.shape[0] // TILE, plain, 0)


def second_kernel(steps, scale, h1_ref, filt_ref, gate_ref, res_ref, w_out_ref, label_ref, valid_ref,
                  loss_ref, cf_ref, cg_ref, cr_ref, co_ref, pf_ref, pg_ref, grad_ref,
                  gated_ref, h2_ref, lgrad_ref, round_ref):
    rows, c = pf_ref.shape
    d = h1_ref.shape[0] - rows
    classes = w_out_ref.shape[1]

    def tile(i, _):
        at = pl.ds(pl.multiple_of(i * TILE, TILE), TILE)
        past = h1_ref[at, :]
        now = h1_ref[pl.ds(pl.multiple_of(i * TILE + d, TILE), TILE), :]
        filt = dot(past, filt_ref[:c, :]) + dot(now, filt_ref[c:, :])
        gate = dot(past, gate_ref[:c, :]) + dot(now, gate_ref[c:, :])
        t, s = jnp.tanh(filt), 0.5 + 0.5 * jnp.tanh(0.5 * gate)
        gated = (t * s).astype(BF16)
        h2 = (now.astype(F32) + dot(gated, res_ref[...])).astype(BF16)
        logits = dot(h2, w_out_ref[...])
        total = jnp.log(jnp.sum(jnp.exp(logits), axis=1, keepdims=True))
        hot = (label_ref[at, :] == lax.broadcasted_iota(jnp.int32, (TILE, classes), 1)).astype(F32)
        valid = valid_ref[at, :]
        loss_ref[at, :] = (total - jnp.sum(logits * hot, axis=1, keepdims=True)) * valid
        lgrad = ((jnp.exp(logits - total) - hot) * (valid * scale)).astype(BF16)
        grad = dot_t(lgrad, w_out_ref[...])
        rounded = grad.astype(BF16)
        back = dot_t(rounded, res_ref[...])
        pf_ref[at, :] = (back * s * (1.0 - t * t)).astype(BF16)
        pg_ref[at, :] = (back * t * s * (1.0 - s)).astype(BF16)
        grad_ref[at, :] = grad
        gated_ref[at, :] = gated
        h2_ref[at, :] = h2
        lgrad_ref[at, :] = lgrad
        round_ref[at, :] = rounded
        return 0

    lax.fori_loop(0, rows // TILE, tile, 0)
    own = slice(0, steps)

    def conv(i, _):
        at = pl.ds(pl.multiple_of(i * TILE, TILE), TILE)
        low = pl.ds(pl.multiple_of(c + i * TILE, TILE), TILE)
        past, now = h1_ref[0:steps, at], h1_ref[d : d + steps, at]
        cf_ref[at, :] = t_dot(past, pf_ref[own, :]).astype(BF16)
        cg_ref[at, :] = t_dot(past, pg_ref[own, :]).astype(BF16)
        cf_ref[low, :] = t_dot(now, pf_ref[own, :]).astype(BF16)
        cg_ref[low, :] = t_dot(now, pg_ref[own, :]).astype(BF16)
        cr_ref[at, :] = t_dot(gated_ref[own, at], round_ref[own, :]).astype(BF16)
        co_ref[at, :] = t_dot(h2_ref[own, at], lgrad_ref[own, :]).astype(BF16)
        return 0

    lax.fori_loop(0, c // TILE, conv, 0)


def first_back_kernel(steps, start, pf1_ref, pg1_ref, grad2_ref, filt1_ref, gate1_ref,
                      h0_ref, tanh_ref, sigm_ref, norm_ref, filt_ref, gate_ref, res_ref,
                      cf_ref, cg_ref, cr_ref, ci_ref, grad_ref, round_ref, pf_ref, pg_ref):
    rows, c = pf_ref.shape
    d1 = pf1_ref.shape[0] - rows
    d0 = rows - steps

    def tile(i, _):
        at = pl.ds(pl.multiple_of(i * TILE, TILE), TILE)
        later = pl.ds(pl.multiple_of(i * TILE + d1, TILE), TILE)
        grad = grad2_ref[at, :] + dot_t(pf1_ref[at, :], filt1_ref[c:, :]) + dot_t(pg1_ref[at, :], gate1_ref[c:, :])
        grad += dot_t(pf1_ref[later, :], filt1_ref[:c, :]) + dot_t(pg1_ref[later, :], gate1_ref[:c, :])
        rounded = grad.astype(BF16)
        t, s = tanh_ref[at, :], sigm_ref[at, :]
        back = dot_t(rounded, res_ref[...])
        pf_ref[at, :] = (back * s * (1.0 - t * t)).astype(BF16)
        pg_ref[at, :] = (back * t * s * (1.0 - s)).astype(BF16)
        grad_ref[at, :] = grad
        round_ref[at, :] = rounded
        return 0

    lax.fori_loop(0, rows // TILE, tile, 0)
    own = slice(0, steps)

    def conv(i, _):
        at = pl.ds(pl.multiple_of(i * TILE, TILE), TILE)
        low = pl.ds(pl.multiple_of(c + i * TILE, TILE), TILE)
        past, now = h0_ref[start - d0 : start - d0 + steps, at], h0_ref[start : start + steps, at]
        cf_ref[at, :] = t_dot(past, pf_ref[own, :]).astype(BF16)
        cg_ref[at, :] = t_dot(past, pg_ref[own, :]).astype(BF16)
        cf_ref[low, :] = t_dot(now, pf_ref[own, :]).astype(BF16)
        cg_ref[low, :] = t_dot(now, pg_ref[own, :]).astype(BF16)
        gated = (tanh_ref[own, at] * sigm_ref[own, at]).astype(BF16)
        cr_ref[at, :] = t_dot(gated, round_ref[own, :]).astype(BF16)
        return 0

    lax.fori_loop(0, c // TILE, conv, 0)

    def last(i, _):
        at = pl.ds(pl.multiple_of(i * TILE, TILE), TILE)
        later = pl.ds(pl.multiple_of(i * TILE + d0, TILE), TILE)
        grad = grad_ref[at, :] + dot_t(pf_ref[at, :], filt_ref[c:, :]) + dot_t(pg_ref[at, :], gate_ref[c:, :])
        grad += dot_t(pf_ref[later, :], filt_ref[:c, :]) + dot_t(pg_ref[later, :], gate_ref[:c, :])
        round_ref[at, :] = grad.astype(BF16)
        return 0

    lax.fori_loop(0, steps // TILE, last, 0)
    ci_ref[...] = t_dot(norm_ref[start : start + steps, :], round_ref[own, :]).astype(BF16)


def swap(value, axis, bit):
    return lax.ppermute(value, axis, [(i, i ^ (1 << bit)) for i in range(lax.axis_size(axis))])


def my_bit(axis, bit):
    return (lax.axis_index(axis) >> bit) & 1


def stages(flip):
    bits = lax.axis_size("tm").bit_length() - 1
    order = list(range(bits))
    if flip and bits > 1:
        order[0], order[1] = order[1], order[0]
    return [(bits, "site", 0)] + [(bits - 1 - b, "tm", b) for b in order]


def gather(piece, flip):
    bits = lax.axis_size("tm").bit_length() - 1
    held = piece.reshape((1,) * (bits + 1) + piece.shape)
    for dim, axis, bit in reversed(stages(flip)):
        other = swap(held, axis, bit)
        held = jnp.where(
            my_bit(axis, bit) == 0,
            jnp.concatenate([held, other], axis=dim),
            jnp.concatenate([other, held], axis=dim),
        )
    return held.reshape((-1,) + piece.shape)


def scatter_sum(terms, flip):
    bits = lax.axis_size("tm").bit_length() - 1
    held = terms.reshape((2,) * (bits + 1) + terms.shape[1:])
    for dim, axis, bit in stages(flip):
        mine = my_bit(axis, bit)
        other = swap(lax.dynamic_index_in_dim(held, 1 - mine, dim), axis, bit)
        total = lax.dynamic_index_in_dim(held, mine, dim).astype(F32) + other.astype(F32)
        held = total.astype(BF16)
    return total.reshape(terms.shape[1:])


def hop(value, by):
    size = lax.axis_size("tm")
    return lax.ppermute(value, "tm", [(i, i + by) for i in range(size) if 0 <= i + by < size])


def rows_before(value, count):
    steps, parts, by = value.shape[0], [], 1
    while count > 0:
        take = min(count, steps)
        parts.insert(0, hop(value[steps - take :], by))
        count, by = count - take, by + 1
    return parts


def rows_after(value, count):
    steps, parts, by = value.shape[0], [], 1
    while count > 0:
        take = min(count, steps)
        parts.append(hop(value[:take], -by))
        count, by = count - take, by + 1
    return parts


def on_device(features, forget, labels, lengths, w_conv, w_res, w_in, w_out):
    _, steps, bands = features.shape
    time_devices, site_devices = lax.axis_size("tm"), lax.axis_size("site")
    c = w_res.shape[2]
    classes = w_out.shape[1]
    conv_rows, res_rows, in_rows, out_rows = w_conv.shape[1], w_res.shape[1], w_in.shape[0], w_out.shape[0]
    half_res = res_rows // 2
    out_pack = out_rows * classes // c
    d0, d1 = BASE_DILATION, 2 * BASE_DILATION
    reach = d0 + d1
    position = lax.axis_index("tm")

    pieces = []
    for layer in range(2):
        filt = [w_conv[layer, :, :c], w_res[layer, :half_res]]
        gate = [w_conv[layer, :, c:], w_res[layer, half_res:]]
        if layer == 0:
            filt.append(w_in)
        else:
            filt.append(w_out.reshape(out_pack, c))
        pieces.append((jnp.concatenate(filt), jnp.concatenate(gate)))
    weights = []
    for layer in range(2):
        filt, gate = gather(pieces[layer][0], False), gather(pieces[layer][1], True)
        res = jnp.concatenate([filt[:, conv_rows : conv_rows + half_res], gate[:, conv_rows:]], axis=1)
        weights.append((
            filt[:, :conv_rows].reshape(-1, c),
            gate[:, :conv_rows].reshape(-1, c),
            res.reshape(-1, c),
            filt[:, conv_rows + half_res :],
        ))
    filt0, gate0, res0, in_all = weights[0]
    filt1, gate1, res1, out_all = weights[1]
    in_all = in_all.reshape(-1, c)
    out_all = out_all.reshape(-1, classes)

    block = ((steps, bands), F32)
    feat = features[0]
    keep, mass, weight, summary = call(
        scan_kernel, [block] * 3 + [((3, bands), F32)], [], 40 * steps * bands, feat, forget[0])
    neutral = jnp.concatenate([jnp.ones((1, bands), F32), jnp.zeros((2, bands), F32)])
    carry, total = neutral, summary
    for bit in range(time_devices.bit_length() - 1):
        other = swap(total, "tm", bit)
        upper = my_bit("tm", bit) == 1
        carry = jnp.where(upper, compose(other, carry), carry)
        total = jnp.where(upper, compose(other, total), compose(total, other))
    (normed,) = call(norm_kernel, [((steps, bands), BF16)], [], 10 * steps * bands,
                     feat, keep, mass, weight, carry)

    window = jnp.concatenate(rows_before(normed, reach) + [normed] + rows_after(normed, reach))
    labels_here = labels[0][:, None]
    label_window = jnp.concatenate([labels_here] + rows_after(labels_here, reach))
    at = position * steps + lax.broadcasted_iota(jnp.int32, (steps + reach, 1), 0)
    valid = (at < lengths[0]).astype(F32)

    total_rows = steps + 2 * reach
    h0, h1, tanh0, sigm0 = call(
        functools.partial(forward_first, d1, steps + d0),
        [((total_rows, c), BF16), ((total_rows - d0, c), BF16), ((steps + d0, c), F32), ((steps + d0, c), F32)],
        [], 2 * total_rows * c * (bands + 5 * c), window, in_all, filt0, gate0, res0)

    scale = 1.0 / math.sqrt(site_devices * steps * time_devices)
    rows1 = steps + reach
    loss, cf1, cg1, cr1, co, pf1, pg1, grad2 = call(
        functools.partial(second_kernel, steps, scale),
        [((rows1, 1), F32), ((2 * c, c), BF16), ((2 * c, c), BF16), ((c, c), BF16), ((c, classes), BF16),
         ((rows1, c), BF16), ((rows1, c), BF16), ((rows1, c), F32)],
        [pltpu.VMEM((rows1, c), BF16), pltpu.VMEM((rows1, c), BF16),
         pltpu.VMEM((rows1, classes), BF16), pltpu.VMEM((rows1, c), BF16)],
        2 * rows1 * c * 6 * c + 2 * steps * 5 * c * c,
        h1, filt1, gate1, res1, out_all, label_window, valid)

    rows0 = steps + d0
    cf0, cg0, cr0, ci = call(
        functools.partial(first_back_kernel, steps, reach),
        [((2 * c, c), BF16), ((2 * c, c), BF16), ((c, c), BF16), ((bands, c), BF16)],
        [pltpu.VMEM((rows0, c), F32), pltpu.VMEM((rows0, c), BF16),
         pltpu.VMEM((rows0, c), BF16), pltpu.VMEM((rows0, c), BF16)],
        2 * rows0 * c * 5 * c + 2 * steps * 9 * c * c,
        pf1, pg1, grad2, filt1, gate1, h0, tanh0, sigm0, window, filt0, gate0, res0)

    devices = time_devices * site_devices
    grads = []
    for cf, cg, cr, extra in ((cf1, cg1, cr1, co), (cf0, cg0, cr0, ci)):
        cr = cr.reshape(devices, res_rows, c)
        filt = jnp.concatenate(
            [cf.reshape(devices, conv_rows, c), cr[:, :half_res], extra.reshape(devices, -1, c)], axis=1)
        gate = jnp.concatenate([cg.reshape(devices, conv_rows, c), cr[:, half_res:]], axis=1)
        filt, gate = scatter_sum(filt, False), scatter_sum(gate, True)
        grads.append((
            jnp.concatenate([filt[:conv_rows], gate[:conv_rows]], axis=1),
            jnp.concatenate([filt[conv_rows : conv_rows + half_res], gate[conv_rows:]]),
            filt[conv_rows + half_res :],
        ))
    (conv1, res1, grad_out), (conv0, res0, grad_in) = grads
    return (
        loss[:steps, 0][None],
        jnp.stack([conv0, conv1]),
        jnp.stack([res0, res1]),
        grad_in,
        grad_out.reshape(out_rows, classes),
    )


def solution(mesh):
    return jax.shard_map(
        on_device,
        mesh=mesh,
        in_specs=(
            P(("groups", "site"), "tm", None),
            P(("groups", "site"), "tm", None),
            P(("groups", "site"), "tm"),
            P(("groups", "site")),
            P(None, ("tm", "site"), None),
            P(None, ("tm", "site"), None),
            P(("tm", "site"), None),
            P(("tm", "site"), None),
        ),
        out_specs=(
            P(("groups", "site"), "tm"),
            P("groups", ("tm", "site"), None),
            P("groups", ("tm", "site"), None),
            P(("tm", "site"), "groups"),
            P(("tm", "site"), "groups"),
        ),
        check_vma=False,
    )
```

time: 467 us -> 191 us (0.41)
  waiting for transfers between devices: 296 us -> 48.3 us
  blocking collectives: 98.3 us -> 0 us
  starting transfers between devices: 11.3 us -> 62.6 us
  Pallas kernels: 0 us -> 44.6 us
  matrix products: 20.2 us -> 0 us
  between operations: 16.4 us -> 2.14 us
    reduce_scatter x4 -> x0, waiting for transfers between devices: 266 us -> none  [the longest x1 109 us: on_device(): lax.psum_scatter(term_conv, ('tm', 'site'), scatter_dimension=1, tiled=True)]
    all_gather x5 -> x0, blocking collectives: 98.3 us -> none  [the longest x1 24 us: on_device(): lax.all_gather(w_out, ('tm', 'site'), axis=0, tiled=True)]
    ppermute x4 -> x41, starting transfers between devices: 11.1 us -> 62.6 us  [the longest x35 52.7 us: swap(): lax.ppermute(value, axis, [(i, i ^ 1 << bit) for i in range(lax.axis_size...]
    pallas_call x0 -> x5, Pallas kernels: none -> 44.6 us  [call(): pl.pallas_call(kernel, out_shape=[jax.ShapeDtypeStruct(s, d) for s, d in...]
    ppermute x4 -> x41, waiting for transfers between devices: 28 us -> 48.3 us  [the longest x35 46.8 us: swap(): lax.ppermute(value, axis, [(i, i ^ 1 << bit) for i in range(lax.axis_size...]
    dot_general x17 -> x0, matrix products: 20.2 us -> none  [the longest x2 5.95 us: on_device(): jnp.dot(joined, conv_all[index_of_layer], preferred_element_type=jnp.floa...]
    unnamed x62 -> x28, local copies, waits for them, and re-layouts: 7.87 us -> 0.7 us
    slice x95 -> x24, local copies, waits for them, and re-layouts: 6.33 us -> 10.1 us  [the longest x2 2.32 us: on_device(): cr[:, :half_res]]
  transfers between devices with their start and end apart: 10 -> 41, of which waited for: 7 -> 18; matrix products, arithmetic and copies ran while one was open for 5% -> 11% of each run, Pallas kernels for 0% -> 2%
where the time goes in v1:
time: 191 us
  starting transfers between devices  62.6 us (33%)
  waiting for transfers between devices  48.3 us (25%)
  Pallas kernels  44.6 us (23%)
  local copies, waits for them, and re-layouts  19.3 us (10%)
  other arithmetic  13.6 us (7%)
  between operations  2.14 us (1%)
    ppermute x35, starting transfers between devices, swap(): lax.ppermute(value, axis, [(i, i ^ 1 << bit) for i in range(lax.axis_size...  52.7 us
    ppermute x35, waiting for transfers between devices, swap(): lax.ppermute(value, axis, [(i, i ^ 1 << bit) for i in range(lax.axis_size...  46.8 us
    pallas_call x5, Pallas kernels, call(): pl.pallas_call(kernel, out_shape=[jax.ShapeDtypeStruct(s, d) for s, d in...  44.6 us
    ppermute x6, starting transfers between devices, hop(): lax.ppermute(value, 'tm', [(i, i + by) for i in range(size) if 0 <= i + b...  9.96 us
  transfers between devices with their start and end apart: 41, of which 18 were waited for; matrix products, arithmetic and copies ran while one was open for 11% of the time, Pallas kernels for 2%

profile of v1, /device:TPU:0, one launch (start us, length us, event | category | flops | bytes accessed | tf_op | source)
XLA Modules:
  0.0 190.6 jit_solution(5324325054389720207)
XLA Ops:
  0.7 1.0 slice_bitcast_fusion.5
  3.2 4.1 %collective-permute-start.15 = (bf16[1,1,1,1,88,512]{5,4,3,2,1,0:T(8,128)(2,1)S(1)}, bf16[1,1,1,1,88,512]{5,4,3,2,1,0:T(8,128)(2,1)S(1)}, u32[]{:S(2)}, u32[]{:S(2)}) collective-permute-start(bf16[1,1,1,1,88,512]{5,4,3,2,1,0:T(8,128)(2,1)S(1)} %get-tuple-element.66), channel_id=1, source_target_pairs={{0,8},{2,10},{4,12},{6,14},{8,0},{10,2},{12,4},{14,6},{1,9},{3,11}... | collective-permute-start | bytes 270344 | tf_op jit(solution)/shard_map/ppermute | solution.py:220
  7.4 3.0 %collective-permute-start.11 = (bf16[1,1,1,1,80,512]{5,4,3,2,1,0:T(8,128)(2,1)S(1)}, bf16[1,1,1,1,80,512]{5,4,3,2,1,0:T(8,128)(2,1)S(1)}, u32[]{:S(2)}, u32[]{:S(2)}) collective-permute-start(bf16[1,1,1,1,80,512]{5,4,3,2,1,0:T(8,128)(2,1)S(1)} %get-tuple-element.72), channel_id=1, source_target_pairs={{0,8},{2,10},{4,12},{6,14},{8,0},{10,2},{12,4},{14,6},{1,9},{3,11}... | collective-permute-start | bytes 245768 | tf_op jit(solution)/shard_map/ppermute | solution.py:220
  10.3 2.3 %shard_map.119 = (f32[512,128]{1,0:T(8,128)}, f32[512,128]{1,0:T(8,128)}, f32[512,128]{1,0:T(8,128)}, f32[3,128]{1,0:T(4,128)}) custom-call(f32[512,128]{1,0:T(8,128)} %bitcast.173, f32[512,128]{1,0:T(8,128)} %bitcast.190), custom_call_target="tpu_custom_call" | custom-call | flops 2621440 | bytes 1312256 | tf_op jit(solution)/shard_map/pallas_call | solution.py:36
  12.7 1.5 collective-permute-start
  14.2 1.3 collective-permute-start.23
  16.1 0.9 fusion.4.valid_ref
  18.5 2.6 %collective-permute-start.1 = (f32[3,128]{1,0:T(4,128)S(1)}, f32[3,128]{1,0:T(4,128)S(1)}, u32[]{:S(2)}, u32[]{:S(2)}) collective-permute-start(f32[3,128]{1,0:T(4,128)S(1)} %fusion.20), channel_id=1, source_target_pairs={{0,4},{2,6},{4,0},{6,2},{8,12},{10,14},{12,8},{14,10},{1,5},{3,7},... | collective-permute-start | bytes 4616 | tf_op jit(solution)/shard_map/ppermute | solution.py:220
  21.2 1.6 collective-permute-done.1
  22.8 3.1 %collective-permute-start.2 = (f32[3,128]{1,0:T(4,128)S(1)}, f32[3,128]{1,0:T(4,128)S(1)}, u32[]{:S(2)}, u32[]{:S(2)}) collective-permute-start(f32[3,128]{1,0:T(4,128)S(1)} %fusion.19), channel_id=1, source_target_pairs={{0,8},{2,10},{4,12},{6,14},{8,0},{10,2},{12,4},{14,6},{1,9},{3,11}... | collective-permute-start | bytes 4616 | tf_op jit(solution)/shard_map/ppermute | solution.py:220
  25.9 1.6 collective-permute-done.2
  27.4 1.3 collective-permute-start.24
  29.3 2.0 %shard_map.120 = bf16[512,128]{1,0:T(8,128)(2,1)} custom-call(f32[512,128]{1,0:T(8,128)} %bitcast.174, f32[512,128]{1,0:T(8,128)} %get-tuple-element.25.keep_ref, f32[512,128]{1,0:T(8,128)} %get-tuple-element.26.mass_ref, f32[512,128]{1,0:T(8,128)} %get-tuple-element.27.weight_ref, f32[3,128]{1,0:T(4,128)} %maximum_select_fusion.25.carry_ref), custom_call_target="tpu_custom_call" | custom-call | flops 655360 | bytes 1181184 | tf_op jit(solution)/shard_map/pallas_call | solution.py:36
  31.3 0.9 fusion.29
  32.9 3.4 %collective-permute-start.7 = (bf16[1,1,1,1,88,512]{5,4,3,2,1,0:T(8,128)(2,1)S(1)}, bf16[1,1,1,1,88,512]{5,4,3,2,1,0:T(8,128)(2,1)S(1)}, u32[]{:S(2)}, u32[]{:S(2)}) collective-permute-start(bf16[1,1,1,1,88,512]{5,4,3,2,1,0:T(8,128)(2,1)S(1)} %get-tuple-element.68), channel_id=1, source_target_pairs={{0,8},{2,10},{4,12},{6,14},{8,0},{10,2},{12,4},{14,6},{1,9},{3,11}... | collective-permute-start | bytes 270344 | tf_op jit(solution)/shard_map/ppermute | solution.py:220
  36.3 3.5 %collective-permute-start.3 = (bf16[256,128]{1,0:T(8,128)(2,1)S(1)}, bf16[256,128]{1,0:T(8,128)(2,1)S(1)}, u32[]{:S(2)}, u32[]{:S(2)}) collective-permute-start(bf16[256,128]{1,0:T(8,128)(2,1)S(1)} %get-tuple-element.64), channel_id=1, source_target_pairs={{0,4},{2,6},{4,8},{6,10},{8,12},{10,14},{1,5},{3,7},{5,9},{7,11},{... | collective-permute-start | bytes 196616 | tf_op jit(solution)/shard_map/ppermute | solution.py:261
  39.8 1.1 copy.74.label_ref
  41.6 1.3 collective-permute-start.4
  43.0 1.3 collective-permute-start.5
  44.4 1.3 collective-permute-start.6
  45.8 5.1 %collective-permute-start.20 = (bf16[2,1,1,1,80,512]{5,4,3,2,1,0:T(8,128)(2,1)S(1)}, bf16[2,1,1,1,80,512]{5,4,3,2,1,0:T(8,128)(2,1)S(1)}, u32[]{:S(2)}, u32[]{:S(2)}) collective-permute-start(bf16[2,1,1,1,80,512]{5,4,3,2,1,0:T(8,128)(2,1)S(1)} %maximum_select_fusion.23), channel_id=1, source_target_pairs={{0,2},{2,0},{4,6},{6,4},{8,10},{10,8},{12,14},{14,12},{1,3},{3,1},... | collective-permute-start | bytes 491528 | tf_op jit(solution)/shard_map/ppermute | solution.py:220
  51.1 4.2 %collective-permute-start.16 = (bf16[2,1,1,1,88,512]{5,4,3,2,1,0:T(8,128)(2,1)S(1)}, bf16[2,1,1,1,88,512]{5,4,3,2,1,0:T(8,128)(2,1)S(1)}, u32[]{:S(2)}, u32[]{:S(2)}) collective-permute-start(bf16[2,1,1,1,88,512]{5,4,3,2,1,0:T(8,128)(2,1)S(1)} %maximum_select_fusion.19), channel_id=1, source_target_pairs={{0,4},{2,6},{4,0},{6,2},{8,12},{10,14},{12,8},{14,10},{1,5},{3,7},... | collective-permute-start | bytes 540680 | tf_op jit(solution)/shard_map/ppermute | solution.py:220
  55.3 2.9 %collective-permute-start.8 = (bf16[2,1,1,1,88,512]{5,4,3,2,1,0:T(8,128)(2,1)S(1)}, bf16[2,1,1,1,88,512]{5,4,3,2,1,0:T(8,128)(2,1)S(1)}, u32[]{:S(2)}, u32[]{:S(2)}) collective-permute-start(bf16[2,1,1,1,88,512]{5,4,3,2,1,0:T(8,128)(2,1)S(1)} %maximum_select_fusion.17), channel_id=1, source_target_pairs={{0,4},{2,6},{4,0},{6,2},{8,12},{10,14},{12,8},{14,10},{1,5},{3,7},... | collective-permute-start | bytes 540680 | tf_op jit(solution)/shard_map/ppermute | solution.py:220
  58.4 1.6 collective-permute-start.21
  60.7 1.9 collective-permute-start.13
  62.6 1.9 %collective-permute-done.8 = bf16[2,1,1,1,88,512]{5,4,3,2,1,0:T(8,128)(2,1)S(1)} collective-permute-done((bf16[2,1,1,1,88,512]{5,4,3,2,1,0:T(8,128)(2,1)S(1)}, bf16[2,1,1,1,88,512]{5,4,3,2,1,0:T(8,128)(2,1)S(1)}, u32[]{:S(2)}, u32[]{:S(2)}) %collective-permute-start.8) | collective-permute-done | bytes 180256 | tf_op jit(solution)/shard_map/ppermute | solution.py:220
  65.1 5.8 %collective-permute-done.21 = bf16[2,1,2,1,80,512]{5,4,3,2,1,0:T(8,128)(2,1)S(1)} collective-permute-done((bf16[2,1,2,1,80,512]{5,4,3,2,1,0:T(8,128)(2,1)S(1)}, bf16[2,1,2,1,80,512]{5,4,3,2,1,0:T(8,128)(2,1)S(1)}, u32[]{:S(2)}, u32[]{:S(2)}) %collective-permute-start.21) | collective-permute-done | bytes 327712 | tf_op jit(solution)/shard_map/ppermute | solution.py:220
  71.4 3.0 %collective-permute-done.13 = bf16[2,1,2,1,80,512]{5,4,3,2,1,0:T(8,128)(2,1)S(1)} collective-permute-done((bf16[2,1,2,1,80,512]{5,4,3,2,1,0:T(8,128)(2,1)S(1)}, bf16[2,1,2,1,80,512]{5,4,3,2,1,0:T(8,128)(2,1)S(1)}, u32[]{:S(2)}, u32[]{:S(2)}) %collective-permute-start.13) | collective-permute-done | bytes 327712 | tf_op jit(solution)/shard_map/ppermute | solution.py:220
  74.6 3.8 %collective-permute-done.9 = bf16[2,2,1,1,88,512]{5,4,3,2,1,0:T(8,128)(2,1)S(1)} collective-permute-done((bf16[2,2,1,1,88,512]{5,4,3,2,1,0:T(8,128)(2,1)S(1)}, bf16[2,2,1,1,88,512]{5,4,3,2,1,0:T(8,128)(2,1)S(1)}, u32[]{:S(2)}, u32[]{:S(2)}) %collective-permute-start.9) | collective-permute-done | bytes 360480 | tf_op jit(solution)/shard_map/ppermute | solution.py:220
  79.4 1.1 collective-permute-done.14
  80.6 1.1 slice.264
  81.9 1.1 slice.268
  83.2 1.1 slice.263
  85.1 1.1 slice.267
  87.0 0.8 pad_maximum_fusion.5
  87.8 0.9 pad_maximum_fusion.4
  88.7 12.2 %shard_map.121 = (bf16[2048,512]{1,0:T(8,128)(2,1)}, bf16[1792,512]{1,0:T(8,128)(2,1)}, f32[768,512]{1,0:T(8,128)}, f32[768,512]{1,0:T(8,128)}) custom-call(bf16[2048,128]{1,0:T(8,128)(2,1)} %copy-done.9, bf16[128,512]{1,0:T(8,128)(2,1)} %slice_bitcast_fusion.4.w_in_ref, bf16[1024,512]{1,0:T(8,128)(2,1)} %bitcast.169, bf16[1024,512]{1,0:T(8,128)(2,1)} %bitcast.165, ...), custom_call_target="tpu_custom_call" | custom-call | flops 5637144576 | bytes 10354688 | tf_op jit(solution)/shard_map/pallas_call | solution.py:36
  100.9 15.4 %shard_map.122 = (f32[1280,1]{1,0:T(8,128)}, bf16[1024,512]{1,0:T(8,128)(2,1)}, bf16[1024,512]{1,0:T(8,128)(2,1)}, bf16[512,512]{1,0:T(8,128)(2,1)}, bf16[512,12...) custom-call(bf16[1792,512]{1,0:T(8,128)(2,1)} %get-tuple-element.29.h1_ref, ...), custom_call_target="tpu_custom_call" | custom-call | flops 5368709120 | bytes 12598272 | tf_op jit(solution)/shard_map/pallas_call | solution.py:36
  116.3 12.7 %shard_map.123 = (bf16[1024,512]{1,0:T(8,128)(2,1)}, bf16[1024,512]{1,0:T(8,128)(2,1)}, bf16[512,512]{1,0:T(8,128)(2,1)}, bf16[128,512]{1,0:T(8,128)(2,1)}) custom-call(bf16[1280,512]{1,0:T(8,128)(2,1)} %get-tuple-element.31.pf1_ref, bf16[1280,512]{1,0:T(8,128)(2,1)} %get-tuple-element.32.pg1_ref, f32[1280,512]{1,0:T(8,128)} %get-tuple-element.33.grad2_ref, ...), custom_call_target="tpu_custom_call" | custom-call | flops 4429185024 | bytes 18481152 | tf_op jit(solution)/shard_map/pallas_call | solution.py:36
  129.0 1.2 fusion.27
  130.4 1.0 pad_maximum_fusion
  131.4 0.9 constant_dynamic-slice_fusion.13
  132.9 0.9 fusion.2
  134.0 1.6 concatenate.899
  135.6 1.2 fusion.28
  137.8 1.7 slice_reduce_fusion
  139.5 1.3 add_convert_fusion.3
  140.8 1.7 collective-permute-start.30
  143.2 1.3 add_convert_fusion.1
  145.2 1.7 collective-permute-start.34
  146.9 4.4 %collective-permute-done.30 = bf16[2,1,2,1,80,512]{5,4,3,2,1,0:T(8,128)(2,1)S(1)} collective-permute-done((bf16[2,1,2,1,80,512]{5,4,3,2,1,0:T(8,128)(2,1)S(1)}, bf16[2,1,2,1,80,512]{5,4,3,2,1,0:T(8,128)(2,1)S(1)}, u32[]{:S(2)}, u32[]{:S(2)}) %collective-permute-start.30) | collective-permute-done | bytes 327712 | tf_op jit(solution)/shard_map/ppermute | solution.py:220
  152.0 5.9 %collective-permute-done.38 = bf16[2,1,2,1,80,512]{5,4,3,2,1,0:T(8,128)(2,1)S(1)} collective-permute-done((bf16[2,1,2,1,80,512]{5,4,3,2,1,0:T(8,128)(2,1)S(1)}, bf16[2,1,2,1,80,512]{5,4,3,2,1,0:T(8,128)(2,1)S(1)}, u32[]{:S(2)}, u32[]{:S(2)}) %collective-permute-start.38) | collective-permute-done | bytes 327712 | tf_op jit(solution)/shard_map/ppermute | solution.py:220
  158.6 1.8 collective-permute-start.27
  160.4 3.2 %collective-permute-done.34 = bf16[2,2,1,1,88,512]{5,4,3,2,1,0:T(8,128)(2,1)S(1)} collective-permute-done((bf16[2,2,1,1,88,512]{5,4,3,2,1,0:T(8,128)(2,1)S(1)}, bf16[2,2,1,1,88,512]{5,4,3,2,1,0:T(8,128)(2,1)S(1)}, u32[]{:S(2)}, u32[]{:S(2)}) %collective-permute-start.34) | collective-permute-done | bytes 360480 | tf_op jit(solution)/shard_map/ppermute | solution.py:220
  163.7 1.7 collective-permute-start.35
  165.4 1.7 collective-permute-done.31
  167.2 2.6 %collective-permute-start.32 = (bf16[1,1,1,1,80,512]{5,4,3,2,1,0:T(8,128)(2,1)S(1)}, bf16[1,1,1,1,80,512]{5,4,3,2,1,0:T(8,128)(2,1)S(1)}, u32[]{:S(2)}, u32[]{:S(2)}) collective-permute-start(bf16[1,1,1,1,80,512]{5,4,3,2,1,0:T(8,128)(2,1)S(1)} %constant_dynamic-slice_fusion.7), channel_id=1, source_target_pairs={{0,8},{2,10},{4,12},{6,14},{8,0},{10,2},{12,4},{14,6},{1,9},{3,11}... | collective-permute-start | bytes 245768 | tf_op jit(solution)/shard_map/ppermute | solution.py:220
  169.8 2.2 %collective-permute-start.40 = (bf16[1,1,1,1,80,512]{5,4,3,2,1,0:T(8,128)(2,1)S(1)}, bf16[1,1,1,1,80,512]{5,4,3,2,1,0:T(8,128)(2,1)S(1)}, u32[]{:S(2)}, u32[]{:S(2)}) collective-permute-start(bf16[1,1,1,1,80,512]{5,4,3,2,1,0:T(8,128)(2,1)S(1)} %constant_dynamic-slice_fusion), channel_id=1, source_target_pairs={{0,8},{2,10},{4,12},{6,14},{8,0},{10,2},{12,4},{14,6},{1,9},{3,11}... | collective-permute-start | bytes 245768 | tf_op jit(solution)/shard_map/ppermute | solution.py:220
  172.1 2.9 %collective-permute-done.32 = bf16[1,1,1,1,80,512]{5,4,3,2,1,0:T(8,128)(2,1)S(1)} collective-permute-done((bf16[1,1,1,1,80,512]{5,4,3,2,1,0:T(8,128)(2,1)S(1)}, bf16[1,1,1,1,80,512]{5,4,3,2,1,0:T(8,128)(2,1)S(1)}, u32[]{:S(2)}, u32[]{:S(2)}) %collective-permute-start.32) | collective-permute-done | bytes 81952 | tf_op jit(solution)/shard_map/ppermute | solution.py:220
  175.0 1.9 %collective-permute-done.40 = bf16[1,1,1,1,80,512]{5,4,3,2,1,0:T(8,128)(2,1)S(1)} collective-permute-done((bf16[1,1,1,1,80,512]{5,4,3,2,1,0:T(8,128)(2,1)S(1)}, bf16[1,1,1,1,80,512]{5,4,3,2,1,0:T(8,128)(2,1)S(1)}, u32[]{:S(2)}, u32[]{:S(2)}) %collective-permute-start.40) | collective-permute-done | bytes 81952 | tf_op jit(solution)/shard_map/ppermute | solution.py:220
  177.8 2.5 %collective-permute-start.36 = (bf16[1,1,1,1,88,512]{5,4,3,2,1,0:T(8,128)(2,1)S(1)}, bf16[1,1,1,1,88,512]{5,4,3,2,1,0:T(8,128)(2,1)S(1)}, u32[]{:S(2)}, u32[]{:S(2)}) collective-permute-start(bf16[1,1,1,1,88,512]{5,4,3,2,1,0:T(8,128)(2,1)S(1)} %constant_dynamic-slice_fusion.3), channel_id=1, source_target_pairs={{0,8},{2,10},{4,12},{6,14},{8,0},{10,2},{12,4},{14,6},{1,9},{3,11}... | collective-permute-start | bytes 270344 | tf_op jit(solution)/shard_map/ppermute | solution.py:220
  180.3 5.8 %collective-permute-done.28 = bf16[1,1,1,1,88,512]{5,4,3,2,1,0:T(8,128)(2,1)S(1)} collective-permute-done((bf16[1,1,1,1,88,512]{5,4,3,2,1,0:T(8,128)(2,1)S(1)}, bf16[1,1,1,1,88,512]{5,4,3,2,1,0:T(8,128)(2,1)S(1)}, u32[]{:S(2)}, u32[]{:S(2)}) %collective-permute-start.28) | collective-permute-done | bytes 90144 | tf_op jit(solution)/shard_map/ppermute | solution.py:220
  186.1 1.6 collective-permute-done.36
  189.8 0.8 pad_maximum_fusion.6
  (167 shorter events, 18.1 us)
Async XLA Ops:
  0.6 20.5 %copy-start.11 = (f32[3,128]{1,0:T(4,128)S(1)}, f32[3,128]{1,0:T(4,128)}, u32[]{:S(2)}) copy-start(f32[3,128]{1,0:T(4,128)} %constant.100.clone.1) | copy-start | bytes 4612
  0.6 13.5 %copy-start.10 = (s32[1,512]{1,0:T(1,128)S(1)}, s32[1,512]{1,0:T(1,128)}, u32[]{:S(2)}) copy-start(s32[1,512]{1,0:T(1,128)} %param.10) | copy-start | bytes 6148
  0.7 16.4 %copy-start.8 = (bf16[8,512]{1,0:T(8,128)(2,1)S(1)}, bf16[8,512]{1,0:T(8,128)(2,1)}, u32[]{:S(2)}) copy-start(bf16[8,512]{1,0:T(8,128)(2,1)} %param.14) | copy-start | bytes 24580
  3.2 42.6 %collective-permute-start.15 = (bf16[1,1,1,1,88,512]{5,4,3,2,1,0:T(8,128)(2,1)S(1)}, bf16[1,1,1,1,88,512]{5,4,3,2,1,0:T(8,128)(2,1)S(1)}, u32[]{:S(2)}, u32[]{:S(2)}) collective-permute-start(bf16[1,1,1,1,88,512]{5,4,3,2,1,0:T(8,128)(2,1)S(1)} %get-tuple-element.66), channel_id=1, source_target_pairs={{0,8},{2,10},{4,12},{6,14},{8,0},{10,2},{12,4},{14,6},{1,9},{3,11}... | collective-permute-start | bytes 270344 | tf_op jit(solution)/shard_map/ppermute | solution.py:220
  7.3 35.7 %collective-permute-start.19 = (bf16[1,1,1,1,80,512]{5,4,3,2,1,0:T(8,128)(2,1)S(1)}, bf16[1,1,1,1,80,512]{5,4,3,2,1,0:T(8,128)(2,1)S(1)}, u32[]{:S(2)}, u32[]{:S(2)}) collective-permute-start(bf16[1,1,1,1,80,512]{5,4,3,2,1,0:T(8,128)(2,1)S(1)} %get-tuple-element.70), channel_id=1, source_target_pairs={{0,8},{2,10},{4,12},{6,14},{8,0},{10,2},{12,4},{14,6},{1,9},{3,11}... | collective-permute-start | bytes 245768 | tf_op jit(solution)/shard_map/ppermute | solution.py:220
  7.4 37.0 %collective-permute-start.11 = (bf16[1,1,1,1,80,512]{5,4,3,2,1,0:T(8,128)(2,1)S(1)}, bf16[1,1,1,1,80,512]{5,4,3,2,1,0:T(8,128)(2,1)S(1)}, u32[]{:S(2)}, u32[]{:S(2)}) collective-permute-start(bf16[1,1,1,1,80,512]{5,4,3,2,1,0:T(8,128)(2,1)S(1)} %get-tuple-element.72), channel_id=1, source_target_pairs={{0,8},{2,10},{4,12},{6,14},{8,0},{10,2},{12,4},{14,6},{1,9},{3,11}... | collective-permute-start | bytes 245768 | tf_op jit(solution)/shard_map/ppermute | solution.py:220
  12.7 4.5 %collective-permute-start = (f32[3,128]{1,0:T(4,128)}, f32[3,128]{1,0:T(4,128)S(1)}, u32[]{:S(2)}, u32[]{:S(2)}) collective-permute-start(f32[3,128]{1,0:T(4,128)} %get-tuple-element.28), channel_id=1, source_target_pairs={{0,2},{2,0},{4,6},{6,4},{8,10},{10,8},{12,14},{14,12},{1,3},{3,1},... | collective-permute-start | bytes 4616 | tf_op jit(solution)/shard_map/ppermute | solution.py:220
  14.2 22.1 %collective-permute-start.23 = (s32[512,1]{0,1:T(1,128)S(1)}, s32[512,1]{0,1:T(1,128)S(1)}, u32[]{:S(2)}, u32[]{:S(2)}) collective-permute-start(s32[512,1]{0,1:T(1,128)S(1)} %bitcast.192), channel_id=1, source_target_pairs={{2,0},{4,2},{6,4},{8,6},{10,8},{12,10},{14,12},{3,1},{5,3},{7,5},{... | collective-permute-start | bytes 6152 | tf_op jit(solution)/shard_map/ppermute | solution.py:261
  18.5 4.2 %collective-permute-start.1 = (f32[3,128]{1,0:T(4,128)S(1)}, f32[3,128]{1,0:T(4,128)S(1)}, u32[]{:S(2)}, u32[]{:S(2)}) collective-permute-start(f32[3,128]{1,0:T(4,128)S(1)} %fusion.20), channel_id=1, source_target_pairs={{0,4},{2,6},{4,0},{6,2},{8,12},{10,14},{12,8},{14,10},{1,5},{3,7},... | collective-permute-start | bytes 4616 | tf_op jit(solution)/shard_map/ppermute | solution.py:220
  22.8 4.7 %collective-permute-start.2 = (f32[3,128]{1,0:T(4,128)S(1)}, f32[3,128]{1,0:T(4,128)S(1)}, u32[]{:S(2)}, u32[]{:S(2)}) collective-permute-start(f32[3,128]{1,0:T(4,128)S(1)} %fusion.19), channel_id=1, source_target_pairs={{0,8},{2,10},{4,12},{6,14},{8,0},{10,2},{12,4},{14,6},{1,9},{3,11}... | collective-permute-start | bytes 4616 | tf_op jit(solution)/shard_map/ppermute | solution.py:220
  27.4 5.5 %collective-permute-start.24 = (s32[256,1]{0,1:T(1,128)S(1)}, s32[256,1]{0,1:T(1,128)S(1)}, u32[]{:S(2)}, u32[]{:S(2)}) collective-permute-start(s32[256,1]{0,1:T(1,128)S(1)} %slice_bitcast_fusion.18), channel_id=1, source_target_pairs={{4,0},{6,2},{8,4},{10,6},{12,8},{14,10},{5,1},{7,3},{9,5},{11,7},{... | collective-permute-start | bytes 3080 | tf_op jit(solution)/shard_map/ppermute | solution.py:261
  32.9 18.0 %collective-permute-start.7 = (bf16[1,1,1,1,88,512]{5,4,3,2,1,0:T(8,128)(2,1)S(1)}, bf16[1,1,1,1,88,512]{5,4,3,2,1,0:T(8,128)(2,1)S(1)}, u32[]{:S(2)}, u32[]{:S(2)}) collective-permute-start(bf16[1,1,1,1,88,512]{5,4,3,2,1,0:T(8,128)(2,1)S(1)} %get-tuple-element.68), channel_id=1, source_target_pairs={{0,8},{2,10},{4,12},{6,14},{8,0},{10,2},{12,4},{14,6},{1,9},{3,11}... | collective-permute-start | bytes 270344 | tf_op jit(solution)/shard_map/ppermute | solution.py:220
  36.3 5.4 %collective-permute-start.3 = (bf16[256,128]{1,0:T(8,128)(2,1)S(1)}, bf16[256,128]{1,0:T(8,128)(2,1)S(1)}, u32[]{:S(2)}, u32[]{:S(2)}) collective-permute-start(bf16[256,128]{1,0:T(8,128)(2,1)S(1)} %get-tuple-element.64), channel_id=1, source_target_pairs={{0,4},{2,6},{4,8},{6,10},{8,12},{10,14},{1,5},{3,7},{5,9},{7,11},{... | collective-permute-start | bytes 196616 | tf_op jit(solution)/shard_map/ppermute | solution.py:261
  41.6 9.4 %collective-permute-start.4 = (bf16[512,128]{1,0:T(8,128)(2,1)}, bf16[512,128]{1,0:T(8,128)(2,1)S(1)}, u32[]{:S(2)}, u32[]{:S(2)}) collective-permute-start(bf16[512,128]{1,0:T(8,128)(2,1)} %shard_map.120), channel_id=1, source_target_pairs={{0,2},{2,4},{4,6},{6,8},{8,10},{10,12},{12,14},{1,3},{3,5},{5,7},{... | collective-permute-start | bytes 393224 | tf_op jit(solution)/shard_map/ppermute | solution.py:261
  43.0 35.5 %collective-permute-start.5 = (bf16[512,128]{1,0:T(8,128)(2,1)}, bf16[512,128]{1,0:T(8,128)(2,1)S(1)}, u32[]{:S(2)}, u32[]{:S(2)}) collective-permute-start(bf16[512,128]{1,0:T(8,128)(2,1)} %shard_map.120), channel_id=1, source_target_pairs={{2,0},{4,2},{6,4},{8,6},{10,8},{12,10},{14,12},{3,1},{5,3},{7,5},{... | collective-permute-start | bytes 393224 | tf_op jit(solution)/shard_map/ppermute | solution.py:261
  44.4 35.0 %collective-permute-start.6 = (bf16[256,128]{1,0:T(8,128)(2,1)S(1)}, bf16[256,128]{1,0:T(8,128)(2,1)S(1)}, u32[]{:S(2)}, u32[]{:S(2)}) collective-permute-start(bf16[256,128]{1,0:T(8,128)(2,1)S(1)} %get-tuple-element.63), channel_id=1, source_target_pairs={{4,0},{6,2},{8,4},{10,6},{12,8},{14,10},{5,1},{7,3},{9,5},{11,7},{... | collective-permute-start | bytes 196616 | tf_op jit(solution)/shard_map/ppermute | solution.py:261
  45.7 9.6 %copy-start.4 = (bf16[512,128]{1,0:T(8,128)(2,1)S(1)}, bf16[512,128]{1,0:T(8,128)(2,1)}, u32[]{:S(2)}) copy-start(bf16[512,128]{1,0:T(8,128)(2,1)} %shard_map.120) | copy-start | bytes 393220
  45.8 9.5 %collective-permute-start.20 = (bf16[2,1,1,1,80,512]{5,4,3,2,1,0:T(8,128)(2,1)S(1)}, bf16[2,1,1,1,80,512]{5,4,3,2,1,0:T(8,128)(2,1)S(1)}, u32[]{:S(2)}, u32[]{:S(2)}) collective-permute-start(bf16[2,1,1,1,80,512]{5,4,3,2,1,0:T(8,128)(2,1)S(1)} %maximum_select_fusion.23), channel_id=1, source_target_pairs={{0,2},{2,0},{4,6},{6,4},{8,10},{10,8},{12,14},{14,12},{1,3},{3,1},... | collective-permute-start | bytes 491528 | tf_op jit(solution)/shard_map/ppermute | solution.py:220
  50.9 7.4 %collective-permute-start.12 = (bf16[2,1,1,1,80,512]{5,4,3,2,1,0:T(8,128)(2,1)S(1)}, bf16[2,1,1,1,80,512]{5,4,3,2,1,0:T(8,128)(2,1)S(1)}, u32[]{:S(2)}, u32[]{:S(2)}) collective-permute-start(bf16[2,1,1,1,80,512]{5,4,3,2,1,0:T(8,128)(2,1)S(1)} %maximum_select_fusion.21), channel_id=1, source_target_pairs={{0,2},{2,0},{4,6},{6,4},{8,10},{10,8},{12,14},{14,12},{1,3},{3,1},... | collective-permute-start | bytes 491528 | tf_op jit(solution)/shard_map/ppermute | solution.py:220
  51.1 9.6 %collective-permute-start.16 = (bf16[2,1,1,1,88,512]{5,4,3,2,1,0:T(8,128)(2,1)S(1)}, bf16[2,1,1,1,88,512]{5,4,3,2,1,0:T(8,128)(2,1)S(1)}, u32[]{:S(2)}, u32[]{:S(2)}) collective-permute-start(bf16[2,1,1,1,88,512]{5,4,3,2,1,0:T(8,128)(2,1)S(1)} %maximum_select_fusion.19), channel_id=1, source_target_pairs={{0,4},{2,6},{4,0},{6,2},{8,12},{10,14},{12,8},{14,10},{1,5},{3,7},... | collective-permute-start | bytes 540680 | tf_op jit(solution)/shard_map/ppermute | solution.py:220
  55.3 9.3 %collective-permute-start.8 = (bf16[2,1,1,1,88,512]{5,4,3,2,1,0:T(8,128)(2,1)S(1)}, bf16[2,1,1,1,88,512]{5,4,3,2,1,0:T(8,128)(2,1)S(1)}, u32[]{:S(2)}, u32[]{:S(2)}) collective-permute-start(bf16[2,1,1,1,88,512]{5,4,3,2,1,0:T(8,128)(2,1)S(1)} %maximum_select_fusion.17), channel_id=1, source_target_pairs={{0,4},{2,6},{4,0},{6,2},{8,12},{10,14},{12,8},{14,10},{1,5},{3,7},... | collective-permute-start | bytes 540680 | tf_op jit(solution)/shard_map/ppermute | solution.py:220
  58.4 12.6 %collective-permute-start.21 = (bf16[2,1,2,1,80,512]{5,4,3,2,1,0:T(8,128)(2,1)S(1)}, bf16[2,1,2,1,80,512]{5,4,3,2,1,0:T(8,128)(2,1)S(1)}, u32[]{:S(2)}, u32[]{:S(2)}) collective-permute-start(bf16[2,1,2,1,80,512]{5,4,3,2,1,0:T(8,128)(2,1)S(1)} %maximum_select_fusion.15), channel_id=1, source_target_pairs={{0,4},{2,6},{4,0},{6,2},{8,12},{10,14},{12,8},{14,10},{1,5},{3,7},... | collective-permute-start | bytes 983048 | tf_op jit(solution)/shard_map/ppermute | solution.py:220
  60.7 13.7 %collective-permute-start.13 = (bf16[2,1,2,1,80,512]{5,4,3,2,1,0:T(8,128)(2,1)S(1)}, bf16[2,1,2,1,80,512]{5,4,3,2,1,0:T(8,128)(2,1)S(1)}, u32[]{:S(2)}, u32[]{:S(2)}) collective-permute-start(bf16[2,1,2,1,80,512]{5,4,3,2,1,0:T(8,128)(2,1)S(1)} %maximum_select_fusion.13), channel_id=1, source_target_pairs={{0,4},{2,6},{4,0},{6,2},{8,12},{10,14},{12,8},{14,10},{1,5},{3,7},... | collective-permute-start | bytes 983048 | tf_op jit(solution)/shard_map/ppermute | solution.py:220
  64.6 14.6 %collective-permute-start.17 = (bf16[2,2,1,1,88,512]{5,4,3,2,1,0:T(8,128)(2,1)S(1)}, bf16[2,2,1,1,88,512]{5,4,3,2,1,0:T(8,128)(2,1)S(1)}, u32[]{:S(2)}, u32[]{:S(2)}) collective-permute-start(bf16[2,2,1,1,88,512]{5,4,3,2,1,0:T(8,128)(2,1)S(1)} %maximum_select_fusion.11), channel_id=1, source_target_pairs={{0,2},{2,0},{4,6},{6,4},{8,10},{10,8},{12,14},{14,12},{1,3},{3,1},... | collective-permute-start | bytes 1081352 | tf_op jit(solution)/shard_map/ppermute | solution.py:220
  70.9 7.4 %collective-permute-start.9 = (bf16[2,2,1,1,88,512]{5,4,3,2,1,0:T(8,128)(2,1)S(1)}, bf16[2,2,1,1,88,512]{5,4,3,2,1,0:T(8,128)(2,1)S(1)}, u32[]{:S(2)}, u32[]{:S(2)}) collective-permute-start(bf16[2,2,1,1,88,512]{5,4,3,2,1,0:T(8,128)(2,1)S(1)} %maximum_select_fusion.9), channel_id=1, source_target_pairs={{0,2},{2,0},{4,6},{6,4},{8,10},{10,8},{12,14},{14,12},{1,3},{3,1},... | collective-permute-start | bytes 1081352 | tf_op jit(solution)/shard_map/ppermute | solution.py:220
  74.4 7.3 %collective-permute-start.22 = (bf16[2,2,2,1,80,512]{5,4,3,2,1,0:T(8,128)(2,1)S(1)}, bf16[2,2,2,1,80,512]{5,4,3,2,1,0:T(8,128)(2,1)S(1)}, u32[]{:S(2)}, u32[]{:S(2)}) collective-permute-start(bf16[2,2,2,1,80,512]{5,4,3,2,1,0:T(8,128)(2,1)S(1)} %maximum_select_fusion.7), channel_id=1, source_target_pairs={{0,1},{1,0},{2,3},{3,2},{4,5},{5,4},{6,7},{7,6},{8,9},{9,8},{10,11... | collective-permute-start | bytes 1966088 | tf_op jit(solution)/shard_map/ppermute | solution.py:220
  78.3 2.1 %collective-permute-start.14 = (bf16[2,2,2,1,80,512]{5,4,3,2,1,0:T(8,128)(2,1)S(1)}, bf16[2,2,2,1,80,512]{5,4,3,2,1,0:T(8,128)(2,1)S(1)}, u32[]{:S(2)}, u32[]{:S(2)}) collective-permute-start(bf16[2,2,2,1,80,512]{5,4,3,2,1,0:T(8,128)(2,1)S(1)} %maximum_select_fusion.6), channel_id=1, source_target_pairs={{0,1},{1,0},{2,3},{3,2},{4,5},{5,4},{6,7},{7,6},{8,9},{9,8},{10,11... | collective-permute-start | bytes 1966088 | tf_op jit(solution)/shard_map/ppermute | solution.py:220
  78.5 4.5 %collective-permute-start.10 = (bf16[2,2,2,1,88,512]{5,4,3,2,1,0:T(8,128)(2,1)S(1)}, bf16[2,2,2,1,88,512]{5,4,3,2,1,0:T(8,128)(2,1)S(1)}, u32[]{:S(2)}, u32[]{:S(2)}) collective-permute-start(bf16[2,2,2,1,88,512]{5,4,3,2,1,0:T(8,128)(2,1)S(1)} %maximum_select_fusion.4), channel_id=1, source_target_pairs={{0,1},{1,0},{2,3},{3,2},{4,5},{5,4},{6,7},{7,6},{8,9},{9,8},{10,11... | collective-permute-start | bytes 2162696 | tf_op jit(solution)/shard_map/ppermute | solution.py:220
  79.2 5.7 %collective-permute-start.18 = (bf16[2,2,2,1,88,512]{5,4,3,2,1,0:T(8,128)(2,1)S(1)}, bf16[2,2,2,1,88,512]{5,4,3,2,1,0:T(8,128)(2,1)S(1)}, u32[]{:S(2)}, u32[]{:S(2)}) collective-permute-start(bf16[2,2,2,1,88,512]{5,4,3,2,1,0:T(8,128)(2,1)S(1)} %maximum_select_fusion.5), channel_id=1, source_target_pairs={{0,1},{1,0},{2,3},{3,2},{4,5},{5,4},{6,7},{7,6},{8,9},{9,8},{10,11... | collective-permute-start | bytes 2162696 | tf_op jit(solution)/shard_map/ppermute | solution.py:220
  79.4 1.2 copy-start.9
  129.0 1.4 copy-start.6
  130.2 2.4 %copy-start.2 = (bf16[16,16,512]{2,1,0:T(8,128)(2,1)}, bf16[16,16,512]{2,1,0:T(8,128)(2,1)S(1)}, u32[]{:S(2)}) copy-start(bf16[16,16,512]{2,1,0:T(8,128)(2,1)S(1)} %get-tuple-element.46) | copy-start | bytes 786436
  131.4 1.5 copy-start.1
  132.4 10.8 %collective-permute-start.25 = (bf16[2,2,2,1,88,512]{5,4,3,2,1,0:T(8,128)(2,1)}, bf16[2,2,2,1,88,512]{5,4,3,2,1,0:T(8,128)(2,1)}, u32[]{:S(2)}, u32[]{:S(2)}) collective-permute-start(bf16[2,2,2,1,88,512]{5,4,3,2,1,0:T(8,128)(2,1)} %constant_dynamic-slice_fusion.13), channel_id=1, source_target_pairs={{0,1},{1,0},{2,3},{3,2},{4,5},{5,4},{6,7},{7,6},{8,9},{9,8},{10,11... | collective-permute-start | bytes 2162696 | tf_op jit(solution)/shard_map/ppermute | solution.py:220
  132.9 3.9 %copy-start = (bf16[1024,512]{1,0:T(8,128)(2,1)S(1)}, bf16[1024,512]{1,0:T(8,128)(2,1)}, u32[]{:S(2)}) copy-start(bf16[1024,512]{1,0:T(8,128)(2,1)} %get-tuple-element.44) | copy-start | bytes 3145732
  133.8 5.6 %collective-permute-start.29 = (bf16[2,2,2,1,80,512]{5,4,3,2,1,0:T(8,128)(2,1)}, bf16[2,2,2,1,80,512]{5,4,3,2,1,0:T(8,128)(2,1)}, u32[]{:S(2)}, u32[]{:S(2)}) collective-permute-start(bf16[2,2,2,1,80,512]{5,4,3,2,1,0:T(8,128)(2,1)} %fusion.2), channel_id=1, source_target_pairs={{0,1},{1,0},{2,3},{3,2},{4,5},{5,4},{6,7},{7,6},{8,9},{9,8},{10,11... | collective-permute-start | bytes 1966088 | tf_op jit(solution)/shard_map/ppermute | solution.py:220
  135.6 1.7 copy-start.5
  135.6 1.7 copy-start.7
  136.9 5.5 %collective-permute-start.37 = (bf16[2,2,2,1,80,512]{5,4,3,2,1,0:T(8,128)(2,1)S(1)}, bf16[2,2,2,1,80,512]{5,4,3,2,1,0:T(8,128)(2,1)S(1)}, u32[]{:S(2)}, u32[]{:S(2)}) collective-permute-start(bf16[2,2,2,1,80,512]{5,4,3,2,1,0:T(8,128)(2,1)S(1)} %fusion), channel_id=1, source_target_pairs={{0,1},{1,0},{2,3},{3,2},{4,5},{5,4},{6,7},{7,6},{8,9},{9,8},{10,11... | collective-permute-start | bytes 1966088 | tf_op jit(solution)/shard_map/ppermute | solution.py:220
  137.5 2.0 %copy-start.3 = (bf16[16,16,512]{2,1,0:T(8,128)(2,1)S(1)}, bf16[16,16,512]{2,1,0:T(8,128)(2,1)}, u32[]{:S(2)}) copy-start(bf16[16,16,512]{2,1,0:T(8,128)(2,1)} %copy-done.2) | copy-start | bytes 786436
  137.6 7.4 %collective-permute-start.33 = (bf16[2,2,2,1,88,512]{5,4,3,2,1,0:T(8,128)(2,1)S(1)}, bf16[2,2,2,1,88,512]{5,4,3,2,1,0:T(8,128)(2,1)S(1)}, u32[]{:S(2)}, u32[]{:S(2)}) collective-permute-start(bf16[2,2,2,1,88,512]{5,4,3,2,1,0:T(8,128)(2,1)S(1)} %constant_dynamic-slice_fusion.6), channel_id=1, source_target_pairs={{0,1},{1,0},{2,3},{3,2},{4,5},{5,4},{6,7},{7,6},{8,9},{9,8},{10,11... | collective-permute-start | bytes 2162696 | tf_op jit(solution)/shard_map/ppermute | solution.py:220
  140.8 10.6 %collective-permute-start.30 = (bf16[2,1,2,1,80,512]{5,4,3,2,1,0:T(8,128)(2,1)S(1)}, bf16[2,1,2,1,80,512]{5,4,3,2,1,0:T(8,128)(2,1)S(1)}, u32[]{:S(2)}, u32[]{:S(2)}) collective-permute-start(bf16[2,1,2,1,80,512]{5,4,3,2,1,0:T(8,128)(2,1)S(1)} %constant_dynamic-slice_fusion.9), channel_id=1, source_target_pairs={{0,4},{2,6},{4,0},{6,2},{8,12},{10,14},{12,8},{14,10},{1,5},{3,7},... | collective-permute-start | bytes 983048 | tf_op jit(solution)/shard_map/ppermute | solution.py:220
  142.6 15.2 %collective-permute-start.38 = (bf16[2,1,2,1,80,512]{5,4,3,2,1,0:T(8,128)(2,1)S(1)}, bf16[2,1,2,1,80,512]{5,4,3,2,1,0:T(8,128)(2,1)S(1)}, u32[]{:S(2)}, u32[]{:S(2)}) collective-permute-start(bf16[2,1,2,1,80,512]{5,4,3,2,1,0:T(8,128)(2,1)S(1)} %constant_dynamic-slice_fusion.2), channel_id=1, source_target_pairs={{0,4},{2,6},{4,0},{6,2},{8,12},{10,14},{12,8},{14,10},{1,5},{3,7},... | collective-permute-start | bytes 983048 | tf_op jit(solution)/shard_map/ppermute | solution.py:220
  144.5 13.9 %collective-permute-start.26 = (bf16[2,2,1,1,88,512]{5,4,3,2,1,0:T(8,128)(2,1)S(1)}, bf16[2,2,1,1,88,512]{5,4,3,2,1,0:T(8,128)(2,1)S(1)}, u32[]{:S(2)}, u32[]{:S(2)}) collective-permute-start(bf16[2,2,1,1,88,512]{5,4,3,2,1,0:T(8,128)(2,1)S(1)} %constant_dynamic-slice_fusion.12), channel_id=1, source_target_pairs={{0,2},{2,0},{4,6},{6,4},{8,10},{10,8},{12,14},{14,12},{1,3},{3,1},... | collective-permute-start | bytes 1081352 | tf_op jit(solution)/shard_map/ppermute | solution.py:220
  145.2 18.4 %collective-permute-start.34 = (bf16[2,2,1,1,88,512]{5,4,3,2,1,0:T(8,128)(2,1)S(1)}, bf16[2,2,1,1,88,512]{5,4,3,2,1,0:T(8,128)(2,1)S(1)}, u32[]{:S(2)}, u32[]{:S(2)}) collective-permute-start(bf16[2,2,1,1,88,512]{5,4,3,2,1,0:T(8,128)(2,1)S(1)} %constant_dynamic-slice_fusion.5), channel_id=1, source_target_pairs={{0,2},{2,0},{4,6},{6,4},{8,10},{10,8},{12,14},{14,12},{1,3},{3,1},... | collective-permute-start | bytes 1081352 | tf_op jit(solution)/shard_map/ppermute | solution.py:220
  151.5 15.6 %collective-permute-start.31 = (bf16[2,1,1,1,80,512]{5,4,3,2,1,0:T(8,128)(2,1)S(1)}, bf16[2,1,1,1,80,512]{5,4,3,2,1,0:T(8,128)(2,1)S(1)}, u32[]{:S(2)}, u32[]{:S(2)}) collective-permute-start(bf16[2,1,1,1,80,512]{5,4,3,2,1,0:T(8,128)(2,1)S(1)} %constant_dynamic-slice_fusion.8), channel_id=1, source_target_pairs={{0,2},{2,0},{4,6},{6,4},{8,10},{10,8},{12,14},{14,12},{1,3},{3,1},... | collective-permute-start | bytes 491528 | tf_op jit(solution)/shard_map/ppermute | solution.py:220
  157.9 11.8 %collective-permute-start.39 = (bf16[2,1,1,1,80,512]{5,4,3,2,1,0:T(8,128)(2,1)S(1)}, bf16[2,1,1,1,80,512]{5,4,3,2,1,0:T(8,128)(2,1)S(1)}, u32[]{:S(2)}, u32[]{:S(2)}) collective-permute-start(bf16[2,1,1,1,80,512]{5,4,3,2,1,0:T(8,128)(2,1)S(1)} %constant_dynamic-slice_fusion.1), channel_id=1, source_target_pairs={{0,2},{2,0},{4,6},{6,4},{8,10},{10,8},{12,14},{14,12},{1,3},{3,1},... | collective-permute-start | bytes 491528 | tf_op jit(solution)/shard_map/ppermute | solution.py:220
  158.6 18.5 %collective-permute-start.27 = (bf16[2,1,1,1,88,512]{5,4,3,2,1,0:T(8,128)(2,1)S(1)}, bf16[2,1,1,1,88,512]{5,4,3,2,1,0:T(8,128)(2,1)S(1)}, u32[]{:S(2)}, u32[]{:S(2)}) collective-permute-start(bf16[2,1,1,1,88,512]{5,4,3,2,1,0:T(8,128)(2,1)S(1)} %constant_dynamic-slice_fusion.11), channel_id=1, source_target_pairs={{0,4},{2,6},{4,0},{6,2},{8,12},{10,14},{12,8},{14,10},{1,5},{3,7},... | collective-permute-start | bytes 540680 | tf_op jit(solution)/shard_map/ppermute | solution.py:220
  163.7 14.0 %collective-permute-start.35 = (bf16[2,1,1,1,88,512]{5,4,3,2,1,0:T(8,128)(2,1)S(1)}, bf16[2,1,1,1,88,512]{5,4,3,2,1,0:T(8,128)(2,1)S(1)}, u32[]{:S(2)}, u32[]{:S(2)}) collective-permute-start(bf16[2,1,1,1,88,512]{5,4,3,2,1,0:T(8,128)(2,1)S(1)} %constant_dynamic-slice_fusion.4), channel_id=1, source_target_pairs={{0,4},{2,6},{4,0},{6,2},{8,12},{10,14},{12,8},{14,10},{1,5},{3,7},... | collective-permute-start | bytes 540680 | tf_op jit(solution)/shard_map/ppermute | solution.py:220
  167.2 7.8 %collective-permute-start.32 = (bf16[1,1,1,1,80,512]{5,4,3,2,1,0:T(8,128)(2,1)S(1)}, bf16[1,1,1,1,80,512]{5,4,3,2,1,0:T(8,128)(2,1)S(1)}, u32[]{:S(2)}, u32[]{:S(2)}) collective-permute-start(bf16[1,1,1,1,80,512]{5,4,3,2,1,0:T(8,128)(2,1)S(1)} %constant_dynamic-slice_fusion.7), channel_id=1, source_target_pairs={{0,8},{2,10},{4,12},{6,14},{8,0},{10,2},{12,4},{14,6},{1,9},{3,11}... | collective-permute-start | bytes 245768 | tf_op jit(solution)/shard_map/ppermute | solution.py:220
  169.8 7.1 %collective-permute-start.40 = (bf16[1,1,1,1,80,512]{5,4,3,2,1,0:T(8,128)(2,1)S(1)}, bf16[1,1,1,1,80,512]{5,4,3,2,1,0:T(8,128)(2,1)S(1)}, u32[]{:S(2)}, u32[]{:S(2)}) collective-permute-start(bf16[1,1,1,1,80,512]{5,4,3,2,1,0:T(8,128)(2,1)S(1)} %constant_dynamic-slice_fusion), channel_id=1, source_target_pairs={{0,8},{2,10},{4,12},{6,14},{8,0},{10,2},{12,4},{14,6},{1,9},{3,11}... | collective-permute-start | bytes 245768 | tf_op jit(solution)/shard_map/ppermute | solution.py:220
  177.1 8.9 %collective-permute-start.28 = (bf16[1,1,1,1,88,512]{5,4,3,2,1,0:T(8,128)(2,1)S(1)}, bf16[1,1,1,1,88,512]{5,4,3,2,1,0:T(8,128)(2,1)S(1)}, u32[]{:S(2)}, u32[]{:S(2)}) collective-permute-start(bf16[1,1,1,1,88,512]{5,4,3,2,1,0:T(8,128)(2,1)S(1)} %constant_dynamic-slice_fusion.10), channel_id=1, source_target_pairs={{0,8},{2,10},{4,12},{6,14},{8,0},{10,2},{12,4},{14,6},{1,9},{3,11}... | collective-permute-start | bytes 270344 | tf_op jit(solution)/shard_map/ppermute | solution.py:220
  177.8 9.9 %collective-permute-start.36 = (bf16[1,1,1,1,88,512]{5,4,3,2,1,0:T(8,128)(2,1)S(1)}, bf16[1,1,1,1,88,512]{5,4,3,2,1,0:T(8,128)(2,1)S(1)}, u32[]{:S(2)}, u32[]{:S(2)}) collective-permute-start(bf16[1,1,1,1,88,512]{5,4,3,2,1,0:T(8,128)(2,1)S(1)} %constant_dynamic-slice_fusion.3), channel_id=1, source_target_pairs={{0,8},{2,10},{4,12},{6,14},{8,0},{10,2},{12,4},{14,6},{1,9},{3,11}... | collective-permute-start | bytes 270344 | tf_op jit(solution)/shard_map/ppermute | solution.py:220

commit v2 on v1

v2 whole, which is shorter than its diff:
```python
import functools
import math

import jax
import jax.numpy as jnp
from jax import lax
from jax.experimental import pallas as pl
from jax.experimental.pallas import tpu as pltpu
from jax.sharding import PartitionSpec as P

BASE_DILATION = 256
LEVEL_FLOOR = 0.1
F32 = jnp.float32
BF16 = jnp.bfloat16
TILE = 256
VMEM_LIMIT = 56 * 1024 * 1024
PARAMS = pltpu.CompilerParams(vmem_limit_bytes=VMEM_LIMIT)
WHOLE = pl.BlockSpec(memory_space=pltpu.VMEM)
SCALAR = pl.BlockSpec(memory_space=pltpu.SMEM)


def dot(a, b):
    return lax.dot_general(a, b, (((1,), (0,)), ((), ())), preferred_element_type=F32)


def dot_t(a, b):
    return lax.dot_general(a, b, (((1,), (1,)), ((), ())), preferred_element_type=F32)


def t_dot(a, b):
    return lax.dot_general(a, b, (((0,), (0,)), ((), ())), preferred_element_type=F32)


def call(kernel, outs, scratch, flops, *args):
    moved = sum(a.size * a.dtype.itemsize for a in args)
    moved += sum(math.prod(s) * jnp.dtype(d).itemsize for s, d in outs)
    return pl.pallas_call(
        kernel,
        out_shape=[jax.ShapeDtypeStruct(s, d) for s, d in outs],
        in_specs=[SCALAR if a.dtype == jnp.int32 and a.shape == (1,) else WHOLE for a in args],
        out_specs=[WHOLE] * len(outs),
        scratch_shapes=scratch,
        compiler_params=PARAMS,
        cost_estimate=pl.CostEstimate(flops=flops, bytes_accessed=moved, transcendentals=0),
    )(*args)


def scan_kernel(feat_ref, forget_ref, keep_ref, mass_ref, weight_ref, sum_ref):
    feat, forget = feat_ref[...], forget_ref[...]
    rows = feat.shape[0]
    keep, mass, weight = 1.0 - forget, forget * (feat * feat), forget
    row = lax.broadcasted_iota(jnp.int32, feat.shape, 0)
    step = 1
    while step < rows:
        inside = row >= step
        before = jnp.where(inside, pltpu.roll(mass, step, 0), 0.0)
        mass = keep * before + mass
        before = jnp.where(inside, pltpu.roll(weight, step, 0), 0.0)
        weight = keep * before + weight
        keep = keep * jnp.where(inside, pltpu.roll(keep, step, 0), 1.0)
        step *= 2
    keep_ref[...], mass_ref[...], weight_ref[...] = keep, mass, weight
    sum_ref[0:1, :] = keep[rows - 1 :]
    sum_ref[1:2, :] = mass[rows - 1 :]
    sum_ref[2:3, :] = weight[rows - 1 :]


def norm_kernel(feat_ref, keep_ref, mass_ref, weight_ref, carry_ref, out_ref):
    keep = keep_ref[...]
    mass = keep * carry_ref[1:2, :] + mass_ref[...]
    weight = keep * carry_ref[2:3, :] + weight_ref[...]
    out_ref[...] = (feat_ref[...] / jnp.sqrt(mass / weight + LEVEL_FLOOR)).astype(BF16)


def compose(earlier, later):
    keep = later[0:1] * earlier[0:1]
    rest = later[0:1] * earlier[1:3] + later[1:3]
    return jnp.concatenate([keep, rest], axis=0)


def rows_of(ref, part=None):
    half = ref.shape[0] // 2
    value = ref[...] if part is None else ref[part * half : (part + 1) * half]
    return value.reshape(-1, value.shape[-1]).astype(BF16)


def place(site_ref, copies):
    mine = site_ref[0]

    def body(tm, _):
        for target, row, own, other, half, at, count in copies:
            target[2 * tm + mine, row : row + count, :] = own[tm, half, at : at + count, :]
            target[2 * tm + 1 - mine, row : row + count, :] = other[tm, half, at : at + count, :]
        return 0

    lax.fori_loop(0, copies[0][2].shape[0], body, 0)


def activate(past, now, filt_ref, gate_ref):
    joined = jnp.concatenate([past, now], axis=1)
    t = jnp.tanh(dot(joined, rows_of(filt_ref)))
    s = 0.5 + 0.5 * jnp.tanh(0.5 * dot(joined, rows_of(gate_ref)))
    return t, s


def tile_at(i, offset=0):
    return pl.ds(pl.multiple_of(i * TILE + offset, TILE), TILE)


def forward_first(before, site_ref, norm_ref, w_in_ref, a_ref, a2_ref, b_ref, b2_ref, c_ref, c2_ref,
                  h0_ref, h1_ref, tanh_ref, sigm_ref, filt_ref, gate_ref, res_ref):
    rows, c = h0_ref.shape
    kept = tanh_ref.shape[0]
    d = rows - h1_ref.shape[0]
    n, r = a_ref.shape[2], res_ref.shape[1] // 2
    place(site_ref, [
        (filt_ref, 0, a_ref, a2_ref, 0, 0, n), (gate_ref, 0, a_ref, a2_ref, 1, 0, n),
        (filt_ref, n, b_ref, b2_ref, 0, 0, n), (gate_ref, n, b_ref, b2_ref, 1, 0, n),
        (res_ref, 0, c_ref, c2_ref, 0, 0, r), (res_ref, r, c_ref, c2_ref, 1, 0, r)])

    def enter(i, _):
        h0_ref[tile_at(i), :] = dot(norm_ref[tile_at(i), :], w_in_ref[...]).astype(BF16)
        return 0

    lax.fori_loop(0, rows // TILE, enter, 0)

    def tile(i):
        now = h0_ref[tile_at(i, d), :]
        t, s = activate(h0_ref[tile_at(i), :], now, filt_ref, gate_ref)
        out = now.astype(F32) + dot((t * s).astype(BF16), rows_of(res_ref))
        h1_ref[tile_at(i), :] = out.astype(BF16)
        return t, s

    def plain(i, _):
        tile(i)
        return 0

    def saving(i, _):
        t, s = tile(i)
        tanh_ref[tile_at(i, -before), :], sigm_ref[tile_at(i, -before), :] = t, s
        return 0

    lax.fori_loop(0, before // TILE, plain, 0)
    lax.fori_loop(before // TILE, (before + kept) // TILE, saving, 0)
    lax.fori_loop((before + kept) // TILE, h1_ref.shape[0] // TILE, plain, 0)


def store_terms(site_ref, keep_ref, send_ref, row, value, first, size, start, count, lane=0):
    mine = site_ref[0] == 0
    at = (slice(row, row + count), slice(lane, lane + value.shape[1]))
    for k in range(value.shape[0] // (2 * size)):
        low = value[2 * k * size + start : 2 * k * size + start + count]
        high = value[(2 * k + 1) * size + start : (2 * k + 1) * size + start + count]
        keep_ref[(first + k,) + at] = jnp.where(mine, low, high).astype(keep_ref.dtype)
        send_ref[(first + k,) + at] = jnp.where(mine, high, low).astype(send_ref.dtype)


def conv_terms(site_ref, keep_ref, send_ref, first, size, res, value):
    c = value.shape[1] // 2
    store_terms(site_ref, keep_ref, send_ref, 0, value[:, c:], first, size, 0, size)
    store_terms(site_ref, keep_ref, send_ref, size + res, value[:, :c], first, size, 0, size)


def res_terms(site_ref, keep_ref, send_ref, first, conv, size, value):
    half = size // 2
    store_terms(site_ref, keep_ref, send_ref, conv, value, first, size, half, half)
    store_terms(site_ref, keep_ref, send_ref, 2 * conv + half, value, first, size, 0, half)


def second_kernel(steps, scale, sizes, site_ref, h1_ref, w_out_ref, label_ref, valid_ref,
                  a_ref, a2_ref, b_ref, b2_ref, c_ref, c2_ref,
                  loss_ref, keep_ref, send_ref, back_ref, grad_ref, filt_ref, gate_ref,
                  res_ref, gated_ref, h2_ref, lgrad_ref, round_ref):
    rows, c = grad_ref.shape
    d = h1_ref.shape[0] - rows
    classes = w_out_ref.shape[1]
    conv, res, _, out = sizes
    n, r = conv // 2, res // 2
    place(site_ref, [
        (res_ref, 0, a_ref, a2_ref, 0, 0, r), (res_ref, r, a_ref, a2_ref, 1, 0, r),
        (filt_ref, 0, b_ref, b2_ref, 0, 0, n), (gate_ref, 0, b_ref, b2_ref, 1, 0, n),
        (filt_ref, n, c_ref, c2_ref, 0, 0, n), (gate_ref, n, c_ref, c2_ref, 1, 0, n)])

    def tile(i, _):
        at = tile_at(i)
        now = h1_ref[tile_at(i, d), :]
        t, s = activate(h1_ref[at, :], now, filt_ref, gate_ref)
        gated = (t * s).astype(BF16)
        h2 = (now.astype(F32) + dot(gated, rows_of(res_ref))).astype(BF16)
        logits = dot(h2, w_out_ref[...])
        total = jnp.log(jnp.sum(jnp.exp(logits), axis=1, keepdims=True))
        hot = (label_ref[at, :] == lax.broadcasted_iota(jnp.int32, (TILE, classes), 1)).astype(F32)
        valid = valid_ref[at, :]
        loss_ref[at, :] = (total - jnp.sum(logits * hot, axis=1, keepdims=True)) * valid
        lgrad = ((jnp.exp(logits - total) - hot) * (valid * scale)).astype(BF16)
        grad = dot_t(lgrad, w_out_ref[...])
        rounded = grad.astype(BF16)
        back = dot_t(rounded, rows_of(res_ref))
        back_ref[at, :c] = (back * s * (1.0 - t * t)).astype(BF16)
        back_ref[at, c:] = (back * t * s * (1.0 - s)).astype(BF16)
        grad_ref[at, :] = grad
        gated_ref[at, :] = gated
        h2_ref[at, :] = h2
        lgrad_ref[at, :] = lgrad
        round_ref[at, :] = rounded
        return 0

    lax.fori_loop(0, rows // TILE, tile, 0)
    own = slice(0, steps)
    targets = (site_ref, keep_ref, send_ref)

    def terms(i, _):
        at = tile_at(i)
        first = i * (TILE // (2 * conv))
        conv_terms(*targets, first, conv, r, t_dot(h1_ref[0:steps, at], back_ref[own, :]))
        conv_terms(*targets, first + c // (2 * conv), conv, r, t_dot(h1_ref[d : d + steps, at], back_ref[own, :]))
        res_terms(*targets, i * (TILE // (2 * res)), conv, res, t_dot(gated_ref[own, at], round_ref[own, :]))
        value = t_dot(h2_ref[own, at], lgrad_ref[own, :])
        count = out * classes // c
        for q in range(c // classes):
            store_terms(*targets, 2 * conv + res, value, i * (TILE // (2 * out)), out, q * count, count, q * classes)
        return 0

    lax.fori_loop(0, c // TILE, terms, 0)


def grad_first(back1_ref, grad2_ref, filt1_ref, gate1_ref, tanh_ref, sigm_ref, res_ref,
               grad_ref, round_ref, back_ref):
    rows, c = grad_ref.shape
    d1 = back1_ref.shape[0] - rows

    def tile(i, _):
        at, later = tile_at(i), tile_at(i, d1)
        grad = grad2_ref[at, :] + dot_t(back1_ref[at, :c], rows_of(filt1_ref, 1))
        grad += dot_t(back1_ref[at, c:], rows_of(gate1_ref, 1))
        grad += dot_t(back1_ref[later, :c], rows_of(filt1_ref, 0))
        grad += dot_t(back1_ref[later, c:], rows_of(gate1_ref, 0))
        rounded = grad.astype(BF16)
        t, s = tanh_ref[at, :], sigm_ref[at, :]
        back = dot_t(rounded, rows_of(res_ref))
        back_ref[at, :c] = (back * s * (1.0 - t * t)).astype(BF16)
        back_ref[at, c:] = (back * t * s * (1.0 - s)).astype(BF16)
        grad_ref[at, :] = grad
        round_ref[at, :] = rounded
        return 0

    lax.fori_loop(0, rows // TILE, tile, 0)


def terms_first(steps, start, sizes, site_ref, back_ref, grad_ref, round_ref, h0_ref, tanh_ref, sigm_ref,
                norm_ref, filt_ref, gate_ref, keep_ref, send_ref, last_ref):
    rows, c = grad_ref.shape
    d0 = rows - steps
    conv, res, enter, _ = sizes
    own = slice(0, steps)
    targets = (site_ref, keep_ref, send_ref)

    def terms(i, _):
        at = tile_at(i)
        first = i * (TILE // (2 * conv))
        past, now = h0_ref[start - d0 : start - d0 + steps, at], h0_ref[start : start + steps, at]
        conv_terms(*targets, first, conv, res // 2, t_dot(past, back_ref[own, :]))
        conv_terms(*targets, first + c // (2 * conv), conv, res // 2, t_dot(now, back_ref[own, :]))
        gated = (tanh_ref[own, at] * sigm_ref[own, at]).astype(BF16)
        res_terms(*targets, i * (TILE // (2 * res)), conv, res, t_dot(gated, round_ref[own, :]))
        return 0

    lax.fori_loop(0, c // TILE, terms, 0)

    def last(i, _):
        at, later = tile_at(i), tile_at(i, d0)
        grad = grad_ref[at, :] + dot_t(back_ref[at, :c], rows_of(filt_ref, 1))
        grad += dot_t(back_ref[at, c:], rows_of(gate_ref, 1))
        grad += dot_t(back_ref[later, :c], rows_of(filt_ref, 0))
        grad += dot_t(back_ref[later, c:], rows_of(gate_ref, 0))
        last_ref[at, :] = grad.astype(BF16)
        return 0

    lax.fori_loop(0, steps // TILE, last, 0)
    value = t_dot(norm_ref[start : start + steps, :], last_ref[...])
    store_terms(*targets, 2 * conv + res, value, 0, enter, 0, enter)


NEAR, FAR, ACROSS = ("tm", 0), ("tm", 1), ("groups", 0)


def swap(value, link):
    axis, bit = link
    return lax.ppermute(value, axis, [(i, i ^ (1 << bit)) for i in range(lax.axis_size(axis))])


def my_bit(link):
    return (lax.axis_index(link[0]) >> link[1]) & 1


def time_bits():
    return lax.axis_size("tm").bit_length() - 1


def dim_of(link):
    return time_bits() if link == ACROSS else time_bits() - 1 - link[1]


def join(held, other, link):
    dim = dim_of(link)
    return jnp.where(
        my_bit(link) == 0,
        jnp.concatenate([held, other], axis=dim),
        jnp.concatenate([other, held], axis=dim),
    )


def together(*values):
    return lax.optimization_barrier(values)


def sum_step(held, link):
    dim, mine = dim_of(link), my_bit(link)
    other = swap(lax.dynamic_index_in_dim(held, 1 - mine, dim), link)
    return lax.dynamic_index_in_dim(held, mine, dim).astype(F32) + other.astype(F32)


def sum_rest(held, gate_rows):
    shape = held.shape[1:]
    held = held.reshape((2,) * time_bits() + shape)
    gate, filt = held[..., :gate_rows, :], held[..., gate_rows:, :]
    filt, gate = sum_step(filt, NEAR).astype(BF16), sum_step(gate, FAR).astype(BF16)
    filt, gate = sum_step(filt, FAR).astype(BF16), sum_step(gate, NEAR).astype(BF16)
    held = jnp.concatenate([gate, filt], axis=-2)
    for bit in range(2, time_bits()):
        total = sum_step(held, ("tm", bit))
        held = total.astype(BF16)
    return total.reshape(shape)


def hop(value, by):
    size = lax.axis_size("tm")
    return lax.ppermute(value, "tm", [(i, i + by) for i in range(size) if 0 <= i + by < size])


def rows_before(value, count):
    steps, parts, by = value.shape[0], [], 1
    while count > 0:
        take = min(count, steps)
        parts.insert(0, hop(value[steps - take :], by))
        count, by = count - take, by + 1
    return parts


def rows_after(value, count):
    steps, parts, by = value.shape[0], [], 1
    while count > 0:
        take = min(count, steps)
        parts.append(hop(value[:take], -by))
        count, by = count - take, by + 1
    return parts


def on_device(features, forget, labels, lengths, w_conv, w_res, w_in, w_out):
    _, steps, bands = features.shape
    time_devices, site_devices = lax.axis_size("tm"), lax.axis_size("site")
    devices = time_devices * site_devices
    c = w_res.shape[2]
    classes = w_out.shape[1]
    conv, res, enter, out = sizes = (w_conv.shape[1], w_res.shape[1], w_in.shape[0], w_out.shape[0])
    half, extra = res // 2, out * classes // c
    aligned = conv % 32 == 0 and res % 32 == 0
    kind = BF16 if aligned else F32
    d0, d1 = BASE_DILATION, 2 * BASE_DILATION
    reach = d0 + d1
    position, site = lax.axis_index("tm"), lax.axis_index("site")
    site_arg = site.astype(jnp.int32)[None]
    core = ("site", 0)

    def own_half(across):
        cols = slice(across * c, (across + 1) * c)
        part = slice(across * half, (across + 1) * half)
        more = w_in if across == 0 else w_out.reshape(extra, c)
        first, second = w_conv[0, :, cols], w_conv[1, :, cols]
        n = conv // 2
        return jnp.concatenate([
            first[:n], w_res[1, part], first[n:], second[:n], w_res[0, part], more, second[n:]])

    n = conv // 2
    cuts = [n, half, n, n, half + enter, n]
    held = jnp.where(my_bit(ACROSS) == 0, own_half(0), own_half(1))
    held = held.reshape((1,) * (time_bits() + 1) + held.shape)

    block = ((steps, bands), F32)
    feat = features[0]
    keep, mass, weight, summary = call(
        scan_kernel, [block] * 3 + [((3, bands), F32)], [], 40 * steps * bands, feat, forget[0])
    labels_here = labels[0][:, None]
    label_window = jnp.concatenate([labels_here] + rows_after(labels_here, reach))
    for bit in reversed(range(2, time_bits())):
        held = join(held, swap(held, ("tm", bit)), ("tm", bit))
    carry = jnp.concatenate([jnp.ones((1, bands), F32), jnp.zeros((2, bands), F32)])
    total = summary

    def carry_step(carry, total, bit):
        other = swap(total, ("tm", bit))
        upper = my_bit(("tm", bit)) == 1
        carry = jnp.where(upper, compose(other, carry), carry)
        return carry, jnp.where(upper, compose(other, total), compose(total, other))

    orders = [(FAR, NEAR, ACROSS), (NEAR, ACROSS, FAR), (ACROSS, FAR, NEAR)]
    bounds = [0, cuts[0] + cuts[1], sum(cuts[:4]), sum(cuts)]
    pieces = [held[..., bounds[k] : bounds[k + 1], :] for k in range(3)]
    bits = list(range(time_bits()))
    for step in range(2):
        take = bits if step == 1 else bits[:1]
        bits = bits[len(take):]
        *pieces, carry, total = together(*pieces, carry, total)
        pieces = [join(p, swap(p, order[step]), order[step]) for p, order in zip(pieces, orders)]
        for bit in take:
            carry, total = carry_step(carry, total, bit)
    (normed,) = call(norm_kernel, [((steps, bands), BF16)], [], 10 * steps * bands,
                     feat, keep, mass, weight, carry)
    *pieces, normed = together(*pieces, normed)
    layers = [[p[..., :cut, :] for p, cut in zip(pieces, cuts[::2])],
              [p[..., cut:, :] for p, cut in zip(pieces, cuts[::2])]]
    first = [join(p, swap(p, order[2]), order[2]) for p, order in zip(layers[0], orders)]
    window = jnp.concatenate(rows_before(normed, reach) + [normed] + rows_after(normed, reach))
    *rest, window = together(*first, *layers[1], window)
    first, second = rest[:3], rest[3:]
    second = [join(p, swap(p, order[2]), order[2]) for p, order in zip(second, orders)]

    def both_cores(parts):
        parts = [p.reshape((time_devices, 2) + p.shape[-2:]) for p in parts]
        pairs = [(p, swap(p, core)) for p in parts]
        return pairs

    def kernel_args(pairs):
        return [v.astype(kind) for pair in pairs for v in pair]

    first = both_cores(first)
    own, other = (v[:, :, half:] for v in first[2])
    extras = jnp.where(site == 0, jnp.stack([own, other], axis=1), jnp.stack([other, own], axis=1))
    in_all = extras[:, :, 0].reshape(-1, c)
    out_all = extras[:, :, 1].reshape(-1, classes)

    at = position * steps + lax.broadcasted_iota(jnp.int32, (steps + reach, 1), 0)
    valid = (at < lengths[0]).astype(F32)

    total_rows, rows0, rows1 = steps + 2 * reach, steps + d0, steps + reach
    conv_all, res_all = ((devices, conv, c), kind), ((devices, res, c), kind)
    h0, h1, tanh0, sigm0, filt0, gate0, res0 = call(
        functools.partial(forward_first, d1),
        [((total_rows, c), BF16), ((total_rows - d0, c), BF16), ((rows0, c), F32), ((rows0, c), F32),
         conv_all, conv_all, res_all],
        [], 2 * total_rows * c * (bands + 5 * c), site_arg, window, in_all, *kernel_args(first))

    second = both_cores(second)
    scale = 1.0 / math.sqrt(site_devices * steps * time_devices)
    package = [((time_devices, 2 * conv + res + extra, c), kind)] * 2
    loss, keep1, send1, back1, grad2, filt1, gate1 = call(
        functools.partial(second_kernel, steps, scale, sizes),
        [((rows1, 1), F32)] + package + [((rows1, 2 * c), BF16), ((rows1, c), F32), conv_all, conv_all],
        [pltpu.VMEM((devices, res, c), kind), pltpu.VMEM((rows1, c), BF16), pltpu.VMEM((rows1, c), BF16),
         pltpu.VMEM((rows1, classes), BF16), pltpu.VMEM((rows1, c), BF16)],
        2 * rows1 * c * 6 * c + 2 * steps * 5 * c * c,
        site_arg, h1, out_all, label_window, valid, *kernel_args(second))

    sum1 = (keep1.astype(F32) + swap(send1.astype(BF16), core).astype(F32)).astype(BF16)
    grad1, round0, back0 = call(
        grad_first, [((rows0, c), F32), ((rows0, c), BF16), ((rows0, 2 * c), BF16)], [],
        2 * rows0 * c * 5 * c, back1, grad2, filt1, gate1, tanh0, sigm0, res0)
    sum1, back0 = together(sum1, back0)
    keep0, send0 = call(
        functools.partial(terms_first, steps, reach, sizes), package, [pltpu.VMEM((steps, c), BF16)],
        2 * steps * 9 * c * c,
        site_arg, back0, grad1, round0, h0, tanh0, sigm0, window, filt0, gate0)
    sum0 = (keep0.astype(F32) + swap(send0.astype(BF16), core).astype(F32)).astype(BF16)

    grads = []
    for held in (sum0, sum1):
        total = sum_rest(held, conv + half)
        gate, filt = total[: conv + half], total[conv + half :]
        grads.append((
            jnp.concatenate([filt[:conv], gate[:conv]], axis=1),
            jnp.concatenate([filt[conv : conv + half], gate[conv:]]),
            filt[conv + half :],
        ))
    (conv0, res0, grad_in), (conv1, res1, grad_out) = grads
    return (
        loss[:steps, 0][None],
        jnp.stack([conv0, conv1]),
        jnp.stack([res0, res1]),
        grad_in,
        unpack_out(grad_out, classes),
    )


def unpack_out(value, classes):
    q = value.shape[1] // classes
    return jnp.concatenate([value[:, k * classes : (k + 1) * classes] for k in range(q)])


def solution(mesh):
    return jax.shard_map(
        on_device,
        mesh=mesh,
        in_specs=(
            P(("groups", "site"), "tm", None),
            P(("groups", "site"), "tm", None),
            P(("groups", "site"), "tm"),
            P(("groups", "site")),
            P(None, ("tm", "site"), None),
            P(None, ("tm", "site"), None),
            P(("tm", "site"), None),
            P(("tm", "site"), None),
        ),
        out_specs=(
            P(("groups", "site"), "tm"),
            P("groups", ("tm", "site"), None),
            P("groups", ("tm", "site"), None),
            P(("tm", "site"), "groups"),
            P(("tm", "site"), "groups"),
        ),
        check_vma=False,
    )
```

time: 191 us -> 182 us (0.953)
  other arithmetic: 13.6 us -> 5.81 us
  Pallas kernels: 44.6 us -> 52.2 us
  starting transfers between devices: 62.6 us -> 55 us
  waiting for transfers between devices: 48.3 us -> 44.8 us
    ppermute x35 -> x34, starting transfers between devices: 52.7 us -> 39.6 us  [swap(): lax.ppermute(value, axis, [(i, i ^ 1 << bit) for i in range(lax.axis_size...]
    unnamed x28 -> x58, local copies, waits for them, and re-layouts: 0.7 us -> 11.9 us
    pallas_call x5 -> x6, Pallas kernels: 44.6 us -> 52.2 us  [call(): pl.pallas_call(kernel, out_shape=[jax.ShapeDtypeStruct(s, d) for s, d in...]
    slice x21 -> x22, local copies, waits for them, and re-layouts: 7.52 us -> 1.71 us  [the longest x1 0.66 us: on_device(): in_all = extras[:, :, 0].reshape(-1, c)]
    ppermute x6, starting transfers between devices: 9.96 us -> 15.3 us  [hop(): lax.ppermute(value, 'tm', [(i, i + by) for i in range(size) if 0 <= i + b...]
    concatenate x18 -> x4, other arithmetic: 4.26 us -> 0.67 us  [the longest x1 0.61 us: unpack_out(): jnp.concatenate([value[:, k * classes:(k + 1) * classes] for k in range(q)])]
    ppermute x35 -> x34, waiting for transfers between devices: 46.8 us -> 43.4 us  [swap(): lax.ppermute(value, axis, [(i, i ^ 1 << bit) for i in range(lax.axis_size...]
    reshape x4 -> x0, local copies, waits for them, and re-layouts: 2.74 us -> none  [the longest x1 0.76 us: on_device(): out_all = out_all.reshape(-1, classes)]
  transfers between devices with their start and end apart: 41 -> 40, of which waited for: 18 -> 14; matrix products, arithmetic and copies ran while one was open for 11% -> 6% of each run, Pallas kernels for 2% -> 20%
where the time goes in v2:
time: 182 us; the launch traced here: 181 us
  starting transfers between devices  55 us (30%)
  Pallas kernels  52.2 us (29%)
  waiting for transfers between devices  44.8 us (25%)
  local copies, waits for them, and re-layouts  21.1 us (12%)
  other arithmetic  5.81 us (3%)
  between operations  2.19 us (1%)
    pallas_call x6, Pallas kernels, call(): pl.pallas_call(kernel, out_shape=[jax.ShapeDtypeStruct(s, d) for s, d in...  52.2 us
    ppermute x34, waiting for transfers between devices, swap(): lax.ppermute(value, axis, [(i, i ^ 1 << bit) for i in range(lax.axis_size...  43.4 us
    ppermute x34, starting transfers between devices, swap(): lax.ppermute(value, axis, [(i, i ^ 1 << bit) for i in range(lax.axis_size...  39.6 us
    ppermute x6, starting transfers between devices, hop(): lax.ppermute(value, 'tm', [(i, i + by) for i in range(size) if 0 <= i + b...  15.3 us
    unnamed x58, local copies, waits for them, and re-layouts  11.9 us
  transfers between devices with their start and end apart: 40, of which 14 were waited for; matrix products, arithmetic and copies ran while one was open for 6% of the time, Pallas kernels for 20%

profile of v2, /device:TPU:0, one launch (start us, length us, event | category | flops | bytes accessed | tf_op | source)
XLA Modules:
  0.0 181.1 jit_solution(11585176773805620417)
XLA Ops:
  0.7 0.8 constant_dynamic-update-slice_fusion.27
  1.5 0.7 constant_dynamic-update-slice_fusion.26
  2.2 0.8 constant_dynamic-update-slice_fusion.25
  3.0 0.8 constant_dynamic-update-slice_fusion.24
  3.7 0.7 constant_dynamic-update-slice_fusion.23
  5.2 0.8 constant_dynamic-update-slice_fusion.21
  5.9 0.7 constant_dynamic-update-slice_fusion.19
  6.7 0.8 constant_dynamic-update-slice_fusion.18
  7.4 0.8 constant_dynamic-update-slice_fusion.17
  8.2 0.7 constant_dynamic-update-slice_fusion.16
  9.6 0.8 constant_dynamic-update-slice_fusion.14
  10.4 4.1 %collective-permute-start = (bf16[1,1,1,1,168,512]{5,4,3,2,1,0:T(8,128)(2,1)S(1)}, bf16[1,1,1,1,168,512]{5,4,3,2,1,0:T(8,128)(2,1)S(1)}, u32[]{:S(2)}, u32[]{:S(2)}) collective-permute-start(bf16[1,1,1,1,168,512]{5,4,3,2,1,0:T(8,128)(2,1)S(1)} %broadcast_select_fusion), channel_id=1, source_target_pairs={{0,8},{2,10},{4,12},{6,14},{8,0},{10,2},{12,4},{14,6},{1,9},{3,11}... | collective-permute-start | bytes 516104 | tf_op jit(solution)/shard_map/ppermute | solution.py:289
  14.5 1.3 collective-permute-start.20
  16.5 1.3 collective-permute-start.21
  17.8 0.8 constant_dynamic-update-slice_fusion.13
  19.3 0.7 constant_dynamic-update-slice_fusion.12
  20.0 0.8 constant_dynamic-update-slice_fusion.11
  21.5 2.3 %shard_map.119 = (f32[512,128]{1,0:T(8,128)}, f32[512,128]{1,0:T(8,128)}, f32[512,128]{1,0:T(8,128)}, f32[3,128]{1,0:T(4,128)}) custom-call(f32[512,128]{1,0:T(8,128)} %bitcast.103, f32[512,128]{1,0:T(8,128)} %bitcast.117), custom_call_target="tpu_custom_call" | custom-call | flops 2621440 | bytes 1312256 | tf_op jit(solution)/shard_map/pallas_call | solution.py:37
  24.5 2.7 %collective-permute-start.4 = (f32[3,128]{1,0:T(4,128)S(1)}, f32[3,128]{1,0:T(4,128)S(1)}, u32[]{:S(2)}, u32[]{:S(2)}) collective-permute-start(f32[3,128]{1,0:T(4,128)S(1)} %copy-done.16), channel_id=1, source_target_pairs={{0,2},{2,0},{4,6},{6,4},{8,10},{10,8},{12,14},{14,12},{1,3},{3,1},... | collective-permute-start | bytes 4616 | tf_op jit(solution)/shard_map/ppermute | solution.py:289
  27.2 0.9 fusion.valid_ref
  28.1 1.5 collective-permute-start.3
  29.6 3.6 %collective-permute-start.1 = (bf16[2,1,1,1,48,512]{5,4,3,2,1,0:T(8,128)(2,1)S(1)}, bf16[2,1,1,1,48,512]{5,4,3,2,1,0:T(8,128)(2,1)S(1)}, u32[]{:S(2)}, u32[]{:S(2)}) collective-permute-start(bf16[2,1,1,1,48,512]{5,4,3,2,1,0:T(8,128)(2,1)S(1)} %slice.353), channel_id=1, source_target_pairs={{0,4},{2,6},{4,0},{6,2},{8,12},{10,14},{12,8},{14,10},{1,5},{3,7},... | collective-permute-start | bytes 294920 | tf_op jit(solution)/shard_map/ppermute | solution.py:289
  33.2 2.6 %collective-permute-done.1 = bf16[2,1,1,1,48,512]{5,4,3,2,1,0:T(8,128)(2,1)S(1)} collective-permute-done((bf16[2,1,1,1,48,512]{5,4,3,2,1,0:T(8,128)(2,1)S(1)}, bf16[2,1,1,1,48,512]{5,4,3,2,1,0:T(8,128)(2,1)S(1)}, u32[]{:S(2)}, u32[]{:S(2)}) %collective-permute-start.1) | collective-permute-done | bytes 98336 | tf_op jit(solution)/shard_map/ppermute | solution.py:289
  35.9 2.1 %collective-permute-start.8 = (f32[3,128]{1,0:T(4,128)S(1)}, f32[3,128]{1,0:T(4,128)S(1)}, u32[]{:S(2)}, u32[]{:S(2)}) collective-permute-start(f32[3,128]{1,0:T(4,128)S(1)} %get-tuple-element.64), channel_id=1, source_target_pairs={{0,4},{2,6},{4,0},{6,2},{8,12},{10,14},{12,8},{14,10},{1,5},{3,7},... | collective-permute-start | bytes 4616 | tf_op jit(solution)/shard_map/ppermute | solution.py:289
  38.0 1.2 copy.25.label_ref
  39.9 1.1 collective-permute-start.5
  41.0 3.1 %collective-permute-start.9 = (f32[3,128]{1,0:T(4,128)S(1)}, f32[3,128]{1,0:T(4,128)S(1)}, u32[]{:S(2)}, u32[]{:S(2)}) collective-permute-start(f32[3,128]{1,0:T(4,128)S(1)} %fusion.5), channel_id=1, source_target_pairs={{0,8},{2,10},{4,12},{6,14},{8,0},{10,2},{12,4},{14,6},{1,9},{3,11}... | collective-permute-start | bytes 4616 | tf_op jit(solution)/shard_map/ppermute | solution.py:289
  44.1 1.6 collective-permute-done.9
  46.2 2.0 %shard_map.120 = bf16[512,128]{1,0:T(8,128)(2,1)} custom-call(f32[512,128]{1,0:T(8,128)} %bitcast.104, f32[512,128]{1,0:T(8,128)} %get-tuple-element.60.keep_ref, f32[512,128]{1,0:T(8,128)} %get-tuple-element.61.mass_ref, f32[512,128]{1,0:T(8,128)} %get-tuple-element.62.weight_ref, f32[3,128]{1,0:T(4,128)} %maximum_select_fusion.16.carry_ref), custom_call_target="tpu_custom_call" | custom-call | flops 655360 | bytes 1181184 | tf_op jit(solution)/shard_map/pallas_call | solution.py:37
  48.4 0.7 copy-done.2
  49.1 3.3 %collective-permute-start.14 = (bf16[512,128]{1,0:T(8,128)(2,1)S(1)}, bf16[512,128]{1,0:T(8,128)(2,1)S(1)}, u32[]{:S(2)}, u32[]{:S(2)}) collective-permute-start(bf16[512,128]{1,0:T(8,128)(2,1)S(1)} %copy-done.2), channel_id=1, source_target_pairs={{0,2},{2,4},{4,6},{6,8},{8,10},{10,12},{12,14},{1,3},{3,5},{5,7},{... | collective-permute-start | bytes 393224 | tf_op jit(solution)/shard_map/ppermute | solution.py:338
  52.5 1.3 collective-permute-start.15
  53.8 6.7 %collective-permute-start.13 = (bf16[256,128]{1,0:T(8,128)(2,1)S(1)}, bf16[256,128]{1,0:T(8,128)(2,1)S(1)}, u32[]{:S(2)}, u32[]{:S(2)}) collective-permute-start(bf16[256,128]{1,0:T(8,128)(2,1)S(1)} %get-tuple-element.120), channel_id=1, source_target_pairs={{0,4},{2,6},{4,8},{6,10},{8,12},{10,14},{1,5},{3,7},{5,9},{7,11},{... | collective-permute-start | bytes 196616 | tf_op jit(solution)/shard_map/ppermute | solution.py:338
  60.7 1.5 collective-permute-start.16
  62.2 0.8 collective-permute-done.13
  63.0 2.5 %collective-permute-start.11 = (bf16[2,1,2,2,32,512]{5,4,3,2,1,0:T(8,128)(2,1)S(1)}, bf16[2,1,2,2,32,512]{5,4,3,2,1,0:T(8,128)(2,1)S(1)}, u32[]{:S(2)}, u32[]{:S(2)}) collective-permute-start(bf16[2,1,2,2,32,512]{5,4,3,2,1,0:T(8,128)(2,1)S(1)} %get-tuple-element.98), channel_id=1, source_target_pairs={{0,4},{2,6},{4,0},{6,2},{8,12},{10,14},{12,8},{14,10},{1,5},{3,7},... | collective-permute-start | bytes 786440 | tf_op jit(solution)/shard_map/ppermute | solution.py:289
  65.5 0.7 collective-permute-start.10
  66.9 4.7 %collective-permute-done.11 = bf16[2,1,2,2,32,512]{5,4,3,2,1,0:T(8,128)(2,1)S(1)} collective-permute-done((bf16[2,1,2,2,32,512]{5,4,3,2,1,0:T(8,128)(2,1)S(1)}, bf16[2,1,2,2,32,512]{5,4,3,2,1,0:T(8,128)(2,1)S(1)}, u32[]{:S(2)}, u32[]{:S(2)}) %collective-permute-start.11) | collective-permute-done | bytes 262176 | tf_op jit(solution)/shard_map/ppermute | solution.py:289
  71.7 1.6 collective-permute-done.10
  73.4 1.1 collective-permute-start.26
  74.5 1.8 collective-permute-start.24
  77.4 3.8 %collective-permute-done.22 = bf16[2,2,2,1,16,512]{5,4,3,2,1,0:T(8,128)(2,1)S(1)} collective-permute-done((bf16[2,2,2,1,16,512]{5,4,3,2,1,0:T(8,128)(2,1)S(1)}, bf16[2,2,2,1,16,512]{5,4,3,2,1,0:T(8,128)(2,1)S(1)}, u32[]{:S(2)}, u32[]{:S(2)}) %collective-permute-start.22) | collective-permute-done | bytes 131104 | tf_op jit(solution)/shard_map/ppermute | solution.py:289
  83.4 0.7 reshape_squeeze.7.w_out_ref
  84.2 0.8 copy-done.17
  85.0 13.3 %shard_map.121 = (bf16[2048,512]{1,0:T(8,128)(2,1)}, bf16[1792,512]{1,0:T(8,128)(2,1)}, f32[768,512]{1,0:T(8,128)}, f32[768,512]{1,0:T(8,128)}, bf16[16,64,512]{...) custom-call(s32[1]{0:T(128)} %bitcast.site_ref, bf16[2048,128]{1,0:T(8,128)(2,1)} %copy-done.5, ...), custom_call_target="tpu_custom_call" | custom-call | flops 5637144576 | bytes 13238276 | tf_op jit(solution)/shard_map/pallas_call | solution.py:37
  98.4 16.1 %shard_map.122 = (f32[1280,1]{1,0:T(8,128)}, bf16[8,168,512]{2,1,0:T(8,128)(2,1)}, bf16[8,168,512]{2,1,0:T(8,128)(2,1)}, bf16[1280,1024]{1,0:T(8,128)(2,1)}, f32...) custom-call(s32[1]{0:T(128)} %bitcast.site_ref, ...), custom_call_target="tpu_custom_call" | custom-call | flops 5368709120 | bytes 14695428 | tf_op jit(solution)/shard_map/pallas_call | solution.py:37
  114.6 9.0 %shard_map.123 = (f32[768,512]{1,0:T(8,128)}, bf16[768,512]{1,0:T(8,128)(2,1)}, bf16[768,1024]{1,0:T(8,128)(2,1)}) custom-call(bf16[1280,1024]{1,0:T(8,128)(2,1)} %get-tuple-element.80.back1_ref, f32[1280,512]{1,0:T(8,128)} %get-tuple-element.81.grad2_ref, bf16[16,64,512]{2,1,0:T(8,128)(2,1)} %get-tuple-element.82.filt1_ref, ...), custom_call_target="tpu_custom_call" | custom-call | flops 2013265920 | bytes 14942208 | tf_op jit(solution)/shard_map/pallas_call | solution.py:37
  125.5 9.5 %shard_map.124 = (bf16[8,168,512]{2,1,0:T(8,128)(2,1)}, bf16[8,168,512]{2,1,0:T(8,128)(2,1)}) custom-call(s32[1]{0:T(128)} %bitcast.site_ref, bf16[768,1024]{1,0:T(8,128)(2,1)} %get-tuple-element.88.back_ref, f32[768,512]{1,0:T(8,128)} %get-tuple-element.89.grad_ref, bf16[768,512]{1,0:T(8,128)(2,1)} %get-tuple-element.90.round_ref, ...), custom_call_target="tpu_custom_call" | custom-call | flops 2415919104 | bytes 14548996 | tf_op jit(solution)/shard_map/pallas_call | solution.py:37
  135.1 1.4 collective-permute-start.36
  136.7 1.5 collective-permute-start.38
  138.2 3.6 %collective-permute-done.36 = bf16[2,1,1,80,512]{4,3,2,1,0:T(8,128)(2,1)S(1)} collective-permute-done((bf16[2,1,1,80,512]{4,3,2,1,0:T(8,128)(2,1)S(1)}, bf16[2,1,1,80,512]{4,3,2,1,0:T(8,128)(2,1)S(1)}, u32[]{:S(2)}, u32[]{:S(2)}) %collective-permute-start.36) | collective-permute-done | bytes 163872 | tf_op jit(solution)/shard_map/ppermute | solution.py:289
  141.9 1.6 collective-permute-done.38
  143.6 1.6 collective-permute-start.39
  145.2 1.7 slice_reduce_fusion
  146.8 7.0 %collective-permute-done.39 = bf16[1,1,1,168,512]{4,3,2,1,0:T(8,128)(2,1)S(1)} collective-permute-done((bf16[1,1,1,168,512]{4,3,2,1,0:T(8,128)(2,1)S(1)}, bf16[1,1,1,168,512]{4,3,2,1,0:T(8,128)(2,1)S(1)}, u32[]{:S(2)}, u32[]{:S(2)}) %collective-permute-start.39) | collective-permute-done | bytes 172064 | tf_op jit(solution)/shard_map/ppermute | solution.py:289
  154.7 0.7 collective-permute-start.32
  155.4 7.9 %collective-permute-done.30 = bf16[2,1,2,80,512]{4,3,2,1,0:T(8,128)(2,1)S(1)} collective-permute-done((bf16[2,1,2,80,512]{4,3,2,1,0:T(8,128)(2,1)S(1)}, bf16[2,1,2,80,512]{4,3,2,1,0:T(8,128)(2,1)S(1)}, u32[]{:S(2)}, u32[]{:S(2)}) %collective-permute-start.30) | collective-permute-done | bytes 327712 | tf_op jit(solution)/shard_map/ppermute | solution.py:289
  163.4 0.9 collective-permute-start.31
  164.5 2.7 %collective-permute-start.33 = (bf16[2,1,1,88,512]{4,3,2,1,0:T(8,128)(2,1)S(1)}, bf16[2,1,1,88,512]{4,3,2,1,0:T(8,128)(2,1)S(1)}, u32[]{:S(2)}, u32[]{:S(2)}) collective-permute-start(bf16[2,1,1,88,512]{4,3,2,1,0:T(8,128)(2,1)S(1)} %constant_dynamic-slice_fusion.4), channel_id=1, source_target_pairs={{0,4},{2,6},{4,0},{6,2},{8,12},{10,14},{12,8},{14,10},{1,5},{3,7},... | collective-permute-start | bytes 540680 | tf_op jit(solution)/shard_map/ppermute | solution.py:289
  167.1 1.7 collective-permute-done.31
  168.8 1.8 collective-permute-done.33
  170.7 2.0 %collective-permute-start.34 = (bf16[1,1,1,168,512]{4,3,2,1,0:T(8,128)(2,1)S(1)}, bf16[1,1,1,168,512]{4,3,2,1,0:T(8,128)(2,1)S(1)}, u32[]{:S(2)}, u32[]{:S(2)}) collective-permute-start(bf16[1,1,1,168,512]{4,3,2,1,0:T(8,128)(2,1)S(1)} %fusion.3), channel_id=1, source_target_pairs={{0,8},{2,10},{4,12},{6,14},{8,0},{10,2},{12,4},{14,6},{1,9},{3,11}... | collective-permute-start | bytes 516104 | tf_op jit(solution)/shard_map/ppermute | solution.py:289
  173.3 5.6 %collective-permute-done.34 = bf16[1,1,1,168,512]{4,3,2,1,0:T(8,128)(2,1)S(1)} collective-permute-done((bf16[1,1,1,168,512]{4,3,2,1,0:T(8,128)(2,1)S(1)}, bf16[1,1,1,168,512]{4,3,2,1,0:T(8,128)(2,1)S(1)}, u32[]{:S(2)}, u32[]{:S(2)}) %collective-permute-start.34) | collective-permute-done | bytes 172064 | tf_op jit(solution)/shard_map/ppermute | solution.py:289
  180.3 0.8 pad_maximum_fusion
  (172 shorter events, 14.9 us)
Async XLA Ops:
  0.6 20.1 %copy-start.3 = (bf16[2,64,1024]{2,1,0:T(8,128)(2,1)S(1)}, bf16[2,64,1024]{2,1,0:T(8,128)(2,1)}, u32[]{:S(2)}) copy-start(bf16[2,64,1024]{2,1,0:T(8,128)(2,1)} %param.12) | copy-start | bytes 786436
  0.6 20.1 %copy-start.11 = (bf16[2,32,512]{2,1,0:T(8,128)(2,1)S(1)}, bf16[2,32,512]{2,1,0:T(8,128)(2,1)}, u32[]{:S(2)}) copy-start(bf16[2,32,512]{2,1,0:T(8,128)(2,1)} %param.13) | copy-start | bytes 196612
  0.7 20.2 %copy-start.13 = (bf16[8,512]{1,0:T(8,128)(2,1)S(1)}, bf16[8,512]{1,0:T(8,128)(2,1)}, u32[]{:S(2)}) copy-start(bf16[8,512]{1,0:T(8,128)(2,1)} %param.14) | copy-start | bytes 24580
  10.4 13.5 %collective-permute-start = (bf16[1,1,1,1,168,512]{5,4,3,2,1,0:T(8,128)(2,1)S(1)}, bf16[1,1,1,1,168,512]{5,4,3,2,1,0:T(8,128)(2,1)S(1)}, u32[]{:S(2)}, u32[]{:S(2)}) collective-permute-start(bf16[1,1,1,1,168,512]{5,4,3,2,1,0:T(8,128)(2,1)S(1)} %broadcast_select_fusion), channel_id=1, source_target_pairs={{0,8},{2,10},{4,12},{6,14},{8,0},{10,2},{12,4},{14,6},{1,9},{3,11}... | collective-permute-start | bytes 516104 | tf_op jit(solution)/shard_map/ppermute | solution.py:289
  14.5 23.5 %collective-permute-start.20 = (s32[512,1]{0,1:T(1,128)}, s32[512,1]{0,1:T(1,128)S(1)}, u32[]{:S(2)}, u32[]{:S(2)}) collective-permute-start(s32[512,1]{0,1:T(1,128)} %bitcast.120), channel_id=1, source_target_pairs={{2,0},{4,2},{6,4},{8,6},{10,8},{12,10},{14,12},{3,1},{5,3},{7,5},{... | collective-permute-start | bytes 6152 | tf_op jit(solution)/shard_map/ppermute | solution.py:338
  16.5 21.5 %collective-permute-start.21 = (s32[256,1]{0,1:T(1,128)S(1)}, s32[256,1]{0,1:T(1,128)S(1)}, u32[]{:S(2)}, u32[]{:S(2)}) collective-permute-start(s32[256,1]{0,1:T(1,128)S(1)} %slice_bitcast_fusion.12), channel_id=1, source_target_pairs={{4,0},{6,2},{8,4},{10,6},{12,8},{14,10},{5,1},{7,3},{9,5},{11,7},{... | collective-permute-start | bytes 3080 | tf_op jit(solution)/shard_map/ppermute | solution.py:338
  21.5 11.7 %copy-start.14 = (f32[3,128]{1,0:T(4,128)S(1)}, f32[3,128]{1,0:T(4,128)}, u32[]{:S(2)}) copy-start(f32[3,128]{1,0:T(4,128)} %constant.73.clone.1) | copy-start | bytes 4612
  23.8 0.7 copy-start.16
  23.9 14.1 %copy-start.15 = (s32[1,512]{1,0:T(1,128)S(1)}, s32[1,512]{1,0:T(1,128)}, u32[]{:S(2)}) copy-start(s32[1,512]{1,0:T(1,128)} %param.10) | copy-start | bytes 6148
  24.5 5.1 %collective-permute-start.4 = (f32[3,128]{1,0:T(4,128)S(1)}, f32[3,128]{1,0:T(4,128)S(1)}, u32[]{:S(2)}, u32[]{:S(2)}) collective-permute-start(f32[3,128]{1,0:T(4,128)S(1)} %copy-done.16), channel_id=1, source_target_pairs={{0,2},{2,0},{4,6},{6,4},{8,10},{10,8},{12,14},{14,12},{1,3},{3,1},... | collective-permute-start | bytes 4616 | tf_op jit(solution)/shard_map/ppermute | solution.py:289
  28.1 7.7 %collective-permute-start.3 = (bf16[2,1,1,1,56,512]{5,4,3,2,1,0:T(8,128)(2,1)S(1)}, bf16[2,1,1,1,56,512]{5,4,3,2,1,0:T(8,128)(2,1)S(1)}, u32[]{:S(2)}, u32[]{:S(2)}) collective-permute-start(bf16[2,1,1,1,56,512]{5,4,3,2,1,0:T(8,128)(2,1)S(1)} %slice.355), channel_id=1, source_target_pairs={{0,16},{16,0},{1,17},{17,1},{2,18},{18,2},{3,19},{19,3},{4,20},{20... | collective-permute-start | bytes 344072 | tf_op jit(solution)/shard_map/ppermute | solution.py:289
  29.6 6.3 %collective-permute-start.2 = (bf16[2,1,1,1,64,512]{5,4,3,2,1,0:T(8,128)(2,1)S(1)}, bf16[2,1,1,1,64,512]{5,4,3,2,1,0:T(8,128)(2,1)S(1)}, u32[]{:S(2)}, u32[]{:S(2)}) collective-permute-start(bf16[2,1,1,1,64,512]{5,4,3,2,1,0:T(8,128)(2,1)S(1)} %slice.354), channel_id=1, source_target_pairs={{0,2},{2,0},{4,6},{6,4},{8,10},{10,8},{12,14},{14,12},{1,3},{3,1},... | collective-permute-start | bytes 393224 | tf_op jit(solution)/shard_map/ppermute | solution.py:289
  29.6 6.2 %collective-permute-start.1 = (bf16[2,1,1,1,48,512]{5,4,3,2,1,0:T(8,128)(2,1)S(1)}, bf16[2,1,1,1,48,512]{5,4,3,2,1,0:T(8,128)(2,1)S(1)}, u32[]{:S(2)}, u32[]{:S(2)}) collective-permute-start(bf16[2,1,1,1,48,512]{5,4,3,2,1,0:T(8,128)(2,1)S(1)} %slice.353), channel_id=1, source_target_pairs={{0,4},{2,6},{4,0},{6,2},{8,12},{10,14},{12,8},{14,10},{1,5},{3,7},... | collective-permute-start | bytes 294920 | tf_op jit(solution)/shard_map/ppermute | solution.py:289
  35.9 5.0 %collective-permute-start.8 = (f32[3,128]{1,0:T(4,128)S(1)}, f32[3,128]{1,0:T(4,128)S(1)}, u32[]{:S(2)}, u32[]{:S(2)}) collective-permute-start(f32[3,128]{1,0:T(4,128)S(1)} %get-tuple-element.64), channel_id=1, source_target_pairs={{0,4},{2,6},{4,0},{6,2},{8,12},{10,14},{12,8},{14,10},{1,5},{3,7},... | collective-permute-start | bytes 4616 | tf_op jit(solution)/shard_map/ppermute | solution.py:289
  39.2 9.1 %collective-permute-start.7 = (bf16[2,1,1,2,56,512]{5,4,3,2,1,0:T(8,128)(2,1)S(1)}, bf16[2,1,1,2,56,512]{5,4,3,2,1,0:T(8,128)(2,1)S(1)}, u32[]{:S(2)}, u32[]{:S(2)}) collective-permute-start(bf16[2,1,1,2,56,512]{5,4,3,2,1,0:T(8,128)(2,1)S(1)} %maximum_select_fusion.12), channel_id=1, source_target_pairs={{0,4},{2,6},{4,0},{6,2},{8,12},{10,14},{12,8},{14,10},{1,5},{3,7},... | collective-permute-start | bytes 688136 | tf_op jit(solution)/shard_map/ppermute | solution.py:289
  39.2 9.1 %collective-permute-start.6 = (bf16[2,1,2,1,64,512]{5,4,3,2,1,0:T(8,128)(2,1)S(1)}, bf16[2,1,2,1,64,512]{5,4,3,2,1,0:T(8,128)(2,1)S(1)}, u32[]{:S(2)}, u32[]{:S(2)}) collective-permute-start(bf16[2,1,2,1,64,512]{5,4,3,2,1,0:T(8,128)(2,1)S(1)} %maximum_select_fusion.9), channel_id=1, source_target_pairs={{0,16},{16,0},{1,17},{17,1},{2,18},{18,2},{3,19},{19,3},{4,20},{20... | collective-permute-start | bytes 786440 | tf_op jit(solution)/shard_map/ppermute | solution.py:289
  39.9 8.3 %collective-permute-start.5 = (bf16[2,2,1,1,48,512]{5,4,3,2,1,0:T(8,128)(2,1)S(1)}, bf16[2,2,1,1,48,512]{5,4,3,2,1,0:T(8,128)(2,1)S(1)}, u32[]{:S(2)}, u32[]{:S(2)}) collective-permute-start(bf16[2,2,1,1,48,512]{5,4,3,2,1,0:T(8,128)(2,1)S(1)} %maximum_select_fusion.13), channel_id=1, source_target_pairs={{0,2},{2,0},{4,6},{6,4},{8,10},{10,8},{12,14},{14,12},{1,3},{3,1},... | collective-permute-start | bytes 589832 | tf_op jit(solution)/shard_map/ppermute | solution.py:289
  41.0 4.6 %collective-permute-start.9 = (f32[3,128]{1,0:T(4,128)S(1)}, f32[3,128]{1,0:T(4,128)S(1)}, u32[]{:S(2)}, u32[]{:S(2)}) collective-permute-start(f32[3,128]{1,0:T(4,128)S(1)} %fusion.5), channel_id=1, source_target_pairs={{0,8},{2,10},{4,12},{6,14},{8,0},{10,2},{12,4},{14,6},{1,9},{3,11}... | collective-permute-start | bytes 4616 | tf_op jit(solution)/shard_map/ppermute | solution.py:289
  48.2 0.9 copy-start.2
  49.1 16.3 %collective-permute-start.14 = (bf16[512,128]{1,0:T(8,128)(2,1)S(1)}, bf16[512,128]{1,0:T(8,128)(2,1)S(1)}, u32[]{:S(2)}, u32[]{:S(2)}) collective-permute-start(bf16[512,128]{1,0:T(8,128)(2,1)S(1)} %copy-done.2), channel_id=1, source_target_pairs={{0,2},{2,4},{4,6},{6,8},{8,10},{10,12},{12,14},{1,3},{3,5},{5,7},{... | collective-permute-start | bytes 393224 | tf_op jit(solution)/shard_map/ppermute | solution.py:338
  52.5 13.8 %collective-permute-start.15 = (bf16[512,128]{1,0:T(8,128)(2,1)S(1)}, bf16[512,128]{1,0:T(8,128)(2,1)S(1)}, u32[]{:S(2)}, u32[]{:S(2)}) collective-permute-start(bf16[512,128]{1,0:T(8,128)(2,1)S(1)} %copy-done.2), channel_id=1, source_target_pairs={{2,0},{4,2},{6,4},{8,6},{10,8},{12,10},{14,12},{3,1},{5,3},{7,5},{... | collective-permute-start | bytes 393224 | tf_op jit(solution)/shard_map/ppermute | solution.py:338
  53.8 9.2 %collective-permute-start.13 = (bf16[256,128]{1,0:T(8,128)(2,1)S(1)}, bf16[256,128]{1,0:T(8,128)(2,1)S(1)}, u32[]{:S(2)}, u32[]{:S(2)}) collective-permute-start(bf16[256,128]{1,0:T(8,128)(2,1)S(1)} %get-tuple-element.120), channel_id=1, source_target_pairs={{0,4},{2,6},{4,8},{6,10},{8,12},{10,14},{1,5},{3,7},{5,9},{7,11},{... | collective-permute-start | bytes 196616 | tf_op jit(solution)/shard_map/ppermute | solution.py:338
  60.5 6.4 %collective-permute-start.12 = (bf16[2,2,1,2,24,512]{5,4,3,2,1,0:T(8,128)(2,1)S(1)}, bf16[2,2,1,2,24,512]{5,4,3,2,1,0:T(8,128)(2,1)S(1)}, u32[]{:S(2)}, u32[]{:S(2)}) collective-permute-start(bf16[2,2,1,2,24,512]{5,4,3,2,1,0:T(8,128)(2,1)S(1)} %slice.312), channel_id=1, source_target_pairs={{0,2},{2,0},{4,6},{6,4},{8,10},{10,8},{12,14},{14,12},{1,3},{3,1},... | collective-permute-start | bytes 589832 | tf_op jit(solution)/shard_map/ppermute | solution.py:289
  60.7 6.2 %collective-permute-start.16 = (bf16[256,128]{1,0:T(8,128)(2,1)S(1)}, bf16[256,128]{1,0:T(8,128)(2,1)S(1)}, u32[]{:S(2)}, u32[]{:S(2)}) collective-permute-start(bf16[256,128]{1,0:T(8,128)(2,1)S(1)} %get-tuple-element.119), channel_id=1, source_target_pairs={{4,0},{6,2},{8,4},{10,6},{12,8},{14,10},{5,1},{7,3},{9,5},{11,7},{... | collective-permute-start | bytes 196616 | tf_op jit(solution)/shard_map/ppermute | solution.py:338
  63.0 8.7 %collective-permute-start.11 = (bf16[2,1,2,2,32,512]{5,4,3,2,1,0:T(8,128)(2,1)S(1)}, bf16[2,1,2,2,32,512]{5,4,3,2,1,0:T(8,128)(2,1)S(1)}, u32[]{:S(2)}, u32[]{:S(2)}) collective-permute-start(bf16[2,1,2,2,32,512]{5,4,3,2,1,0:T(8,128)(2,1)S(1)} %get-tuple-element.98), channel_id=1, source_target_pairs={{0,4},{2,6},{4,0},{6,2},{8,12},{10,14},{12,8},{14,10},{1,5},{3,7},... | collective-permute-start | bytes 786440 | tf_op jit(solution)/shard_map/ppermute | solution.py:289
  65.5 7.8 %collective-permute-start.10 = (bf16[2,2,2,1,32,512]{5,4,3,2,1,0:T(8,128)(2,1)S(1)}, bf16[2,2,2,1,32,512]{5,4,3,2,1,0:T(8,128)(2,1)S(1)}, u32[]{:S(2)}, u32[]{:S(2)}) collective-permute-start(bf16[2,2,2,1,32,512]{5,4,3,2,1,0:T(8,128)(2,1)S(1)} %slice.310), channel_id=1, source_target_pairs={{0,16},{16,0},{1,17},{17,1},{2,18},{18,2},{3,19},{19,3},{4,20},{20... | collective-permute-start | bytes 786440 | tf_op jit(solution)/shard_map/ppermute | solution.py:289
  66.8 10.0 %copy-start.5 = (bf16[2048,128]{1,0:T(8,128)(2,1)}, bf16[2048,128]{1,0:T(8,128)(2,1)S(1)}, u32[]{:S(2)}) copy-start(bf16[2048,128]{1,0:T(8,128)(2,1)S(1)} %constant_dynamic-update-slice_fusion.28.norm_ref) | copy-start | bytes 1572868
  66.9 15.0 %copy-start.4 = (bf16[2,2,2,2,24,512]{5,4,3,2,1,0:T(8,128)(2,1)}, bf16[2,2,2,2,24,512]{5,4,3,2,1,0:T(8,128)(2,1)S(1)}, u32[]{:S(2)}) copy-start(bf16[2,2,2,2,24,512]{5,4,3,2,1,0:T(8,128)(2,1)S(1)} %maximum_select_fusion.7) | copy-start | bytes 1179652
  71.7 10.3 %copy-start.6 = (bf16[2,2,2,2,32,512]{5,4,3,2,1,0:T(8,128)(2,1)}, bf16[2,2,2,2,32,512]{5,4,3,2,1,0:T(8,128)(2,1)S(1)}, u32[]{:S(2)}) copy-start(bf16[2,2,2,2,32,512]{5,4,3,2,1,0:T(8,128)(2,1)S(1)} %maximum_select_fusion.2) | copy-start | bytes 1572868
  73.4 9.3 %copy-start.7 = (bf16[2,2,2,2,32,512]{5,4,3,2,1,0:T(8,128)(2,1)}, bf16[2,2,2,2,32,512]{5,4,3,2,1,0:T(8,128)(2,1)S(1)}, u32[]{:S(2)}) copy-start(bf16[2,2,2,2,32,512]{5,4,3,2,1,0:T(8,128)(2,1)S(1)} %maximum_select_fusion.1) | copy-start | bytes 1572868
  73.4 7.9 %collective-permute-start.26 = (bf16[2,2,1,2,32,512]{5,4,3,2,1,0:T(8,128)(2,1)S(1)}, bf16[2,2,1,2,32,512]{5,4,3,2,1,0:T(8,128)(2,1)S(1)}, u32[]{:S(2)}, u32[]{:S(2)}) collective-permute-start(bf16[2,2,1,2,32,512]{5,4,3,2,1,0:T(8,128)(2,1)S(1)} %slice.315), channel_id=1, source_target_pairs={{0,2},{2,0},{4,6},{6,4},{8,10},{10,8},{12,14},{14,12},{1,3},{3,1},... | collective-permute-start | bytes 786440 | tf_op jit(solution)/shard_map/ppermute | solution.py:289
  74.5 7.4 %collective-permute-start.24 = (bf16[2,1,2,2,32,512]{5,4,3,2,1,0:T(8,128)(2,1)S(1)}, bf16[2,1,2,2,32,512]{5,4,3,2,1,0:T(8,128)(2,1)S(1)}, u32[]{:S(2)}, u32[]{:S(2)}) collective-permute-start(bf16[2,1,2,2,32,512]{5,4,3,2,1,0:T(8,128)(2,1)S(1)} %get-tuple-element.75), channel_id=1, source_target_pairs={{0,4},{2,6},{4,0},{6,2},{8,12},{10,14},{12,8},{14,10},{1,5},{3,7},... | collective-permute-start | bytes 786440 | tf_op jit(solution)/shard_map/ppermute | solution.py:289
  76.2 5.0 %collective-permute-start.22 = (bf16[2,2,2,1,16,512]{5,4,3,2,1,0:T(8,128)(2,1)S(1)}, bf16[2,2,2,1,16,512]{5,4,3,2,1,0:T(8,128)(2,1)S(1)}, u32[]{:S(2)}, u32[]{:S(2)}) collective-permute-start(bf16[2,2,2,1,16,512]{5,4,3,2,1,0:T(8,128)(2,1)S(1)} %slice.313), channel_id=1, source_target_pairs={{0,16},{16,0},{1,17},{17,1},{2,18},{18,2},{3,19},{19,3},{4,20},{20... | collective-permute-start | bytes 393224 | tf_op jit(solution)/shard_map/ppermute | solution.py:289
  76.8 5.2 %collective-permute-start.17 = (bf16[8,2,24,512]{3,2,1,0:T(8,128)(2,1)S(1)}, bf16[8,2,24,512]{3,2,1,0:T(8,128)(2,1)S(1)}, u32[]{:S(2)}, u32[]{:S(2)}) collective-permute-start(bf16[8,2,24,512]{3,2,1,0:T(8,128)(2,1)S(1)} %bitcast.105), channel_id=1, source_target_pairs={{0,1},{1,0},{2,3},{3,2},{4,5},{5,4},{6,7},{7,6},{8,9},{9,8},{10,11... | collective-permute-start | bytes 1179656 | tf_op jit(solution)/shard_map/ppermute | solution.py:289
  76.9 7.3 %collective-permute-start.18 = (bf16[8,2,32,512]{3,2,1,0:T(8,128)(2,1)S(1)}, bf16[8,2,32,512]{3,2,1,0:T(8,128)(2,1)S(1)}, u32[]{:S(2)}, u32[]{:S(2)}) collective-permute-start(bf16[8,2,32,512]{3,2,1,0:T(8,128)(2,1)S(1)} %bitcast.111), channel_id=1, source_target_pairs={{0,1},{1,0},{2,3},{3,2},{4,5},{5,4},{6,7},{7,6},{8,9},{9,8},{10,11... | collective-permute-start | bytes 1572872 | tf_op jit(solution)/shard_map/ppermute | solution.py:289
  81.2 3.0 %collective-permute-start.19 = (bf16[8,2,32,512]{3,2,1,0:T(8,128)(2,1)S(1)}, bf16[8,2,32,512]{3,2,1,0:T(8,128)(2,1)}, u32[]{:S(2)}, u32[]{:S(2)}) collective-permute-start(bf16[8,2,32,512]{3,2,1,0:T(8,128)(2,1)S(1)} %bitcast.109), channel_id=1, source_target_pairs={{0,1},{1,0},{2,3},{3,2},{4,5},{5,4},{6,7},{7,6},{8,9},{9,8},{10,11... | collective-permute-start | bytes 1572872 | tf_op jit(solution)/shard_map/ppermute | solution.py:289
  81.2 1.5 copy-start.10
  81.3 17.1 %collective-permute-start.23 = (bf16[8,2,16,512]{3,2,1,0:T(8,128)(2,1)S(1)}, bf16[8,2,16,512]{3,2,1,0:T(8,128)(2,1)}, u32[]{:S(2)}, u32[]{:S(2)}) collective-permute-start(bf16[8,2,16,512]{3,2,1,0:T(8,128)(2,1)S(1)} %maximum_select_fusion.11.a_ref), channel_id=1, source_target_pairs={{0,1},{1,0},{2,3},{3,2},{4,5},{5,4},{6,7},{7,6},{8,9},{9,8},{10,11... | collective-permute-start | bytes 786440 | tf_op jit(solution)/shard_map/ppermute | solution.py:289
  81.9 2.3 %copy-start.8 = (bf16[2,2,2,2,32,512]{5,4,3,2,1,0:T(8,128)(2,1)}, bf16[2,2,2,2,32,512]{5,4,3,2,1,0:T(8,128)(2,1)S(1)}, u32[]{:S(2)}) copy-start(bf16[2,2,2,2,32,512]{5,4,3,2,1,0:T(8,128)(2,1)S(1)} %maximum_select_fusion.4) | copy-start | bytes 1572868
  81.9 16.4 %collective-permute-start.27 = (bf16[8,2,32,512]{3,2,1,0:T(8,128)(2,1)S(1)}, bf16[8,2,32,512]{3,2,1,0:T(8,128)(2,1)}, u32[]{:S(2)}, u32[]{:S(2)}) collective-permute-start(bf16[8,2,32,512]{3,2,1,0:T(8,128)(2,1)S(1)} %bitcast.113), channel_id=1, source_target_pairs={{0,1},{1,0},{2,3},{3,2},{4,5},{5,4},{6,7},{7,6},{8,9},{9,8},{10,11... | collective-permute-start | bytes 1572872 | tf_op jit(solution)/shard_map/ppermute | solution.py:289
  82.1 16.3 %copy-start.9 = (bf16[2,2,2,2,32,512]{5,4,3,2,1,0:T(8,128)(2,1)}, bf16[2,2,2,2,32,512]{5,4,3,2,1,0:T(8,128)(2,1)S(1)}, u32[]{:S(2)}) copy-start(bf16[2,2,2,2,32,512]{5,4,3,2,1,0:T(8,128)(2,1)S(1)} %maximum_select_fusion.3) | copy-start | bytes 1572868
  82.1 2.1 %copy-start.12 = (bf16[8,2,24,512]{3,2,1,0:T(8,128)(2,1)}, bf16[8,2,24,512]{3,2,1,0:T(8,128)(2,1)S(1)}, u32[]{:S(2)}) copy-start(bf16[8,2,24,512]{3,2,1,0:T(8,128)(2,1)S(1)} %collective-permute-done.17.c2_ref) | copy-start | bytes 1179652
  82.1 16.2 %collective-permute-start.25 = (bf16[8,2,32,512]{3,2,1,0:T(8,128)(2,1)S(1)}, bf16[8,2,32,512]{3,2,1,0:T(8,128)(2,1)}, u32[]{:S(2)}, u32[]{:S(2)}) collective-permute-start(bf16[8,2,32,512]{3,2,1,0:T(8,128)(2,1)S(1)} %bitcast.115), channel_id=1, source_target_pairs={{0,1},{1,0},{2,3},{3,2},{4,5},{5,4},{6,7},{7,6},{8,9},{9,8},{10,11... | collective-permute-start | bytes 1572872 | tf_op jit(solution)/shard_map/ppermute | solution.py:289
  84.2 0.8 copy-start.17
  114.4 9.1 %collective-permute-start.28 = (bf16[8,168,512]{2,1,0:T(8,128)(2,1)}, bf16[8,168,512]{2,1,0:T(8,128)(2,1)S(1)}, u32[]{:S(2)}, u32[]{:S(2)}) collective-permute-start(bf16[8,168,512]{2,1,0:T(8,128)(2,1)} %get-tuple-element.79), channel_id=1, source_target_pairs={{0,1},{1,0},{2,3},{3,2},{4,5},{5,4},{6,7},{7,6},{8,9},{9,8},{10,11... | collective-permute-start | bytes 4128776 | tf_op jit(solution)/shard_map/ppermute | solution.py:289
  114.6 9.0 %copy-start.1 = (bf16[8,168,512]{2,1,0:T(8,128)(2,1)S(1)}, bf16[8,168,512]{2,1,0:T(8,128)(2,1)}, u32[]{:S(2)}) copy-start(bf16[8,168,512]{2,1,0:T(8,128)(2,1)} %get-tuple-element.78) | copy-start | bytes 4128772
  124.1 10.9 %collective-permute-start.35 = (bf16[2,1,2,80,512]{4,3,2,1,0:T(8,128)(2,1)S(1)}, bf16[2,1,2,80,512]{4,3,2,1,0:T(8,128)(2,1)S(1)}, u32[]{:S(2)}, u32[]{:S(2)}) collective-permute-start(bf16[2,1,2,80,512]{4,3,2,1,0:T(8,128)(2,1)S(1)} %constant_dynamic-slice_fusion.3), channel_id=1, source_target_pairs={{0,4},{2,6},{4,0},{6,2},{8,12},{10,14},{12,8},{14,10},{1,5},{3,7},... | collective-permute-start | bytes 983048 | tf_op jit(solution)/shard_map/ppermute | solution.py:289
  124.8 11.7 %collective-permute-start.37 = (bf16[2,2,1,88,512]{4,3,2,1,0:T(8,128)(2,1)S(1)}, bf16[2,2,1,88,512]{4,3,2,1,0:T(8,128)(2,1)S(1)}, u32[]{:S(2)}, u32[]{:S(2)}) collective-permute-start(bf16[2,2,1,88,512]{4,3,2,1,0:T(8,128)(2,1)S(1)} %constant_dynamic-slice_fusion.1), channel_id=1, source_target_pairs={{0,2},{2,0},{4,6},{6,4},{8,10},{10,8},{12,14},{14,12},{1,3},{3,1},... | collective-permute-start | bytes 1081352 | tf_op jit(solution)/shard_map/ppermute | solution.py:289
  135.0 19.0 %collective-permute-start.29 = (bf16[8,168,512]{2,1,0:T(8,128)(2,1)}, bf16[8,168,512]{2,1,0:T(8,128)(2,1)S(1)}, u32[]{:S(2)}, u32[]{:S(2)}) collective-permute-start(bf16[8,168,512]{2,1,0:T(8,128)(2,1)} %get-tuple-element.95), channel_id=1, source_target_pairs={{0,1},{1,0},{2,3},{3,2},{4,5},{5,4},{6,7},{7,6},{8,9},{9,8},{10,11... | collective-permute-start | bytes 4128776 | tf_op jit(solution)/shard_map/ppermute | solution.py:289
  135.1 6.7 %collective-permute-start.36 = (bf16[2,1,1,80,512]{4,3,2,1,0:T(8,128)(2,1)S(1)}, bf16[2,1,1,80,512]{4,3,2,1,0:T(8,128)(2,1)S(1)}, u32[]{:S(2)}, u32[]{:S(2)}) collective-permute-start(bf16[2,1,1,80,512]{4,3,2,1,0:T(8,128)(2,1)S(1)} %constant_dynamic-slice_fusion.2), channel_id=1, source_target_pairs={{0,2},{2,0},{4,6},{6,4},{8,10},{10,8},{12,14},{14,12},{1,3},{3,1},... | collective-permute-start | bytes 491528 | tf_op jit(solution)/shard_map/ppermute | solution.py:289
  136.7 17.3 %copy-start = (bf16[8,168,512]{2,1,0:T(8,128)(2,1)S(1)}, bf16[8,168,512]{2,1,0:T(8,128)(2,1)}, u32[]{:S(2)}) copy-start(bf16[8,168,512]{2,1,0:T(8,128)(2,1)} %get-tuple-element.94) | copy-start | bytes 4128772
  136.7 6.7 %collective-permute-start.38 = (bf16[2,1,1,88,512]{4,3,2,1,0:T(8,128)(2,1)S(1)}, bf16[2,1,1,88,512]{4,3,2,1,0:T(8,128)(2,1)S(1)}, u32[]{:S(2)}, u32[]{:S(2)}) collective-permute-start(bf16[2,1,1,88,512]{4,3,2,1,0:T(8,128)(2,1)S(1)} %constant_dynamic-slice_fusion), channel_id=1, source_target_pairs={{0,4},{2,6},{4,0},{6,2},{8,12},{10,14},{12,8},{14,10},{1,5},{3,7},... | collective-permute-start | bytes 540680 | tf_op jit(solution)/shard_map/ppermute | solution.py:289
  143.6 10.3 %collective-permute-start.39 = (bf16[1,1,1,168,512]{4,3,2,1,0:T(8,128)(2,1)S(1)}, bf16[1,1,1,168,512]{4,3,2,1,0:T(8,128)(2,1)S(1)}, u32[]{:S(2)}, u32[]{:S(2)}) collective-permute-start(bf16[1,1,1,168,512]{4,3,2,1,0:T(8,128)(2,1)S(1)} %fusion.1), channel_id=1, source_target_pairs={{0,8},{2,10},{4,12},{6,14},{8,0},{10,2},{12,4},{14,6},{1,9},{3,11}... | collective-permute-start | bytes 516104 | tf_op jit(solution)/shard_map/ppermute | solution.py:289
  154.5 8.8 %collective-permute-start.30 = (bf16[2,1,2,80,512]{4,3,2,1,0:T(8,128)(2,1)S(1)}, bf16[2,1,2,80,512]{4,3,2,1,0:T(8,128)(2,1)S(1)}, u32[]{:S(2)}, u32[]{:S(2)}) collective-permute-start(bf16[2,1,2,80,512]{4,3,2,1,0:T(8,128)(2,1)S(1)} %constant_dynamic-slice_fusion.7), channel_id=1, source_target_pairs={{0,4},{2,6},{4,0},{6,2},{8,12},{10,14},{12,8},{14,10},{1,5},{3,7},... | collective-permute-start | bytes 983048 | tf_op jit(solution)/shard_map/ppermute | solution.py:289
  154.7 9.6 %collective-permute-start.32 = (bf16[2,2,1,88,512]{4,3,2,1,0:T(8,128)(2,1)S(1)}, bf16[2,2,1,88,512]{4,3,2,1,0:T(8,128)(2,1)S(1)}, u32[]{:S(2)}, u32[]{:S(2)}) collective-permute-start(bf16[2,2,1,88,512]{4,3,2,1,0:T(8,128)(2,1)S(1)} %constant_dynamic-slice_fusion.5), channel_id=1, source_target_pairs={{0,2},{2,0},{4,6},{6,4},{8,10},{10,8},{12,14},{14,12},{1,3},{3,1},... | collective-permute-start | bytes 1081352 | tf_op jit(solution)/shard_map/ppermute | solution.py:289
  163.4 5.4 %collective-permute-start.31 = (bf16[2,1,1,80,512]{4,3,2,1,0:T(8,128)(2,1)S(1)}, bf16[2,1,1,80,512]{4,3,2,1,0:T(8,128)(2,1)S(1)}, u32[]{:S(2)}, u32[]{:S(2)}) collective-permute-start(bf16[2,1,1,80,512]{4,3,2,1,0:T(8,128)(2,1)S(1)} %constant_dynamic-slice_fusion.6), channel_id=1, source_target_pairs={{0,2},{2,0},{4,6},{6,4},{8,10},{10,8},{12,14},{14,12},{1,3},{3,1},... | collective-permute-start | bytes 491528 | tf_op jit(solution)/shard_map/ppermute | solution.py:289
  164.5 6.1 %collective-permute-start.33 = (bf16[2,1,1,88,512]{4,3,2,1,0:T(8,128)(2,1)S(1)}, bf16[2,1,1,88,512]{4,3,2,1,0:T(8,128)(2,1)S(1)}, u32[]{:S(2)}, u32[]{:S(2)}) collective-permute-start(bf16[2,1,1,88,512]{4,3,2,1,0:T(8,128)(2,1)S(1)} %constant_dynamic-slice_fusion.4), channel_id=1, source_target_pairs={{0,4},{2,6},{4,0},{6,2},{8,12},{10,14},{12,8},{14,10},{1,5},{3,7},... | collective-permute-start | bytes 540680 | tf_op jit(solution)/shard_map/ppermute | solution.py:289
  170.7 8.2 %collective-permute-start.34 = (bf16[1,1,1,168,512]{4,3,2,1,0:T(8,128)(2,1)S(1)}, bf16[1,1,1,168,512]{4,3,2,1,0:T(8,128)(2,1)S(1)}, u32[]{:S(2)}, u32[]{:S(2)}) collective-permute-start(bf16[1,1,1,168,512]{4,3,2,1,0:T(8,128)(2,1)S(1)} %fusion.3), channel_id=1, source_target_pairs={{0,8},{2,10},{4,12},{6,14},{8,0},{10,2},{12,4},{14,6},{1,9},{3,11}... | collective-permute-start | bytes 516104 | tf_op jit(solution)/shard_map/ppermute | solution.py:289

commit v3 on v2

--- a/solution.py
+++ b/solution.py
@@ -13,7 +13,7 @@
 F32 = jnp.float32
 BF16 = jnp.bfloat16
 TILE = 256
-VMEM_LIMIT = 56 * 1024 * 1024
+VMEM_LIMIT = 20 * 1024 * 1024
 PARAMS = pltpu.CompilerParams(vmem_limit_bytes=VMEM_LIMIT)
 WHOLE = pl.BlockSpec(memory_space=pltpu.VMEM)
 SCALAR = pl.BlockSpec(memory_space=pltpu.SMEM)
@@ -37,7 +37,7 @@
     return pl.pallas_call(
         kernel,
         out_shape=[jax.ShapeDtypeStruct(s, d) for s, d in outs],
-        in_specs=[SCALAR if a.dtype == jnp.int32 and a.shape == (1,) else WHOLE for a in args],
+        in_specs=[SCALAR if a.dtype == jnp.int32 and a.ndim == 1 else WHOLE for a in args],
         out_specs=[WHOLE] * len(outs),
         scratch_shapes=scratch,
         compiler_params=PARAMS,
@@ -45,8 +45,11 @@
     )(*args)
 
 
-def scan_kernel(feat_ref, forget_ref, keep_ref, mass_ref, weight_ref, sum_ref):
-    feat, forget = feat_ref[...], forget_ref[...]
+CARRY_ROWS = 8
+LABEL_ROWS = 16
+
+
+def scan(feat, forget):
     rows = feat.shape[0]
     keep, mass, weight = 1.0 - forget, forget * (feat * feat), forget
     row = lax.broadcasted_iota(jnp.int32, feat.shape, 0)
@@ -59,23 +62,69 @@
         weight = keep * before + weight
         keep = keep * jnp.where(inside, pltpu.roll(keep, step, 0), 1.0)
         step *= 2
-    keep_ref[...], mass_ref[...], weight_ref[...] = keep, mass, weight
-    sum_ref[0:1, :] = keep[rows - 1 :]
-    sum_ref[1:2, :] = mass[rows - 1 :]
-    sum_ref[2:3, :] = weight[rows - 1 :]
-
-
-def norm_kernel(feat_ref, keep_ref, mass_ref, weight_ref, carry_ref, out_ref):
+    return keep, mass, weight
+
+
+def scan_kernel(feat_ref, forget_ref, keep_ref, mass_ref, weight_ref, carry_ref):
+    rows, bands = feat_ref.shape
+    values = scan(feat_ref[...], forget_ref[...])
+    carry_ref[...] = jnp.zeros_like(carry_ref)
+    for k, (ref, value) in enumerate(zip((keep_ref, mass_ref, weight_ref), values)):
+        ref[...] = value
+        rest = value[rows - 1 :]
+        for part in range(3):
+            rounded = rest.astype(BF16).astype(F32)
+            carry_ref[part : part + 1, k * bands : (k + 1) * bands] = rounded
+            rest = rest - rounded
+
+
+def pack_kernel(scalar_ref, feat_ref, forget_ref, conv_ref, res_ref, in_ref, out_ref,
+                keep_ref, mass_ref, weight_ref, pack_ref, carry_ref):
+    scan_kernel(feat_ref, forget_ref, keep_ref, mass_ref, weight_ref, carry_ref)
+    c = pack_ref.shape[1]
+    n, half, more = conv_ref.shape[1] // 2, res_ref.shape[1] // 2, in_ref.shape[0]
+
+    def fill(across):
+        cols = slice(across * c, (across + 1) * c)
+        part = slice(across * half, (across + 1) * half)
+        at = 0
+
+        def put(value):
+            nonlocal at
+            pack_ref[at : at + value.shape[0], :] = value
+            at += value.shape[0]
+
+        put(conv_ref[0, :n, cols])
+        put(res_ref[1, part, :])
+        put(conv_ref[0, n:, cols])
+        put(conv_ref[1, :n, cols])
+        put(res_ref[0, part, :])
+        put((out_ref if across else in_ref)[...])
+        put(carry_ref[...].astype(BF16))
+        put(conv_ref[1, n:, cols])
+
+    pl.when(scalar_ref[1] == 0)(lambda: fill(0))
+    pl.when(scalar_ref[1] == 1)(lambda: fill(1))
+
+
+def norm_kernel(scalar_ref, feat_ref, keep_ref, mass_ref, weight_ref, carry_ref, label_ref, out_ref):
+    bands = feat_ref.shape[1]
+    mass0 = jnp.zeros((1, bands), F32)
+    weight0 = jnp.zeros((1, bands), F32)
+    for j in range(carry_ref.shape[0]):
+        parts = carry_ref[j].astype(F32)
+        value = (parts[0:1] + parts[1:2]) + parts[2:3]
+        before = j < scalar_ref[2]
+        keep = value[:, :bands]
+        mass0 = jnp.where(before, keep * mass0 + value[:, bands : 2 * bands], mass0)
+        weight0 = jnp.where(before, keep * weight0 + value[:, 2 * bands : 3 * bands], weight0)
     keep = keep_ref[...]
-    mass = keep * carry_ref[1:2, :] + mass_ref[...]
-    weight = keep * carry_ref[2:3, :] + weight_ref[...]
-    out_ref[...] = (feat_ref[...] / jnp.sqrt(mass / weight + LEVEL_FLOOR)).astype(BF16)
-
-
-def compose(earlier, later):
-    keep = later[0:1] * earlier[0:1]
-    rest = later[0:1] * earlier[1:3] + later[1:3]
-    return jnp.concatenate([keep, rest], axis=0)
+    mass = keep * mass0 + mass_ref[...]
+    weight = keep * weight0 + weight_ref[...]
+    normed = (feat_ref[...] / jnp.sqrt(mass / weight + LEVEL_FLOOR)).astype(BF16)
+    out_ref[LABEL_ROWS:, :] = normed
+    out_ref[:LABEL_ROWS, :] = jnp.zeros((LABEL_ROWS, bands), BF16)
+    out_ref[: label_ref.shape[0], :] = label_ref[...].astype(F32).astype(BF16)
 
 
 def rows_of(ref, part=None):
@@ -103,14 +152,18 @@
     return t, s
 
 
+def slopes(t, s):
+    return s * (1.0 - t * t), t * s * (1.0 - s)
+
+
 def tile_at(i, offset=0):
     return pl.ds(pl.multiple_of(i * TILE + offset, TILE), TILE)
 
 
 def forward_first(before, site_ref, norm_ref, w_in_ref, a_ref, a2_ref, b_ref, b2_ref, c_ref, c2_ref,
-                  h0_ref, h1_ref, tanh_ref, sigm_ref, filt_ref, gate_ref, res_ref):
+                  h0_ref, h1_ref, gated_ref, filtd_ref, gated_d_ref, filt_ref, gate_ref, res_ref):
     rows, c = h0_ref.shape
-    kept = tanh_ref.shape[0]
+    kept, steps = filtd_ref.shape[0], gated_ref.shape[0]
     d = rows - h1_ref.shape[0]
     n, r = a_ref.shape[2], res_ref.shape[1] // 2
     place(site_ref, [
@@ -118,31 +171,21 @@
         (filt_ref, n, b_ref, b2_ref, 0, 0, n), (gate_ref, n, b_ref, b2_ref, 1, 0, n),
         (res_ref, 0, c_ref, c2_ref, 0, 0, r), (res_ref, r, c_ref, c2_ref, 1, 0, r)])
 
-    def enter(i, _):
-        h0_ref[tile_at(i), :] = dot(norm_ref[tile_at(i), :], w_in_ref[...]).astype(BF16)
-        return 0
-
-    lax.fori_loop(0, rows // TILE, enter, 0)
-
-    def tile(i):
-        now = h0_ref[tile_at(i, d), :]
-        t, s = activate(h0_ref[tile_at(i), :], now, filt_ref, gate_ref)
-        out = now.astype(F32) + dot((t * s).astype(BF16), rows_of(res_ref))
-        h1_ref[tile_at(i), :] = out.astype(BF16)
-        return t, s
-
-    def plain(i, _):
-        tile(i)
-        return 0
-
-    def saving(i, _):
-        t, s = tile(i)
-        tanh_ref[tile_at(i, -before), :], sigm_ref[tile_at(i, -before), :] = t, s
-        return 0
-
-    lax.fori_loop(0, before // TILE, plain, 0)
-    lax.fori_loop(before // TILE, (before + kept) // TILE, saving, 0)
-    lax.fori_loop((before + kept) // TILE, h1_ref.shape[0] // TILE, plain, 0)
+    for i in range(rows // TILE):
+        at = slice(i * TILE, (i + 1) * TILE)
+        h0_ref[at, :] = dot(norm_ref[at, :], w_in_ref[...]).astype(BF16)
+    for i in range(h1_ref.shape[0] // TILE):
+        at = slice(i * TILE, (i + 1) * TILE)
+        now = h0_ref[i * TILE + d : (i + 1) * TILE + d, :]
+        t, s = activate(h0_ref[at, :], now, filt_ref, gate_ref)
+        gated = (t * s).astype(BF16)
+        h1_ref[at, :] = (now.astype(F32) + dot(gated, rows_of(res_ref))).astype(BF16)
+        first = i * TILE - before
+        if 0 <= first < kept:
+            own = slice(first, first + TILE)
+            filtd_ref[own, :], gated_d_ref[own, :] = (v.astype(BF16) for v in slopes(t, s))
+            if first < steps:
+                gated_ref[own, :] = gated
 
 
 def store_terms(site_ref, keep_ref, send_ref, row, value, first, size, start, count, lane=0):
@@ -167,11 +210,11 @@
     store_terms(site_ref, keep_ref, send_ref, 2 * conv + half, value, first, size, 0, half)
 
 
-def second_kernel(steps, scale, sizes, site_ref, h1_ref, w_out_ref, label_ref, valid_ref,
+def second_kernel(steps, scale, sizes, site_ref, h1_ref, w_out_ref, label_ref,
                   a_ref, a2_ref, b_ref, b2_ref, c_ref, c2_ref,
                   loss_ref, keep_ref, send_ref, back_ref, grad_ref, filt_ref, gate_ref,
                   res_ref, gated_ref, h2_ref, lgrad_ref, round_ref):
-    rows, c = grad_ref.shape
+    rows, c = back_ref.shape[0], grad_ref.shape[1]
     d = h1_ref.shape[0] - rows
     classes = w_out_ref.shape[1]
     conv, res, _, out = sizes
@@ -181,31 +224,43 @@
         (filt_ref, 0, b_ref, b2_ref, 0, 0, n), (gate_ref, 0, b_ref, b2_ref, 1, 0, n),
         (filt_ref, n, c_ref, c2_ref, 0, 0, n), (gate_ref, n, c_ref, c2_ref, 1, 0, n)])
 
-    def tile(i, _):
-        at = tile_at(i)
-        now = h1_ref[tile_at(i, d), :]
+    lanes = label_ref.shape[1]
+    class_row = lax.broadcasted_iota(jnp.int32, (classes, lanes), 0).astype(F32)
+    unit = class_row == lax.broadcasted_iota(jnp.int32, (lanes, lanes), 1).astype(F32)
+    row = lax.broadcasted_iota(jnp.int32, (TILE, 1), 0)
+    left = site_ref[3] - site_ref[2] * steps
+
+    for i in range(rows // TILE):
+        at = slice(i * TILE, (i + 1) * TILE)
+        now = h1_ref[i * TILE + d : (i + 1) * TILE + d, :]
         t, s = activate(h1_ref[at, :], now, filt_ref, gate_ref)
         gated = (t * s).astype(BF16)
         h2 = (now.astype(F32) + dot(gated, rows_of(res_ref))).astype(BF16)
         logits = dot(h2, w_out_ref[...])
         total = jnp.log(jnp.sum(jnp.exp(logits), axis=1, keepdims=True))
-        hot = (label_ref[at, :] == lax.broadcasted_iota(jnp.int32, (TILE, classes), 1)).astype(F32)
-        valid = valid_ref[at, :]
-        loss_ref[at, :] = (total - jnp.sum(logits * hot, axis=1, keepdims=True)) * valid
+        groups = range(i * TILE // lanes, (i + 1) * TILE // lanes)
+        hot = jnp.concatenate(
+            [(class_row == label_ref[k : k + 1, :].astype(F32)).astype(F32).T for k in groups])
+        valid = (row + i * TILE < left).astype(F32)
         lgrad = ((jnp.exp(logits - total) - hot) * (valid * scale)).astype(BF16)
         grad = dot_t(lgrad, w_out_ref[...])
         rounded = grad.astype(BF16)
         back = dot_t(rounded, rows_of(res_ref))
-        back_ref[at, :c] = (back * s * (1.0 - t * t)).astype(BF16)
-        back_ref[at, c:] = (back * t * s * (1.0 - s)).astype(BF16)
-        grad_ref[at, :] = grad
-        gated_ref[at, :] = gated
-        h2_ref[at, :] = h2
-        lgrad_ref[at, :] = lgrad
-        round_ref[at, :] = rounded
-        return 0
-
-    lax.fori_loop(0, rows // TILE, tile, 0)
+        filtd, gated_d = slopes(t, s)
+        back_ref[at, :c] = (back * filtd).astype(BF16)
+        back_ref[at, c:] = (back * gated_d).astype(BF16)
+        if i * TILE < grad_ref.shape[0]:
+            grad_ref[at, :] = grad
+        if i * TILE < steps:
+            loss = (total - jnp.sum(logits * hot, axis=1, keepdims=True)) * valid
+            for j, k in enumerate(groups):
+                part = jnp.where(unit, loss[j * lanes : (j + 1) * lanes], 0.0)
+                loss_ref[k : k + 1, :] = jnp.sum(part, axis=0, keepdims=True)
+            gated_ref[at, :] = gated
+            h2_ref[at, :] = h2
+            lgrad_ref[at, :] = lgrad
+            round_ref[at, :] = rounded
+
     own = slice(0, steps)
     targets = (site_ref, keep_ref, send_ref)
 
@@ -221,10 +276,10 @@
             store_terms(*targets, 2 * conv + res, value, i * (TILE // (2 * out)), out, q * count, count, q * classes)
         return 0
 
-    lax.fori_loop(0, c // TILE, terms, 0)
-
-
-def grad_first(back1_ref, grad2_ref, filt1_ref, gate1_ref, tanh_ref, sigm_ref, res_ref,
+    lax.fori_loop(0, c // TILE, terms, 0, unroll=True)
+
+
+def grad_first(back1_ref, grad2_ref, filt1_ref, gate1_ref, filtd_ref, gated_d_ref, res_ref,
                grad_ref, round_ref, back_ref):
     rows, c = grad_ref.shape
     d1 = back1_ref.shape[0] - rows
@@ -236,18 +291,17 @@
         grad += dot_t(back1_ref[later, :c], rows_of(filt1_ref, 0))
         grad += dot_t(back1_ref[later, c:], rows_of(gate1_ref, 0))
         rounded = grad.astype(BF16)
-        t, s = tanh_ref[at, :], sigm_ref[at, :]
         back = dot_t(rounded, rows_of(res_ref))
-        back_ref[at, :c] = (back * s * (1.0 - t * t)).astype(BF16)
-        back_ref[at, c:] = (back * t * s * (1.0 - s)).astype(BF16)
+        back_ref[at, :c] = (back * filtd_ref[at, :].astype(F32)).astype(BF16)
+        back_ref[at, c:] = (back * gated_d_ref[at, :].astype(F32)).astype(BF16)
         grad_ref[at, :] = grad
         round_ref[at, :] = rounded
         return 0
 
-    lax.fori_loop(0, rows // TILE, tile, 0)
-
-
-def terms_first(steps, start, sizes, site_ref, back_ref, grad_ref, round_ref, h0_ref, tanh_ref, sigm_ref,
+    lax.fori_loop(0, rows // TILE, tile, 0, unroll=True)
+
+
+def terms_first(steps, start, sizes, site_ref, back_ref, grad_ref, round_ref, h0_ref, gated_ref,
                 norm_ref, filt_ref, gate_ref, keep_ref, send_ref, last_ref):
     rows, c = grad_ref.shape
     d0 = rows - steps
@@ -261,11 +315,10 @@
         past, now = h0_ref[start - d0 : start - d0 + steps, at], h0_ref[start : start + steps, at]
         conv_terms(*targets, first, conv, res // 2, t_dot(past, back_ref[own, :]))
         conv_terms(*targets, first + c // (2 * conv), conv, res // 2, t_dot(now, back_ref[own, :]))
-        gated = (tanh_ref[own, at] * sigm_ref[own, at]).astype(BF16)
-        res_terms(*targets, i * (TILE // (2 * res)), conv, res, t_dot(gated, round_ref[own, :]))
+        res_terms(*targets, i * (TILE // (2 * res)), conv, res, t_dot(gated_ref[own, at], round_ref[own, :]))
         return 0
 
-    lax.fori_loop(0, c // TILE, terms, 0)
+    lax.fori_loop(0, c // TILE, terms, 0, unroll=True)
 
     def last(i, _):
         at, later = tile_at(i), tile_at(i, d0)
@@ -276,7 +329,7 @@
         last_ref[at, :] = grad.astype(BF16)
         return 0
 
-    lax.fori_loop(0, steps // TILE, last, 0)
+    lax.fori_loop(0, steps // TILE, last, 0, unroll=True)
     value = t_dot(norm_ref[start : start + steps, :], last_ref[...])
     store_terms(*targets, 2 * conv + res, value, 0, enter, 0, enter)
 
@@ -339,19 +392,19 @@
 
 
 def rows_before(value, count):
-    steps, parts, by = value.shape[0], [], 1
+    steps, parts, by = value.shape[0] - LABEL_ROWS, [], 1
     while count > 0:
         take = min(count, steps)
-        parts.insert(0, hop(value[steps - take :], by))
+        parts.insert(0, hop(value[LABEL_ROWS + steps - take :], by))
         count, by = count - take, by + 1
     return parts
 
 
 def rows_after(value, count):
-    steps, parts, by = value.shape[0], [], 1
+    steps, parts, by = value.shape[0] - LABEL_ROWS, [], 1
     while count > 0:
         take = min(count, steps)
-        parts.append(hop(value[:take], -by))
+        parts.append(hop(value[: LABEL_ROWS + take], -by))
         count, by = count - take, by + 1
     return parts
 
@@ -369,58 +422,54 @@
     d0, d1 = BASE_DILATION, 2 * BASE_DILATION
     reach = d0 + d1
     position, site = lax.axis_index("tm"), lax.axis_index("site")
-    site_arg = site.astype(jnp.int32)[None]
+    across = my_bit(ACROSS)
+    scalars = jnp.stack([site, across, position, lengths[0]]).astype(jnp.int32)
     core = ("site", 0)
-
-    def own_half(across):
-        cols = slice(across * c, (across + 1) * c)
-        part = slice(across * half, (across + 1) * half)
-        more = w_in if across == 0 else w_out.reshape(extra, c)
-        first, second = w_conv[0, :, cols], w_conv[1, :, cols]
-        n = conv // 2
-        return jnp.concatenate([
-            first[:n], w_res[1, part], first[n:], second[:n], w_res[0, part], more, second[n:]])
-
-    n = conv // 2
-    cuts = [n, half, n, n, half + enter, n]
-    held = jnp.where(my_bit(ACROSS) == 0, own_half(0), own_half(1))
-    held = held.reshape((1,) * (time_bits() + 1) + held.shape)
 
     block = ((steps, bands), F32)
     feat = features[0]
-    keep, mass, weight, summary = call(
-        scan_kernel, [block] * 3 + [((3, bands), F32)], [], 40 * steps * bands, feat, forget[0])
-    labels_here = labels[0][:, None]
-    label_window = jnp.concatenate([labels_here] + rows_after(labels_here, reach))
+    out_rows = w_out.reshape(extra, c)
+    if aligned:
+        packed = 2 * (conv + half) + enter + CARRY_ROWS
+        keep, mass, weight, held, _ = call(
+            pack_kernel, [block] * 3 + [((packed, c), BF16), ((CARRY_ROWS, c), F32)], [], 40 * steps * bands,
+            scalars, feat, forget[0], w_conv, w_res, w_in, out_rows)
+    else:
+        keep, mass, weight, carry = call(
+            scan_kernel, [block] * 3 + [((CARRY_ROWS, c), F32)], [], 40 * steps * bands, feat, forget[0])
+        n = conv // 2
+        conv_own = jnp.where(across == 0, w_conv[:, :, :c], w_conv[:, :, c:])
+        res_own = jnp.where(across == 0, w_res[:, :half], w_res[:, half:])
+        held = jnp.concatenate([
+            conv_own[0, :n], res_own[1], conv_own[0, n:], conv_own[1, :n], res_own[0],
+            jnp.where(across == 0, w_in, out_rows), carry.astype(BF16), conv_own[1, n:]])
+    n = conv // 2
+    cuts = [n, half, n, n, half + enter + CARRY_ROWS, n]
+    held = held.reshape((1,) * (time_bits() + 1) + held.shape)
     for bit in reversed(range(2, time_bits())):
         held = join(held, swap(held, ("tm", bit)), ("tm", bit))
-    carry = jnp.concatenate([jnp.ones((1, bands), F32), jnp.zeros((2, bands), F32)])
-    total = summary
-
-    def carry_step(carry, total, bit):
-        other = swap(total, ("tm", bit))
-        upper = my_bit(("tm", bit)) == 1
-        carry = jnp.where(upper, compose(other, carry), carry)
-        return carry, jnp.where(upper, compose(other, total), compose(total, other))
-
-    orders = [(FAR, NEAR, ACROSS), (NEAR, ACROSS, FAR), (ACROSS, FAR, NEAR)]
+
+    orders = [(ACROSS, FAR, NEAR), (NEAR, ACROSS, FAR), (FAR, NEAR, ACROSS)]
     bounds = [0, cuts[0] + cuts[1], sum(cuts[:4]), sum(cuts)]
     pieces = [held[..., bounds[k] : bounds[k + 1], :] for k in range(3)]
-    bits = list(range(time_bits()))
     for step in range(2):
-        take = bits if step == 1 else bits[:1]
-        bits = bits[len(take):]
-        *pieces, carry, total = together(*pieces, carry, total)
+        pieces = together(*pieces)
         pieces = [join(p, swap(p, order[step]), order[step]) for p, order in zip(pieces, orders)]
-        for bit in take:
-            carry, total = carry_step(carry, total, bit)
-    (normed,) = call(norm_kernel, [((steps, bands), BF16)], [], 10 * steps * bands,
-                     feat, keep, mass, weight, carry)
-    *pieces, normed = together(*pieces, normed)
+    at = half + enter
+    carries = pieces[2][..., at : at + CARRY_ROWS, :].reshape(time_devices, CARRY_ROWS, c)
+    pieces[2] = jnp.concatenate([pieces[2][..., :at, :], pieces[2][..., at + CARRY_ROWS :, :]], axis=-2)
+    cuts[4] = at
+    label_rows = steps // bands
+    (normed,) = call(norm_kernel, [((LABEL_ROWS + steps, bands), BF16)], [], 10 * steps * bands,
+                     scalars, feat, keep, mass, weight, carries, labels[0].reshape(label_rows, bands))
+    pieces = together(*pieces)
     layers = [[p[..., :cut, :] for p, cut in zip(pieces, cuts[::2])],
               [p[..., cut:, :] for p, cut in zip(pieces, cuts[::2])]]
     first = [join(p, swap(p, order[2]), order[2]) for p, order in zip(layers[0], orders)]
-    window = jnp.concatenate(rows_before(normed, reach) + [normed] + rows_after(normed, reach))
+    past, future = rows_before(normed, reach), rows_after(normed, reach)
+    window = jnp.concatenate(past + [normed[LABEL_ROWS:]] + [v[LABEL_ROWS:] for v in future])
+    label_window = jnp.concatenate(
+        [v[: (v.shape[0] - LABEL_ROWS) // bands] for v in [normed] + future])
     *rest, window = together(*first, *layers[1], window)
     first, second = rest[:3], rest[3:]
     second = [join(p, swap(p, order[2]), order[2]) for p, order in zip(second, orders)]
@@ -439,37 +488,34 @@
     in_all = extras[:, :, 0].reshape(-1, c)
     out_all = extras[:, :, 1].reshape(-1, classes)
 
-    at = position * steps + lax.broadcasted_iota(jnp.int32, (steps + reach, 1), 0)
-    valid = (at < lengths[0]).astype(F32)
-
     total_rows, rows0, rows1 = steps + 2 * reach, steps + d0, steps + reach
     conv_all, res_all = ((devices, conv, c), kind), ((devices, res, c), kind)
-    h0, h1, tanh0, sigm0, filt0, gate0, res0 = call(
+    h0, h1, gated0, filtd0, gated_d0, filt0, gate0, res0 = call(
         functools.partial(forward_first, d1),
-        [((total_rows, c), BF16), ((total_rows - d0, c), BF16), ((rows0, c), F32), ((rows0, c), F32),
+        [((total_rows, c), BF16), ((total_rows - d0, c), BF16), ((steps, c), BF16), ((rows0, c), BF16), ((rows0, c), BF16),
          conv_all, conv_all, res_all],
-        [], 2 * total_rows * c * (bands + 5 * c), site_arg, window, in_all, *kernel_args(first))
+        [], 2 * total_rows * c * (bands + 5 * c), scalars, window, in_all, *kernel_args(first))
 
     second = both_cores(second)
     scale = 1.0 / math.sqrt(site_devices * steps * time_devices)
     package = [((time_devices, 2 * conv + res + extra, c), kind)] * 2
     loss, keep1, send1, back1, grad2, filt1, gate1 = call(
         functools.partial(second_kernel, steps, scale, sizes),
-        [((rows1, 1), F32)] + package + [((rows1, 2 * c), BF16), ((rows1, c), F32), conv_all, conv_all],
-        [pltpu.VMEM((devices, res, c), kind), pltpu.VMEM((rows1, c), BF16), pltpu.VMEM((rows1, c), BF16),
-         pltpu.VMEM((rows1, classes), BF16), pltpu.VMEM((rows1, c), BF16)],
+        [((label_rows, bands), F32)] + package + [((rows1, 2 * c), BF16), ((rows0, c), F32), conv_all, conv_all],
+        [pltpu.VMEM((devices, res, c), kind), pltpu.VMEM((steps, c), BF16), pltpu.VMEM((steps, c), BF16),
+         pltpu.VMEM((steps, classes), BF16), pltpu.VMEM((steps, c), BF16)],
         2 * rows1 * c * 6 * c + 2 * steps * 5 * c * c,
-        site_arg, h1, out_all, label_window, valid, *kernel_args(second))
+        scalars, h1, out_all, label_window, *kernel_args(second))
 
     sum1 = (keep1.astype(F32) + swap(send1.astype(BF16), core).astype(F32)).astype(BF16)
     grad1, round0, back0 = call(
         grad_first, [((rows0, c), F32), ((rows0, c), BF16), ((rows0, 2 * c), BF16)], [],
-        2 * rows0 * c * 5 * c, back1, grad2, filt1, gate1, tanh0, sigm0, res0)
+        2 * rows0 * c * 5 * c, back1, grad2, filt1, gate1, filtd0, gated_d0, res0)
     sum1, back0 = together(sum1, back0)
     keep0, send0 = call(
         functools.partial(terms_first, steps, reach, sizes), package, [pltpu.VMEM((steps, c), BF16)],
         2 * steps * 9 * c * c,
-        site_arg, back0, grad1, round0, h0, tanh0, sigm0, window, filt0, gate0)
+        scalars, back0, grad1, round0, h0, gated0, window, filt0, gate0)
     sum0 = (keep0.astype(F32) + swap(send0.astype(BF16), core).astype(F32)).astype(BF16)
 
     grads = []
@@ -483,7 +529,7 @@
         ))
     (conv0, res0, grad_in), (conv1, res1, grad_out) = grads
     return (
-        loss[:steps, 0][None],
+        loss.reshape(1, steps),
         jnp.stack([conv0, conv1]),
         jnp.stack([res0, res1]),
         grad_in,

time: 182 us -> 172 us (0.945)
  Pallas kernels: 52.2 us -> 29.3 us
  waiting for transfers between devices: 44.8 us -> 58.1 us
  starting transfers between devices: 55 us -> 48.2 us
  local copies, waits for them, and re-layouts: 21.1 us -> 24.7 us
  other arithmetic: 5.81 us -> 8.61 us
    pallas_call x6, Pallas kernels: 52.2 us -> 29.3 us  [call(): pl.pallas_call(kernel, out_shape=[jax.ShapeDtypeStruct(s, d) for s, d in...]
    ppermute x34 -> x31, waiting for transfers between devices: 43.4 us -> 56 us  [swap(): lax.ppermute(value, axis, [(i, i ^ 1 << bit) for i in range(lax.axis_size...]
    unnamed x58 -> x74, local copies, waits for them, and re-layouts: 11.9 us -> 22.6 us
    ppermute x6 -> x4, starting transfers between devices: 15.3 us -> 9.88 us  [hop(): lax.ppermute(value, 'tm', [(i, i + by) for i in range(size) if 0 <= i + b...]
    concatenate x7 -> x1, local copies, waits for them, and re-layouts: 4.17 us -> 0.01 us  [on_device(): jnp.concatenate(past + [normed[LABEL_ROWS:]] + [v[LABEL_ROWS:] for v in f...]
    slice x3 -> x9, local copies, waits for them, and re-layouts: 2.37 us -> 0.07 us  [the longest x1 0.02 us: on_device(): pieces[2][..., at + CARRY_ROWS:, :]]
    ppermute x34 -> x31, starting transfers between devices: 39.6 us -> 38.3 us  [swap(): lax.ppermute(value, axis, [(i, i ^ 1 << bit) for i in range(lax.axis_size...]
  transfers between devices with their start and end apart: 40 -> 35, of which waited for: 14 -> 18; matrix products, arithmetic and copies ran while one was open for 6% -> 2% of each run, Pallas kernels for 20% -> 9%
where the time goes in v3:
time: 172 us; the launch traced here: 171 us
  waiting for transfers between devices  58.1 us (34%)
  starting transfers between devices  48.2 us (28%)
  Pallas kernels  29.3 us (17%)
  local copies, waits for them, and re-layouts  24.7 us (14%)
  other arithmetic  8.61 us (5%)
  between operations  2.1 us (1%)
    ppermute x31, waiting for transfers between devices, swap(): lax.ppermute(value, axis, [(i, i ^ 1 << bit) for i in range(lax.axis_size...  56 us
    ppermute x31, starting transfers between devices, swap(): lax.ppermute(value, axis, [(i, i ^ 1 << bit) for i in range(lax.axis_size...  38.3 us
    pallas_call x6, Pallas kernels, call(): pl.pallas_call(kernel, out_shape=[jax.ShapeDtypeStruct(s, d) for s, d in...  29.3 us
    unnamed x74, local copies, waits for them, and re-layouts  22.6 us
    ppermute x4, starting transfers between devices, hop(): lax.ppermute(value, 'tm', [(i, i + by) for i in range(size) if 0 <= i + b...  9.88 us
  transfers between devices with their start and end apart: 35, of which 18 were waited for; matrix products, arithmetic and copies ran while one was open for 2% of the time, Pallas kernels for 9%

profile of v3, /device:TPU:0, one launch (start us, length us, event | category | flops | bytes accessed | tf_op | source)
XLA Modules:
  0.0 171.1 jit_solution(6188536360192899673)
XLA Ops:
  2.1 0.9 copy-done.10
  3.0 0.9 copy-done.26
  4.0 0.9 copy-done.27
  4.9 0.8 copy-done.28
  6.5 1.8 %shard_map.119 = (f32[512,128]{1,0:T(8,128)S(1)}, f32[512,128]{1,0:T(8,128)S(1)}, f32[512,128]{1,0:T(8,128)S(1)}, bf16[176,512]{1,0:T(8,128)(2,1)S(1)}, f32[8,512]{1,0:T(8,128)}) custom-call(s32[4]{0:T(128)S(1)} %pad_add_fusion.scalar_ref.site_ref, f32[512,128]{1,0:T(8,128)S(1)} %bitcast.55, f32[512,128]{1,0:T(8,128)S(1)} %bitcast.64, ...), custom_call_target="tpu_custom_call" | custom-call | flops 2621440 | bytes 1851408 | tf_op jit(solution)/shard_map/pallas_call | solution.py:37
  8.3 4.0 %collective-permute-start = (bf16[1,1,1,1,176,512]{5,4,3,2,1,0:T(8,128)(2,1)S(1)}, bf16[1,1,1,1,176,512]{5,4,3,2,1,0:T(8,128)(2,1)S(1)}, u32[]{:S(2)}, u32[]{:S(2)}) collective-permute-start(bf16[1,1,1,1,176,512]{5,4,3,2,1,0:T(8,128)(2,1)S(1)} %bitcast.66), channel_id=1, source_target_pairs={{0,8},{2,10},{4,12},{6,14},{8,0},{10,2},{12,4},{14,6},{1,9},{3,11}... | collective-permute-start | bytes 540680 | tf_op jit(solution)/shard_map/ppermute | solution.py:342
  12.3 8.4 %collective-permute-done = bf16[1,1,1,1,176,512]{5,4,3,2,1,0:T(8,128)(2,1)S(1)} collective-permute-done((bf16[1,1,1,1,176,512]{5,4,3,2,1,0:T(8,128)(2,1)S(1)}, bf16[1,1,1,1,176,512]{5,4,3,2,1,0:T(8,128)(2,1)S(1)}, u32[]{:S(2)}, u32[]{:S(2)}) %collective-permute-start) | collective-permute-done | bytes 180256 | tf_op jit(solution)/shard_map/ppermute | solution.py:342
  20.8 1.6 collective-permute-start.1
  23.1 1.5 collective-permute-start.2
  24.6 0.9 collective-permute-done.1
  25.5 1.9 %collective-permute-done.3 = bf16[2,1,1,1,64,512]{5,4,3,2,1,0:T(8,128)(2,1)S(1)} collective-permute-done((bf16[2,1,1,1,64,512]{5,4,3,2,1,0:T(8,128)(2,1)S(1)}, bf16[2,1,1,1,64,512]{5,4,3,2,1,0:T(8,128)(2,1)S(1)}, u32[]{:S(2)}, u32[]{:S(2)}) %collective-permute-start.3) | collective-permute-done | bytes 131104 | tf_op jit(solution)/shard_map/ppermute | solution.py:342
  28.1 1.4 collective-permute-start.4
  29.5 1.5 collective-permute-start.6
  31.5 2.3 %collective-permute-done.4 = bf16[2,1,1,2,48,512]{5,4,3,2,1,0:T(8,128)(2,1)S(1)} collective-permute-done((bf16[2,1,1,2,48,512]{5,4,3,2,1,0:T(8,128)(2,1)S(1)}, bf16[2,1,1,2,48,512]{5,4,3,2,1,0:T(8,128)(2,1)S(1)}, u32[]{:S(2)}, u32[]{:S(2)}) %collective-permute-start.4) | collective-permute-done | bytes 196640 | tf_op jit(solution)/shard_map/ppermute | solution.py:342
  33.9 2.0 %collective-permute-done.6 = bf16[2,2,1,1,64,512]{5,4,3,2,1,0:T(8,128)(2,1)S(1)} collective-permute-done((bf16[2,2,1,1,64,512]{5,4,3,2,1,0:T(8,128)(2,1)S(1)}, bf16[2,2,1,1,64,512]{5,4,3,2,1,0:T(8,128)(2,1)S(1)}, u32[]{:S(2)}, u32[]{:S(2)}) %collective-permute-start.6) | collective-permute-done | bytes 262176 | tf_op jit(solution)/shard_map/ppermute | solution.py:342
  36.7 1.3 collective-permute-start.12
  38.1 5.5 %collective-permute-start.10 = (bf16[256,128]{1,0:T(8,128)(2,1)S(1)}, bf16[256,128]{1,0:T(8,128)(2,1)S(1)}, u32[]{:S(2)}, u32[]{:S(2)}) collective-permute-start(bf16[256,128]{1,0:T(8,128)(2,1)S(1)} %slice.233), channel_id=1, source_target_pairs={{0,4},{2,6},{4,8},{6,10},{8,12},{10,14},{1,5},{3,7},{5,9},{7,11},{... | collective-permute-start | bytes 196616 | tf_op jit(solution)/shard_map/ppermute | solution.py:391
  43.6 1.8 %collective-permute-start.11 = (bf16[512,128]{1,0:T(8,128)(2,1)S(1)}, bf16[512,128]{1,0:T(8,128)(2,1)S(1)}, u32[]{:S(2)}, u32[]{:S(2)}) collective-permute-start(bf16[512,128]{1,0:T(8,128)(2,1)S(1)} %slice.234), channel_id=1, source_target_pairs={{0,2},{2,4},{4,6},{6,8},{8,10},{10,12},{12,14},{1,3},{3,5},{5,7},{... | collective-permute-start | bytes 393224 | tf_op jit(solution)/shard_map/ppermute | solution.py:391
  46.2 1.3 collective-permute-start.13
  47.6 3.1 %collective-permute-start.8 = (bf16[2,1,2,2,32,512]{5,4,3,2,1,0:T(8,128)(2,1)S(1)}, bf16[2,1,2,2,32,512]{5,4,3,2,1,0:T(8,128)(2,1)S(1)}, u32[]{:S(2)}, u32[]{:S(2)}) collective-permute-start(bf16[2,1,2,2,32,512]{5,4,3,2,1,0:T(8,128)(2,1)S(1)} %get-tuple-element.90), channel_id=1, source_target_pairs={{0,4},{2,6},{4,0},{6,2},{8,12},{10,14},{12,8},{14,10},{1,5},{3,7},... | collective-permute-start | bytes 786440 | tf_op jit(solution)/shard_map/ppermute | solution.py:342
  50.7 2.2 %collective-permute-done.13 = bf16[272,128]{1,0:T(8,128)(2,1)S(1)} collective-permute-done((bf16[272,128]{1,0:T(8,128)(2,1)S(1)}, bf16[272,128]{1,0:T(8,128)(2,1)S(1)}, u32[]{:S(2)}, u32[]{:S(2)}) %collective-permute-start.13) | collective-permute-done | bytes 69664 | tf_op jit(solution)/shard_map/ppermute | solution.py:391
  52.8 2.4 %collective-permute-start.7 = (bf16[2,2,1,2,32,512]{5,4,3,2,1,0:T(8,128)(2,1)S(1)}, bf16[2,2,1,2,32,512]{5,4,3,2,1,0:T(8,128)(2,1)S(1)}, u32[]{:S(2)}, u32[]{:S(2)}) collective-permute-start(bf16[2,2,1,2,32,512]{5,4,3,2,1,0:T(8,128)(2,1)S(1)} %slice.180), channel_id=1, source_target_pairs={{0,2},{2,0},{4,6},{6,4},{8,10},{10,8},{12,14},{14,12},{1,3},{3,1},... | collective-permute-start | bytes 786440 | tf_op jit(solution)/shard_map/ppermute | solution.py:342
  55.7 3.9 %collective-permute-done.7 = bf16[2,2,1,2,32,512]{5,4,3,2,1,0:T(8,128)(2,1)S(1)} collective-permute-done((bf16[2,2,1,2,32,512]{5,4,3,2,1,0:T(8,128)(2,1)S(1)}, bf16[2,2,1,2,32,512]{5,4,3,2,1,0:T(8,128)(2,1)S(1)}, u32[]{:S(2)}, u32[]{:S(2)}) %collective-permute-start.7) | collective-permute-done | bytes 262176 | tf_op jit(solution)/shard_map/ppermute | solution.py:342
  59.7 1.8 %collective-permute-start.21 = (bf16[2,2,2,1,32,512]{5,4,3,2,1,0:T(8,128)(2,1)S(1)}, bf16[2,2,2,1,32,512]{5,4,3,2,1,0:T(8,128)(2,1)S(1)}, u32[]{:S(2)}, u32[]{:S(2)}) collective-permute-start(bf16[2,2,2,1,32,512]{5,4,3,2,1,0:T(8,128)(2,1)S(1)} %slice.185), channel_id=1, source_target_pairs={{0,16},{16,0},{1,17},{17,1},{2,18},{18,2},{3,19},{19,3},{4,20},{20... | collective-permute-start | bytes 786440 | tf_op jit(solution)/shard_map/ppermute | solution.py:342
  61.5 3.2 %collective-permute-start.19 = (bf16[2,1,2,2,32,512]{5,4,3,2,1,0:T(8,128)(2,1)S(1)}, bf16[2,1,2,2,32,512]{5,4,3,2,1,0:T(8,128)(2,1)S(1)}, u32[]{:S(2)}, u32[]{:S(2)}) collective-permute-start(bf16[2,1,2,2,32,512]{5,4,3,2,1,0:T(8,128)(2,1)S(1)} %get-tuple-element.66), channel_id=1, source_target_pairs={{0,4},{2,6},{4,0},{6,2},{8,12},{10,14},{12,8},{14,10},{1,5},{3,7},... | collective-permute-start | bytes 786440 | tf_op jit(solution)/shard_map/ppermute | solution.py:342
  64.6 2.0 %collective-permute-start.17 = (bf16[2,2,1,2,16,512]{5,4,3,2,1,0:T(8,128)(2,1)S(1)}, bf16[2,2,1,2,16,512]{5,4,3,2,1,0:T(8,128)(2,1)S(1)}, u32[]{:S(2)}, u32[]{:S(2)}) collective-permute-start(bf16[2,2,1,2,16,512]{5,4,3,2,1,0:T(8,128)(2,1)S(1)} %slice.183), channel_id=1, source_target_pairs={{0,2},{2,0},{4,6},{6,4},{8,10},{10,8},{12,14},{14,12},{1,3},{3,1},... | collective-permute-start | bytes 393224 | tf_op jit(solution)/shard_map/ppermute | solution.py:342
  67.3 2.4 %collective-permute-done.17 = bf16[2,2,1,2,16,512]{5,4,3,2,1,0:T(8,128)(2,1)S(1)} collective-permute-done((bf16[2,2,1,2,16,512]{5,4,3,2,1,0:T(8,128)(2,1)S(1)}, bf16[2,2,1,2,16,512]{5,4,3,2,1,0:T(8,128)(2,1)S(1)}, u32[]{:S(2)}, u32[]{:S(2)}) %collective-permute-start.17) | collective-permute-done | bytes 131104 | tf_op jit(solution)/shard_map/ppermute | solution.py:342
  71.0 0.9 maximum_select_fusion.4
  73.6 1.0 copy-done.30
  74.6 1.0 copy-done.34
  75.6 7.8 %shard_map.121 = (bf16[2048,512]{1,0:T(8,128)(2,1)S(1)}, bf16[1792,512]{1,0:T(8,128)(2,1)S(1)}, bf16[512,512]{1,0:T(8,128)(2,1)S(1)}, bf16[768,512]{1,0:T(8,128)...) custom-call(s32[4]{0:T(128)S(1)} %pad_add_fusion.scalar_ref.site_ref, ...), custom_call_target="tpu_custom_call" | custom-call | flops 5637144576 | bytes 12189712 | tf_op jit(solution)/shard_map/pallas_call | solution.py:37
  83.4 1.3 copy-done
  84.7 1.0 copy-done.8
  85.7 0.9 copy-done.16
  88.2 12.8 %shard_map.122 = (f32[4,128]{1,0:T(4,128)}, bf16[8,168,512]{2,1,0:T(8,128)(2,1)S(1)}, bf16[8,168,512]{2,1,0:T(8,128)(2,1)}, bf16[1280,1024]{1,0:T(8,128)(2,1)S(1...) custom-call(s32[4]{0:T(128)S(1)} %pad_add_fusion.scalar_ref.site_ref, ...), custom_call_target="tpu_custom_call" | custom-call | flops 5368709120 | bytes 13636112 | tf_op jit(solution)/shard_map/pallas_call | solution.py:37
  101.0 1.2 copy-done.2
  102.2 1.1 copy-done.4
  103.3 1.0 copy-done.12
  104.3 1.0 copy-done.14
  105.7 1.4 copy-done.3
  107.2 1.2 copy-done.13
  108.4 1.2 copy-done.15
  109.6 1.1 copy-done.17
  110.7 1.0 copy-done.23
  111.8 2.5 %shard_map.123 = (f32[768,512]{1,0:T(8,128)S(1)}, bf16[768,512]{1,0:T(8,128)(2,1)S(1)}, bf16[768,1024]{1,0:T(8,128)(2,1)S(1)}) custom-call(bf16[1280,1024]{1,0:T(8,128)(2,1)S(1)} %get-tuple-element.71.back1_ref, f32[768,512]{1,0:T(8,128)S(1)} %copy-done.3, bf16[16,64,512]{2,1,0:T(8,128)(2,1)S(1)} %copy-done.13, bf16[16,64,512]{2,1,0:T(8,128)(2,1)S(1)} %copy-done.15, ...), custom_call_target="tpu_custom_call" | custom-call | flops 2013265920 | bytes 12320768 | tf_op jit(solution)/shard_map/pallas_call | solution.py:37
  114.4 1.8 %add_convert_fusion.1 = bf16[8,168,512]{2,1,0:T(8,128)(2,1)S(1)} fusion(bf16[8,168,512]{2,1,0:T(8,128)(2,1)} %collective-permute-done.23, bf16[8,168,512]{2,1,0:T(8,128)(2,1)S(1)} %copy-done.5), kind=kLoop, calls=%fused_computation.1 | loop fusion | flops 2752512 | bytes 4128768 | tf_op jit(solution)/shard_map/convert_element_type | solution.py:510
  116.5 2.1 %collective-permute-start.32 = (bf16[2,2,1,88,512]{4,3,2,1,0:T(8,128)(2,1)S(1)}, bf16[2,2,1,88,512]{4,3,2,1,0:T(8,128)(2,1)S(1)}, u32[]{:S(2)}, u32[]{:S(2)}) collective-permute-start(bf16[2,2,1,88,512]{4,3,2,1,0:T(8,128)(2,1)S(1)} %constant_dynamic-slice_fusion.1), channel_id=1, source_target_pairs={{0,2},{2,0},{4,6},{6,4},{8,10},{10,8},{12,14},{14,12},{1,3},{3,1},... | collective-permute-start | bytes 1081352 | tf_op jit(solution)/shard_map/ppermute | solution.py:342
  118.6 3.7 %shard_map.124 = (bf16[8,168,512]{2,1,0:T(8,128)(2,1)S(1)}, bf16[8,168,512]{2,1,0:T(8,128)(2,1)S(1)}) custom-call(s32[4]{0:T(128)S(1)} %pad_add_fusion.scalar_ref.site_ref, bf16[768,1024]{1,0:T(8,128)(2,1)S(1)} %get-tuple-element.79.back_ref, f32[768,512]{1,0:T(8,128)S(1)} %get-tuple-element.80.grad_ref, bf16[768,512]{1,0:T(8,128)(2,1)S(1)} %get-tuple-element.81.round_ref, ...), custom_call_target="tpu_custom_call" | custom-call | flops 2415919104 | bytes 11927568 | tf_op jit(solution)/shard_map/pallas_call | solution.py:37
  122.4 3.7 %collective-permute-done.30 = bf16[2,1,2,80,512]{4,3,2,1,0:T(8,128)(2,1)S(1)} collective-permute-done((bf16[2,1,2,80,512]{4,3,2,1,0:T(8,128)(2,1)S(1)}, bf16[2,1,2,80,512]{4,3,2,1,0:T(8,128)(2,1)S(1)}, u32[]{:S(2)}, u32[]{:S(2)}) %collective-permute-start.30) | collective-permute-done | bytes 327712 | tf_op jit(solution)/shard_map/ppermute | solution.py:342
  126.3 2.1 %collective-permute-start.31 = (bf16[2,1,1,80,512]{4,3,2,1,0:T(8,128)(2,1)S(1)}, bf16[2,1,1,80,512]{4,3,2,1,0:T(8,128)(2,1)S(1)}, u32[]{:S(2)}, u32[]{:S(2)}) collective-permute-start(bf16[2,1,1,80,512]{4,3,2,1,0:T(8,128)(2,1)S(1)} %constant_dynamic-slice_fusion.2), channel_id=1, source_target_pairs={{0,2},{2,0},{4,6},{6,4},{8,10},{10,8},{12,14},{14,12},{1,3},{3,1},... | collective-permute-start | bytes 491528 | tf_op jit(solution)/shard_map/ppermute | solution.py:342
  129.2 2.7 %collective-permute-done.31 = bf16[2,1,1,80,512]{4,3,2,1,0:T(8,128)(2,1)S(1)} collective-permute-done((bf16[2,1,1,80,512]{4,3,2,1,0:T(8,128)(2,1)S(1)}, bf16[2,1,1,80,512]{4,3,2,1,0:T(8,128)(2,1)S(1)}, u32[]{:S(2)}, u32[]{:S(2)}) %collective-permute-start.31) | collective-permute-done | bytes 163872 | tf_op jit(solution)/shard_map/ppermute | solution.py:342
  132.0 2.1 %collective-permute-done.33 = bf16[2,1,1,88,512]{4,3,2,1,0:T(8,128)(2,1)S(1)} collective-permute-done((bf16[2,1,1,88,512]{4,3,2,1,0:T(8,128)(2,1)S(1)}, bf16[2,1,1,88,512]{4,3,2,1,0:T(8,128)(2,1)S(1)}, u32[]{:S(2)}, u32[]{:S(2)}) %collective-permute-start.33) | collective-permute-done | bytes 180256 | tf_op jit(solution)/shard_map/ppermute | solution.py:342
  134.1 0.9 collective-permute-start.34
  135.0 8.0 %collective-permute-done.34 = bf16[1,1,1,168,512]{4,3,2,1,0:T(8,128)(2,1)S(1)} collective-permute-done((bf16[1,1,1,168,512]{4,3,2,1,0:T(8,128)(2,1)S(1)}, bf16[1,1,1,168,512]{4,3,2,1,0:T(8,128)(2,1)S(1)}, u32[]{:S(2)}, u32[]{:S(2)}) %collective-permute-start.34) | collective-permute-done | bytes 172064 | tf_op jit(solution)/shard_map/ppermute | solution.py:342
  143.1 1.7 %add_convert_fusion = bf16[8,168,512]{2,1,0:T(8,128)(2,1)S(1)} fusion(bf16[8,168,512]{2,1,0:T(8,128)(2,1)} %collective-permute-done.24, bf16[8,168,512]{2,1,0:T(8,128)(2,1)S(1)} %get-tuple-element.86), kind=kLoop, calls=%fused_computation | loop fusion | flops 2752512 | bytes 4128768 | tf_op jit(solution)/shard_map/convert_element_type | solution.py:519
  145.2 1.1 collective-permute-start.27
  146.3 7.2 %collective-permute-done.25 = bf16[2,1,2,80,512]{4,3,2,1,0:T(8,128)(2,1)S(1)} collective-permute-done((bf16[2,1,2,80,512]{4,3,2,1,0:T(8,128)(2,1)S(1)}, bf16[2,1,2,80,512]{4,3,2,1,0:T(8,128)(2,1)S(1)}, u32[]{:S(2)}, u32[]{:S(2)}) %collective-permute-start.25) | collective-permute-done | bytes 327712 | tf_op jit(solution)/shard_map/ppermute | solution.py:342
  153.7 1.4 collective-permute-start.26
  155.3 2.3 %collective-permute-start.28 = (bf16[2,1,1,88,512]{4,3,2,1,0:T(8,128)(2,1)S(1)}, bf16[2,1,1,88,512]{4,3,2,1,0:T(8,128)(2,1)S(1)}, u32[]{:S(2)}, u32[]{:S(2)}) collective-permute-start(bf16[2,1,1,88,512]{4,3,2,1,0:T(8,128)(2,1)S(1)} %constant_dynamic-slice_fusion.4), channel_id=1, source_target_pairs={{0,4},{2,6},{4,0},{6,2},{8,12},{10,14},{12,8},{14,10},{1,5},{3,7},... | collective-permute-start | bytes 540680 | tf_op jit(solution)/shard_map/ppermute | solution.py:342
  157.6 1.5 collective-permute-done.26
  159.1 3.3 %collective-permute-done.28 = bf16[2,1,1,88,512]{4,3,2,1,0:T(8,128)(2,1)S(1)} collective-permute-done((bf16[2,1,1,88,512]{4,3,2,1,0:T(8,128)(2,1)S(1)}, bf16[2,1,1,88,512]{4,3,2,1,0:T(8,128)(2,1)S(1)}, u32[]{:S(2)}, u32[]{:S(2)}) %collective-permute-start.28) | collective-permute-done | bytes 180256 | tf_op jit(solution)/shard_map/ppermute | solution.py:342
  162.5 0.9 collective-permute-start.29
  164.0 4.9 %collective-permute-done.29 = bf16[1,1,1,168,512]{4,3,2,1,0:T(8,128)(2,1)S(1)} collective-permute-done((bf16[1,1,1,168,512]{4,3,2,1,0:T(8,128)(2,1)S(1)}, bf16[1,1,1,168,512]{4,3,2,1,0:T(8,128)(2,1)S(1)}, u32[]{:S(2)}, u32[]{:S(2)}) %collective-permute-start.29) | collective-permute-done | bytes 172064 | tf_op jit(solution)/shard_map/ppermute | solution.py:342
  170.3 0.8 pad_maximum_fusion
  (167 shorter events, 15.3 us)
Async XLA Ops:
  2.1 1.0 copy-start.10
  3.0 0.9 copy-start.26
  4.0 0.9 copy-start.27
  8.3 12.4 %collective-permute-start = (bf16[1,1,1,1,176,512]{5,4,3,2,1,0:T(8,128)(2,1)S(1)}, bf16[1,1,1,1,176,512]{5,4,3,2,1,0:T(8,128)(2,1)S(1)}, u32[]{:S(2)}, u32[]{:S(2)}) collective-permute-start(bf16[1,1,1,1,176,512]{5,4,3,2,1,0:T(8,128)(2,1)S(1)} %bitcast.66), channel_id=1, source_target_pairs={{0,8},{2,10},{4,12},{6,14},{8,0},{10,2},{12,4},{14,6},{1,9},{3,11}... | collective-permute-start | bytes 540680 | tf_op jit(solution)/shard_map/ppermute | solution.py:342
  20.8 4.7 %collective-permute-start.1 = (bf16[2,1,1,1,48,512]{5,4,3,2,1,0:T(8,128)(2,1)S(1)}, bf16[2,1,1,1,48,512]{5,4,3,2,1,0:T(8,128)(2,1)S(1)}, u32[]{:S(2)}, u32[]{:S(2)}) collective-permute-start(bf16[2,1,1,1,48,512]{5,4,3,2,1,0:T(8,128)(2,1)S(1)} %slice.227), channel_id=1, source_target_pairs={{0,16},{16,0},{1,17},{17,1},{2,18},{18,2},{3,19},{19,3},{4,20},{20... | collective-permute-start | bytes 294920 | tf_op jit(solution)/shard_map/ppermute | solution.py:342
  22.4 5.0 %collective-permute-start.3 = (bf16[2,1,1,1,64,512]{5,4,3,2,1,0:T(8,128)(2,1)S(1)}, bf16[2,1,1,1,64,512]{5,4,3,2,1,0:T(8,128)(2,1)S(1)}, u32[]{:S(2)}, u32[]{:S(2)}) collective-permute-start(bf16[2,1,1,1,64,512]{5,4,3,2,1,0:T(8,128)(2,1)S(1)} %get-tuple-element.50), channel_id=1, source_target_pairs={{0,4},{2,6},{4,0},{6,2},{8,12},{10,14},{12,8},{14,10},{1,5},{3,7},... | collective-permute-start | bytes 393224 | tf_op jit(solution)/shard_map/ppermute | solution.py:342
  23.1 5.0 %collective-permute-start.2 = (bf16[2,1,1,1,64,512]{5,4,3,2,1,0:T(8,128)(2,1)S(1)}, bf16[2,1,1,1,64,512]{5,4,3,2,1,0:T(8,128)(2,1)S(1)}, u32[]{:S(2)}, u32[]{:S(2)}) collective-permute-start(bf16[2,1,1,1,64,512]{5,4,3,2,1,0:T(8,128)(2,1)S(1)} %get-tuple-element.49), channel_id=1, source_target_pairs={{0,2},{2,0},{4,6},{6,4},{8,10},{10,8},{12,14},{14,12},{1,3},{3,1},... | collective-permute-start | bytes 393224 | tf_op jit(solution)/shard_map/ppermute | solution.py:342
  27.4 8.5 %copy-start.11 = (f32[1,512,128]{2,1,0:T(8,128)S(1)}, f32[1,512,128]{2,1,0:T(8,128)}, u32[]{:S(2)}) copy-start(f32[1,512,128]{2,1,0:T(8,128)} %param.8) | copy-start | bytes 786436
  27.4 8.5 %copy-start.32 = (s32[1,512]{1,0:T(1,128)S(1)}, s32[1,512]{1,0:T(1,128)}, u32[]{:S(2)}) copy-start(s32[1,512]{1,0:T(1,128)} %param.10) | copy-start | bytes 6148
  28.1 5.7 %collective-permute-start.4 = (bf16[2,1,1,2,48,512]{5,4,3,2,1,0:T(8,128)(2,1)S(1)}, bf16[2,1,1,2,48,512]{5,4,3,2,1,0:T(8,128)(2,1)S(1)}, u32[]{:S(2)}, u32[]{:S(2)}) collective-permute-start(bf16[2,1,1,2,48,512]{5,4,3,2,1,0:T(8,128)(2,1)S(1)} %maximum_select_fusion.13), channel_id=1, source_target_pairs={{0,4},{2,6},{4,0},{6,2},{8,12},{10,14},{12,8},{14,10},{1,5},{3,7},... | collective-permute-start | bytes 589832 | tf_op jit(solution)/shard_map/ppermute | solution.py:342
  29.5 6.4 %collective-permute-start.6 = (bf16[2,2,1,1,64,512]{5,4,3,2,1,0:T(8,128)(2,1)S(1)}, bf16[2,2,1,1,64,512]{5,4,3,2,1,0:T(8,128)(2,1)S(1)}, u32[]{:S(2)}, u32[]{:S(2)}) collective-permute-start(bf16[2,2,1,1,64,512]{5,4,3,2,1,0:T(8,128)(2,1)S(1)} %maximum_select_fusion.10), channel_id=1, source_target_pairs={{0,2},{2,0},{4,6},{6,4},{8,10},{10,8},{12,14},{14,12},{1,3},{3,1},... | collective-permute-start | bytes 786440 | tf_op jit(solution)/shard_map/ppermute | solution.py:342
  31.0 14.4 %collective-permute-start.5 = (bf16[2,1,2,1,64,512]{5,4,3,2,1,0:T(8,128)(2,1)S(1)}, bf16[2,1,2,1,64,512]{5,4,3,2,1,0:T(8,128)(2,1)S(1)}, u32[]{:S(2)}, u32[]{:S(2)}) collective-permute-start(bf16[2,1,2,1,64,512]{5,4,3,2,1,0:T(8,128)(2,1)S(1)} %maximum_select_fusion.9), channel_id=1, source_target_pairs={{0,16},{16,0},{1,17},{17,1},{2,18},{18,2},{3,19},{19,3},{4,20},{20... | collective-permute-start | bytes 786440 | tf_op jit(solution)/shard_map/ppermute | solution.py:342
  36.7 18.6 %collective-permute-start.12 = (bf16[528,128]{1,0:T(8,128)(2,1)S(1)}, bf16[528,128]{1,0:T(8,128)(2,1)S(1)}, u32[]{:S(2)}, u32[]{:S(2)}) collective-permute-start(bf16[528,128]{1,0:T(8,128)(2,1)S(1)} %shard_map.120), channel_id=1, source_target_pairs={{2,0},{4,2},{6,4},{8,6},{10,8},{12,10},{14,12},{3,1},{5,3},{7,5},{... | collective-permute-start | bytes 405512 | tf_op jit(solution)/shard_map/ppermute | solution.py:391
  38.1 9.5 %collective-permute-start.10 = (bf16[256,128]{1,0:T(8,128)(2,1)S(1)}, bf16[256,128]{1,0:T(8,128)(2,1)S(1)}, u32[]{:S(2)}, u32[]{:S(2)}) collective-permute-start(bf16[256,128]{1,0:T(8,128)(2,1)S(1)} %slice.233), channel_id=1, source_target_pairs={{0,4},{2,6},{4,8},{6,10},{8,12},{10,14},{1,5},{3,7},{5,9},{7,11},{... | collective-permute-start | bytes 196616 | tf_op jit(solution)/shard_map/ppermute | solution.py:391
  43.6 11.7 %collective-permute-start.11 = (bf16[512,128]{1,0:T(8,128)(2,1)S(1)}, bf16[512,128]{1,0:T(8,128)(2,1)S(1)}, u32[]{:S(2)}, u32[]{:S(2)}) collective-permute-start(bf16[512,128]{1,0:T(8,128)(2,1)S(1)} %slice.234), channel_id=1, source_target_pairs={{0,2},{2,4},{4,6},{6,8},{8,10},{10,12},{12,14},{1,3},{3,5},{5,7},{... | collective-permute-start | bytes 393224 | tf_op jit(solution)/shard_map/ppermute | solution.py:391
  45.5 9.9 %collective-permute-start.9 = (bf16[2,2,2,1,24,512]{5,4,3,2,1,0:T(8,128)(2,1)S(1)}, bf16[2,2,2,1,24,512]{5,4,3,2,1,0:T(8,128)(2,1)S(1)}, u32[]{:S(2)}, u32[]{:S(2)}) collective-permute-start(bf16[2,2,2,1,24,512]{5,4,3,2,1,0:T(8,128)(2,1)S(1)} %slice.182), channel_id=1, source_target_pairs={{0,16},{16,0},{1,17},{17,1},{2,18},{18,2},{3,19},{19,3},{4,20},{20... | collective-permute-start | bytes 589832 | tf_op jit(solution)/shard_map/ppermute | solution.py:342
  46.2 6.6 %collective-permute-start.13 = (bf16[272,128]{1,0:T(8,128)(2,1)S(1)}, bf16[272,128]{1,0:T(8,128)(2,1)S(1)}, u32[]{:S(2)}, u32[]{:S(2)}) collective-permute-start(bf16[272,128]{1,0:T(8,128)(2,1)S(1)} %slice.236), channel_id=1, source_target_pairs={{4,0},{6,2},{8,4},{10,6},{12,8},{14,10},{5,1},{7,3},{9,5},{11,7},{... | collective-permute-start | bytes 208904 | tf_op jit(solution)/shard_map/ppermute | solution.py:391
  47.6 8.1 %collective-permute-start.8 = (bf16[2,1,2,2,32,512]{5,4,3,2,1,0:T(8,128)(2,1)S(1)}, bf16[2,1,2,2,32,512]{5,4,3,2,1,0:T(8,128)(2,1)S(1)}, u32[]{:S(2)}, u32[]{:S(2)}) collective-permute-start(bf16[2,1,2,2,32,512]{5,4,3,2,1,0:T(8,128)(2,1)S(1)} %get-tuple-element.90), channel_id=1, source_target_pairs={{0,4},{2,6},{4,0},{6,2},{8,12},{10,14},{12,8},{14,10},{1,5},{3,7},... | collective-permute-start | bytes 786440 | tf_op jit(solution)/shard_map/ppermute | solution.py:342
  52.8 6.8 %collective-permute-start.7 = (bf16[2,2,1,2,32,512]{5,4,3,2,1,0:T(8,128)(2,1)S(1)}, bf16[2,2,1,2,32,512]{5,4,3,2,1,0:T(8,128)(2,1)S(1)}, u32[]{:S(2)}, u32[]{:S(2)}) collective-permute-start(bf16[2,2,1,2,32,512]{5,4,3,2,1,0:T(8,128)(2,1)S(1)} %slice.180), channel_id=1, source_target_pairs={{0,2},{2,0},{4,6},{6,4},{8,10},{10,8},{12,14},{14,12},{1,3},{3,1},... | collective-permute-start | bytes 786440 | tf_op jit(solution)/shard_map/ppermute | solution.py:342
  55.4 18.2 %copy-start.18 = (bf16[2048,128]{1,0:T(8,128)(2,1)}, bf16[2048,128]{1,0:T(8,128)(2,1)S(1)}, u32[]{:S(2)}) copy-start(bf16[2048,128]{1,0:T(8,128)(2,1)S(1)} %slice_dynamic-update-slice_fusion.1.norm_ref) | copy-start | bytes 1572868
  59.7 10.7 %collective-permute-start.21 = (bf16[2,2,2,1,32,512]{5,4,3,2,1,0:T(8,128)(2,1)S(1)}, bf16[2,2,2,1,32,512]{5,4,3,2,1,0:T(8,128)(2,1)S(1)}, u32[]{:S(2)}, u32[]{:S(2)}) collective-permute-start(bf16[2,2,2,1,32,512]{5,4,3,2,1,0:T(8,128)(2,1)S(1)} %slice.185), channel_id=1, source_target_pairs={{0,16},{16,0},{1,17},{17,1},{2,18},{18,2},{3,19},{19,3},{4,20},{20... | collective-permute-start | bytes 786440 | tf_op jit(solution)/shard_map/ppermute | solution.py:342
  61.5 9.5 %collective-permute-start.19 = (bf16[2,1,2,2,32,512]{5,4,3,2,1,0:T(8,128)(2,1)S(1)}, bf16[2,1,2,2,32,512]{5,4,3,2,1,0:T(8,128)(2,1)S(1)}, u32[]{:S(2)}, u32[]{:S(2)}) collective-permute-start(bf16[2,1,2,2,32,512]{5,4,3,2,1,0:T(8,128)(2,1)S(1)} %get-tuple-element.66), channel_id=1, source_target_pairs={{0,4},{2,6},{4,0},{6,2},{8,12},{10,14},{12,8},{14,10},{1,5},{3,7},... | collective-permute-start | bytes 786440 | tf_op jit(solution)/shard_map/ppermute | solution.py:342
  64.6 5.0 %collective-permute-start.17 = (bf16[2,2,1,2,16,512]{5,4,3,2,1,0:T(8,128)(2,1)S(1)}, bf16[2,2,1,2,16,512]{5,4,3,2,1,0:T(8,128)(2,1)S(1)}, u32[]{:S(2)}, u32[]{:S(2)}) collective-permute-start(bf16[2,2,1,2,16,512]{5,4,3,2,1,0:T(8,128)(2,1)S(1)} %slice.183), channel_id=1, source_target_pairs={{0,2},{2,0},{4,6},{6,4},{8,10},{10,8},{12,14},{14,12},{1,3},{3,1},... | collective-permute-start | bytes 393224 | tf_op jit(solution)/shard_map/ppermute | solution.py:342
  66.7 5.2 %collective-permute-start.14 = (bf16[8,2,24,512]{3,2,1,0:T(8,128)(2,1)S(1)}, bf16[8,2,24,512]{3,2,1,0:T(8,128)(2,1)S(1)}, u32[]{:S(2)}, u32[]{:S(2)}) collective-permute-start(bf16[8,2,24,512]{3,2,1,0:T(8,128)(2,1)S(1)} %bitcast.57), channel_id=1, source_target_pairs={{0,1},{1,0},{2,3},{3,2},{4,5},{5,4},{6,7},{7,6},{8,9},{9,8},{10,11... | collective-permute-start | bytes 1179656 | tf_op jit(solution)/shard_map/ppermute | solution.py:342
  66.7 6.1 %collective-permute-start.15 = (bf16[8,2,32,512]{3,2,1,0:T(8,128)(2,1)S(1)}, bf16[8,2,32,512]{3,2,1,0:T(8,128)(2,1)S(1)}, u32[]{:S(2)}, u32[]{:S(2)}) collective-permute-start(bf16[8,2,32,512]{3,2,1,0:T(8,128)(2,1)S(1)} %bitcast.62), channel_id=1, source_target_pairs={{0,1},{1,0},{2,3},{3,2},{4,5},{5,4},{6,7},{7,6},{8,9},{9,8},{10,11... | collective-permute-start | bytes 1572872 | tf_op jit(solution)/shard_map/ppermute | solution.py:342
  69.6 4.0 %collective-permute-start.16 = (bf16[8,2,32,512]{3,2,1,0:T(8,128)(2,1)S(1)}, bf16[8,2,32,512]{3,2,1,0:T(8,128)(2,1)}, u32[]{:S(2)}, u32[]{:S(2)}) collective-permute-start(bf16[8,2,32,512]{3,2,1,0:T(8,128)(2,1)S(1)} %bitcast.60), channel_id=1, source_target_pairs={{0,1},{1,0},{2,3},{3,2},{4,5},{5,4},{6,7},{7,6},{8,9},{9,8},{10,11... | collective-permute-start | bytes 1572872 | tf_op jit(solution)/shard_map/ppermute | solution.py:342
  70.3 17.9 %collective-permute-start.18 = (bf16[8,2,16,512]{3,2,1,0:T(8,128)(2,1)}, bf16[8,2,16,512]{3,2,1,0:T(8,128)(2,1)}, u32[]{:S(2)}, u32[]{:S(2)}) collective-permute-start(bf16[8,2,16,512]{3,2,1,0:T(8,128)(2,1)} %bitcast.14.a_ref), channel_id=1, source_target_pairs={{0,1},{1,0},{2,3},{3,2},{4,5},{5,4},{6,7},{7,6},{8,9},{9,8},{10,11... | collective-permute-start | bytes 786440 | tf_op jit(solution)/shard_map/ppermute | solution.py:342
  70.9 1.7 %copy-start.24 = (bf16[8,2,32,512]{3,2,1,0:T(8,128)(2,1)}, bf16[8,2,32,512]{3,2,1,0:T(8,128)(2,1)S(1)}, u32[]{:S(2)}) copy-start(bf16[8,2,32,512]{3,2,1,0:T(8,128)(2,1)S(1)} %maximum_select_fusion.5.c_ref) | copy-start | bytes 1572868
  70.9 17.3 %collective-permute-start.22 = (bf16[8,2,32,512]{3,2,1,0:T(8,128)(2,1)S(1)}, bf16[8,2,32,512]{3,2,1,0:T(8,128)(2,1)}, u32[]{:S(2)}, u32[]{:S(2)}) collective-permute-start(bf16[8,2,32,512]{3,2,1,0:T(8,128)(2,1)S(1)} %maximum_select_fusion.5.c_ref), channel_id=1, source_target_pairs={{0,1},{1,0},{2,3},{3,2},{4,5},{5,4},{6,7},{7,6},{8,9},{9,8},{10,11... | collective-permute-start | bytes 1572872 | tf_op jit(solution)/shard_map/ppermute | solution.py:342
  71.9 16.3 %collective-permute-start.20 = (bf16[8,2,32,512]{3,2,1,0:T(8,128)(2,1)}, bf16[8,2,32,512]{3,2,1,0:T(8,128)(2,1)}, u32[]{:S(2)}, u32[]{:S(2)}) collective-permute-start(bf16[8,2,32,512]{3,2,1,0:T(8,128)(2,1)} %bitcast.15.b_ref), channel_id=1, source_target_pairs={{0,1},{1,0},{2,3},{3,2},{4,5},{5,4},{6,7},{7,6},{8,9},{9,8},{10,11... | collective-permute-start | bytes 1572872 | tf_op jit(solution)/shard_map/ppermute | solution.py:342
  73.6 1.0 copy-start.30
  74.6 1.0 copy-start.34
  75.6 12.6 %copy-start.25 = (bf16[8,2,32,512]{3,2,1,0:T(8,128)(2,1)S(1)}, bf16[8,2,32,512]{3,2,1,0:T(8,128)(2,1)}, u32[]{:S(2)}) copy-start(bf16[8,2,32,512]{3,2,1,0:T(8,128)(2,1)} %copy-done.24) | copy-start | bytes 1572868
  83.4 1.3 copy-start
  84.7 1.0 copy-start.8
  85.7 0.9 copy-start.16
  88.2 12.8 %copy-start.6 = (bf16[16,64,512]{2,1,0:T(8,128)(2,1)}, bf16[16,64,512]{2,1,0:T(8,128)(2,1)S(1)}, u32[]{:S(2)}) copy-start(bf16[16,64,512]{2,1,0:T(8,128)(2,1)S(1)} %get-tuple-element.84.filt_ref) | copy-start | bytes 3145732
  101.0 1.2 copy-start.2
  102.2 1.1 copy-start.4
  103.3 1.0 copy-start.12
  104.3 1.0 copy-start.14
  105.3 9.1 %collective-permute-start.23 = (bf16[8,168,512]{2,1,0:T(8,128)(2,1)}, bf16[8,168,512]{2,1,0:T(8,128)(2,1)}, u32[]{:S(2)}, u32[]{:S(2)}) collective-permute-start(bf16[8,168,512]{2,1,0:T(8,128)(2,1)} %get-tuple-element.70), channel_id=1, source_target_pairs={{0,1},{1,0},{2,3},{3,2},{4,5},{5,4},{6,7},{7,6},{8,9},{9,8},{10,11... | collective-permute-start | bytes 4128776 | tf_op jit(solution)/shard_map/ppermute | solution.py:342
  105.7 1.4 copy-start.3
  107.1 1.2 copy-start.13
  108.4 1.2 copy-start.15
  109.6 1.1 copy-start.17
  110.7 1.0 copy-start.23
  111.8 2.6 %copy-start.5 = (bf16[8,168,512]{2,1,0:T(8,128)(2,1)S(1)}, bf16[8,168,512]{2,1,0:T(8,128)(2,1)}, u32[]{:S(2)}) copy-start(bf16[8,168,512]{2,1,0:T(8,128)(2,1)} %copy-done.4) | copy-start | bytes 4128772
  114.4 4.3 %copy-start.9 = (bf16[16,64,512]{2,1,0:T(8,128)(2,1)S(1)}, bf16[16,64,512]{2,1,0:T(8,128)(2,1)}, u32[]{:S(2)}) copy-start(bf16[16,64,512]{2,1,0:T(8,128)(2,1)} %copy-done.8) | copy-start | bytes 3145732
  114.4 4.3 %copy-start.21 = (bf16[512,512]{1,0:T(8,128)(2,1)S(1)}, bf16[512,512]{1,0:T(8,128)(2,1)}, u32[]{:S(2)}) copy-start(bf16[512,512]{1,0:T(8,128)(2,1)} %copy-done.20) | copy-start | bytes 1572868
  116.2 2.4 %copy-start.7 = (bf16[16,64,512]{2,1,0:T(8,128)(2,1)S(1)}, bf16[16,64,512]{2,1,0:T(8,128)(2,1)}, u32[]{:S(2)}) copy-start(bf16[16,64,512]{2,1,0:T(8,128)(2,1)} %copy-done.6) | copy-start | bytes 3145732
  116.3 2.4 %copy-start.1 = (bf16[2048,512]{1,0:T(8,128)(2,1)S(1)}, bf16[2048,512]{1,0:T(8,128)(2,1)}, u32[]{:S(2)}) copy-start(bf16[2048,512]{1,0:T(8,128)(2,1)} %copy-done) | copy-start | bytes 6291460
  116.3 2.4 %copy-start.19 = (bf16[2048,128]{1,0:T(8,128)(2,1)S(1)}, bf16[2048,128]{1,0:T(8,128)(2,1)}, u32[]{:S(2)}) copy-start(bf16[2048,128]{1,0:T(8,128)(2,1)} %copy-done.18) | copy-start | bytes 1572868
  116.4 9.7 %collective-permute-start.30 = (bf16[2,1,2,80,512]{4,3,2,1,0:T(8,128)(2,1)S(1)}, bf16[2,1,2,80,512]{4,3,2,1,0:T(8,128)(2,1)S(1)}, u32[]{:S(2)}, u32[]{:S(2)}) collective-permute-start(bf16[2,1,2,80,512]{4,3,2,1,0:T(8,128)(2,1)S(1)} %constant_dynamic-slice_fusion.3), channel_id=1, source_target_pairs={{0,4},{2,6},{4,0},{6,2},{8,12},{10,14},{12,8},{14,10},{1,5},{3,7},... | collective-permute-start | bytes 983048 | tf_op jit(solution)/shard_map/ppermute | solution.py:342
  116.5 11.8 %collective-permute-start.32 = (bf16[2,2,1,88,512]{4,3,2,1,0:T(8,128)(2,1)S(1)}, bf16[2,2,1,88,512]{4,3,2,1,0:T(8,128)(2,1)S(1)}, u32[]{:S(2)}, u32[]{:S(2)}) collective-permute-start(bf16[2,2,1,88,512]{4,3,2,1,0:T(8,128)(2,1)S(1)} %constant_dynamic-slice_fusion.1), channel_id=1, source_target_pairs={{0,2},{2,0},{4,6},{6,4},{8,10},{10,8},{12,14},{14,12},{1,3},{3,1},... | collective-permute-start | bytes 1081352 | tf_op jit(solution)/shard_map/ppermute | solution.py:342
  122.3 20.8 %collective-permute-start.24 = (bf16[8,168,512]{2,1,0:T(8,128)(2,1)S(1)}, bf16[8,168,512]{2,1,0:T(8,128)(2,1)}, u32[]{:S(2)}, u32[]{:S(2)}) collective-permute-start(bf16[8,168,512]{2,1,0:T(8,128)(2,1)S(1)} %get-tuple-element.87), channel_id=1, source_target_pairs={{0,1},{1,0},{2,3},{3,2},{4,5},{5,4},{6,7},{7,6},{8,9},{9,8},{10,11... | collective-permute-start | bytes 4128776 | tf_op jit(solution)/shard_map/ppermute | solution.py:342
  126.3 5.6 %collective-permute-start.31 = (bf16[2,1,1,80,512]{4,3,2,1,0:T(8,128)(2,1)S(1)}, bf16[2,1,1,80,512]{4,3,2,1,0:T(8,128)(2,1)S(1)}, u32[]{:S(2)}, u32[]{:S(2)}) collective-permute-start(bf16[2,1,1,80,512]{4,3,2,1,0:T(8,128)(2,1)S(1)} %constant_dynamic-slice_fusion.2), channel_id=1, source_target_pairs={{0,2},{2,0},{4,6},{6,4},{8,10},{10,8},{12,14},{14,12},{1,3},{3,1},... | collective-permute-start | bytes 491528 | tf_op jit(solution)/shard_map/ppermute | solution.py:342
  128.5 5.6 %collective-permute-start.33 = (bf16[2,1,1,88,512]{4,3,2,1,0:T(8,128)(2,1)S(1)}, bf16[2,1,1,88,512]{4,3,2,1,0:T(8,128)(2,1)S(1)}, u32[]{:S(2)}, u32[]{:S(2)}) collective-permute-start(bf16[2,1,1,88,512]{4,3,2,1,0:T(8,128)(2,1)S(1)} %constant_dynamic-slice_fusion), channel_id=1, source_target_pairs={{0,4},{2,6},{4,0},{6,2},{8,12},{10,14},{12,8},{14,10},{1,5},{3,7},... | collective-permute-start | bytes 540680 | tf_op jit(solution)/shard_map/ppermute | solution.py:342
  134.1 8.9 %collective-permute-start.34 = (bf16[1,1,1,168,512]{4,3,2,1,0:T(8,128)(2,1)S(1)}, bf16[1,1,1,168,512]{4,3,2,1,0:T(8,128)(2,1)S(1)}, u32[]{:S(2)}, u32[]{:S(2)}) collective-permute-start(bf16[1,1,1,168,512]{4,3,2,1,0:T(8,128)(2,1)S(1)} %fusion), channel_id=1, source_target_pairs={{0,8},{2,10},{4,12},{6,14},{8,0},{10,2},{12,4},{14,6},{1,9},{3,11}... | collective-permute-start | bytes 516104 | tf_op jit(solution)/shard_map/ppermute | solution.py:342
  145.0 8.6 %collective-permute-start.25 = (bf16[2,1,2,80,512]{4,3,2,1,0:T(8,128)(2,1)S(1)}, bf16[2,1,2,80,512]{4,3,2,1,0:T(8,128)(2,1)S(1)}, u32[]{:S(2)}, u32[]{:S(2)}) collective-permute-start(bf16[2,1,2,80,512]{4,3,2,1,0:T(8,128)(2,1)S(1)} %constant_dynamic-slice_fusion.7), channel_id=1, source_target_pairs={{0,4},{2,6},{4,0},{6,2},{8,12},{10,14},{12,8},{14,10},{1,5},{3,7},... | collective-permute-start | bytes 983048 | tf_op jit(solution)/shard_map/ppermute | solution.py:342
  145.2 9.9 %collective-permute-start.27 = (bf16[2,2,1,88,512]{4,3,2,1,0:T(8,128)(2,1)S(1)}, bf16[2,2,1,88,512]{4,3,2,1,0:T(8,128)(2,1)S(1)}, u32[]{:S(2)}, u32[]{:S(2)}) collective-permute-start(bf16[2,2,1,88,512]{4,3,2,1,0:T(8,128)(2,1)S(1)} %constant_dynamic-slice_fusion.5), channel_id=1, source_target_pairs={{0,2},{2,0},{4,6},{6,4},{8,10},{10,8},{12,14},{14,12},{1,3},{3,1},... | collective-permute-start | bytes 1081352 | tf_op jit(solution)/shard_map/ppermute | solution.py:342
  153.7 5.4 %collective-permute-start.26 = (bf16[2,1,1,80,512]{4,3,2,1,0:T(8,128)(2,1)S(1)}, bf16[2,1,1,80,512]{4,3,2,1,0:T(8,128)(2,1)S(1)}, u32[]{:S(2)}, u32[]{:S(2)}) collective-permute-start(bf16[2,1,1,80,512]{4,3,2,1,0:T(8,128)(2,1)S(1)} %constant_dynamic-slice_fusion.6), channel_id=1, source_target_pairs={{0,2},{2,0},{4,6},{6,4},{8,10},{10,8},{12,14},{14,12},{1,3},{3,1},... | collective-permute-start | bytes 491528 | tf_op jit(solution)/shard_map/ppermute | solution.py:342
  155.3 7.1 %collective-permute-start.28 = (bf16[2,1,1,88,512]{4,3,2,1,0:T(8,128)(2,1)S(1)}, bf16[2,1,1,88,512]{4,3,2,1,0:T(8,128)(2,1)S(1)}, u32[]{:S(2)}, u32[]{:S(2)}) collective-permute-start(bf16[2,1,1,88,512]{4,3,2,1,0:T(8,128)(2,1)S(1)} %constant_dynamic-slice_fusion.4), channel_id=1, source_target_pairs={{0,4},{2,6},{4,0},{6,2},{8,12},{10,14},{12,8},{14,10},{1,5},{3,7},... | collective-permute-start | bytes 540680 | tf_op jit(solution)/shard_map/ppermute | solution.py:342
  162.5 6.4 %collective-permute-start.29 = (bf16[1,1,1,168,512]{4,3,2,1,0:T(8,128)(2,1)S(1)}, bf16[1,1,1,168,512]{4,3,2,1,0:T(8,128)(2,1)S(1)}, u32[]{:S(2)}, u32[]{:S(2)}) collective-permute-start(bf16[1,1,1,168,512]{4,3,2,1,0:T(8,128)(2,1)S(1)} %fusion.2), channel_id=1, source_target_pairs={{0,8},{2,10},{4,12},{6,14},{8,0},{10,2},{12,4},{14,6},{1,9},{3,11}... | collective-permute-start | bytes 516104 | tf_op jit(solution)/shard_map/ppermute | solution.py:342
  (6 other events, 4.7 us)

commit v4 on v3

v4 whole, which is shorter than its diff:
```python
import functools
import itertools
import math

import jax
import jax.numpy as jnp
from jax import lax
from jax.experimental import pallas as pl
from jax.experimental.pallas import tpu as pltpu
from jax.sharding import PartitionSpec as P

BASE_DILATION = 256
LEVEL_FLOOR = 0.1
F32 = jnp.float32
BF16 = jnp.bfloat16
TILE = 256
VMEM_LIMIT = 24 * 1024 * 1024
FIRST_LIMIT = 56 * 1024 * 1024
WHOLE = pl.BlockSpec(memory_space=pltpu.VMEM)
SCALAR = pl.BlockSpec(memory_space=pltpu.SMEM)
STAYS = pl.BlockSpec(memory_space=pltpu.HBM)


def dot(a, b):
    return lax.dot_general(a, b, (((1,), (0,)), ((), ())), preferred_element_type=F32)


def dot_t(a, b):
    return lax.dot_general(a, b, (((1,), (1,)), ((), ())), preferred_element_type=F32)


def t_dot(a, b):
    return lax.dot_general(a, b, (((0,), (0,)), ((), ())), preferred_element_type=F32)


def call(kernel, outs, scratch, flops, *args, far=0, limit=VMEM_LIMIT):
    outs = [o + (False,) * (3 - len(o)) for o in outs]
    moved = sum(a.size * a.dtype.itemsize for a in args)
    moved += sum(math.prod(s) * jnp.dtype(d).itemsize for s, d, _ in outs)
    near = args[: len(args) - far]
    return pl.pallas_call(
        kernel,
        out_shape=[jax.ShapeDtypeStruct(s, d) for s, d, _ in outs],
        in_specs=[SCALAR if a.dtype == jnp.int32 and a.ndim == 1 else WHOLE for a in near] + [STAYS] * far,
        out_specs=[STAYS if stays else WHOLE for _, _, stays in outs],
        scratch_shapes=scratch,
        compiler_params=pltpu.CompilerParams(vmem_limit_bytes=limit),
        cost_estimate=pl.CostEstimate(flops=flops, bytes_accessed=moved, transcendentals=0),
    )(*args)


def by_core(core, first, second):
    return first + core * (second - first)


def spots(tm, count):
    near, far, rest, step = tm & 1, (tm >> 1) & 1, tm >> 2, count // 4
    return (2 * near + far) * step + rest, (2 * far + near) * step + rest


CARRY_ROWS = 8
LABEL_ROWS = 16


def scan(feat, forget):
    rows = feat.shape[0]
    keep, mass, weight = 1.0 - forget, forget * (feat * feat), forget
    row = lax.broadcasted_iota(jnp.int32, feat.shape, 0)
    step = 1
    while step < rows:
        inside = row >= step
        before = jnp.where(inside, pltpu.roll(mass, step, 0), 0.0)
        mass = keep * before + mass
        before = jnp.where(inside, pltpu.roll(weight, step, 0), 0.0)
        weight = keep * before + weight
        keep = keep * jnp.where(inside, pltpu.roll(keep, step, 0), 1.0)
        step *= 2
    return keep, mass, weight


def scan_kernel(feat_ref, forget_ref, keep_ref, mass_ref, weight_ref, carry_ref):
    rows, bands = feat_ref.shape
    values = scan(feat_ref[...], forget_ref[...])
    carry_ref[...] = jnp.zeros_like(carry_ref)
    for k, (ref, value) in enumerate(zip((keep_ref, mass_ref, weight_ref), values)):
        ref[...] = value
        rest = value[rows - 1 :]
        for part in range(3):
            rounded = rest.astype(BF16).astype(F32)
            carry_ref[part : part + 1, k * bands : (k + 1) * bands] = rounded
            rest = rest - rounded


def pack_kernel(scalar_ref, feat_ref, forget_ref, conv_ref, res_ref, in_ref, out_ref,
                keep_ref, mass_ref, weight_ref, pack_ref, carry_ref):
    scan_kernel(feat_ref, forget_ref, keep_ref, mass_ref, weight_ref, carry_ref)
    c = pack_ref.shape[1]
    cut, half, more = conv_ref.shape[1] * 3 // 4, res_ref.shape[1] // 2, in_ref.shape[0]

    def fill(across):
        cols = slice(across * c, (across + 1) * c)
        part = slice(across * half, (across + 1) * half)
        at = 0

        def put(value):
            nonlocal at
            pack_ref[at : at + value.shape[0], :] = value
            at += value.shape[0]

        put(conv_ref[0, :, cols])
        put(carry_ref[...].astype(BF16))
        put(conv_ref[1, :cut, cols])
        put(res_ref[0, part, :])
        if across:
            put(jnp.concatenate([out_ref[k * more : (k + 1) * more, :] for k in range(c // out_ref.shape[1])], axis=1))
        else:
            put(in_ref[...])
        put(res_ref[1, part, :])
        put(conv_ref[1, cut:, cols])

    pl.when(scalar_ref[1] == 0)(lambda: fill(0))
    pl.when(scalar_ref[1] == 1)(lambda: fill(1))


def norm_kernel(scalar_ref, feat_ref, keep_ref, mass_ref, weight_ref, carry_ref, label_ref, out_ref):
    bands = feat_ref.shape[1]
    mass0 = jnp.zeros((1, bands), F32)
    weight0 = jnp.zeros((1, bands), F32)
    for tm in range(carry_ref.shape[0]):
        first, second = spots(tm, carry_ref.shape[0])
        parts = carry_ref[by_core(scalar_ref[0], first, second)].astype(F32)
        value = (parts[0:1] + parts[1:2]) + parts[2:3]
        before = tm < scalar_ref[2]
        keep = value[:, :bands]
        mass0 = jnp.where(before, keep * mass0 + value[:, bands : 2 * bands], mass0)
        weight0 = jnp.where(before, keep * weight0 + value[:, 2 * bands : 3 * bands], weight0)
    keep = keep_ref[...]
    mass = keep * mass0 + mass_ref[...]
    weight = keep * weight0 + weight_ref[...]
    normed = (feat_ref[...] / jnp.sqrt(mass / weight + LEVEL_FLOOR)).astype(BF16)
    out_ref[LABEL_ROWS:, :] = normed
    out_ref[:LABEL_ROWS, :] = jnp.zeros((LABEL_ROWS, bands), BF16)
    out_ref[: label_ref.shape[0], :] = label_ref[...].astype(F32).astype(BF16)


def rows_of(value):
    return value.reshape(-1, value.shape[-1]).astype(BF16)


def halves(conv_ref, gate):
    half = conv_ref.shape[1] // 2
    return rows_of(conv_ref[gate, :half]), rows_of(conv_ref[gate, half:])


def place(core, pair, puts):
    for ref, own in zip(pair, (True, False)):
        s = core if own else 1 - core
        rest = ref.shape[0] // 8
        bits = rest.bit_length() - 1
        for steps in itertools.product((0, 1), repeat=3):
            base = (4 * steps[0] + 2 * steps[1] + steps[2]) * rest

            def put(p, _):
                high = sum(((p >> (bits - 1 - b)) & 1) << b for b in range(bits))
                puts(s, steps, high, ref, base + p)
                return 0

            if rest <= 2:
                for p in range(rest):
                    put(p, 0)
            else:
                lax.fori_loop(0, rest, put, 0)


def place_main(conv_ref, row):
    def put(s, steps, high, ref, k):
        third, second, first = steps
        across = by_core(s, third, second)
        tm = 4 * high + 2 * by_core(s, second, first) + by_core(s, first, third)
        conv_ref[across, 2 * tm + s, row : row + ref.shape[1], :] = ref[k].astype(conv_ref.dtype)

    return put


def place_side(layer, conv_ref, res_ref, *extra):
    def put(s, steps, high, ref, k):
        far, near, across = steps
        device = 2 * (4 * high + 2 * far + near) + s
        half = res_ref.shape[1] // 2
        res_ref[device, across * half : (across + 1) * half, :] = ref[k, :half, :].astype(res_ref.dtype)
        value = ref[k, half:, :]
        if layer == 1:
            conv_ref[across, device, conv_ref.shape[2] - value.shape[0] :, :] = value.astype(conv_ref.dtype)
            return
        in_ref, out_ref = extra
        value = value.astype(F32)
        if across == 0:
            in_ref[device] = value
            return
        count, classes = value.shape[0], out_ref.shape[2]
        for q in range(value.shape[1] // classes):
            out_ref[device, q * count : (q + 1) * count, :] = value[:, q * classes : (q + 1) * classes]

    return put


def activate(past, now, conv_ref):
    joined = jnp.concatenate([past, now], axis=1)
    t = jnp.tanh(dot(joined, rows_of(conv_ref[0])))
    s = 0.5 + 0.5 * jnp.tanh(0.5 * dot(joined, rows_of(conv_ref[1])))
    return t, s


def slopes(t, s):
    return s * (1.0 - t * t), t * s * (1.0 - s)


def tile_of(i, offset=0):
    return slice(i * TILE + offset, (i + 1) * TILE + offset)


def copies(pairs, sems):
    return [pltpu.make_async_copy(a, b, sems.at[k]) for k, (a, b) in enumerate(pairs)]


def forward_first(before, steps, scalar_ref, norm_ref, a_ref, a2_ref, b_ref, b2_ref,
                  h1_ref, w_out_ref, h0_far, gated_far, slope_far, conv_far, res_far,
                  h0_ref, gated_ref, slope_ref, conv_ref, res_ref, in_ref, out_ref, sems):
    rows = h0_ref.shape[0]
    kept = slope_ref.shape[1]
    d = rows - h1_ref.shape[0]
    core = scalar_ref[0]
    place(core, (a_ref, a2_ref), place_main(conv_ref, 0))
    place(core, (b_ref, b2_ref), place_side(0, conv_ref, res_ref, in_ref, out_ref))
    w_out_ref[...] = rows_of(out_ref[...])
    w_in = rows_of(in_ref[...])
    for i in range(rows // TILE):
        h0_ref[tile_of(i), :] = dot(norm_ref[tile_of(i), :], w_in).astype(BF16)
    moves = copies([(conv_ref, conv_far), (res_ref, res_far), (h0_ref.at[before : before + kept], h0_far),
                    (gated_ref, gated_far), (slope_ref, slope_far)], sems)
    for move in moves[:3]:
        move.start()
    for i in range(h1_ref.shape[0] // TILE):
        now = h0_ref[tile_of(i, d), :]
        t, s = activate(h0_ref[tile_of(i), :], now, conv_ref)
        gated = (t * s).astype(BF16)
        h1_ref[tile_of(i), :] = (now.astype(F32) + dot(gated, rows_of(res_ref[...]))).astype(BF16)
        first = i * TILE - before
        if 0 <= first < kept:
            own = slice(first, first + TILE)
            slope_ref[0, own, :], slope_ref[1, own, :] = (v.astype(BF16) for v in slopes(t, s))
            if first < steps:
                gated_ref[own, :] = gated
            if first + TILE == kept:
                for move in moves[3:]:
                    move.start()
    for move in moves:
        move.wait()


def store_terms(core, keep_ref, send_ref, row, value, first, size, start, count, lane=0):
    at = (slice(row, row + count), slice(lane, lane + value.shape[1]))
    for k in range(value.shape[0] // (2 * size)):
        low = value[2 * k * size + start : 2 * k * size + start + count]
        high = value[(2 * k + 1) * size + start : (2 * k + 1) * size + start + count]
        one, two = spots(first + k, keep_ref.shape[0])
        keep_ref[(by_core(core, one, two),) + at] = jnp.where(core == 0, low, high).astype(keep_ref.dtype)
        send_ref[(by_core(core, two, one),) + at] = jnp.where(core == 0, high, low).astype(send_ref.dtype)


def conv_terms(targets, first, size, value):
    c = value.shape[1] // 2
    store_terms(*targets, 0, value[:, :c], first, size, 0, size)
    store_terms(*targets, size, value[:, c:], first, size, 0, size)


def second_kernel(steps, scale, sizes, scalar_ref, h1_ref, w_out_ref, label_ref, a_ref, a2_ref, b_ref, b2_ref,
                  loss_ref, keep_ref, send_ref, back_ref, grad_ref, conv_ref,
                  res_ref, gated_ref, h2_ref, lgrad_ref, round_ref):
    rows, c = back_ref.shape[0], grad_ref.shape[1]
    d = h1_ref.shape[0] - rows
    classes = w_out_ref.shape[1]
    conv, res, _, out = sizes
    core = scalar_ref[0]
    place(core, (a_ref, a2_ref), place_main(conv_ref, 0))
    place(core, (b_ref, b2_ref), place_side(1, conv_ref, res_ref))

    lanes = label_ref.shape[1]
    class_row = lax.broadcasted_iota(jnp.int32, (classes, lanes), 0).astype(F32)
    unit = class_row == lax.broadcasted_iota(jnp.int32, (lanes, lanes), 1).astype(F32)
    row = lax.broadcasted_iota(jnp.int32, (TILE, 1), 0)
    left = scalar_ref[3] - scalar_ref[2] * steps

    for i in range(rows // TILE):
        at = tile_of(i)
        now = h1_ref[tile_of(i, d), :]
        t, s = activate(h1_ref[at, :], now, conv_ref)
        gated = (t * s).astype(BF16)
        h2 = (now.astype(F32) + dot(gated, rows_of(res_ref[...]))).astype(BF16)
        logits = dot(h2, w_out_ref[...])
        total = jnp.log(jnp.sum(jnp.exp(logits), axis=1, keepdims=True))
        groups = range(i * TILE // lanes, (i + 1) * TILE // lanes)
        hot = jnp.concatenate(
            [(class_row == label_ref[k : k + 1, :].astype(F32)).astype(F32).T for k in groups])
        valid = (row + i * TILE < left).astype(F32)
        lgrad = ((jnp.exp(logits - total) - hot) * (valid * scale)).astype(BF16)
        grad = dot_t(lgrad, w_out_ref[...])
        rounded = grad.astype(BF16)
        back = dot_t(rounded, rows_of(res_ref[...]))
        filter_slope, gate_slope = slopes(t, s)
        back_ref[at, :c] = (back * filter_slope).astype(BF16)
        back_ref[at, c:] = (back * gate_slope).astype(BF16)
        if i * TILE < grad_ref.shape[0]:
            grad_ref[at, :] = grad
        if i * TILE < steps:
            loss = (total - jnp.sum(logits * hot, axis=1, keepdims=True)) * valid
            for j, k in enumerate(groups):
                part = jnp.where(unit, loss[j * lanes : (j + 1) * lanes], 0.0)
                loss_ref[k : k + 1, :] = jnp.sum(part, axis=0, keepdims=True)
            gated_ref[at, :] = gated
            h2_ref[at, :] = h2
            lgrad_ref[at, :] = lgrad
            round_ref[at, :] = rounded

    own = slice(0, steps)
    targets = (core, keep_ref, send_ref)
    for i in range(c // TILE):
        at = tile_of(i)
        first, per = i * (TILE // (2 * conv)), c // (2 * conv)
        conv_terms(targets, first, conv, t_dot(h1_ref[0:steps, at], back_ref[own, :]))
        conv_terms(targets, first + per, conv, t_dot(h1_ref[d : d + steps, at], back_ref[own, :]))
        value = t_dot(gated_ref[own, at], round_ref[own, :])
        store_terms(*targets, 2 * conv, value, i * (TILE // (2 * res)), res, 0, res)
        value = t_dot(h2_ref[own, at], lgrad_ref[own, :])
        count = out * classes // c
        for q in range(c // classes):
            store_terms(*targets, 2 * conv + res, value, i * (TILE // (2 * out)), out, q * count, count, q * classes)


def grad_below(grad, back_ref, i, d, weights):
    c = back_ref.shape[1] // 2
    (filt_past, filt_now), (gate_past, gate_now) = weights
    grad = grad + dot_t(back_ref[tile_of(i), :c], filt_now) + dot_t(back_ref[tile_of(i), c:], gate_now)
    return grad + dot_t(back_ref[tile_of(i, d), :c], filt_past) + dot_t(back_ref[tile_of(i, d), c:], gate_past)


def grad_first(back1_ref, grad2_ref, conv1_ref, slope_far, res_far,
               grad_ref, round_ref, back_ref, slope_ref, res_ref, sems):
    rows, c = back_ref.shape[0], grad_ref.shape[1]
    d1 = back1_ref.shape[0] - rows
    moves = copies([(slope_far, slope_ref), (res_far, res_ref)], sems)
    for move in moves:
        move.start()
    weights = halves(conv1_ref, 0), halves(conv1_ref, 1)
    for i in range(rows // TILE):
        at = tile_of(i)
        grad = grad_below(grad2_ref[at, :], back1_ref, i, d1, weights)
        rounded = grad.astype(BF16)
        if i == 0:
            for move in moves:
                move.wait()
        back = dot_t(rounded, rows_of(res_ref[...]))
        back_ref[at, :c] = (back * slope_ref[0, at, :].astype(F32)).astype(BF16)
        back_ref[at, c:] = (back * slope_ref[1, at, :].astype(F32)).astype(BF16)
        if i * TILE < grad_ref.shape[0]:
            grad_ref[at, :] = grad
            round_ref[at, :] = rounded


def terms_first(sizes, scalar_ref, back_ref, grad_ref, round_ref, norm_ref, h0_far, gated_far, conv_far,
                keep_ref, send_ref, h0_ref, gated_ref, conv_ref, last_ref, sems):
    steps, c = grad_ref.shape
    d0 = back_ref.shape[0] - steps
    conv, res, enter, _ = sizes
    moves = copies([(h0_far, h0_ref), (gated_far, gated_ref), (conv_far, conv_ref)], sems)
    for move in moves:
        move.start()
    own = slice(0, steps)
    targets = (scalar_ref[0], keep_ref, send_ref)
    moves[0].wait()
    for i in range(c // TILE):
        at = tile_of(i)
        first, per = i * (TILE // (2 * conv)), c // (2 * conv)
        conv_terms(targets, first, conv, t_dot(h0_ref[0:steps, at], back_ref[own, :]))
        conv_terms(targets, first + per, conv, t_dot(h0_ref[d0 : d0 + steps, at], back_ref[own, :]))
        if i == 0:
            moves[1].wait()
        value = t_dot(gated_ref[:, at], round_ref[...])
        store_terms(*targets, 2 * conv, value, i * (TILE // (2 * res)), res, 0, res)
    moves[2].wait()
    weights = halves(conv_ref, 0), halves(conv_ref, 1)
    for i in range(steps // TILE):
        last_ref[tile_of(i), :] = grad_below(grad_ref[tile_of(i), :], back_ref, i, d0, weights).astype(BF16)
    value = t_dot(norm_ref[...], last_ref[...])
    store_terms(*targets, 2 * conv + res, value, 0, enter, 0, enter)


NEAR, FAR, ACROSS = ("tm", 0), ("tm", 1), ("groups", 0)
CORE = ("site", 0)


def swap(value, links):
    names = ("groups", "tm", "site")
    sizes = [lax.axis_size(name) for name in names]
    pairs = []
    for at in itertools.product(*(range(size) for size in sizes)):
        axis, bit = links[at[2]]
        to = tuple(i ^ (1 << bit) if name == axis else i for name, i in zip(names, at))
        pairs.append(tuple((p[0] * sizes[1] + p[1]) * sizes[2] + p[2] for p in (at, to)))
    return lax.ppermute(value, names, pairs)


def my_bit(links):
    first, second = ((lax.axis_index(axis) >> bit) & 1 for axis, bit in links)
    return jnp.where(lax.axis_index("site") == 0, first, second)


def time_bits():
    return lax.axis_size("tm").bit_length() - 1


def grow(held, links):
    other = swap(held, links)
    return jnp.where(
        my_bit(links) == 0, jnp.concatenate([held, other]), jnp.concatenate([other, held]))


def together(*values):
    return lax.optimization_barrier(values)


def sum_step(held, links, dim=0):
    mine = my_bit(links)
    other = swap(lax.dynamic_index_in_dim(held, 1 - mine, dim), links)
    return lax.dynamic_index_in_dim(held, mine, dim).astype(F32) + other.astype(F32)


def sum_rest(held):
    shape, bits = held.shape[1:], time_bits()
    held = held.reshape((2,) * bits + shape)
    held = sum_step(held, (NEAR, FAR)).astype(BF16)
    total = sum_step(held, (FAR, NEAR), 1)
    for bit in range(2, bits):
        total = sum_step(total.astype(BF16), (("tm", bit),) * 2, 2 + bits - 1 - bit)
    return total.reshape(shape)


def hop(value, by):
    size = lax.axis_size("tm")
    return lax.ppermute(value, "tm", [(i, i + by) for i in range(size) if 0 <= i + by < size])


def rows_before(value, count):
    steps, parts, by = value.shape[0] - LABEL_ROWS, [], 1
    while count > 0:
        take = min(count, steps)
        parts.insert(0, hop(value[LABEL_ROWS + steps - take :], by))
        count, by = count - take, by + 1
    return parts


def rows_after(value, count):
    steps, parts, by = value.shape[0] - LABEL_ROWS, [], 1
    while count > 0:
        take = min(count, steps)
        parts.append(hop(value[: LABEL_ROWS + take], -by))
        count, by = count - take, by + 1
    return parts


def on_device(features, forget, labels, lengths, w_conv, w_res, w_in, w_out):
    _, steps, bands = features.shape
    time_devices, site_devices = lax.axis_size("tm"), lax.axis_size("site")
    devices = time_devices * site_devices
    c = w_res.shape[2]
    classes = w_out.shape[1]
    conv, res, enter, out = sizes = (w_conv.shape[1], w_res.shape[1], w_in.shape[0], w_out.shape[0])
    half, cut = res // 2, conv * 3 // 4
    aligned = conv % 64 == 0 and res % 32 == 0
    kind = BF16 if aligned else F32
    d0, d1 = BASE_DILATION, 2 * BASE_DILATION
    reach = d0 + d1
    across = my_bit((ACROSS, ACROSS))
    scalars = jnp.stack(
        [lax.axis_index("site"), across, lax.axis_index("tm"), lengths[0]]).astype(jnp.int32)

    block = ((steps, bands), F32)
    feat = features[0]
    if aligned:
        packed = 2 * (conv + half) + enter + CARRY_ROWS
        keep, mass, weight, held, _ = call(
            pack_kernel, [block] * 3 + [((packed, c), BF16), ((CARRY_ROWS, c), F32)], [], 40 * steps * bands,
            scalars, feat, forget[0], w_conv, w_res, w_in, w_out, limit=FIRST_LIMIT)
    else:
        keep, mass, weight, carry = call(
            scan_kernel, [block] * 3 + [((CARRY_ROWS, c), F32)], [], 40 * steps * bands, feat, forget[0])
        conv_own = jnp.where(across == 0, w_conv[:, :, :c], w_conv[:, :, c:])
        res_own = jnp.where(across == 0, w_res[:, :half], w_res[:, half:])
        out_own = jnp.concatenate([w_out[k * enter : (k + 1) * enter] for k in range(c // classes)], axis=1)
        held = jnp.concatenate([
            conv_own[0], carry.astype(BF16), conv_own[1, :cut], res_own[0],
            jnp.where(across == 0, w_in, out_own), res_own[1], conv_own[1, cut:]])
    held = held[None]
    for bit in reversed(range(2, time_bits())):
        held = grow(held, (("tm", bit),) * 2)

    main_links = [(NEAR, FAR), (FAR, ACROSS), (ACROSS, NEAR)]
    side_links = [(ACROSS, ACROSS), (NEAR, NEAR), (FAR, FAR)]
    ends = conv + CARRY_ROWS + cut
    main, side = held[:, :ends], held[:, ends:]
    main, side = grow(main, main_links[0]), grow(side, side_links[0])
    carry = main[:, conv : conv + CARRY_ROWS]
    main = jnp.concatenate([main[:, :conv], main[:, conv + CARRY_ROWS :]], axis=1)
    main, side, carry = together(main, side, carry)
    carry = grow(carry, (FAR, NEAR))
    main, side = grow(main, main_links[1]), grow(side, side_links[1])
    label_rows = steps // bands
    bits = time_bits()
    carry = carry.reshape((2,) * bits + (CARRY_ROWS, c))
    carry = carry.transpose((1, 0) + tuple(range(bits - 1, 1, -1)) + (bits, bits + 1))
    (normed,) = call(norm_kernel, [((LABEL_ROWS + steps, bands), BF16)], [], 10 * steps * bands,
                     scalars, feat, keep, mass, weight, carry.reshape(time_devices, CARRY_ROWS, c),
                     labels[0].reshape(label_rows, bands))
    main, side = together(main, side)
    first = [main[:, :conv], side[:, : half + enter]]
    second = [main[:, conv:], side[:, half + enter :]]

    def last_step(parts):
        return [grow(p, links[2]) for p, links in zip(parts, (main_links, side_links))]

    def both_cores(parts):
        return [v.astype(kind) for p in parts for v in (p, swap(p, (CORE, CORE)))]

    first = both_cores(last_step(first))
    past, future = rows_before(normed, reach), rows_after(normed, reach)
    own_normed = normed[LABEL_ROWS:]
    window = jnp.concatenate(past + [own_normed] + [v[LABEL_ROWS:] for v in future])
    label_window = jnp.concatenate(
        [v[: (v.shape[0] - LABEL_ROWS) // bands] for v in [normed] + future])
    *first, window, second[0], second[1] = together(*first, window, *second)

    total_rows, rows0, rows1 = steps + 2 * reach, steps + d0, steps + reach
    conv_all, res_all = ((2, devices, conv, c), kind), ((devices, res, c), kind)
    V, sems = pltpu.VMEM, pltpu.SemaphoreType.DMA
    h1, out_all, *kept = call(
        functools.partial(forward_first, d1, steps),
        [((total_rows - d0, c), BF16), ((c, classes), BF16), ((rows0, c), BF16, True), ((steps, c), BF16, True),
         ((2, rows0, c), BF16, True), conv_all + (True,), res_all + (True,)],
        [V((total_rows, c), BF16), V((steps, c), BF16), V((2, rows0, c), BF16), V(*conv_all), V(*res_all),
         V((devices, enter, c), F32), V((devices, out, classes), F32), sems((5,))],
        2 * total_rows * c * (bands + 5 * c), scalars, window, *first)
    h0, gated0, slope0, conv0, res0 = kept

    second = both_cores(last_step(second))
    scale = 1.0 / math.sqrt(site_devices * steps * time_devices)
    package = [((time_devices, 2 * conv + res + enter, c), kind)] * 2
    loss, keep1, send1, back1, grad2, conv1 = call(
        functools.partial(second_kernel, steps, scale, sizes),
        [((label_rows, bands), F32)] + package + [((rows1, 2 * c), BF16), ((rows0, c), F32), conv_all],
        [V(*res_all), V((steps, c), BF16), V((steps, c), BF16), V((steps, classes), BF16), V((steps, c), BF16)],
        2 * rows1 * c * 6 * c + 2 * steps * 5 * c * c,
        scalars, h1, out_all, label_window, *second)

    core = (CORE, CORE)
    sum1 = (keep1.astype(F32) + swap(send1.astype(BF16), core).astype(F32)).astype(BF16)
    grad1, round0, back0 = call(
        grad_first, [((steps, c), F32), ((steps, c), BF16), ((rows0, 2 * c), BF16)],
        [V((2, rows0, c), BF16), V(*res_all), sems((2,))],
        2 * rows0 * c * 5 * c, back1, grad2, conv1, slope0, res0, far=2)
    sum1, back0 = together(sum1, back0)
    keep0, send0 = call(
        functools.partial(terms_first, sizes), package,
        [V((rows0, c), BF16), V((steps, c), BF16), V(*conv_all), V((steps, c), BF16), sems((3,))],
        2 * steps * 9 * c * c,
        scalars, back0, grad1, round0, own_normed, h0, gated0, conv0, far=3)
    sum0 = (keep0.astype(F32) + swap(send0.astype(BF16), core).astype(F32)).astype(BF16)

    convs, ress, extras = [], [], []
    for held in (sum0, sum1):
        total = sum_rest(held)
        convs.append(jnp.concatenate([total[:conv], total[conv : 2 * conv]], axis=1))
        ress.append(total[2 * conv : 2 * conv + res])
        extras.append(total[2 * conv + res :])
    grad_in, grad_out = extras
    return (
        loss.reshape(1, steps),
        jnp.stack(convs),
        jnp.stack(ress),
        grad_in,
        jnp.concatenate([grad_out[:, k * classes : (k + 1) * classes] for k in range(c // classes)]),
    )


def solution(mesh):
    return jax.shard_map(
        on_device,
        mesh=mesh,
        in_specs=(
            P(("groups", "site"), "tm", None),
            P(("groups", "site"), "tm", None),
            P(("groups", "site"), "tm"),
            P(("groups", "site")),
            P(None, ("tm", "site"), None),
            P(None, ("tm", "site"), None),
            P(("tm", "site"), None),
            P(("tm", "site"), None),
        ),
        out_specs=(
            P(("groups", "site"), "tm"),
            P("groups", ("tm", "site"), None),
            P("groups", ("tm", "site"), None),
            P(("tm", "site"), "groups"),
            P(("tm", "site"), "groups"),
        ),
        check_vma=False,
    )
```

time: 172 us -> 170 us (0.988)
  waiting for transfers between devices: 58.1 us -> 73.1 us
  starting transfers between devices: 48.2 us -> 35.5 us
  local copies, waits for them, and re-layouts: 24.7 us -> 16 us
  other arithmetic: 8.61 us -> 13.5 us
    ppermute x31 -> x22, waiting for transfers between devices: 56 us -> 73.1 us  [swap(): return lax.ppermute(value, names, pairs)]
    ppermute x31 -> x22, starting transfers between devices: 38.3 us -> 27.1 us  [swap(): return lax.ppermute(value, names, pairs)]
    unnamed x74 -> x48, local copies, waits for them, and re-layouts: 22.6 us -> 12.3 us
    convert_element_type x8 -> x4, other arithmetic: 0.59 us -> 2.83 us  [the longest x2 1.67 us: sum_rest(): held = sum_step(held, (NEAR, FAR)).astype(BF16)]
    ppermute x4, waiting for transfers between devices: 2.19 us -> 0.01 us  [hop(): lax.ppermute(value, 'tm', [(i, i + by) for i in range(size) if 0 <= i + b...]
    select_n x14 -> x10, other arithmetic: 2.06 us -> 4.16 us  [grow(): jnp.where(my_bit(links) == 0, jnp.concatenate([held, other]), jnp.concate...]
  transfers between devices with their start and end apart: 35 -> 26, of which waited for: 18 -> 15; matrix products, arithmetic and copies ran while one was open for 2% -> 5% of each run, Pallas kernels for 9% -> 9%
where the time goes in v4:
time: 170 us
  waiting for transfers between devices  73.1 us (43%)
  starting transfers between devices  35.5 us (21%)
  Pallas kernels  29.8 us (18%)
  local copies, waits for them, and re-layouts  16 us (9%)
  other arithmetic  13.5 us (8%)
  between operations  1.94 us (1%)
    ppermute x22, waiting for transfers between devices, swap(): return lax.ppermute(value, names, pairs)  73.1 us
    pallas_call x6, Pallas kernels, call(): pl.pallas_call(kernel, out_shape=[jax.ShapeDtypeStruct(s, d) for s, d, _...  29.8 us
    ppermute x22, starting transfers between devices, swap(): return lax.ppermute(value, names, pairs)  27.1 us
    unnamed x48, local copies, waits for them, and re-layouts  12.3 us
    ppermute x4, starting transfers between devices, hop(): lax.ppermute(value, 'tm', [(i, i + by) for i in range(size) if 0 <= i + b...  8.45 us
    select_n x10, other arithmetic, grow(): jnp.where(my_bit(links) == 0, jnp.concatenate([held, other]), jnp.concate...  4.16 us
  transfers between devices with their start and end apart: 26, of which 15 were waited for; matrix products, arithmetic and copies ran while one was open for 5% of the time, Pallas kernels for 9%

profile of v4, /device:TPU:0, one launch (start us, length us, event | category | flops | bytes accessed | tf_op | source)
XLA Modules:
  0.0 169.9 jit_solution(3681525498679757307)
XLA Ops:
  1.3 0.7 pad_add_fusion.scalar_ref
  1.9 2.7 %shard_map.119 = (f32[512,128]{1,0:T(8,128)}, f32[512,128]{1,0:T(8,128)}, f32[512,128]{1,0:T(8,128)}, bf16[176,512]{1,0:T(8,128)(2,1)}, f32[8,512]{1,0:T(8,128)}) custom-call(s32[4]{0:T(128)} %pad_add_fusion.scalar_ref, f32[512,128]{1,0:T(8,128)} %bitcast.34, f32[512,128]{1,0:T(8,128)} %bitcast.42, bf16[2,64,1024]{2,1,0:T(8,128)(2,1)} %conv_ref.1, ...), custom_call_target="tpu_custom_call" | custom-call | flops 2621440 | bytes 1851408 | tf_op jit(solution)/shard_map/pallas_call | solution.py:41
  4.6 4.0 %collective-permute-start = (bf16[1,176,512]{2,1,0:T(8,128)(2,1)}, bf16[1,176,512]{2,1,0:T(8,128)(2,1)S(1)}, u32[]{:S(2)}, u32[]{:S(2)}) collective-permute-start(bf16[1,176,512]{2,1,0:T(8,128)(2,1)} %bitcast.44), channel_id=1, source_target_pairs={{0,8},{1,9},{2,10},{3,11},{4,12},{5,13},{6,14},{7,15},{8,0},{9,1},... | collective-permute-start | bytes 540680 | tf_op jit(solution)/shard_map/ppermute | solution.py:410
  8.7 8.6 %collective-permute-done = bf16[1,176,512]{2,1,0:T(8,128)(2,1)S(1)} collective-permute-done((bf16[1,176,512]{2,1,0:T(8,128)(2,1)}, bf16[1,176,512]{2,1,0:T(8,128)(2,1)S(1)}, u32[]{:S(2)}, u32[]{:S(2)}) %collective-permute-start) | collective-permute-done | bytes 180256 | tf_op jit(solution)/shard_map/ppermute | solution.py:410
  17.3 1.1 maximum_select_fusion.7
  18.4 1.6 collective-permute-start.1
  20.0 1.6 collective-permute-start.2
  21.6 3.3 %collective-permute-done.2 = bf16[2,56,512]{2,1,0:T(8,128)(2,1)S(1)} collective-permute-done((bf16[2,56,512]{2,1,0:T(8,128)(2,1)S(1)}, bf16[2,56,512]{2,1,0:T(8,128)(2,1)S(1)}, u32[]{:S(2)}, u32[]{:S(2)}) %collective-permute-start.2) | collective-permute-done | bytes 114720 | tf_op jit(solution)/shard_map/ppermute | solution.py:410
  25.1 0.8 collective-permute-start.3
  26.0 1.3 collective-permute-start.4
  27.2 4.8 %collective-permute-done.4 = bf16[4,56,512]{2,1,0:T(8,128)(2,1)S(1)} collective-permute-done((bf16[4,56,512]{2,1,0:T(8,128)(2,1)S(1)}, bf16[4,56,512]{2,1,0:T(8,128)(2,1)S(1)}, u32[]{:S(2)}, u32[]{:S(2)}) %collective-permute-start.4) | collective-permute-done | bytes 229408 | tf_op jit(solution)/shard_map/ppermute | solution.py:410
  32.2 1.5 collective-permute-done.3
  33.8 1.3 maximum_select_fusion.1
  35.1 1.6 collective-permute-start.5
  36.7 0.8 collective-permute-start.9
  37.5 3.1 %collective-permute-done.9 = bf16[4,8,512]{2,1,0:T(8,128)(2,1)S(1)} collective-permute-done((bf16[4,8,512]{2,1,0:T(8,128)(2,1)S(1)}, bf16[4,8,512]{2,1,0:T(8,128)(2,1)S(1)}, u32[]{:S(2)}, u32[]{:S(2)}) %collective-permute-start.9) | collective-permute-done | bytes 32800 | tf_op jit(solution)/shard_map/ppermute | solution.py:410
  40.7 0.7 shard_map.120
  41.5 2.7 %collective-permute-start.10 = (bf16[256,128]{1,0:T(8,128)(2,1)S(1)}, bf16[256,128]{1,0:T(8,128)(2,1)S(1)}, u32[]{:S(2)}, u32[]{:S(2)}) collective-permute-start(bf16[256,128]{1,0:T(8,128)(2,1)S(1)} %slice.148), channel_id=1, source_target_pairs={{0,4},{2,6},{4,8},{6,10},{8,12},{10,14},{1,5},{3,7},{5,9},{7,11},{... | collective-permute-start | bytes 196616 | tf_op jit(solution)/shard_map/ppermute | solution.py:450
  44.1 3.2 %collective-permute-start.11 = (bf16[512,128]{1,0:T(8,128)(2,1)S(1)}, bf16[512,128]{1,0:T(8,128)(2,1)S(1)}, u32[]{:S(2)}, u32[]{:S(2)}) collective-permute-start(bf16[512,128]{1,0:T(8,128)(2,1)S(1)} %slice.149.norm_ref), channel_id=1, source_target_pairs={{0,2},{2,4},{4,6},{6,8},{8,10},{10,12},{12,14},{1,3},{3,5},{5,7},{... | collective-permute-start | bytes 393224 | tf_op jit(solution)/shard_map/ppermute | solution.py:450
  47.4 1.4 maximum_select_fusion.a_ref
  48.7 1.2 collective-permute-start.6
  49.9 1.3 collective-permute-start.12
  51.2 1.3 collective-permute-start.13
  52.6 4.7 %collective-permute-start.7 = (bf16[8,24,512]{2,1,0:T(8,128)(2,1)S(1)}, bf16[8,24,512]{2,1,0:T(8,128)(2,1)S(1)}, u32[]{:S(2)}, u32[]{:S(2)}) collective-permute-start(bf16[8,24,512]{2,1,0:T(8,128)(2,1)S(1)} %slice.114), channel_id=1, source_target_pairs={{0,4},{1,5},{2,6},{3,7},{4,0},{5,1},{6,2},{7,3},{8,12},{9,13},{10,... | collective-permute-start | bytes 589832 | tf_op jit(solution)/shard_map/ppermute | solution.py:410
  57.3 7.1 %collective-permute-done.7 = bf16[8,24,512]{2,1,0:T(8,128)(2,1)S(1)} collective-permute-done((bf16[8,24,512]{2,1,0:T(8,128)(2,1)S(1)}, bf16[8,24,512]{2,1,0:T(8,128)(2,1)S(1)}, u32[]{:S(2)}, u32[]{:S(2)}) %collective-permute-start.7) | collective-permute-done | bytes 196640 | tf_op jit(solution)/shard_map/ppermute | solution.py:410
  64.6 1.0 slice.120
  65.6 0.6 collective-permute-done.8.b2_ref
  66.2 1.5 collective-permute-start.14
  67.7 6.3 %collective-permute-done.14 = bf16[8,48,512]{2,1,0:T(8,128)(2,1)S(1)} collective-permute-done((bf16[8,48,512]{2,1,0:T(8,128)(2,1)S(1)}, bf16[8,48,512]{2,1,0:T(8,128)(2,1)S(1)}, u32[]{:S(2)}, u32[]{:S(2)}) %collective-permute-start.14) | collective-permute-done | bytes 393248 | tf_op jit(solution)/shard_map/ppermute | solution.py:410
  74.9 8.1 %shard_map.121 = (bf16[1792,512]{1,0:T(8,128)(2,1)S(1)}, bf16[512,128]{1,0:T(8,128)(2,1)S(1)}, bf16[768,512]{1,0:T(8,128)(2,1)S(1)}, bf16[512,512]{1,0:T(8,128)(...) custom-call(s32[4]{0:T(128)S(1)} %copy-done.12, ...), custom_call_target="tpu_custom_call" | custom-call | flops 5637144576 | bytes 10878992 | tf_op jit(solution)/shard_map/pallas_call | solution.py:41
  83.0 1.2 copy-done.2
  84.2 1.3 copy-done.14
  85.5 0.9 copy-done.16
  86.4 0.8 copy-done.18
  87.2 11.2 %shard_map.122 = (f32[4,128]{1,0:T(4,128)}, bf16[8,168,512]{2,1,0:T(8,128)(2,1)S(1)}, bf16[8,168,512]{2,1,0:T(8,128)(2,1)}, bf16[1280,1024]{1,0:T(8,128)(2,1)S(1...) custom-call(s32[4]{0:T(128)S(1)} %copy-done.12, bf16[1792,512]{1,0:T(8,128)(2,1)S(1)} %get-tuple-element.55.h1_ref, ...), custom_call_target="tpu_custom_call" | custom-call | flops 5368709120 | bytes 13636112 | tf_op jit(solution)/shard_map/pallas_call | solution.py:41
  98.4 1.4 copy-done
  99.8 1.1 copy-done.4
  100.9 1.1 copy-done.6
  102.0 0.4 collective-permute-start.18
  102.4 1.6 copy-done.1
  104.0 1.4 copy-done.3
  105.4 1.4 copy-done.5
  106.8 2.9 %shard_map.123 = (f32[512,512]{1,0:T(8,128)S(1)}, bf16[512,512]{1,0:T(8,128)(2,1)S(1)}, bf16[768,1024]{1,0:T(8,128)(2,1)S(1)}) custom-call(bf16[1280,1024]{1,0:T(8,128)(2,1)S(1)} %get-tuple-element.62.back1_ref, f32[768,512]{1,0:T(8,128)S(1)} %copy-done.5, bf16[2,16,64,512]{3,2,1,0:T(8,128)(2,1)S(1)} %copy-done.1, bf16[2,768,512]{2,1,0:T(8,128)(2,1)S(1)} %copy-done.3, ...), custom_call_target="tpu_custom_call" | custom-call | flops 2013265920 | bytes 11534336 | tf_op jit(solution)/shard_map/pallas_call | solution.py:41
  109.7 1.9 %add_convert_fusion.1 = bf16[8,168,512]{2,1,0:T(8,128)(2,1)S(1)} fusion(bf16[8,168,512]{2,1,0:T(8,128)(2,1)} %collective-permute-done.18, bf16[8,168,512]{2,1,0:T(8,128)(2,1)S(1)} %copy-done.7), kind=kLoop, calls=%fused_computation.1 | loop fusion | flops 2752512 | bytes 4128768 | tf_op jit(solution)/shard_map/convert_element_type | solution.py:565
  111.6 0.9 constant_dynamic-slice_fusion.2
  112.6 1.7 collective-permute-start.23
  114.3 4.2 %shard_map.124 = (bf16[8,168,512]{2,1,0:T(8,128)(2,1)S(1)}, bf16[8,168,512]{2,1,0:T(8,128)(2,1)S(1)}) custom-call(s32[4]{0:T(128)S(1)} %copy-done.12, bf16[768,1024]{1,0:T(8,128)(2,1)S(1)} %get-tuple-element.68.back_ref, f32[512,512]{1,0:T(8,128)S(1)} %get-tuple-element.69.grad_ref, bf16[512,512]{1,0:T(8,128)(2,1)S(1)} %get-tuple-element.70.round_ref, ...), custom_call_target="tpu_custom_call" | custom-call | flops 2415919104 | bytes 9437200 | tf_op jit(solution)/shard_map/pallas_call | solution.py:41
  118.6 5.2 %collective-permute-done.23 = bf16[1,2,2,168,512]{4,3,2,1,0:T(8,128)(2,1)} collective-permute-done((bf16[1,2,2,168,512]{4,3,2,1,0:T(8,128)(2,1)}, bf16[1,2,2,168,512]{4,3,2,1,0:T(8,128)(2,1)}, u32[]{:S(2)}, u32[]{:S(2)}) %collective-permute-start.23) | collective-permute-done | bytes 688160 | tf_op jit(solution)/shard_map/ppermute | solution.py:410
  123.8 1.5 add_convert_fusion.2
  125.3 0.8 constant_dynamic-slice_fusion.1
  126.5 7.2 %collective-permute-done.24 = bf16[1,1,2,168,512]{4,3,2,1,0:T(8,128)(2,1)} collective-permute-done((bf16[1,1,2,168,512]{4,3,2,1,0:T(8,128)(2,1)}, bf16[1,1,2,168,512]{4,3,2,1,0:T(8,128)(2,1)}, u32[]{:S(2)}, u32[]{:S(2)}) %collective-permute-start.24) | collective-permute-done | bytes 344096 | tf_op jit(solution)/shard_map/ppermute | solution.py:410
  133.6 1.1 add_convert_fusion.4
  134.7 3.2 %collective-permute-start.25 = (bf16[1,1,1,168,512]{4,3,2,1,0:T(8,128)(2,1)S(1)}, bf16[1,1,1,168,512]{4,3,2,1,0:T(8,128)(2,1)S(1)}, u32[]{:S(2)}, u32[]{:S(2)}) collective-permute-start(bf16[1,1,1,168,512]{4,3,2,1,0:T(8,128)(2,1)S(1)} %constant_dynamic-slice_fusion), channel_id=1, source_target_pairs={{0,8},{1,9},{2,10},{3,11},{4,12},{5,13},{6,14},{7,15},{8,0},{9,1},... | collective-permute-start | bytes 516104 | tf_op jit(solution)/shard_map/ppermute | solution.py:410
  138.0 1.7 %add_convert_fusion = bf16[8,168,512]{2,1,0:T(8,128)(2,1)S(1)} fusion(bf16[8,168,512]{2,1,0:T(8,128)(2,1)} %collective-permute-done.19, bf16[8,168,512]{2,1,0:T(8,128)(2,1)S(1)} %get-tuple-element.74), kind=kLoop, calls=%fused_computation | loop fusion | flops 2752512 | bytes 4128768 | tf_op jit(solution)/shard_map/convert_element_type | solution.py:576
  139.8 1.2 collective-permute-start.20
  141.0 3.5 %collective-permute-done.25 = bf16[1,1,1,168,512]{4,3,2,1,0:T(8,128)(2,1)S(1)} collective-permute-done((bf16[1,1,1,168,512]{4,3,2,1,0:T(8,128)(2,1)S(1)}, bf16[1,1,1,168,512]{4,3,2,1,0:T(8,128)(2,1)S(1)}, u32[]{:S(2)}, u32[]{:S(2)}) %collective-permute-start.25) | collective-permute-done | bytes 172064 | tf_op jit(solution)/shard_map/ppermute | solution.py:410
  144.5 6.2 %collective-permute-done.20 = bf16[1,2,2,168,512]{4,3,2,1,0:T(8,128)(2,1)S(1)} collective-permute-done((bf16[1,2,2,168,512]{4,3,2,1,0:T(8,128)(2,1)S(1)}, bf16[1,2,2,168,512]{4,3,2,1,0:T(8,128)(2,1)S(1)}, u32[]{:S(2)}, u32[]{:S(2)}) %collective-permute-start.20) | collective-permute-done | bytes 688160 | tf_op jit(solution)/shard_map/ppermute | solution.py:410
  151.0 0.5 collective-permute-start.21
  151.5 6.8 %collective-permute-done.21 = bf16[1,1,2,168,512]{4,3,2,1,0:T(8,128)(2,1)S(1)} collective-permute-done((bf16[1,1,2,168,512]{4,3,2,1,0:T(8,128)(2,1)S(1)}, bf16[1,1,2,168,512]{4,3,2,1,0:T(8,128)(2,1)S(1)}, u32[]{:S(2)}, u32[]{:S(2)}) %collective-permute-start.21) | collective-permute-done | bytes 344096 | tf_op jit(solution)/shard_map/ppermute | solution.py:410
  158.5 0.6 pad_maximum_fusion.3
  159.2 8.5 %collective-permute-done.22 = bf16[1,1,1,168,512]{4,3,2,1,0:T(8,128)(2,1)S(1)} collective-permute-done((bf16[1,1,1,168,512]{4,3,2,1,0:T(8,128)(2,1)S(1)}, bf16[1,1,1,168,512]{4,3,2,1,0:T(8,128)(2,1)S(1)}, u32[]{:S(2)}, u32[]{:S(2)}) %collective-permute-start.22) | collective-permute-done | bytes 172064 | tf_op jit(solution)/shard_map/ppermute | solution.py:410
  167.8 0.6 slice_bitcast_fusion.7
  168.4 0.7 pad_maximum_fusion.2
  169.0 0.8 pad_maximum_fusion
  (98 shorter events, 2.7 us)
Async XLA Ops:
  4.6 12.7 %collective-permute-start = (bf16[1,176,512]{2,1,0:T(8,128)(2,1)}, bf16[1,176,512]{2,1,0:T(8,128)(2,1)S(1)}, u32[]{:S(2)}, u32[]{:S(2)}) collective-permute-start(bf16[1,176,512]{2,1,0:T(8,128)(2,1)} %bitcast.44), channel_id=1, source_target_pairs={{0,8},{1,9},{2,10},{3,11},{4,12},{5,13},{6,14},{7,15},{8,0},{9,1},... | collective-permute-start | bytes 540680 | tf_op jit(solution)/shard_map/ppermute | solution.py:410
  18.4 6.5 %collective-permute-start.1 = (bf16[2,120,512]{2,1,0:T(8,128)(2,1)S(1)}, bf16[2,120,512]{2,1,0:T(8,128)(2,1)S(1)}, u32[]{:S(2)}, u32[]{:S(2)}) collective-permute-start(bf16[2,120,512]{2,1,0:T(8,128)(2,1)S(1)} %slice.143), channel_id=1, source_target_pairs={{0,2},{1,5},{2,0},{3,7},{4,6},{5,1},{6,4},{7,3},{8,10},{9,13},{10,... | collective-permute-start | bytes 737288 | tf_op jit(solution)/shard_map/ppermute | solution.py:410
  20.0 4.9 %collective-permute-start.2 = (bf16[2,56,512]{2,1,0:T(8,128)(2,1)S(1)}, bf16[2,56,512]{2,1,0:T(8,128)(2,1)S(1)}, u32[]{:S(2)}, u32[]{:S(2)}) collective-permute-start(bf16[2,56,512]{2,1,0:T(8,128)(2,1)S(1)} %slice.146), channel_id=1, source_target_pairs={{0,16},{1,17},{2,18},{3,19},{4,20},{5,21},{6,22},{7,23},{8,24},{9,... | collective-permute-start | bytes 344072 | tf_op jit(solution)/shard_map/ppermute | solution.py:410
  25.1 8.6 %collective-permute-start.3 = (bf16[4,112,512]{2,1,0:T(8,128)(2,1)S(1)}, bf16[4,112,512]{2,1,0:T(8,128)(2,1)}, u32[]{:S(2)}, u32[]{:S(2)}) collective-permute-start(bf16[4,112,512]{2,1,0:T(8,128)(2,1)S(1)} %pad_maximum_fusion.1), channel_id=1, source_target_pairs={{0,4},{1,17},{2,6},{3,19},{4,0},{5,21},{6,2},{7,23},{8,12},{9,25},... | collective-permute-start | bytes 1376264 | tf_op jit(solution)/shard_map/ppermute | solution.py:410
  26.0 6.1 %collective-permute-start.4 = (bf16[4,56,512]{2,1,0:T(8,128)(2,1)S(1)}, bf16[4,56,512]{2,1,0:T(8,128)(2,1)S(1)}, u32[]{:S(2)}, u32[]{:S(2)}) collective-permute-start(bf16[4,56,512]{2,1,0:T(8,128)(2,1)S(1)} %maximum_select_fusion.8), channel_id=1, source_target_pairs={{0,2},{1,3},{2,0},{3,1},{4,6},{5,7},{6,4},{7,5},{8,10},{9,11},{10,... | collective-permute-start | bytes 688136 | tf_op jit(solution)/shard_map/ppermute | solution.py:410
  32.2 8.5 %copy-start.8 = (f32[1,512,128]{2,1,0:T(8,128)S(1)}, f32[1,512,128]{2,1,0:T(8,128)}, u32[]{:S(2)}) copy-start(f32[1,512,128]{2,1,0:T(8,128)} %param.8) | copy-start | bytes 786436
  32.2 8.5 %copy-start.9 = (f32[512,128]{1,0:T(8,128)S(1)}, f32[512,128]{1,0:T(8,128)}, u32[]{:S(2)}) copy-start(f32[512,128]{1,0:T(8,128)} %get-tuple-element.46.keep_ref) | copy-start | bytes 786436
  32.2 8.5 %copy-start.10 = (f32[512,128]{1,0:T(8,128)S(1)}, f32[512,128]{1,0:T(8,128)}, u32[]{:S(2)}) copy-start(f32[512,128]{1,0:T(8,128)} %get-tuple-element.47.mass_ref) | copy-start | bytes 786436
  32.2 8.5 %copy-start.11 = (f32[512,128]{1,0:T(8,128)S(1)}, f32[512,128]{1,0:T(8,128)}, u32[]{:S(2)}) copy-start(f32[512,128]{1,0:T(8,128)} %get-tuple-element.48.weight_ref) | copy-start | bytes 786436
  32.2 8.5 %copy-start.12 = (s32[4]{0:T(128)S(1)}, s32[4]{0:T(128)}, u32[]{:S(2)}) copy-start(s32[4]{0:T(128)} %pad_add_fusion.scalar_ref) | copy-start | bytes 52
  32.2 8.5 %copy-start.13 = (s32[1,512]{1,0:T(1,128)S(1)}, s32[1,512]{1,0:T(1,128)}, u32[]{:S(2)}) copy-start(s32[1,512]{1,0:T(1,128)} %param.10) | copy-start | bytes 6148
  35.1 12.3 %copy-start.21 = (bf16[8,112,512]{2,1,0:T(8,128)(2,1)}, bf16[8,112,512]{2,1,0:T(8,128)(2,1)S(1)}, u32[]{:S(2)}) copy-start(bf16[8,112,512]{2,1,0:T(8,128)(2,1)S(1)} %maximum_select_fusion.1) | copy-start | bytes 2752516
  35.1 12.2 %collective-permute-start.5 = (bf16[8,64,512]{2,1,0:T(8,128)(2,1)S(1)}, bf16[8,64,512]{2,1,0:T(8,128)(2,1)}, u32[]{:S(2)}, u32[]{:S(2)}) collective-permute-start(bf16[8,64,512]{2,1,0:T(8,128)(2,1)S(1)} %slice.113), channel_id=1, source_target_pairs={{0,16},{1,3},{2,18},{3,1},{4,20},{5,7},{6,22},{7,5},{8,24},{9,11},... | collective-permute-start | bytes 1572872 | tf_op jit(solution)/shard_map/ppermute | solution.py:410
  36.7 3.9 %collective-permute-start.9 = (bf16[4,8,512]{2,1,0:T(8,128)(2,1)S(1)}, bf16[4,8,512]{2,1,0:T(8,128)(2,1)S(1)}, u32[]{:S(2)}, u32[]{:S(2)}) collective-permute-start(bf16[4,8,512]{2,1,0:T(8,128)(2,1)S(1)} %slice.147), channel_id=1, source_target_pairs={{0,4},{1,3},{2,6},{3,1},{4,0},{5,7},{6,2},{7,5},{8,12},{9,11},{10,... | collective-permute-start | bytes 98312 | tf_op jit(solution)/shard_map/ppermute | solution.py:410
  41.5 11.1 %collective-permute-start.10 = (bf16[256,128]{1,0:T(8,128)(2,1)S(1)}, bf16[256,128]{1,0:T(8,128)(2,1)S(1)}, u32[]{:S(2)}, u32[]{:S(2)}) collective-permute-start(bf16[256,128]{1,0:T(8,128)(2,1)S(1)} %slice.148), channel_id=1, source_target_pairs={{0,4},{2,6},{4,8},{6,10},{8,12},{10,14},{1,5},{3,7},{5,9},{7,11},{... | collective-permute-start | bytes 196616 | tf_op jit(solution)/shard_map/ppermute | solution.py:450
  44.1 8.4 %collective-permute-start.11 = (bf16[512,128]{1,0:T(8,128)(2,1)S(1)}, bf16[512,128]{1,0:T(8,128)(2,1)S(1)}, u32[]{:S(2)}, u32[]{:S(2)}) collective-permute-start(bf16[512,128]{1,0:T(8,128)(2,1)S(1)} %slice.149.norm_ref), channel_id=1, source_target_pairs={{0,2},{2,4},{4,6},{6,8},{8,10},{10,12},{12,14},{1,3},{3,5},{5,7},{... | collective-permute-start | bytes 393224 | tf_op jit(solution)/shard_map/ppermute | solution.py:450
  48.7 17.5 %collective-permute-start.6 = (bf16[16,64,512]{2,1,0:T(8,128)(2,1)S(1)}, bf16[16,64,512]{2,1,0:T(8,128)(2,1)S(1)}, u32[]{:S(2)}, u32[]{:S(2)}) collective-permute-start(bf16[16,64,512]{2,1,0:T(8,128)(2,1)S(1)} %maximum_select_fusion.a_ref), channel_id=1, source_target_pairs={{0,1},{1,0},{2,3},{3,2},{4,5},{5,4},{6,7},{7,6},{8,9},{9,8},{10,11... | collective-permute-start | bytes 3145736 | tf_op jit(solution)/shard_map/ppermute | solution.py:410
  49.9 14.6 %collective-permute-start.12 = (bf16[528,128]{1,0:T(8,128)(2,1)S(1)}, bf16[528,128]{1,0:T(8,128)(2,1)S(1)}, u32[]{:S(2)}, u32[]{:S(2)}) collective-permute-start(bf16[528,128]{1,0:T(8,128)(2,1)S(1)} %shard_map.120), channel_id=1, source_target_pairs={{2,0},{4,2},{6,4},{8,6},{10,8},{12,10},{14,12},{3,1},{5,3},{7,5},{... | collective-permute-start | bytes 405512 | tf_op jit(solution)/shard_map/ppermute | solution.py:450
  51.2 13.3 %collective-permute-start.13 = (bf16[272,128]{1,0:T(8,128)(2,1)S(1)}, bf16[272,128]{1,0:T(8,128)(2,1)S(1)}, u32[]{:S(2)}, u32[]{:S(2)}) collective-permute-start(bf16[272,128]{1,0:T(8,128)(2,1)S(1)} %slice.151), channel_id=1, source_target_pairs={{4,0},{6,2},{8,4},{10,6},{12,8},{14,10},{5,1},{7,3},{9,5},{11,7},{... | collective-permute-start | bytes 208904 | tf_op jit(solution)/shard_map/ppermute | solution.py:450
  52.6 11.8 %collective-permute-start.7 = (bf16[8,24,512]{2,1,0:T(8,128)(2,1)S(1)}, bf16[8,24,512]{2,1,0:T(8,128)(2,1)S(1)}, u32[]{:S(2)}, u32[]{:S(2)}) collective-permute-start(bf16[8,24,512]{2,1,0:T(8,128)(2,1)S(1)} %slice.114), channel_id=1, source_target_pairs={{0,4},{1,5},{2,6},{3,7},{4,0},{5,1},{6,2},{7,3},{8,12},{9,13},{10,... | collective-permute-start | bytes 589832 | tf_op jit(solution)/shard_map/ppermute | solution.py:410
  64.4 1.8 %collective-permute-start.8 = (bf16[16,24,512]{2,1,0:T(8,128)(2,1)S(1)}, bf16[16,24,512]{2,1,0:T(8,128)(2,1)S(1)}, u32[]{:S(2)}, u32[]{:S(2)}) collective-permute-start(bf16[16,24,512]{2,1,0:T(8,128)(2,1)S(1)} %maximum_select_fusion.6.b_ref), channel_id=1, source_target_pairs={{0,1},{1,0},{2,3},{3,2},{4,5},{5,4},{6,7},{7,6},{8,9},{9,8},{10,11... | collective-permute-start | bytes 1179656 | tf_op jit(solution)/shard_map/ppermute | solution.py:410
  66.2 7.8 %collective-permute-start.14 = (bf16[8,48,512]{2,1,0:T(8,128)(2,1)S(1)}, bf16[8,48,512]{2,1,0:T(8,128)(2,1)S(1)}, u32[]{:S(2)}, u32[]{:S(2)}) collective-permute-start(bf16[8,48,512]{2,1,0:T(8,128)(2,1)S(1)} %slice.120), channel_id=1, source_target_pairs={{0,16},{1,3},{2,18},{3,1},{4,20},{5,7},{6,22},{7,5},{8,24},{9,11},... | collective-permute-start | bytes 1179656 | tf_op jit(solution)/shard_map/ppermute | solution.py:410
  67.7 6.9 %collective-permute-start.16 = (bf16[8,32,512]{2,1,0:T(8,128)(2,1)S(1)}, bf16[8,32,512]{2,1,0:T(8,128)(2,1)S(1)}, u32[]{:S(2)}, u32[]{:S(2)}) collective-permute-start(bf16[8,32,512]{2,1,0:T(8,128)(2,1)S(1)} %slice.121), channel_id=1, source_target_pairs={{0,4},{1,5},{2,6},{3,7},{4,0},{5,1},{6,2},{7,3},{8,12},{9,13},{10,... | collective-permute-start | bytes 786440 | tf_op jit(solution)/shard_map/ppermute | solution.py:410
  74.1 13.1 %collective-permute-start.15 = (bf16[16,48,512]{2,1,0:T(8,128)(2,1)S(1)}, bf16[16,48,512]{2,1,0:T(8,128)(2,1)S(1)}, u32[]{:S(2)}, u32[]{:S(2)}) collective-permute-start(bf16[16,48,512]{2,1,0:T(8,128)(2,1)S(1)} %maximum_select_fusion.2.a_ref), channel_id=1, source_target_pairs={{0,1},{1,0},{2,3},{3,2},{4,5},{5,4},{6,7},{7,6},{8,9},{9,8},{10,11... | collective-permute-start | bytes 2359304 | tf_op jit(solution)/shard_map/ppermute | solution.py:410
  74.7 12.5 %collective-permute-start.17 = (bf16[16,32,512]{2,1,0:T(8,128)(2,1)S(1)}, bf16[16,32,512]{2,1,0:T(8,128)(2,1)S(1)}, u32[]{:S(2)}, u32[]{:S(2)}) collective-permute-start(bf16[16,32,512]{2,1,0:T(8,128)(2,1)S(1)} %maximum_select_fusion.3.b_ref), channel_id=1, source_target_pairs={{0,1},{1,0},{2,3},{3,2},{4,5},{5,4},{6,7},{7,6},{8,9},{9,8},{10,11... | collective-permute-start | bytes 1572872 | tf_op jit(solution)/shard_map/ppermute | solution.py:410
  83.0 1.2 copy-start.2
  84.2 1.3 copy-start.14
  85.5 0.9 copy-start.16
  86.4 0.8 copy-start.18
  98.4 1.4 copy-start
  99.8 1.1 copy-start.4
  100.9 1.1 copy-start.6
  102.0 7.7 %collective-permute-start.18 = (bf16[8,168,512]{2,1,0:T(8,128)(2,1)}, bf16[8,168,512]{2,1,0:T(8,128)(2,1)}, u32[]{:S(2)}, u32[]{:S(2)}) collective-permute-start(bf16[8,168,512]{2,1,0:T(8,128)(2,1)} %get-tuple-element.61), channel_id=1, source_target_pairs={{0,1},{1,0},{2,3},{3,2},{4,5},{5,4},{6,7},{7,6},{8,9},{9,8},{10,11... | collective-permute-start | bytes 4128776 | tf_op jit(solution)/shard_map/ppermute | solution.py:410
  102.4 1.6 copy-start.1
  104.0 1.4 copy-start.3
  105.4 1.4 copy-start.5
  106.8 2.9 %copy-start.7 = (bf16[8,168,512]{2,1,0:T(8,128)(2,1)S(1)}, bf16[8,168,512]{2,1,0:T(8,128)(2,1)}, u32[]{:S(2)}) copy-start(bf16[8,168,512]{2,1,0:T(8,128)(2,1)} %copy-done.6) | copy-start | bytes 4128772
  109.7 4.5 %copy-start.15 = (bf16[2,16,64,512]{3,2,1,0:T(8,128)(2,1)S(1)}, bf16[2,16,64,512]{3,2,1,0:T(8,128)(2,1)}, u32[]{:S(2)}) copy-start(bf16[2,16,64,512]{3,2,1,0:T(8,128)(2,1)} %copy-done.14) | copy-start | bytes 6291460
  111.6 6.9 %copy-start.20 = (bf16[8,168,512]{2,1,0:T(8,128)(2,1)}, bf16[8,168,512]{2,1,0:T(8,128)(2,1)S(1)}, u32[]{:S(2)}) copy-start(bf16[8,168,512]{2,1,0:T(8,128)(2,1)S(1)} %add_convert_fusion.1) | copy-start | bytes 4128772
  111.6 2.6 %copy-start.17 = (bf16[768,512]{1,0:T(8,128)(2,1)S(1)}, bf16[768,512]{1,0:T(8,128)(2,1)}, u32[]{:S(2)}) copy-start(bf16[768,512]{1,0:T(8,128)(2,1)} %copy-done.16) | copy-start | bytes 2359300
  111.6 2.6 %copy-start.19 = (bf16[512,512]{1,0:T(8,128)(2,1)S(1)}, bf16[512,512]{1,0:T(8,128)(2,1)}, u32[]{:S(2)}) copy-start(bf16[512,512]{1,0:T(8,128)(2,1)} %copy-done.18) | copy-start | bytes 1572868
  112.6 11.3 %collective-permute-start.23 = (bf16[1,2,2,168,512]{4,3,2,1,0:T(8,128)(2,1)}, bf16[1,2,2,168,512]{4,3,2,1,0:T(8,128)(2,1)}, u32[]{:S(2)}, u32[]{:S(2)}) collective-permute-start(bf16[1,2,2,168,512]{4,3,2,1,0:T(8,128)(2,1)} %constant_dynamic-slice_fusion.2), channel_id=1, source_target_pairs={{0,2},{1,5},{2,0},{3,7},{4,6},{5,1},{6,4},{7,3},{8,10},{9,13},{10,... | collective-permute-start | bytes 2064392 | tf_op jit(solution)/shard_map/ppermute | solution.py:410
  118.5 19.5 %collective-permute-start.19 = (bf16[8,168,512]{2,1,0:T(8,128)(2,1)S(1)}, bf16[8,168,512]{2,1,0:T(8,128)(2,1)}, u32[]{:S(2)}, u32[]{:S(2)}) collective-permute-start(bf16[8,168,512]{2,1,0:T(8,128)(2,1)S(1)} %get-tuple-element.75), channel_id=1, source_target_pairs={{0,1},{1,0},{2,3},{3,2},{4,5},{5,4},{6,7},{7,6},{8,9},{9,8},{10,11... | collective-permute-start | bytes 4128776 | tf_op jit(solution)/shard_map/ppermute | solution.py:410
  126.1 7.6 %collective-permute-start.24 = (bf16[1,1,2,168,512]{4,3,2,1,0:T(8,128)(2,1)}, bf16[1,1,2,168,512]{4,3,2,1,0:T(8,128)(2,1)}, u32[]{:S(2)}, u32[]{:S(2)}) collective-permute-start(bf16[1,1,2,168,512]{4,3,2,1,0:T(8,128)(2,1)} %constant_dynamic-slice_fusion.1), channel_id=1, source_target_pairs={{0,4},{1,3},{2,6},{3,1},{4,0},{5,7},{6,2},{7,5},{8,12},{9,11},{10,... | collective-permute-start | bytes 1032200 | tf_op jit(solution)/shard_map/ppermute | solution.py:410
  134.7 9.7 %collective-permute-start.25 = (bf16[1,1,1,168,512]{4,3,2,1,0:T(8,128)(2,1)S(1)}, bf16[1,1,1,168,512]{4,3,2,1,0:T(8,128)(2,1)S(1)}, u32[]{:S(2)}, u32[]{:S(2)}) collective-permute-start(bf16[1,1,1,168,512]{4,3,2,1,0:T(8,128)(2,1)S(1)} %constant_dynamic-slice_fusion), channel_id=1, source_target_pairs={{0,8},{1,9},{2,10},{3,11},{4,12},{5,13},{6,14},{7,15},{8,0},{9,1},... | collective-permute-start | bytes 516104 | tf_op jit(solution)/shard_map/ppermute | solution.py:410
  139.8 11.0 %collective-permute-start.20 = (bf16[1,2,2,168,512]{4,3,2,1,0:T(8,128)(2,1)S(1)}, bf16[1,2,2,168,512]{4,3,2,1,0:T(8,128)(2,1)S(1)}, u32[]{:S(2)}, u32[]{:S(2)}) collective-permute-start(bf16[1,2,2,168,512]{4,3,2,1,0:T(8,128)(2,1)S(1)} %constant_dynamic-slice_fusion.5), channel_id=1, source_target_pairs={{0,2},{1,5},{2,0},{3,7},{4,6},{5,1},{6,4},{7,3},{8,10},{9,13},{10,... | collective-permute-start | bytes 2064392 | tf_op jit(solution)/shard_map/ppermute | solution.py:410
  151.0 7.3 %collective-permute-start.21 = (bf16[1,1,2,168,512]{4,3,2,1,0:T(8,128)(2,1)S(1)}, bf16[1,1,2,168,512]{4,3,2,1,0:T(8,128)(2,1)S(1)}, u32[]{:S(2)}, u32[]{:S(2)}) collective-permute-start(bf16[1,1,2,168,512]{4,3,2,1,0:T(8,128)(2,1)S(1)} %constant_dynamic-slice_fusion.4), channel_id=1, source_target_pairs={{0,4},{1,3},{2,6},{3,1},{4,0},{5,7},{6,2},{7,5},{8,12},{9,11},{10,... | collective-permute-start | bytes 1032200 | tf_op jit(solution)/shard_map/ppermute | solution.py:410
  158.4 9.2 %collective-permute-start.22 = (bf16[1,1,1,168,512]{4,3,2,1,0:T(8,128)(2,1)S(1)}, bf16[1,1,1,168,512]{4,3,2,1,0:T(8,128)(2,1)S(1)}, u32[]{:S(2)}, u32[]{:S(2)}) collective-permute-start(bf16[1,1,1,168,512]{4,3,2,1,0:T(8,128)(2,1)S(1)} %constant_dynamic-slice_fusion.3), channel_id=1, source_target_pairs={{0,8},{1,9},{2,10},{3,11},{4,12},{5,13},{6,14},{7,15},{8,0},{9,1},... | collective-permute-start | bytes 516104 | tf_op jit(solution)/shard_map/ppermute | solution.py:410

commit v5 on v4

--- a/solution.py
+++ b/solution.py
@@ -18,7 +18,6 @@
 FIRST_LIMIT = 56 * 1024 * 1024
 WHOLE = pl.BlockSpec(memory_space=pltpu.VMEM)
 SCALAR = pl.BlockSpec(memory_space=pltpu.SMEM)
-STAYS = pl.BlockSpec(memory_space=pltpu.HBM)
 
 
 def dot(a, b):
@@ -33,16 +32,14 @@
     return lax.dot_general(a, b, (((0,), (0,)), ((), ())), preferred_element_type=F32)
 
 
-def call(kernel, outs, scratch, flops, *args, far=0, limit=VMEM_LIMIT):
-    outs = [o + (False,) * (3 - len(o)) for o in outs]
+def call(kernel, outs, scratch, flops, *args, limit=VMEM_LIMIT):
     moved = sum(a.size * a.dtype.itemsize for a in args)
-    moved += sum(math.prod(s) * jnp.dtype(d).itemsize for s, d, _ in outs)
-    near = args[: len(args) - far]
+    moved += sum(math.prod(s) * jnp.dtype(d).itemsize for s, d in outs)
     return pl.pallas_call(
         kernel,
-        out_shape=[jax.ShapeDtypeStruct(s, d) for s, d, _ in outs],
-        in_specs=[SCALAR if a.dtype == jnp.int32 and a.ndim == 1 else WHOLE for a in near] + [STAYS] * far,
-        out_specs=[STAYS if stays else WHOLE for _, _, stays in outs],
+        out_shape=[jax.ShapeDtypeStruct(s, d) for s, d in outs],
+        in_specs=[SCALAR if a.dtype == jnp.int32 and a.ndim == 1 else WHOLE for a in args],
+        out_specs=[WHOLE] * len(outs),
         scratch_shapes=scratch,
         compiler_params=pltpu.CompilerParams(vmem_limit_bytes=limit),
         cost_estimate=pl.CostEstimate(flops=flops, bytes_accessed=moved, transcendentals=0),
@@ -219,13 +216,9 @@
     return slice(i * TILE + offset, (i + 1) * TILE + offset)
 
 
-def copies(pairs, sems):
-    return [pltpu.make_async_copy(a, b, sems.at[k]) for k, (a, b) in enumerate(pairs)]
-
-
 def forward_first(before, steps, scalar_ref, norm_ref, a_ref, a2_ref, b_ref, b2_ref,
-                  h1_ref, w_out_ref, h0_far, gated_far, slope_far, conv_far, res_far,
-                  h0_ref, gated_ref, slope_ref, conv_ref, res_ref, in_ref, out_ref, sems):
+                  h1_ref, w_out_ref, kept_ref, gated_ref, slope_ref, conv_ref, res_ref,
+                  h0_ref, in_ref, out_ref):
     rows = h0_ref.shape[0]
     kept = slope_ref.shape[1]
     d = rows - h1_ref.shape[0]
@@ -236,10 +229,7 @@
     w_in = rows_of(in_ref[...])
     for i in range(rows // TILE):
         h0_ref[tile_of(i), :] = dot(norm_ref[tile_of(i), :], w_in).astype(BF16)
-    moves = copies([(conv_ref, conv_far), (res_ref, res_far), (h0_ref.at[before : before + kept], h0_far),
-                    (gated_ref, gated_far), (slope_ref, slope_far)], sems)
-    for move in moves[:3]:
-        move.start()
+    kept_ref[...] = h0_ref[before : before + kept, :]
     for i in range(h1_ref.shape[0] // TILE):
         now = h0_ref[tile_of(i, d), :]
         t, s = activate(h0_ref[tile_of(i), :], now, conv_ref)
@@ -251,11 +241,6 @@
             slope_ref[0, own, :], slope_ref[1, own, :] = (v.astype(BF16) for v in slopes(t, s))
             if first < steps:
                 gated_ref[own, :] = gated
-            if first + TILE == kept:
-                for move in moves[3:]:
-                    move.start()
-    for move in moves:
-        move.wait()
 
 
 def store_terms(core, keep_ref, send_ref, row, value, first, size, start, count, lane=0):
@@ -275,8 +260,9 @@
 
 
 def second_kernel(steps, scale, sizes, scalar_ref, h1_ref, w_out_ref, label_ref, a_ref, a2_ref, b_ref, b2_ref,
-                  loss_ref, keep_ref, send_ref, back_ref, grad_ref, conv_ref,
-                  res_ref, gated_ref, h2_ref, lgrad_ref, round_ref):
+                  slope0_ref, res0_ref,
+                  loss_ref, keep_ref, send_ref, grad0_ref, round0_ref, back0_ref,
+                  back_ref, grad_ref, conv_ref, res_ref, gated_ref, h2_ref, lgrad_ref, round_ref):
     rows, c = back_ref.shape[0], grad_ref.shape[1]
     d = h1_ref.shape[0] - rows
     classes = w_out_ref.shape[1]
@@ -336,6 +322,19 @@
         for q in range(c // classes):
             store_terms(*targets, 2 * conv + res, value, i * (TILE // (2 * out)), out, q * count, count, q * classes)
 
+    rows0 = back0_ref.shape[0]
+    weights = halves(conv_ref, 0), halves(conv_ref, 1)
+    for i in range(rows0 // TILE):
+        at = tile_of(i)
+        grad = grad_below(grad_ref[at, :], back_ref, i, rows - rows0, weights)
+        rounded = grad.astype(BF16)
+        back = dot_t(rounded, rows_of(res0_ref[...]))
+        back0_ref[at, :c] = (back * slope0_ref[0, at, :].astype(F32)).astype(BF16)
+        back0_ref[at, c:] = (back * slope0_ref[1, at, :].astype(F32)).astype(BF16)
+        if i * TILE < steps:
+            grad0_ref[at, :] = grad
+            round0_ref[at, :] = rounded
+
 
 def grad_below(grad, back_ref, i, d, weights):
     c = back_ref.shape[1] // 2
@@ -344,50 +343,20 @@
     return grad + dot_t(back_ref[tile_of(i, d), :c], filt_past) + dot_t(back_ref[tile_of(i, d), c:], gate_past)
 
 
-def grad_first(back1_ref, grad2_ref, conv1_ref, slope_far, res_far,
-               grad_ref, round_ref, back_ref, slope_ref, res_ref, sems):
-    rows, c = back_ref.shape[0], grad_ref.shape[1]
-    d1 = back1_ref.shape[0] - rows
-    moves = copies([(slope_far, slope_ref), (res_far, res_ref)], sems)
-    for move in moves:
-        move.start()
-    weights = halves(conv1_ref, 0), halves(conv1_ref, 1)
-    for i in range(rows // TILE):
-        at = tile_of(i)
-        grad = grad_below(grad2_ref[at, :], back1_ref, i, d1, weights)
-        rounded = grad.astype(BF16)
-        if i == 0:
-            for move in moves:
-                move.wait()
-        back = dot_t(rounded, rows_of(res_ref[...]))
-        back_ref[at, :c] = (back * slope_ref[0, at, :].astype(F32)).astype(BF16)
-        back_ref[at, c:] = (back * slope_ref[1, at, :].astype(F32)).astype(BF16)
-        if i * TILE < grad_ref.shape[0]:
-            grad_ref[at, :] = grad
-            round_ref[at, :] = rounded
-
-
-def terms_first(sizes, scalar_ref, back_ref, grad_ref, round_ref, norm_ref, h0_far, gated_far, conv_far,
-                keep_ref, send_ref, h0_ref, gated_ref, conv_ref, last_ref, sems):
+def terms_first(sizes, scalar_ref, back_ref, grad_ref, round_ref, norm_ref, h0_ref, gated_ref, conv_ref,
+                keep_ref, send_ref, last_ref):
     steps, c = grad_ref.shape
     d0 = back_ref.shape[0] - steps
     conv, res, enter, _ = sizes
-    moves = copies([(h0_far, h0_ref), (gated_far, gated_ref), (conv_far, conv_ref)], sems)
-    for move in moves:
-        move.start()
     own = slice(0, steps)
     targets = (scalar_ref[0], keep_ref, send_ref)
-    moves[0].wait()
     for i in range(c // TILE):
         at = tile_of(i)
         first, per = i * (TILE // (2 * conv)), c // (2 * conv)
         conv_terms(targets, first, conv, t_dot(h0_ref[0:steps, at], back_ref[own, :]))
         conv_terms(targets, first + per, conv, t_dot(h0_ref[d0 : d0 + steps, at], back_ref[own, :]))
-        if i == 0:
-            moves[1].wait()
         value = t_dot(gated_ref[:, at], round_ref[...])
         store_terms(*targets, 2 * conv, value, i * (TILE // (2 * res)), res, 0, res)
-    moves[2].wait()
     weights = halves(conv_ref, 0), halves(conv_ref, 1)
     for i in range(steps // TILE):
         last_ref[tile_of(i), :] = grad_below(grad_ref[tile_of(i), :], back_ref, i, d0, weights).astype(BF16)
@@ -435,14 +404,21 @@
     return lax.dynamic_index_in_dim(held, mine, dim).astype(F32) + other.astype(F32)
 
 
-def sum_rest(held):
-    shape, bits = held.shape[1:], time_bits()
-    held = held.reshape((2,) * bits + shape)
-    held = sum_step(held, (NEAR, FAR)).astype(BF16)
-    total = sum_step(held, (FAR, NEAR), 1)
-    for bit in range(2, bits):
-        total = sum_step(total.astype(BF16), (("tm", bit),) * 2, 2 + bits - 1 - bit)
-    return total.reshape(shape)
+def sum_steps():
+    bits = time_bits()
+
+    def first(held):
+        return sum_step(held.reshape((2,) * bits + held.shape[1:]), (NEAR, FAR)).astype(BF16)
+
+    def later(links, dim, last):
+        def step(held):
+            total = sum_step(held, links, dim)
+            return total if last else total.astype(BF16)
+
+        return step
+
+    rest = [later((("tm", bit),) * 2, 1 + bits - bit, bit == bits - 1) for bit in range(2, bits)]
+    return [first, later((FAR, NEAR), 1, not rest)] + rest
 
 
 def hop(value, by):
@@ -514,6 +490,7 @@
     main, side, carry = together(main, side, carry)
     carry = grow(carry, (FAR, NEAR))
     main, side = grow(main, main_links[1]), grow(side, side_links[1])
+    main, side, carry = together(main, side, carry)
     label_rows = steps // bands
     bits = time_bits()
     carry = carry.reshape((2,) * bits + (CARRY_ROWS, c))
@@ -521,7 +498,7 @@
     (normed,) = call(norm_kernel, [((LABEL_ROWS + steps, bands), BF16)], [], 10 * steps * bands,
                      scalars, feat, keep, mass, weight, carry.reshape(time_devices, CARRY_ROWS, c),
                      labels[0].reshape(label_rows, bands))
-    main, side = together(main, side)
+    main, side, normed = together(main, side, normed)
     first = [main[:, :conv], side[:, : half + enter]]
     second = [main[:, conv:], side[:, half + enter :]]
 
@@ -531,53 +508,58 @@
     def both_cores(parts):
         return [v.astype(kind) for p in parts for v in (p, swap(p, (CORE, CORE)))]
 
-    first = both_cores(last_step(first))
+    first = last_step(first)
     past, future = rows_before(normed, reach), rows_after(normed, reach)
+    *first, second[0], second[1], past, future = together(*first, *second, past, future)
     own_normed = normed[LABEL_ROWS:]
     window = jnp.concatenate(past + [own_normed] + [v[LABEL_ROWS:] for v in future])
     label_window = jnp.concatenate(
         [v[: (v.shape[0] - LABEL_ROWS) // bands] for v in [normed] + future])
-    *first, window, second[0], second[1] = together(*first, window, *second)
+    first, second = both_cores(first), last_step(second)
 
     total_rows, rows0, rows1 = steps + 2 * reach, steps + d0, steps + reach
     conv_all, res_all = ((2, devices, conv, c), kind), ((devices, res, c), kind)
-    V, sems = pltpu.VMEM, pltpu.SemaphoreType.DMA
-    h1, out_all, *kept = call(
+    V = pltpu.VMEM
+    h1, out_all, h0, gated0, slope0, conv0, res0 = call(
         functools.partial(forward_first, d1, steps),
-        [((total_rows - d0, c), BF16), ((c, classes), BF16), ((rows0, c), BF16, True), ((steps, c), BF16, True),
-         ((2, rows0, c), BF16, True), conv_all + (True,), res_all + (True,)],
-        [V((total_rows, c), BF16), V((steps, c), BF16), V((2, rows0, c), BF16), V(*conv_all), V(*res_all),
-         V((devices, enter, c), F32), V((devices, out, classes), F32), sems((5,))],
+        [((total_rows - d0, c), BF16), ((c, classes), BF16), ((rows0, c), BF16), ((steps, c), BF16),
+         ((2, rows0, c), BF16), conv_all, res_all],
+        [V((total_rows, c), BF16), V((devices, enter, c), F32), V((devices, out, classes), F32)],
         2 * total_rows * c * (bands + 5 * c), scalars, window, *first)
-    h0, gated0, slope0, conv0, res0 = kept
-
-    second = both_cores(last_step(second))
+
+    *second, h1 = together(*second, h1)
+    second = both_cores(second)
     scale = 1.0 / math.sqrt(site_devices * steps * time_devices)
     package = [((time_devices, 2 * conv + res + enter, c), kind)] * 2
-    loss, keep1, send1, back1, grad2, conv1 = call(
+    loss, keep1, send1, grad1, round0, back0 = call(
         functools.partial(second_kernel, steps, scale, sizes),
-        [((label_rows, bands), F32)] + package + [((rows1, 2 * c), BF16), ((rows0, c), F32), conv_all],
-        [V(*res_all), V((steps, c), BF16), V((steps, c), BF16), V((steps, classes), BF16), V((steps, c), BF16)],
-        2 * rows1 * c * 6 * c + 2 * steps * 5 * c * c,
-        scalars, h1, out_all, label_window, *second)
-
-    core = (CORE, CORE)
-    sum1 = (keep1.astype(F32) + swap(send1.astype(BF16), core).astype(F32)).astype(BF16)
-    grad1, round0, back0 = call(
-        grad_first, [((steps, c), F32), ((steps, c), BF16), ((rows0, 2 * c), BF16)],
-        [V((2, rows0, c), BF16), V(*res_all), sems((2,))],
-        2 * rows0 * c * 5 * c, back1, grad2, conv1, slope0, res0, far=2)
-    sum1, back0 = together(sum1, back0)
+        [((label_rows, bands), F32)] + package + [((steps, c), F32), ((steps, c), BF16), ((rows0, 2 * c), BF16)],
+        [V((rows1, 2 * c), BF16), V((rows0, c), F32), V(*conv_all), V(*res_all),
+         V((steps, c), BF16), V((steps, c), BF16), V((steps, classes), BF16), V((steps, c), BF16)],
+        2 * rows1 * c * 6 * c + 2 * steps * 5 * c * c + 2 * rows0 * c * 5 * c,
+        scalars, h1, out_all, label_window, *second, slope0, res0)
+
+    def core_sum(keep, send):
+        other = swap(send.astype(BF16), (CORE, CORE))
+        return (keep.astype(F32) + other.astype(F32)).astype(BF16)
+
+    sum1 = core_sum(keep1, send1)
     keep0, send0 = call(
-        functools.partial(terms_first, sizes), package,
-        [V((rows0, c), BF16), V((steps, c), BF16), V(*conv_all), V((steps, c), BF16), sems((3,))],
-        2 * steps * 9 * c * c,
-        scalars, back0, grad1, round0, own_normed, h0, gated0, conv0, far=3)
-    sum0 = (keep0.astype(F32) + swap(send0.astype(BF16), core).astype(F32)).astype(BF16)
+        functools.partial(terms_first, sizes), package, [V((steps, c), BF16)],
+        2 * steps * 9 * c * c, scalars, back0, grad1, round0, own_normed, h0, gated0, conv0)
+    sum1, keep0, send0 = together(sum1, keep0, send0)
+
+    chain1, chain0 = sum_steps(), [core_sum] + sum_steps()
+    sum1, sum0 = chain1[0](sum1), chain0[0](keep0, send0)
+    for step in range(1, len(chain0)):
+        sum1, sum0 = together(sum1, sum0)
+        if step < len(chain1):
+            sum1 = chain1[step](sum1)
+        sum0 = chain0[step](sum0)
 
     convs, ress, extras = [], [], []
     for held in (sum0, sum1):
-        total = sum_rest(held)
+        total = held.reshape(held.shape[-2:])
         convs.append(jnp.concatenate([total[:conv], total[conv : 2 * conv]], axis=1))
         ress.append(total[2 * conv : 2 * conv + res])
         extras.append(total[2 * conv + res :])

time: 170 us -> 145 us (0.85)
  local copies, waits for them, and re-layouts: 16 us -> 3.11 us
  waiting for transfers between devices: 73.1 us -> 63.5 us
  starting transfers between devices: 35.5 us -> 39.4 us
  Pallas kernels: 29.8 us -> 26.2 us
  other arithmetic: 13.5 us -> 10.9 us
    unnamed x48 -> x16, local copies, waits for them, and re-layouts: 12.3 us -> 0.94 us
    ppermute x22, waiting for transfers between devices: 73.1 us -> 62 us  [swap(): return lax.ppermute(value, names, pairs)]
    pallas_call x6 -> x5, Pallas kernels: 29.8 us -> 26.2 us  [call(): pl.pallas_call(kernel, out_shape=[jax.ShapeDtypeStruct(s, d) for s, d in...]
    ppermute x4, starting transfers between devices: 8.45 us -> 11.9 us  [hop(): lax.ppermute(value, 'tm', [(i, i + by) for i in range(size) if 0 <= i + b...]
    select_n x10, other arithmetic: 4.16 us -> 1.8 us  [grow(): jnp.where(my_bit(links) == 0, jnp.concatenate([held, other]), jnp.concate...]
  transfers between devices with their start and end apart: 26 -> 26, of which waited for: 15 -> 13; matrix products, arithmetic and copies ran while one was open for 5% -> 3% of each run, Pallas kernels for 9% -> 2%
where the time goes in v5:
time: 145 us
  waiting for transfers between devices  63.5 us (44%)
  starting transfers between devices  39.4 us (27%)
  Pallas kernels  26.2 us (18%)
  other arithmetic  10.9 us (8%)
  local copies, waits for them, and re-layouts  3.11 us (2%)
  between operations  1.82 us (1%)
    ppermute x22, waiting for transfers between devices, swap(): return lax.ppermute(value, names, pairs)  62 us
    ppermute x22, starting transfers between devices, swap(): return lax.ppermute(value, names, pairs)  27.5 us
    pallas_call x5, Pallas kernels, call(): pl.pallas_call(kernel, out_shape=[jax.ShapeDtypeStruct(s, d) for s, d in...  26.2 us
    ppermute x4, starting transfers between devices, hop(): lax.ppermute(value, 'tm', [(i, i + by) for i in range(size) if 0 <= i + b...  11.9 us
    convert_element_type x2, other arithmetic, core_sum(): return (keep.astype(F32) + other.astype(F32)).astype(BF16)  3.2 us
  transfers between devices with their start and end apart: 26, of which 13 were waited for; matrix products, arithmetic and copies ran while one was open for 3% of the time, Pallas kernels for 2%

profile of v5, /device:TPU:0, one launch (start us, length us, event | category | flops | bytes accessed | tf_op | source)
XLA Modules:
  0.0 145.0 jit_solution(11862186314829514644)
XLA Ops:
  1.3 0.7 pad_add_fusion.scalar_ref
  1.9 2.7 %shard_map.119 = (f32[512,128]{1,0:T(8,128)}, f32[512,128]{1,0:T(8,128)}, f32[512,128]{1,0:T(8,128)}, bf16[176,512]{1,0:T(8,128)(2,1)}, f32[8,512]{1,0:T(8,128)}) custom-call(s32[4]{0:T(128)} %pad_add_fusion.scalar_ref, f32[512,128]{1,0:T(8,128)} %bitcast.34, f32[512,128]{1,0:T(8,128)} %bitcast.42, bf16[2,64,1024]{2,1,0:T(8,128)(2,1)} %conv_ref.1, ...), custom_call_target="tpu_custom_call" | custom-call | flops 2621440 | bytes 1851408 | tf_op jit(solution)/shard_map/pallas_call | solution.py:38
  4.6 4.0 %collective-permute-start = (bf16[1,176,512]{2,1,0:T(8,128)(2,1)}, bf16[1,176,512]{2,1,0:T(8,128)(2,1)S(1)}, u32[]{:S(2)}, u32[]{:S(2)}) collective-permute-start(bf16[1,176,512]{2,1,0:T(8,128)(2,1)} %bitcast.44), channel_id=1, source_target_pairs={{0,8},{1,9},{2,10},{3,11},{4,12},{5,13},{6,14},{7,15},{8,0},{9,1},... | collective-permute-start | bytes 540680 | tf_op jit(solution)/shard_map/ppermute | solution.py:379
  8.7 8.6 %collective-permute-done = bf16[1,176,512]{2,1,0:T(8,128)(2,1)S(1)} collective-permute-done((bf16[1,176,512]{2,1,0:T(8,128)(2,1)}, bf16[1,176,512]{2,1,0:T(8,128)(2,1)S(1)}, u32[]{:S(2)}, u32[]{:S(2)}) %collective-permute-start) | collective-permute-done | bytes 180256 | tf_op jit(solution)/shard_map/ppermute | solution.py:379
  17.3 1.1 maximum_select_fusion.7
  18.4 1.6 %collective-permute-start.1 = (bf16[2,120,512]{2,1,0:T(8,128)(2,1)S(1)}, bf16[2,120,512]{2,1,0:T(8,128)(2,1)S(1)}, u32[]{:S(2)}, u32[]{:S(2)}) collective-permute-start(bf16[2,120,512]{2,1,0:T(8,128)(2,1)S(1)} %slice.143), channel_id=1, source_target_pairs={{0,2},{1,5},{2,0},{3,7},{4,6},{5,1},{6,4},{7,3},{8,10},{9,13},{10,... | collective-permute-start | bytes 737288 | tf_op jit(solution)/shard_map/ppermute | solution.py:379
  20.0 1.6 %collective-permute-start.2 = (bf16[2,56,512]{2,1,0:T(8,128)(2,1)S(1)}, bf16[2,56,512]{2,1,0:T(8,128)(2,1)S(1)}, u32[]{:S(2)}, u32[]{:S(2)}) collective-permute-start(bf16[2,56,512]{2,1,0:T(8,128)(2,1)S(1)} %slice.146), channel_id=1, source_target_pairs={{0,16},{1,17},{2,18},{3,19},{4,20},{5,21},{6,22},{7,23},{8,24},{9,... | collective-permute-start | bytes 344072 | tf_op jit(solution)/shard_map/ppermute | solution.py:379
  21.6 3.3 %collective-permute-done.2 = bf16[2,56,512]{2,1,0:T(8,128)(2,1)S(1)} collective-permute-done((bf16[2,56,512]{2,1,0:T(8,128)(2,1)S(1)}, bf16[2,56,512]{2,1,0:T(8,128)(2,1)S(1)}, u32[]{:S(2)}, u32[]{:S(2)}) %collective-permute-start.2) | collective-permute-done | bytes 114720 | tf_op jit(solution)/shard_map/ppermute | solution.py:379
  24.9 0.1 maximum_select_fusion.4
  25.1 0.8 collective-permute-start.3
  26.0 1.3 collective-permute-start.4
  27.2 1.2 collective-permute-start.5
  28.5 5.5 %collective-permute-done.5 = bf16[4,8,512]{2,1,0:T(8,128)(2,1)S(1)} collective-permute-done((bf16[4,8,512]{2,1,0:T(8,128)(2,1)S(1)}, bf16[4,8,512]{2,1,0:T(8,128)(2,1)S(1)}, u32[]{:S(2)}, u32[]{:S(2)}) %collective-permute-start.5) | collective-permute-done | bytes 32800 | tf_op jit(solution)/shard_map/ppermute | solution.py:379
  34.1 0.1 maximum_select_fusion.5
  34.2 0.1 maximum_select_fusion.1
  34.4 0.6 copy-done
  35.0 0.1 copy-done.1
  35.1 0.1 copy-done.2
  35.1 0.1 copy-done.3
  35.2 0.7 shard_map.120
  36.0 1.6 %collective-permute-start.6 = (bf16[8,64,512]{2,1,0:T(8,128)(2,1)S(1)}, bf16[8,64,512]{2,1,0:T(8,128)(2,1)S(1)}, u32[]{:S(2)}, u32[]{:S(2)}) collective-permute-start(bf16[8,64,512]{2,1,0:T(8,128)(2,1)S(1)} %slice.113), channel_id=1, source_target_pairs={{0,16},{1,3},{2,18},{3,1},{4,20},{5,7},{6,22},{7,5},{8,24},{9,11},... | collective-permute-start | bytes 1572872 | tf_op jit(solution)/shard_map/ppermute | solution.py:379
  37.6 0.8 collective-permute-start.7
  38.5 1.3 collective-permute-start.10
  39.8 4.6 %collective-permute-start.9 = (bf16[512,128]{1,0:T(8,128)(2,1)S(1)}, bf16[512,128]{1,0:T(8,128)(2,1)S(1)}, u32[]{:S(2)}, u32[]{:S(2)}) collective-permute-start(bf16[512,128]{1,0:T(8,128)(2,1)S(1)} %slice.118.norm_ref), channel_id=1, source_target_pairs={{0,2},{2,4},{4,6},{6,8},{8,10},{10,12},{12,14},{1,3},{3,5},{5,7},{... | collective-permute-start | bytes 393224 | tf_op jit(solution)/shard_map/ppermute | solution.py:426
  44.4 1.3 collective-permute-start.11
  45.7 4.7 %collective-permute-start.8 = (bf16[256,128]{1,0:T(8,128)(2,1)S(1)}, bf16[256,128]{1,0:T(8,128)(2,1)S(1)}, u32[]{:S(2)}, u32[]{:S(2)}) collective-permute-start(bf16[256,128]{1,0:T(8,128)(2,1)S(1)} %slice.117), channel_id=1, source_target_pairs={{0,4},{2,6},{4,8},{6,10},{8,12},{10,14},{1,5},{3,7},{5,9},{7,11},{... | collective-permute-start | bytes 196616 | tf_op jit(solution)/shard_map/ppermute | solution.py:426
  50.5 0.2 maximum_select_fusion.a_ref
  50.7 1.5 %collective-permute-done.8 = bf16[256,128]{1,0:T(8,128)(2,1)S(1)} collective-permute-done((bf16[256,128]{1,0:T(8,128)(2,1)S(1)}, bf16[256,128]{1,0:T(8,128)(2,1)S(1)}, u32[]{:S(2)}, u32[]{:S(2)}) %collective-permute-start.8) | collective-permute-done | bytes 65568 | tf_op jit(solution)/shard_map/ppermute | solution.py:426
  52.2 0.5 collective-permute-start.15
  52.7 2.4 %collective-permute-start.13 = (bf16[8,32,512]{2,1,0:T(8,128)(2,1)S(1)}, bf16[8,32,512]{2,1,0:T(8,128)(2,1)S(1)}, u32[]{:S(2)}, u32[]{:S(2)}) collective-permute-start(bf16[8,32,512]{2,1,0:T(8,128)(2,1)S(1)} %slice.116), channel_id=1, source_target_pairs={{0,4},{1,5},{2,6},{3,7},{4,0},{5,1},{6,2},{7,3},{8,12},{9,13},{10,... | collective-permute-start | bytes 786440 | tf_op jit(solution)/shard_map/ppermute | solution.py:379
  55.1 0.5 collective-permute-start.12
  55.7 5.9 %collective-permute-done.13 = bf16[8,32,512]{2,1,0:T(8,128)(2,1)S(1)} collective-permute-done((bf16[8,32,512]{2,1,0:T(8,128)(2,1)S(1)}, bf16[8,32,512]{2,1,0:T(8,128)(2,1)S(1)}, u32[]{:S(2)}, u32[]{:S(2)}) %collective-permute-start.13) | collective-permute-done | bytes 262176 | tf_op jit(solution)/shard_map/ppermute | solution.py:379
  61.6 0.1 maximum_select_fusion.3.b_ref
  61.7 1.1 collective-permute-done.12
  62.9 0.1 maximum_select_fusion.2.a_ref
  63.0 7.1 %shard_map.121 = (bf16[1792,512]{1,0:T(8,128)(2,1)S(1)}, bf16[512,128]{1,0:T(8,128)(2,1)S(1)}, bf16[768,512]{1,0:T(8,128)(2,1)S(1)}, bf16[512,512]{1,0:T(8,128)(...) custom-call(s32[4]{0:T(128)S(1)} %copy-done.4, ...), custom_call_target="tpu_custom_call" | custom-call | flops 5637144576 | bytes 10878992 | tf_op jit(solution)/shard_map/pallas_call | solution.py:38
  70.3 0.5 collective-permute-start.17
  70.8 2.5 %collective-permute-done.17.b2_ref = bf16[16,32,512]{2,1,0:T(8,128)(2,1)S(1)} collective-permute-done((bf16[16,32,512]{2,1,0:T(8,128)(2,1)S(1)}, bf16[16,32,512]{2,1,0:T(8,128)(2,1)S(1)}, u32[]{:S(2)}, u32[]{:S(2)}) %collective-permute-start.17) | collective-permute-done | bytes 524320 | tf_op jit(solution)/shard_map/ppermute | solution.py:379
  73.3 12.3 %shard_map.122 = (f32[4,128]{1,0:T(4,128)}, bf16[8,168,512]{2,1,0:T(8,128)(2,1)S(1)}, bf16[8,168,512]{2,1,0:T(8,128)(2,1)S(1)}, f32[512,512]{1,0:T(8,128)S(1)}, ...) custom-call(s32[4]{0:T(128)S(1)} %copy-done.4, bf16[1792,512]{1,0:T(8,128)(2,1)S(1)} %get-tuple-element.75.h1_ref, ...), custom_call_target="tpu_custom_call" | custom-call | flops 7381975040 | bytes 12587536 | tf_op jit(solution)/shard_map/pallas_call | solution.py:38
  85.6 0.2 collective-permute-start.18
  85.8 3.3 %shard_map.123 = (bf16[8,168,512]{2,1,0:T(8,128)(2,1)S(1)}, bf16[8,168,512]{2,1,0:T(8,128)(2,1)S(1)}) custom-call(s32[4]{0:T(128)S(1)} %copy-done.4, bf16[768,1024]{1,0:T(8,128)(2,1)S(1)} %get-tuple-element.84.back_ref, f32[512,512]{1,0:T(8,128)S(1)} %get-tuple-element.85.grad_ref, bf16[512,512]{1,0:T(8,128)(2,1)S(1)} %get-tuple-element.86.round_ref, ...), custom_call_target="tpu_custom_call" | custom-call | flops 2415919104 | bytes 9437200 | tf_op jit(solution)/shard_map/pallas_call | solution.py:38
  89.2 1.5 %add_convert_fusion.1 = bf16[8,168,512]{2,1,0:T(8,128)(2,1)} fusion(bf16[8,168,512]{2,1,0:T(8,128)(2,1)S(1)} %collective-permute-done.18, bf16[8,168,512]{2,1,0:T(8,128)(2,1)S(1)} %get-tuple-element.82), kind=kLoop, calls=%fused_computation.1 | loop fusion | flops 2752512 | bytes 4128768 | tf_op jit(solution)/shard_map/convert_element_type | solution.py:544
  90.6 0.4 collective-permute-start.20
  91.0 1.1 constant_dynamic-slice_fusion.5
  92.2 2.3 %collective-permute-start.19 = (bf16[1,2,2,168,512]{4,3,2,1,0:T(8,128)(2,1)S(1)}, bf16[1,2,2,168,512]{4,3,2,1,0:T(8,128)(2,1)}, u32[]{:S(2)}, u32[]{:S(2)}) collective-permute-start(bf16[1,2,2,168,512]{4,3,2,1,0:T(8,128)(2,1)S(1)} %constant_dynamic-slice_fusion.5), channel_id=1, source_target_pairs={{0,2},{1,5},{2,0},{3,7},{4,6},{5,1},{6,4},{7,3},{8,10},{9,13},{10,... | collective-permute-start | bytes 2064392 | tf_op jit(solution)/shard_map/ppermute | solution.py:379
  94.4 9.0 %collective-permute-done.19 = bf16[1,2,2,168,512]{4,3,2,1,0:T(8,128)(2,1)} collective-permute-done((bf16[1,2,2,168,512]{4,3,2,1,0:T(8,128)(2,1)S(1)}, bf16[1,2,2,168,512]{4,3,2,1,0:T(8,128)(2,1)}, u32[]{:S(2)}, u32[]{:S(2)}) %collective-permute-start.19) | collective-permute-done | bytes 688160 | tf_op jit(solution)/shard_map/ppermute | solution.py:379
  103.4 1.5 %add_convert_fusion.3 = bf16[1,2,2,168,512]{4,3,2,1,0:T(8,128)(2,1)S(1)} fusion(bf16[1,2,2,168,512]{4,3,2,1,0:T(8,128)(2,1)} %collective-permute-done.19, bf16[2,2,2,168,512]{4,3,2,1,0:T(8,128)(2,1)} %bitcast.41, s32[]{:T(128)S(6)} %select_n.157), kind=kLoop, calls=%fused_computation.3 | loop fusion | flops 1376256 | bytes 2064388 | tf_op jit(solution)/shard_map/convert_element_type | solution.py:411
  104.9 1.7 %add_convert_fusion = bf16[8,168,512]{2,1,0:T(8,128)(2,1)S(1)} fusion(bf16[8,168,512]{2,1,0:T(8,128)(2,1)} %collective-permute-done.20, bf16[8,168,512]{2,1,0:T(8,128)(2,1)S(1)} %get-tuple-element.93), kind=kLoop, calls=%fused_computation | loop fusion | flops 2752512 | bytes 4128768 | tf_op jit(solution)/shard_map/convert_element_type | solution.py:544
  106.8 2.1 %collective-permute-start.22 = (bf16[1,2,2,168,512]{4,3,2,1,0:T(8,128)(2,1)S(1)}, bf16[1,2,2,168,512]{4,3,2,1,0:T(8,128)(2,1)}, u32[]{:S(2)}, u32[]{:S(2)}) collective-permute-start(bf16[1,2,2,168,512]{4,3,2,1,0:T(8,128)(2,1)S(1)} %constant_dynamic-slice_fusion.3), channel_id=1, source_target_pairs={{0,2},{1,5},{2,0},{3,7},{4,6},{5,1},{6,4},{7,3},{8,10},{9,13},{10,... | collective-permute-start | bytes 2064392 | tf_op jit(solution)/shard_map/ppermute | solution.py:379
  108.9 0.7 collective-permute-start.21
  109.6 10.0 %collective-permute-done.21 = bf16[1,1,2,168,512]{4,3,2,1,0:T(8,128)(2,1)S(1)} collective-permute-done((bf16[1,1,2,168,512]{4,3,2,1,0:T(8,128)(2,1)S(1)}, bf16[1,1,2,168,512]{4,3,2,1,0:T(8,128)(2,1)S(1)}, u32[]{:S(2)}, u32[]{:S(2)}) %collective-permute-start.21) | collective-permute-done | bytes 344096 | tf_op jit(solution)/shard_map/ppermute | solution.py:379
  119.6 0.1 add_convert_fusion.5
  119.7 0.9 collective-permute-done.22
  120.6 1.3 add_convert_fusion.2
  121.9 3.4 %collective-permute-start.23 = (bf16[1,1,1,168,512]{4,3,2,1,0:T(8,128)(2,1)S(1)}, bf16[1,1,1,168,512]{4,3,2,1,0:T(8,128)(2,1)S(1)}, u32[]{:S(2)}, u32[]{:S(2)}) collective-permute-start(bf16[1,1,1,168,512]{4,3,2,1,0:T(8,128)(2,1)S(1)} %constant_dynamic-slice_fusion.2), channel_id=1, source_target_pairs={{0,8},{1,9},{2,10},{3,11},{4,12},{5,13},{6,14},{7,15},{8,0},{9,1},... | collective-permute-start | bytes 516104 | tf_op jit(solution)/shard_map/ppermute | solution.py:379
  125.3 1.4 collective-permute-start.24
  126.7 5.7 %collective-permute-done.23 = bf16[1,1,1,168,512]{4,3,2,1,0:T(8,128)(2,1)S(1)} collective-permute-done((bf16[1,1,1,168,512]{4,3,2,1,0:T(8,128)(2,1)S(1)}, bf16[1,1,1,168,512]{4,3,2,1,0:T(8,128)(2,1)S(1)}, u32[]{:S(2)}, u32[]{:S(2)}) %collective-permute-start.23) | collective-permute-done | bytes 172064 | tf_op jit(solution)/shard_map/ppermute | solution.py:379
  132.5 2.9 %collective-permute-done.24 = bf16[1,1,2,168,512]{4,3,2,1,0:T(8,128)(2,1)S(1)} collective-permute-done((bf16[1,1,2,168,512]{4,3,2,1,0:T(8,128)(2,1)S(1)}, bf16[1,1,2,168,512]{4,3,2,1,0:T(8,128)(2,1)S(1)}, u32[]{:S(2)}, u32[]{:S(2)}) %collective-permute-start.24) | collective-permute-done | bytes 344096 | tf_op jit(solution)/shard_map/ppermute | solution.py:379
  135.4 0.1 add_convert_fusion.4
  135.6 0.6 pad_maximum_fusion.3
  136.3 6.5 %collective-permute-done.25 = bf16[1,1,1,168,512]{4,3,2,1,0:T(8,128)(2,1)S(1)} collective-permute-done((bf16[1,1,1,168,512]{4,3,2,1,0:T(8,128)(2,1)S(1)}, bf16[1,1,1,168,512]{4,3,2,1,0:T(8,128)(2,1)S(1)}, u32[]{:S(2)}, u32[]{:S(2)}) %collective-permute-start.25) | collective-permute-done | bytes 172064 | tf_op jit(solution)/shard_map/ppermute | solution.py:379
  142.8 0.6 slice_bitcast_fusion.6
  143.5 0.7 pad_maximum_fusion.2
  144.1 0.8 pad_maximum_fusion
  (65 shorter events, 1.0 us)
Async XLA Ops:
  4.6 12.7 %collective-permute-start = (bf16[1,176,512]{2,1,0:T(8,128)(2,1)}, bf16[1,176,512]{2,1,0:T(8,128)(2,1)S(1)}, u32[]{:S(2)}, u32[]{:S(2)}) collective-permute-start(bf16[1,176,512]{2,1,0:T(8,128)(2,1)} %bitcast.44), channel_id=1, source_target_pairs={{0,8},{1,9},{2,10},{3,11},{4,12},{5,13},{6,14},{7,15},{8,0},{9,1},... | collective-permute-start | bytes 540680 | tf_op jit(solution)/shard_map/ppermute | solution.py:379
  18.4 6.5 %collective-permute-start.1 = (bf16[2,120,512]{2,1,0:T(8,128)(2,1)S(1)}, bf16[2,120,512]{2,1,0:T(8,128)(2,1)S(1)}, u32[]{:S(2)}, u32[]{:S(2)}) collective-permute-start(bf16[2,120,512]{2,1,0:T(8,128)(2,1)S(1)} %slice.143), channel_id=1, source_target_pairs={{0,2},{1,5},{2,0},{3,7},{4,6},{5,1},{6,4},{7,3},{8,10},{9,13},{10,... | collective-permute-start | bytes 737288 | tf_op jit(solution)/shard_map/ppermute | solution.py:379
  20.0 4.9 %collective-permute-start.2 = (bf16[2,56,512]{2,1,0:T(8,128)(2,1)S(1)}, bf16[2,56,512]{2,1,0:T(8,128)(2,1)S(1)}, u32[]{:S(2)}, u32[]{:S(2)}) collective-permute-start(bf16[2,56,512]{2,1,0:T(8,128)(2,1)S(1)} %slice.146), channel_id=1, source_target_pairs={{0,16},{1,17},{2,18},{3,19},{4,20},{5,21},{6,22},{7,23},{8,24},{9,... | collective-permute-start | bytes 344072 | tf_op jit(solution)/shard_map/ppermute | solution.py:379
  25.1 9.1 %collective-permute-start.3 = (bf16[4,112,512]{2,1,0:T(8,128)(2,1)S(1)}, bf16[4,112,512]{2,1,0:T(8,128)(2,1)S(1)}, u32[]{:S(2)}, u32[]{:S(2)}) collective-permute-start(bf16[4,112,512]{2,1,0:T(8,128)(2,1)S(1)} %pad_maximum_fusion.1), channel_id=1, source_target_pairs={{0,4},{1,17},{2,6},{3,19},{4,0},{5,21},{6,2},{7,23},{8,12},{9,25},... | collective-permute-start | bytes 1376264 | tf_op jit(solution)/shard_map/ppermute | solution.py:379
  26.0 8.1 %collective-permute-start.4 = (bf16[4,56,512]{2,1,0:T(8,128)(2,1)S(1)}, bf16[4,56,512]{2,1,0:T(8,128)(2,1)S(1)}, u32[]{:S(2)}, u32[]{:S(2)}) collective-permute-start(bf16[4,56,512]{2,1,0:T(8,128)(2,1)S(1)} %maximum_select_fusion.8), channel_id=1, source_target_pairs={{0,2},{1,3},{2,0},{3,1},{4,6},{5,7},{6,4},{7,5},{8,10},{9,11},{10,... | collective-permute-start | bytes 688136 | tf_op jit(solution)/shard_map/ppermute | solution.py:379
  27.2 6.8 %collective-permute-start.5 = (bf16[4,8,512]{2,1,0:T(8,128)(2,1)S(1)}, bf16[4,8,512]{2,1,0:T(8,128)(2,1)S(1)}, u32[]{:S(2)}, u32[]{:S(2)}) collective-permute-start(bf16[4,8,512]{2,1,0:T(8,128)(2,1)S(1)} %slice.147), channel_id=1, source_target_pairs={{0,4},{1,3},{2,6},{3,1},{4,0},{5,7},{6,2},{7,5},{8,12},{9,11},{10,... | collective-permute-start | bytes 98312 | tf_op jit(solution)/shard_map/ppermute | solution.py:379
  34.0 1.0 copy-start
  34.0 1.0 copy-start.1
  34.0 1.1 copy-start.2
  34.1 1.2 copy-start.3
  34.1 1.2 copy-start.4
  34.1 1.1 copy-start.5
  36.0 14.5 %collective-permute-start.6 = (bf16[8,64,512]{2,1,0:T(8,128)(2,1)S(1)}, bf16[8,64,512]{2,1,0:T(8,128)(2,1)S(1)}, u32[]{:S(2)}, u32[]{:S(2)}) collective-permute-start(bf16[8,64,512]{2,1,0:T(8,128)(2,1)S(1)} %slice.113), channel_id=1, source_target_pairs={{0,16},{1,3},{2,18},{3,1},{4,20},{5,7},{6,22},{7,5},{8,24},{9,11},... | collective-permute-start | bytes 1572872 | tf_op jit(solution)/shard_map/ppermute | solution.py:379
  37.6 8.1 %collective-permute-start.7 = (bf16[8,24,512]{2,1,0:T(8,128)(2,1)S(1)}, bf16[8,24,512]{2,1,0:T(8,128)(2,1)S(1)}, u32[]{:S(2)}, u32[]{:S(2)}) collective-permute-start(bf16[8,24,512]{2,1,0:T(8,128)(2,1)S(1)} %slice.114), channel_id=1, source_target_pairs={{0,4},{1,5},{2,6},{3,7},{4,0},{5,1},{6,2},{7,3},{8,12},{9,13},{10,... | collective-permute-start | bytes 589832 | tf_op jit(solution)/shard_map/ppermute | solution.py:379
  38.5 13.6 %collective-permute-start.10 = (bf16[528,128]{1,0:T(8,128)(2,1)S(1)}, bf16[528,128]{1,0:T(8,128)(2,1)S(1)}, u32[]{:S(2)}, u32[]{:S(2)}) collective-permute-start(bf16[528,128]{1,0:T(8,128)(2,1)S(1)} %shard_map.120), channel_id=1, source_target_pairs={{2,0},{4,2},{6,4},{8,6},{10,8},{12,10},{14,12},{3,1},{5,3},{7,5},{... | collective-permute-start | bytes 405512 | tf_op jit(solution)/shard_map/ppermute | solution.py:426
  39.8 12.3 %collective-permute-start.9 = (bf16[512,128]{1,0:T(8,128)(2,1)S(1)}, bf16[512,128]{1,0:T(8,128)(2,1)S(1)}, u32[]{:S(2)}, u32[]{:S(2)}) collective-permute-start(bf16[512,128]{1,0:T(8,128)(2,1)S(1)} %slice.118.norm_ref), channel_id=1, source_target_pairs={{0,2},{2,4},{4,6},{6,8},{8,10},{10,12},{12,14},{1,3},{3,5},{5,7},{... | collective-permute-start | bytes 393224 | tf_op jit(solution)/shard_map/ppermute | solution.py:426
  44.4 7.8 %collective-permute-start.11 = (bf16[272,128]{1,0:T(8,128)(2,1)S(1)}, bf16[272,128]{1,0:T(8,128)(2,1)S(1)}, u32[]{:S(2)}, u32[]{:S(2)}) collective-permute-start(bf16[272,128]{1,0:T(8,128)(2,1)S(1)} %slice.119), channel_id=1, source_target_pairs={{4,0},{6,2},{8,4},{10,6},{12,8},{14,10},{5,1},{7,3},{9,5},{11,7},{... | collective-permute-start | bytes 208904 | tf_op jit(solution)/shard_map/ppermute | solution.py:426
  45.7 6.4 %collective-permute-start.8 = (bf16[256,128]{1,0:T(8,128)(2,1)S(1)}, bf16[256,128]{1,0:T(8,128)(2,1)S(1)}, u32[]{:S(2)}, u32[]{:S(2)}) collective-permute-start(bf16[256,128]{1,0:T(8,128)(2,1)S(1)} %slice.117), channel_id=1, source_target_pairs={{0,4},{2,6},{4,8},{6,10},{8,12},{10,14},{1,5},{3,7},{5,9},{7,11},{... | collective-permute-start | bytes 196616 | tf_op jit(solution)/shard_map/ppermute | solution.py:426
  52.2 10.9 %collective-permute-start.14 = (bf16[16,64,512]{2,1,0:T(8,128)(2,1)S(1)}, bf16[16,64,512]{2,1,0:T(8,128)(2,1)S(1)}, u32[]{:S(2)}, u32[]{:S(2)}) collective-permute-start(bf16[16,64,512]{2,1,0:T(8,128)(2,1)S(1)} %maximum_select_fusion.a_ref), channel_id=1, source_target_pairs={{0,1},{1,0},{2,3},{3,2},{4,5},{5,4},{6,7},{7,6},{8,9},{9,8},{10,11... | collective-permute-start | bytes 3145736 | tf_op jit(solution)/shard_map/ppermute | solution.py:379
  52.2 10.8 %collective-permute-start.15 = (bf16[16,24,512]{2,1,0:T(8,128)(2,1)S(1)}, bf16[16,24,512]{2,1,0:T(8,128)(2,1)S(1)}, u32[]{:S(2)}, u32[]{:S(2)}) collective-permute-start(bf16[16,24,512]{2,1,0:T(8,128)(2,1)S(1)} %maximum_select_fusion.6.b_ref), channel_id=1, source_target_pairs={{0,1},{1,0},{2,3},{3,2},{4,5},{5,4},{6,7},{7,6},{8,9},{9,8},{10,11... | collective-permute-start | bytes 1179656 | tf_op jit(solution)/shard_map/ppermute | solution.py:379
  52.7 8.9 %collective-permute-start.13 = (bf16[8,32,512]{2,1,0:T(8,128)(2,1)S(1)}, bf16[8,32,512]{2,1,0:T(8,128)(2,1)S(1)}, u32[]{:S(2)}, u32[]{:S(2)}) collective-permute-start(bf16[8,32,512]{2,1,0:T(8,128)(2,1)S(1)} %slice.116), channel_id=1, source_target_pairs={{0,4},{1,5},{2,6},{3,7},{4,0},{5,1},{6,2},{7,3},{8,12},{9,13},{10,... | collective-permute-start | bytes 786440 | tf_op jit(solution)/shard_map/ppermute | solution.py:379
  55.1 7.8 %collective-permute-start.12 = (bf16[8,48,512]{2,1,0:T(8,128)(2,1)S(1)}, bf16[8,48,512]{2,1,0:T(8,128)(2,1)S(1)}, u32[]{:S(2)}, u32[]{:S(2)}) collective-permute-start(bf16[8,48,512]{2,1,0:T(8,128)(2,1)S(1)} %slice.115), channel_id=1, source_target_pairs={{0,16},{1,3},{2,18},{3,1},{4,20},{5,7},{6,22},{7,5},{8,24},{9,11},... | collective-permute-start | bytes 1179656 | tf_op jit(solution)/shard_map/ppermute | solution.py:379
  70.2 3.1 %collective-permute-start.16 = (bf16[16,48,512]{2,1,0:T(8,128)(2,1)S(1)}, bf16[16,48,512]{2,1,0:T(8,128)(2,1)S(1)}, u32[]{:S(2)}, u32[]{:S(2)}) collective-permute-start(bf16[16,48,512]{2,1,0:T(8,128)(2,1)S(1)} %maximum_select_fusion.2.a_ref), channel_id=1, source_target_pairs={{0,1},{1,0},{2,3},{3,2},{4,5},{5,4},{6,7},{7,6},{8,9},{9,8},{10,11... | collective-permute-start | bytes 2359304 | tf_op jit(solution)/shard_map/ppermute | solution.py:379
  70.3 3.0 %collective-permute-start.17 = (bf16[16,32,512]{2,1,0:T(8,128)(2,1)S(1)}, bf16[16,32,512]{2,1,0:T(8,128)(2,1)S(1)}, u32[]{:S(2)}, u32[]{:S(2)}) collective-permute-start(bf16[16,32,512]{2,1,0:T(8,128)(2,1)S(1)} %maximum_select_fusion.3.b_ref), channel_id=1, source_target_pairs={{0,1},{1,0},{2,3},{3,2},{4,5},{5,4},{6,7},{7,6},{8,9},{9,8},{10,11... | collective-permute-start | bytes 1572872 | tf_op jit(solution)/shard_map/ppermute | solution.py:379
  85.6 3.5 %collective-permute-start.18 = (bf16[8,168,512]{2,1,0:T(8,128)(2,1)S(1)}, bf16[8,168,512]{2,1,0:T(8,128)(2,1)S(1)}, u32[]{:S(2)}, u32[]{:S(2)}) collective-permute-start(bf16[8,168,512]{2,1,0:T(8,128)(2,1)S(1)} %get-tuple-element.83), channel_id=1, source_target_pairs={{0,1},{1,0},{2,3},{3,2},{4,5},{5,4},{6,7},{7,6},{8,9},{9,8},{10,11... | collective-permute-start | bytes 4128776 | tf_op jit(solution)/shard_map/ppermute | solution.py:379
  90.6 14.3 %collective-permute-start.20 = (bf16[8,168,512]{2,1,0:T(8,128)(2,1)S(1)}, bf16[8,168,512]{2,1,0:T(8,128)(2,1)}, u32[]{:S(2)}, u32[]{:S(2)}) collective-permute-start(bf16[8,168,512]{2,1,0:T(8,128)(2,1)S(1)} %get-tuple-element.94), channel_id=1, source_target_pairs={{0,1},{1,0},{2,3},{3,2},{4,5},{5,4},{6,7},{7,6},{8,9},{9,8},{10,11... | collective-permute-start | bytes 4128776 | tf_op jit(solution)/shard_map/ppermute | solution.py:379
  92.2 11.3 %collective-permute-start.19 = (bf16[1,2,2,168,512]{4,3,2,1,0:T(8,128)(2,1)S(1)}, bf16[1,2,2,168,512]{4,3,2,1,0:T(8,128)(2,1)}, u32[]{:S(2)}, u32[]{:S(2)}) collective-permute-start(bf16[1,2,2,168,512]{4,3,2,1,0:T(8,128)(2,1)S(1)} %constant_dynamic-slice_fusion.5), channel_id=1, source_target_pairs={{0,2},{1,5},{2,0},{3,7},{4,6},{5,1},{6,4},{7,3},{8,10},{9,13},{10,... | collective-permute-start | bytes 2064392 | tf_op jit(solution)/shard_map/ppermute | solution.py:379
  106.8 13.8 %collective-permute-start.22 = (bf16[1,2,2,168,512]{4,3,2,1,0:T(8,128)(2,1)S(1)}, bf16[1,2,2,168,512]{4,3,2,1,0:T(8,128)(2,1)}, u32[]{:S(2)}, u32[]{:S(2)}) collective-permute-start(bf16[1,2,2,168,512]{4,3,2,1,0:T(8,128)(2,1)S(1)} %constant_dynamic-slice_fusion.3), channel_id=1, source_target_pairs={{0,2},{1,5},{2,0},{3,7},{4,6},{5,1},{6,4},{7,3},{8,10},{9,13},{10,... | collective-permute-start | bytes 2064392 | tf_op jit(solution)/shard_map/ppermute | solution.py:379
  108.9 10.7 %collective-permute-start.21 = (bf16[1,1,2,168,512]{4,3,2,1,0:T(8,128)(2,1)S(1)}, bf16[1,1,2,168,512]{4,3,2,1,0:T(8,128)(2,1)S(1)}, u32[]{:S(2)}, u32[]{:S(2)}) collective-permute-start(bf16[1,1,2,168,512]{4,3,2,1,0:T(8,128)(2,1)S(1)} %constant_dynamic-slice_fusion.4), channel_id=1, source_target_pairs={{0,4},{1,3},{2,6},{3,1},{4,0},{5,7},{6,2},{7,5},{8,12},{9,11},{10,... | collective-permute-start | bytes 1032200 | tf_op jit(solution)/shard_map/ppermute | solution.py:379
  121.9 10.6 %collective-permute-start.23 = (bf16[1,1,1,168,512]{4,3,2,1,0:T(8,128)(2,1)S(1)}, bf16[1,1,1,168,512]{4,3,2,1,0:T(8,128)(2,1)S(1)}, u32[]{:S(2)}, u32[]{:S(2)}) collective-permute-start(bf16[1,1,1,168,512]{4,3,2,1,0:T(8,128)(2,1)S(1)} %constant_dynamic-slice_fusion.2), channel_id=1, source_target_pairs={{0,8},{1,9},{2,10},{3,11},{4,12},{5,13},{6,14},{7,15},{8,0},{9,1},... | collective-permute-start | bytes 516104 | tf_op jit(solution)/shard_map/ppermute | solution.py:379
  125.3 10.1 %collective-permute-start.24 = (bf16[1,1,2,168,512]{4,3,2,1,0:T(8,128)(2,1)S(1)}, bf16[1,1,2,168,512]{4,3,2,1,0:T(8,128)(2,1)S(1)}, u32[]{:S(2)}, u32[]{:S(2)}) collective-permute-start(bf16[1,1,2,168,512]{4,3,2,1,0:T(8,128)(2,1)S(1)} %constant_dynamic-slice_fusion.1), channel_id=1, source_target_pairs={{0,4},{1,3},{2,6},{3,1},{4,0},{5,7},{6,2},{7,5},{8,12},{9,11},{10,... | collective-permute-start | bytes 1032200 | tf_op jit(solution)/shard_map/ppermute | solution.py:379
  135.6 7.2 %collective-permute-start.25 = (bf16[1,1,1,168,512]{4,3,2,1,0:T(8,128)(2,1)S(1)}, bf16[1,1,1,168,512]{4,3,2,1,0:T(8,128)(2,1)S(1)}, u32[]{:S(2)}, u32[]{:S(2)}) collective-permute-start(bf16[1,1,1,168,512]{4,3,2,1,0:T(8,128)(2,1)S(1)} %constant_dynamic-slice_fusion), channel_id=1, source_target_pairs={{0,8},{1,9},{2,10},{3,11},{4,12},{5,13},{6,14},{7,15},{8,0},{9,1},... | collective-permute-start | bytes 516104 | tf_op jit(solution)/shard_map/ppermute | solution.py:379

commit v6 on v5

--- a/solution.py
+++ b/solution.py
@@ -55,7 +55,6 @@
     return (2 * near + far) * step + rest, (2 * far + near) * step + rest
 
 
-CARRY_ROWS = 8
 LABEL_ROWS = 16
 
 
@@ -76,21 +75,14 @@
 
 
 def scan_kernel(feat_ref, forget_ref, keep_ref, mass_ref, weight_ref, carry_ref):
-    rows, bands = feat_ref.shape
+    rows = feat_ref.shape[0]
     values = scan(feat_ref[...], forget_ref[...])
-    carry_ref[...] = jnp.zeros_like(carry_ref)
     for k, (ref, value) in enumerate(zip((keep_ref, mass_ref, weight_ref), values)):
         ref[...] = value
-        rest = value[rows - 1 :]
-        for part in range(3):
-            rounded = rest.astype(BF16).astype(F32)
-            carry_ref[part : part + 1, k * bands : (k + 1) * bands] = rounded
-            rest = rest - rounded
-
-
-def pack_kernel(scalar_ref, feat_ref, forget_ref, conv_ref, res_ref, in_ref, out_ref,
-                keep_ref, mass_ref, weight_ref, pack_ref, carry_ref):
-    scan_kernel(feat_ref, forget_ref, keep_ref, mass_ref, weight_ref, carry_ref)
+        carry_ref[k : k + 1, :] = value[rows - 1 :]
+
+
+def pack_kernel(scalar_ref, conv_ref, res_ref, in_ref, out_ref, pack_ref):
     c = pack_ref.shape[1]
     cut, half, more = conv_ref.shape[1] * 3 // 4, res_ref.shape[1] // 2, in_ref.shape[0]
 
@@ -105,7 +97,6 @@
             at += value.shape[0]
 
         put(conv_ref[0, :, cols])
-        put(carry_ref[...].astype(BF16))
         put(conv_ref[1, :cut, cols])
         put(res_ref[0, part, :])
         if across:
@@ -124,13 +115,10 @@
     mass0 = jnp.zeros((1, bands), F32)
     weight0 = jnp.zeros((1, bands), F32)
     for tm in range(carry_ref.shape[0]):
-        first, second = spots(tm, carry_ref.shape[0])
-        parts = carry_ref[by_core(scalar_ref[0], first, second)].astype(F32)
-        value = (parts[0:1] + parts[1:2]) + parts[2:3]
         before = tm < scalar_ref[2]
-        keep = value[:, :bands]
-        mass0 = jnp.where(before, keep * mass0 + value[:, bands : 2 * bands], mass0)
-        weight0 = jnp.where(before, keep * weight0 + value[:, 2 * bands : 3 * bands], weight0)
+        keep, mass, weight = (carry_ref[tm, k : k + 1, :] for k in range(3))
+        mass0 = jnp.where(before, keep * mass0 + mass, mass0)
+        weight0 = jnp.where(before, keep * weight0 + weight, weight0)
     keep = keep_ref[...]
     mass = keep * mass0 + mass_ref[...]
     weight = keep * weight0 + weight_ref[...]
@@ -364,6 +352,23 @@
     store_terms(*targets, 2 * conv + res, value, 0, enter, 0, enter)
 
 
+def finish_kernel(sizes, one0_ref, two0_ref, one1_ref, two1_ref, conv_ref, res_ref, in_ref, out_ref):
+    conv, res, _, _ = sizes
+    for layer, (one, two) in enumerate(((one0_ref, two0_ref), (one1_ref, two1_ref))):
+        total = one[...].astype(F32) + two[...].astype(F32)
+        c = total.shape[1]
+        conv_ref[layer, :, :c] = total[:conv]
+        conv_ref[layer, :, c:] = total[conv : 2 * conv]
+        res_ref[layer] = total[2 * conv : 2 * conv + res]
+        rest = total[2 * conv + res :]
+        if layer == 0:
+            in_ref[...] = rest
+        else:
+            count, classes = rest.shape[0], out_ref.shape[1]
+            for q in range(c // classes):
+                out_ref[q * count : (q + 1) * count, :] = rest[:, q * classes : (q + 1) * classes]
+
+
 NEAR, FAR, ACROSS = ("tm", 0), ("tm", 1), ("groups", 0)
 CORE = ("site", 0)
 
@@ -388,37 +393,33 @@
     return lax.axis_size("tm").bit_length() - 1
 
 
-def grow(held, links):
-    other = swap(held, links)
+def arranged(held, other, links):
     return jnp.where(
         my_bit(links) == 0, jnp.concatenate([held, other]), jnp.concatenate([other, held]))
 
 
+def grow(held, links):
+    return arranged(held, swap(held, links), links)
+
+
 def together(*values):
     return lax.optimization_barrier(values)
 
 
-def sum_step(held, links, dim=0):
+def sum_step(addends, links, dim):
     mine = my_bit(links)
-    other = swap(lax.dynamic_index_in_dim(held, 1 - mine, dim), links)
-    return lax.dynamic_index_in_dim(held, mine, dim).astype(F32) + other.astype(F32)
+
+    def half(index):
+        one, two = (lax.dynamic_index_in_dim(v, index, dim).astype(F32) for v in addends)
+        return (one + two).astype(BF16)
+
+    return half(mine), swap(half(1 - mine), links)
 
 
 def sum_steps():
     bits = time_bits()
-
-    def first(held):
-        return sum_step(held.reshape((2,) * bits + held.shape[1:]), (NEAR, FAR)).astype(BF16)
-
-    def later(links, dim, last):
-        def step(held):
-            total = sum_step(held, links, dim)
-            return total if last else total.astype(BF16)
-
-        return step
-
-    rest = [later((("tm", bit),) * 2, 1 + bits - bit, bit == bits - 1) for bit in range(2, bits)]
-    return [first, later((FAR, NEAR), 1, not rest)] + rest
+    rest = [((("tm", bit),) * 2, 1 + bits - bit) for bit in range(2, bits)]
+    return [((NEAR, FAR), 0), ((FAR, NEAR), 1)] + rest
 
 
 def hop(value, by):
@@ -460,62 +461,55 @@
     scalars = jnp.stack(
         [lax.axis_index("site"), across, lax.axis_index("tm"), lengths[0]]).astype(jnp.int32)
 
-    block = ((steps, bands), F32)
-    feat = features[0]
     if aligned:
-        packed = 2 * (conv + half) + enter + CARRY_ROWS
-        keep, mass, weight, held, _ = call(
-            pack_kernel, [block] * 3 + [((packed, c), BF16), ((CARRY_ROWS, c), F32)], [], 40 * steps * bands,
-            scalars, feat, forget[0], w_conv, w_res, w_in, w_out, limit=FIRST_LIMIT)
+        (held,) = call(pack_kernel, [((2 * (conv + half) + enter, c), BF16)], [], 1,
+                       scalars, w_conv, w_res, w_in, w_out, limit=FIRST_LIMIT)
     else:
-        keep, mass, weight, carry = call(
-            scan_kernel, [block] * 3 + [((CARRY_ROWS, c), F32)], [], 40 * steps * bands, feat, forget[0])
         conv_own = jnp.where(across == 0, w_conv[:, :, :c], w_conv[:, :, c:])
         res_own = jnp.where(across == 0, w_res[:, :half], w_res[:, half:])
         out_own = jnp.concatenate([w_out[k * enter : (k + 1) * enter] for k in range(c // classes)], axis=1)
         held = jnp.concatenate([
-            conv_own[0], carry.astype(BF16), conv_own[1, :cut], res_own[0],
+            conv_own[0], conv_own[1, :cut], res_own[0],
             jnp.where(across == 0, w_in, out_own), res_own[1], conv_own[1, cut:]])
-    held = held[None]
+    held, feat, forget = together(held[None], features[0], forget[0])
+    block = ((steps, bands), F32)
+    keep, mass, weight, carry = call(
+        scan_kernel, [block] * 3 + [((3, bands), F32)], [], 40 * steps * bands, feat, forget, limit=FIRST_LIMIT)
+    carry = carry[None]
     for bit in reversed(range(2, time_bits())):
         held = grow(held, (("tm", bit),) * 2)
+    for bit in range(2):
+        carry = grow(carry, (("tm", bit),) * 2)
+    held, carry = together(held, carry)
 
     main_links = [(NEAR, FAR), (FAR, ACROSS), (ACROSS, NEAR)]
     side_links = [(ACROSS, ACROSS), (NEAR, NEAR), (FAR, FAR)]
-    ends = conv + CARRY_ROWS + cut
-    main, side = held[:, :ends], held[:, ends:]
+    main, side = held[:, : conv + cut], held[:, conv + cut :]
     main, side = grow(main, main_links[0]), grow(side, side_links[0])
-    carry = main[:, conv : conv + CARRY_ROWS]
-    main = jnp.concatenate([main[:, :conv], main[:, conv + CARRY_ROWS :]], axis=1)
-    main, side, carry = together(main, side, carry)
-    carry = grow(carry, (FAR, NEAR))
+    for bit in range(2, time_bits()):
+        carry = grow(carry, (("tm", bit),) * 2)
+    label_rows = steps // bands
+    (normed,) = call(norm_kernel, [((LABEL_ROWS + steps, bands), BF16)], [], 10 * steps * bands,
+                     scalars, feat, keep, mass, weight, carry, labels[0].reshape(label_rows, bands))
+    main, side, normed = together(main, side, normed)
     main, side = grow(main, main_links[1]), grow(side, side_links[1])
-    main, side, carry = together(main, side, carry)
-    label_rows = steps // bands
-    bits = time_bits()
-    carry = carry.reshape((2,) * bits + (CARRY_ROWS, c))
-    carry = carry.transpose((1, 0) + tuple(range(bits - 1, 1, -1)) + (bits, bits + 1))
-    (normed,) = call(norm_kernel, [((LABEL_ROWS + steps, bands), BF16)], [], 10 * steps * bands,
-                     scalars, feat, keep, mass, weight, carry.reshape(time_devices, CARRY_ROWS, c),
-                     labels[0].reshape(label_rows, bands))
-    main, side, normed = together(main, side, normed)
+    past, future = rows_before(normed, reach), rows_after(normed, reach)
+    main, side, past, future = together(main, side, past, future)
     first = [main[:, :conv], side[:, : half + enter]]
     second = [main[:, conv:], side[:, half + enter :]]
 
-    def last_step(parts):
-        return [grow(p, links[2]) for p, links in zip(parts, (main_links, side_links))]
+    last_links = (main_links[2], side_links[2])
 
     def both_cores(parts):
         return [v.astype(kind) for p in parts for v in (p, swap(p, (CORE, CORE)))]
 
-    first = last_step(first)
-    past, future = rows_before(normed, reach), rows_after(normed, reach)
-    *first, second[0], second[1], past, future = together(*first, *second, past, future)
+    first = [grow(p, links) for p, links in zip(first, last_links)]
+    *first, second[0], second[1] = together(*first, *second)
     own_normed = normed[LABEL_ROWS:]
     window = jnp.concatenate(past + [own_normed] + [v[LABEL_ROWS:] for v in future])
     label_window = jnp.concatenate(
         [v[: (v.shape[0] - LABEL_ROWS) // bands] for v in [normed] + future])
-    first, second = both_cores(first), last_step(second)
+    first, others = both_cores(first), [swap(p, links) for p, links in zip(second, last_links)]
 
     total_rows, rows0, rows1 = steps + 2 * reach, steps + d0, steps + reach
     conv_all, res_all = ((2, devices, conv, c), kind), ((devices, res, c), kind)
@@ -527,8 +521,8 @@
         [V((total_rows, c), BF16), V((devices, enter, c), F32), V((devices, out, classes), F32)],
         2 * total_rows * c * (bands + 5 * c), scalars, window, *first)
 
-    *second, h1 = together(*second, h1)
-    second = both_cores(second)
+    others[0], others[1], h1 = together(*others, h1)
+    second = both_cores([arranged(*v) for v in zip(second, others, last_links)])
     scale = 1.0 / math.sqrt(site_devices * steps * time_devices)
     package = [((time_devices, 2 * conv + res + enter, c), kind)] * 2
     loss, keep1, send1, grad1, round0, back0 = call(
@@ -539,38 +533,30 @@
         2 * rows1 * c * 6 * c + 2 * steps * 5 * c * c + 2 * rows0 * c * 5 * c,
         scalars, h1, out_all, label_window, *second, slope0, res0)
 
-    def core_sum(keep, send):
+    def core_step(keep, send):
         other = swap(send.astype(BF16), (CORE, CORE))
-        return (keep.astype(F32) + other.astype(F32)).astype(BF16)
-
-    sum1 = core_sum(keep1, send1)
+        shape = (2,) * time_bits() + keep.shape[1:]
+        return keep.reshape(shape), other.reshape(shape)
+
+    sums1 = core_step(keep1, send1)
     keep0, send0 = call(
         functools.partial(terms_first, sizes), package, [V((steps, c), BF16)],
         2 * steps * 9 * c * c, scalars, back0, grad1, round0, own_normed, h0, gated0, conv0)
-    sum1, keep0, send0 = together(sum1, keep0, send0)
-
-    chain1, chain0 = sum_steps(), [core_sum] + sum_steps()
-    sum1, sum0 = chain1[0](sum1), chain0[0](keep0, send0)
-    for step in range(1, len(chain0)):
-        sum1, sum0 = together(sum1, sum0)
-        if step < len(chain1):
-            sum1 = chain1[step](sum1)
-        sum0 = chain0[step](sum0)
-
-    convs, ress, extras = [], [], []
-    for held in (sum0, sum1):
-        total = held.reshape(held.shape[-2:])
-        convs.append(jnp.concatenate([total[:conv], total[conv : 2 * conv]], axis=1))
-        ress.append(total[2 * conv : 2 * conv + res])
-        extras.append(total[2 * conv + res :])
-    grad_in, grad_out = extras
-    return (
-        loss.reshape(1, steps),
-        jnp.stack(convs),
-        jnp.stack(ress),
-        grad_in,
-        jnp.concatenate([grad_out[:, k * classes : (k + 1) * classes] for k in range(c // classes)]),
-    )
+    sums1, keep0, send0 = together(sums1, keep0, send0)
+
+    order = sum_steps()
+    sums1, sums0 = sum_step(sums1, *order[0]), core_step(keep0, send0)
+    for step in range(len(order)):
+        sums1, sums0 = together(sums1, sums0)
+        if step + 1 < len(order):
+            sums1 = sum_step(sums1, *order[step + 1])
+        sums0 = sum_step(sums0, *order[step])
+    rows = 2 * conv + res + enter
+    grad_conv, grad_res, grad_in, grad_out = call(
+        functools.partial(finish_kernel, sizes),
+        [((2, conv, 2 * c), F32), ((2, res, c), F32), ((enter, c), F32), ((out, classes), F32)], [], 1,
+        *(v.reshape(rows, c) for v in sums0 + sums1))
+    return loss.reshape(1, steps), grad_conv, grad_res, grad_in, grad_out
 
 
 def solution(mesh):

time: 145 us -> 141 us (0.972)
  waiting for transfers between devices: 63.5 us -> 55.6 us
  starting transfers between devices: 39.4 us -> 43.4 us
  Pallas kernels: 26.2 us -> 29.7 us
  other arithmetic: 10.9 us -> 9.04 us
  local copies, waits for them, and re-layouts: 3.11 us -> 1.57 us
    ppermute x22 -> x24, waiting for transfers between devices: 62 us -> 54 us  [swap(): return lax.ppermute(value, names, pairs)]
    ppermute x22 -> x24, starting transfers between devices: 27.5 us -> 31.7 us  [swap(): return lax.ppermute(value, names, pairs)]
    pallas_call x5 -> x7, Pallas kernels: 26.2 us -> 29.7 us  [call(): pl.pallas_call(kernel, out_shape=[jax.ShapeDtypeStruct(s, d) for s, d in...]
    another operation x4 -> x0, other arithmetic: 1.53 us -> none  [the longest x3 0.87 us: on_device(): jnp.stack(convs)]
  transfers between devices with their start and end apart: 26 -> 28, of which waited for: 13 -> 14; matrix products, arithmetic and copies ran while one was open for 3% -> 3% of each run, Pallas kernels for 2% -> 9%
where the time goes in v6:
time: 141 us
  waiting for transfers between devices  55.6 us (39%)
  starting transfers between devices  43.4 us (31%)
  Pallas kernels  29.7 us (21%)
  other arithmetic  9.04 us (6%)
  between operations  1.76 us (1%)
  local copies, waits for them, and re-layouts  1.57 us (1%)
    ppermute x24, waiting for transfers between devices, swap(): return lax.ppermute(value, names, pairs)  54 us
    ppermute x24, starting transfers between devices, swap(): return lax.ppermute(value, names, pairs)  31.7 us
    pallas_call x7, Pallas kernels, call(): pl.pallas_call(kernel, out_shape=[jax.ShapeDtypeStruct(s, d) for s, d in...  29.7 us
    ppermute x4, starting transfers between devices, hop(): lax.ppermute(value, 'tm', [(i, i + by) for i in range(size) if 0 <= i + b...  11.7 us
    convert_element_type x6, other arithmetic, half(): return (one + two).astype(BF16)  5.87 us
  transfers between devices with their start and end apart: 28, of which 14 were waited for; matrix products, arithmetic and copies ran while one was open for 3% of the time, Pallas kernels for 9%

profile of v6, /device:TPU:0, one launch (start us, length us, event | category | flops | bytes accessed | tf_op | source)
XLA Modules:
  0.0 141.0 jit_solution(15190240264535012944)
XLA Ops:
  1.3 0.6 pad_add_fusion.scalar_ref
  2.0 1.7 %shard_map.119 = bf16[168,512]{1,0:T(8,128)(2,1)} custom-call(s32[4]{0:T(128)} %pad_add_fusion.scalar_ref, bf16[2,64,1024]{2,1,0:T(8,128)(2,1)} %conv_ref.1, bf16[2,32,512]{2,1,0:T(8,128)(2,1)} %res_ref.1, bf16[8,512]{1,0:T(8,128)(2,1)} %in_ref.1, bf16[32,128]{1,0:T(8,128)(2,1)} %out_ref.1), custom_call_target="tpu_custom_call" | custom-call | flops 1 | bytes 516112 | tf_op jit(solution)/shard_map/pallas_call | solution.py:38
  3.7 2.3 %shard_map.120 = (f32[512,128]{1,0:T(8,128)}, f32[512,128]{1,0:T(8,128)}, f32[512,128]{1,0:T(8,128)}, f32[3,128]{1,0:T(4,128)}) custom-call(f32[512,128]{1,0:T(8,128)} %bitcast.20, f32[512,128]{1,0:T(8,128)} %bitcast.28), custom_call_target="tpu_custom_call" | custom-call | flops 2621440 | bytes 1312256 | tf_op jit(solution)/shard_map/pallas_call | solution.py:38
  6.0 3.0 %collective-permute-start.1 = (f32[1,3,128]{2,1,0:T(4,128)}, f32[1,3,128]{2,1,0:T(4,128)S(1)}, u32[]{:S(2)}, u32[]{:S(2)}) collective-permute-start(f32[1,3,128]{2,1,0:T(4,128)} %bitcast.29), channel_id=1, source_target_pairs={{0,2},{1,3},{2,0},{3,1},{4,6},{5,7},{6,4},{7,5},{8,10},{9,11},{10,... | collective-permute-start | bytes 4616 | tf_op jit(solution)/shard_map/ppermute | solution.py:384
  9.0 2.6 %collective-permute-start = (bf16[1,168,512]{2,1,0:T(8,128)(2,1)}, bf16[1,168,512]{2,1,0:T(8,128)(2,1)S(1)}, u32[]{:S(2)}, u32[]{:S(2)}) collective-permute-start(bf16[1,168,512]{2,1,0:T(8,128)(2,1)} %bitcast.26), channel_id=1, source_target_pairs={{0,8},{1,9},{2,10},{3,11},{4,12},{5,13},{6,14},{7,15},{8,0},{9,1},... | collective-permute-start | bytes 516104 | tf_op jit(solution)/shard_map/ppermute | solution.py:384
  11.6 0.8 maximum_select_fusion.11
  12.4 1.6 %collective-permute-start.2 = (f32[2,3,128]{2,1,0:T(4,128)S(1)}, f32[2,3,128]{2,1,0:T(4,128)S(1)}, u32[]{:S(2)}, u32[]{:S(2)}) collective-permute-start(f32[2,3,128]{2,1,0:T(4,128)S(1)} %maximum_select_fusion.11), channel_id=1, source_target_pairs={{0,4},{1,5},{2,6},{3,7},{4,0},{5,1},{6,2},{7,3},{8,12},{9,13},{10,... | collective-permute-start | bytes 9224 | tf_op jit(solution)/shard_map/ppermute | solution.py:384
  14.0 2.0 %collective-permute-done.2 = f32[2,3,128]{2,1,0:T(4,128)S(1)} collective-permute-done((f32[2,3,128]{2,1,0:T(4,128)S(1)}, f32[2,3,128]{2,1,0:T(4,128)S(1)}, u32[]{:S(2)}, u32[]{:S(2)}) %collective-permute-start.2) | collective-permute-done | bytes 3104 | tf_op jit(solution)/shard_map/ppermute | solution.py:384
  16.0 3.7 %collective-permute-done = bf16[1,168,512]{2,1,0:T(8,128)(2,1)S(1)} collective-permute-done((bf16[1,168,512]{2,1,0:T(8,128)(2,1)}, bf16[1,168,512]{2,1,0:T(8,128)(2,1)S(1)}, u32[]{:S(2)}, u32[]{:S(2)}) %collective-permute-start) | collective-permute-done | bytes 172064 | tf_op jit(solution)/shard_map/ppermute | solution.py:384
  19.7 1.1 maximum_select_fusion.7
  20.7 0.1 collective-permute-start.5
  20.8 1.6 %collective-permute-start.4 = (bf16[2,56,512]{2,1,0:T(8,128)(2,1)S(1)}, bf16[2,56,512]{2,1,0:T(8,128)(2,1)S(1)}, u32[]{:S(2)}, u32[]{:S(2)}) collective-permute-start(bf16[2,56,512]{2,1,0:T(8,128)(2,1)S(1)} %slice.44), channel_id=1, source_target_pairs={{0,16},{1,17},{2,18},{3,19},{4,20},{5,21},{6,22},{7,23},{8,24},{9,... | collective-permute-start | bytes 344072 | tf_op jit(solution)/shard_map/ppermute | solution.py:384
  22.4 0.6 collective-permute-start.3
  23.0 2.4 %collective-permute-done.5 = f32[4,3,128]{2,1,0:T(4,128)S(1)} collective-permute-done((f32[4,3,128]{2,1,0:T(4,128)S(1)}, f32[4,3,128]{2,1,0:T(4,128)S(1)}, u32[]{:S(2)}, u32[]{:S(2)}) %collective-permute-start.5) | collective-permute-done | bytes 6176 | tf_op jit(solution)/shard_map/ppermute | solution.py:384
  25.4 0.7 shard_map.121
  26.2 2.3 %collective-permute-done.3 = bf16[2,112,512]{2,1,0:T(8,128)(2,1)S(1)} collective-permute-done((bf16[2,112,512]{2,1,0:T(8,128)(2,1)S(1)}, bf16[2,112,512]{2,1,0:T(8,128)(2,1)S(1)}, u32[]{:S(2)}, u32[]{:S(2)}) %collective-permute-start.3) | collective-permute-done | bytes 229408 | tf_op jit(solution)/shard_map/ppermute | solution.py:384
  28.5 0.1 maximum_select_fusion.4
  28.5 4.1 %collective-permute-start.6 = (bf16[4,112,512]{2,1,0:T(8,128)(2,1)S(1)}, bf16[4,112,512]{2,1,0:T(8,128)(2,1)S(1)}, u32[]{:S(2)}, u32[]{:S(2)}) collective-permute-start(bf16[4,112,512]{2,1,0:T(8,128)(2,1)S(1)} %maximum_select_fusion.4), channel_id=1, source_target_pairs={{0,4},{1,17},{2,6},{3,19},{4,0},{5,21},{6,2},{7,23},{8,12},{9,25},... | collective-permute-start | bytes 1376264 | tf_op jit(solution)/shard_map/ppermute | solution.py:384
  32.6 0.6 collective-permute-start.7
  33.2 1.3 collective-permute-start.10
  34.5 4.6 %collective-permute-start.9 = (bf16[512,128]{1,0:T(8,128)(2,1)S(1)}, bf16[512,128]{1,0:T(8,128)(2,1)S(1)}, u32[]{:S(2)}, u32[]{:S(2)}) collective-permute-start(bf16[512,128]{1,0:T(8,128)(2,1)S(1)} %slice.46.norm_ref), channel_id=1, source_target_pairs={{0,2},{2,4},{4,6},{6,8},{8,10},{10,12},{12,14},{1,3},{3,5},{5,7},{... | collective-permute-start | bytes 393224 | tf_op jit(solution)/shard_map/ppermute | solution.py:427
  39.1 1.3 collective-permute-start.11
  40.4 4.5 %collective-permute-start.8 = (bf16[256,128]{1,0:T(8,128)(2,1)S(1)}, bf16[256,128]{1,0:T(8,128)(2,1)S(1)}, u32[]{:S(2)}, u32[]{:S(2)}) collective-permute-start(bf16[256,128]{1,0:T(8,128)(2,1)S(1)} %slice.45), channel_id=1, source_target_pairs={{0,4},{2,6},{4,8},{6,10},{8,12},{10,14},{1,5},{3,7},{5,9},{7,11},{... | collective-permute-start | bytes 196616 | tf_op jit(solution)/shard_map/ppermute | solution.py:427
  45.0 0.1 maximum_select_fusion.5
  45.1 0.1 maximum_select_fusion.1
  45.2 1.6 %collective-permute-done.8 = bf16[256,128]{1,0:T(8,128)(2,1)S(1)} collective-permute-done((bf16[256,128]{1,0:T(8,128)(2,1)S(1)}, bf16[256,128]{1,0:T(8,128)(2,1)S(1)}, u32[]{:S(2)}, u32[]{:S(2)}) %collective-permute-start.8) | collective-permute-done | bytes 65568 | tf_op jit(solution)/shard_map/ppermute | solution.py:427
  46.9 0.6 copy-done.8
  47.5 0.7 copy-done.6
  48.2 0.6 collective-permute-start.12
  48.8 2.4 %collective-permute-start.13 = (bf16[8,24,512]{2,1,0:T(8,128)(2,1)S(1)}, bf16[8,24,512]{2,1,0:T(8,128)(2,1)S(1)}, u32[]{:S(2)}, u32[]{:S(2)}) collective-permute-start(bf16[8,24,512]{2,1,0:T(8,128)(2,1)S(1)} %slice.49), channel_id=1, source_target_pairs={{0,4},{1,5},{2,6},{3,7},{4,0},{5,1},{6,2},{7,3},{8,12},{9,13},{10,... | collective-permute-start | bytes 589832 | tf_op jit(solution)/shard_map/ppermute | solution.py:384
  51.3 3.6 %collective-permute-done.13 = bf16[8,24,512]{2,1,0:T(8,128)(2,1)S(1)} collective-permute-done((bf16[8,24,512]{2,1,0:T(8,128)(2,1)S(1)}, bf16[8,24,512]{2,1,0:T(8,128)(2,1)S(1)}, u32[]{:S(2)}, u32[]{:S(2)}) %collective-permute-start.13) | collective-permute-done | bytes 196640 | tf_op jit(solution)/shard_map/ppermute | solution.py:384
  55.0 2.5 %collective-permute-done.12 = bf16[8,64,512]{2,1,0:T(8,128)(2,1)S(1)} collective-permute-done((bf16[8,64,512]{2,1,0:T(8,128)(2,1)S(1)}, bf16[8,64,512]{2,1,0:T(8,128)(2,1)S(1)}, u32[]{:S(2)}, u32[]{:S(2)}) %collective-permute-start.12) | collective-permute-done | bytes 524320 | tf_op jit(solution)/shard_map/ppermute | solution.py:384
  57.4 0.2 maximum_select_fusion.a_ref
  57.8 0.5 collective-permute-start.17
  58.4 0.6 collective-permute-start.14
  59.0 2.4 %collective-permute-start.15 = (bf16[8,32,512]{2,1,0:T(8,128)(2,1)S(1)}, bf16[8,32,512]{2,1,0:T(8,128)(2,1)S(1)}, u32[]{:S(2)}, u32[]{:S(2)}) collective-permute-start(bf16[8,32,512]{2,1,0:T(8,128)(2,1)S(1)} %slice.51), channel_id=1, source_target_pairs={{0,4},{1,5},{2,6},{3,7},{4,0},{5,1},{6,2},{7,3},{8,12},{9,13},{10,... | collective-permute-start | bytes 786440 | tf_op jit(solution)/shard_map/ppermute | solution.py:384
  61.3 7.2 %shard_map.122 = (bf16[1792,512]{1,0:T(8,128)(2,1)S(1)}, bf16[512,128]{1,0:T(8,128)(2,1)S(1)}, bf16[768,512]{1,0:T(8,128)(2,1)S(1)}, bf16[512,512]{1,0:T(8,128)(...) custom-call(s32[4]{0:T(128)S(1)} %copy-done.4, ...), custom_call_target="tpu_custom_call" | custom-call | flops 5637144576 | bytes 10878992 | tf_op jit(solution)/shard_map/pallas_call | solution.py:38
  68.6 0.1 maximum_select_fusion.2.a_ref
  68.8 1.7 %collective-permute-start.18 = (bf16[16,48,512]{2,1,0:T(8,128)(2,1)S(1)}, bf16[16,48,512]{2,1,0:T(8,128)(2,1)S(1)}, u32[]{:S(2)}, u32[]{:S(2)}) collective-permute-start(bf16[16,48,512]{2,1,0:T(8,128)(2,1)S(1)} %maximum_select_fusion.2.a_ref), channel_id=1, source_target_pairs={{0,1},{1,0},{2,3},{3,2},{4,5},{5,4},{6,7},{7,6},{8,9},{9,8},{10,11... | collective-permute-start | bytes 2359304 | tf_op jit(solution)/shard_map/ppermute | solution.py:384
  70.4 0.1 maximum_select_fusion.3.b_ref
  70.5 0.1 collective-permute-start.19
  70.6 2.5 %collective-permute-done.19.b2_ref = bf16[16,32,512]{2,1,0:T(8,128)(2,1)S(1)} collective-permute-done((bf16[16,32,512]{2,1,0:T(8,128)(2,1)S(1)}, bf16[16,32,512]{2,1,0:T(8,128)(2,1)S(1)}, u32[]{:S(2)}, u32[]{:S(2)}) %collective-permute-start.19) | collective-permute-done | bytes 524320 | tf_op jit(solution)/shard_map/ppermute | solution.py:384
  73.1 12.3 %shard_map.123 = (f32[4,128]{1,0:T(4,128)}, bf16[8,168,512]{2,1,0:T(8,128)(2,1)S(1)}, bf16[8,168,512]{2,1,0:T(8,128)(2,1)S(1)}, f32[512,512]{1,0:T(8,128)S(1)}, ...) custom-call(s32[4]{0:T(128)S(1)} %copy-done.4, bf16[1792,512]{1,0:T(8,128)(2,1)S(1)} %get-tuple-element.88.h1_ref, ...), custom_call_target="tpu_custom_call" | custom-call | flops 7381975040 | bytes 12587536 | tf_op jit(solution)/shard_map/pallas_call | solution.py:38
  85.5 0.4 collective-permute-start.20
  85.9 4.5 %shard_map.124 = (bf16[8,168,512]{2,1,0:T(8,128)(2,1)S(1)}, bf16[8,168,512]{2,1,0:T(8,128)(2,1)}) custom-call(s32[4]{0:T(128)S(1)} %copy-done.4, bf16[768,1024]{1,0:T(8,128)(2,1)S(1)} %get-tuple-element.97.back_ref, f32[512,512]{1,0:T(8,128)S(1)} %get-tuple-element.98.grad_ref, bf16[512,512]{1,0:T(8,128)(2,1)S(1)} %get-tuple-element.99.round_ref, ...), custom_call_target="tpu_custom_call" | custom-call | flops 2415919104 | bytes 9437200 | tf_op jit(solution)/shard_map/pallas_call | solution.py:38
  90.4 0.1 collective-permute-start.22
  90.5 1.7 %add_convert_fusion.2 = (bf16[1,2,2,168,512]{4,3,2,1,0:T(8,128)(2,1)S(1)}, bf16[1,2,2,168,512]{4,3,2,1,0:T(8,128)(2,1)S(1)}) fusion(bf16[2,2,2,168,512]{4,3,2,1,0:T(8,128)(2,1)} %bitcast.10, s32[]{:T(128)S(6)} %select_n.191, bf16[2,2,2,168,512]{4,3,2,1,0:T(8,128)(2,1)S(1)} %bitcast.18, s32[]{:T(128)S(6)} %select_n.190), kind=kLoop, calls=%fused_computation.2 | loop fusion | flops 2752512 | bytes 4128776 | tf_op jit(solution)/shard_map/convert_element_type | solution.py:414
  92.2 1.2 collective-permute-start.21
  93.4 9.9 %collective-permute-done.21 = bf16[1,2,2,168,512]{4,3,2,1,0:T(8,128)(2,1)} collective-permute-done((bf16[1,2,2,168,512]{4,3,2,1,0:T(8,128)(2,1)S(1)}, bf16[1,2,2,168,512]{4,3,2,1,0:T(8,128)(2,1)}, u32[]{:S(2)}, u32[]{:S(2)}) %collective-permute-start.21) | collective-permute-done | bytes 688160 | tf_op jit(solution)/shard_map/ppermute | solution.py:384
  103.3 2.5 %add_convert_fusion = (bf16[1,2,2,168,512]{4,3,2,1,0:T(8,128)(2,1)}, bf16[1,2,2,168,512]{4,3,2,1,0:T(8,128)(2,1)S(1)}) fusion(bf16[2,2,2,168,512]{4,3,2,1,0:T(8,128)(2,1)} %bitcast.12, s32[]{:T(128)S(6)} %select_n.191, bf16[2,2,2,168,512]{4,3,2,1,0:T(8,128)(2,1)S(1)} %bitcast.19, s32[]{:T(128)S(6)} %select_n.190), kind=kLoop, calls=%fused_computation | loop fusion | flops 2752512 | bytes 4128776 | tf_op jit(solution)/shard_map/convert_element_type | solution.py:414
  105.9 1.1 collective-permute-start.24
  107.0 1.3 add_convert_fusion.6
  108.3 2.3 %collective-permute-start.23 = (bf16[1,1,2,168,512]{4,3,2,1,0:T(8,128)(2,1)S(1)}, bf16[1,1,2,168,512]{4,3,2,1,0:T(8,128)(2,1)S(1)}, u32[]{:S(2)}, u32[]{:S(2)}) collective-permute-start(bf16[1,1,2,168,512]{4,3,2,1,0:T(8,128)(2,1)S(1)} %get-tuple-element.131), channel_id=1, source_target_pairs={{0,4},{1,3},{2,6},{3,1},{4,0},{5,7},{6,2},{7,5},{8,12},{9,11},{10,... | collective-permute-start | bytes 1032200 | tf_op jit(solution)/shard_map/ppermute | solution.py:384
  110.6 8.7 %collective-permute-done.23 = bf16[1,1,2,168,512]{4,3,2,1,0:T(8,128)(2,1)S(1)} collective-permute-done((bf16[1,1,2,168,512]{4,3,2,1,0:T(8,128)(2,1)S(1)}, bf16[1,1,2,168,512]{4,3,2,1,0:T(8,128)(2,1)S(1)}, u32[]{:S(2)}, u32[]{:S(2)}) %collective-permute-start.23) | collective-permute-done | bytes 344096 | tf_op jit(solution)/shard_map/ppermute | solution.py:384
  119.2 1.5 %collective-permute-done.24 = bf16[1,2,2,168,512]{4,3,2,1,0:T(8,128)(2,1)S(1)} collective-permute-done((bf16[1,2,2,168,512]{4,3,2,1,0:T(8,128)(2,1)}, bf16[1,2,2,168,512]{4,3,2,1,0:T(8,128)(2,1)S(1)}, u32[]{:S(2)}, u32[]{:S(2)}) %collective-permute-start.24) | collective-permute-done | bytes 688160 | tf_op jit(solution)/shard_map/ppermute | solution.py:384
  120.7 0.2 add_convert_fusion.4
  120.9 1.4 collective-permute-start.26
  122.3 0.1 add_convert_fusion.10
  122.5 8.5 %collective-permute-done.25 = bf16[1,1,1,168,512]{4,3,2,1,0:T(8,128)(2,1)S(1)} collective-permute-done((bf16[1,1,1,168,512]{4,3,2,1,0:T(8,128)(2,1)S(1)}, bf16[1,1,1,168,512]{4,3,2,1,0:T(8,128)(2,1)S(1)}, u32[]{:S(2)}, u32[]{:S(2)}) %collective-permute-start.25) | collective-permute-done | bytes 172064 | tf_op jit(solution)/shard_map/ppermute | solution.py:384
  130.9 0.9 collective-permute-done.26
  131.9 0.1 add_convert_fusion.8
  132.0 2.6 %collective-permute-start.27 = (bf16[1,1,1,168,512]{4,3,2,1,0:T(8,128)(2,1)S(1)}, bf16[1,1,1,168,512]{4,3,2,1,0:T(8,128)(2,1)S(1)}, u32[]{:S(2)}, u32[]{:S(2)}) collective-permute-start(bf16[1,1,1,168,512]{4,3,2,1,0:T(8,128)(2,1)S(1)} %get-tuple-element.133), channel_id=1, source_target_pairs={{0,8},{1,9},{2,10},{3,11},{4,12},{5,13},{6,14},{7,15},{8,0},{9,1},... | collective-permute-start | bytes 516104 | tf_op jit(solution)/shard_map/ppermute | solution.py:384
  134.6 5.6 %collective-permute-done.27 = bf16[1,1,1,168,512]{4,3,2,1,0:T(8,128)(2,1)S(1)} collective-permute-done((bf16[1,1,1,168,512]{4,3,2,1,0:T(8,128)(2,1)S(1)}, bf16[1,1,1,168,512]{4,3,2,1,0:T(8,128)(2,1)S(1)}, u32[]{:S(2)}, u32[]{:S(2)}) %collective-permute-start.27) | collective-permute-done | bytes 172064 | tf_op jit(solution)/shard_map/ppermute | solution.py:384
  140.2 0.9 shard_map.125
  (62 shorter events, 0.6 us)
Async XLA Ops:
  0.6 24.7 %copy-start = (f32[1,512,128]{2,1,0:T(8,128)S(1)}, f32[1,512,128]{2,1,0:T(8,128)}, u32[]{:S(2)}) copy-start(f32[1,512,128]{2,1,0:T(8,128)} %param.8) | copy-start | bytes 786436
  0.6 24.7 %copy-start.5 = (s32[1,512]{1,0:T(1,128)S(1)}, s32[1,512]{1,0:T(1,128)}, u32[]{:S(2)}) copy-start(s32[1,512]{1,0:T(1,128)} %param.10) | copy-start | bytes 6148
  2.0 23.4 %copy-start.4 = (s32[4]{0:T(128)S(1)}, s32[4]{0:T(128)}, u32[]{:S(2)}) copy-start(s32[4]{0:T(128)} %pad_add_fusion.scalar_ref) | copy-start | bytes 52
  6.0 19.4 %copy-start.1 = (f32[512,128]{1,0:T(8,128)S(1)}, f32[512,128]{1,0:T(8,128)}, u32[]{:S(2)}) copy-start(f32[512,128]{1,0:T(8,128)} %get-tuple-element.70.keep_ref) | copy-start | bytes 786436
  6.0 19.4 %copy-start.2 = (f32[512,128]{1,0:T(8,128)S(1)}, f32[512,128]{1,0:T(8,128)}, u32[]{:S(2)}) copy-start(f32[512,128]{1,0:T(8,128)} %get-tuple-element.71.mass_ref) | copy-start | bytes 786436
  6.0 19.4 %copy-start.3 = (f32[512,128]{1,0:T(8,128)S(1)}, f32[512,128]{1,0:T(8,128)}, u32[]{:S(2)}) copy-start(f32[512,128]{1,0:T(8,128)} %get-tuple-element.72.weight_ref) | copy-start | bytes 786436
  6.0 5.6 %collective-permute-start.1 = (f32[1,3,128]{2,1,0:T(4,128)}, f32[1,3,128]{2,1,0:T(4,128)S(1)}, u32[]{:S(2)}, u32[]{:S(2)}) collective-permute-start(f32[1,3,128]{2,1,0:T(4,128)} %bitcast.29), channel_id=1, source_target_pairs={{0,2},{1,3},{2,0},{3,1},{4,6},{5,7},{6,4},{7,5},{8,10},{9,11},{10,... | collective-permute-start | bytes 4616 | tf_op jit(solution)/shard_map/ppermute | solution.py:384
  9.0 10.6 %collective-permute-start = (bf16[1,168,512]{2,1,0:T(8,128)(2,1)}, bf16[1,168,512]{2,1,0:T(8,128)(2,1)S(1)}, u32[]{:S(2)}, u32[]{:S(2)}) collective-permute-start(bf16[1,168,512]{2,1,0:T(8,128)(2,1)} %bitcast.26), channel_id=1, source_target_pairs={{0,8},{1,9},{2,10},{3,11},{4,12},{5,13},{6,14},{7,15},{8,0},{9,1},... | collective-permute-start | bytes 516104 | tf_op jit(solution)/shard_map/ppermute | solution.py:384
  12.4 3.6 %collective-permute-start.2 = (f32[2,3,128]{2,1,0:T(4,128)S(1)}, f32[2,3,128]{2,1,0:T(4,128)S(1)}, u32[]{:S(2)}, u32[]{:S(2)}) collective-permute-start(f32[2,3,128]{2,1,0:T(4,128)S(1)} %maximum_select_fusion.11), channel_id=1, source_target_pairs={{0,4},{1,5},{2,6},{3,7},{4,0},{5,1},{6,2},{7,3},{8,12},{9,13},{10,... | collective-permute-start | bytes 9224 | tf_op jit(solution)/shard_map/ppermute | solution.py:384
  20.7 4.6 %collective-permute-start.5 = (f32[4,3,128]{2,1,0:T(4,128)S(1)}, f32[4,3,128]{2,1,0:T(4,128)S(1)}, u32[]{:S(2)}, u32[]{:S(2)}) collective-permute-start(f32[4,3,128]{2,1,0:T(4,128)S(1)} %maximum_select_fusion.10), channel_id=1, source_target_pairs={{0,8},{1,9},{2,10},{3,11},{4,12},{5,13},{6,14},{7,15},{8,0},{9,1},... | collective-permute-start | bytes 18440 | tf_op jit(solution)/shard_map/ppermute | solution.py:384
  20.8 5.3 %collective-permute-start.4 = (bf16[2,56,512]{2,1,0:T(8,128)(2,1)S(1)}, bf16[2,56,512]{2,1,0:T(8,128)(2,1)S(1)}, u32[]{:S(2)}, u32[]{:S(2)}) collective-permute-start(bf16[2,56,512]{2,1,0:T(8,128)(2,1)S(1)} %slice.44), channel_id=1, source_target_pairs={{0,16},{1,17},{2,18},{3,19},{4,20},{5,21},{6,22},{7,23},{8,24},{9,... | collective-permute-start | bytes 344072 | tf_op jit(solution)/shard_map/ppermute | solution.py:384
  22.4 6.1 %collective-permute-start.3 = (bf16[2,112,512]{2,1,0:T(8,128)(2,1)S(1)}, bf16[2,112,512]{2,1,0:T(8,128)(2,1)S(1)}, u32[]{:S(2)}, u32[]{:S(2)}) collective-permute-start(bf16[2,112,512]{2,1,0:T(8,128)(2,1)S(1)} %slice.43), channel_id=1, source_target_pairs={{0,2},{1,5},{2,0},{3,7},{4,6},{5,1},{6,4},{7,3},{8,10},{9,13},{10,... | collective-permute-start | bytes 688136 | tf_op jit(solution)/shard_map/ppermute | solution.py:384
  28.5 16.5 %collective-permute-start.6 = (bf16[4,112,512]{2,1,0:T(8,128)(2,1)S(1)}, bf16[4,112,512]{2,1,0:T(8,128)(2,1)S(1)}, u32[]{:S(2)}, u32[]{:S(2)}) collective-permute-start(bf16[4,112,512]{2,1,0:T(8,128)(2,1)S(1)} %maximum_select_fusion.4), channel_id=1, source_target_pairs={{0,4},{1,17},{2,6},{3,19},{4,0},{5,21},{6,2},{7,23},{8,12},{9,25},... | collective-permute-start | bytes 1376264 | tf_op jit(solution)/shard_map/ppermute | solution.py:384
  32.6 7.8 %collective-permute-start.7 = (bf16[4,56,512]{2,1,0:T(8,128)(2,1)S(1)}, bf16[4,56,512]{2,1,0:T(8,128)(2,1)S(1)}, u32[]{:S(2)}, u32[]{:S(2)}) collective-permute-start(bf16[4,56,512]{2,1,0:T(8,128)(2,1)S(1)} %maximum_select_fusion.8), channel_id=1, source_target_pairs={{0,2},{1,3},{2,0},{3,1},{4,6},{5,7},{6,4},{7,5},{8,10},{9,11},{10,... | collective-permute-start | bytes 688136 | tf_op jit(solution)/shard_map/ppermute | solution.py:384
  33.2 14.3 %collective-permute-start.10 = (bf16[528,128]{1,0:T(8,128)(2,1)S(1)}, bf16[528,128]{1,0:T(8,128)(2,1)S(1)}, u32[]{:S(2)}, u32[]{:S(2)}) collective-permute-start(bf16[528,128]{1,0:T(8,128)(2,1)S(1)} %shard_map.121), channel_id=1, source_target_pairs={{2,0},{4,2},{6,4},{8,6},{10,8},{12,10},{14,12},{3,1},{5,3},{7,5},{... | collective-permute-start | bytes 405512 | tf_op jit(solution)/shard_map/ppermute | solution.py:427
  34.5 12.3 %collective-permute-start.9 = (bf16[512,128]{1,0:T(8,128)(2,1)S(1)}, bf16[512,128]{1,0:T(8,128)(2,1)S(1)}, u32[]{:S(2)}, u32[]{:S(2)}) collective-permute-start(bf16[512,128]{1,0:T(8,128)(2,1)S(1)} %slice.46.norm_ref), channel_id=1, source_target_pairs={{0,2},{2,4},{4,6},{6,8},{8,10},{10,12},{12,14},{1,3},{3,5},{5,7},{... | collective-permute-start | bytes 393224 | tf_op jit(solution)/shard_map/ppermute | solution.py:427
  39.1 7.8 %collective-permute-start.11 = (bf16[272,128]{1,0:T(8,128)(2,1)S(1)}, bf16[272,128]{1,0:T(8,128)(2,1)S(1)}, u32[]{:S(2)}, u32[]{:S(2)}) collective-permute-start(bf16[272,128]{1,0:T(8,128)(2,1)S(1)} %slice.47), channel_id=1, source_target_pairs={{4,0},{6,2},{8,4},{10,6},{12,8},{14,10},{5,1},{7,3},{9,5},{11,7},{... | collective-permute-start | bytes 208904 | tf_op jit(solution)/shard_map/ppermute | solution.py:427
  40.4 6.4 %collective-permute-start.8 = (bf16[256,128]{1,0:T(8,128)(2,1)S(1)}, bf16[256,128]{1,0:T(8,128)(2,1)S(1)}, u32[]{:S(2)}, u32[]{:S(2)}) collective-permute-start(bf16[256,128]{1,0:T(8,128)(2,1)S(1)} %slice.45), channel_id=1, source_target_pairs={{0,4},{2,6},{4,8},{6,10},{8,12},{10,14},{1,5},{3,7},{5,9},{7,11},{... | collective-permute-start | bytes 196616 | tf_op jit(solution)/shard_map/ppermute | solution.py:427
  46.9 0.6 copy-start.8
  46.9 0.6 copy-start.10
  47.5 0.7 copy-start.6
  48.2 9.2 %collective-permute-start.12 = (bf16[8,64,512]{2,1,0:T(8,128)(2,1)S(1)}, bf16[8,64,512]{2,1,0:T(8,128)(2,1)S(1)}, u32[]{:S(2)}, u32[]{:S(2)}) collective-permute-start(bf16[8,64,512]{2,1,0:T(8,128)(2,1)S(1)} %slice.48), channel_id=1, source_target_pairs={{0,16},{1,3},{2,18},{3,1},{4,20},{5,7},{6,22},{7,5},{8,24},{9,11},... | collective-permute-start | bytes 1572872 | tf_op jit(solution)/shard_map/ppermute | solution.py:384
  48.8 6.1 %collective-permute-start.13 = (bf16[8,24,512]{2,1,0:T(8,128)(2,1)S(1)}, bf16[8,24,512]{2,1,0:T(8,128)(2,1)S(1)}, u32[]{:S(2)}, u32[]{:S(2)}) collective-permute-start(bf16[8,24,512]{2,1,0:T(8,128)(2,1)S(1)} %slice.49), channel_id=1, source_target_pairs={{0,4},{1,5},{2,6},{3,7},{4,0},{5,1},{6,2},{7,3},{8,12},{9,13},{10,... | collective-permute-start | bytes 589832 | tf_op jit(solution)/shard_map/ppermute | solution.py:384
  51.3 6.4 %copy-start.9 = (bf16[256,128]{1,0:T(8,128)(2,1)S(1)}, bf16[256,128]{1,0:T(8,128)(2,1)}, u32[]{:S(2)}) copy-start(bf16[256,128]{1,0:T(8,128)(2,1)} %copy-done.8) | copy-start | bytes 196612
  54.9 3.4 %copy-start.7 = (bf16[528,128]{1,0:T(8,128)(2,1)S(1)}, bf16[528,128]{1,0:T(8,128)(2,1)}, u32[]{:S(2)}) copy-start(bf16[528,128]{1,0:T(8,128)(2,1)} %copy-done.6) | copy-start | bytes 405508
  54.9 3.4 %copy-start.11 = (bf16[272,128]{1,0:T(8,128)(2,1)S(1)}, bf16[272,128]{1,0:T(8,128)(2,1)}, u32[]{:S(2)}) copy-start(bf16[272,128]{1,0:T(8,128)(2,1)} %copy-done.10) | copy-start | bytes 208900
  57.6 3.7 %collective-permute-start.16 = (bf16[16,64,512]{2,1,0:T(8,128)(2,1)S(1)}, bf16[16,64,512]{2,1,0:T(8,128)(2,1)S(1)}, u32[]{:S(2)}, u32[]{:S(2)}) collective-permute-start(bf16[16,64,512]{2,1,0:T(8,128)(2,1)S(1)} %maximum_select_fusion.a_ref), channel_id=1, source_target_pairs={{0,1},{1,0},{2,3},{3,2},{4,5},{5,4},{6,7},{7,6},{8,9},{9,8},{10,11... | collective-permute-start | bytes 3145736 | tf_op jit(solution)/shard_map/ppermute | solution.py:384
  57.8 3.6 %collective-permute-start.17 = (bf16[16,24,512]{2,1,0:T(8,128)(2,1)S(1)}, bf16[16,24,512]{2,1,0:T(8,128)(2,1)S(1)}, u32[]{:S(2)}, u32[]{:S(2)}) collective-permute-start(bf16[16,24,512]{2,1,0:T(8,128)(2,1)S(1)} %maximum_select_fusion.6.b_ref), channel_id=1, source_target_pairs={{0,1},{1,0},{2,3},{3,2},{4,5},{5,4},{6,7},{7,6},{8,9},{9,8},{10,11... | collective-permute-start | bytes 1179656 | tf_op jit(solution)/shard_map/ppermute | solution.py:384
  58.4 10.2 %collective-permute-start.14 = (bf16[8,48,512]{2,1,0:T(8,128)(2,1)S(1)}, bf16[8,48,512]{2,1,0:T(8,128)(2,1)S(1)}, u32[]{:S(2)}, u32[]{:S(2)}) collective-permute-start(bf16[8,48,512]{2,1,0:T(8,128)(2,1)S(1)} %slice.50), channel_id=1, source_target_pairs={{0,16},{1,3},{2,18},{3,1},{4,20},{5,7},{6,22},{7,5},{8,24},{9,11},... | collective-permute-start | bytes 1179656 | tf_op jit(solution)/shard_map/ppermute | solution.py:384
  59.0 9.6 %collective-permute-start.15 = (bf16[8,32,512]{2,1,0:T(8,128)(2,1)S(1)}, bf16[8,32,512]{2,1,0:T(8,128)(2,1)S(1)}, u32[]{:S(2)}, u32[]{:S(2)}) collective-permute-start(bf16[8,32,512]{2,1,0:T(8,128)(2,1)S(1)} %slice.51), channel_id=1, source_target_pairs={{0,4},{1,5},{2,6},{3,7},{4,0},{5,1},{6,2},{7,3},{8,12},{9,13},{10,... | collective-permute-start | bytes 786440 | tf_op jit(solution)/shard_map/ppermute | solution.py:384
  68.6 2.0 %slice-start = ((bf16[528,128]{1,0:T(8,128)(2,1)}), bf16[4,128]{1,0:T(4,128)(2,1)S(1)}, s32[]{:S(2)}) async-start(bf16[528,128]{1,0:T(8,128)(2,1)} %copy-done.6), calls=%async_computation | async-start | bytes 2048 | tf_op jit(solution)/shard_map/slice | solution.py:511
  68.6 2.0 %slice-start.1 = ((bf16[272,128]{1,0:T(8,128)(2,1)}), bf16[2,128]{1,0:T(2,128)(2,1)S(1)}, s32[]{:S(2)}) async-start(bf16[272,128]{1,0:T(8,128)(2,1)} %copy-done.10), calls=%async_computation.1 | async-start | bytes 1024 | tf_op jit(solution)/shard_map/slice | solution.py:511
  68.8 4.3 %collective-permute-start.18 = (bf16[16,48,512]{2,1,0:T(8,128)(2,1)S(1)}, bf16[16,48,512]{2,1,0:T(8,128)(2,1)S(1)}, u32[]{:S(2)}, u32[]{:S(2)}) collective-permute-start(bf16[16,48,512]{2,1,0:T(8,128)(2,1)S(1)} %maximum_select_fusion.2.a_ref), channel_id=1, source_target_pairs={{0,1},{1,0},{2,3},{3,2},{4,5},{5,4},{6,7},{7,6},{8,9},{9,8},{10,11... | collective-permute-start | bytes 2359304 | tf_op jit(solution)/shard_map/ppermute | solution.py:384
  70.5 2.6 %collective-permute-start.19 = (bf16[16,32,512]{2,1,0:T(8,128)(2,1)S(1)}, bf16[16,32,512]{2,1,0:T(8,128)(2,1)S(1)}, u32[]{:S(2)}, u32[]{:S(2)}) collective-permute-start(bf16[16,32,512]{2,1,0:T(8,128)(2,1)S(1)} %maximum_select_fusion.3.b_ref), channel_id=1, source_target_pairs={{0,1},{1,0},{2,3},{3,2},{4,5},{5,4},{6,7},{7,6},{8,9},{9,8},{10,11... | collective-permute-start | bytes 1572872 | tf_op jit(solution)/shard_map/ppermute | solution.py:384
  85.5 4.9 %collective-permute-start.20 = (bf16[8,168,512]{2,1,0:T(8,128)(2,1)S(1)}, bf16[8,168,512]{2,1,0:T(8,128)(2,1)}, u32[]{:S(2)}, u32[]{:S(2)}) collective-permute-start(bf16[8,168,512]{2,1,0:T(8,128)(2,1)S(1)} %get-tuple-element.96), channel_id=1, source_target_pairs={{0,1},{1,0},{2,3},{3,2},{4,5},{5,4},{6,7},{7,6},{8,9},{9,8},{10,11... | collective-permute-start | bytes 4128776 | tf_op jit(solution)/shard_map/ppermute | solution.py:384
  90.4 12.9 %collective-permute-start.22 = (bf16[8,168,512]{2,1,0:T(8,128)(2,1)}, bf16[8,168,512]{2,1,0:T(8,128)(2,1)}, u32[]{:S(2)}, u32[]{:S(2)}) collective-permute-start(bf16[8,168,512]{2,1,0:T(8,128)(2,1)} %get-tuple-element.108), channel_id=1, source_target_pairs={{0,1},{1,0},{2,3},{3,2},{4,5},{5,4},{6,7},{7,6},{8,9},{9,8},{10,11... | collective-permute-start | bytes 4128776 | tf_op jit(solution)/shard_map/ppermute | solution.py:384
  92.2 11.1 %collective-permute-start.21 = (bf16[1,2,2,168,512]{4,3,2,1,0:T(8,128)(2,1)S(1)}, bf16[1,2,2,168,512]{4,3,2,1,0:T(8,128)(2,1)}, u32[]{:S(2)}, u32[]{:S(2)}) collective-permute-start(bf16[1,2,2,168,512]{4,3,2,1,0:T(8,128)(2,1)S(1)} %get-tuple-element.127), channel_id=1, source_target_pairs={{0,2},{1,5},{2,0},{3,7},{4,6},{5,1},{6,4},{7,3},{8,10},{9,13},{10,... | collective-permute-start | bytes 2064392 | tf_op jit(solution)/shard_map/ppermute | solution.py:384
  105.9 14.8 %collective-permute-start.24 = (bf16[1,2,2,168,512]{4,3,2,1,0:T(8,128)(2,1)}, bf16[1,2,2,168,512]{4,3,2,1,0:T(8,128)(2,1)S(1)}, u32[]{:S(2)}, u32[]{:S(2)}) collective-permute-start(bf16[1,2,2,168,512]{4,3,2,1,0:T(8,128)(2,1)} %get-tuple-element.125), channel_id=1, source_target_pairs={{0,2},{1,5},{2,0},{3,7},{4,6},{5,1},{6,4},{7,3},{8,10},{9,13},{10,... | collective-permute-start | bytes 2064392 | tf_op jit(solution)/shard_map/ppermute | solution.py:384
  108.3 11.0 %collective-permute-start.23 = (bf16[1,1,2,168,512]{4,3,2,1,0:T(8,128)(2,1)S(1)}, bf16[1,1,2,168,512]{4,3,2,1,0:T(8,128)(2,1)S(1)}, u32[]{:S(2)}, u32[]{:S(2)}) collective-permute-start(bf16[1,1,2,168,512]{4,3,2,1,0:T(8,128)(2,1)S(1)} %get-tuple-element.131), channel_id=1, source_target_pairs={{0,4},{1,3},{2,6},{3,1},{4,0},{5,7},{6,2},{7,5},{8,12},{9,11},{10,... | collective-permute-start | bytes 1032200 | tf_op jit(solution)/shard_map/ppermute | solution.py:384
  120.9 11.0 %collective-permute-start.26 = (bf16[1,1,2,168,512]{4,3,2,1,0:T(8,128)(2,1)S(1)}, bf16[1,1,2,168,512]{4,3,2,1,0:T(8,128)(2,1)S(1)}, u32[]{:S(2)}, u32[]{:S(2)}) collective-permute-start(bf16[1,1,2,168,512]{4,3,2,1,0:T(8,128)(2,1)S(1)} %get-tuple-element.129), channel_id=1, source_target_pairs={{0,4},{1,3},{2,6},{3,1},{4,0},{5,7},{6,2},{7,5},{8,12},{9,11},{10,... | collective-permute-start | bytes 1032200 | tf_op jit(solution)/shard_map/ppermute | solution.py:384
  122.4 8.5 %collective-permute-start.25 = (bf16[1,1,1,168,512]{4,3,2,1,0:T(8,128)(2,1)S(1)}, bf16[1,1,1,168,512]{4,3,2,1,0:T(8,128)(2,1)S(1)}, u32[]{:S(2)}, u32[]{:S(2)}) collective-permute-start(bf16[1,1,1,168,512]{4,3,2,1,0:T(8,128)(2,1)S(1)} %get-tuple-element.135), channel_id=1, source_target_pairs={{0,8},{1,9},{2,10},{3,11},{4,12},{5,13},{6,14},{7,15},{8,0},{9,1},... | collective-permute-start | bytes 516104 | tf_op jit(solution)/shard_map/ppermute | solution.py:384
  132.0 8.2 %collective-permute-start.27 = (bf16[1,1,1,168,512]{4,3,2,1,0:T(8,128)(2,1)S(1)}, bf16[1,1,1,168,512]{4,3,2,1,0:T(8,128)(2,1)S(1)}, u32[]{:S(2)}, u32[]{:S(2)}) collective-permute-start(bf16[1,1,1,168,512]{4,3,2,1,0:T(8,128)(2,1)S(1)} %get-tuple-element.133), channel_id=1, source_target_pairs={{0,8},{1,9},{2,10},{3,11},{4,12},{5,13},{6,14},{7,15},{8,0},{9,1},... | collective-permute-start | bytes 516104 | tf_op jit(solution)/shard_map/ppermute | solution.py:384

commit v7 on v6

--- a/solution.py
+++ b/solution.py
@@ -110,7 +110,7 @@
     pl.when(scalar_ref[1] == 1)(lambda: fill(1))
 
 
-def norm_kernel(scalar_ref, feat_ref, keep_ref, mass_ref, weight_ref, carry_ref, label_ref, out_ref):
+def norm_kernel(scalar_ref, feat_ref, keep_ref, mass_ref, weight_ref, carry_ref, label_ref, out_ref, low_ref, high_ref):
     bands = feat_ref.shape[1]
     mass0 = jnp.zeros((1, bands), F32)
     weight0 = jnp.zeros((1, bands), F32)
@@ -123,9 +123,15 @@
     mass = keep * mass0 + mass_ref[...]
     weight = keep * weight0 + weight_ref[...]
     normed = (feat_ref[...] / jnp.sqrt(mass / weight + LEVEL_FLOOR)).astype(BF16)
-    out_ref[LABEL_ROWS:, :] = normed
-    out_ref[:LABEL_ROWS, :] = jnp.zeros((LABEL_ROWS, bands), BF16)
-    out_ref[: label_ref.shape[0], :] = label_ref[...].astype(F32).astype(BF16)
+    label = jnp.concatenate(
+        [label_ref[...].astype(F32), jnp.zeros((LABEL_ROWS - label_ref.shape[0], bands), F32)]).astype(BF16)
+    part = low_ref.shape[0] - LABEL_ROWS
+    first, last = normed[:part], normed[normed.shape[0] - part :]
+    upper = (scalar_ref[2] >> 1) & 1 == 1
+    for ref, value in (
+        (out_ref, normed), (low_ref, jnp.where(upper, first, last)), (high_ref, jnp.where(upper, last, first))):
+        ref[:LABEL_ROWS, :] = label
+        ref[LABEL_ROWS:, :] = value
 
 
 def rows_of(value):
@@ -204,15 +210,33 @@
     return slice(i * TILE + offset, (i + 1) * TILE + offset)
 
 
-def forward_first(before, steps, scalar_ref, norm_ref, a_ref, a2_ref, b_ref, b2_ref,
-                  h1_ref, w_out_ref, kept_ref, gated_ref, slope_ref, conv_ref, res_ref,
-                  h0_ref, in_ref, out_ref):
+def halo(scalar_ref, own_ref, even_ref, odd_ref, low_ref, high_ref, window_ref, label_ref):
+    steps, part = own_ref.shape[0] - LABEL_ROWS, low_ref.shape[0] - LABEL_ROWS
+    lane = own_ref.shape[1]
+    odd, upper = scalar_ref[2] & 1 == 1, (scalar_ref[2] >> 1) & 1 == 1
+    even, uneven, low, high = even_ref[...], odd_ref[...], low_ref[...], high_ref[...]
+    at, row = 0, 0
+    for value, ahead in ((jnp.where(upper, low, high), False), (jnp.where(odd, even, uneven), False),
+                         (own_ref[...], True), (jnp.where(odd, uneven, even), True),
+                         (jnp.where(upper, high, low), True)):
+        count = value.shape[0] - LABEL_ROWS
+        window_ref[at : at + count, :] = value[LABEL_ROWS:]
+        at += count
+        if ahead:
+            label_ref[row : row + count // lane, :] = value[:LABEL_ROWS].astype(F32)[: count // lane]
+            row += count // lane
+
+
+def forward_first(before, steps, scalar_ref, own_ref, even_ref, odd_ref, low_ref, high_ref,
+                  a_ref, a2_ref, b_ref, b2_ref, h1_ref, w_out_ref, label_ref, kept_ref, gated_ref, slope_ref, conv_ref, res_ref,
+                  norm_ref, h0_ref, in_ref, out_ref):
     rows = h0_ref.shape[0]
     kept = slope_ref.shape[1]
     d = rows - h1_ref.shape[0]
     core = scalar_ref[0]
     place(core, (a_ref, a2_ref), place_main(conv_ref, 0))
     place(core, (b_ref, b2_ref), place_side(0, conv_ref, res_ref, in_ref, out_ref))
+    halo(scalar_ref, own_ref, even_ref, odd_ref, low_ref, high_ref, norm_ref, label_ref)
     w_out_ref[...] = rows_of(out_ref[...])
     w_in = rows_of(in_ref[...])
     for i in range(rows // TILE):
@@ -275,7 +299,7 @@
         total = jnp.log(jnp.sum(jnp.exp(logits), axis=1, keepdims=True))
         groups = range(i * TILE // lanes, (i + 1) * TILE // lanes)
         hot = jnp.concatenate(
-            [(class_row == label_ref[k : k + 1, :].astype(F32)).astype(F32).T for k in groups])
+            [(class_row == label_ref[k : k + 1, :]).astype(F32).T for k in groups])
         valid = (row + i * TILE < left).astype(F32)
         lgrad = ((jnp.exp(logits - total) - hot) * (valid * scale)).astype(BF16)
         grad = dot_t(lgrad, w_out_ref[...])
@@ -348,7 +372,7 @@
     weights = halves(conv_ref, 0), halves(conv_ref, 1)
     for i in range(steps // TILE):
         last_ref[tile_of(i), :] = grad_below(grad_ref[tile_of(i), :], back_ref, i, d0, weights).astype(BF16)
-    value = t_dot(norm_ref[...], last_ref[...])
+    value = t_dot(norm_ref[LABEL_ROWS:, :], last_ref[...])
     store_terms(*targets, 2 * conv + res, value, 0, enter, 0, enter)
 
 
@@ -406,14 +430,19 @@
     return lax.optimization_barrier(values)
 
 
-def sum_step(addends, links, dim):
+def add(addends, taken):
+    total = 0.0
+    for v in addends:
+        starts = [taken[d] if d in taken and v.shape[d] == 2 else 0 for d in range(time_bits())]
+        sizes = [1 if d in taken else v.shape[d] for d in range(time_bits())]
+        total = total + lax.dynamic_slice(v, starts + [0, 0], sizes + list(v.shape[-2:])).astype(F32)
+    return total
+
+
+def sum_step(addends, taken, links, dim):
     mine = my_bit(links)
-
-    def half(index):
-        one, two = (lax.dynamic_index_in_dim(v, index, dim).astype(F32) for v in addends)
-        return (one + two).astype(BF16)
-
-    return half(mine), swap(half(1 - mine), links)
+    other = swap(add(addends, taken | {dim: 1 - mine}).astype(BF16), links)
+    return addends + [other], taken | {dim: mine}
 
 
 def sum_steps():
@@ -422,27 +451,12 @@
     return [((NEAR, FAR), 0), ((FAR, NEAR), 1)] + rest
 
 
-def hop(value, by):
-    size = lax.axis_size("tm")
-    return lax.ppermute(value, "tm", [(i, i + by) for i in range(size) if 0 <= i + by < size])
-
-
-def rows_before(value, count):
-    steps, parts, by = value.shape[0] - LABEL_ROWS, [], 1
-    while count > 0:
-        take = min(count, steps)
-        parts.insert(0, hop(value[LABEL_ROWS + steps - take :], by))
-        count, by = count - take, by + 1
-    return parts
-
-
-def rows_after(value, count):
-    steps, parts, by = value.shape[0] - LABEL_ROWS, [], 1
-    while count > 0:
-        take = min(count, steps)
-        parts.append(hop(value[: LABEL_ROWS + take], -by))
-        count, by = count - take, by + 1
-    return parts
+def exchange(value, reach):
+    size, pairs = lax.axis_size("tm"), []
+    for i in range(size - reach):
+        if (i // reach) % 2 == 1:
+            pairs += [(i, i + reach), (i + reach, i)]
+    return lax.ppermute(value, "tm", pairs)
 
 
 def on_device(features, forget, labels, lengths, w_conv, w_res, w_in, w_out):
@@ -474,27 +488,27 @@
     held, feat, forget = together(held[None], features[0], forget[0])
     block = ((steps, bands), F32)
     keep, mass, weight, carry = call(
-        scan_kernel, [block] * 3 + [((3, bands), F32)], [], 40 * steps * bands, feat, forget, limit=FIRST_LIMIT)
+        scan_kernel, [block] * 3 + [((3, bands), F32)], [], 2 * 10**9, feat, forget, limit=FIRST_LIMIT)
     carry = carry[None]
     for bit in reversed(range(2, time_bits())):
         held = grow(held, (("tm", bit),) * 2)
-    for bit in range(2):
-        carry = grow(carry, (("tm", bit),) * 2)
+    carry = grow(carry, (NEAR, NEAR))
     held, carry = together(held, carry)
 
     main_links = [(NEAR, FAR), (FAR, ACROSS), (ACROSS, NEAR)]
     side_links = [(ACROSS, ACROSS), (NEAR, NEAR), (FAR, FAR)]
     main, side = held[:, : conv + cut], held[:, conv + cut :]
     main, side = grow(main, main_links[0]), grow(side, side_links[0])
-    for bit in range(2, time_bits()):
+    for bit in range(1, time_bits()):
         carry = grow(carry, (("tm", bit),) * 2)
     label_rows = steps // bands
-    (normed,) = call(norm_kernel, [((LABEL_ROWS + steps, bands), BF16)], [], 10 * steps * bands,
+    normed, low, high = call(norm_kernel, [((LABEL_ROWS + r, bands), BF16) for r in (steps, reach - steps, reach - steps)],
+                             [], 10**8,
                      scalars, feat, keep, mass, weight, carry, labels[0].reshape(label_rows, bands))
-    main, side, normed = together(main, side, normed)
+    main, side, normed, low, high = together(main, side, normed, low, high)
     main, side = grow(main, main_links[1]), grow(side, side_links[1])
-    past, future = rows_before(normed, reach), rows_after(normed, reach)
-    main, side, past, future = together(main, side, past, future)
+    around = [swap(normed, (NEAR, NEAR)), exchange(normed, 1), swap(low, (FAR, FAR)), exchange(high, 2)]
+    main, side, around = together(main, side, around)
     first = [main[:, :conv], side[:, : half + enter]]
     second = [main[:, conv:], side[:, half + enter :]]
 
@@ -505,21 +519,17 @@
 
     first = [grow(p, links) for p, links in zip(first, last_links)]
     *first, second[0], second[1] = together(*first, *second)
-    own_normed = normed[LABEL_ROWS:]
-    window = jnp.concatenate(past + [own_normed] + [v[LABEL_ROWS:] for v in future])
-    label_window = jnp.concatenate(
-        [v[: (v.shape[0] - LABEL_ROWS) // bands] for v in [normed] + future])
     first, others = both_cores(first), [swap(p, links) for p, links in zip(second, last_links)]
 
     total_rows, rows0, rows1 = steps + 2 * reach, steps + d0, steps + reach
     conv_all, res_all = ((2, devices, conv, c), kind), ((devices, res, c), kind)
     V = pltpu.VMEM
-    h1, out_all, h0, gated0, slope0, conv0, res0 = call(
+    h1, out_all, label_window, h0, gated0, slope0, conv0, res0 = call(
         functools.partial(forward_first, d1, steps),
-        [((total_rows - d0, c), BF16), ((c, classes), BF16), ((rows0, c), BF16), ((steps, c), BF16),
+        [((total_rows - d0, c), BF16), ((c, classes), BF16), ((rows1 // bands, bands), F32), ((rows0, c), BF16), ((steps, c), BF16),
          ((2, rows0, c), BF16), conv_all, res_all],
-        [V((total_rows, c), BF16), V((devices, enter, c), F32), V((devices, out, classes), F32)],
-        2 * total_rows * c * (bands + 5 * c), scalars, window, *first)
+        [V((total_rows, bands), BF16), V((total_rows, c), BF16), V((devices, enter, c), F32), V((devices, out, classes), F32)],
+        2 * total_rows * c * (bands + 5 * c), scalars, normed, *around, *first)
 
     others[0], others[1], h1 = together(*others, h1)
     second = both_cores([arranged(*v) for v in zip(second, others, last_links)])
@@ -536,26 +546,30 @@
     def core_step(keep, send):
         other = swap(send.astype(BF16), (CORE, CORE))
         shape = (2,) * time_bits() + keep.shape[1:]
-        return keep.reshape(shape), other.reshape(shape)
+        return [keep.reshape(shape), other.reshape(shape)]
 
     sums1 = core_step(keep1, send1)
+    sums1, back0 = together(sums1, back0)
     keep0, send0 = call(
         functools.partial(terms_first, sizes), package, [V((steps, c), BF16)],
-        2 * steps * 9 * c * c, scalars, back0, grad1, round0, own_normed, h0, gated0, conv0)
-    sums1, keep0, send0 = together(sums1, keep0, send0)
+        2 * steps * 9 * c * c, scalars, back0, grad1, round0, normed, h0, gated0, conv0)
 
     order = sum_steps()
-    sums1, sums0 = sum_step(sums1, *order[0]), core_step(keep0, send0)
+    taken0, taken1 = {}, {}
+    sums1, taken1 = sum_step(sums1, taken1, *order[0])
+    sums0 = core_step(keep0, send0)
     for step in range(len(order)):
         sums1, sums0 = together(sums1, sums0)
         if step + 1 < len(order):
-            sums1 = sum_step(sums1, *order[step + 1])
-        sums0 = sum_step(sums0, *order[step])
+            sums1, taken1 = sum_step(sums1, taken1, *order[step + 1])
+        sums0, taken0 = sum_step(sums0, taken0, *order[step])
     rows = 2 * conv + res + enter
+    parts = [v.reshape(rows, c) for sums, taken in ((sums0, taken0), (sums1, taken1))
+             for v in (add(sums[:-1], taken), sums[-1])]
     grad_conv, grad_res, grad_in, grad_out = call(
         functools.partial(finish_kernel, sizes),
         [((2, conv, 2 * c), F32), ((2, res, c), F32), ((enter, c), F32), ((out, classes), F32)], [], 1,
-        *(v.reshape(rows, c) for v in sums0 + sums1))
+        *parts)
     return loss.reshape(1, steps), grad_conv, grad_res, grad_in, grad_out
 
 

time: 141 us -> 144 us (1.021)
  starting transfers between devices: 43.4 us -> 39 us
  other arithmetic: 9.04 us -> 13 us
  waiting for transfers between devices: 55.6 us -> 59.4 us
    ppermute x4 -> x2, starting transfers between devices: 11.7 us -> 1.31 us  [exchange(): return lax.ppermute(value, 'tm', pairs)]
    ppermute x24 -> x26, starting transfers between devices: 31.7 us -> 37.7 us  [swap(): return lax.ppermute(value, names, pairs)]
    ppermute x24 -> x26, waiting for transfers between devices: 54 us -> 59.4 us  [swap(): return lax.ppermute(value, names, pairs)]
    convert_element_type x6, other arithmetic: 5.87 us -> 9.69 us  [sum_step(): other = swap(add(addends, taken | {dim: 1 - mine}).astype(BF16), links)]
    ppermute x4 -> x2, waiting for transfers between devices: 1.64 us -> 0.01 us  [exchange(): return lax.ppermute(value, 'tm', pairs)]
  transfers between devices with their start and end apart: 28 -> 28, of which waited for: 14 -> 16; matrix products, arithmetic and copies ran while one was open for 3% -> 5% of each run, Pallas kernels for 9% -> 7%
where the time goes in v7:
time: 144 us
  waiting for transfers between devices  59.4 us (41%)
  starting transfers between devices  39 us (27%)
  Pallas kernels  30.1 us (21%)
  other arithmetic  13 us (9%)
  between operations  1.56 us (1%)
    ppermute x26, waiting for transfers between devices, swap(): return lax.ppermute(value, names, pairs)  59.4 us
    ppermute x26, starting transfers between devices, swap(): return lax.ppermute(value, names, pairs)  37.7 us
    pallas_call x7, Pallas kernels, call(): pl.pallas_call(kernel, out_shape=[jax.ShapeDtypeStruct(s, d) for s, d in...  30.1 us
    convert_element_type x6, other arithmetic, sum_step(): other = swap(add(addends, taken | {dim: 1 - mine}).astype(BF16), links)  9.69 us
  transfers between devices with their start and end apart: 28, of which 16 were waited for; matrix products, arithmetic and copies ran while one was open for 5% of the time, Pallas kernels for 7%

profile of v7, /device:TPU:0, one launch (start us, length us, event | category | flops | bytes accessed | tf_op | source)
XLA Modules:
  0.0 144.1 jit_solution(11893627414016356440)
XLA Ops:
  1.3 0.7 pad_add_fusion.scalar_ref
  1.9 1.7 %shard_map.119 = bf16[168,512]{1,0:T(8,128)(2,1)} custom-call(s32[4]{0:T(128)} %pad_add_fusion.scalar_ref, bf16[2,64,1024]{2,1,0:T(8,128)(2,1)} %conv_ref.1, bf16[2,32,512]{2,1,0:T(8,128)(2,1)} %res_ref.1, bf16[8,512]{1,0:T(8,128)(2,1)} %in_ref.1, bf16[32,128]{1,0:T(8,128)(2,1)} %out_ref.1), custom_call_target="tpu_custom_call" | custom-call | flops 1 | bytes 516112 | tf_op jit(solution)/shard_map/pallas_call | solution.py:38
  3.6 4.0 %collective-permute-start = (bf16[1,168,512]{2,1,0:T(8,128)(2,1)}, bf16[1,168,512]{2,1,0:T(8,128)(2,1)S(1)}, u32[]{:S(2)}, u32[]{:S(2)}) collective-permute-start(bf16[1,168,512]{2,1,0:T(8,128)(2,1)} %bitcast.35), channel_id=1, source_target_pairs={{0,8},{1,9},{2,10},{3,11},{4,12},{5,13},{6,14},{7,15},{8,0},{9,1},... | collective-permute-start | bytes 516104 | tf_op jit(solution)/shard_map/ppermute | solution.py:408
  7.7 2.3 %shard_map.120 = (f32[512,128]{1,0:T(8,128)}, f32[512,128]{1,0:T(8,128)}, f32[512,128]{1,0:T(8,128)}, f32[3,128]{1,0:T(4,128)}) custom-call(f32[512,128]{1,0:T(8,128)} %bitcast.26, f32[512,128]{1,0:T(8,128)} %bitcast.39), custom_call_target="tpu_custom_call" | custom-call | flops 2000000000 | bytes 1312256 | tf_op jit(solution)/shard_map/pallas_call | solution.py:38
  10.0 1.6 %collective-permute-start.1 = (f32[1,3,128]{2,1,0:T(4,128)}, f32[1,3,128]{2,1,0:T(4,128)S(1)}, u32[]{:S(2)}, u32[]{:S(2)}) collective-permute-start(f32[1,3,128]{2,1,0:T(4,128)} %bitcast.37), channel_id=1, source_target_pairs={{0,2},{1,3},{2,0},{3,1},{4,6},{5,7},{6,4},{7,5},{8,10},{9,11},{10,... | collective-permute-start | bytes 4616 | tf_op jit(solution)/shard_map/ppermute | solution.py:408
  11.6 2.3 %collective-permute-done.1 = f32[1,3,128]{2,1,0:T(4,128)S(1)} collective-permute-done((f32[1,3,128]{2,1,0:T(4,128)}, f32[1,3,128]{2,1,0:T(4,128)S(1)}, u32[]{:S(2)}, u32[]{:S(2)}) %collective-permute-start.1) | collective-permute-done | bytes 1568 | tf_op jit(solution)/shard_map/ppermute | solution.py:408
  13.9 0.8 maximum_select_fusion.11
  14.6 1.4 collective-permute-done
  16.1 0.8 collective-permute-start.4
  16.9 2.8 %collective-permute-done.4 = f32[2,3,128]{2,1,0:T(4,128)S(1)} collective-permute-done((f32[2,3,128]{2,1,0:T(4,128)S(1)}, f32[2,3,128]{2,1,0:T(4,128)S(1)}, u32[]{:S(2)}, u32[]{:S(2)}) %collective-permute-start.4) | collective-permute-done | bytes 3104 | tf_op jit(solution)/shard_map/ppermute | solution.py:408
  19.7 2.0 %collective-permute-start.5 = (f32[4,3,128]{2,1,0:T(4,128)S(1)}, f32[4,3,128]{2,1,0:T(4,128)S(1)}, u32[]{:S(2)}, u32[]{:S(2)}) collective-permute-start(f32[4,3,128]{2,1,0:T(4,128)S(1)} %maximum_select_fusion.10), channel_id=1, source_target_pairs={{0,8},{1,9},{2,10},{3,11},{4,12},{5,13},{6,14},{7,15},{8,0},{9,1},... | collective-permute-start | bytes 18440 | tf_op jit(solution)/shard_map/ppermute | solution.py:408
  21.8 1.6 %collective-permute-start.3 = (bf16[2,56,512]{2,1,0:T(8,128)(2,1)S(1)}, bf16[2,56,512]{2,1,0:T(8,128)(2,1)S(1)}, u32[]{:S(2)}, u32[]{:S(2)}) collective-permute-start(bf16[2,56,512]{2,1,0:T(8,128)(2,1)S(1)} %slice.19), channel_id=1, source_target_pairs={{0,16},{1,17},{2,18},{3,19},{4,20},{5,21},{6,22},{7,23},{8,24},{9,... | collective-permute-start | bytes 344072 | tf_op jit(solution)/shard_map/ppermute | solution.py:408
  23.3 1.5 %collective-permute-start.2 = (bf16[2,112,512]{2,1,0:T(8,128)(2,1)S(1)}, bf16[2,112,512]{2,1,0:T(8,128)(2,1)S(1)}, u32[]{:S(2)}, u32[]{:S(2)}) collective-permute-start(bf16[2,112,512]{2,1,0:T(8,128)(2,1)S(1)} %slice.18), channel_id=1, source_target_pairs={{0,2},{1,5},{2,0},{3,7},{4,6},{5,1},{6,4},{7,3},{8,10},{9,13},{10,... | collective-permute-start | bytes 688136 | tf_op jit(solution)/shard_map/ppermute | solution.py:408
  24.9 0.7 shard_map.121
  25.7 1.0 collective-permute-done.3
  26.7 2.7 %collective-permute-done.2 = bf16[2,112,512]{2,1,0:T(8,128)(2,1)S(1)} collective-permute-done((bf16[2,112,512]{2,1,0:T(8,128)(2,1)S(1)}, bf16[2,112,512]{2,1,0:T(8,128)(2,1)S(1)}, u32[]{:S(2)}, u32[]{:S(2)}) %collective-permute-start.2) | collective-permute-done | bytes 229408 | tf_op jit(solution)/shard_map/ppermute | solution.py:408
  29.4 2.1 %collective-permute-start.6 = (bf16[4,112,512]{2,1,0:T(8,128)(2,1)S(1)}, bf16[4,112,512]{2,1,0:T(8,128)(2,1)S(1)}, u32[]{:S(2)}, u32[]{:S(2)}) collective-permute-start(bf16[4,112,512]{2,1,0:T(8,128)(2,1)S(1)} %maximum_select_fusion.4), channel_id=1, source_target_pairs={{0,4},{1,17},{2,6},{3,19},{4,0},{5,21},{6,2},{7,23},{8,12},{9,25},... | collective-permute-start | bytes 1376264 | tf_op jit(solution)/shard_map/ppermute | solution.py:408
  31.5 1.5 %collective-permute-start.7 = (bf16[4,56,512]{2,1,0:T(8,128)(2,1)S(1)}, bf16[4,56,512]{2,1,0:T(8,128)(2,1)S(1)}, u32[]{:S(2)}, u32[]{:S(2)}) collective-permute-start(bf16[4,56,512]{2,1,0:T(8,128)(2,1)S(1)} %maximum_select_fusion.8), channel_id=1, source_target_pairs={{0,2},{1,3},{2,0},{3,1},{4,6},{5,7},{6,4},{7,5},{8,10},{9,11},{10,... | collective-permute-start | bytes 688136 | tf_op jit(solution)/shard_map/ppermute | solution.py:408
  33.0 0.5 collective-permute-start.8
  33.6 0.7 collective-permute-start.9
  34.2 4.3 %collective-permute-start.10 = (bf16[272,128]{1,0:T(8,128)(2,1)S(1)}, bf16[272,128]{1,0:T(8,128)(2,1)S(1)}, u32[]{:S(2)}, u32[]{:S(2)}) collective-permute-start(bf16[272,128]{1,0:T(8,128)(2,1)S(1)} %get-tuple-element.94), channel_id=1, source_target_pairs={{0,4},{1,5},{2,6},{3,7},{4,0},{5,1},{6,2},{7,3},{8,12},{9,13},{10,... | collective-permute-start | bytes 208904 | tf_op jit(solution)/shard_map/ppermute | solution.py:408
  38.5 0.7 collective-permute-start.11
  39.2 0.1 maximum_select_fusion.5
  39.3 0.9 collective-permute-done.6
  40.2 0.1 maximum_select_fusion.1
  40.3 2.3 %collective-permute-done.10.low_ref = bf16[272,128]{1,0:T(8,128)(2,1)S(1)} collective-permute-done((bf16[272,128]{1,0:T(8,128)(2,1)S(1)}, bf16[272,128]{1,0:T(8,128)(2,1)S(1)}, u32[]{:S(2)}, u32[]{:S(2)}) %collective-permute-start.10) | collective-permute-done | bytes 69664 | tf_op jit(solution)/shard_map/ppermute | solution.py:408
  42.7 0.4 collective-permute-start.12
  43.1 4.4 %collective-permute-start.13 = (bf16[8,24,512]{2,1,0:T(8,128)(2,1)S(1)}, bf16[8,24,512]{2,1,0:T(8,128)(2,1)S(1)}, u32[]{:S(2)}, u32[]{:S(2)}) collective-permute-start(bf16[8,24,512]{2,1,0:T(8,128)(2,1)S(1)} %slice.21), channel_id=1, source_target_pairs={{0,4},{1,5},{2,6},{3,7},{4,0},{5,1},{6,2},{7,3},{8,12},{9,13},{10,... | collective-permute-start | bytes 589832 | tf_op jit(solution)/shard_map/ppermute | solution.py:408
  47.5 3.6 %collective-permute-done.13 = bf16[8,24,512]{2,1,0:T(8,128)(2,1)S(1)} collective-permute-done((bf16[8,24,512]{2,1,0:T(8,128)(2,1)S(1)}, bf16[8,24,512]{2,1,0:T(8,128)(2,1)S(1)}, u32[]{:S(2)}, u32[]{:S(2)}) %collective-permute-start.13) | collective-permute-done | bytes 196640 | tf_op jit(solution)/shard_map/ppermute | solution.py:408
  51.2 0.8 collective-permute-done.12
  52.0 0.2 maximum_select_fusion.a_ref
  52.2 0.5 collective-permute-start.17
  52.7 0.3 collective-permute-start.14
  53.0 4.3 %collective-permute-start.15 = (bf16[8,32,512]{2,1,0:T(8,128)(2,1)S(1)}, bf16[8,32,512]{2,1,0:T(8,128)(2,1)S(1)}, u32[]{:S(2)}, u32[]{:S(2)}) collective-permute-start(bf16[8,32,512]{2,1,0:T(8,128)(2,1)S(1)} %slice.23), channel_id=1, source_target_pairs={{0,4},{1,5},{2,6},{3,7},{4,0},{5,1},{6,2},{7,3},{8,12},{9,13},{10,... | collective-permute-start | bytes 786440 | tf_op jit(solution)/shard_map/ppermute | solution.py:408
  57.3 7.4 %shard_map.122 = (bf16[1792,512]{1,0:T(8,128)(2,1)S(1)}, bf16[512,128]{1,0:T(8,128)(2,1)S(1)}, f32[10,128]{1,0:T(8,128)S(1)}, bf16[768,512]{1,0:T(8,128)(2,1)S(1...) custom-call(s32[4]{0:T(128)S(1)} %copy-done.4, ...), custom_call_target="tpu_custom_call" | custom-call | flops 5637144576 | bytes 10904592 | tf_op jit(solution)/shard_map/pallas_call | solution.py:38
  64.8 0.1 maximum_select_fusion.2.a_ref
  65.0 0.1 maximum_select_fusion.3.b_ref
  65.1 0.6 collective-permute-start.19
  65.6 2.4 %collective-permute-done.19.b2_ref = bf16[16,32,512]{2,1,0:T(8,128)(2,1)S(1)} collective-permute-done((bf16[16,32,512]{2,1,0:T(8,128)(2,1)S(1)}, bf16[16,32,512]{2,1,0:T(8,128)(2,1)S(1)}, u32[]{:S(2)}, u32[]{:S(2)}) %collective-permute-start.19) | collective-permute-done | bytes 524320 | tf_op jit(solution)/shard_map/ppermute | solution.py:408
  68.0 12.5 %shard_map.123 = (f32[4,128]{1,0:T(4,128)}, bf16[8,168,512]{2,1,0:T(8,128)(2,1)S(1)}, bf16[8,168,512]{2,1,0:T(8,128)(2,1)S(1)}, f32[512,512]{1,0:T(8,128)S(1)}, ...) custom-call(s32[4]{0:T(128)S(1)} %copy-done.4, bf16[1792,512]{1,0:T(8,128)(2,1)S(1)} %get-tuple-element.107.h1_ref, ...), custom_call_target="tpu_custom_call" | custom-call | flops 7381975040 | bytes 12590096 | tf_op jit(solution)/shard_map/pallas_call | solution.py:38
  80.5 0.2 collective-permute-start.20
  80.7 3.0 %collective-permute-done.20 = bf16[8,168,512]{2,1,0:T(8,128)(2,1)S(1)} collective-permute-done((bf16[8,168,512]{2,1,0:T(8,128)(2,1)S(1)}, bf16[8,168,512]{2,1,0:T(8,128)(2,1)S(1)}, u32[]{:S(2)}, u32[]{:S(2)}) %collective-permute-start.20) | collective-permute-done | bytes 1376288 | tf_op jit(solution)/shard_map/ppermute | solution.py:408
  83.7 4.5 %shard_map.124 = (bf16[8,168,512]{2,1,0:T(8,128)(2,1)S(1)}, bf16[8,168,512]{2,1,0:T(8,128)(2,1)}) custom-call(s32[4]{0:T(128)S(1)} %copy-done.4, bf16[768,1024]{1,0:T(8,128)(2,1)S(1)} %get-tuple-element.120.back_ref, f32[512,512]{1,0:T(8,128)S(1)} %get-tuple-element.121.grad_ref, bf16[512,512]{1,0:T(8,128)(2,1)S(1)} %get-tuple-element.122.round_ref, ...), custom_call_target="tpu_custom_call" | custom-call | flops 2415919104 | bytes 9441296 | tf_op jit(solution)/shard_map/pallas_call | solution.py:38
  88.2 0.1 collective-permute-start.22
  88.3 1.3 add_convert_fusion.1
  89.6 2.1 %collective-permute-start.21 = (bf16[1,2,2,168,512]{4,3,2,1,0:T(8,128)(2,1)S(1)}, bf16[1,2,2,168,512]{4,3,2,1,0:T(8,128)(2,1)S(1)}, u32[]{:S(2)}, u32[]{:S(2)}) collective-permute-start(bf16[1,2,2,168,512]{4,3,2,1,0:T(8,128)(2,1)S(1)} %add_convert_fusion.1), channel_id=1, source_target_pairs={{0,2},{1,5},{2,0},{3,7},{4,6},{5,1},{6,4},{7,3},{8,10},{9,13},{10,... | collective-permute-start | bytes 2064392 | tf_op jit(solution)/shard_map/ppermute | solution.py:408
  91.7 8.9 %collective-permute-done.21 = bf16[1,2,2,168,512]{4,3,2,1,0:T(8,128)(2,1)S(1)} collective-permute-done((bf16[1,2,2,168,512]{4,3,2,1,0:T(8,128)(2,1)S(1)}, bf16[1,2,2,168,512]{4,3,2,1,0:T(8,128)(2,1)S(1)}, u32[]{:S(2)}, u32[]{:S(2)}) %collective-permute-start.21) | collective-permute-done | bytes 688160 | tf_op jit(solution)/shard_map/ppermute | solution.py:408
  100.6 0.9 copy-done.8
  101.5 2.1 %add_convert_fusion = bf16[1,2,2,168,512]{4,3,2,1,0:T(8,128)(2,1)} fusion(bf16[2,2,2,168,512]{4,3,2,1,0:T(8,128)(2,1)} %bitcast.12, s32[]{:T(128)S(6)} %select_n.213, bf16[2,2,2,168,512]{4,3,2,1,0:T(8,128)(2,1)S(1)} %bitcast.23), kind=kLoop, calls=%fused_computation | loop fusion | flops 1376256 | bytes 2064388 | tf_op jit(solution)/shard_map/convert_element_type | solution.py:444
  103.6 2.0 %collective-permute-start.24 = (bf16[1,2,2,168,512]{4,3,2,1,0:T(8,128)(2,1)}, bf16[1,2,2,168,512]{4,3,2,1,0:T(8,128)(2,1)}, u32[]{:S(2)}, u32[]{:S(2)}) collective-permute-start(bf16[1,2,2,168,512]{4,3,2,1,0:T(8,128)(2,1)} %add_convert_fusion), channel_id=1, source_target_pairs={{0,2},{1,5},{2,0},{3,7},{4,6},{5,1},{6,4},{7,3},{8,10},{9,13},{10,... | collective-permute-start | bytes 2064392 | tf_op jit(solution)/shard_map/ppermute | solution.py:408
  105.6 1.2 add_convert_fusion.3
  106.8 1.2 collective-permute-start.23
  108.0 9.1 %collective-permute-done.23 = bf16[1,1,2,168,512]{4,3,2,1,0:T(8,128)(2,1)} collective-permute-done((bf16[1,1,2,168,512]{4,3,2,1,0:T(8,128)(2,1)S(1)}, bf16[1,1,2,168,512]{4,3,2,1,0:T(8,128)(2,1)}, u32[]{:S(2)}, u32[]{:S(2)}) %collective-permute-start.23) | collective-permute-done | bytes 344096 | tf_op jit(solution)/shard_map/ppermute | solution.py:408
  117.1 1.5 %collective-permute-done.24 = bf16[1,2,2,168,512]{4,3,2,1,0:T(8,128)(2,1)} collective-permute-done((bf16[1,2,2,168,512]{4,3,2,1,0:T(8,128)(2,1)}, bf16[1,2,2,168,512]{4,3,2,1,0:T(8,128)(2,1)}, u32[]{:S(2)}, u32[]{:S(2)}) %collective-permute-start.24) | collective-permute-done | bytes 688160 | tf_op jit(solution)/shard_map/ppermute | solution.py:408
  118.5 1.9 %add_convert_fusion.2 = bf16[1,1,2,168,512]{4,3,2,1,0:T(8,128)(2,1)} fusion(bf16[1,2,2,168,512]{4,3,2,1,0:T(8,128)(2,1)} %collective-permute-done.24, s32[]{:T(128)S(6)} %select_n.216, bf16[2,2,2,168,512]{4,3,2,1,0:T(8,128)(2,1)} %bitcast.12, s32[]{:T(128)S(6)} %select_n.214, bf16[2,2,2,168,512]{4,3,2,1,0:T(8,128)(2,1)S(1)} %bitcast.24), kind=kLoop, calls=%fused_computation.5 | loop fusion | flops 1032192 | bytes 1376264 | tf_op jit(solution)/shard_map/convert_element_type | solution.py:444
  120.4 1.4 collective-permute-start.26
  121.8 1.8 %add_convert_fusion.5 = bf16[1,1,1,168,512]{4,3,2,1,0:T(8,128)(2,1)} fusion(bf16[1,1,2,168,512]{4,3,2,1,0:T(8,128)(2,1)} %collective-permute-done.23, s32[]{:T(128)S(6)} %select_n.218, bf16[1,2,2,168,512]{4,3,2,1,0:T(8,128)(2,1)} %copy-done.8, s32[]{:T(128)S(6)} %select_n.217, bf16[2,2,2,168,512]{4,3,2,1,0:T(8,128)(2,1)} %bitcast.33, s32[]{:T(128)S(6)} %select_n.214, ...), kind=kLoop, calls=%fused_computation.15 | loop fusion | flops 688128 | bytes 860172 | tf_op jit(solution)/shard_map/convert_element_type | solution.py:444
  123.6 0.1 collective-permute-start.25
  123.8 10.0 %collective-permute-done.25 = bf16[1,1,1,168,512]{4,3,2,1,0:T(8,128)(2,1)S(1)} collective-permute-done((bf16[1,1,1,168,512]{4,3,2,1,0:T(8,128)(2,1)}, bf16[1,1,1,168,512]{4,3,2,1,0:T(8,128)(2,1)S(1)}, u32[]{:S(2)}, u32[]{:S(2)}) %collective-permute-start.25) | collective-permute-done | bytes 172064 | tf_op jit(solution)/shard_map/ppermute | solution.py:408
  133.8 1.3 add_convert_fusion.4
  135.1 0.2 collective-permute-start.27
  135.3 1.2 add_bitcast_fusion.one1_ref
  136.4 6.7 %collective-permute-done.27 = bf16[1,1,1,168,512]{4,3,2,1,0:T(8,128)(2,1)S(1)} collective-permute-done((bf16[1,1,1,168,512]{4,3,2,1,0:T(8,128)(2,1)S(1)}, bf16[1,1,1,168,512]{4,3,2,1,0:T(8,128)(2,1)S(1)}, u32[]{:S(2)}, u32[]{:S(2)}) %collective-permute-start.27) | collective-permute-done | bytes 172064 | tf_op jit(solution)/shard_map/ppermute | solution.py:408
  143.1 0.9 shard_map.125
  (43 shorter events, 0.5 us)
Async XLA Ops:
  3.6 12.4 %copy-start.7 = (bf16[168,512]{1,0:T(8,128)(2,1)S(1)}, bf16[168,512]{1,0:T(8,128)(2,1)}, u32[]{:S(2)}) copy-start(bf16[168,512]{1,0:T(8,128)(2,1)} %shard_map.119) | copy-start | bytes 516100
  3.6 12.4 %collective-permute-start = (bf16[1,168,512]{2,1,0:T(8,128)(2,1)}, bf16[1,168,512]{2,1,0:T(8,128)(2,1)S(1)}, u32[]{:S(2)}, u32[]{:S(2)}) collective-permute-start(bf16[1,168,512]{2,1,0:T(8,128)(2,1)} %bitcast.35), channel_id=1, source_target_pairs={{0,8},{1,9},{2,10},{3,11},{4,12},{5,13},{6,14},{7,15},{8,0},{9,1},... | collective-permute-start | bytes 516104 | tf_op jit(solution)/shard_map/ppermute | solution.py:408
  10.0 14.9 %copy-start = (f32[1,512,128]{2,1,0:T(8,128)S(1)}, f32[1,512,128]{2,1,0:T(8,128)}, u32[]{:S(2)}) copy-start(f32[1,512,128]{2,1,0:T(8,128)} %param.8) | copy-start | bytes 786436
  10.0 14.9 %copy-start.1 = (f32[512,128]{1,0:T(8,128)S(1)}, f32[512,128]{1,0:T(8,128)}, u32[]{:S(2)}) copy-start(f32[512,128]{1,0:T(8,128)} %get-tuple-element.84.keep_ref) | copy-start | bytes 786436
  10.0 14.9 %copy-start.2 = (f32[512,128]{1,0:T(8,128)S(1)}, f32[512,128]{1,0:T(8,128)}, u32[]{:S(2)}) copy-start(f32[512,128]{1,0:T(8,128)} %get-tuple-element.85.mass_ref) | copy-start | bytes 786436
  10.0 14.9 %copy-start.3 = (f32[512,128]{1,0:T(8,128)S(1)}, f32[512,128]{1,0:T(8,128)}, u32[]{:S(2)}) copy-start(f32[512,128]{1,0:T(8,128)} %get-tuple-element.86.weight_ref) | copy-start | bytes 786436
  10.0 14.9 %copy-start.4 = (s32[4]{0:T(128)S(1)}, s32[4]{0:T(128)}, u32[]{:S(2)}) copy-start(s32[4]{0:T(128)} %pad_add_fusion.scalar_ref) | copy-start | bytes 52
  10.0 14.9 %copy-start.5 = (s32[1,512]{1,0:T(1,128)S(1)}, s32[1,512]{1,0:T(1,128)}, u32[]{:S(2)}) copy-start(s32[1,512]{1,0:T(1,128)} %param.10) | copy-start | bytes 6148
  10.0 3.9 %collective-permute-start.1 = (f32[1,3,128]{2,1,0:T(4,128)}, f32[1,3,128]{2,1,0:T(4,128)S(1)}, u32[]{:S(2)}, u32[]{:S(2)}) collective-permute-start(f32[1,3,128]{2,1,0:T(4,128)} %bitcast.37), channel_id=1, source_target_pairs={{0,2},{1,3},{2,0},{3,1},{4,6},{5,7},{6,4},{7,5},{8,10},{9,11},{10,... | collective-permute-start | bytes 4616 | tf_op jit(solution)/shard_map/ppermute | solution.py:408
  16.1 3.7 %collective-permute-start.4 = (f32[2,3,128]{2,1,0:T(4,128)S(1)}, f32[2,3,128]{2,1,0:T(4,128)S(1)}, u32[]{:S(2)}, u32[]{:S(2)}) collective-permute-start(f32[2,3,128]{2,1,0:T(4,128)S(1)} %maximum_select_fusion.11), channel_id=1, source_target_pairs={{0,4},{1,5},{2,6},{3,7},{4,0},{5,1},{6,2},{7,3},{8,12},{9,13},{10,... | collective-permute-start | bytes 9224 | tf_op jit(solution)/shard_map/ppermute | solution.py:408
  19.7 5.1 %collective-permute-start.5 = (f32[4,3,128]{2,1,0:T(4,128)S(1)}, f32[4,3,128]{2,1,0:T(4,128)S(1)}, u32[]{:S(2)}, u32[]{:S(2)}) collective-permute-start(f32[4,3,128]{2,1,0:T(4,128)S(1)} %maximum_select_fusion.10), channel_id=1, source_target_pairs={{0,8},{1,9},{2,10},{3,11},{4,12},{5,13},{6,14},{7,15},{8,0},{9,1},... | collective-permute-start | bytes 18440 | tf_op jit(solution)/shard_map/ppermute | solution.py:408
  21.8 4.9 %collective-permute-start.3 = (bf16[2,56,512]{2,1,0:T(8,128)(2,1)S(1)}, bf16[2,56,512]{2,1,0:T(8,128)(2,1)S(1)}, u32[]{:S(2)}, u32[]{:S(2)}) collective-permute-start(bf16[2,56,512]{2,1,0:T(8,128)(2,1)S(1)} %slice.19), channel_id=1, source_target_pairs={{0,16},{1,17},{2,18},{3,19},{4,20},{5,21},{6,22},{7,23},{8,24},{9,... | collective-permute-start | bytes 344072 | tf_op jit(solution)/shard_map/ppermute | solution.py:408
  23.3 6.0 %collective-permute-start.2 = (bf16[2,112,512]{2,1,0:T(8,128)(2,1)S(1)}, bf16[2,112,512]{2,1,0:T(8,128)(2,1)S(1)}, u32[]{:S(2)}, u32[]{:S(2)}) collective-permute-start(bf16[2,112,512]{2,1,0:T(8,128)(2,1)S(1)} %slice.18), channel_id=1, source_target_pairs={{0,2},{1,5},{2,0},{3,7},{4,6},{5,1},{6,4},{7,3},{8,10},{9,13},{10,... | collective-permute-start | bytes 688136 | tf_op jit(solution)/shard_map/ppermute | solution.py:408
  29.4 10.7 %collective-permute-start.6 = (bf16[4,112,512]{2,1,0:T(8,128)(2,1)S(1)}, bf16[4,112,512]{2,1,0:T(8,128)(2,1)S(1)}, u32[]{:S(2)}, u32[]{:S(2)}) collective-permute-start(bf16[4,112,512]{2,1,0:T(8,128)(2,1)S(1)} %maximum_select_fusion.4), channel_id=1, source_target_pairs={{0,4},{1,17},{2,6},{3,19},{4,0},{5,21},{6,2},{7,23},{8,12},{9,25},... | collective-permute-start | bytes 1376264 | tf_op jit(solution)/shard_map/ppermute | solution.py:408
  31.5 7.0 %collective-permute-start.7 = (bf16[4,56,512]{2,1,0:T(8,128)(2,1)S(1)}, bf16[4,56,512]{2,1,0:T(8,128)(2,1)S(1)}, u32[]{:S(2)}, u32[]{:S(2)}) collective-permute-start(bf16[4,56,512]{2,1,0:T(8,128)(2,1)S(1)} %maximum_select_fusion.8), channel_id=1, source_target_pairs={{0,2},{1,3},{2,0},{3,1},{4,6},{5,7},{6,4},{7,5},{8,10},{9,11},{10,... | collective-permute-start | bytes 688136 | tf_op jit(solution)/shard_map/ppermute | solution.py:408
  33.0 9.6 %collective-permute-start.8 = (bf16[528,128]{1,0:T(8,128)(2,1)S(1)}, bf16[528,128]{1,0:T(8,128)(2,1)S(1)}, u32[]{:S(2)}, u32[]{:S(2)}) collective-permute-start(bf16[528,128]{1,0:T(8,128)(2,1)S(1)} %get-tuple-element.93.own_ref.norm_ref), channel_id=1, source_target_pairs={{0,2},{1,3},{2,0},{3,1},{4,6},{5,7},{6,4},{7,5},{8,10},{9,11},{10,... | collective-permute-start | bytes 405512 | tf_op jit(solution)/shard_map/ppermute | solution.py:408
  33.6 9.1 %collective-permute-start.9 = (bf16[528,128]{1,0:T(8,128)(2,1)S(1)}, bf16[528,128]{1,0:T(8,128)(2,1)S(1)}, u32[]{:S(2)}, u32[]{:S(2)}) collective-permute-start(bf16[528,128]{1,0:T(8,128)(2,1)S(1)} %get-tuple-element.93.own_ref.norm_ref), channel_id=1, source_target_pairs={{2,4},{4,2},{6,8},{8,6},{10,12},{12,10},{3,5},{5,3},{7,9},{9,7},{1... | collective-permute-start | bytes 405512 | tf_op jit(solution)/shard_map/ppermute | solution.py:459
  34.2 8.5 %collective-permute-start.10 = (bf16[272,128]{1,0:T(8,128)(2,1)S(1)}, bf16[272,128]{1,0:T(8,128)(2,1)S(1)}, u32[]{:S(2)}, u32[]{:S(2)}) collective-permute-start(bf16[272,128]{1,0:T(8,128)(2,1)S(1)} %get-tuple-element.94), channel_id=1, source_target_pairs={{0,4},{1,5},{2,6},{3,7},{4,0},{5,1},{6,2},{7,3},{8,12},{9,13},{10,... | collective-permute-start | bytes 208904 | tf_op jit(solution)/shard_map/ppermute | solution.py:408
  38.5 4.2 %collective-permute-start.11 = (bf16[272,128]{1,0:T(8,128)(2,1)S(1)}, bf16[272,128]{1,0:T(8,128)(2,1)S(1)}, u32[]{:S(2)}, u32[]{:S(2)}) collective-permute-start(bf16[272,128]{1,0:T(8,128)(2,1)S(1)} %get-tuple-element.95), channel_id=1, source_target_pairs={{4,8},{8,4},{6,10},{10,6},{5,9},{9,5},{7,11},{11,7},{20,24},{24,20... | collective-permute-start | bytes 208904 | tf_op jit(solution)/shard_map/ppermute | solution.py:459
  42.7 9.2 %collective-permute-start.12 = (bf16[8,64,512]{2,1,0:T(8,128)(2,1)S(1)}, bf16[8,64,512]{2,1,0:T(8,128)(2,1)S(1)}, u32[]{:S(2)}, u32[]{:S(2)}) collective-permute-start(bf16[8,64,512]{2,1,0:T(8,128)(2,1)S(1)} %slice.20), channel_id=1, source_target_pairs={{0,16},{1,3},{2,18},{3,1},{4,20},{5,7},{6,22},{7,5},{8,24},{9,11},... | collective-permute-start | bytes 1572872 | tf_op jit(solution)/shard_map/ppermute | solution.py:408
  43.1 8.0 %collective-permute-start.13 = (bf16[8,24,512]{2,1,0:T(8,128)(2,1)S(1)}, bf16[8,24,512]{2,1,0:T(8,128)(2,1)S(1)}, u32[]{:S(2)}, u32[]{:S(2)}) collective-permute-start(bf16[8,24,512]{2,1,0:T(8,128)(2,1)S(1)} %slice.21), channel_id=1, source_target_pairs={{0,4},{1,5},{2,6},{3,7},{4,0},{5,1},{6,2},{7,3},{8,12},{9,13},{10,... | collective-permute-start | bytes 589832 | tf_op jit(solution)/shard_map/ppermute | solution.py:408
  52.1 5.2 %collective-permute-start.16 = (bf16[16,64,512]{2,1,0:T(8,128)(2,1)S(1)}, bf16[16,64,512]{2,1,0:T(8,128)(2,1)S(1)}, u32[]{:S(2)}, u32[]{:S(2)}) collective-permute-start(bf16[16,64,512]{2,1,0:T(8,128)(2,1)S(1)} %maximum_select_fusion.a_ref), channel_id=1, source_target_pairs={{0,1},{1,0},{2,3},{3,2},{4,5},{5,4},{6,7},{7,6},{8,9},{9,8},{10,11... | collective-permute-start | bytes 3145736 | tf_op jit(solution)/shard_map/ppermute | solution.py:408
  52.2 5.1 %collective-permute-start.17 = (bf16[16,24,512]{2,1,0:T(8,128)(2,1)S(1)}, bf16[16,24,512]{2,1,0:T(8,128)(2,1)S(1)}, u32[]{:S(2)}, u32[]{:S(2)}) collective-permute-start(bf16[16,24,512]{2,1,0:T(8,128)(2,1)S(1)} %maximum_select_fusion.6.b_ref), channel_id=1, source_target_pairs={{0,1},{1,0},{2,3},{3,2},{4,5},{5,4},{6,7},{7,6},{8,9},{9,8},{10,11... | collective-permute-start | bytes 1179656 | tf_op jit(solution)/shard_map/ppermute | solution.py:408
  52.7 12.0 %collective-permute-start.14 = (bf16[8,48,512]{2,1,0:T(8,128)(2,1)S(1)}, bf16[8,48,512]{2,1,0:T(8,128)(2,1)S(1)}, u32[]{:S(2)}, u32[]{:S(2)}) collective-permute-start(bf16[8,48,512]{2,1,0:T(8,128)(2,1)S(1)} %slice.22), channel_id=1, source_target_pairs={{0,16},{1,3},{2,18},{3,1},{4,20},{5,7},{6,22},{7,5},{8,24},{9,11},... | collective-permute-start | bytes 1179656 | tf_op jit(solution)/shard_map/ppermute | solution.py:408
  53.0 11.7 %collective-permute-start.15 = (bf16[8,32,512]{2,1,0:T(8,128)(2,1)S(1)}, bf16[8,32,512]{2,1,0:T(8,128)(2,1)S(1)}, u32[]{:S(2)}, u32[]{:S(2)}) collective-permute-start(bf16[8,32,512]{2,1,0:T(8,128)(2,1)S(1)} %slice.23), channel_id=1, source_target_pairs={{0,4},{1,5},{2,6},{3,7},{4,0},{5,1},{6,2},{7,3},{8,12},{9,13},{10,... | collective-permute-start | bytes 786440 | tf_op jit(solution)/shard_map/ppermute | solution.py:408
  64.9 3.1 %collective-permute-start.18 = (bf16[16,48,512]{2,1,0:T(8,128)(2,1)S(1)}, bf16[16,48,512]{2,1,0:T(8,128)(2,1)S(1)}, u32[]{:S(2)}, u32[]{:S(2)}) collective-permute-start(bf16[16,48,512]{2,1,0:T(8,128)(2,1)S(1)} %maximum_select_fusion.2.a_ref), channel_id=1, source_target_pairs={{0,1},{1,0},{2,3},{3,2},{4,5},{5,4},{6,7},{7,6},{8,9},{9,8},{10,11... | collective-permute-start | bytes 2359304 | tf_op jit(solution)/shard_map/ppermute | solution.py:408
  65.1 2.9 %collective-permute-start.19 = (bf16[16,32,512]{2,1,0:T(8,128)(2,1)S(1)}, bf16[16,32,512]{2,1,0:T(8,128)(2,1)S(1)}, u32[]{:S(2)}, u32[]{:S(2)}) collective-permute-start(bf16[16,32,512]{2,1,0:T(8,128)(2,1)S(1)} %maximum_select_fusion.3.b_ref), channel_id=1, source_target_pairs={{0,1},{1,0},{2,3},{3,2},{4,5},{5,4},{6,7},{7,6},{8,9},{9,8},{10,11... | collective-permute-start | bytes 1572872 | tf_op jit(solution)/shard_map/ppermute | solution.py:408
  80.5 3.2 %collective-permute-start.20 = (bf16[8,168,512]{2,1,0:T(8,128)(2,1)S(1)}, bf16[8,168,512]{2,1,0:T(8,128)(2,1)S(1)}, u32[]{:S(2)}, u32[]{:S(2)}) collective-permute-start(bf16[8,168,512]{2,1,0:T(8,128)(2,1)S(1)} %get-tuple-element.116), channel_id=1, source_target_pairs={{0,1},{1,0},{2,3},{3,2},{4,5},{5,4},{6,7},{7,6},{8,9},{9,8},{10,11... | collective-permute-start | bytes 4128776 | tf_op jit(solution)/shard_map/ppermute | solution.py:408
  83.7 4.5 %copy-start.6 = (bf16[8,168,512]{2,1,0:T(8,128)(2,1)}, bf16[8,168,512]{2,1,0:T(8,128)(2,1)S(1)}, u32[]{:S(2)}) copy-start(bf16[8,168,512]{2,1,0:T(8,128)(2,1)S(1)} %collective-permute-done.20) | copy-start | bytes 4128772
  88.2 13.3 %collective-permute-start.22 = (bf16[8,168,512]{2,1,0:T(8,128)(2,1)}, bf16[8,168,512]{2,1,0:T(8,128)(2,1)}, u32[]{:S(2)}, u32[]{:S(2)}) collective-permute-start(bf16[8,168,512]{2,1,0:T(8,128)(2,1)} %get-tuple-element.127), channel_id=1, source_target_pairs={{0,1},{1,0},{2,3},{3,2},{4,5},{5,4},{6,7},{7,6},{8,9},{9,8},{10,11... | collective-permute-start | bytes 4128776 | tf_op jit(solution)/shard_map/ppermute | solution.py:408
  89.6 11.0 %collective-permute-start.21 = (bf16[1,2,2,168,512]{4,3,2,1,0:T(8,128)(2,1)S(1)}, bf16[1,2,2,168,512]{4,3,2,1,0:T(8,128)(2,1)S(1)}, u32[]{:S(2)}, u32[]{:S(2)}) collective-permute-start(bf16[1,2,2,168,512]{4,3,2,1,0:T(8,128)(2,1)S(1)} %add_convert_fusion.1), channel_id=1, source_target_pairs={{0,2},{1,5},{2,0},{3,7},{4,6},{5,1},{6,4},{7,3},{8,10},{9,13},{10,... | collective-permute-start | bytes 2064392 | tf_op jit(solution)/shard_map/ppermute | solution.py:408
  100.6 0.9 copy-start.8
  103.6 14.9 %collective-permute-start.24 = (bf16[1,2,2,168,512]{4,3,2,1,0:T(8,128)(2,1)}, bf16[1,2,2,168,512]{4,3,2,1,0:T(8,128)(2,1)}, u32[]{:S(2)}, u32[]{:S(2)}) collective-permute-start(bf16[1,2,2,168,512]{4,3,2,1,0:T(8,128)(2,1)} %add_convert_fusion), channel_id=1, source_target_pairs={{0,2},{1,5},{2,0},{3,7},{4,6},{5,1},{6,4},{7,3},{8,10},{9,13},{10,... | collective-permute-start | bytes 2064392 | tf_op jit(solution)/shard_map/ppermute | solution.py:408
  106.8 10.3 %collective-permute-start.23 = (bf16[1,1,2,168,512]{4,3,2,1,0:T(8,128)(2,1)S(1)}, bf16[1,1,2,168,512]{4,3,2,1,0:T(8,128)(2,1)}, u32[]{:S(2)}, u32[]{:S(2)}) collective-permute-start(bf16[1,1,2,168,512]{4,3,2,1,0:T(8,128)(2,1)S(1)} %add_convert_fusion.3), channel_id=1, source_target_pairs={{0,4},{1,3},{2,6},{3,1},{4,0},{5,7},{6,2},{7,5},{8,12},{9,11},{10,... | collective-permute-start | bytes 1032200 | tf_op jit(solution)/shard_map/ppermute | solution.py:408
  120.4 13.3 %collective-permute-start.26 = (bf16[1,1,2,168,512]{4,3,2,1,0:T(8,128)(2,1)}, bf16[1,1,2,168,512]{4,3,2,1,0:T(8,128)(2,1)S(1)}, u32[]{:S(2)}, u32[]{:S(2)}) collective-permute-start(bf16[1,1,2,168,512]{4,3,2,1,0:T(8,128)(2,1)} %add_convert_fusion.2), channel_id=1, source_target_pairs={{0,4},{1,3},{2,6},{3,1},{4,0},{5,7},{6,2},{7,5},{8,12},{9,11},{10,... | collective-permute-start | bytes 1032200 | tf_op jit(solution)/shard_map/ppermute | solution.py:408
  123.6 10.1 %collective-permute-start.25 = (bf16[1,1,1,168,512]{4,3,2,1,0:T(8,128)(2,1)}, bf16[1,1,1,168,512]{4,3,2,1,0:T(8,128)(2,1)S(1)}, u32[]{:S(2)}, u32[]{:S(2)}) collective-permute-start(bf16[1,1,1,168,512]{4,3,2,1,0:T(8,128)(2,1)} %add_convert_fusion.5), channel_id=1, source_target_pairs={{0,8},{1,9},{2,10},{3,11},{4,12},{5,13},{6,14},{7,15},{8,0},{9,1},... | collective-permute-start | bytes 516104 | tf_op jit(solution)/shard_map/ppermute | solution.py:408
  135.1 8.0 %collective-permute-start.27 = (bf16[1,1,1,168,512]{4,3,2,1,0:T(8,128)(2,1)S(1)}, bf16[1,1,1,168,512]{4,3,2,1,0:T(8,128)(2,1)S(1)}, u32[]{:S(2)}, u32[]{:S(2)}) collective-permute-start(bf16[1,1,1,168,512]{4,3,2,1,0:T(8,128)(2,1)S(1)} %get-tuple-element.153), channel_id=1, source_target_pairs={{0,8},{1,9},{2,10},{3,11},{4,12},{5,13},{6,14},{7,15},{8,0},{9,1},... | collective-permute-start | bytes 516104 | tf_op jit(solution)/shard_map/ppermute | solution.py:408

commit v8 on v7

--- a/solution.py
+++ b/solution.py
@@ -82,32 +82,16 @@
         carry_ref[k : k + 1, :] = value[rows - 1 :]
 
 
-def pack_kernel(scalar_ref, conv_ref, res_ref, in_ref, out_ref, pack_ref):
-    c = pack_ref.shape[1]
-    cut, half, more = conv_ref.shape[1] * 3 // 4, res_ref.shape[1] // 2, in_ref.shape[0]
-
-    def fill(across):
-        cols = slice(across * c, (across + 1) * c)
-        part = slice(across * half, (across + 1) * half)
-        at = 0
-
-        def put(value):
-            nonlocal at
-            pack_ref[at : at + value.shape[0], :] = value
-            at += value.shape[0]
-
-        put(conv_ref[0, :, cols])
-        put(conv_ref[1, :cut, cols])
-        put(res_ref[0, part, :])
-        if across:
-            put(jnp.concatenate([out_ref[k * more : (k + 1) * more, :] for k in range(c // out_ref.shape[1])], axis=1))
-        else:
-            put(in_ref[...])
-        put(res_ref[1, part, :])
-        put(conv_ref[1, cut:, cols])
-
-    pl.when(scalar_ref[1] == 0)(lambda: fill(0))
-    pl.when(scalar_ref[1] == 1)(lambda: fill(1))
+def pack_kernel(conv_ref, res_ref, in_ref, out_ref, first_ref, second_ref):
+    conv, res, more, c = conv_ref.shape[1], res_ref.shape[1], in_ref.shape[0], first_ref.shape[1]
+    for layer, ref in enumerate((first_ref, second_ref)):
+        ref[:conv, :] = conv_ref[layer, :, :c]
+        ref[conv : 2 * conv, :] = conv_ref[layer, :, c:]
+        ref[2 * conv : 2 * conv + res, :] = res_ref[layer]
+    at = 2 * conv + res
+    first_ref[at : at + more, :] = in_ref[...]
+    first_ref[at + more : at + 2 * more, :] = jnp.concatenate(
+        [out_ref[k * more : (k + 1) * more, :] for k in range(c // out_ref.shape[1])], axis=1)
 
 
 def norm_kernel(scalar_ref, feat_ref, keep_ref, mass_ref, weight_ref, carry_ref, label_ref, out_ref, low_ref, high_ref):
@@ -115,7 +99,7 @@
     mass0 = jnp.zeros((1, bands), F32)
     weight0 = jnp.zeros((1, bands), F32)
     for tm in range(carry_ref.shape[0]):
-        before = tm < scalar_ref[2]
+        before = tm < scalar_ref[1]
         keep, mass, weight = (carry_ref[tm, k : k + 1, :] for k in range(3))
         mass0 = jnp.where(before, keep * mass0 + mass, mass0)
         weight0 = jnp.where(before, keep * weight0 + weight, weight0)
@@ -127,7 +111,7 @@
         [label_ref[...].astype(F32), jnp.zeros((LABEL_ROWS - label_ref.shape[0], bands), F32)]).astype(BF16)
     part = low_ref.shape[0] - LABEL_ROWS
     first, last = normed[:part], normed[normed.shape[0] - part :]
-    upper = (scalar_ref[2] >> 1) & 1 == 1
+    upper = (scalar_ref[1] >> 1) & 1 == 1
     for ref, value in (
         (out_ref, normed), (low_ref, jnp.where(upper, first, last)), (high_ref, jnp.where(upper, last, first))):
         ref[:LABEL_ROWS, :] = label
@@ -143,17 +127,28 @@
     return rows_of(conv_ref[gate, :half]), rows_of(conv_ref[gate, half:])
 
 
-def place(core, pair, puts):
+def place(core, pair, conv_ref, res_ref, in_ref=None, out_ref=None):
+    conv, res = conv_ref.shape[2], res_ref.shape[1]
     for ref, own in zip(pair, (True, False)):
         s = core if own else 1 - core
-        rest = ref.shape[0] // 8
+        rest = ref.shape[0] // 4
         bits = rest.bit_length() - 1
-        for steps in itertools.product((0, 1), repeat=3):
-            base = (4 * steps[0] + 2 * steps[1] + steps[2]) * rest
-
-            def put(p, _):
+        for second, first in itertools.product((0, 1), repeat=2):
+
+            def put(p, _, second=second, first=first, ref=ref, s=s):
                 high = sum(((p >> (bits - 1 - b)) & 1) << b for b in range(bits))
-                puts(s, steps, high, ref, base + p)
+                device = 2 * (4 * high + 2 * by_core(s, second, first) + by_core(s, first, second)) + s
+                k = (2 * second + first) * rest + p
+                conv_ref[0, device] = ref[k, :conv, :].astype(conv_ref.dtype)
+                conv_ref[1, device] = ref[k, conv : 2 * conv, :].astype(conv_ref.dtype)
+                res_ref[device] = ref[k, 2 * conv : 2 * conv + res, :].astype(res_ref.dtype)
+                if in_ref is not None:
+                    value = ref[k, 2 * conv + res :, :].astype(F32)
+                    count, classes = value.shape[0] // 2, out_ref.shape[2]
+                    in_ref[device] = value[:count]
+                    for q in range(value.shape[1] // classes):
+                        out_ref[device, q * count : (q + 1) * count, :] = (
+                            value[count:, q * classes : (q + 1) * classes])
                 return 0
 
             if rest <= 2:
@@ -163,38 +158,6 @@
                 lax.fori_loop(0, rest, put, 0)
 
 
-def place_main(conv_ref, row):
-    def put(s, steps, high, ref, k):
-        third, second, first = steps
-        across = by_core(s, third, second)
-        tm = 4 * high + 2 * by_core(s, second, first) + by_core(s, first, third)
-        conv_ref[across, 2 * tm + s, row : row + ref.shape[1], :] = ref[k].astype(conv_ref.dtype)
-
-    return put
-
-
-def place_side(layer, conv_ref, res_ref, *extra):
-    def put(s, steps, high, ref, k):
-        far, near, across = steps
-        device = 2 * (4 * high + 2 * far + near) + s
-        half = res_ref.shape[1] // 2
-        res_ref[device, across * half : (across + 1) * half, :] = ref[k, :half, :].astype(res_ref.dtype)
-        value = ref[k, half:, :]
-        if layer == 1:
-            conv_ref[across, device, conv_ref.shape[2] - value.shape[0] :, :] = value.astype(conv_ref.dtype)
-            return
-        in_ref, out_ref = extra
-        value = value.astype(F32)
-        if across == 0:
-            in_ref[device] = value
-            return
-        count, classes = value.shape[0], out_ref.shape[2]
-        for q in range(value.shape[1] // classes):
-            out_ref[device, q * count : (q + 1) * count, :] = value[:, q * classes : (q + 1) * classes]
-
-    return put
-
-
 def activate(past, now, conv_ref):
     joined = jnp.concatenate([past, now], axis=1)
     t = jnp.tanh(dot(joined, rows_of(conv_ref[0])))
@@ -213,7 +176,7 @@
 def halo(scalar_ref, own_ref, even_ref, odd_ref, low_ref, high_ref, window_ref, label_ref):
     steps, part = own_ref.shape[0] - LABEL_ROWS, low_ref.shape[0] - LABEL_ROWS
     lane = own_ref.shape[1]
-    odd, upper = scalar_ref[2] & 1 == 1, (scalar_ref[2] >> 1) & 1 == 1
+    odd, upper = scalar_ref[1] & 1 == 1, (scalar_ref[1] >> 1) & 1 == 1
     even, uneven, low, high = even_ref[...], odd_ref[...], low_ref[...], high_ref[...]
     at, row = 0, 0
     for value, ahead in ((jnp.where(upper, low, high), False), (jnp.where(odd, even, uneven), False),
@@ -228,14 +191,13 @@
 
 
 def forward_first(before, steps, scalar_ref, own_ref, even_ref, odd_ref, low_ref, high_ref,
-                  a_ref, a2_ref, b_ref, b2_ref, h1_ref, w_out_ref, label_ref, kept_ref, gated_ref, slope_ref, conv_ref, res_ref,
+                  here_ref, there_ref, h1_ref, w_out_ref, label_ref, kept_ref, gated_ref, slope_ref, conv_ref, res_ref,
                   norm_ref, h0_ref, in_ref, out_ref):
     rows = h0_ref.shape[0]
     kept = slope_ref.shape[1]
     d = rows - h1_ref.shape[0]
     core = scalar_ref[0]
-    place(core, (a_ref, a2_ref), place_main(conv_ref, 0))
-    place(core, (b_ref, b2_ref), place_side(0, conv_ref, res_ref, in_ref, out_ref))
+    place(core, (here_ref, there_ref), conv_ref, res_ref, in_ref, out_ref)
     halo(scalar_ref, own_ref, even_ref, odd_ref, low_ref, high_ref, norm_ref, label_ref)
     w_out_ref[...] = rows_of(out_ref[...])
     w_in = rows_of(in_ref[...])
@@ -271,7 +233,7 @@
     store_terms(*targets, size, value[:, c:], first, size, 0, size)
 
 
-def second_kernel(steps, scale, sizes, scalar_ref, h1_ref, w_out_ref, label_ref, a_ref, a2_ref, b_ref, b2_ref,
+def second_kernel(steps, scale, sizes, scalar_ref, h1_ref, w_out_ref, label_ref, here_ref, there_ref,
                   slope0_ref, res0_ref,
                   loss_ref, keep_ref, send_ref, grad0_ref, round0_ref, back0_ref,
                   back_ref, grad_ref, conv_ref, res_ref, gated_ref, h2_ref, lgrad_ref, round_ref):
@@ -280,14 +242,13 @@
     classes = w_out_ref.shape[1]
     conv, res, _, out = sizes
     core = scalar_ref[0]
-    place(core, (a_ref, a2_ref), place_main(conv_ref, 0))
-    place(core, (b_ref, b2_ref), place_side(1, conv_ref, res_ref))
+    place(core, (here_ref, there_ref), conv_ref, res_ref)
 
     lanes = label_ref.shape[1]
     class_row = lax.broadcasted_iota(jnp.int32, (classes, lanes), 0).astype(F32)
     unit = class_row == lax.broadcasted_iota(jnp.int32, (lanes, lanes), 1).astype(F32)
     row = lax.broadcasted_iota(jnp.int32, (TILE, 1), 0)
-    left = scalar_ref[3] - scalar_ref[2] * steps
+    left = scalar_ref[2] - scalar_ref[1] * steps
 
     for i in range(rows // TILE):
         at = tile_of(i)
@@ -393,19 +354,17 @@
                 out_ref[q * count : (q + 1) * count, :] = rest[:, q * classes : (q + 1) * classes]
 
 
-NEAR, FAR, ACROSS = ("tm", 0), ("tm", 1), ("groups", 0)
+NEAR, FAR = ("tm", 0), ("tm", 1)
 CORE = ("site", 0)
 
 
 def swap(value, links):
-    names = ("groups", "tm", "site")
-    sizes = [lax.axis_size(name) for name in names]
-    pairs = []
-    for at in itertools.product(*(range(size) for size in sizes)):
-        axis, bit = links[at[2]]
-        to = tuple(i ^ (1 << bit) if name == axis else i for name, i in zip(names, at))
-        pairs.append(tuple((p[0] * sizes[1] + p[1]) * sizes[2] + p[2] for p in (at, to)))
-    return lax.ppermute(value, names, pairs)
+    count, pairs = lax.axis_size("site"), []
+    for tm, site in itertools.product(range(lax.axis_size("tm")), range(count)):
+        axis, bit = links[site]
+        to = (tm ^ (1 << bit), site) if axis == "tm" else (tm, site ^ (1 << bit))
+        pairs.append((tm * count + site, to[0] * count + to[1]))
+    return lax.ppermute(value, ("tm", "site"), pairs)
 
 
 def my_bit(links):
@@ -430,19 +389,26 @@
     return lax.optimization_barrier(values)
 
 
-def add(addends, taken):
-    total = 0.0
-    for v in addends:
-        starts = [taken[d] if d in taken and v.shape[d] == 2 else 0 for d in range(time_bits())]
-        sizes = [1 if d in taken else v.shape[d] for d in range(time_bits())]
-        total = total + lax.dynamic_slice(v, starts + [0, 0], sizes + list(v.shape[-2:])).astype(F32)
-    return total
-
-
-def sum_step(addends, taken, links, dim):
-    mine = my_bit(links)
-    other = swap(add(addends, taken | {dim: 1 - mine}).astype(BF16), links)
-    return addends + [other], taken | {dim: mine}
+def half_kernel(bits, sent, scalar_ref, one_ref, two_ref, out_ref):
+    position = scalar_ref[1]
+    mine = by_core(scalar_ref[0], (position >> bits[0]) & 1, (position >> bits[1]) & 1)
+    index = 1 - mine if sent else mine
+    for p in range(out_ref.shape[0]):
+        out_ref[p] = (one_ref[p, index].astype(F32) + two_ref[p, index].astype(F32)).astype(BF16)
+
+
+def sum_step(addends, scalars, links, dim):
+    shape = addends[0].shape
+    outer, rows = math.prod(shape[:dim]), math.prod(shape[dim + 1 : -1])
+    flat = [v.reshape(outer, 2, rows, shape[-1]) for v in addends]
+
+    def half(sent):
+        bits = tuple(bit for _, bit in links)
+        (value,) = call(functools.partial(half_kernel, bits, sent), [((outer, rows, shape[-1]), BF16)], [],
+                        2 * 10**8, scalars, *flat)
+        return value.reshape(shape[:dim] + (1,) + shape[dim + 1 :])
+
+    return [half(False), swap(half(True), links)]
 
 
 def sum_steps():
@@ -466,60 +432,48 @@
     c = w_res.shape[2]
     classes = w_out.shape[1]
     conv, res, enter, out = sizes = (w_conv.shape[1], w_res.shape[1], w_in.shape[0], w_out.shape[0])
-    half, cut = res // 2, conv * 3 // 4
     aligned = conv % 64 == 0 and res % 32 == 0
     kind = BF16 if aligned else F32
     d0, d1 = BASE_DILATION, 2 * BASE_DILATION
     reach = d0 + d1
-    across = my_bit((ACROSS, ACROSS))
-    scalars = jnp.stack(
-        [lax.axis_index("site"), across, lax.axis_index("tm"), lengths[0]]).astype(jnp.int32)
+    scalars = jnp.stack([lax.axis_index("site"), lax.axis_index("tm"), lengths[0]]).astype(jnp.int32)
 
     if aligned:
-        (held,) = call(pack_kernel, [((2 * (conv + half) + enter, c), BF16)], [], 1,
-                       scalars, w_conv, w_res, w_in, w_out, limit=FIRST_LIMIT)
+        held0, held1 = call(pack_kernel, [((2 * conv + res + 2 * enter, c), BF16), ((2 * conv + res, c), BF16)], [], 1,
+                            w_conv, w_res, w_in, w_out, limit=FIRST_LIMIT)
     else:
-        conv_own = jnp.where(across == 0, w_conv[:, :, :c], w_conv[:, :, c:])
-        res_own = jnp.where(across == 0, w_res[:, :half], w_res[:, half:])
         out_own = jnp.concatenate([w_out[k * enter : (k + 1) * enter] for k in range(c // classes)], axis=1)
-        held = jnp.concatenate([
-            conv_own[0], conv_own[1, :cut], res_own[0],
-            jnp.where(across == 0, w_in, out_own), res_own[1], conv_own[1, cut:]])
-    held, feat, forget = together(held[None], features[0], forget[0])
+        held0, held1 = (jnp.concatenate([w_conv[k, :, :c], w_conv[k, :, c:], w_res[k]] + more)
+                        for k, more in ((0, [w_in, out_own]), (1, [])))
+    held0, held1, feat, forget = together(held0[None], held1[None], features[0], forget[0])
     block = ((steps, bands), F32)
     keep, mass, weight, carry = call(
         scan_kernel, [block] * 3 + [((3, bands), F32)], [], 2 * 10**9, feat, forget, limit=FIRST_LIMIT)
     carry = carry[None]
-    for bit in reversed(range(2, time_bits())):
-        held = grow(held, (("tm", bit),) * 2)
-    carry = grow(carry, (NEAR, NEAR))
-    held, carry = together(held, carry)
-
-    main_links = [(NEAR, FAR), (FAR, ACROSS), (ACROSS, NEAR)]
-    side_links = [(ACROSS, ACROSS), (NEAR, NEAR), (FAR, FAR)]
-    main, side = held[:, : conv + cut], held[:, conv + cut :]
-    main, side = grow(main, main_links[0]), grow(side, side_links[0])
-    for bit in range(1, time_bits()):
-        carry = grow(carry, (("tm", bit),) * 2)
+    far = [(("tm", bit),) * 2 for bit in reversed(range(2, time_bits()))]
+    turns = [(NEAR, FAR), (FAR, NEAR)]
+    for links in far:
+        held0 = grow(held0, links)
+    for link in (NEAR, FAR):
+        carry = grow(carry, (link, link))
+    held0, carry, held1 = together(held0, carry, held1)
+    held0 = grow(held0, turns[0])
+    for links in reversed(far):
+        carry = grow(carry, links)
+    for links in far:
+        held1 = grow(held1, links)
     label_rows = steps // bands
     normed, low, high = call(norm_kernel, [((LABEL_ROWS + r, bands), BF16) for r in (steps, reach - steps, reach - steps)],
                              [], 10**8,
                      scalars, feat, keep, mass, weight, carry, labels[0].reshape(label_rows, bands))
-    main, side, normed, low, high = together(main, side, normed, low, high)
-    main, side = grow(main, main_links[1]), grow(side, side_links[1])
+    held0, normed, low, high, held1 = together(held0, normed, low, high, held1)
+    held0, held1 = grow(held0, turns[1]), grow(held1, turns[0])
     around = [swap(normed, (NEAR, NEAR)), exchange(normed, 1), swap(low, (FAR, FAR)), exchange(high, 2)]
-    main, side, around = together(main, side, around)
-    first = [main[:, :conv], side[:, : half + enter]]
-    second = [main[:, conv:], side[:, half + enter :]]
-
-    last_links = (main_links[2], side_links[2])
-
-    def both_cores(parts):
-        return [v.astype(kind) for p in parts for v in (p, swap(p, (CORE, CORE)))]
-
-    first = [grow(p, links) for p, links in zip(first, last_links)]
-    *first, second[0], second[1] = together(*first, *second)
-    first, others = both_cores(first), [swap(p, links) for p, links in zip(second, last_links)]
+    held0, held1, around = together(held0, held1, around)
+    other1 = swap(held1, turns[1])
+
+    def both_cores(held):
+        return held.astype(kind), swap(held, (CORE, CORE)).astype(kind)
 
     total_rows, rows0, rows1 = steps + 2 * reach, steps + d0, steps + reach
     conv_all, res_all = ((2, devices, conv, c), kind), ((devices, res, c), kind)
@@ -529,10 +483,10 @@
         [((total_rows - d0, c), BF16), ((c, classes), BF16), ((rows1 // bands, bands), F32), ((rows0, c), BF16), ((steps, c), BF16),
          ((2, rows0, c), BF16), conv_all, res_all],
         [V((total_rows, bands), BF16), V((total_rows, c), BF16), V((devices, enter, c), F32), V((devices, out, classes), F32)],
-        2 * total_rows * c * (bands + 5 * c), scalars, normed, *around, *first)
-
-    others[0], others[1], h1 = together(*others, h1)
-    second = both_cores([arranged(*v) for v in zip(second, others, last_links)])
+        2 * total_rows * c * (bands + 5 * c), scalars, normed, *around, *both_cores(held0))
+
+    other1, h1 = together(other1, h1)
+    second = both_cores(arranged(held1, other1, turns[1]))
     scale = 1.0 / math.sqrt(site_devices * steps * time_devices)
     package = [((time_devices, 2 * conv + res + enter, c), kind)] * 2
     loss, keep1, send1, grad1, round0, back0 = call(
@@ -549,23 +503,20 @@
         return [keep.reshape(shape), other.reshape(shape)]
 
     sums1 = core_step(keep1, send1)
-    sums1, back0 = together(sums1, back0)
     keep0, send0 = call(
         functools.partial(terms_first, sizes), package, [V((steps, c), BF16)],
         2 * steps * 9 * c * c, scalars, back0, grad1, round0, normed, h0, gated0, conv0)
+    sums1, keep0, send0 = together(sums1, keep0, send0)
 
     order = sum_steps()
-    taken0, taken1 = {}, {}
-    sums1, taken1 = sum_step(sums1, taken1, *order[0])
-    sums0 = core_step(keep0, send0)
+    sums1, sums0 = sum_step(sums1, scalars, *order[0]), core_step(keep0, send0)
     for step in range(len(order)):
         sums1, sums0 = together(sums1, sums0)
         if step + 1 < len(order):
-            sums1, taken1 = sum_step(sums1, taken1, *order[step + 1])
-        sums0, taken0 = sum_step(sums0, taken0, *order[step])
+            sums1 = sum_step(sums1, scalars, *order[step + 1])
+        sums0 = sum_step(sums0, scalars, *order[step])
     rows = 2 * conv + res + enter
-    parts = [v.reshape(rows, c) for sums, taken in ((sums0, taken0), (sums1, taken1))
-             for v in (add(sums[:-1], taken), sums[-1])]
+    parts = [v.reshape(rows, c) for v in sums0 + sums1]
     grad_conv, grad_res, grad_in, grad_out = call(
         functools.partial(finish_kernel, sizes),
         [((2, conv, 2 * c), F32), ((2, res, c), F32), ((enter, c), F32), ((out, classes), F32)], [], 1,

time: 144 us -> 131 us (0.910)
  other arithmetic: 13 us -> 1.57 us
  waiting for transfers between devices: 59.4 us -> 48.9 us
  Pallas kernels: 30.1 us -> 36.5 us
  local copies, waits for them, and re-layouts: 1.01 us -> 2.86 us
    ppermute x26 -> x21, waiting for transfers between devices: 59.4 us -> 48.9 us  [swap(): return lax.ppermute(value, ('tm', 'site'), pairs)]
    convert_element_type x6 -> x0, other arithmetic: 9.69 us -> none  [sum_step(): other = swap(add(addends, taken | {dim: 1 - mine}).astype(BF16), links)]
    pallas_call x7 -> x19, Pallas kernels: 30.1 us -> 36.5 us  [call(): pl.pallas_call(kernel, out_shape=[jax.ShapeDtypeStruct(s, d) for s, d in...]
    unnamed x18 -> x14, local copies, waits for them, and re-layouts: 0.89 us -> 2.86 us
    ppermute x26 -> x21, starting transfers between devices: 37.7 us -> 37.7 us  [swap(): return lax.ppermute(value, ('tm', 'site'), pairs)]
  transfers between devices with their start and end apart: 28 -> 23, of which waited for: 16 -> 14; matrix products, arithmetic and copies ran while one was open for 5% -> 1% of each run, Pallas kernels for 7% -> 13%
where the time goes in v8:
time: 131 us; the launch traced here: 130 us
  waiting for transfers between devices  48.9 us (37%)
  starting transfers between devices  39 us (30%)
  Pallas kernels  36.5 us (28%)
  local copies, waits for them, and re-layouts  2.86 us (2%)
  other arithmetic  1.57 us (1%)
  between operations  1.56 us (1%)
    ppermute x21, waiting for transfers between devices, swap(): return lax.ppermute(value, ('tm', 'site'), pairs)  48.9 us
    ppermute x21, starting transfers between devices, swap(): return lax.ppermute(value, ('tm', 'site'), pairs)  37.7 us
    pallas_call x19, Pallas kernels, call(): pl.pallas_call(kernel, out_shape=[jax.ShapeDtypeStruct(s, d) for s, d in...  36.5 us
    unnamed x14, local copies, waits for them, and re-layouts  2.86 us
  transfers between devices with their start and end apart: 23, of which 14 were waited for; matrix products, arithmetic and copies ran while one was open for 1% of the time, Pallas kernels for 13%

profile of v8, /device:TPU:0, one launch (start us, length us, event | category | flops | bytes accessed | tf_op | source)
XLA Modules:
  0.0 130.4 jit_solution(16019778215777283155)
XLA Ops:
  0.6 1.8 %shard_map.119 = (bf16[176,512]{1,0:T(8,128)(2,1)}, bf16[160,512]{1,0:T(8,128)(2,1)}) custom-call(bf16[2,64,1024]{2,1,0:T(8,128)(2,1)} %conv_ref.1, bf16[2,32,512]{2,1,0:T(8,128)(2,1)} %res_ref.1, bf16[8,512]{1,0:T(8,128)(2,1)} %in_ref.1, bf16[32,128]{1,0:T(8,128)(2,1)} %out_ref.1), custom_call_target="tpu_custom_call" | custom-call | flops 1 | bytes 688128 | tf_op jit(solution)/shard_map/pallas_call | solution.py:38
  2.4 2.4 %shard_map.120 = (f32[512,128]{1,0:T(8,128)}, f32[512,128]{1,0:T(8,128)}, f32[512,128]{1,0:T(8,128)}, f32[3,128]{1,0:T(4,128)}) custom-call(f32[512,128]{1,0:T(8,128)} %bitcast.70, f32[512,128]{1,0:T(8,128)} %bitcast.83), custom_call_target="tpu_custom_call" | custom-call | flops 2000000000 | bytes 1312256 | tf_op jit(solution)/shard_map/pallas_call | solution.py:38
  4.8 3.0 %collective-permute-start.1 = (f32[1,3,128]{2,1,0:T(4,128)}, f32[1,3,128]{2,1,0:T(4,128)S(1)}, u32[]{:S(2)}, u32[]{:S(2)}) collective-permute-start(f32[1,3,128]{2,1,0:T(4,128)} %bitcast.81), channel_id=1, source_target_pairs={{0,2},{1,3},{2,0},{3,1},{4,6},{5,7},{6,4},{7,5},{8,10},{9,11},{10,... | collective-permute-start | bytes 4616 | tf_op jit(solution)/shard_map/ppermute | solution.py:367
  7.8 2.6 %collective-permute-start = (bf16[1,176,512]{2,1,0:T(8,128)(2,1)S(1)}, bf16[1,176,512]{2,1,0:T(8,128)(2,1)S(1)}, u32[]{:S(2)}, u32[]{:S(2)}) collective-permute-start(bf16[1,176,512]{2,1,0:T(8,128)(2,1)S(1)} %bitcast.77), channel_id=1, source_target_pairs={{0,8},{1,9},{2,10},{3,11},{4,12},{5,13},{6,14},{7,15},{8,0},{9,1},... | collective-permute-start | bytes 540680 | tf_op jit(solution)/shard_map/ppermute | solution.py:367
  10.3 0.8 maximum_select_fusion.8
  11.1 1.6 %collective-permute-start.2 = (f32[2,3,128]{2,1,0:T(4,128)S(1)}, f32[2,3,128]{2,1,0:T(4,128)S(1)}, u32[]{:S(2)}, u32[]{:S(2)}) collective-permute-start(f32[2,3,128]{2,1,0:T(4,128)S(1)} %maximum_select_fusion.8), channel_id=1, source_target_pairs={{0,4},{1,5},{2,6},{3,7},{4,0},{5,1},{6,2},{7,3},{8,12},{9,13},{10,... | collective-permute-start | bytes 9224 | tf_op jit(solution)/shard_map/ppermute | solution.py:367
  12.7 2.0 %collective-permute-done.2 = f32[2,3,128]{2,1,0:T(4,128)S(1)} collective-permute-done((f32[2,3,128]{2,1,0:T(4,128)S(1)}, f32[2,3,128]{2,1,0:T(4,128)S(1)}, u32[]{:S(2)}, u32[]{:S(2)}) %collective-permute-start.2) | collective-permute-done | bytes 3104 | tf_op jit(solution)/shard_map/ppermute | solution.py:367
  14.7 3.8 %collective-permute-done = bf16[1,176,512]{2,1,0:T(8,128)(2,1)S(1)} collective-permute-done((bf16[1,176,512]{2,1,0:T(8,128)(2,1)S(1)}, bf16[1,176,512]{2,1,0:T(8,128)(2,1)S(1)}, u32[]{:S(2)}, u32[]{:S(2)}) %collective-permute-start) | collective-permute-done | bytes 180256 | tf_op jit(solution)/shard_map/ppermute | solution.py:367
  18.6 0.5 collective-permute-start.3
  19.8 2.9 %collective-permute-start.5 = (bf16[1,160,512]{2,1,0:T(8,128)(2,1)S(1)}, bf16[1,160,512]{2,1,0:T(8,128)(2,1)S(1)}, u32[]{:S(2)}, u32[]{:S(2)}) collective-permute-start(bf16[1,160,512]{2,1,0:T(8,128)(2,1)S(1)} %bitcast.79), channel_id=1, source_target_pairs={{0,8},{1,9},{2,10},{3,11},{4,12},{5,13},{6,14},{7,15},{8,0},{9,1},... | collective-permute-start | bytes 491528 | tf_op jit(solution)/shard_map/ppermute | solution.py:367
  22.7 0.1 pad_add_fusion.scalar_ref
  22.8 1.5 %collective-permute-done.4 = f32[4,3,128]{2,1,0:T(4,128)S(1)} collective-permute-done((f32[4,3,128]{2,1,0:T(4,128)S(1)}, f32[4,3,128]{2,1,0:T(4,128)S(1)}, u32[]{:S(2)}, u32[]{:S(2)}) %collective-permute-start.4) | collective-permute-done | bytes 6176 | tf_op jit(solution)/shard_map/ppermute | solution.py:367
  24.4 0.9 copy-done.1
  25.3 0.9 copy-done.2
  26.3 0.9 copy-done.3
  27.2 0.7 shard_map.121
  28.0 0.1 maximum_select_fusion.2
  28.1 3.3 %collective-permute-start.6 = (bf16[4,176,512]{2,1,0:T(8,128)(2,1)S(1)}, bf16[4,176,512]{2,1,0:T(8,128)(2,1)S(1)}, u32[]{:S(2)}, u32[]{:S(2)}) collective-permute-start(bf16[4,176,512]{2,1,0:T(8,128)(2,1)S(1)} %maximum_select_fusion.2), channel_id=1, source_target_pairs={{0,4},{1,3},{2,6},{3,1},{4,0},{5,7},{6,2},{7,5},{8,12},{9,11},{10,... | collective-permute-start | bytes 2162696 | tf_op jit(solution)/shard_map/ppermute | solution.py:367
  31.4 1.2 collective-permute-start.7
  32.6 0.7 collective-permute-start.9
  33.3 4.7 %collective-permute-start.8 = (bf16[528,128]{1,0:T(8,128)(2,1)S(1)}, bf16[528,128]{1,0:T(8,128)(2,1)S(1)}, u32[]{:S(2)}, u32[]{:S(2)}) collective-permute-start(bf16[528,128]{1,0:T(8,128)(2,1)S(1)} %get-tuple-element.88.own_ref.norm_ref), channel_id=1, source_target_pairs={{0,2},{1,3},{2,0},{3,1},{4,6},{5,7},{6,4},{7,5},{8,10},{9,11},{10,... | collective-permute-start | bytes 405512 | tf_op jit(solution)/shard_map/ppermute | solution.py:367
  38.0 2.5 %collective-permute-start.10 = (bf16[272,128]{1,0:T(8,128)(2,1)S(1)}, bf16[272,128]{1,0:T(8,128)(2,1)S(1)}, u32[]{:S(2)}, u32[]{:S(2)}) collective-permute-start(bf16[272,128]{1,0:T(8,128)(2,1)S(1)} %get-tuple-element.89), channel_id=1, source_target_pairs={{0,4},{1,5},{2,6},{3,7},{4,0},{5,1},{6,2},{7,3},{8,12},{9,13},{10,... | collective-permute-start | bytes 208904 | tf_op jit(solution)/shard_map/ppermute | solution.py:367
  40.5 1.4 %collective-permute-done.7 = bf16[2,160,512]{2,1,0:T(8,128)(2,1)S(1)} collective-permute-done((bf16[2,160,512]{2,1,0:T(8,128)(2,1)S(1)}, bf16[2,160,512]{2,1,0:T(8,128)(2,1)S(1)}, u32[]{:S(2)}, u32[]{:S(2)}) %collective-permute-start.7) | collective-permute-done | bytes 327712 | tf_op jit(solution)/shard_map/ppermute | solution.py:367
  42.0 0.7 collective-permute-start.11
  42.6 0.1 maximum_select_fusion.3
  42.7 3.1 %collective-permute-done.6 = bf16[4,176,512]{2,1,0:T(8,128)(2,1)S(1)} collective-permute-done((bf16[4,176,512]{2,1,0:T(8,128)(2,1)S(1)}, bf16[4,176,512]{2,1,0:T(8,128)(2,1)S(1)}, u32[]{:S(2)}, u32[]{:S(2)}) %collective-permute-start.6) | collective-permute-done | bytes 720928 | tf_op jit(solution)/shard_map/ppermute | solution.py:367
  45.9 0.2 maximum_select_fusion.here_ref
  46.1 2.5 %collective-permute-done.10.low_ref = bf16[272,128]{1,0:T(8,128)(2,1)S(1)} collective-permute-done((bf16[272,128]{1,0:T(8,128)(2,1)S(1)}, bf16[272,128]{1,0:T(8,128)(2,1)S(1)}, u32[]{:S(2)}, u32[]{:S(2)}) %collective-permute-start.10) | collective-permute-done | bytes 69664 | tf_op jit(solution)/shard_map/ppermute | solution.py:367
  48.6 1.8 %collective-permute-start.13 = (bf16[8,176,512]{2,1,0:T(8,128)(2,1)S(1)}, bf16[8,176,512]{2,1,0:T(8,128)(2,1)S(1)}, u32[]{:S(2)}, u32[]{:S(2)}) collective-permute-start(bf16[8,176,512]{2,1,0:T(8,128)(2,1)S(1)} %maximum_select_fusion.here_ref), channel_id=1, source_target_pairs={{0,1},{1,0},{2,3},{3,2},{4,5},{5,4},{6,7},{7,6},{8,9},{9,8},{10,11... | collective-permute-start | bytes 4325384 | tf_op jit(solution)/shard_map/ppermute | solution.py:367
  50.4 3.4 %collective-permute-start.12 = (bf16[4,160,512]{2,1,0:T(8,128)(2,1)S(1)}, bf16[4,160,512]{2,1,0:T(8,128)(2,1)S(1)}, u32[]{:S(2)}, u32[]{:S(2)}) collective-permute-start(bf16[4,160,512]{2,1,0:T(8,128)(2,1)S(1)} %maximum_select_fusion.3), channel_id=1, source_target_pairs={{0,4},{1,3},{2,6},{3,1},{4,0},{5,7},{6,2},{7,5},{8,12},{9,11},{10,... | collective-permute-start | bytes 1966088 | tf_op jit(solution)/shard_map/ppermute | solution.py:367
  53.8 7.4 %shard_map.122 = (bf16[1792,512]{1,0:T(8,128)(2,1)S(1)}, bf16[512,128]{1,0:T(8,128)(2,1)S(1)}, f32[10,128]{1,0:T(8,128)S(1)}, bf16[768,512]{1,0:T(8,128)(2,1)S(1...) custom-call(s32[3]{0:T(128)S(1)} %pad_add_fusion.scalar_ref, ...), custom_call_target="tpu_custom_call" | custom-call | flops 5637144576 | bytes 10904588 | tf_op jit(solution)/shard_map/pallas_call | solution.py:38
  61.2 1.2 collective-permute-done.12
  62.4 0.2 maximum_select_fusion.1.here_ref
  62.6 0.1 collective-permute-start.14
  62.7 3.0 %collective-permute-done.14.there_ref = bf16[8,160,512]{2,1,0:T(8,128)(2,1)S(1)} collective-permute-done((bf16[8,160,512]{2,1,0:T(8,128)(2,1)S(1)}, bf16[8,160,512]{2,1,0:T(8,128)(2,1)S(1)}, u32[]{:S(2)}, u32[]{:S(2)}) %collective-permute-start.14) | collective-permute-done | bytes 1310752 | tf_op jit(solution)/shard_map/ppermute | solution.py:367
  65.7 12.3 %shard_map.123 = (f32[4,128]{1,0:T(4,128)}, bf16[8,168,512]{2,1,0:T(8,128)(2,1)S(1)}, bf16[8,168,512]{2,1,0:T(8,128)(2,1)S(1)}, f32[512,512]{1,0:T(8,128)S(1)}, ...) custom-call(s32[3]{0:T(128)S(1)} %pad_add_fusion.scalar_ref, bf16[1792,512]{1,0:T(8,128)(2,1)S(1)} %get-tuple-element.98.h1_ref, ...), custom_call_target="tpu_custom_call" | custom-call | flops 7381975040 | bytes 12590092 | tf_op jit(solution)/shard_map/pallas_call | solution.py:38
  78.0 0.2 collective-permute-start.15
  78.2 3.4 %shard_map.124 = (bf16[8,168,512]{2,1,0:T(8,128)(2,1)S(1)}, bf16[8,168,512]{2,1,0:T(8,128)(2,1)S(1)}) custom-call(s32[3]{0:T(128)S(1)} %pad_add_fusion.scalar_ref, bf16[768,1024]{1,0:T(8,128)(2,1)S(1)} %get-tuple-element.107.back_ref, f32[512,512]{1,0:T(8,128)S(1)} %get-tuple-element.108.grad_ref, bf16[512,512]{1,0:T(8,128)(2,1)S(1)} %get-tuple-element.109.round_ref, ...), custom_call_target="tpu_custom_call" | custom-call | flops 2415919104 | bytes 9441292 | tf_op jit(solution)/shard_map/pallas_call | solution.py:38
  81.6 0.4 collective-permute-start.17
  82.1 0.7 shard_map.126
  82.8 0.9 collective-permute-start.16
  83.7 0.7 shard_map.125
  84.4 9.4 %collective-permute-done.16 = bf16[1,2,2,168,512]{4,3,2,1,0:T(8,128)(2,1)S(1)} collective-permute-done((bf16[1,2,2,168,512]{4,3,2,1,0:T(8,128)(2,1)S(1)}, bf16[1,2,2,168,512]{4,3,2,1,0:T(8,128)(2,1)S(1)}, u32[]{:S(2)}, u32[]{:S(2)}) %collective-permute-start.16) | collective-permute-done | bytes 688160 | tf_op jit(solution)/shard_map/ppermute | solution.py:367
  93.8 0.7 shard_map.130
  94.5 0.9 collective-permute-start.19
  95.4 0.6 shard_map.128
  96.0 1.8 %collective-permute-start.18 = (bf16[1,1,2,168,512]{4,3,2,1,0:T(8,128)(2,1)S(1)}, bf16[1,1,2,168,512]{4,3,2,1,0:T(8,128)(2,1)S(1)}, u32[]{:S(2)}, u32[]{:S(2)}) collective-permute-start(bf16[1,1,2,168,512]{4,3,2,1,0:T(8,128)(2,1)S(1)} %bitcast.69), channel_id=1, source_target_pairs={{0,4},{1,3},{2,6},{3,1},{4,0},{5,7},{6,2},{7,5},{8,12},{9,11},{10,... | collective-permute-start | bytes 1032200 | tf_op jit(solution)/shard_map/ppermute | solution.py:367
  97.8 0.6 shard_map.127
  98.5 0.7 shard_map.129
  99.2 7.9 %collective-permute-done.18 = bf16[1,1,2,168,512]{4,3,2,1,0:T(8,128)(2,1)S(1)} collective-permute-done((bf16[1,1,2,168,512]{4,3,2,1,0:T(8,128)(2,1)S(1)}, bf16[1,1,2,168,512]{4,3,2,1,0:T(8,128)(2,1)S(1)}, u32[]{:S(2)}, u32[]{:S(2)}) %collective-permute-start.18) | collective-permute-done | bytes 344096 | tf_op jit(solution)/shard_map/ppermute | solution.py:367
  107.1 2.1 %collective-permute-done.19 = bf16[1,2,2,168,512]{4,3,2,1,0:T(8,128)(2,1)S(1)} collective-permute-done((bf16[1,2,2,168,512]{4,3,2,1,0:T(8,128)(2,1)S(1)}, bf16[1,2,2,168,512]{4,3,2,1,0:T(8,128)(2,1)S(1)}, u32[]{:S(2)}, u32[]{:S(2)}) %collective-permute-start.19) | collective-permute-done | bytes 688160 | tf_op jit(solution)/shard_map/ppermute | solution.py:367
  109.2 0.6 shard_map.134
  109.8 1.1 collective-permute-start.21
  110.9 0.6 shard_map.132
  111.5 2.5 %collective-permute-start.20 = (bf16[1,1,1,168,512]{4,3,2,1,0:T(8,128)(2,1)S(1)}, bf16[1,1,1,168,512]{4,3,2,1,0:T(8,128)(2,1)S(1)}, u32[]{:S(2)}, u32[]{:S(2)}) collective-permute-start(bf16[1,1,1,168,512]{4,3,2,1,0:T(8,128)(2,1)S(1)} %bitcast.74), channel_id=1, source_target_pairs={{0,8},{1,9},{2,10},{3,11},{4,12},{5,13},{6,14},{7,15},{8,0},{9,1},... | collective-permute-start | bytes 516104 | tf_op jit(solution)/shard_map/ppermute | solution.py:367
  114.0 0.6 shard_map.131
  114.6 0.6 shard_map.133
  115.2 4.1 %collective-permute-done.20 = bf16[1,1,1,168,512]{4,3,2,1,0:T(8,128)(2,1)S(1)} collective-permute-done((bf16[1,1,1,168,512]{4,3,2,1,0:T(8,128)(2,1)S(1)}, bf16[1,1,1,168,512]{4,3,2,1,0:T(8,128)(2,1)S(1)}, u32[]{:S(2)}, u32[]{:S(2)}) %collective-permute-start.20) | collective-permute-done | bytes 172064 | tf_op jit(solution)/shard_map/ppermute | solution.py:367
  119.4 1.3 %collective-permute-done.21 = bf16[1,1,2,168,512]{4,3,2,1,0:T(8,128)(2,1)S(1)} collective-permute-done((bf16[1,1,2,168,512]{4,3,2,1,0:T(8,128)(2,1)S(1)}, bf16[1,1,2,168,512]{4,3,2,1,0:T(8,128)(2,1)S(1)}, u32[]{:S(2)}, u32[]{:S(2)}) %collective-permute-start.21) | collective-permute-done | bytes 344096 | tf_op jit(solution)/shard_map/ppermute | solution.py:367
  120.7 0.6 shard_map.136
  121.3 2.2 %collective-permute-start.22 = (bf16[1,1,1,168,512]{4,3,2,1,0:T(8,128)(2,1)S(1)}, bf16[1,1,1,168,512]{4,3,2,1,0:T(8,128)(2,1)S(1)}, u32[]{:S(2)}, u32[]{:S(2)}) collective-permute-start(bf16[1,1,1,168,512]{4,3,2,1,0:T(8,128)(2,1)S(1)} %bitcast.75), channel_id=1, source_target_pairs={{0,8},{1,9},{2,10},{3,11},{4,12},{5,13},{6,14},{7,15},{8,0},{9,1},... | collective-permute-start | bytes 516104 | tf_op jit(solution)/shard_map/ppermute | solution.py:367
  123.5 0.6 shard_map.135
  124.1 5.4 %collective-permute-done.22 = bf16[1,1,1,168,512]{4,3,2,1,0:T(8,128)(2,1)S(1)} collective-permute-done((bf16[1,1,1,168,512]{4,3,2,1,0:T(8,128)(2,1)S(1)}, bf16[1,1,1,168,512]{4,3,2,1,0:T(8,128)(2,1)S(1)}, u32[]{:S(2)}, u32[]{:S(2)}) %collective-permute-start.22) | collective-permute-done | bytes 172064 | tf_op jit(solution)/shard_map/ppermute | solution.py:367
  129.5 0.9 shard_map.137
  (25 shorter events, 0.2 us)
Async XLA Ops:
  2.4 5.4 %copy-start.5 = (bf16[176,512]{1,0:T(8,128)(2,1)S(1)}, bf16[176,512]{1,0:T(8,128)(2,1)}, u32[]{:S(2)}) copy-start(bf16[176,512]{1,0:T(8,128)(2,1)} %get-tuple-element.70) | copy-start | bytes 540676
  2.4 17.4 %copy-start.6 = (bf16[160,512]{1,0:T(8,128)(2,1)S(1)}, bf16[160,512]{1,0:T(8,128)(2,1)}, u32[]{:S(2)}) copy-start(bf16[160,512]{1,0:T(8,128)(2,1)} %get-tuple-element.71) | copy-start | bytes 491524
  2.4 22.0 %copy-start = (f32[1,512,128]{2,1,0:T(8,128)S(1)}, f32[1,512,128]{2,1,0:T(8,128)}, u32[]{:S(2)}) copy-start(f32[1,512,128]{2,1,0:T(8,128)} %param.8) | copy-start | bytes 786436
  2.4 22.0 %copy-start.4 = (s32[1,512]{1,0:T(1,128)S(1)}, s32[1,512]{1,0:T(1,128)}, u32[]{:S(2)}) copy-start(s32[1,512]{1,0:T(1,128)} %param.10) | copy-start | bytes 6148
  4.8 5.6 %collective-permute-start.1 = (f32[1,3,128]{2,1,0:T(4,128)}, f32[1,3,128]{2,1,0:T(4,128)S(1)}, u32[]{:S(2)}, u32[]{:S(2)}) collective-permute-start(f32[1,3,128]{2,1,0:T(4,128)} %bitcast.81), channel_id=1, source_target_pairs={{0,2},{1,3},{2,0},{3,1},{4,6},{5,7},{6,4},{7,5},{8,10},{9,11},{10,... | collective-permute-start | bytes 4616 | tf_op jit(solution)/shard_map/ppermute | solution.py:367
  7.8 10.8 %collective-permute-start = (bf16[1,176,512]{2,1,0:T(8,128)(2,1)S(1)}, bf16[1,176,512]{2,1,0:T(8,128)(2,1)S(1)}, u32[]{:S(2)}, u32[]{:S(2)}) collective-permute-start(bf16[1,176,512]{2,1,0:T(8,128)(2,1)S(1)} %bitcast.77), channel_id=1, source_target_pairs={{0,8},{1,9},{2,10},{3,11},{4,12},{5,13},{6,14},{7,15},{8,0},{9,1},... | collective-permute-start | bytes 540680 | tf_op jit(solution)/shard_map/ppermute | solution.py:367
  11.1 3.6 %collective-permute-start.2 = (f32[2,3,128]{2,1,0:T(4,128)S(1)}, f32[2,3,128]{2,1,0:T(4,128)S(1)}, u32[]{:S(2)}, u32[]{:S(2)}) collective-permute-start(f32[2,3,128]{2,1,0:T(4,128)S(1)} %maximum_select_fusion.8), channel_id=1, source_target_pairs={{0,4},{1,5},{2,6},{3,7},{4,0},{5,1},{6,2},{7,3},{8,12},{9,13},{10,... | collective-permute-start | bytes 9224 | tf_op jit(solution)/shard_map/ppermute | solution.py:367
  18.6 9.4 %collective-permute-start.3 = (bf16[2,176,512]{2,1,0:T(8,128)(2,1)S(1)}, bf16[2,176,512]{2,1,0:T(8,128)(2,1)S(1)}, u32[]{:S(2)}, u32[]{:S(2)}) collective-permute-start(bf16[2,176,512]{2,1,0:T(8,128)(2,1)S(1)} %maximum_select_fusion.4), channel_id=1, source_target_pairs={{0,2},{1,5},{2,0},{3,7},{4,6},{5,1},{6,4},{7,3},{8,10},{9,13},{10,... | collective-permute-start | bytes 1081352 | tf_op jit(solution)/shard_map/ppermute | solution.py:367
  19.7 4.6 %collective-permute-start.4 = (f32[4,3,128]{2,1,0:T(4,128)S(1)}, f32[4,3,128]{2,1,0:T(4,128)S(1)}, u32[]{:S(2)}, u32[]{:S(2)}) collective-permute-start(f32[4,3,128]{2,1,0:T(4,128)S(1)} %maximum_select_fusion.7), channel_id=1, source_target_pairs={{0,8},{1,9},{2,10},{3,11},{4,12},{5,13},{6,14},{7,15},{8,0},{9,1},... | collective-permute-start | bytes 18440 | tf_op jit(solution)/shard_map/ppermute | solution.py:367
  19.8 8.1 %collective-permute-start.5 = (bf16[1,160,512]{2,1,0:T(8,128)(2,1)S(1)}, bf16[1,160,512]{2,1,0:T(8,128)(2,1)S(1)}, u32[]{:S(2)}, u32[]{:S(2)}) collective-permute-start(bf16[1,160,512]{2,1,0:T(8,128)(2,1)S(1)} %bitcast.79), channel_id=1, source_target_pairs={{0,8},{1,9},{2,10},{3,11},{4,12},{5,13},{6,14},{7,15},{8,0},{9,1},... | collective-permute-start | bytes 491528 | tf_op jit(solution)/shard_map/ppermute | solution.py:367
  24.4 1.0 copy-start.1
  25.3 0.9 copy-start.2
  26.3 0.9 copy-start.3
  28.1 17.7 %collective-permute-start.6 = (bf16[4,176,512]{2,1,0:T(8,128)(2,1)S(1)}, bf16[4,176,512]{2,1,0:T(8,128)(2,1)S(1)}, u32[]{:S(2)}, u32[]{:S(2)}) collective-permute-start(bf16[4,176,512]{2,1,0:T(8,128)(2,1)S(1)} %maximum_select_fusion.2), channel_id=1, source_target_pairs={{0,4},{1,3},{2,6},{3,1},{4,0},{5,7},{6,2},{7,5},{8,12},{9,11},{10,... | collective-permute-start | bytes 2162696 | tf_op jit(solution)/shard_map/ppermute | solution.py:367
  31.4 10.5 %collective-permute-start.7 = (bf16[2,160,512]{2,1,0:T(8,128)(2,1)S(1)}, bf16[2,160,512]{2,1,0:T(8,128)(2,1)S(1)}, u32[]{:S(2)}, u32[]{:S(2)}) collective-permute-start(bf16[2,160,512]{2,1,0:T(8,128)(2,1)S(1)} %maximum_select_fusion.5), channel_id=1, source_target_pairs={{0,2},{1,5},{2,0},{3,7},{4,6},{5,1},{6,4},{7,3},{8,10},{9,13},{10,... | collective-permute-start | bytes 983048 | tf_op jit(solution)/shard_map/ppermute | solution.py:367
  32.6 16.0 %collective-permute-start.9 = (bf16[528,128]{1,0:T(8,128)(2,1)S(1)}, bf16[528,128]{1,0:T(8,128)(2,1)S(1)}, u32[]{:S(2)}, u32[]{:S(2)}) collective-permute-start(bf16[528,128]{1,0:T(8,128)(2,1)S(1)} %get-tuple-element.88.own_ref.norm_ref), channel_id=1, source_target_pairs={{2,4},{4,2},{6,8},{8,6},{10,12},{12,10},{3,5},{5,3},{7,9},{9,7},{1... | collective-permute-start | bytes 405512 | tf_op jit(solution)/shard_map/ppermute | solution.py:425
  33.3 15.3 %collective-permute-start.8 = (bf16[528,128]{1,0:T(8,128)(2,1)S(1)}, bf16[528,128]{1,0:T(8,128)(2,1)S(1)}, u32[]{:S(2)}, u32[]{:S(2)}) collective-permute-start(bf16[528,128]{1,0:T(8,128)(2,1)S(1)} %get-tuple-element.88.own_ref.norm_ref), channel_id=1, source_target_pairs={{0,2},{1,3},{2,0},{3,1},{4,6},{5,7},{6,4},{7,5},{8,10},{9,11},{10,... | collective-permute-start | bytes 405512 | tf_op jit(solution)/shard_map/ppermute | solution.py:367
  38.0 10.6 %collective-permute-start.10 = (bf16[272,128]{1,0:T(8,128)(2,1)S(1)}, bf16[272,128]{1,0:T(8,128)(2,1)S(1)}, u32[]{:S(2)}, u32[]{:S(2)}) collective-permute-start(bf16[272,128]{1,0:T(8,128)(2,1)S(1)} %get-tuple-element.89), channel_id=1, source_target_pairs={{0,4},{1,5},{2,6},{3,7},{4,0},{5,1},{6,2},{7,3},{8,12},{9,13},{10,... | collective-permute-start | bytes 208904 | tf_op jit(solution)/shard_map/ppermute | solution.py:367
  42.0 6.6 %collective-permute-start.11 = (bf16[272,128]{1,0:T(8,128)(2,1)S(1)}, bf16[272,128]{1,0:T(8,128)(2,1)S(1)}, u32[]{:S(2)}, u32[]{:S(2)}) collective-permute-start(bf16[272,128]{1,0:T(8,128)(2,1)S(1)} %get-tuple-element.90), channel_id=1, source_target_pairs={{4,8},{8,4},{6,10},{10,6},{5,9},{9,5},{7,11},{11,7},{20,24},{24,20... | collective-permute-start | bytes 208904 | tf_op jit(solution)/shard_map/ppermute | solution.py:425
  48.6 5.2 %collective-permute-start.13 = (bf16[8,176,512]{2,1,0:T(8,128)(2,1)S(1)}, bf16[8,176,512]{2,1,0:T(8,128)(2,1)S(1)}, u32[]{:S(2)}, u32[]{:S(2)}) collective-permute-start(bf16[8,176,512]{2,1,0:T(8,128)(2,1)S(1)} %maximum_select_fusion.here_ref), channel_id=1, source_target_pairs={{0,1},{1,0},{2,3},{3,2},{4,5},{5,4},{6,7},{7,6},{8,9},{9,8},{10,11... | collective-permute-start | bytes 4325384 | tf_op jit(solution)/shard_map/ppermute | solution.py:367
  50.4 11.9 %collective-permute-start.12 = (bf16[4,160,512]{2,1,0:T(8,128)(2,1)S(1)}, bf16[4,160,512]{2,1,0:T(8,128)(2,1)S(1)}, u32[]{:S(2)}, u32[]{:S(2)}) collective-permute-start(bf16[4,160,512]{2,1,0:T(8,128)(2,1)S(1)} %maximum_select_fusion.3), channel_id=1, source_target_pairs={{0,4},{1,3},{2,6},{3,1},{4,0},{5,7},{6,2},{7,5},{8,12},{9,11},{10,... | collective-permute-start | bytes 1966088 | tf_op jit(solution)/shard_map/ppermute | solution.py:367
  62.6 3.1 %collective-permute-start.14 = (bf16[8,160,512]{2,1,0:T(8,128)(2,1)S(1)}, bf16[8,160,512]{2,1,0:T(8,128)(2,1)S(1)}, u32[]{:S(2)}, u32[]{:S(2)}) collective-permute-start(bf16[8,160,512]{2,1,0:T(8,128)(2,1)S(1)} %maximum_select_fusion.1.here_ref), channel_id=1, source_target_pairs={{0,1},{1,0},{2,3},{3,2},{4,5},{5,4},{6,7},{7,6},{8,9},{9,8},{10,11... | collective-permute-start | bytes 3932168 | tf_op jit(solution)/shard_map/ppermute | solution.py:367
  78.0 3.6 %collective-permute-start.15 = (bf16[8,168,512]{2,1,0:T(8,128)(2,1)S(1)}, bf16[8,168,512]{2,1,0:T(8,128)(2,1)S(1)}, u32[]{:S(2)}, u32[]{:S(2)}) collective-permute-start(bf16[8,168,512]{2,1,0:T(8,128)(2,1)S(1)} %get-tuple-element.106), channel_id=1, source_target_pairs={{0,1},{1,0},{2,3},{3,2},{4,5},{5,4},{6,7},{7,6},{8,9},{9,8},{10,11... | collective-permute-start | bytes 4128776 | tf_op jit(solution)/shard_map/ppermute | solution.py:367
  81.6 12.2 %collective-permute-start.17 = (bf16[8,168,512]{2,1,0:T(8,128)(2,1)S(1)}, bf16[8,168,512]{2,1,0:T(8,128)(2,1)S(1)}, u32[]{:S(2)}, u32[]{:S(2)}) collective-permute-start(bf16[8,168,512]{2,1,0:T(8,128)(2,1)S(1)} %get-tuple-element.118), channel_id=1, source_target_pairs={{0,1},{1,0},{2,3},{3,2},{4,5},{5,4},{6,7},{7,6},{8,9},{9,8},{10,11... | collective-permute-start | bytes 4128776 | tf_op jit(solution)/shard_map/ppermute | solution.py:367
  82.8 11.0 %collective-permute-start.16 = (bf16[1,2,2,168,512]{4,3,2,1,0:T(8,128)(2,1)S(1)}, bf16[1,2,2,168,512]{4,3,2,1,0:T(8,128)(2,1)S(1)}, u32[]{:S(2)}, u32[]{:S(2)}) collective-permute-start(bf16[1,2,2,168,512]{4,3,2,1,0:T(8,128)(2,1)S(1)} %bitcast.65), channel_id=1, source_target_pairs={{0,2},{1,5},{2,0},{3,7},{4,6},{5,1},{6,4},{7,3},{8,10},{9,13},{10,... | collective-permute-start | bytes 2064392 | tf_op jit(solution)/shard_map/ppermute | solution.py:367
  94.5 14.7 %collective-permute-start.19 = (bf16[1,2,2,168,512]{4,3,2,1,0:T(8,128)(2,1)S(1)}, bf16[1,2,2,168,512]{4,3,2,1,0:T(8,128)(2,1)S(1)}, u32[]{:S(2)}, u32[]{:S(2)}) collective-permute-start(bf16[1,2,2,168,512]{4,3,2,1,0:T(8,128)(2,1)S(1)} %bitcast.64), channel_id=1, source_target_pairs={{0,2},{1,5},{2,0},{3,7},{4,6},{5,1},{6,4},{7,3},{8,10},{9,13},{10,... | collective-permute-start | bytes 2064392 | tf_op jit(solution)/shard_map/ppermute | solution.py:367
  96.0 11.1 %collective-permute-start.18 = (bf16[1,1,2,168,512]{4,3,2,1,0:T(8,128)(2,1)S(1)}, bf16[1,1,2,168,512]{4,3,2,1,0:T(8,128)(2,1)S(1)}, u32[]{:S(2)}, u32[]{:S(2)}) collective-permute-start(bf16[1,1,2,168,512]{4,3,2,1,0:T(8,128)(2,1)S(1)} %bitcast.69), channel_id=1, source_target_pairs={{0,4},{1,3},{2,6},{3,1},{4,0},{5,7},{6,2},{7,5},{8,12},{9,11},{10,... | collective-permute-start | bytes 1032200 | tf_op jit(solution)/shard_map/ppermute | solution.py:367
  109.8 10.9 %collective-permute-start.21 = (bf16[1,1,2,168,512]{4,3,2,1,0:T(8,128)(2,1)S(1)}, bf16[1,1,2,168,512]{4,3,2,1,0:T(8,128)(2,1)S(1)}, u32[]{:S(2)}, u32[]{:S(2)}) collective-permute-start(bf16[1,1,2,168,512]{4,3,2,1,0:T(8,128)(2,1)S(1)} %bitcast.68), channel_id=1, source_target_pairs={{0,4},{1,3},{2,6},{3,1},{4,0},{5,7},{6,2},{7,5},{8,12},{9,11},{10,... | collective-permute-start | bytes 1032200 | tf_op jit(solution)/shard_map/ppermute | solution.py:367
  111.5 7.9 %collective-permute-start.20 = (bf16[1,1,1,168,512]{4,3,2,1,0:T(8,128)(2,1)S(1)}, bf16[1,1,1,168,512]{4,3,2,1,0:T(8,128)(2,1)S(1)}, u32[]{:S(2)}, u32[]{:S(2)}) collective-permute-start(bf16[1,1,1,168,512]{4,3,2,1,0:T(8,128)(2,1)S(1)} %bitcast.74), channel_id=1, source_target_pairs={{0,8},{1,9},{2,10},{3,11},{4,12},{5,13},{6,14},{7,15},{8,0},{9,1},... | collective-permute-start | bytes 516104 | tf_op jit(solution)/shard_map/ppermute | solution.py:367
  121.3 8.2 %collective-permute-start.22 = (bf16[1,1,1,168,512]{4,3,2,1,0:T(8,128)(2,1)S(1)}, bf16[1,1,1,168,512]{4,3,2,1,0:T(8,128)(2,1)S(1)}, u32[]{:S(2)}, u32[]{:S(2)}) collective-permute-start(bf16[1,1,1,168,512]{4,3,2,1,0:T(8,128)(2,1)S(1)} %bitcast.75), channel_id=1, source_target_pairs={{0,8},{1,9},{2,10},{3,11},{4,12},{5,13},{6,14},{7,15},{8,0},{9,1},... | collective-permute-start | bytes 516104 | tf_op jit(solution)/shard_map/ppermute | solution.py:367

commit v9 on v8

--- a/solution.py
+++ b/solution.py
@@ -82,7 +82,9 @@
         carry_ref[k : k + 1, :] = value[rows - 1 :]
 
 
-def pack_kernel(conv_ref, res_ref, in_ref, out_ref, first_ref, second_ref):
+def pack_kernel(feat_ref, forget_ref, conv_ref, res_ref, in_ref, out_ref,
+                keep_ref, mass_ref, weight_ref, carry_ref, first_ref, second_ref):
+    scan_kernel(feat_ref, forget_ref, keep_ref, mass_ref, weight_ref, carry_ref)
     conv, res, more, c = conv_ref.shape[1], res_ref.shape[1], in_ref.shape[0], first_ref.shape[1]
     for layer, ref in enumerate((first_ref, second_ref)):
         ref[:conv, :] = conv_ref[layer, :, :c]
@@ -397,7 +399,7 @@
         out_ref[p] = (one_ref[p, index].astype(F32) + two_ref[p, index].astype(F32)).astype(BF16)
 
 
-def sum_step(addends, scalars, links, dim):
+def halves_of(addends, scalars, links, dim):
     shape = addends[0].shape
     outer, rows = math.prod(shape[:dim]), math.prod(shape[dim + 1 : -1])
     flat = [v.reshape(outer, 2, rows, shape[-1]) for v in addends]
@@ -408,7 +410,12 @@
                         2 * 10**8, scalars, *flat)
         return value.reshape(shape[:dim] + (1,) + shape[dim + 1 :])
 
-    return [half(False), swap(half(True), links)]
+    return half(False), half(True)
+
+
+def sum_step(addends, scalars, links, dim):
+    kept, sent = halves_of(addends, scalars, links, dim)
+    return [kept, swap(sent, links)]
 
 
 def sum_steps():
@@ -438,17 +445,18 @@
     reach = d0 + d1
     scalars = jnp.stack([lax.axis_index("site"), lax.axis_index("tm"), lengths[0]]).astype(jnp.int32)
 
+    feat = features[0]
+    scanned = [((steps, bands), F32)] * 3 + [((3, bands), F32)]
     if aligned:
-        held0, held1 = call(pack_kernel, [((2 * conv + res + 2 * enter, c), BF16), ((2 * conv + res, c), BF16)], [], 1,
-                            w_conv, w_res, w_in, w_out, limit=FIRST_LIMIT)
+        keep, mass, weight, carry, held0, held1 = call(
+            pack_kernel, scanned + [((2 * conv + res + 2 * enter, c), BF16), ((2 * conv + res, c), BF16)], [],
+            2 * 10**9, feat, forget[0], w_conv, w_res, w_in, w_out, limit=FIRST_LIMIT)
     else:
+        keep, mass, weight, carry = call(scan_kernel, scanned, [], 2 * 10**9, feat, forget[0], limit=FIRST_LIMIT)
         out_own = jnp.concatenate([w_out[k * enter : (k + 1) * enter] for k in range(c // classes)], axis=1)
         held0, held1 = (jnp.concatenate([w_conv[k, :, :c], w_conv[k, :, c:], w_res[k]] + more)
                         for k, more in ((0, [w_in, out_own]), (1, [])))
-    held0, held1, feat, forget = together(held0[None], held1[None], features[0], forget[0])
-    block = ((steps, bands), F32)
-    keep, mass, weight, carry = call(
-        scan_kernel, [block] * 3 + [((3, bands), F32)], [], 2 * 10**9, feat, forget, limit=FIRST_LIMIT)
+    held0, held1 = held0[None], held1[None]
     carry = carry[None]
     far = [(("tm", bit),) * 2 for bit in reversed(range(2, time_bits()))]
     turns = [(NEAR, FAR), (FAR, NEAR)]
@@ -465,15 +473,18 @@
     label_rows = steps // bands
     normed, low, high = call(norm_kernel, [((LABEL_ROWS + r, bands), BF16) for r in (steps, reach - steps, reach - steps)],
                              [], 10**8,
-                     scalars, feat, keep, mass, weight, carry, labels[0].reshape(label_rows, bands))
+                     scalars, feat, keep, mass, weight, carry, labels[0].reshape(label_rows, bands), limit=FIRST_LIMIT)
     held0, normed, low, high, held1 = together(held0, normed, low, high, held1)
-    held0, held1 = grow(held0, turns[1]), grow(held1, turns[0])
+    held0 = grow(held0, turns[1])
     around = [swap(normed, (NEAR, NEAR)), exchange(normed, 1), swap(low, (FAR, FAR)), exchange(high, 2)]
     held0, held1, around = together(held0, held1, around)
-    other1 = swap(held1, turns[1])
 
     def both_cores(held):
         return held.astype(kind), swap(held, (CORE, CORE)).astype(kind)
+
+    first, held1 = both_cores(held0), grow(held1, turns[0])
+    first, held1 = together(first, held1)
+    other1 = swap(held1, turns[1])
 
     total_rows, rows0, rows1 = steps + 2 * reach, steps + d0, steps + reach
     conv_all, res_all = ((2, devices, conv, c), kind), ((devices, res, c), kind)
@@ -483,7 +494,7 @@
         [((total_rows - d0, c), BF16), ((c, classes), BF16), ((rows1 // bands, bands), F32), ((rows0, c), BF16), ((steps, c), BF16),
          ((2, rows0, c), BF16), conv_all, res_all],
         [V((total_rows, bands), BF16), V((total_rows, c), BF16), V((devices, enter, c), F32), V((devices, out, classes), F32)],
-        2 * total_rows * c * (bands + 5 * c), scalars, normed, *around, *both_cores(held0))
+        2 * total_rows * c * (bands + 5 * c), scalars, normed, *around, *first)
 
     other1, h1 = together(other1, h1)
     second = both_cores(arranged(held1, other1, turns[1]))
@@ -502,14 +513,15 @@
         shape = (2,) * time_bits() + keep.shape[1:]
         return [keep.reshape(shape), other.reshape(shape)]
 
-    sums1 = core_step(keep1, send1)
+    order = sum_steps()
+    kept1, sent1 = halves_of(core_step(keep1, send1), scalars, *order[0])
+    sent1, back0 = together(sent1, back0)
+    sums1 = [kept1, swap(sent1, order[0][0])]
     keep0, send0 = call(
         functools.partial(terms_first, sizes), package, [V((steps, c), BF16)],
         2 * steps * 9 * c * c, scalars, back0, grad1, round0, normed, h0, gated0, conv0)
-    sums1, keep0, send0 = together(sums1, keep0, send0)
-
-    order = sum_steps()
-    sums1, sums0 = sum_step(sums1, scalars, *order[0]), core_step(keep0, send0)
+
+    sums0 = core_step(keep0, send0)
     for step in range(len(order)):
         sums1, sums0 = together(sums1, sums0)
         if step + 1 < len(order):

time: 131 us -> 136 us (1.038)
  waiting for transfers between devices: 48.9 us -> 57.2 us
  local copies, waits for them, and re-layouts: 2.86 us -> 0.02 us
  other arithmetic: 1.57 us -> 3.7 us
  starting transfers between devices: 39 us -> 36.9 us
    ppermute x21, waiting for transfers between devices: 48.9 us -> 57.2 us  [swap(): return lax.ppermute(value, ('tm', 'site'), pairs)]
    unnamed x14 -> x10, local copies, waits for them, and re-layouts: 2.86 us -> 0.02 us
    ppermute x21, starting transfers between devices: 37.7 us -> 35.5 us  [swap(): return lax.ppermute(value, ('tm', 'site'), pairs)]
    select_n x9, other arithmetic: 1.5 us -> 3.12 us  [arranged(): jnp.where(my_bit(links) == 0, jnp.concatenate([held, other]), jnp.concate...]
    pallas_call x19 -> x18, Pallas kernels: 36.5 us -> 36.2 us  [call(): pl.pallas_call(kernel, out_shape=[jax.ShapeDtypeStruct(s, d) for s, d in...]
  transfers between devices with their start and end apart: 23 -> 23, of which waited for: 14 -> 16; matrix products, arithmetic and copies ran while one was open for 1% -> 2% of each run, Pallas kernels for 13% -> 11%
where the time goes in v9:
time: 136 us
  waiting for transfers between devices  57.2 us (42%)
  starting transfers between devices  36.9 us (27%)
  Pallas kernels  36.2 us (27%)
  other arithmetic  3.7 us (3%)
  between operations  1.52 us (1%)
    ppermute x21, waiting for transfers between devices, swap(): return lax.ppermute(value, ('tm', 'site'), pairs)  57.2 us
    pallas_call x18, Pallas kernels, call(): pl.pallas_call(kernel, out_shape=[jax.ShapeDtypeStruct(s, d) for s, d in...  36.2 us
    ppermute x21, starting transfers between devices, swap(): return lax.ppermute(value, ('tm', 'site'), pairs)  35.5 us
    select_n x9, other arithmetic, arranged(): jnp.where(my_bit(links) == 0, jnp.concatenate([held, other]), jnp.concate...  3.12 us
  transfers between devices with their start and end apart: 23, of which 16 were waited for; matrix products, arithmetic and copies ran while one was open for 2% of the time, Pallas kernels for 11%

profile of v9, /device:TPU:0, one launch (start us, length us, event | category | flops | bytes accessed | tf_op | source)
XLA Modules:
  0.0 135.6 jit_solution(5502536797353230992)
XLA Ops:
  0.6 2.7 %shard_map.119 = (f32[512,128]{1,0:T(8,128)}, f32[512,128]{1,0:T(8,128)}, f32[512,128]{1,0:T(8,128)}, f32[3,128]{1,0:T(4,128)}, bf16[176,512]{1,0:T(8,128)(2,1)}, /*index=5*/bf16[160,512]{1,0:T(8,128)(2,1)}) custom-call(f32[512,128]{1,0:T(8,128)} %bitcast.72, f32[512,128]{1,0:T(8,128)} %bitcast.81, bf16[2,64,1024]{2,1,0:T(8,128)(2,1)} %conv_ref.1, ...), custom_call_target="tpu_custom_call" | custom-call | flops 2000000000 | bytes 2000384 | tf_op jit(solution)/shard_map/pallas_call | solution.py:38
  3.3 3.0 %collective-permute-start.1 = (f32[1,3,128]{2,1,0:T(4,128)}, f32[1,3,128]{2,1,0:T(4,128)S(1)}, u32[]{:S(2)}, u32[]{:S(2)}) collective-permute-start(f32[1,3,128]{2,1,0:T(4,128)} %bitcast.79), channel_id=1, source_target_pairs={{0,2},{1,3},{2,0},{3,1},{4,6},{5,7},{6,4},{7,5},{8,10},{9,11},{10,... | collective-permute-start | bytes 4616 | tf_op jit(solution)/shard_map/ppermute | solution.py:369
  6.4 2.6 %collective-permute-start = (bf16[1,176,512]{2,1,0:T(8,128)(2,1)}, bf16[1,176,512]{2,1,0:T(8,128)(2,1)S(1)}, u32[]{:S(2)}, u32[]{:S(2)}) collective-permute-start(bf16[1,176,512]{2,1,0:T(8,128)(2,1)} %bitcast.74), channel_id=1, source_target_pairs={{0,8},{1,9},{2,10},{3,11},{4,12},{5,13},{6,14},{7,15},{8,0},{9,1},... | collective-permute-start | bytes 540680 | tf_op jit(solution)/shard_map/ppermute | solution.py:369
  9.0 0.8 maximum_select_fusion.8
  9.7 1.6 %collective-permute-start.2 = (f32[2,3,128]{2,1,0:T(4,128)S(1)}, f32[2,3,128]{2,1,0:T(4,128)S(1)}, u32[]{:S(2)}, u32[]{:S(2)}) collective-permute-start(f32[2,3,128]{2,1,0:T(4,128)S(1)} %maximum_select_fusion.8), channel_id=1, source_target_pairs={{0,4},{1,5},{2,6},{3,7},{4,0},{5,1},{6,2},{7,3},{8,12},{9,13},{10,... | collective-permute-start | bytes 9224 | tf_op jit(solution)/shard_map/ppermute | solution.py:369
  11.3 2.0 %collective-permute-done.2 = f32[2,3,128]{2,1,0:T(4,128)S(1)} collective-permute-done((f32[2,3,128]{2,1,0:T(4,128)S(1)}, f32[2,3,128]{2,1,0:T(4,128)S(1)}, u32[]{:S(2)}, u32[]{:S(2)}) %collective-permute-start.2) | collective-permute-done | bytes 3104 | tf_op jit(solution)/shard_map/ppermute | solution.py:369
  13.3 4.0 %collective-permute-done = bf16[1,176,512]{2,1,0:T(8,128)(2,1)S(1)} collective-permute-done((bf16[1,176,512]{2,1,0:T(8,128)(2,1)}, bf16[1,176,512]{2,1,0:T(8,128)(2,1)S(1)}, u32[]{:S(2)}, u32[]{:S(2)}) %collective-permute-start) | collective-permute-done | bytes 180256 | tf_op jit(solution)/shard_map/ppermute | solution.py:369
  17.3 1.1 maximum_select_fusion.4
  18.4 0.5 collective-permute-start.3
  19.6 0.1 collective-permute-start.4
  19.7 2.9 %collective-permute-start.5 = (bf16[1,160,512]{2,1,0:T(8,128)(2,1)}, bf16[1,160,512]{2,1,0:T(8,128)(2,1)S(1)}, u32[]{:S(2)}, u32[]{:S(2)}) collective-permute-start(bf16[1,160,512]{2,1,0:T(8,128)(2,1)} %bitcast.76), channel_id=1, source_target_pairs={{0,8},{1,9},{2,10},{3,11},{4,12},{5,13},{6,14},{7,15},{8,0},{9,1},... | collective-permute-start | bytes 491528 | tf_op jit(solution)/shard_map/ppermute | solution.py:369
  22.6 0.6 pad_add_fusion.scalar_ref
  23.2 1.0 collective-permute-done.4
  24.2 0.6 maximum_select_fusion.6.carry_ref
  24.8 2.1 %shard_map.120 = (bf16[528,128]{1,0:T(8,128)(2,1)}, bf16[272,128]{1,0:T(8,128)(2,1)}, bf16[272,128]{1,0:T(8,128)(2,1)}) custom-call(s32[3]{0:T(128)} %pad_add_fusion.scalar_ref, f32[512,128]{1,0:T(8,128)} %bitcast.73, f32[512,128]{1,0:T(8,128)} %get-tuple-element.71.keep_ref, f32[512,128]{1,0:T(8,128)} %get-tuple-element.72.mass_ref, ...), custom_call_target="tpu_custom_call" | custom-call | flops 100000000 | bytes 1337356 | tf_op jit(solution)/shard_map/pallas_call | solution.py:38
  26.9 0.2 collective-permute-done.5
  27.1 0.1 maximum_select_fusion.2
  27.2 4.0 %collective-permute-start.6 = (bf16[4,176,512]{2,1,0:T(8,128)(2,1)S(1)}, bf16[4,176,512]{2,1,0:T(8,128)(2,1)S(1)}, u32[]{:S(2)}, u32[]{:S(2)}) collective-permute-start(bf16[4,176,512]{2,1,0:T(8,128)(2,1)S(1)} %maximum_select_fusion.2), channel_id=1, source_target_pairs={{0,4},{1,3},{2,6},{3,1},{4,0},{5,7},{6,2},{7,5},{8,12},{9,11},{10,... | collective-permute-start | bytes 2162696 | tf_op jit(solution)/shard_map/ppermute | solution.py:369
  31.3 0.8 collective-permute-start.8
  32.1 2.7 %collective-permute-start.7 = (bf16[528,128]{1,0:T(8,128)(2,1)S(1)}, bf16[528,128]{1,0:T(8,128)(2,1)S(1)}, u32[]{:S(2)}, u32[]{:S(2)}) collective-permute-start(bf16[528,128]{1,0:T(8,128)(2,1)S(1)} %copy-done.1), channel_id=1, source_target_pairs={{0,2},{1,3},{2,0},{3,1},{4,6},{5,7},{6,4},{7,5},{8,10},{9,11},{10,... | collective-permute-start | bytes 405512 | tf_op jit(solution)/shard_map/ppermute | solution.py:369
  34.8 4.4 %collective-permute-start.9 = (bf16[272,128]{1,0:T(8,128)(2,1)S(1)}, bf16[272,128]{1,0:T(8,128)(2,1)S(1)}, u32[]{:S(2)}, u32[]{:S(2)}) collective-permute-start(bf16[272,128]{1,0:T(8,128)(2,1)S(1)} %copy-done.4), channel_id=1, source_target_pairs={{0,4},{1,5},{2,6},{3,7},{4,0},{5,1},{6,2},{7,3},{8,12},{9,13},{10,... | collective-permute-start | bytes 208904 | tf_op jit(solution)/shard_map/ppermute | solution.py:369
  39.1 0.7 collective-permute-start.10
  39.8 2.9 %collective-permute-done.6 = bf16[4,176,512]{2,1,0:T(8,128)(2,1)S(1)} collective-permute-done((bf16[4,176,512]{2,1,0:T(8,128)(2,1)S(1)}, bf16[4,176,512]{2,1,0:T(8,128)(2,1)S(1)}, u32[]{:S(2)}, u32[]{:S(2)}) %collective-permute-start.6) | collective-permute-done | bytes 720928 | tf_op jit(solution)/shard_map/ppermute | solution.py:369
  42.7 0.2 maximum_select_fusion.here_ref
  43.0 2.0 %collective-permute-done.9.low_ref = bf16[272,128]{1,0:T(8,128)(2,1)S(1)} collective-permute-done((bf16[272,128]{1,0:T(8,128)(2,1)S(1)}, bf16[272,128]{1,0:T(8,128)(2,1)S(1)}, u32[]{:S(2)}, u32[]{:S(2)}) %collective-permute-start.9) | collective-permute-done | bytes 69664 | tf_op jit(solution)/shard_map/ppermute | solution.py:369
  45.0 2.0 %collective-permute-start.11 = (bf16[8,176,512]{2,1,0:T(8,128)(2,1)S(1)}, bf16[8,176,512]{2,1,0:T(8,128)(2,1)S(1)}, u32[]{:S(2)}, u32[]{:S(2)}) collective-permute-start(bf16[8,176,512]{2,1,0:T(8,128)(2,1)S(1)} %maximum_select_fusion.here_ref), channel_id=1, source_target_pairs={{0,1},{1,0},{2,3},{3,2},{4,5},{5,4},{6,7},{7,6},{8,9},{9,8},{10,11... | collective-permute-start | bytes 4325384 | tf_op jit(solution)/shard_map/ppermute | solution.py:369
  47.0 2.2 %collective-permute-start.12 = (bf16[2,160,512]{2,1,0:T(8,128)(2,1)S(1)}, bf16[2,160,512]{2,1,0:T(8,128)(2,1)S(1)}, u32[]{:S(2)}, u32[]{:S(2)}) collective-permute-start(bf16[2,160,512]{2,1,0:T(8,128)(2,1)S(1)} %maximum_select_fusion.5), channel_id=1, source_target_pairs={{0,2},{1,5},{2,0},{3,7},{4,6},{5,1},{6,4},{7,3},{8,10},{9,13},{10,... | collective-permute-start | bytes 983048 | tf_op jit(solution)/shard_map/ppermute | solution.py:369
  49.2 5.1 %collective-permute-done.12 = bf16[2,160,512]{2,1,0:T(8,128)(2,1)S(1)} collective-permute-done((bf16[2,160,512]{2,1,0:T(8,128)(2,1)S(1)}, bf16[2,160,512]{2,1,0:T(8,128)(2,1)S(1)}, u32[]{:S(2)}, u32[]{:S(2)}) %collective-permute-start.12) | collective-permute-done | bytes 327712 | tf_op jit(solution)/shard_map/ppermute | solution.py:369
  54.2 0.1 maximum_select_fusion.3
  54.3 0.1 collective-permute-start.13
  54.4 7.2 %shard_map.121 = (bf16[1792,512]{1,0:T(8,128)(2,1)S(1)}, bf16[512,128]{1,0:T(8,128)(2,1)S(1)}, f32[10,128]{1,0:T(8,128)S(1)}, bf16[768,512]{1,0:T(8,128)(2,1)S(1...) custom-call(s32[3]{0:T(128)S(1)} %copy-done, ...), custom_call_target="tpu_custom_call" | custom-call | flops 5637144576 | bytes 10904588 | tf_op jit(solution)/shard_map/pallas_call | solution.py:38
  61.6 3.3 %collective-permute-done.13 = bf16[4,160,512]{2,1,0:T(8,128)(2,1)S(1)} collective-permute-done((bf16[4,160,512]{2,1,0:T(8,128)(2,1)S(1)}, bf16[4,160,512]{2,1,0:T(8,128)(2,1)S(1)}, u32[]{:S(2)}, u32[]{:S(2)}) %collective-permute-start.13) | collective-permute-done | bytes 655392 | tf_op jit(solution)/shard_map/ppermute | solution.py:369
  65.0 0.2 maximum_select_fusion.1.here_ref
  65.3 3.0 %collective-permute-done.14.there_ref = bf16[8,160,512]{2,1,0:T(8,128)(2,1)S(1)} collective-permute-done((bf16[8,160,512]{2,1,0:T(8,128)(2,1)S(1)}, bf16[8,160,512]{2,1,0:T(8,128)(2,1)S(1)}, u32[]{:S(2)}, u32[]{:S(2)}) %collective-permute-start.14) | collective-permute-done | bytes 1310752 | tf_op jit(solution)/shard_map/ppermute | solution.py:369
  68.3 12.3 %shard_map.122 = (f32[4,128]{1,0:T(4,128)}, bf16[8,168,512]{2,1,0:T(8,128)(2,1)S(1)}, bf16[8,168,512]{2,1,0:T(8,128)(2,1)S(1)}, f32[512,512]{1,0:T(8,128)S(1)}, ...) custom-call(s32[3]{0:T(128)S(1)} %copy-done, bf16[1792,512]{1,0:T(8,128)(2,1)S(1)} %get-tuple-element.94.h1_ref, ...), custom_call_target="tpu_custom_call" | custom-call | flops 7381975040 | bytes 12590092 | tf_op jit(solution)/shard_map/pallas_call | solution.py:38
  80.6 0.2 collective-permute-start.15
  80.8 3.0 %collective-permute-done.15 = bf16[8,168,512]{2,1,0:T(8,128)(2,1)S(1)} collective-permute-done((bf16[8,168,512]{2,1,0:T(8,128)(2,1)S(1)}, bf16[8,168,512]{2,1,0:T(8,128)(2,1)S(1)}, u32[]{:S(2)}, u32[]{:S(2)}) %collective-permute-start.15) | collective-permute-done | bytes 1376288 | tf_op jit(solution)/shard_map/ppermute | solution.py:369
  83.8 0.7 shard_map.124
  84.5 3.3 %shard_map.125 = (bf16[8,168,512]{2,1,0:T(8,128)(2,1)S(1)}, bf16[8,168,512]{2,1,0:T(8,128)(2,1)S(1)}) custom-call(s32[3]{0:T(128)S(1)} %copy-done, bf16[768,1024]{1,0:T(8,128)(2,1)S(1)} %get-tuple-element.105.back_ref, f32[512,512]{1,0:T(8,128)S(1)} %get-tuple-element.106.grad_ref, bf16[512,512]{1,0:T(8,128)(2,1)S(1)} %get-tuple-element.107.round_ref, ...), custom_call_target="tpu_custom_call" | custom-call | flops 2415919104 | bytes 9441292 | tf_op jit(solution)/shard_map/pallas_call | solution.py:38
  87.9 0.2 collective-permute-start.17
  88.1 2.0 %collective-permute-start.16 = (bf16[1,2,2,168,512]{4,3,2,1,0:T(8,128)(2,1)S(1)}, bf16[1,2,2,168,512]{4,3,2,1,0:T(8,128)(2,1)S(1)}, u32[]{:S(2)}, u32[]{:S(2)}) collective-permute-start(bf16[1,2,2,168,512]{4,3,2,1,0:T(8,128)(2,1)S(1)} %bitcast.62), channel_id=1, source_target_pairs={{0,2},{1,5},{2,0},{3,7},{4,6},{5,1},{6,4},{7,3},{8,10},{9,13},{10,... | collective-permute-start | bytes 2064392 | tf_op jit(solution)/shard_map/ppermute | solution.py:369
  90.1 0.7 shard_map.123
  90.8 8.2 %collective-permute-done.16 = bf16[1,2,2,168,512]{4,3,2,1,0:T(8,128)(2,1)S(1)} collective-permute-done((bf16[1,2,2,168,512]{4,3,2,1,0:T(8,128)(2,1)S(1)}, bf16[1,2,2,168,512]{4,3,2,1,0:T(8,128)(2,1)S(1)}, u32[]{:S(2)}, u32[]{:S(2)}) %collective-permute-start.16) | collective-permute-done | bytes 688160 | tf_op jit(solution)/shard_map/ppermute | solution.py:369
  99.0 0.7 shard_map.129
  99.7 2.1 %collective-permute-start.19 = (bf16[1,2,2,168,512]{4,3,2,1,0:T(8,128)(2,1)S(1)}, bf16[1,2,2,168,512]{4,3,2,1,0:T(8,128)(2,1)S(1)}, u32[]{:S(2)}, u32[]{:S(2)}) collective-permute-start(bf16[1,2,2,168,512]{4,3,2,1,0:T(8,128)(2,1)S(1)} %bitcast.63), channel_id=1, source_target_pairs={{0,2},{1,5},{2,0},{3,7},{4,6},{5,1},{6,4},{7,3},{8,10},{9,13},{10,... | collective-permute-start | bytes 2064392 | tf_op jit(solution)/shard_map/ppermute | solution.py:369
  101.8 0.6 shard_map.127
  102.5 0.1 collective-permute-start.18
  102.5 0.6 shard_map.126
  103.2 0.7 shard_map.128
  103.9 9.1 %collective-permute-done.18 = bf16[1,1,2,168,512]{4,3,2,1,0:T(8,128)(2,1)S(1)} collective-permute-done((bf16[1,1,2,168,512]{4,3,2,1,0:T(8,128)(2,1)S(1)}, bf16[1,1,2,168,512]{4,3,2,1,0:T(8,128)(2,1)S(1)}, u32[]{:S(2)}, u32[]{:S(2)}) %collective-permute-start.18) | collective-permute-done | bytes 344096 | tf_op jit(solution)/shard_map/ppermute | solution.py:369
  113.0 1.0 collective-permute-done.19
  114.0 0.6 shard_map.133
  114.6 0.5 collective-permute-start.21
  115.1 0.6 shard_map.131
  115.7 2.7 %collective-permute-start.20 = (bf16[1,1,1,168,512]{4,3,2,1,0:T(8,128)(2,1)S(1)}, bf16[1,1,1,168,512]{4,3,2,1,0:T(8,128)(2,1)S(1)}, u32[]{:S(2)}, u32[]{:S(2)}) collective-permute-start(bf16[1,1,1,168,512]{4,3,2,1,0:T(8,128)(2,1)S(1)} %bitcast.70), channel_id=1, source_target_pairs={{0,8},{1,9},{2,10},{3,11},{4,12},{5,13},{6,14},{7,15},{8,0},{9,1},... | collective-permute-start | bytes 516104 | tf_op jit(solution)/shard_map/ppermute | solution.py:369
  118.5 0.6 shard_map.130
  119.1 0.6 shard_map.132
  119.7 5.3 %collective-permute-done.20 = bf16[1,1,1,168,512]{4,3,2,1,0:T(8,128)(2,1)S(1)} collective-permute-done((bf16[1,1,1,168,512]{4,3,2,1,0:T(8,128)(2,1)S(1)}, bf16[1,1,1,168,512]{4,3,2,1,0:T(8,128)(2,1)S(1)}, u32[]{:S(2)}, u32[]{:S(2)}) %collective-permute-start.20) | collective-permute-done | bytes 172064 | tf_op jit(solution)/shard_map/ppermute | solution.py:369
  125.0 0.6 collective-permute-done.21
  125.6 0.6 shard_map.135
  126.2 1.5 %collective-permute-start.22 = (bf16[1,1,1,168,512]{4,3,2,1,0:T(8,128)(2,1)S(1)}, bf16[1,1,1,168,512]{4,3,2,1,0:T(8,128)(2,1)S(1)}, u32[]{:S(2)}, u32[]{:S(2)}) collective-permute-start(bf16[1,1,1,168,512]{4,3,2,1,0:T(8,128)(2,1)S(1)} %bitcast.71), channel_id=1, source_target_pairs={{0,8},{1,9},{2,10},{3,11},{4,12},{5,13},{6,14},{7,15},{8,0},{9,1},... | collective-permute-start | bytes 516104 | tf_op jit(solution)/shard_map/ppermute | solution.py:369
  127.7 0.6 shard_map.134
  128.3 6.4 %collective-permute-done.22 = bf16[1,1,1,168,512]{4,3,2,1,0:T(8,128)(2,1)S(1)} collective-permute-done((bf16[1,1,1,168,512]{4,3,2,1,0:T(8,128)(2,1)S(1)}, bf16[1,1,1,168,512]{4,3,2,1,0:T(8,128)(2,1)S(1)}, u32[]{:S(2)}, u32[]{:S(2)}) %collective-permute-start.22) | collective-permute-done | bytes 172064 | tf_op jit(solution)/shard_map/ppermute | solution.py:369
  134.7 0.9 shard_map.136
  (20 shorter events, 0.1 us)
Async XLA Ops:
  3.3 23.7 %copy-start.2 = (bf16[160,512]{1,0:T(8,128)(2,1)S(1)}, bf16[160,512]{1,0:T(8,128)(2,1)}, u32[]{:S(2)}) copy-start(bf16[160,512]{1,0:T(8,128)(2,1)} %get-tuple-element.69) | copy-start | bytes 491524
  3.3 5.6 %collective-permute-start.1 = (f32[1,3,128]{2,1,0:T(4,128)}, f32[1,3,128]{2,1,0:T(4,128)S(1)}, u32[]{:S(2)}, u32[]{:S(2)}) collective-permute-start(f32[1,3,128]{2,1,0:T(4,128)} %bitcast.79), channel_id=1, source_target_pairs={{0,2},{1,3},{2,0},{3,1},{4,6},{5,7},{6,4},{7,5},{8,10},{9,11},{10,... | collective-permute-start | bytes 4616 | tf_op jit(solution)/shard_map/ppermute | solution.py:369
  6.4 11.0 %collective-permute-start = (bf16[1,176,512]{2,1,0:T(8,128)(2,1)}, bf16[1,176,512]{2,1,0:T(8,128)(2,1)S(1)}, u32[]{:S(2)}, u32[]{:S(2)}) collective-permute-start(bf16[1,176,512]{2,1,0:T(8,128)(2,1)} %bitcast.74), channel_id=1, source_target_pairs={{0,8},{1,9},{2,10},{3,11},{4,12},{5,13},{6,14},{7,15},{8,0},{9,1},... | collective-permute-start | bytes 540680 | tf_op jit(solution)/shard_map/ppermute | solution.py:369
  9.7 3.6 %collective-permute-start.2 = (f32[2,3,128]{2,1,0:T(4,128)S(1)}, f32[2,3,128]{2,1,0:T(4,128)S(1)}, u32[]{:S(2)}, u32[]{:S(2)}) collective-permute-start(f32[2,3,128]{2,1,0:T(4,128)S(1)} %maximum_select_fusion.8), channel_id=1, source_target_pairs={{0,4},{1,5},{2,6},{3,7},{4,0},{5,1},{6,2},{7,3},{8,12},{9,13},{10,... | collective-permute-start | bytes 9224 | tf_op jit(solution)/shard_map/ppermute | solution.py:369
  18.4 8.7 %collective-permute-start.3 = (bf16[2,176,512]{2,1,0:T(8,128)(2,1)S(1)}, bf16[2,176,512]{2,1,0:T(8,128)(2,1)S(1)}, u32[]{:S(2)}, u32[]{:S(2)}) collective-permute-start(bf16[2,176,512]{2,1,0:T(8,128)(2,1)S(1)} %maximum_select_fusion.4), channel_id=1, source_target_pairs={{0,2},{1,5},{2,0},{3,7},{4,6},{5,1},{6,4},{7,3},{8,10},{9,13},{10,... | collective-permute-start | bytes 1081352 | tf_op jit(solution)/shard_map/ppermute | solution.py:369
  19.6 4.6 %collective-permute-start.4 = (f32[4,3,128]{2,1,0:T(4,128)S(1)}, f32[4,3,128]{2,1,0:T(4,128)S(1)}, u32[]{:S(2)}, u32[]{:S(2)}) collective-permute-start(f32[4,3,128]{2,1,0:T(4,128)S(1)} %maximum_select_fusion.7), channel_id=1, source_target_pairs={{0,8},{1,9},{2,10},{3,11},{4,12},{5,13},{6,14},{7,15},{8,0},{9,1},... | collective-permute-start | bytes 18440 | tf_op jit(solution)/shard_map/ppermute | solution.py:369
  19.7 7.4 %collective-permute-start.5 = (bf16[1,160,512]{2,1,0:T(8,128)(2,1)}, bf16[1,160,512]{2,1,0:T(8,128)(2,1)S(1)}, u32[]{:S(2)}, u32[]{:S(2)}) collective-permute-start(bf16[1,160,512]{2,1,0:T(8,128)(2,1)} %bitcast.76), channel_id=1, source_target_pairs={{0,8},{1,9},{2,10},{3,11},{4,12},{5,13},{6,14},{7,15},{8,0},{9,1},... | collective-permute-start | bytes 491528 | tf_op jit(solution)/shard_map/ppermute | solution.py:369
  26.9 4.4 %copy-start.1 = (bf16[528,128]{1,0:T(8,128)(2,1)S(1)}, bf16[528,128]{1,0:T(8,128)(2,1)}, u32[]{:S(2)}) copy-start(bf16[528,128]{1,0:T(8,128)(2,1)} %get-tuple-element.81.own_ref.norm_ref) | copy-start | bytes 405508
  26.9 7.9 %copy-start.4 = (bf16[272,128]{1,0:T(8,128)(2,1)S(1)}, bf16[272,128]{1,0:T(8,128)(2,1)}, u32[]{:S(2)}) copy-start(bf16[272,128]{1,0:T(8,128)(2,1)} %get-tuple-element.82) | copy-start | bytes 208900
  26.9 12.3 %copy-start.3 = (bf16[272,128]{1,0:T(8,128)(2,1)S(1)}, bf16[272,128]{1,0:T(8,128)(2,1)}, u32[]{:S(2)}) copy-start(bf16[272,128]{1,0:T(8,128)(2,1)} %get-tuple-element.83) | copy-start | bytes 208900
  27.2 15.5 %collective-permute-start.6 = (bf16[4,176,512]{2,1,0:T(8,128)(2,1)S(1)}, bf16[4,176,512]{2,1,0:T(8,128)(2,1)S(1)}, u32[]{:S(2)}, u32[]{:S(2)}) collective-permute-start(bf16[4,176,512]{2,1,0:T(8,128)(2,1)S(1)} %maximum_select_fusion.2), channel_id=1, source_target_pairs={{0,4},{1,3},{2,6},{3,1},{4,0},{5,7},{6,2},{7,5},{8,12},{9,11},{10,... | collective-permute-start | bytes 2162696 | tf_op jit(solution)/shard_map/ppermute | solution.py:369
  31.3 23.1 %copy-start = (s32[3]{0:T(128)S(1)}, s32[3]{0:T(128)}, u32[]{:S(2)}) copy-start(s32[3]{0:T(128)} %pad_add_fusion.scalar_ref) | copy-start | bytes 40
  31.3 13.7 %collective-permute-start.8 = (bf16[528,128]{1,0:T(8,128)(2,1)S(1)}, bf16[528,128]{1,0:T(8,128)(2,1)S(1)}, u32[]{:S(2)}, u32[]{:S(2)}) collective-permute-start(bf16[528,128]{1,0:T(8,128)(2,1)S(1)} %copy-done.1), channel_id=1, source_target_pairs={{2,4},{4,2},{6,8},{8,6},{10,12},{12,10},{3,5},{5,3},{7,9},{9,7},{1... | collective-permute-start | bytes 405512 | tf_op jit(solution)/shard_map/ppermute | solution.py:432
  32.1 12.9 %collective-permute-start.7 = (bf16[528,128]{1,0:T(8,128)(2,1)S(1)}, bf16[528,128]{1,0:T(8,128)(2,1)S(1)}, u32[]{:S(2)}, u32[]{:S(2)}) collective-permute-start(bf16[528,128]{1,0:T(8,128)(2,1)S(1)} %copy-done.1), channel_id=1, source_target_pairs={{0,2},{1,3},{2,0},{3,1},{4,6},{5,7},{6,4},{7,5},{8,10},{9,11},{10,... | collective-permute-start | bytes 405512 | tf_op jit(solution)/shard_map/ppermute | solution.py:369
  34.8 10.2 %collective-permute-start.9 = (bf16[272,128]{1,0:T(8,128)(2,1)S(1)}, bf16[272,128]{1,0:T(8,128)(2,1)S(1)}, u32[]{:S(2)}, u32[]{:S(2)}) collective-permute-start(bf16[272,128]{1,0:T(8,128)(2,1)S(1)} %copy-done.4), channel_id=1, source_target_pairs={{0,4},{1,5},{2,6},{3,7},{4,0},{5,1},{6,2},{7,3},{8,12},{9,13},{10,... | collective-permute-start | bytes 208904 | tf_op jit(solution)/shard_map/ppermute | solution.py:369
  39.1 5.8 %collective-permute-start.10 = (bf16[272,128]{1,0:T(8,128)(2,1)S(1)}, bf16[272,128]{1,0:T(8,128)(2,1)S(1)}, u32[]{:S(2)}, u32[]{:S(2)}) collective-permute-start(bf16[272,128]{1,0:T(8,128)(2,1)S(1)} %copy-done.3), channel_id=1, source_target_pairs={{4,8},{8,4},{6,10},{10,6},{5,9},{9,5},{7,11},{11,7},{20,24},{24,20... | collective-permute-start | bytes 208904 | tf_op jit(solution)/shard_map/ppermute | solution.py:432
  45.0 9.3 %collective-permute-start.11 = (bf16[8,176,512]{2,1,0:T(8,128)(2,1)S(1)}, bf16[8,176,512]{2,1,0:T(8,128)(2,1)S(1)}, u32[]{:S(2)}, u32[]{:S(2)}) collective-permute-start(bf16[8,176,512]{2,1,0:T(8,128)(2,1)S(1)} %maximum_select_fusion.here_ref), channel_id=1, source_target_pairs={{0,1},{1,0},{2,3},{3,2},{4,5},{5,4},{6,7},{7,6},{8,9},{9,8},{10,11... | collective-permute-start | bytes 4325384 | tf_op jit(solution)/shard_map/ppermute | solution.py:369
  47.0 7.2 %collective-permute-start.12 = (bf16[2,160,512]{2,1,0:T(8,128)(2,1)S(1)}, bf16[2,160,512]{2,1,0:T(8,128)(2,1)S(1)}, u32[]{:S(2)}, u32[]{:S(2)}) collective-permute-start(bf16[2,160,512]{2,1,0:T(8,128)(2,1)S(1)} %maximum_select_fusion.5), channel_id=1, source_target_pairs={{0,2},{1,5},{2,0},{3,7},{4,6},{5,1},{6,4},{7,3},{8,10},{9,13},{10,... | collective-permute-start | bytes 983048 | tf_op jit(solution)/shard_map/ppermute | solution.py:369
  54.3 10.7 %collective-permute-start.13 = (bf16[4,160,512]{2,1,0:T(8,128)(2,1)S(1)}, bf16[4,160,512]{2,1,0:T(8,128)(2,1)S(1)}, u32[]{:S(2)}, u32[]{:S(2)}) collective-permute-start(bf16[4,160,512]{2,1,0:T(8,128)(2,1)S(1)} %maximum_select_fusion.3), channel_id=1, source_target_pairs={{0,4},{1,3},{2,6},{3,1},{4,0},{5,7},{6,2},{7,5},{8,12},{9,11},{10,... | collective-permute-start | bytes 1966088 | tf_op jit(solution)/shard_map/ppermute | solution.py:369
  65.2 3.1 %collective-permute-start.14 = (bf16[8,160,512]{2,1,0:T(8,128)(2,1)S(1)}, bf16[8,160,512]{2,1,0:T(8,128)(2,1)S(1)}, u32[]{:S(2)}, u32[]{:S(2)}) collective-permute-start(bf16[8,160,512]{2,1,0:T(8,128)(2,1)S(1)} %maximum_select_fusion.1.here_ref), channel_id=1, source_target_pairs={{0,1},{1,0},{2,3},{3,2},{4,5},{5,4},{6,7},{7,6},{8,9},{9,8},{10,11... | collective-permute-start | bytes 3932168 | tf_op jit(solution)/shard_map/ppermute | solution.py:369
  80.6 3.2 %collective-permute-start.15 = (bf16[8,168,512]{2,1,0:T(8,128)(2,1)S(1)}, bf16[8,168,512]{2,1,0:T(8,128)(2,1)S(1)}, u32[]{:S(2)}, u32[]{:S(2)}) collective-permute-start(bf16[8,168,512]{2,1,0:T(8,128)(2,1)S(1)} %get-tuple-element.102), channel_id=1, source_target_pairs={{0,1},{1,0},{2,3},{3,2},{4,5},{5,4},{6,7},{7,6},{8,9},{9,8},{10,11... | collective-permute-start | bytes 4128776 | tf_op jit(solution)/shard_map/ppermute | solution.py:369
  87.9 11.1 %collective-permute-start.17 = (bf16[8,168,512]{2,1,0:T(8,128)(2,1)S(1)}, bf16[8,168,512]{2,1,0:T(8,128)(2,1)S(1)}, u32[]{:S(2)}, u32[]{:S(2)}) collective-permute-start(bf16[8,168,512]{2,1,0:T(8,128)(2,1)S(1)} %get-tuple-element.112), channel_id=1, source_target_pairs={{0,1},{1,0},{2,3},{3,2},{4,5},{5,4},{6,7},{7,6},{8,9},{9,8},{10,11... | collective-permute-start | bytes 4128776 | tf_op jit(solution)/shard_map/ppermute | solution.py:369
  88.1 10.9 %collective-permute-start.16 = (bf16[1,2,2,168,512]{4,3,2,1,0:T(8,128)(2,1)S(1)}, bf16[1,2,2,168,512]{4,3,2,1,0:T(8,128)(2,1)S(1)}, u32[]{:S(2)}, u32[]{:S(2)}) collective-permute-start(bf16[1,2,2,168,512]{4,3,2,1,0:T(8,128)(2,1)S(1)} %bitcast.62), channel_id=1, source_target_pairs={{0,2},{1,5},{2,0},{3,7},{4,6},{5,1},{6,4},{7,3},{8,10},{9,13},{10,... | collective-permute-start | bytes 2064392 | tf_op jit(solution)/shard_map/ppermute | solution.py:369
  99.7 14.2 %collective-permute-start.19 = (bf16[1,2,2,168,512]{4,3,2,1,0:T(8,128)(2,1)S(1)}, bf16[1,2,2,168,512]{4,3,2,1,0:T(8,128)(2,1)S(1)}, u32[]{:S(2)}, u32[]{:S(2)}) collective-permute-start(bf16[1,2,2,168,512]{4,3,2,1,0:T(8,128)(2,1)S(1)} %bitcast.63), channel_id=1, source_target_pairs={{0,2},{1,5},{2,0},{3,7},{4,6},{5,1},{6,4},{7,3},{8,10},{9,13},{10,... | collective-permute-start | bytes 2064392 | tf_op jit(solution)/shard_map/ppermute | solution.py:369
  102.5 10.5 %collective-permute-start.18 = (bf16[1,1,2,168,512]{4,3,2,1,0:T(8,128)(2,1)S(1)}, bf16[1,1,2,168,512]{4,3,2,1,0:T(8,128)(2,1)S(1)}, u32[]{:S(2)}, u32[]{:S(2)}) collective-permute-start(bf16[1,1,2,168,512]{4,3,2,1,0:T(8,128)(2,1)S(1)} %bitcast.67), channel_id=1, source_target_pairs={{0,4},{1,3},{2,6},{3,1},{4,0},{5,7},{6,2},{7,5},{8,12},{9,11},{10,... | collective-permute-start | bytes 1032200 | tf_op jit(solution)/shard_map/ppermute | solution.py:369
  114.6 11.0 %collective-permute-start.21 = (bf16[1,1,2,168,512]{4,3,2,1,0:T(8,128)(2,1)S(1)}, bf16[1,1,2,168,512]{4,3,2,1,0:T(8,128)(2,1)S(1)}, u32[]{:S(2)}, u32[]{:S(2)}) collective-permute-start(bf16[1,1,2,168,512]{4,3,2,1,0:T(8,128)(2,1)S(1)} %bitcast.66), channel_id=1, source_target_pairs={{0,4},{1,3},{2,6},{3,1},{4,0},{5,7},{6,2},{7,5},{8,12},{9,11},{10,... | collective-permute-start | bytes 1032200 | tf_op jit(solution)/shard_map/ppermute | solution.py:369
  115.7 9.3 %collective-permute-start.20 = (bf16[1,1,1,168,512]{4,3,2,1,0:T(8,128)(2,1)S(1)}, bf16[1,1,1,168,512]{4,3,2,1,0:T(8,128)(2,1)S(1)}, u32[]{:S(2)}, u32[]{:S(2)}) collective-permute-start(bf16[1,1,1,168,512]{4,3,2,1,0:T(8,128)(2,1)S(1)} %bitcast.70), channel_id=1, source_target_pairs={{0,8},{1,9},{2,10},{3,11},{4,12},{5,13},{6,14},{7,15},{8,0},{9,1},... | collective-permute-start | bytes 516104 | tf_op jit(solution)/shard_map/ppermute | solution.py:369
  126.2 8.5 %collective-permute-start.22 = (bf16[1,1,1,168,512]{4,3,2,1,0:T(8,128)(2,1)S(1)}, bf16[1,1,1,168,512]{4,3,2,1,0:T(8,128)(2,1)S(1)}, u32[]{:S(2)}, u32[]{:S(2)}) collective-permute-start(bf16[1,1,1,168,512]{4,3,2,1,0:T(8,128)(2,1)S(1)} %bitcast.71), channel_id=1, source_target_pairs={{0,8},{1,9},{2,10},{3,11},{4,12},{5,13},{6,14},{7,15},{8,0},{9,1},... | collective-permute-start | bytes 516104 | tf_op jit(solution)/shard_map/ppermute | solution.py:369

commit v10 on v9

--- a/solution.py
+++ b/solution.py
@@ -203,20 +203,22 @@
     halo(scalar_ref, own_ref, even_ref, odd_ref, low_ref, high_ref, norm_ref, label_ref)
     w_out_ref[...] = rows_of(out_ref[...])
     w_in = rows_of(in_ref[...])
-    for i in range(rows // TILE):
-        h0_ref[tile_of(i), :] = dot(norm_ref[tile_of(i), :], w_in).astype(BF16)
+    for i in range(rows // steps):
+        at = slice(i * steps, (i + 1) * steps)
+        h0_ref[at, :] = dot(norm_ref[at, :], w_in).astype(BF16)
     kept_ref[...] = h0_ref[before : before + kept, :]
-    for i in range(h1_ref.shape[0] // TILE):
-        now = h0_ref[tile_of(i, d), :]
-        t, s = activate(h0_ref[tile_of(i), :], now, conv_ref)
+    cuts = [0, before, before + steps, before + kept, h1_ref.shape[0]]
+    for start, end in zip(cuts, cuts[1:]):
+        at = slice(start, end)
+        now = h0_ref[start + d : end + d, :]
+        t, s = activate(h0_ref[at, :], now, conv_ref)
         gated = (t * s).astype(BF16)
-        h1_ref[tile_of(i), :] = (now.astype(F32) + dot(gated, rows_of(res_ref[...]))).astype(BF16)
-        first = i * TILE - before
-        if 0 <= first < kept:
-            own = slice(first, first + TILE)
+        h1_ref[at, :] = (now.astype(F32) + dot(gated, rows_of(res_ref[...]))).astype(BF16)
+        if before <= start < before + kept:
+            own = slice(start - before, end - before)
             slope_ref[0, own, :], slope_ref[1, own, :] = (v.astype(BF16) for v in slopes(t, s))
-            if first < steps:
-                gated_ref[own, :] = gated
+            if start == before:
+                gated_ref[...] = gated
 
 
 def store_terms(core, keep_ref, send_ref, row, value, first, size, start, count, lane=0):
@@ -413,11 +415,6 @@
     return half(False), half(True)
 
 
-def sum_step(addends, scalars, links, dim):
-    kept, sent = halves_of(addends, scalars, links, dim)
-    return [kept, swap(sent, links)]
-
-
 def sum_steps():
     bits = time_bits()
     rest = [((("tm", bit),) * 2, 1 + bits - bit) for bit in range(2, bits)]
@@ -475,16 +472,14 @@
                              [], 10**8,
                      scalars, feat, keep, mass, weight, carry, labels[0].reshape(label_rows, bands), limit=FIRST_LIMIT)
     held0, normed, low, high, held1 = together(held0, normed, low, high, held1)
-    held0 = grow(held0, turns[1])
+    held0, held1 = grow(held0, turns[1]), grow(held1, turns[0])
     around = [swap(normed, (NEAR, NEAR)), exchange(normed, 1), swap(low, (FAR, FAR)), exchange(high, 2)]
     held0, held1, around = together(held0, held1, around)
 
     def both_cores(held):
         return held.astype(kind), swap(held, (CORE, CORE)).astype(kind)
 
-    first, held1 = both_cores(held0), grow(held1, turns[0])
-    first, held1 = together(first, held1)
-    other1 = swap(held1, turns[1])
+    first, other1 = both_cores(held0), swap(held1, turns[1])
 
     total_rows, rows0, rows1 = steps + 2 * reach, steps + d0, steps + reach
     conv_all, res_all = ((2, devices, conv, c), kind), ((devices, res, c), kind)
@@ -513,20 +508,23 @@
         shape = (2,) * time_bits() + keep.shape[1:]
         return [keep.reshape(shape), other.reshape(shape)]
 
-    order = sum_steps()
-    kept1, sent1 = halves_of(core_step(keep1, send1), scalars, *order[0])
-    sent1, back0 = together(sent1, back0)
-    sums1 = [kept1, swap(sent1, order[0][0])]
+    sums1 = core_step(keep1, send1)
     keep0, send0 = call(
         functools.partial(terms_first, sizes), package, [V((steps, c), BF16)],
         2 * steps * 9 * c * c, scalars, back0, grad1, round0, normed, h0, gated0, conv0)
-
-    sums0 = core_step(keep0, send0)
-    for step in range(len(order)):
-        sums1, sums0 = together(sums1, sums0)
-        if step + 1 < len(order):
-            sums1 = sum_step(sums1, scalars, *order[step + 1])
-        sums0 = sum_step(sums0, scalars, *order[step])
+    sums1, keep0, send0 = together(sums1, keep0, send0)
+
+    order = sum_steps()
+    kept1, sent1 = halves_of(sums1, scalars, *order[0])
+    sums1, sums0 = [kept1, swap(sent1, order[0][0])], core_step(keep0, send0)
+    for step, (links, dim) in enumerate(order):
+        more = step + 1 < len(order)
+        kept0, sent0 = halves_of(sums0, scalars, links, dim)
+        if more:
+            kept1, sent1 = halves_of(sums1, scalars, *order[step + 1])
+            sent1, sent0 = together(sent1, sent0)
+            sums1 = [kept1, swap(sent1, order[step + 1][0])]
+        sums0 = [kept0, swap(sent0, links)]
     rows = 2 * conv + res + enter
     parts = [v.reshape(rows, c) for v in sums0 + sums1]
     grad_conv, grad_res, grad_in, grad_out = call(

time: 136 us -> 130 us (0.956)
  waiting for transfers between devices: 57.2 us -> 51.1 us
    ppermute x21, waiting for transfers between devices: 57.2 us -> 51.1 us  [swap(): return lax.ppermute(value, ('tm', 'site'), pairs)]
  transfers between devices with their start and end apart: 23 -> 23, of which waited for: 16 -> 14; matrix products, arithmetic and copies ran while one was open for 2% -> 2% of each run, Pallas kernels for 11% -> 14%
where the time goes in v10:
time: 130 us
  waiting for transfers between devices  51.1 us (39%)
  starting transfers between devices  37.9 us (29%)
  Pallas kernels  35.6 us (27%)
  other arithmetic  3.7 us (3%)
  between operations  1.53 us (1%)
    ppermute x21, waiting for transfers between devices, swap(): return lax.ppermute(value, ('tm', 'site'), pairs)  51.1 us
    ppermute x21, starting transfers between devices, swap(): return lax.ppermute(value, ('tm', 'site'), pairs)  36.4 us
    pallas_call x18, Pallas kernels, call(): pl.pallas_call(kernel, out_shape=[jax.ShapeDtypeStruct(s, d) for s, d in...  35.6 us
    select_n x9, other arithmetic, arranged(): jnp.where(my_bit(links) == 0, jnp.concatenate([held, other]), jnp.concate...  3.12 us
  transfers between devices with their start and end apart: 23, of which 14 were waited for; matrix products, arithmetic and copies ran while one was open for 2% of the time, Pallas kernels for 14%

profile of v10, /device:TPU:0, one launch (start us, length us, event | category | flops | bytes accessed | tf_op | source)
XLA Modules:
  0.0 129.9 jit_solution(143557576809481804)
XLA Ops:
  0.6 2.7 %shard_map.119 = (f32[512,128]{1,0:T(8,128)}, f32[512,128]{1,0:T(8,128)}, f32[512,128]{1,0:T(8,128)}, f32[3,128]{1,0:T(4,128)}, bf16[176,512]{1,0:T(8,128)(2,1)}, /*index=5*/bf16[160,512]{1,0:T(8,128)(2,1)}) custom-call(f32[512,128]{1,0:T(8,128)} %bitcast.67, f32[512,128]{1,0:T(8,128)} %bitcast.76, bf16[2,64,1024]{2,1,0:T(8,128)(2,1)} %conv_ref.1, ...), custom_call_target="tpu_custom_call" | custom-call | flops 2000000000 | bytes 2000384 | tf_op jit(solution)/shard_map/pallas_call | solution.py:38
  3.3 3.0 %collective-permute-start.1 = (f32[1,3,128]{2,1,0:T(4,128)}, f32[1,3,128]{2,1,0:T(4,128)S(1)}, u32[]{:S(2)}, u32[]{:S(2)}) collective-permute-start(f32[1,3,128]{2,1,0:T(4,128)} %bitcast.74), channel_id=1, source_target_pairs={{0,2},{1,3},{2,0},{3,1},{4,6},{5,7},{6,4},{7,5},{8,10},{9,11},{10,... | collective-permute-start | bytes 4616 | tf_op jit(solution)/shard_map/ppermute | solution.py:371
  6.4 2.6 %collective-permute-start = (bf16[1,176,512]{2,1,0:T(8,128)(2,1)}, bf16[1,176,512]{2,1,0:T(8,128)(2,1)S(1)}, u32[]{:S(2)}, u32[]{:S(2)}) collective-permute-start(bf16[1,176,512]{2,1,0:T(8,128)(2,1)} %bitcast.69), channel_id=1, source_target_pairs={{0,8},{1,9},{2,10},{3,11},{4,12},{5,13},{6,14},{7,15},{8,0},{9,1},... | collective-permute-start | bytes 540680 | tf_op jit(solution)/shard_map/ppermute | solution.py:371
  9.0 0.8 maximum_select_fusion.8
  9.7 1.6 %collective-permute-start.2 = (f32[2,3,128]{2,1,0:T(4,128)S(1)}, f32[2,3,128]{2,1,0:T(4,128)S(1)}, u32[]{:S(2)}, u32[]{:S(2)}) collective-permute-start(f32[2,3,128]{2,1,0:T(4,128)S(1)} %maximum_select_fusion.8), channel_id=1, source_target_pairs={{0,4},{1,5},{2,6},{3,7},{4,0},{5,1},{6,2},{7,3},{8,12},{9,13},{10,... | collective-permute-start | bytes 9224 | tf_op jit(solution)/shard_map/ppermute | solution.py:371
  11.3 2.0 %collective-permute-done.2 = f32[2,3,128]{2,1,0:T(4,128)S(1)} collective-permute-done((f32[2,3,128]{2,1,0:T(4,128)S(1)}, f32[2,3,128]{2,1,0:T(4,128)S(1)}, u32[]{:S(2)}, u32[]{:S(2)}) %collective-permute-start.2) | collective-permute-done | bytes 3104 | tf_op jit(solution)/shard_map/ppermute | solution.py:371
  13.3 4.0 %collective-permute-done = bf16[1,176,512]{2,1,0:T(8,128)(2,1)S(1)} collective-permute-done((bf16[1,176,512]{2,1,0:T(8,128)(2,1)}, bf16[1,176,512]{2,1,0:T(8,128)(2,1)S(1)}, u32[]{:S(2)}, u32[]{:S(2)}) %collective-permute-start) | collective-permute-done | bytes 180256 | tf_op jit(solution)/shard_map/ppermute | solution.py:371
  17.3 1.1 maximum_select_fusion.4
  18.4 0.5 collective-permute-start.3
  19.6 0.1 collective-permute-start.4
  19.7 2.9 %collective-permute-start.5 = (bf16[1,160,512]{2,1,0:T(8,128)(2,1)}, bf16[1,160,512]{2,1,0:T(8,128)(2,1)S(1)}, u32[]{:S(2)}, u32[]{:S(2)}) collective-permute-start(bf16[1,160,512]{2,1,0:T(8,128)(2,1)} %bitcast.71), channel_id=1, source_target_pairs={{0,8},{1,9},{2,10},{3,11},{4,12},{5,13},{6,14},{7,15},{8,0},{9,1},... | collective-permute-start | bytes 491528 | tf_op jit(solution)/shard_map/ppermute | solution.py:371
  22.6 0.6 pad_add_fusion.scalar_ref
  23.2 1.0 collective-permute-done.4
  24.2 0.6 maximum_select_fusion.6.carry_ref
  24.8 2.1 %shard_map.120 = (bf16[528,128]{1,0:T(8,128)(2,1)}, bf16[272,128]{1,0:T(8,128)(2,1)}, bf16[272,128]{1,0:T(8,128)(2,1)}) custom-call(s32[3]{0:T(128)} %pad_add_fusion.scalar_ref, f32[512,128]{1,0:T(8,128)} %bitcast.68, f32[512,128]{1,0:T(8,128)} %get-tuple-element.62.keep_ref, f32[512,128]{1,0:T(8,128)} %get-tuple-element.63.mass_ref, ...), custom_call_target="tpu_custom_call" | custom-call | flops 100000000 | bytes 1337356 | tf_op jit(solution)/shard_map/pallas_call | solution.py:38
  26.9 0.2 collective-permute-done.5
  27.1 0.1 maximum_select_fusion.2
  27.2 4.0 %collective-permute-start.6 = (bf16[4,176,512]{2,1,0:T(8,128)(2,1)S(1)}, bf16[4,176,512]{2,1,0:T(8,128)(2,1)S(1)}, u32[]{:S(2)}, u32[]{:S(2)}) collective-permute-start(bf16[4,176,512]{2,1,0:T(8,128)(2,1)S(1)} %maximum_select_fusion.2), channel_id=1, source_target_pairs={{0,4},{1,3},{2,6},{3,1},{4,0},{5,7},{6,2},{7,5},{8,12},{9,11},{10,... | collective-permute-start | bytes 2162696 | tf_op jit(solution)/shard_map/ppermute | solution.py:371
  31.3 1.4 %collective-permute-start.7 = (bf16[2,160,512]{2,1,0:T(8,128)(2,1)S(1)}, bf16[2,160,512]{2,1,0:T(8,128)(2,1)S(1)}, u32[]{:S(2)}, u32[]{:S(2)}) collective-permute-start(bf16[2,160,512]{2,1,0:T(8,128)(2,1)S(1)} %maximum_select_fusion.5), channel_id=1, source_target_pairs={{0,2},{1,5},{2,0},{3,7},{4,6},{5,1},{6,4},{7,3},{8,10},{9,13},{10,... | collective-permute-start | bytes 983048 | tf_op jit(solution)/shard_map/ppermute | solution.py:371
  32.6 0.7 collective-permute-start.9
  33.3 4.7 %collective-permute-start.8 = (bf16[528,128]{1,0:T(8,128)(2,1)S(1)}, bf16[528,128]{1,0:T(8,128)(2,1)S(1)}, u32[]{:S(2)}, u32[]{:S(2)}) collective-permute-start(bf16[528,128]{1,0:T(8,128)(2,1)S(1)} %copy-done.1), channel_id=1, source_target_pairs={{0,2},{1,3},{2,0},{3,1},{4,6},{5,7},{6,4},{7,5},{8,10},{9,11},{10,... | collective-permute-start | bytes 405512 | tf_op jit(solution)/shard_map/ppermute | solution.py:371
  38.0 1.6 %collective-permute-start.10 = (bf16[272,128]{1,0:T(8,128)(2,1)S(1)}, bf16[272,128]{1,0:T(8,128)(2,1)S(1)}, u32[]{:S(2)}, u32[]{:S(2)}) collective-permute-start(bf16[272,128]{1,0:T(8,128)(2,1)S(1)} %copy-done.4), channel_id=1, source_target_pairs={{0,4},{1,5},{2,6},{3,7},{4,0},{5,1},{6,2},{7,3},{8,12},{9,13},{10,... | collective-permute-start | bytes 208904 | tf_op jit(solution)/shard_map/ppermute | solution.py:371
  39.6 2.2 %collective-permute-done.7 = bf16[2,160,512]{2,1,0:T(8,128)(2,1)S(1)} collective-permute-done((bf16[2,160,512]{2,1,0:T(8,128)(2,1)S(1)}, bf16[2,160,512]{2,1,0:T(8,128)(2,1)S(1)}, u32[]{:S(2)}, u32[]{:S(2)}) %collective-permute-start.7) | collective-permute-done | bytes 327712 | tf_op jit(solution)/shard_map/ppermute | solution.py:371
  41.8 0.8 collective-permute-start.11
  42.6 0.1 maximum_select_fusion.3
  42.7 0.0 copy-start
  42.8 2.7 %collective-permute-done.6 = bf16[4,176,512]{2,1,0:T(8,128)(2,1)S(1)} collective-permute-done((bf16[4,176,512]{2,1,0:T(8,128)(2,1)S(1)}, bf16[4,176,512]{2,1,0:T(8,128)(2,1)S(1)}, u32[]{:S(2)}, u32[]{:S(2)}) %collective-permute-start.6) | collective-permute-done | bytes 720928 | tf_op jit(solution)/shard_map/ppermute | solution.py:371
  45.5 0.2 maximum_select_fusion.here_ref
  45.7 2.7 %collective-permute-done.10.low_ref = bf16[272,128]{1,0:T(8,128)(2,1)S(1)} collective-permute-done((bf16[272,128]{1,0:T(8,128)(2,1)S(1)}, bf16[272,128]{1,0:T(8,128)(2,1)S(1)}, u32[]{:S(2)}, u32[]{:S(2)}) %collective-permute-start.10) | collective-permute-done | bytes 69664 | tf_op jit(solution)/shard_map/ppermute | solution.py:371
  48.5 2.0 %collective-permute-start.13 = (bf16[8,176,512]{2,1,0:T(8,128)(2,1)S(1)}, bf16[8,176,512]{2,1,0:T(8,128)(2,1)S(1)}, u32[]{:S(2)}, u32[]{:S(2)}) collective-permute-start(bf16[8,176,512]{2,1,0:T(8,128)(2,1)S(1)} %maximum_select_fusion.here_ref), channel_id=1, source_target_pairs={{0,1},{1,0},{2,3},{3,2},{4,5},{5,4},{6,7},{7,6},{8,9},{9,8},{10,11... | collective-permute-start | bytes 4325384 | tf_op jit(solution)/shard_map/ppermute | solution.py:371
  50.5 2.9 %collective-permute-start.12 = (bf16[4,160,512]{2,1,0:T(8,128)(2,1)S(1)}, bf16[4,160,512]{2,1,0:T(8,128)(2,1)S(1)}, u32[]{:S(2)}, u32[]{:S(2)}) collective-permute-start(bf16[4,160,512]{2,1,0:T(8,128)(2,1)S(1)} %maximum_select_fusion.3), channel_id=1, source_target_pairs={{0,4},{1,3},{2,6},{3,1},{4,0},{5,7},{6,2},{7,5},{8,12},{9,11},{10,... | collective-permute-start | bytes 1966088 | tf_op jit(solution)/shard_map/ppermute | solution.py:371
  53.4 6.5 %shard_map.121 = (bf16[1792,512]{1,0:T(8,128)(2,1)S(1)}, bf16[512,128]{1,0:T(8,128)(2,1)S(1)}, f32[10,128]{1,0:T(8,128)S(1)}, bf16[768,512]{1,0:T(8,128)(2,1)S(1...) custom-call(s32[3]{0:T(128)S(1)} %copy-done, ...), custom_call_target="tpu_custom_call" | custom-call | flops 5637144576 | bytes 10904588 | tf_op jit(solution)/shard_map/pallas_call | solution.py:38
  59.9 2.0 %collective-permute-done.12 = bf16[4,160,512]{2,1,0:T(8,128)(2,1)S(1)} collective-permute-done((bf16[4,160,512]{2,1,0:T(8,128)(2,1)S(1)}, bf16[4,160,512]{2,1,0:T(8,128)(2,1)S(1)}, u32[]{:S(2)}, u32[]{:S(2)}) %collective-permute-start.12) | collective-permute-done | bytes 655392 | tf_op jit(solution)/shard_map/ppermute | solution.py:371
  61.9 0.2 maximum_select_fusion.1.here_ref
  62.2 0.1 collective-permute-start.14
  62.2 3.0 %collective-permute-done.14.there_ref = bf16[8,160,512]{2,1,0:T(8,128)(2,1)S(1)} collective-permute-done((bf16[8,160,512]{2,1,0:T(8,128)(2,1)S(1)}, bf16[8,160,512]{2,1,0:T(8,128)(2,1)S(1)}, u32[]{:S(2)}, u32[]{:S(2)}) %collective-permute-start.14) | collective-permute-done | bytes 1310752 | tf_op jit(solution)/shard_map/ppermute | solution.py:371
  65.3 12.3 %shard_map.122 = (f32[4,128]{1,0:T(4,128)}, bf16[8,168,512]{2,1,0:T(8,128)(2,1)S(1)}, bf16[8,168,512]{2,1,0:T(8,128)(2,1)S(1)}, f32[512,512]{1,0:T(8,128)S(1)}, ...) custom-call(s32[3]{0:T(128)S(1)} %copy-done, bf16[1792,512]{1,0:T(8,128)(2,1)S(1)} %get-tuple-element.82.h1_ref, ...), custom_call_target="tpu_custom_call" | custom-call | flops 7381975040 | bytes 12590092 | tf_op jit(solution)/shard_map/pallas_call | solution.py:38
  77.6 0.2 collective-permute-start.15
  77.8 3.4 %shard_map.123 = (bf16[8,168,512]{2,1,0:T(8,128)(2,1)S(1)}, bf16[8,168,512]{2,1,0:T(8,128)(2,1)S(1)}) custom-call(s32[3]{0:T(128)S(1)} %copy-done, bf16[768,1024]{1,0:T(8,128)(2,1)S(1)} %get-tuple-element.91.back_ref, f32[512,512]{1,0:T(8,128)S(1)} %get-tuple-element.92.grad_ref, bf16[512,512]{1,0:T(8,128)(2,1)S(1)} %get-tuple-element.93.round_ref, ...), custom_call_target="tpu_custom_call" | custom-call | flops 2415919104 | bytes 9441292 | tf_op jit(solution)/shard_map/pallas_call | solution.py:38
  81.3 0.4 collective-permute-start.16
  81.7 0.7 shard_map.126
  82.4 1.4 %collective-permute-start.17 = (bf16[1,2,2,168,512]{4,3,2,1,0:T(8,128)(2,1)S(1)}, bf16[1,2,2,168,512]{4,3,2,1,0:T(8,128)(2,1)S(1)}, u32[]{:S(2)}, u32[]{:S(2)}) collective-permute-start(bf16[1,2,2,168,512]{4,3,2,1,0:T(8,128)(2,1)S(1)} %bitcast.58), channel_id=1, source_target_pairs={{0,2},{1,5},{2,0},{3,7},{4,6},{5,1},{6,4},{7,3},{8,10},{9,13},{10,... | collective-permute-start | bytes 2064392 | tf_op jit(solution)/shard_map/ppermute | solution.py:371
  83.8 0.7 shard_map.125
  84.5 8.9 %collective-permute-done.17 = bf16[1,2,2,168,512]{4,3,2,1,0:T(8,128)(2,1)S(1)} collective-permute-done((bf16[1,2,2,168,512]{4,3,2,1,0:T(8,128)(2,1)S(1)}, bf16[1,2,2,168,512]{4,3,2,1,0:T(8,128)(2,1)S(1)}, u32[]{:S(2)}, u32[]{:S(2)}) %collective-permute-start.17) | collective-permute-done | bytes 688160 | tf_op jit(solution)/shard_map/ppermute | solution.py:371
  93.4 0.6 shard_map.127
  94.1 0.7 shard_map.128
  94.8 1.4 %collective-permute-start.18 = (bf16[1,2,2,168,512]{4,3,2,1,0:T(8,128)(2,1)S(1)}, bf16[1,2,2,168,512]{4,3,2,1,0:T(8,128)(2,1)S(1)}, u32[]{:S(2)}, u32[]{:S(2)}) collective-permute-start(bf16[1,2,2,168,512]{4,3,2,1,0:T(8,128)(2,1)S(1)} %bitcast.57), channel_id=1, source_target_pairs={{0,2},{1,5},{2,0},{3,7},{4,6},{5,1},{6,4},{7,3},{8,10},{9,13},{10,... | collective-permute-start | bytes 2064392 | tf_op jit(solution)/shard_map/ppermute | solution.py:371
  96.1 1.7 %collective-permute-start.19 = (bf16[1,1,2,168,512]{4,3,2,1,0:T(8,128)(2,1)S(1)}, bf16[1,1,2,168,512]{4,3,2,1,0:T(8,128)(2,1)S(1)}, u32[]{:S(2)}, u32[]{:S(2)}) collective-permute-start(bf16[1,1,2,168,512]{4,3,2,1,0:T(8,128)(2,1)S(1)} %bitcast.61), channel_id=1, source_target_pairs={{0,4},{1,3},{2,6},{3,1},{4,0},{5,7},{6,2},{7,5},{8,12},{9,11},{10,... | collective-permute-start | bytes 1032200 | tf_op jit(solution)/shard_map/ppermute | solution.py:371
  97.9 0.6 shard_map.130
  98.5 0.7 shard_map.124
  99.2 7.9 %collective-permute-done.19 = bf16[1,1,2,168,512]{4,3,2,1,0:T(8,128)(2,1)S(1)} collective-permute-done((bf16[1,1,2,168,512]{4,3,2,1,0:T(8,128)(2,1)S(1)}, bf16[1,1,2,168,512]{4,3,2,1,0:T(8,128)(2,1)S(1)}, u32[]{:S(2)}, u32[]{:S(2)}) %collective-permute-start.19) | collective-permute-done | bytes 344096 | tf_op jit(solution)/shard_map/ppermute | solution.py:371
  107.1 0.6 shard_map.131
  107.7 1.7 %collective-permute-done.18 = bf16[1,2,2,168,512]{4,3,2,1,0:T(8,128)(2,1)S(1)} collective-permute-done((bf16[1,2,2,168,512]{4,3,2,1,0:T(8,128)(2,1)S(1)}, bf16[1,2,2,168,512]{4,3,2,1,0:T(8,128)(2,1)S(1)}, u32[]{:S(2)}, u32[]{:S(2)}) %collective-permute-start.18) | collective-permute-done | bytes 688160 | tf_op jit(solution)/shard_map/ppermute | solution.py:371
  109.5 0.6 shard_map.132
  110.1 0.5 collective-permute-start.20
  110.6 3.1 %collective-permute-start.22 = (bf16[1,1,1,168,512]{4,3,2,1,0:T(8,128)(2,1)S(1)}, bf16[1,1,1,168,512]{4,3,2,1,0:T(8,128)(2,1)S(1)}, u32[]{:S(2)}, u32[]{:S(2)}) collective-permute-start(bf16[1,1,1,168,512]{4,3,2,1,0:T(8,128)(2,1)S(1)} %bitcast.63), channel_id=1, source_target_pairs={{0,8},{1,9},{2,10},{3,11},{4,12},{5,13},{6,14},{7,15},{8,0},{9,1},... | collective-permute-start | bytes 516104 | tf_op jit(solution)/shard_map/ppermute | solution.py:371
  113.6 0.6 shard_map.129
  114.3 6.3 %collective-permute-done.20 = bf16[1,1,2,168,512]{4,3,2,1,0:T(8,128)(2,1)S(1)} collective-permute-done((bf16[1,1,2,168,512]{4,3,2,1,0:T(8,128)(2,1)S(1)}, bf16[1,1,2,168,512]{4,3,2,1,0:T(8,128)(2,1)S(1)}, u32[]{:S(2)}, u32[]{:S(2)}) %collective-permute-start.20) | collective-permute-done | bytes 344096 | tf_op jit(solution)/shard_map/ppermute | solution.py:371
  120.5 0.6 shard_map.134
  121.1 0.4 collective-permute-start.21
  121.5 0.6 shard_map.135
  122.1 0.6 shard_map.133
  122.7 6.3 %collective-permute-done.21 = bf16[1,1,1,168,512]{4,3,2,1,0:T(8,128)(2,1)S(1)} collective-permute-done((bf16[1,1,1,168,512]{4,3,2,1,0:T(8,128)(2,1)S(1)}, bf16[1,1,1,168,512]{4,3,2,1,0:T(8,128)(2,1)S(1)}, u32[]{:S(2)}, u32[]{:S(2)}) %collective-permute-start.21) | collective-permute-done | bytes 172064 | tf_op jit(solution)/shard_map/ppermute | solution.py:371
  129.0 0.9 shard_map.136
  (20 shorter events, 0.1 us)
Async XLA Ops:
  3.3 23.7 %copy-start.2 = (bf16[160,512]{1,0:T(8,128)(2,1)S(1)}, bf16[160,512]{1,0:T(8,128)(2,1)}, u32[]{:S(2)}) copy-start(bf16[160,512]{1,0:T(8,128)(2,1)} %get-tuple-element.60) | copy-start | bytes 491524
  3.3 5.6 %collective-permute-start.1 = (f32[1,3,128]{2,1,0:T(4,128)}, f32[1,3,128]{2,1,0:T(4,128)S(1)}, u32[]{:S(2)}, u32[]{:S(2)}) collective-permute-start(f32[1,3,128]{2,1,0:T(4,128)} %bitcast.74), channel_id=1, source_target_pairs={{0,2},{1,3},{2,0},{3,1},{4,6},{5,7},{6,4},{7,5},{8,10},{9,11},{10,... | collective-permute-start | bytes 4616 | tf_op jit(solution)/shard_map/ppermute | solution.py:371
  6.4 11.0 %collective-permute-start = (bf16[1,176,512]{2,1,0:T(8,128)(2,1)}, bf16[1,176,512]{2,1,0:T(8,128)(2,1)S(1)}, u32[]{:S(2)}, u32[]{:S(2)}) collective-permute-start(bf16[1,176,512]{2,1,0:T(8,128)(2,1)} %bitcast.69), channel_id=1, source_target_pairs={{0,8},{1,9},{2,10},{3,11},{4,12},{5,13},{6,14},{7,15},{8,0},{9,1},... | collective-permute-start | bytes 540680 | tf_op jit(solution)/shard_map/ppermute | solution.py:371
  9.7 3.6 %collective-permute-start.2 = (f32[2,3,128]{2,1,0:T(4,128)S(1)}, f32[2,3,128]{2,1,0:T(4,128)S(1)}, u32[]{:S(2)}, u32[]{:S(2)}) collective-permute-start(f32[2,3,128]{2,1,0:T(4,128)S(1)} %maximum_select_fusion.8), channel_id=1, source_target_pairs={{0,4},{1,5},{2,6},{3,7},{4,0},{5,1},{6,2},{7,3},{8,12},{9,13},{10,... | collective-permute-start | bytes 9224 | tf_op jit(solution)/shard_map/ppermute | solution.py:371
  18.4 8.7 %collective-permute-start.3 = (bf16[2,176,512]{2,1,0:T(8,128)(2,1)S(1)}, bf16[2,176,512]{2,1,0:T(8,128)(2,1)S(1)}, u32[]{:S(2)}, u32[]{:S(2)}) collective-permute-start(bf16[2,176,512]{2,1,0:T(8,128)(2,1)S(1)} %maximum_select_fusion.4), channel_id=1, source_target_pairs={{0,2},{1,5},{2,0},{3,7},{4,6},{5,1},{6,4},{7,3},{8,10},{9,13},{10,... | collective-permute-start | bytes 1081352 | tf_op jit(solution)/shard_map/ppermute | solution.py:371
  19.6 4.6 %collective-permute-start.4 = (f32[4,3,128]{2,1,0:T(4,128)S(1)}, f32[4,3,128]{2,1,0:T(4,128)S(1)}, u32[]{:S(2)}, u32[]{:S(2)}) collective-permute-start(f32[4,3,128]{2,1,0:T(4,128)S(1)} %maximum_select_fusion.7), channel_id=1, source_target_pairs={{0,8},{1,9},{2,10},{3,11},{4,12},{5,13},{6,14},{7,15},{8,0},{9,1},... | collective-permute-start | bytes 18440 | tf_op jit(solution)/shard_map/ppermute | solution.py:371
  19.7 7.4 %collective-permute-start.5 = (bf16[1,160,512]{2,1,0:T(8,128)(2,1)}, bf16[1,160,512]{2,1,0:T(8,128)(2,1)S(1)}, u32[]{:S(2)}, u32[]{:S(2)}) collective-permute-start(bf16[1,160,512]{2,1,0:T(8,128)(2,1)} %bitcast.71), channel_id=1, source_target_pairs={{0,8},{1,9},{2,10},{3,11},{4,12},{5,13},{6,14},{7,15},{8,0},{9,1},... | collective-permute-start | bytes 491528 | tf_op jit(solution)/shard_map/ppermute | solution.py:371
  26.9 5.8 %copy-start.1 = (bf16[528,128]{1,0:T(8,128)(2,1)S(1)}, bf16[528,128]{1,0:T(8,128)(2,1)}, u32[]{:S(2)}) copy-start(bf16[528,128]{1,0:T(8,128)(2,1)} %get-tuple-element.72.own_ref.norm_ref) | copy-start | bytes 405508
  26.9 11.1 %copy-start.4 = (bf16[272,128]{1,0:T(8,128)(2,1)S(1)}, bf16[272,128]{1,0:T(8,128)(2,1)}, u32[]{:S(2)}) copy-start(bf16[272,128]{1,0:T(8,128)(2,1)} %get-tuple-element.73) | copy-start | bytes 208900
  26.9 14.9 %copy-start.3 = (bf16[272,128]{1,0:T(8,128)(2,1)S(1)}, bf16[272,128]{1,0:T(8,128)(2,1)}, u32[]{:S(2)}) copy-start(bf16[272,128]{1,0:T(8,128)(2,1)} %get-tuple-element.74) | copy-start | bytes 208900
  27.2 18.2 %collective-permute-start.6 = (bf16[4,176,512]{2,1,0:T(8,128)(2,1)S(1)}, bf16[4,176,512]{2,1,0:T(8,128)(2,1)S(1)}, u32[]{:S(2)}, u32[]{:S(2)}) collective-permute-start(bf16[4,176,512]{2,1,0:T(8,128)(2,1)S(1)} %maximum_select_fusion.2), channel_id=1, source_target_pairs={{0,4},{1,3},{2,6},{3,1},{4,0},{5,7},{6,2},{7,5},{8,12},{9,11},{10,... | collective-permute-start | bytes 2162696 | tf_op jit(solution)/shard_map/ppermute | solution.py:371
  31.3 10.5 %collective-permute-start.7 = (bf16[2,160,512]{2,1,0:T(8,128)(2,1)S(1)}, bf16[2,160,512]{2,1,0:T(8,128)(2,1)S(1)}, u32[]{:S(2)}, u32[]{:S(2)}) collective-permute-start(bf16[2,160,512]{2,1,0:T(8,128)(2,1)S(1)} %maximum_select_fusion.5), channel_id=1, source_target_pairs={{0,2},{1,5},{2,0},{3,7},{4,6},{5,1},{6,4},{7,3},{8,10},{9,13},{10,... | collective-permute-start | bytes 983048 | tf_op jit(solution)/shard_map/ppermute | solution.py:371
  32.6 15.8 %collective-permute-start.9 = (bf16[528,128]{1,0:T(8,128)(2,1)S(1)}, bf16[528,128]{1,0:T(8,128)(2,1)S(1)}, u32[]{:S(2)}, u32[]{:S(2)}) collective-permute-start(bf16[528,128]{1,0:T(8,128)(2,1)S(1)} %copy-done.1), channel_id=1, source_target_pairs={{2,4},{4,2},{6,8},{8,6},{10,12},{12,10},{3,5},{5,3},{7,9},{9,7},{1... | collective-permute-start | bytes 405512 | tf_op jit(solution)/shard_map/ppermute | solution.py:429
  33.3 15.2 %collective-permute-start.8 = (bf16[528,128]{1,0:T(8,128)(2,1)S(1)}, bf16[528,128]{1,0:T(8,128)(2,1)S(1)}, u32[]{:S(2)}, u32[]{:S(2)}) collective-permute-start(bf16[528,128]{1,0:T(8,128)(2,1)S(1)} %copy-done.1), channel_id=1, source_target_pairs={{0,2},{1,3},{2,0},{3,1},{4,6},{5,7},{6,4},{7,5},{8,10},{9,11},{10,... | collective-permute-start | bytes 405512 | tf_op jit(solution)/shard_map/ppermute | solution.py:371
  38.0 10.4 %collective-permute-start.10 = (bf16[272,128]{1,0:T(8,128)(2,1)S(1)}, bf16[272,128]{1,0:T(8,128)(2,1)S(1)}, u32[]{:S(2)}, u32[]{:S(2)}) collective-permute-start(bf16[272,128]{1,0:T(8,128)(2,1)S(1)} %copy-done.4), channel_id=1, source_target_pairs={{0,4},{1,5},{2,6},{3,7},{4,0},{5,1},{6,2},{7,3},{8,12},{9,13},{10,... | collective-permute-start | bytes 208904 | tf_op jit(solution)/shard_map/ppermute | solution.py:371
  41.8 6.7 %collective-permute-start.11 = (bf16[272,128]{1,0:T(8,128)(2,1)S(1)}, bf16[272,128]{1,0:T(8,128)(2,1)S(1)}, u32[]{:S(2)}, u32[]{:S(2)}) collective-permute-start(bf16[272,128]{1,0:T(8,128)(2,1)S(1)} %copy-done.3), channel_id=1, source_target_pairs={{4,8},{8,4},{6,10},{10,6},{5,9},{9,5},{7,11},{11,7},{20,24},{24,20... | collective-permute-start | bytes 208904 | tf_op jit(solution)/shard_map/ppermute | solution.py:429
  42.7 10.6 %copy-start = (s32[3]{0:T(128)S(1)}, s32[3]{0:T(128)}, u32[]{:S(2)}) copy-start(s32[3]{0:T(128)} %pad_add_fusion.scalar_ref) | copy-start | bytes 40
  48.5 4.9 %collective-permute-start.13 = (bf16[8,176,512]{2,1,0:T(8,128)(2,1)S(1)}, bf16[8,176,512]{2,1,0:T(8,128)(2,1)S(1)}, u32[]{:S(2)}, u32[]{:S(2)}) collective-permute-start(bf16[8,176,512]{2,1,0:T(8,128)(2,1)S(1)} %maximum_select_fusion.here_ref), channel_id=1, source_target_pairs={{0,1},{1,0},{2,3},{3,2},{4,5},{5,4},{6,7},{7,6},{8,9},{9,8},{10,11... | collective-permute-start | bytes 4325384 | tf_op jit(solution)/shard_map/ppermute | solution.py:371
  50.5 11.5 %collective-permute-start.12 = (bf16[4,160,512]{2,1,0:T(8,128)(2,1)S(1)}, bf16[4,160,512]{2,1,0:T(8,128)(2,1)S(1)}, u32[]{:S(2)}, u32[]{:S(2)}) collective-permute-start(bf16[4,160,512]{2,1,0:T(8,128)(2,1)S(1)} %maximum_select_fusion.3), channel_id=1, source_target_pairs={{0,4},{1,3},{2,6},{3,1},{4,0},{5,7},{6,2},{7,5},{8,12},{9,11},{10,... | collective-permute-start | bytes 1966088 | tf_op jit(solution)/shard_map/ppermute | solution.py:371
  62.2 3.1 %collective-permute-start.14 = (bf16[8,160,512]{2,1,0:T(8,128)(2,1)S(1)}, bf16[8,160,512]{2,1,0:T(8,128)(2,1)S(1)}, u32[]{:S(2)}, u32[]{:S(2)}) collective-permute-start(bf16[8,160,512]{2,1,0:T(8,128)(2,1)S(1)} %maximum_select_fusion.1.here_ref), channel_id=1, source_target_pairs={{0,1},{1,0},{2,3},{3,2},{4,5},{5,4},{6,7},{7,6},{8,9},{9,8},{10,11... | collective-permute-start | bytes 3932168 | tf_op jit(solution)/shard_map/ppermute | solution.py:371
  77.6 3.7 %collective-permute-start.15 = (bf16[8,168,512]{2,1,0:T(8,128)(2,1)S(1)}, bf16[8,168,512]{2,1,0:T(8,128)(2,1)S(1)}, u32[]{:S(2)}, u32[]{:S(2)}) collective-permute-start(bf16[8,168,512]{2,1,0:T(8,128)(2,1)S(1)} %get-tuple-element.90), channel_id=1, source_target_pairs={{0,1},{1,0},{2,3},{3,2},{4,5},{5,4},{6,7},{7,6},{8,9},{9,8},{10,11... | collective-permute-start | bytes 4128776 | tf_op jit(solution)/shard_map/ppermute | solution.py:371
  81.3 12.8 %collective-permute-start.16 = (bf16[8,168,512]{2,1,0:T(8,128)(2,1)S(1)}, bf16[8,168,512]{2,1,0:T(8,128)(2,1)S(1)}, u32[]{:S(2)}, u32[]{:S(2)}) collective-permute-start(bf16[8,168,512]{2,1,0:T(8,128)(2,1)S(1)} %get-tuple-element.100), channel_id=1, source_target_pairs={{0,1},{1,0},{2,3},{3,2},{4,5},{5,4},{6,7},{7,6},{8,9},{9,8},{10,11... | collective-permute-start | bytes 4128776 | tf_op jit(solution)/shard_map/ppermute | solution.py:371
  82.4 11.0 %collective-permute-start.17 = (bf16[1,2,2,168,512]{4,3,2,1,0:T(8,128)(2,1)S(1)}, bf16[1,2,2,168,512]{4,3,2,1,0:T(8,128)(2,1)S(1)}, u32[]{:S(2)}, u32[]{:S(2)}) collective-permute-start(bf16[1,2,2,168,512]{4,3,2,1,0:T(8,128)(2,1)S(1)} %bitcast.58), channel_id=1, source_target_pairs={{0,2},{1,5},{2,0},{3,7},{4,6},{5,1},{6,4},{7,3},{8,10},{9,13},{10,... | collective-permute-start | bytes 2064392 | tf_op jit(solution)/shard_map/ppermute | solution.py:371
  94.8 14.7 %collective-permute-start.18 = (bf16[1,2,2,168,512]{4,3,2,1,0:T(8,128)(2,1)S(1)}, bf16[1,2,2,168,512]{4,3,2,1,0:T(8,128)(2,1)S(1)}, u32[]{:S(2)}, u32[]{:S(2)}) collective-permute-start(bf16[1,2,2,168,512]{4,3,2,1,0:T(8,128)(2,1)S(1)} %bitcast.57), channel_id=1, source_target_pairs={{0,2},{1,5},{2,0},{3,7},{4,6},{5,1},{6,4},{7,3},{8,10},{9,13},{10,... | collective-permute-start | bytes 2064392 | tf_op jit(solution)/shard_map/ppermute | solution.py:371
  96.1 11.0 %collective-permute-start.19 = (bf16[1,1,2,168,512]{4,3,2,1,0:T(8,128)(2,1)S(1)}, bf16[1,1,2,168,512]{4,3,2,1,0:T(8,128)(2,1)S(1)}, u32[]{:S(2)}, u32[]{:S(2)}) collective-permute-start(bf16[1,1,2,168,512]{4,3,2,1,0:T(8,128)(2,1)S(1)} %bitcast.61), channel_id=1, source_target_pairs={{0,4},{1,3},{2,6},{3,1},{4,0},{5,7},{6,2},{7,5},{8,12},{9,11},{10,... | collective-permute-start | bytes 1032200 | tf_op jit(solution)/shard_map/ppermute | solution.py:371
  110.1 10.4 %collective-permute-start.20 = (bf16[1,1,2,168,512]{4,3,2,1,0:T(8,128)(2,1)S(1)}, bf16[1,1,2,168,512]{4,3,2,1,0:T(8,128)(2,1)S(1)}, u32[]{:S(2)}, u32[]{:S(2)}) collective-permute-start(bf16[1,1,2,168,512]{4,3,2,1,0:T(8,128)(2,1)S(1)} %bitcast.62), channel_id=1, source_target_pairs={{0,4},{1,3},{2,6},{3,1},{4,0},{5,7},{6,2},{7,5},{8,12},{9,11},{10,... | collective-permute-start | bytes 1032200 | tf_op jit(solution)/shard_map/ppermute | solution.py:371
  110.6 12.2 %collective-permute-start.22 = (bf16[1,1,1,168,512]{4,3,2,1,0:T(8,128)(2,1)S(1)}, bf16[1,1,1,168,512]{4,3,2,1,0:T(8,128)(2,1)S(1)}, u32[]{:S(2)}, u32[]{:S(2)}) collective-permute-start(bf16[1,1,1,168,512]{4,3,2,1,0:T(8,128)(2,1)S(1)} %bitcast.63), channel_id=1, source_target_pairs={{0,8},{1,9},{2,10},{3,11},{4,12},{5,13},{6,14},{7,15},{8,0},{9,1},... | collective-permute-start | bytes 516104 | tf_op jit(solution)/shard_map/ppermute | solution.py:371
  121.1 7.9 %collective-permute-start.21 = (bf16[1,1,1,168,512]{4,3,2,1,0:T(8,128)(2,1)S(1)}, bf16[1,1,1,168,512]{4,3,2,1,0:T(8,128)(2,1)S(1)}, u32[]{:S(2)}, u32[]{:S(2)}) collective-permute-start(bf16[1,1,1,168,512]{4,3,2,1,0:T(8,128)(2,1)S(1)} %bitcast.66), channel_id=1, source_target_pairs={{0,8},{1,9},{2,10},{3,11},{4,12},{5,13},{6,14},{7,15},{8,0},{9,1},... | collective-permute-start | bytes 516104 | tf_op jit(solution)/shard_map/ppermute | solution.py:371

commit v11 on v10

--- a/solution.py
+++ b/solution.py
@@ -251,21 +251,22 @@
     lanes = label_ref.shape[1]
     class_row = lax.broadcasted_iota(jnp.int32, (classes, lanes), 0).astype(F32)
     unit = class_row == lax.broadcasted_iota(jnp.int32, (lanes, lanes), 1).astype(F32)
-    row = lax.broadcasted_iota(jnp.int32, (TILE, 1), 0)
+    cuts = [0, steps, 2 * steps, rows]
     left = scalar_ref[2] - scalar_ref[1] * steps
 
-    for i in range(rows // TILE):
-        at = tile_of(i)
-        now = h1_ref[tile_of(i, d), :]
+    for start, end in zip(cuts, cuts[1:]):
+        at = slice(start, end)
+        row = lax.broadcasted_iota(jnp.int32, (end - start, 1), 0)
+        now = h1_ref[start + d : end + d, :]
         t, s = activate(h1_ref[at, :], now, conv_ref)
         gated = (t * s).astype(BF16)
         h2 = (now.astype(F32) + dot(gated, rows_of(res_ref[...]))).astype(BF16)
         logits = dot(h2, w_out_ref[...])
         total = jnp.log(jnp.sum(jnp.exp(logits), axis=1, keepdims=True))
-        groups = range(i * TILE // lanes, (i + 1) * TILE // lanes)
+        groups = range(start // lanes, end // lanes)
         hot = jnp.concatenate(
             [(class_row == label_ref[k : k + 1, :]).astype(F32).T for k in groups])
-        valid = (row + i * TILE < left).astype(F32)
+        valid = (row + start < left).astype(F32)
         lgrad = ((jnp.exp(logits - total) - hot) * (valid * scale)).astype(BF16)
         grad = dot_t(lgrad, w_out_ref[...])
         rounded = grad.astype(BF16)
@@ -273,9 +274,10 @@
         filter_slope, gate_slope = slopes(t, s)
         back_ref[at, :c] = (back * filter_slope).astype(BF16)
         back_ref[at, c:] = (back * gate_slope).astype(BF16)
-        if i * TILE < grad_ref.shape[0]:
-            grad_ref[at, :] = grad
-        if i * TILE < steps:
+        kept = min(end, grad_ref.shape[0])
+        if start < kept:
+            grad_ref[start:kept, :] = grad[: kept - start]
+        if start < steps:
             loss = (total - jnp.sum(logits * hot, axis=1, keepdims=True)) * valid
             for j, k in enumerate(groups):
                 part = jnp.where(unit, loss[j * lanes : (j + 1) * lanes], 0.0)
@@ -516,15 +518,18 @@
 
     order = sum_steps()
     kept1, sent1 = halves_of(sums1, scalars, *order[0])
-    sums1, sums0 = [kept1, swap(sent1, order[0][0])], core_step(keep0, send0)
-    for step, (links, dim) in enumerate(order):
-        more = step + 1 < len(order)
-        kept0, sent0 = halves_of(sums0, scalars, links, dim)
-        if more:
-            kept1, sent1 = halves_of(sums1, scalars, *order[step + 1])
+    other1 = swap(sent1, order[0][0])
+    kept0, sent0 = halves_of(core_step(keep0, send0), scalars, *order[0])
+    other1, sent0 = together(other1, sent0)
+    for step, (links, _) in enumerate(order):
+        if step + 1 < len(order):
+            kept1, sent1 = halves_of([kept1, other1], scalars, *order[step + 1])
             sent1, sent0 = together(sent1, sent0)
-            sums1 = [kept1, swap(sent1, order[step + 1][0])]
-        sums0 = [kept0, swap(sent0, links)]
+            other1 = swap(sent1, order[step + 1][0])
+        other0 = swap(sent0, links)
+        if step + 1 < len(order):
+            kept0, sent0 = halves_of([kept0, other0], scalars, *order[step + 1])
+    sums0, sums1 = [kept0, other0], [kept1, other1]
     rows = 2 * conv + res + enter
     parts = [v.reshape(rows, c) for v in sums0 + sums1]
     grad_conv, grad_res, grad_in, grad_out = call(

time: 130 us -> 128 us (0.985)
  Pallas kernels: 35.6 us -> 34.2 us
    pallas_call x18, Pallas kernels: 35.6 us -> 34.2 us  [call(): pl.pallas_call(kernel, out_shape=[jax.ShapeDtypeStruct(s, d) for s, d in...]
where the time goes in v11:
time: 128 us
  waiting for transfers between devices  50.4 us (39%)
  starting transfers between devices  37.9 us (30%)
  Pallas kernels  34.2 us (27%)
  other arithmetic  3.7 us (3%)
  between operations  1.53 us (1%)
    ppermute x21, waiting for transfers between devices, swap(): return lax.ppermute(value, ('tm', 'site'), pairs)  50.4 us
    ppermute x21, starting transfers between devices, swap(): return lax.ppermute(value, ('tm', 'site'), pairs)  36.4 us
    pallas_call x18, Pallas kernels, call(): pl.pallas_call(kernel, out_shape=[jax.ShapeDtypeStruct(s, d) for s, d in...  34.2 us
    select_n x9, other arithmetic, arranged(): jnp.where(my_bit(links) == 0, jnp.concatenate([held, other]), jnp.concate...  3.12 us
  transfers between devices with their start and end apart: 23, of which 14 were waited for; matrix products, arithmetic and copies ran while one was open for 2% of the time, Pallas kernels for 14%

profile of v11, /device:TPU:0, one launch (start us, length us, event | category | flops | bytes accessed | tf_op | source)
XLA Modules:
  0.0 127.8 jit_solution(3156225796394297177)
XLA Ops:
  0.6 2.7 %shard_map.119 = (f32[512,128]{1,0:T(8,128)}, f32[512,128]{1,0:T(8,128)}, f32[512,128]{1,0:T(8,128)}, f32[3,128]{1,0:T(4,128)}, bf16[176,512]{1,0:T(8,128)(2,1)}, /*index=5*/bf16[160,512]{1,0:T(8,128)(2,1)}) custom-call(f32[512,128]{1,0:T(8,128)} %bitcast.67, f32[512,128]{1,0:T(8,128)} %bitcast.76, bf16[2,64,1024]{2,1,0:T(8,128)(2,1)} %conv_ref.1, ...), custom_call_target="tpu_custom_call" | custom-call | flops 2000000000 | bytes 2000384 | tf_op jit(solution)/shard_map/pallas_call | solution.py:38
  3.3 3.0 %collective-permute-start.1 = (f32[1,3,128]{2,1,0:T(4,128)}, f32[1,3,128]{2,1,0:T(4,128)S(1)}, u32[]{:S(2)}, u32[]{:S(2)}) collective-permute-start(f32[1,3,128]{2,1,0:T(4,128)} %bitcast.74), channel_id=1, source_target_pairs={{0,2},{1,3},{2,0},{3,1},{4,6},{5,7},{6,4},{7,5},{8,10},{9,11},{10,... | collective-permute-start | bytes 4616 | tf_op jit(solution)/shard_map/ppermute | solution.py:373
  6.4 2.6 %collective-permute-start = (bf16[1,176,512]{2,1,0:T(8,128)(2,1)}, bf16[1,176,512]{2,1,0:T(8,128)(2,1)S(1)}, u32[]{:S(2)}, u32[]{:S(2)}) collective-permute-start(bf16[1,176,512]{2,1,0:T(8,128)(2,1)} %bitcast.69), channel_id=1, source_target_pairs={{0,8},{1,9},{2,10},{3,11},{4,12},{5,13},{6,14},{7,15},{8,0},{9,1},... | collective-permute-start | bytes 540680 | tf_op jit(solution)/shard_map/ppermute | solution.py:373
  9.0 0.8 maximum_select_fusion.8
  9.7 1.6 %collective-permute-start.2 = (f32[2,3,128]{2,1,0:T(4,128)S(1)}, f32[2,3,128]{2,1,0:T(4,128)S(1)}, u32[]{:S(2)}, u32[]{:S(2)}) collective-permute-start(f32[2,3,128]{2,1,0:T(4,128)S(1)} %maximum_select_fusion.8), channel_id=1, source_target_pairs={{0,4},{1,5},{2,6},{3,7},{4,0},{5,1},{6,2},{7,3},{8,12},{9,13},{10,... | collective-permute-start | bytes 9224 | tf_op jit(solution)/shard_map/ppermute | solution.py:373
  11.3 2.0 %collective-permute-done.2 = f32[2,3,128]{2,1,0:T(4,128)S(1)} collective-permute-done((f32[2,3,128]{2,1,0:T(4,128)S(1)}, f32[2,3,128]{2,1,0:T(4,128)S(1)}, u32[]{:S(2)}, u32[]{:S(2)}) %collective-permute-start.2) | collective-permute-done | bytes 3104 | tf_op jit(solution)/shard_map/ppermute | solution.py:373
  13.3 4.0 %collective-permute-done = bf16[1,176,512]{2,1,0:T(8,128)(2,1)S(1)} collective-permute-done((bf16[1,176,512]{2,1,0:T(8,128)(2,1)}, bf16[1,176,512]{2,1,0:T(8,128)(2,1)S(1)}, u32[]{:S(2)}, u32[]{:S(2)}) %collective-permute-start) | collective-permute-done | bytes 180256 | tf_op jit(solution)/shard_map/ppermute | solution.py:373
  17.3 1.1 maximum_select_fusion.4
  18.4 0.5 collective-permute-start.3
  19.6 0.1 collective-permute-start.4
  19.7 2.9 %collective-permute-start.5 = (bf16[1,160,512]{2,1,0:T(8,128)(2,1)}, bf16[1,160,512]{2,1,0:T(8,128)(2,1)S(1)}, u32[]{:S(2)}, u32[]{:S(2)}) collective-permute-start(bf16[1,160,512]{2,1,0:T(8,128)(2,1)} %bitcast.71), channel_id=1, source_target_pairs={{0,8},{1,9},{2,10},{3,11},{4,12},{5,13},{6,14},{7,15},{8,0},{9,1},... | collective-permute-start | bytes 491528 | tf_op jit(solution)/shard_map/ppermute | solution.py:373
  22.6 0.6 pad_add_fusion.scalar_ref
  23.2 1.0 collective-permute-done.4
  24.2 0.6 maximum_select_fusion.6.carry_ref
  24.8 2.1 %shard_map.120 = (bf16[528,128]{1,0:T(8,128)(2,1)}, bf16[272,128]{1,0:T(8,128)(2,1)}, bf16[272,128]{1,0:T(8,128)(2,1)}) custom-call(s32[3]{0:T(128)} %pad_add_fusion.scalar_ref, f32[512,128]{1,0:T(8,128)} %bitcast.68, f32[512,128]{1,0:T(8,128)} %get-tuple-element.64.keep_ref, f32[512,128]{1,0:T(8,128)} %get-tuple-element.65.mass_ref, ...), custom_call_target="tpu_custom_call" | custom-call | flops 100000000 | bytes 1337356 | tf_op jit(solution)/shard_map/pallas_call | solution.py:38
  26.9 0.2 collective-permute-done.5
  27.1 0.1 maximum_select_fusion.2
  27.2 4.0 %collective-permute-start.6 = (bf16[4,176,512]{2,1,0:T(8,128)(2,1)S(1)}, bf16[4,176,512]{2,1,0:T(8,128)(2,1)S(1)}, u32[]{:S(2)}, u32[]{:S(2)}) collective-permute-start(bf16[4,176,512]{2,1,0:T(8,128)(2,1)S(1)} %maximum_select_fusion.2), channel_id=1, source_target_pairs={{0,4},{1,3},{2,6},{3,1},{4,0},{5,7},{6,2},{7,5},{8,12},{9,11},{10,... | collective-permute-start | bytes 2162696 | tf_op jit(solution)/shard_map/ppermute | solution.py:373
  31.3 1.4 %collective-permute-start.7 = (bf16[2,160,512]{2,1,0:T(8,128)(2,1)S(1)}, bf16[2,160,512]{2,1,0:T(8,128)(2,1)S(1)}, u32[]{:S(2)}, u32[]{:S(2)}) collective-permute-start(bf16[2,160,512]{2,1,0:T(8,128)(2,1)S(1)} %maximum_select_fusion.5), channel_id=1, source_target_pairs={{0,2},{1,5},{2,0},{3,7},{4,6},{5,1},{6,4},{7,3},{8,10},{9,13},{10,... | collective-permute-start | bytes 983048 | tf_op jit(solution)/shard_map/ppermute | solution.py:373
  32.6 0.7 collective-permute-start.9
  33.3 4.7 %collective-permute-start.8 = (bf16[528,128]{1,0:T(8,128)(2,1)S(1)}, bf16[528,128]{1,0:T(8,128)(2,1)S(1)}, u32[]{:S(2)}, u32[]{:S(2)}) collective-permute-start(bf16[528,128]{1,0:T(8,128)(2,1)S(1)} %copy-done.1), channel_id=1, source_target_pairs={{0,2},{1,3},{2,0},{3,1},{4,6},{5,7},{6,4},{7,5},{8,10},{9,11},{10,... | collective-permute-start | bytes 405512 | tf_op jit(solution)/shard_map/ppermute | solution.py:373
  38.0 1.6 %collective-permute-start.10 = (bf16[272,128]{1,0:T(8,128)(2,1)S(1)}, bf16[272,128]{1,0:T(8,128)(2,1)S(1)}, u32[]{:S(2)}, u32[]{:S(2)}) collective-permute-start(bf16[272,128]{1,0:T(8,128)(2,1)S(1)} %copy-done.4), channel_id=1, source_target_pairs={{0,4},{1,5},{2,6},{3,7},{4,0},{5,1},{6,2},{7,3},{8,12},{9,13},{10,... | collective-permute-start | bytes 208904 | tf_op jit(solution)/shard_map/ppermute | solution.py:373
  39.6 2.2 %collective-permute-done.7 = bf16[2,160,512]{2,1,0:T(8,128)(2,1)S(1)} collective-permute-done((bf16[2,160,512]{2,1,0:T(8,128)(2,1)S(1)}, bf16[2,160,512]{2,1,0:T(8,128)(2,1)S(1)}, u32[]{:S(2)}, u32[]{:S(2)}) %collective-permute-start.7) | collective-permute-done | bytes 327712 | tf_op jit(solution)/shard_map/ppermute | solution.py:373
  41.8 0.8 collective-permute-start.11
  42.6 0.1 maximum_select_fusion.3
  42.7 0.0 copy-start
  42.8 2.7 %collective-permute-done.6 = bf16[4,176,512]{2,1,0:T(8,128)(2,1)S(1)} collective-permute-done((bf16[4,176,512]{2,1,0:T(8,128)(2,1)S(1)}, bf16[4,176,512]{2,1,0:T(8,128)(2,1)S(1)}, u32[]{:S(2)}, u32[]{:S(2)}) %collective-permute-start.6) | collective-permute-done | bytes 720928 | tf_op jit(solution)/shard_map/ppermute | solution.py:373
  45.5 0.2 maximum_select_fusion.here_ref
  45.7 2.7 %collective-permute-done.10.low_ref = bf16[272,128]{1,0:T(8,128)(2,1)S(1)} collective-permute-done((bf16[272,128]{1,0:T(8,128)(2,1)S(1)}, bf16[272,128]{1,0:T(8,128)(2,1)S(1)}, u32[]{:S(2)}, u32[]{:S(2)}) %collective-permute-start.10) | collective-permute-done | bytes 69664 | tf_op jit(solution)/shard_map/ppermute | solution.py:373
  48.5 2.0 %collective-permute-start.13 = (bf16[8,176,512]{2,1,0:T(8,128)(2,1)S(1)}, bf16[8,176,512]{2,1,0:T(8,128)(2,1)S(1)}, u32[]{:S(2)}, u32[]{:S(2)}) collective-permute-start(bf16[8,176,512]{2,1,0:T(8,128)(2,1)S(1)} %maximum_select_fusion.here_ref), channel_id=1, source_target_pairs={{0,1},{1,0},{2,3},{3,2},{4,5},{5,4},{6,7},{7,6},{8,9},{9,8},{10,11... | collective-permute-start | bytes 4325384 | tf_op jit(solution)/shard_map/ppermute | solution.py:373
  50.5 2.9 %collective-permute-start.12 = (bf16[4,160,512]{2,1,0:T(8,128)(2,1)S(1)}, bf16[4,160,512]{2,1,0:T(8,128)(2,1)S(1)}, u32[]{:S(2)}, u32[]{:S(2)}) collective-permute-start(bf16[4,160,512]{2,1,0:T(8,128)(2,1)S(1)} %maximum_select_fusion.3), channel_id=1, source_target_pairs={{0,4},{1,3},{2,6},{3,1},{4,0},{5,7},{6,2},{7,5},{8,12},{9,11},{10,... | collective-permute-start | bytes 1966088 | tf_op jit(solution)/shard_map/ppermute | solution.py:373
  53.4 6.5 %shard_map.121 = (bf16[1792,512]{1,0:T(8,128)(2,1)S(1)}, bf16[512,128]{1,0:T(8,128)(2,1)S(1)}, f32[10,128]{1,0:T(8,128)S(1)}, bf16[768,512]{1,0:T(8,128)(2,1)S(1...) custom-call(s32[3]{0:T(128)S(1)} %copy-done, ...), custom_call_target="tpu_custom_call" | custom-call | flops 5637144576 | bytes 10904588 | tf_op jit(solution)/shard_map/pallas_call | solution.py:38
  59.9 2.0 %collective-permute-done.12 = bf16[4,160,512]{2,1,0:T(8,128)(2,1)S(1)} collective-permute-done((bf16[4,160,512]{2,1,0:T(8,128)(2,1)S(1)}, bf16[4,160,512]{2,1,0:T(8,128)(2,1)S(1)}, u32[]{:S(2)}, u32[]{:S(2)}) %collective-permute-start.12) | collective-permute-done | bytes 655392 | tf_op jit(solution)/shard_map/ppermute | solution.py:373
  61.9 0.2 maximum_select_fusion.1.here_ref
  62.2 0.1 collective-permute-start.14
  62.2 3.0 %collective-permute-done.14.there_ref = bf16[8,160,512]{2,1,0:T(8,128)(2,1)S(1)} collective-permute-done((bf16[8,160,512]{2,1,0:T(8,128)(2,1)S(1)}, bf16[8,160,512]{2,1,0:T(8,128)(2,1)S(1)}, u32[]{:S(2)}, u32[]{:S(2)}) %collective-permute-start.14) | collective-permute-done | bytes 1310752 | tf_op jit(solution)/shard_map/ppermute | solution.py:373
  65.3 11.0 %shard_map.122 = (f32[4,128]{1,0:T(4,128)}, bf16[8,168,512]{2,1,0:T(8,128)(2,1)S(1)}, bf16[8,168,512]{2,1,0:T(8,128)(2,1)S(1)}, f32[512,512]{1,0:T(8,128)S(1)}, ...) custom-call(s32[3]{0:T(128)S(1)} %copy-done, bf16[1792,512]{1,0:T(8,128)(2,1)S(1)} %get-tuple-element.84.h1_ref, ...), custom_call_target="tpu_custom_call" | custom-call | flops 7381975040 | bytes 12590092 | tf_op jit(solution)/shard_map/pallas_call | solution.py:38
  76.3 0.2 collective-permute-start.15
  76.5 3.3 %shard_map.123 = (bf16[8,168,512]{2,1,0:T(8,128)(2,1)S(1)}, bf16[8,168,512]{2,1,0:T(8,128)(2,1)S(1)}) custom-call(s32[3]{0:T(128)S(1)} %copy-done, bf16[768,1024]{1,0:T(8,128)(2,1)S(1)} %get-tuple-element.93.back_ref, f32[512,512]{1,0:T(8,128)S(1)} %get-tuple-element.94.grad_ref, bf16[512,512]{1,0:T(8,128)(2,1)S(1)} %get-tuple-element.95.round_ref, ...), custom_call_target="tpu_custom_call" | custom-call | flops 2415919104 | bytes 9441292 | tf_op jit(solution)/shard_map/pallas_call | solution.py:38
  79.8 0.4 collective-permute-start.16
  80.3 0.7 shard_map.126
  81.0 1.4 %collective-permute-start.17 = (bf16[1,2,2,168,512]{4,3,2,1,0:T(8,128)(2,1)S(1)}, bf16[1,2,2,168,512]{4,3,2,1,0:T(8,128)(2,1)S(1)}, u32[]{:S(2)}, u32[]{:S(2)}) collective-permute-start(bf16[1,2,2,168,512]{4,3,2,1,0:T(8,128)(2,1)S(1)} %bitcast.58), channel_id=1, source_target_pairs={{0,2},{1,5},{2,0},{3,7},{4,6},{5,1},{6,4},{7,3},{8,10},{9,13},{10,... | collective-permute-start | bytes 2064392 | tf_op jit(solution)/shard_map/ppermute | solution.py:373
  82.4 0.7 shard_map.125
  83.1 0.7 shard_map.127
  83.8 8.2 %collective-permute-done.17 = bf16[1,2,2,168,512]{4,3,2,1,0:T(8,128)(2,1)S(1)} collective-permute-done((bf16[1,2,2,168,512]{4,3,2,1,0:T(8,128)(2,1)S(1)}, bf16[1,2,2,168,512]{4,3,2,1,0:T(8,128)(2,1)S(1)}, u32[]{:S(2)}, u32[]{:S(2)}) %collective-permute-start.17) | collective-permute-done | bytes 688160 | tf_op jit(solution)/shard_map/ppermute | solution.py:373
  92.0 0.6 shard_map.128
  92.6 1.4 %collective-permute-start.18 = (bf16[1,2,2,168,512]{4,3,2,1,0:T(8,128)(2,1)S(1)}, bf16[1,2,2,168,512]{4,3,2,1,0:T(8,128)(2,1)S(1)}, u32[]{:S(2)}, u32[]{:S(2)}) collective-permute-start(bf16[1,2,2,168,512]{4,3,2,1,0:T(8,128)(2,1)S(1)} %bitcast.57), channel_id=1, source_target_pairs={{0,2},{1,5},{2,0},{3,7},{4,6},{5,1},{6,4},{7,3},{8,10},{9,13},{10,... | collective-permute-start | bytes 2064392 | tf_op jit(solution)/shard_map/ppermute | solution.py:373
  94.0 1.7 %collective-permute-start.19 = (bf16[1,1,2,168,512]{4,3,2,1,0:T(8,128)(2,1)S(1)}, bf16[1,1,2,168,512]{4,3,2,1,0:T(8,128)(2,1)S(1)}, u32[]{:S(2)}, u32[]{:S(2)}) collective-permute-start(bf16[1,1,2,168,512]{4,3,2,1,0:T(8,128)(2,1)S(1)} %bitcast.61), channel_id=1, source_target_pairs={{0,4},{1,3},{2,6},{3,1},{4,0},{5,7},{6,2},{7,5},{8,12},{9,11},{10,... | collective-permute-start | bytes 1032200 | tf_op jit(solution)/shard_map/ppermute | solution.py:373
  95.8 0.7 shard_map.124
  96.5 0.6 shard_map.130
  97.1 7.9 %collective-permute-done.19 = bf16[1,1,2,168,512]{4,3,2,1,0:T(8,128)(2,1)S(1)} collective-permute-done((bf16[1,1,2,168,512]{4,3,2,1,0:T(8,128)(2,1)S(1)}, bf16[1,1,2,168,512]{4,3,2,1,0:T(8,128)(2,1)S(1)}, u32[]{:S(2)}, u32[]{:S(2)}) %collective-permute-start.19) | collective-permute-done | bytes 344096 | tf_op jit(solution)/shard_map/ppermute | solution.py:373
  105.0 0.6 shard_map.131
  105.6 1.7 %collective-permute-done.18 = bf16[1,2,2,168,512]{4,3,2,1,0:T(8,128)(2,1)S(1)} collective-permute-done((bf16[1,2,2,168,512]{4,3,2,1,0:T(8,128)(2,1)S(1)}, bf16[1,2,2,168,512]{4,3,2,1,0:T(8,128)(2,1)S(1)}, u32[]{:S(2)}, u32[]{:S(2)}) %collective-permute-start.18) | collective-permute-done | bytes 688160 | tf_op jit(solution)/shard_map/ppermute | solution.py:373
  107.3 0.6 shard_map.132
  108.0 0.5 collective-permute-start.20
  108.4 3.1 %collective-permute-start.22 = (bf16[1,1,1,168,512]{4,3,2,1,0:T(8,128)(2,1)S(1)}, bf16[1,1,1,168,512]{4,3,2,1,0:T(8,128)(2,1)S(1)}, u32[]{:S(2)}, u32[]{:S(2)}) collective-permute-start(bf16[1,1,1,168,512]{4,3,2,1,0:T(8,128)(2,1)S(1)} %bitcast.63), channel_id=1, source_target_pairs={{0,8},{1,9},{2,10},{3,11},{4,12},{5,13},{6,14},{7,15},{8,0},{9,1},... | collective-permute-start | bytes 516104 | tf_op jit(solution)/shard_map/ppermute | solution.py:373
  111.5 0.6 shard_map.129
  112.1 6.3 %collective-permute-done.20 = bf16[1,1,2,168,512]{4,3,2,1,0:T(8,128)(2,1)S(1)} collective-permute-done((bf16[1,1,2,168,512]{4,3,2,1,0:T(8,128)(2,1)S(1)}, bf16[1,1,2,168,512]{4,3,2,1,0:T(8,128)(2,1)S(1)}, u32[]{:S(2)}, u32[]{:S(2)}) %collective-permute-start.20) | collective-permute-done | bytes 344096 | tf_op jit(solution)/shard_map/ppermute | solution.py:373
  118.4 0.6 shard_map.134
  119.0 0.4 collective-permute-start.21
  119.4 0.6 shard_map.135
  120.0 0.6 shard_map.133
  120.6 6.3 %collective-permute-done.21 = bf16[1,1,1,168,512]{4,3,2,1,0:T(8,128)(2,1)S(1)} collective-permute-done((bf16[1,1,1,168,512]{4,3,2,1,0:T(8,128)(2,1)S(1)}, bf16[1,1,1,168,512]{4,3,2,1,0:T(8,128)(2,1)S(1)}, u32[]{:S(2)}, u32[]{:S(2)}) %collective-permute-start.21) | collective-permute-done | bytes 172064 | tf_op jit(solution)/shard_map/ppermute | solution.py:373
  126.9 0.9 shard_map.136
  (20 shorter events, 0.1 us)
Async XLA Ops:
  3.3 23.7 %copy-start.2 = (bf16[160,512]{1,0:T(8,128)(2,1)S(1)}, bf16[160,512]{1,0:T(8,128)(2,1)}, u32[]{:S(2)}) copy-start(bf16[160,512]{1,0:T(8,128)(2,1)} %get-tuple-element.62) | copy-start | bytes 491524
  3.3 5.6 %collective-permute-start.1 = (f32[1,3,128]{2,1,0:T(4,128)}, f32[1,3,128]{2,1,0:T(4,128)S(1)}, u32[]{:S(2)}, u32[]{:S(2)}) collective-permute-start(f32[1,3,128]{2,1,0:T(4,128)} %bitcast.74), channel_id=1, source_target_pairs={{0,2},{1,3},{2,0},{3,1},{4,6},{5,7},{6,4},{7,5},{8,10},{9,11},{10,... | collective-permute-start | bytes 4616 | tf_op jit(solution)/shard_map/ppermute | solution.py:373
  6.4 11.0 %collective-permute-start = (bf16[1,176,512]{2,1,0:T(8,128)(2,1)}, bf16[1,176,512]{2,1,0:T(8,128)(2,1)S(1)}, u32[]{:S(2)}, u32[]{:S(2)}) collective-permute-start(bf16[1,176,512]{2,1,0:T(8,128)(2,1)} %bitcast.69), channel_id=1, source_target_pairs={{0,8},{1,9},{2,10},{3,11},{4,12},{5,13},{6,14},{7,15},{8,0},{9,1},... | collective-permute-start | bytes 540680 | tf_op jit(solution)/shard_map/ppermute | solution.py:373
  9.7 3.6 %collective-permute-start.2 = (f32[2,3,128]{2,1,0:T(4,128)S(1)}, f32[2,3,128]{2,1,0:T(4,128)S(1)}, u32[]{:S(2)}, u32[]{:S(2)}) collective-permute-start(f32[2,3,128]{2,1,0:T(4,128)S(1)} %maximum_select_fusion.8), channel_id=1, source_target_pairs={{0,4},{1,5},{2,6},{3,7},{4,0},{5,1},{6,2},{7,3},{8,12},{9,13},{10,... | collective-permute-start | bytes 9224 | tf_op jit(solution)/shard_map/ppermute | solution.py:373
  18.4 8.7 %collective-permute-start.3 = (bf16[2,176,512]{2,1,0:T(8,128)(2,1)S(1)}, bf16[2,176,512]{2,1,0:T(8,128)(2,1)S(1)}, u32[]{:S(2)}, u32[]{:S(2)}) collective-permute-start(bf16[2,176,512]{2,1,0:T(8,128)(2,1)S(1)} %maximum_select_fusion.4), channel_id=1, source_target_pairs={{0,2},{1,5},{2,0},{3,7},{4,6},{5,1},{6,4},{7,3},{8,10},{9,13},{10,... | collective-permute-start | bytes 1081352 | tf_op jit(solution)/shard_map/ppermute | solution.py:373
  19.6 4.6 %collective-permute-start.4 = (f32[4,3,128]{2,1,0:T(4,128)S(1)}, f32[4,3,128]{2,1,0:T(4,128)S(1)}, u32[]{:S(2)}, u32[]{:S(2)}) collective-permute-start(f32[4,3,128]{2,1,0:T(4,128)S(1)} %maximum_select_fusion.7), channel_id=1, source_target_pairs={{0,8},{1,9},{2,10},{3,11},{4,12},{5,13},{6,14},{7,15},{8,0},{9,1},... | collective-permute-start | bytes 18440 | tf_op jit(solution)/shard_map/ppermute | solution.py:373
  19.7 7.4 %collective-permute-start.5 = (bf16[1,160,512]{2,1,0:T(8,128)(2,1)}, bf16[1,160,512]{2,1,0:T(8,128)(2,1)S(1)}, u32[]{:S(2)}, u32[]{:S(2)}) collective-permute-start(bf16[1,160,512]{2,1,0:T(8,128)(2,1)} %bitcast.71), channel_id=1, source_target_pairs={{0,8},{1,9},{2,10},{3,11},{4,12},{5,13},{6,14},{7,15},{8,0},{9,1},... | collective-permute-start | bytes 491528 | tf_op jit(solution)/shard_map/ppermute | solution.py:373
  26.9 5.8 %copy-start.1 = (bf16[528,128]{1,0:T(8,128)(2,1)S(1)}, bf16[528,128]{1,0:T(8,128)(2,1)}, u32[]{:S(2)}) copy-start(bf16[528,128]{1,0:T(8,128)(2,1)} %get-tuple-element.74.own_ref.norm_ref) | copy-start | bytes 405508
  26.9 11.1 %copy-start.4 = (bf16[272,128]{1,0:T(8,128)(2,1)S(1)}, bf16[272,128]{1,0:T(8,128)(2,1)}, u32[]{:S(2)}) copy-start(bf16[272,128]{1,0:T(8,128)(2,1)} %get-tuple-element.75) | copy-start | bytes 208900
  26.9 14.9 %copy-start.3 = (bf16[272,128]{1,0:T(8,128)(2,1)S(1)}, bf16[272,128]{1,0:T(8,128)(2,1)}, u32[]{:S(2)}) copy-start(bf16[272,128]{1,0:T(8,128)(2,1)} %get-tuple-element.76) | copy-start | bytes 208900
  27.2 18.2 %collective-permute-start.6 = (bf16[4,176,512]{2,1,0:T(8,128)(2,1)S(1)}, bf16[4,176,512]{2,1,0:T(8,128)(2,1)S(1)}, u32[]{:S(2)}, u32[]{:S(2)}) collective-permute-start(bf16[4,176,512]{2,1,0:T(8,128)(2,1)S(1)} %maximum_select_fusion.2), channel_id=1, source_target_pairs={{0,4},{1,3},{2,6},{3,1},{4,0},{5,7},{6,2},{7,5},{8,12},{9,11},{10,... | collective-permute-start | bytes 2162696 | tf_op jit(solution)/shard_map/ppermute | solution.py:373
  31.3 10.5 %collective-permute-start.7 = (bf16[2,160,512]{2,1,0:T(8,128)(2,1)S(1)}, bf16[2,160,512]{2,1,0:T(8,128)(2,1)S(1)}, u32[]{:S(2)}, u32[]{:S(2)}) collective-permute-start(bf16[2,160,512]{2,1,0:T(8,128)(2,1)S(1)} %maximum_select_fusion.5), channel_id=1, source_target_pairs={{0,2},{1,5},{2,0},{3,7},{4,6},{5,1},{6,4},{7,3},{8,10},{9,13},{10,... | collective-permute-start | bytes 983048 | tf_op jit(solution)/shard_map/ppermute | solution.py:373
  32.6 15.8 %collective-permute-start.9 = (bf16[528,128]{1,0:T(8,128)(2,1)S(1)}, bf16[528,128]{1,0:T(8,128)(2,1)S(1)}, u32[]{:S(2)}, u32[]{:S(2)}) collective-permute-start(bf16[528,128]{1,0:T(8,128)(2,1)S(1)} %copy-done.1), channel_id=1, source_target_pairs={{2,4},{4,2},{6,8},{8,6},{10,12},{12,10},{3,5},{5,3},{7,9},{9,7},{1... | collective-permute-start | bytes 405512 | tf_op jit(solution)/shard_map/ppermute | solution.py:431
  33.3 15.2 %collective-permute-start.8 = (bf16[528,128]{1,0:T(8,128)(2,1)S(1)}, bf16[528,128]{1,0:T(8,128)(2,1)S(1)}, u32[]{:S(2)}, u32[]{:S(2)}) collective-permute-start(bf16[528,128]{1,0:T(8,128)(2,1)S(1)} %copy-done.1), channel_id=1, source_target_pairs={{0,2},{1,3},{2,0},{3,1},{4,6},{5,7},{6,4},{7,5},{8,10},{9,11},{10,... | collective-permute-start | bytes 405512 | tf_op jit(solution)/shard_map/ppermute | solution.py:373
  38.0 10.4 %collective-permute-start.10 = (bf16[272,128]{1,0:T(8,128)(2,1)S(1)}, bf16[272,128]{1,0:T(8,128)(2,1)S(1)}, u32[]{:S(2)}, u32[]{:S(2)}) collective-permute-start(bf16[272,128]{1,0:T(8,128)(2,1)S(1)} %copy-done.4), channel_id=1, source_target_pairs={{0,4},{1,5},{2,6},{3,7},{4,0},{5,1},{6,2},{7,3},{8,12},{9,13},{10,... | collective-permute-start | bytes 208904 | tf_op jit(solution)/shard_map/ppermute | solution.py:373
  41.8 6.7 %collective-permute-start.11 = (bf16[272,128]{1,0:T(8,128)(2,1)S(1)}, bf16[272,128]{1,0:T(8,128)(2,1)S(1)}, u32[]{:S(2)}, u32[]{:S(2)}) collective-permute-start(bf16[272,128]{1,0:T(8,128)(2,1)S(1)} %copy-done.3), channel_id=1, source_target_pairs={{4,8},{8,4},{6,10},{10,6},{5,9},{9,5},{7,11},{11,7},{20,24},{24,20... | collective-permute-start | bytes 208904 | tf_op jit(solution)/shard_map/ppermute | solution.py:431
  42.7 10.6 %copy-start = (s32[3]{0:T(128)S(1)}, s32[3]{0:T(128)}, u32[]{:S(2)}) copy-start(s32[3]{0:T(128)} %pad_add_fusion.scalar_ref) | copy-start | bytes 40
  48.5 4.9 %collective-permute-start.13 = (bf16[8,176,512]{2,1,0:T(8,128)(2,1)S(1)}, bf16[8,176,512]{2,1,0:T(8,128)(2,1)S(1)}, u32[]{:S(2)}, u32[]{:S(2)}) collective-permute-start(bf16[8,176,512]{2,1,0:T(8,128)(2,1)S(1)} %maximum_select_fusion.here_ref), channel_id=1, source_target_pairs={{0,1},{1,0},{2,3},{3,2},{4,5},{5,4},{6,7},{7,6},{8,9},{9,8},{10,11... | collective-permute-start | bytes 4325384 | tf_op jit(solution)/shard_map/ppermute | solution.py:373
  50.5 11.5 %collective-permute-start.12 = (bf16[4,160,512]{2,1,0:T(8,128)(2,1)S(1)}, bf16[4,160,512]{2,1,0:T(8,128)(2,1)S(1)}, u32[]{:S(2)}, u32[]{:S(2)}) collective-permute-start(bf16[4,160,512]{2,1,0:T(8,128)(2,1)S(1)} %maximum_select_fusion.3), channel_id=1, source_target_pairs={{0,4},{1,3},{2,6},{3,1},{4,0},{5,7},{6,2},{7,5},{8,12},{9,11},{10,... | collective-permute-start | bytes 1966088 | tf_op jit(solution)/shard_map/ppermute | solution.py:373
  62.2 3.1 %collective-permute-start.14 = (bf16[8,160,512]{2,1,0:T(8,128)(2,1)S(1)}, bf16[8,160,512]{2,1,0:T(8,128)(2,1)S(1)}, u32[]{:S(2)}, u32[]{:S(2)}) collective-permute-start(bf16[8,160,512]{2,1,0:T(8,128)(2,1)S(1)} %maximum_select_fusion.1.here_ref), channel_id=1, source_target_pairs={{0,1},{1,0},{2,3},{3,2},{4,5},{5,4},{6,7},{7,6},{8,9},{9,8},{10,11... | collective-permute-start | bytes 3932168 | tf_op jit(solution)/shard_map/ppermute | solution.py:373
  76.3 3.6 %collective-permute-start.15 = (bf16[8,168,512]{2,1,0:T(8,128)(2,1)S(1)}, bf16[8,168,512]{2,1,0:T(8,128)(2,1)S(1)}, u32[]{:S(2)}, u32[]{:S(2)}) collective-permute-start(bf16[8,168,512]{2,1,0:T(8,128)(2,1)S(1)} %get-tuple-element.92), channel_id=1, source_target_pairs={{0,1},{1,0},{2,3},{3,2},{4,5},{5,4},{6,7},{7,6},{8,9},{9,8},{10,11... | collective-permute-start | bytes 4128776 | tf_op jit(solution)/shard_map/ppermute | solution.py:373
  79.8 3.2 %collective-permute-start.16 = (bf16[8,168,512]{2,1,0:T(8,128)(2,1)S(1)}, bf16[8,168,512]{2,1,0:T(8,128)(2,1)S(1)}, u32[]{:S(2)}, u32[]{:S(2)}) collective-permute-start(bf16[8,168,512]{2,1,0:T(8,128)(2,1)S(1)} %get-tuple-element.102), channel_id=1, source_target_pairs={{0,1},{1,0},{2,3},{3,2},{4,5},{5,4},{6,7},{7,6},{8,9},{9,8},{10,11... | collective-permute-start | bytes 4128776 | tf_op jit(solution)/shard_map/ppermute | solution.py:373
  81.0 11.0 %collective-permute-start.17 = (bf16[1,2,2,168,512]{4,3,2,1,0:T(8,128)(2,1)S(1)}, bf16[1,2,2,168,512]{4,3,2,1,0:T(8,128)(2,1)S(1)}, u32[]{:S(2)}, u32[]{:S(2)}) collective-permute-start(bf16[1,2,2,168,512]{4,3,2,1,0:T(8,128)(2,1)S(1)} %bitcast.58), channel_id=1, source_target_pairs={{0,2},{1,5},{2,0},{3,7},{4,6},{5,1},{6,4},{7,3},{8,10},{9,13},{10,... | collective-permute-start | bytes 2064392 | tf_op jit(solution)/shard_map/ppermute | solution.py:373
  92.6 14.7 %collective-permute-start.18 = (bf16[1,2,2,168,512]{4,3,2,1,0:T(8,128)(2,1)S(1)}, bf16[1,2,2,168,512]{4,3,2,1,0:T(8,128)(2,1)S(1)}, u32[]{:S(2)}, u32[]{:S(2)}) collective-permute-start(bf16[1,2,2,168,512]{4,3,2,1,0:T(8,128)(2,1)S(1)} %bitcast.57), channel_id=1, source_target_pairs={{0,2},{1,5},{2,0},{3,7},{4,6},{5,1},{6,4},{7,3},{8,10},{9,13},{10,... | collective-permute-start | bytes 2064392 | tf_op jit(solution)/shard_map/ppermute | solution.py:373
  94.0 11.0 %collective-permute-start.19 = (bf16[1,1,2,168,512]{4,3,2,1,0:T(8,128)(2,1)S(1)}, bf16[1,1,2,168,512]{4,3,2,1,0:T(8,128)(2,1)S(1)}, u32[]{:S(2)}, u32[]{:S(2)}) collective-permute-start(bf16[1,1,2,168,512]{4,3,2,1,0:T(8,128)(2,1)S(1)} %bitcast.61), channel_id=1, source_target_pairs={{0,4},{1,3},{2,6},{3,1},{4,0},{5,7},{6,2},{7,5},{8,12},{9,11},{10,... | collective-permute-start | bytes 1032200 | tf_op jit(solution)/shard_map/ppermute | solution.py:373
  108.0 10.4 %collective-permute-start.20 = (bf16[1,1,2,168,512]{4,3,2,1,0:T(8,128)(2,1)S(1)}, bf16[1,1,2,168,512]{4,3,2,1,0:T(8,128)(2,1)S(1)}, u32[]{:S(2)}, u32[]{:S(2)}) collective-permute-start(bf16[1,1,2,168,512]{4,3,2,1,0:T(8,128)(2,1)S(1)} %bitcast.62), channel_id=1, source_target_pairs={{0,4},{1,3},{2,6},{3,1},{4,0},{5,7},{6,2},{7,5},{8,12},{9,11},{10,... | collective-permute-start | bytes 1032200 | tf_op jit(solution)/shard_map/ppermute | solution.py:373
  108.4 12.2 %collective-permute-start.22 = (bf16[1,1,1,168,512]{4,3,2,1,0:T(8,128)(2,1)S(1)}, bf16[1,1,1,168,512]{4,3,2,1,0:T(8,128)(2,1)S(1)}, u32[]{:S(2)}, u32[]{:S(2)}) collective-permute-start(bf16[1,1,1,168,512]{4,3,2,1,0:T(8,128)(2,1)S(1)} %bitcast.63), channel_id=1, source_target_pairs={{0,8},{1,9},{2,10},{3,11},{4,12},{5,13},{6,14},{7,15},{8,0},{9,1},... | collective-permute-start | bytes 516104 | tf_op jit(solution)/shard_map/ppermute | solution.py:373
  119.0 7.9 %collective-permute-start.21 = (bf16[1,1,1,168,512]{4,3,2,1,0:T(8,128)(2,1)S(1)}, bf16[1,1,1,168,512]{4,3,2,1,0:T(8,128)(2,1)S(1)}, u32[]{:S(2)}, u32[]{:S(2)}) collective-permute-start(bf16[1,1,1,168,512]{4,3,2,1,0:T(8,128)(2,1)S(1)} %bitcast.66), channel_id=1, source_target_pairs={{0,8},{1,9},{2,10},{3,11},{4,12},{5,13},{6,14},{7,15},{8,0},{9,1},... | collective-permute-start | bytes 516104 | tf_op jit(solution)/shard_map/ppermute | solution.py:373

commit v12 on v11

--- a/solution.py
+++ b/solution.py
@@ -56,6 +56,7 @@
 
 
 LABEL_ROWS = 16
+WIDE_ROWS = 8
 
 
 def scan(feat, forget):
@@ -96,7 +97,7 @@
         [out_ref[k * more : (k + 1) * more, :] for k in range(c // out_ref.shape[1])], axis=1)
 
 
-def norm_kernel(scalar_ref, feat_ref, keep_ref, mass_ref, weight_ref, carry_ref, label_ref, out_ref, low_ref, high_ref):
+def norm_kernel(scalar_ref, feat_ref, keep_ref, mass_ref, weight_ref, carry_ref, label_ref, out_ref, wide_ref, high_ref):
     bands = feat_ref.shape[1]
     mass0 = jnp.zeros((1, bands), F32)
     weight0 = jnp.zeros((1, bands), F32)
@@ -111,13 +112,18 @@
     normed = (feat_ref[...] / jnp.sqrt(mass / weight + LEVEL_FLOOR)).astype(BF16)
     label = jnp.concatenate(
         [label_ref[...].astype(F32), jnp.zeros((LABEL_ROWS - label_ref.shape[0], bands), F32)]).astype(BF16)
-    part = low_ref.shape[0] - LABEL_ROWS
+    part = high_ref.shape[0] - LABEL_ROWS
     first, last = normed[:part], normed[normed.shape[0] - part :]
     upper = (scalar_ref[1] >> 1) & 1 == 1
-    for ref, value in (
-        (out_ref, normed), (low_ref, jnp.where(upper, first, last)), (high_ref, jnp.where(upper, last, first))):
+    for ref, value in ((out_ref, normed), (high_ref, jnp.where(upper, last, first))):
         ref[:LABEL_ROWS, :] = label
         ref[LABEL_ROWS:, :] = value
+    high = normed.shape[0] * bands // wide_ref.shape[1]
+    wide_ref[high:, :] = jnp.zeros((WIDE_ROWS, wide_ref.shape[1]), BF16)
+    for q in range(wide_ref.shape[1] // bands):
+        lanes = slice(q * bands, (q + 1) * bands)
+        wide_ref[:high, lanes] = normed[q * high : (q + 1) * high]
+        wide_ref[high : high + 1, lanes] = label_ref[q : q + 1, :].astype(F32).astype(BF16)
 
 
 def rows_of(value):
@@ -175,24 +181,45 @@
     return slice(i * TILE + offset, (i + 1) * TILE + offset)
 
 
-def halo(scalar_ref, own_ref, even_ref, odd_ref, low_ref, high_ref, window_ref, label_ref):
-    steps, part = own_ref.shape[0] - LABEL_ROWS, low_ref.shape[0] - LABEL_ROWS
-    lane = own_ref.shape[1]
+def halo(scalar_ref, own_ref, first_ref, second_ref, odd_ref, high_ref, window_ref, label_ref):
+    part, lane = high_ref.shape[0] - LABEL_ROWS, own_ref.shape[1]
+    core = scalar_ref[0]
     odd, upper = scalar_ref[1] & 1 == 1, (scalar_ref[1] >> 1) & 1 == 1
-    even, uneven, low, high = even_ref[...], odd_ref[...], low_ref[...], high_ref[...]
+
+    def rows_form(wide):
+        count = wide.shape[0] - WIDE_ROWS
+        groups = [slice(q * lane, (q + 1) * lane) for q in range(wide.shape[1] // lane)]
+        rows = jnp.concatenate([wide[:count, g] for g in groups])
+        labels = jnp.concatenate([wide[count:, g].astype(F32)[:1] for g in groups])
+        return rows, labels
+
+    first, second = first_ref[...], second_ref[...]
+    near, near_labels = rows_form(jnp.where(core == 0, first, second))
+    far, far_labels = rows_form(jnp.where(core == 0, second, first))
+    high, far_high = high_ref[LABEL_ROWS:, :], far.shape[0] - part
+    uneven = odd_ref[LABEL_ROWS:, :]
+    count = part // lane
+
+    def labels_of(ref):
+        return ref[:LABEL_ROWS, :].astype(F32)
+
+    parts = [
+        (jnp.where(upper, far[far_high:], high), None),
+        (jnp.where(odd, near, uneven), None),
+        (own_ref[LABEL_ROWS:, :], labels_of(own_ref)[: near_labels.shape[0]]),
+        (jnp.where(odd, uneven, near), jnp.where(odd, labels_of(odd_ref)[: near_labels.shape[0]], near_labels)),
+        (jnp.where(upper, high, far[:part]), jnp.where(upper, labels_of(high_ref)[:count], far_labels[:count])),
+    ]
     at, row = 0, 0
-    for value, ahead in ((jnp.where(upper, low, high), False), (jnp.where(odd, even, uneven), False),
-                         (own_ref[...], True), (jnp.where(odd, uneven, even), True),
-                         (jnp.where(upper, high, low), True)):
-        count = value.shape[0] - LABEL_ROWS
-        window_ref[at : at + count, :] = value[LABEL_ROWS:]
-        at += count
-        if ahead:
-            label_ref[row : row + count // lane, :] = value[:LABEL_ROWS].astype(F32)[: count // lane]
-            row += count // lane
-
-
-def forward_first(before, steps, scalar_ref, own_ref, even_ref, odd_ref, low_ref, high_ref,
+    for value, labels in parts:
+        window_ref[at : at + value.shape[0], :] = value
+        at += value.shape[0]
+        if labels is not None:
+            label_ref[row : row + labels.shape[0], :] = labels
+            row += labels.shape[0]
+
+
+def forward_first(before, steps, scalar_ref, own_ref, near_ref, far_ref, odd_ref, high_ref,
                   here_ref, there_ref, h1_ref, w_out_ref, label_ref, kept_ref, gated_ref, slope_ref, conv_ref, res_ref,
                   norm_ref, h0_ref, in_ref, out_ref):
     rows = h0_ref.shape[0]
@@ -200,7 +227,7 @@
     d = rows - h1_ref.shape[0]
     core = scalar_ref[0]
     place(core, (here_ref, there_ref), conv_ref, res_ref, in_ref, out_ref)
-    halo(scalar_ref, own_ref, even_ref, odd_ref, low_ref, high_ref, norm_ref, label_ref)
+    halo(scalar_ref, own_ref, near_ref, far_ref, odd_ref, high_ref, norm_ref, label_ref)
     w_out_ref[...] = rows_of(out_ref[...])
     w_in = rows_of(in_ref[...])
     for i in range(rows // steps):
@@ -470,12 +497,22 @@
     for links in far:
         held1 = grow(held1, links)
     label_rows = steps // bands
-    normed, low, high = call(norm_kernel, [((LABEL_ROWS + r, bands), BF16) for r in (steps, reach - steps, reach - steps)],
+    wide_rows = steps * bands // c + WIDE_ROWS
+    normed, wide, high = call(
+        norm_kernel,
+        [((LABEL_ROWS + steps, bands), BF16), ((wide_rows, c), BF16), ((LABEL_ROWS + reach - steps, bands), BF16)],
                              [], 10**8,
                      scalars, feat, keep, mass, weight, carry, labels[0].reshape(label_rows, bands), limit=FIRST_LIMIT)
-    held0, normed, low, high, held1 = together(held0, normed, low, high, held1)
-    held0, held1 = grow(held0, turns[1]), grow(held1, turns[0])
-    around = [swap(normed, (NEAR, NEAR)), exchange(normed, 1), swap(low, (FAR, FAR)), exchange(high, 2)]
+    held0, normed, wide, high, held1 = together(held0, normed, wide, high, held1)
+
+    def grow_with(held, links):
+        rows = held.shape[0] * held.shape[1]
+        other = swap(jnp.concatenate([held.reshape(rows, c), wide]), links)
+        return arranged(held, other[:rows].reshape(held.shape), links), other[rows:]
+
+    held0, second_wide = grow_with(held0, turns[1])
+    held1, first_wide = grow_with(held1, turns[0])
+    around = [first_wide, second_wide, exchange(normed, 1), exchange(high, 2)]
     held0, held1, around = together(held0, held1, around)
 
     def both_cores(held):

time: 128 us -> 128 us (level)
  starting transfers between devices: 37.9 us -> 30.2 us
  waiting for transfers between devices: 50.4 us -> 56 us
    ppermute x21 -> x19, starting transfers between devices: 36.4 us -> 28.7 us  [swap(): return lax.ppermute(value, ('tm', 'site'), pairs)]
    ppermute x21 -> x19, waiting for transfers between devices: 50.4 us -> 56 us  [swap(): return lax.ppermute(value, ('tm', 'site'), pairs)]
  transfers between devices with their start and end apart: 23 -> 21, of which waited for: 14 -> 14; matrix products, arithmetic and copies ran while one was open for 2% -> 3% of each run, Pallas kernels for 14% -> 15%
where the time goes in v12:
time: 128 us
  waiting for transfers between devices  56 us (44%)
  Pallas kernels  34.5 us (27%)
  starting transfers between devices  30.2 us (24%)
  other arithmetic  4.56 us (4%)
  between operations  1.59 us (1%)
    ppermute x19, waiting for transfers between devices, swap(): return lax.ppermute(value, ('tm', 'site'), pairs)  56 us
    pallas_call x18, Pallas kernels, call(): pl.pallas_call(kernel, out_shape=[jax.ShapeDtypeStruct(s, d) for s, d in...  34.5 us
    ppermute x19, starting transfers between devices, swap(): return lax.ppermute(value, ('tm', 'site'), pairs)  28.7 us
    select_n x9, other arithmetic, arranged(): jnp.where(my_bit(links) == 0, jnp.concatenate([held, other]), jnp.concate...  3.12 us
  transfers between devices with their start and end apart: 21, of which 14 were waited for; matrix products, arithmetic and copies ran while one was open for 3% of the time, Pallas kernels for 15%

profile of v12, /device:TPU:0, one launch (start us, length us, event | category | flops | bytes accessed | tf_op | source)
XLA Modules:
  0.0 127.6 jit_solution(12206940579909634622)
XLA Ops:
  0.6 2.7 %shard_map.119 = (f32[512,128]{1,0:T(8,128)}, f32[512,128]{1,0:T(8,128)}, f32[512,128]{1,0:T(8,128)}, f32[3,128]{1,0:T(4,128)}, bf16[176,512]{1,0:T(8,128)(2,1)}, /*index=5*/bf16[160,512]{1,0:T(8,128)(2,1)}) custom-call(f32[512,128]{1,0:T(8,128)} %bitcast.75, f32[512,128]{1,0:T(8,128)} %bitcast.84, bf16[2,64,1024]{2,1,0:T(8,128)(2,1)} %conv_ref.1, ...), custom_call_target="tpu_custom_call" | custom-call | flops 2000000000 | bytes 2000384 | tf_op jit(solution)/shard_map/pallas_call | solution.py:38
  3.3 3.0 %collective-permute-start.1 = (f32[1,3,128]{2,1,0:T(4,128)}, f32[1,3,128]{2,1,0:T(4,128)S(1)}, u32[]{:S(2)}, u32[]{:S(2)}) collective-permute-start(f32[1,3,128]{2,1,0:T(4,128)} %bitcast.82), channel_id=1, source_target_pairs={{0,2},{1,3},{2,0},{3,1},{4,6},{5,7},{6,4},{7,5},{8,10},{9,11},{10,... | collective-permute-start | bytes 4616 | tf_op jit(solution)/shard_map/ppermute | solution.py:400
  6.4 2.6 %collective-permute-start = (bf16[1,176,512]{2,1,0:T(8,128)(2,1)}, bf16[1,176,512]{2,1,0:T(8,128)(2,1)S(1)}, u32[]{:S(2)}, u32[]{:S(2)}) collective-permute-start(bf16[1,176,512]{2,1,0:T(8,128)(2,1)} %bitcast.77), channel_id=1, source_target_pairs={{0,8},{1,9},{2,10},{3,11},{4,12},{5,13},{6,14},{7,15},{8,0},{9,1},... | collective-permute-start | bytes 540680 | tf_op jit(solution)/shard_map/ppermute | solution.py:400
  9.0 0.8 maximum_select_fusion.8
  9.7 1.6 %collective-permute-start.2 = (f32[2,3,128]{2,1,0:T(4,128)S(1)}, f32[2,3,128]{2,1,0:T(4,128)S(1)}, u32[]{:S(2)}, u32[]{:S(2)}) collective-permute-start(f32[2,3,128]{2,1,0:T(4,128)S(1)} %maximum_select_fusion.8), channel_id=1, source_target_pairs={{0,4},{1,5},{2,6},{3,7},{4,0},{5,1},{6,2},{7,3},{8,12},{9,13},{10,... | collective-permute-start | bytes 9224 | tf_op jit(solution)/shard_map/ppermute | solution.py:400
  11.3 2.0 %collective-permute-done.2 = f32[2,3,128]{2,1,0:T(4,128)S(1)} collective-permute-done((f32[2,3,128]{2,1,0:T(4,128)S(1)}, f32[2,3,128]{2,1,0:T(4,128)S(1)}, u32[]{:S(2)}, u32[]{:S(2)}) %collective-permute-start.2) | collective-permute-done | bytes 3104 | tf_op jit(solution)/shard_map/ppermute | solution.py:400
  13.3 4.0 %collective-permute-done = bf16[1,176,512]{2,1,0:T(8,128)(2,1)S(1)} collective-permute-done((bf16[1,176,512]{2,1,0:T(8,128)(2,1)}, bf16[1,176,512]{2,1,0:T(8,128)(2,1)S(1)}, u32[]{:S(2)}, u32[]{:S(2)}) %collective-permute-start) | collective-permute-done | bytes 180256 | tf_op jit(solution)/shard_map/ppermute | solution.py:400
  17.4 1.1 maximum_select_fusion.4
  18.4 0.5 collective-permute-start.3
  19.6 0.1 collective-permute-start.4
  19.7 2.9 %collective-permute-start.5 = (bf16[1,160,512]{2,1,0:T(8,128)(2,1)}, bf16[1,160,512]{2,1,0:T(8,128)(2,1)S(1)}, u32[]{:S(2)}, u32[]{:S(2)}) collective-permute-start(bf16[1,160,512]{2,1,0:T(8,128)(2,1)} %bitcast.79), channel_id=1, source_target_pairs={{0,8},{1,9},{2,10},{3,11},{4,12},{5,13},{6,14},{7,15},{8,0},{9,1},... | collective-permute-start | bytes 491528 | tf_op jit(solution)/shard_map/ppermute | solution.py:400
  22.6 0.6 pad_add_fusion.scalar_ref
  23.2 1.0 collective-permute-done.4
  24.2 0.6 maximum_select_fusion.6.carry_ref
  24.8 2.2 %shard_map.120 = (bf16[528,128]{1,0:T(8,128)(2,1)}, bf16[136,512]{1,0:T(8,128)(2,1)}, bf16[272,128]{1,0:T(8,128)(2,1)}) custom-call(s32[3]{0:T(128)} %pad_add_fusion.scalar_ref, f32[512,128]{1,0:T(8,128)} %bitcast.76, f32[512,128]{1,0:T(8,128)} %get-tuple-element.64.keep_ref, f32[512,128]{1,0:T(8,128)} %get-tuple-element.65.mass_ref, ...), custom_call_target="tpu_custom_call" | custom-call | flops 100000000 | bytes 1406988 | tf_op jit(solution)/shard_map/pallas_call | solution.py:38
  27.0 0.1 collective-permute-done.5
  27.1 0.1 maximum_select_fusion.2
  27.3 0.6 copy-done.2
  27.9 0.1 pad_maximum_fusion
  28.0 3.4 %collective-permute-start.6 = (bf16[840,512]{1,0:T(8,128)(2,1)S(1)}, bf16[840,512]{1,0:T(8,128)(2,1)S(1)}, u32[]{:S(2)}, u32[]{:S(2)}) collective-permute-start(bf16[840,512]{1,0:T(8,128)(2,1)S(1)} %pad_maximum_fusion), channel_id=1, source_target_pairs={{0,4},{1,3},{2,6},{3,1},{4,0},{5,7},{6,2},{7,5},{8,12},{9,11},{10,... | collective-permute-start | bytes 2580488 | tf_op jit(solution)/shard_map/ppermute | solution.py:400
  31.4 0.8 pad_maximum_fusion.1
  32.2 1.3 %collective-permute-start.7 = (bf16[456,512]{1,0:T(8,128)(2,1)}, bf16[456,512]{1,0:T(8,128)(2,1)S(1)}, u32[]{:S(2)}, u32[]{:S(2)}) collective-permute-start(bf16[456,512]{1,0:T(8,128)(2,1)} %pad_maximum_fusion.1), channel_id=1, source_target_pairs={{0,2},{1,5},{2,0},{3,7},{4,6},{5,1},{6,4},{7,3},{8,10},{9,13},{10,... | collective-permute-start | bytes 1400840 | tf_op jit(solution)/shard_map/ppermute | solution.py:400
  33.5 0.7 collective-permute-start.9
  34.2 0.8 collective-permute-start.8
  35.0 11.0 %collective-permute-done.7 = bf16[456,512]{1,0:T(8,128)(2,1)S(1)} collective-permute-done((bf16[456,512]{1,0:T(8,128)(2,1)}, bf16[456,512]{1,0:T(8,128)(2,1)S(1)}, u32[]{:S(2)}, u32[]{:S(2)}) %collective-permute-start.7) | collective-permute-done | bytes 466976 | tf_op jit(solution)/shard_map/ppermute | solution.py:400
  46.1 0.1 maximum_select_fusion.3
  46.2 1.4 %collective-permute-done.6 = bf16[840,512]{1,0:T(8,128)(2,1)S(1)} collective-permute-done((bf16[840,512]{1,0:T(8,128)(2,1)S(1)}, bf16[840,512]{1,0:T(8,128)(2,1)S(1)}, u32[]{:S(2)}, u32[]{:S(2)}) %collective-permute-start.6) | collective-permute-done | bytes 860192 | tf_op jit(solution)/shard_map/ppermute | solution.py:400
  47.6 0.0 copy-start
  47.6 0.2 maximum_select_fusion.here_ref
  47.9 3.2 %collective-permute-start.11 = (bf16[8,176,512]{2,1,0:T(8,128)(2,1)S(1)}, bf16[8,176,512]{2,1,0:T(8,128)(2,1)S(1)}, u32[]{:S(2)}, u32[]{:S(2)}) collective-permute-start(bf16[8,176,512]{2,1,0:T(8,128)(2,1)S(1)} %maximum_select_fusion.here_ref), channel_id=1, source_target_pairs={{0,1},{1,0},{2,3},{3,2},{4,5},{5,4},{6,7},{7,6},{8,9},{9,8},{10,11... | collective-permute-start | bytes 4325384 | tf_op jit(solution)/shard_map/ppermute | solution.py:400
  51.1 1.7 %collective-permute-start.10 = (bf16[4,160,512]{2,1,0:T(8,128)(2,1)S(1)}, bf16[4,160,512]{2,1,0:T(8,128)(2,1)S(1)}, u32[]{:S(2)}, u32[]{:S(2)}) collective-permute-start(bf16[4,160,512]{2,1,0:T(8,128)(2,1)S(1)} %maximum_select_fusion.3), channel_id=1, source_target_pairs={{0,4},{1,3},{2,6},{3,1},{4,0},{5,7},{6,2},{7,5},{8,12},{9,11},{10,... | collective-permute-start | bytes 1966088 | tf_op jit(solution)/shard_map/ppermute | solution.py:400
  52.8 1.1 collective-permute-done.11.there_ref
  53.9 6.6 %shard_map.121 = (bf16[1792,512]{1,0:T(8,128)(2,1)S(1)}, bf16[512,128]{1,0:T(8,128)(2,1)S(1)}, f32[10,128]{1,0:T(8,128)S(1)}, bf16[768,512]{1,0:T(8,128)(2,1)S(1...) custom-call(s32[3]{0:T(128)S(1)} %copy-done, ...), custom_call_target="tpu_custom_call" | custom-call | flops 5637144576 | bytes 10978316 | tf_op jit(solution)/shard_map/pallas_call | solution.py:38
  60.5 1.1 collective-permute-done.10
  61.7 0.2 maximum_select_fusion.1.here_ref
  61.9 0.1 collective-permute-start.12
  61.9 3.0 %collective-permute-done.12.there_ref = bf16[8,160,512]{2,1,0:T(8,128)(2,1)S(1)} collective-permute-done((bf16[8,160,512]{2,1,0:T(8,128)(2,1)S(1)}, bf16[8,160,512]{2,1,0:T(8,128)(2,1)S(1)}, u32[]{:S(2)}, u32[]{:S(2)}) %collective-permute-start.12) | collective-permute-done | bytes 1310752 | tf_op jit(solution)/shard_map/ppermute | solution.py:400
  65.0 11.1 %shard_map.122 = (f32[4,128]{1,0:T(4,128)}, bf16[8,168,512]{2,1,0:T(8,128)(2,1)S(1)}, bf16[8,168,512]{2,1,0:T(8,128)(2,1)S(1)}, f32[512,512]{1,0:T(8,128)S(1)}, ...) custom-call(s32[3]{0:T(128)S(1)} %copy-done, bf16[1792,512]{1,0:T(8,128)(2,1)S(1)} %get-tuple-element.84.h1_ref, ...), custom_call_target="tpu_custom_call" | custom-call | flops 7381975040 | bytes 12590092 | tf_op jit(solution)/shard_map/pallas_call | solution.py:38
  76.0 0.2 collective-permute-start.13
  76.2 3.3 %shard_map.123 = (bf16[8,168,512]{2,1,0:T(8,128)(2,1)S(1)}, bf16[8,168,512]{2,1,0:T(8,128)(2,1)S(1)}) custom-call(s32[3]{0:T(128)S(1)} %copy-done, bf16[768,1024]{1,0:T(8,128)(2,1)S(1)} %get-tuple-element.93.back_ref, f32[512,512]{1,0:T(8,128)S(1)} %get-tuple-element.94.grad_ref, bf16[512,512]{1,0:T(8,128)(2,1)S(1)} %get-tuple-element.95.round_ref, ...), custom_call_target="tpu_custom_call" | custom-call | flops 2415919104 | bytes 9441292 | tf_op jit(solution)/shard_map/pallas_call | solution.py:38
  79.6 0.4 collective-permute-start.14
  80.0 0.7 shard_map.126
  80.8 2.2 %collective-permute-start.15 = (bf16[1,2,2,168,512]{4,3,2,1,0:T(8,128)(2,1)S(1)}, bf16[1,2,2,168,512]{4,3,2,1,0:T(8,128)(2,1)S(1)}, u32[]{:S(2)}, u32[]{:S(2)}) collective-permute-start(bf16[1,2,2,168,512]{4,3,2,1,0:T(8,128)(2,1)S(1)} %bitcast.62), channel_id=1, source_target_pairs={{0,2},{1,5},{2,0},{3,7},{4,6},{5,1},{6,4},{7,3},{8,10},{9,13},{10,... | collective-permute-start | bytes 2064392 | tf_op jit(solution)/shard_map/ppermute | solution.py:400
  83.0 0.7 shard_map.125
  83.7 0.7 shard_map.127
  84.4 7.5 %collective-permute-done.15 = bf16[1,2,2,168,512]{4,3,2,1,0:T(8,128)(2,1)S(1)} collective-permute-done((bf16[1,2,2,168,512]{4,3,2,1,0:T(8,128)(2,1)S(1)}, bf16[1,2,2,168,512]{4,3,2,1,0:T(8,128)(2,1)S(1)}, u32[]{:S(2)}, u32[]{:S(2)}) %collective-permute-start.15) | collective-permute-done | bytes 688160 | tf_op jit(solution)/shard_map/ppermute | solution.py:400
  91.9 0.6 shard_map.128
  92.6 2.1 %collective-permute-start.16 = (bf16[1,2,2,168,512]{4,3,2,1,0:T(8,128)(2,1)S(1)}, bf16[1,2,2,168,512]{4,3,2,1,0:T(8,128)(2,1)S(1)}, u32[]{:S(2)}, u32[]{:S(2)}) collective-permute-start(bf16[1,2,2,168,512]{4,3,2,1,0:T(8,128)(2,1)S(1)} %bitcast.61), channel_id=1, source_target_pairs={{0,2},{1,5},{2,0},{3,7},{4,6},{5,1},{6,4},{7,3},{8,10},{9,13},{10,... | collective-permute-start | bytes 2064392 | tf_op jit(solution)/shard_map/ppermute | solution.py:400
  94.6 0.7 shard_map.124
  95.4 0.6 shard_map.130
  96.0 9.4 %collective-permute-done.17 = bf16[1,1,2,168,512]{4,3,2,1,0:T(8,128)(2,1)S(1)} collective-permute-done((bf16[1,1,2,168,512]{4,3,2,1,0:T(8,128)(2,1)S(1)}, bf16[1,1,2,168,512]{4,3,2,1,0:T(8,128)(2,1)S(1)}, u32[]{:S(2)}, u32[]{:S(2)}) %collective-permute-start.17) | collective-permute-done | bytes 344096 | tf_op jit(solution)/shard_map/ppermute | solution.py:400
  105.4 0.6 shard_map.131
  106.0 0.8 collective-permute-done.16
  106.8 0.6 shard_map.132
  107.5 0.8 collective-permute-start.18
  108.3 2.1 %collective-permute-start.20 = (bf16[1,1,1,168,512]{4,3,2,1,0:T(8,128)(2,1)S(1)}, bf16[1,1,1,168,512]{4,3,2,1,0:T(8,128)(2,1)S(1)}, u32[]{:S(2)}, u32[]{:S(2)}) collective-permute-start(bf16[1,1,1,168,512]{4,3,2,1,0:T(8,128)(2,1)S(1)} %bitcast.67), channel_id=1, source_target_pairs={{0,8},{1,9},{2,10},{3,11},{4,12},{5,13},{6,14},{7,15},{8,0},{9,1},... | collective-permute-start | bytes 516104 | tf_op jit(solution)/shard_map/ppermute | solution.py:400
  110.4 0.6 shard_map.129
  111.0 7.5 %collective-permute-done.18 = bf16[1,1,2,168,512]{4,3,2,1,0:T(8,128)(2,1)S(1)} collective-permute-done((bf16[1,1,2,168,512]{4,3,2,1,0:T(8,128)(2,1)S(1)}, bf16[1,1,2,168,512]{4,3,2,1,0:T(8,128)(2,1)S(1)}, u32[]{:S(2)}, u32[]{:S(2)}) %collective-permute-start.18) | collective-permute-done | bytes 344096 | tf_op jit(solution)/shard_map/ppermute | solution.py:400
  118.5 0.6 shard_map.134
  119.1 0.4 collective-permute-start.19
  119.6 0.6 shard_map.135
  120.2 0.6 shard_map.133
  120.8 5.9 %collective-permute-done.19 = bf16[1,1,1,168,512]{4,3,2,1,0:T(8,128)(2,1)S(1)} collective-permute-done((bf16[1,1,1,168,512]{4,3,2,1,0:T(8,128)(2,1)S(1)}, bf16[1,1,1,168,512]{4,3,2,1,0:T(8,128)(2,1)S(1)}, u32[]{:S(2)}, u32[]{:S(2)}) %collective-permute-start.19) | collective-permute-done | bytes 172064 | tf_op jit(solution)/shard_map/ppermute | solution.py:400
  126.7 0.9 shard_map.136
  (22 shorter events, 0.2 us)
Async XLA Ops:
  3.3 23.7 %copy-start.3 = (bf16[160,512]{1,0:T(8,128)(2,1)S(1)}, bf16[160,512]{1,0:T(8,128)(2,1)}, u32[]{:S(2)}) copy-start(bf16[160,512]{1,0:T(8,128)(2,1)} %get-tuple-element.62) | copy-start | bytes 491524
  3.3 5.6 %collective-permute-start.1 = (f32[1,3,128]{2,1,0:T(4,128)}, f32[1,3,128]{2,1,0:T(4,128)S(1)}, u32[]{:S(2)}, u32[]{:S(2)}) collective-permute-start(f32[1,3,128]{2,1,0:T(4,128)} %bitcast.82), channel_id=1, source_target_pairs={{0,2},{1,3},{2,0},{3,1},{4,6},{5,7},{6,4},{7,5},{8,10},{9,11},{10,... | collective-permute-start | bytes 4616 | tf_op jit(solution)/shard_map/ppermute | solution.py:400
  6.4 11.0 %collective-permute-start = (bf16[1,176,512]{2,1,0:T(8,128)(2,1)}, bf16[1,176,512]{2,1,0:T(8,128)(2,1)S(1)}, u32[]{:S(2)}, u32[]{:S(2)}) collective-permute-start(bf16[1,176,512]{2,1,0:T(8,128)(2,1)} %bitcast.77), channel_id=1, source_target_pairs={{0,8},{1,9},{2,10},{3,11},{4,12},{5,13},{6,14},{7,15},{8,0},{9,1},... | collective-permute-start | bytes 540680 | tf_op jit(solution)/shard_map/ppermute | solution.py:400
  9.7 3.6 %collective-permute-start.2 = (f32[2,3,128]{2,1,0:T(4,128)S(1)}, f32[2,3,128]{2,1,0:T(4,128)S(1)}, u32[]{:S(2)}, u32[]{:S(2)}) collective-permute-start(f32[2,3,128]{2,1,0:T(4,128)S(1)} %maximum_select_fusion.8), channel_id=1, source_target_pairs={{0,4},{1,5},{2,6},{3,7},{4,0},{5,1},{6,2},{7,3},{8,12},{9,13},{10,... | collective-permute-start | bytes 9224 | tf_op jit(solution)/shard_map/ppermute | solution.py:400
  18.4 8.7 %collective-permute-start.3 = (bf16[2,176,512]{2,1,0:T(8,128)(2,1)S(1)}, bf16[2,176,512]{2,1,0:T(8,128)(2,1)S(1)}, u32[]{:S(2)}, u32[]{:S(2)}) collective-permute-start(bf16[2,176,512]{2,1,0:T(8,128)(2,1)S(1)} %maximum_select_fusion.4), channel_id=1, source_target_pairs={{0,2},{1,5},{2,0},{3,7},{4,6},{5,1},{6,4},{7,3},{8,10},{9,13},{10,... | collective-permute-start | bytes 1081352 | tf_op jit(solution)/shard_map/ppermute | solution.py:400
  19.6 4.6 %collective-permute-start.4 = (f32[4,3,128]{2,1,0:T(4,128)S(1)}, f32[4,3,128]{2,1,0:T(4,128)S(1)}, u32[]{:S(2)}, u32[]{:S(2)}) collective-permute-start(f32[4,3,128]{2,1,0:T(4,128)S(1)} %maximum_select_fusion.7), channel_id=1, source_target_pairs={{0,8},{1,9},{2,10},{3,11},{4,12},{5,13},{6,14},{7,15},{8,0},{9,1},... | collective-permute-start | bytes 18440 | tf_op jit(solution)/shard_map/ppermute | solution.py:400
  19.7 7.4 %collective-permute-start.5 = (bf16[1,160,512]{2,1,0:T(8,128)(2,1)}, bf16[1,160,512]{2,1,0:T(8,128)(2,1)S(1)}, u32[]{:S(2)}, u32[]{:S(2)}) collective-permute-start(bf16[1,160,512]{2,1,0:T(8,128)(2,1)} %bitcast.79), channel_id=1, source_target_pairs={{0,8},{1,9},{2,10},{3,11},{4,12},{5,13},{6,14},{7,15},{8,0},{9,1},... | collective-permute-start | bytes 491528 | tf_op jit(solution)/shard_map/ppermute | solution.py:400
  27.0 0.9 copy-start.2
  27.3 6.2 %copy-start.4 = (bf16[272,128]{1,0:T(8,128)(2,1)S(1)}, bf16[272,128]{1,0:T(8,128)(2,1)}, u32[]{:S(2)}) copy-start(bf16[272,128]{1,0:T(8,128)(2,1)} %get-tuple-element.76) | copy-start | bytes 208900
  27.3 6.9 %copy-start.1 = (bf16[528,128]{1,0:T(8,128)(2,1)S(1)}, bf16[528,128]{1,0:T(8,128)(2,1)}, u32[]{:S(2)}) copy-start(bf16[528,128]{1,0:T(8,128)(2,1)} %get-tuple-element.75.own_ref.norm_ref) | copy-start | bytes 405508
  28.0 19.6 %collective-permute-start.6 = (bf16[840,512]{1,0:T(8,128)(2,1)S(1)}, bf16[840,512]{1,0:T(8,128)(2,1)S(1)}, u32[]{:S(2)}, u32[]{:S(2)}) collective-permute-start(bf16[840,512]{1,0:T(8,128)(2,1)S(1)} %pad_maximum_fusion), channel_id=1, source_target_pairs={{0,4},{1,3},{2,6},{3,1},{4,0},{5,7},{6,2},{7,5},{8,12},{9,11},{10,... | collective-permute-start | bytes 2580488 | tf_op jit(solution)/shard_map/ppermute | solution.py:400
  32.2 13.8 %collective-permute-start.7 = (bf16[456,512]{1,0:T(8,128)(2,1)}, bf16[456,512]{1,0:T(8,128)(2,1)S(1)}, u32[]{:S(2)}, u32[]{:S(2)}) collective-permute-start(bf16[456,512]{1,0:T(8,128)(2,1)} %pad_maximum_fusion.1), channel_id=1, source_target_pairs={{0,2},{1,5},{2,0},{3,7},{4,6},{5,1},{6,4},{7,3},{8,10},{9,13},{10,... | collective-permute-start | bytes 1400840 | tf_op jit(solution)/shard_map/ppermute | solution.py:400
  33.5 14.4 %collective-permute-start.9 = (bf16[272,128]{1,0:T(8,128)(2,1)S(1)}, bf16[272,128]{1,0:T(8,128)(2,1)S(1)}, u32[]{:S(2)}, u32[]{:S(2)}) collective-permute-start(bf16[272,128]{1,0:T(8,128)(2,1)S(1)} %copy-done.4), channel_id=1, source_target_pairs={{4,8},{8,4},{6,10},{10,6},{5,9},{9,5},{7,11},{11,7},{20,24},{24,20... | collective-permute-start | bytes 208904 | tf_op jit(solution)/shard_map/ppermute | solution.py:458
  34.2 13.7 %collective-permute-start.8 = (bf16[528,128]{1,0:T(8,128)(2,1)S(1)}, bf16[528,128]{1,0:T(8,128)(2,1)S(1)}, u32[]{:S(2)}, u32[]{:S(2)}) collective-permute-start(bf16[528,128]{1,0:T(8,128)(2,1)S(1)} %copy-done.1), channel_id=1, source_target_pairs={{2,4},{4,2},{6,8},{8,6},{10,12},{12,10},{3,5},{5,3},{7,9},{9,7},{1... | collective-permute-start | bytes 405512 | tf_op jit(solution)/shard_map/ppermute | solution.py:458
  47.6 6.3 %copy-start = (s32[3]{0:T(128)S(1)}, s32[3]{0:T(128)}, u32[]{:S(2)}) copy-start(s32[3]{0:T(128)} %pad_add_fusion.scalar_ref) | copy-start | bytes 40
  47.9 6.0 %collective-permute-start.11 = (bf16[8,176,512]{2,1,0:T(8,128)(2,1)S(1)}, bf16[8,176,512]{2,1,0:T(8,128)(2,1)S(1)}, u32[]{:S(2)}, u32[]{:S(2)}) collective-permute-start(bf16[8,176,512]{2,1,0:T(8,128)(2,1)S(1)} %maximum_select_fusion.here_ref), channel_id=1, source_target_pairs={{0,1},{1,0},{2,3},{3,2},{4,5},{5,4},{6,7},{7,6},{8,9},{9,8},{10,11... | collective-permute-start | bytes 4325384 | tf_op jit(solution)/shard_map/ppermute | solution.py:400
  51.1 10.6 %collective-permute-start.10 = (bf16[4,160,512]{2,1,0:T(8,128)(2,1)S(1)}, bf16[4,160,512]{2,1,0:T(8,128)(2,1)S(1)}, u32[]{:S(2)}, u32[]{:S(2)}) collective-permute-start(bf16[4,160,512]{2,1,0:T(8,128)(2,1)S(1)} %maximum_select_fusion.3), channel_id=1, source_target_pairs={{0,4},{1,3},{2,6},{3,1},{4,0},{5,7},{6,2},{7,5},{8,12},{9,11},{10,... | collective-permute-start | bytes 1966088 | tf_op jit(solution)/shard_map/ppermute | solution.py:400
  61.9 3.1 %collective-permute-start.12 = (bf16[8,160,512]{2,1,0:T(8,128)(2,1)S(1)}, bf16[8,160,512]{2,1,0:T(8,128)(2,1)S(1)}, u32[]{:S(2)}, u32[]{:S(2)}) collective-permute-start(bf16[8,160,512]{2,1,0:T(8,128)(2,1)S(1)} %maximum_select_fusion.1.here_ref), channel_id=1, source_target_pairs={{0,1},{1,0},{2,3},{3,2},{4,5},{5,4},{6,7},{7,6},{8,9},{9,8},{10,11... | collective-permute-start | bytes 3932168 | tf_op jit(solution)/shard_map/ppermute | solution.py:400
  76.0 3.6 %collective-permute-start.13 = (bf16[8,168,512]{2,1,0:T(8,128)(2,1)S(1)}, bf16[8,168,512]{2,1,0:T(8,128)(2,1)S(1)}, u32[]{:S(2)}, u32[]{:S(2)}) collective-permute-start(bf16[8,168,512]{2,1,0:T(8,128)(2,1)S(1)} %get-tuple-element.92), channel_id=1, source_target_pairs={{0,1},{1,0},{2,3},{3,2},{4,5},{5,4},{6,7},{7,6},{8,9},{9,8},{10,11... | collective-permute-start | bytes 4128776 | tf_op jit(solution)/shard_map/ppermute | solution.py:400
  79.6 4.1 %collective-permute-start.14 = (bf16[8,168,512]{2,1,0:T(8,128)(2,1)S(1)}, bf16[8,168,512]{2,1,0:T(8,128)(2,1)S(1)}, u32[]{:S(2)}, u32[]{:S(2)}) collective-permute-start(bf16[8,168,512]{2,1,0:T(8,128)(2,1)S(1)} %get-tuple-element.102), channel_id=1, source_target_pairs={{0,1},{1,0},{2,3},{3,2},{4,5},{5,4},{6,7},{7,6},{8,9},{9,8},{10,11... | collective-permute-start | bytes 4128776 | tf_op jit(solution)/shard_map/ppermute | solution.py:400
  80.8 11.2 %collective-permute-start.15 = (bf16[1,2,2,168,512]{4,3,2,1,0:T(8,128)(2,1)S(1)}, bf16[1,2,2,168,512]{4,3,2,1,0:T(8,128)(2,1)S(1)}, u32[]{:S(2)}, u32[]{:S(2)}) collective-permute-start(bf16[1,2,2,168,512]{4,3,2,1,0:T(8,128)(2,1)S(1)} %bitcast.62), channel_id=1, source_target_pairs={{0,2},{1,5},{2,0},{3,7},{4,6},{5,1},{6,4},{7,3},{8,10},{9,13},{10,... | collective-permute-start | bytes 2064392 | tf_op jit(solution)/shard_map/ppermute | solution.py:400
  92.6 14.3 %collective-permute-start.16 = (bf16[1,2,2,168,512]{4,3,2,1,0:T(8,128)(2,1)S(1)}, bf16[1,2,2,168,512]{4,3,2,1,0:T(8,128)(2,1)S(1)}, u32[]{:S(2)}, u32[]{:S(2)}) collective-permute-start(bf16[1,2,2,168,512]{4,3,2,1,0:T(8,128)(2,1)S(1)} %bitcast.61), channel_id=1, source_target_pairs={{0,2},{1,5},{2,0},{3,7},{4,6},{5,1},{6,4},{7,3},{8,10},{9,13},{10,... | collective-permute-start | bytes 2064392 | tf_op jit(solution)/shard_map/ppermute | solution.py:400
  94.6 10.8 %collective-permute-start.17 = (bf16[1,1,2,168,512]{4,3,2,1,0:T(8,128)(2,1)S(1)}, bf16[1,1,2,168,512]{4,3,2,1,0:T(8,128)(2,1)S(1)}, u32[]{:S(2)}, u32[]{:S(2)}) collective-permute-start(bf16[1,1,2,168,512]{4,3,2,1,0:T(8,128)(2,1)S(1)} %bitcast.65), channel_id=1, source_target_pairs={{0,4},{1,3},{2,6},{3,1},{4,0},{5,7},{6,2},{7,5},{8,12},{9,11},{10,... | collective-permute-start | bytes 1032200 | tf_op jit(solution)/shard_map/ppermute | solution.py:400
  107.5 11.1 %collective-permute-start.18 = (bf16[1,1,2,168,512]{4,3,2,1,0:T(8,128)(2,1)S(1)}, bf16[1,1,2,168,512]{4,3,2,1,0:T(8,128)(2,1)S(1)}, u32[]{:S(2)}, u32[]{:S(2)}) collective-permute-start(bf16[1,1,2,168,512]{4,3,2,1,0:T(8,128)(2,1)S(1)} %bitcast.66), channel_id=1, source_target_pairs={{0,4},{1,3},{2,6},{3,1},{4,0},{5,7},{6,2},{7,5},{8,12},{9,11},{10,... | collective-permute-start | bytes 1032200 | tf_op jit(solution)/shard_map/ppermute | solution.py:400
  108.3 12.5 %collective-permute-start.20 = (bf16[1,1,1,168,512]{4,3,2,1,0:T(8,128)(2,1)S(1)}, bf16[1,1,1,168,512]{4,3,2,1,0:T(8,128)(2,1)S(1)}, u32[]{:S(2)}, u32[]{:S(2)}) collective-permute-start(bf16[1,1,1,168,512]{4,3,2,1,0:T(8,128)(2,1)S(1)} %bitcast.67), channel_id=1, source_target_pairs={{0,8},{1,9},{2,10},{3,11},{4,12},{5,13},{6,14},{7,15},{8,0},{9,1},... | collective-permute-start | bytes 516104 | tf_op jit(solution)/shard_map/ppermute | solution.py:400
  119.1 7.6 %collective-permute-start.19 = (bf16[1,1,1,168,512]{4,3,2,1,0:T(8,128)(2,1)S(1)}, bf16[1,1,1,168,512]{4,3,2,1,0:T(8,128)(2,1)S(1)}, u32[]{:S(2)}, u32[]{:S(2)}) collective-permute-start(bf16[1,1,1,168,512]{4,3,2,1,0:T(8,128)(2,1)S(1)} %bitcast.70), channel_id=1, source_target_pairs={{0,8},{1,9},{2,10},{3,11},{4,12},{5,13},{6,14},{7,15},{8,0},{9,1},... | collective-permute-start | bytes 516104 | tf_op jit(solution)/shard_map/ppermute | solution.py:400

commit v13 on v12

--- a/solution.py
+++ b/solution.py
@@ -510,8 +510,22 @@
         other = swap(jnp.concatenate([held.reshape(rows, c), wide]), links)
         return arranged(held, other[:rows].reshape(held.shape), links), other[rows:]
 
+    def grow_split(held, links):
+        groups, count = lax.axis_size("groups"), held.shape[1] // 2
+        if groups % 2 or held.shape[1] % 2:
+            return grow_with(held, links)
+        plane = lax.axis_index("groups") & 1
+        part = lax.dynamic_slice_in_dim(held, plane * count, count, 1)
+        rows = part.shape[0] * count
+        other = swap(jnp.concatenate([part.reshape(rows, c), wide]), links)
+        came = other[:rows].reshape(part.shape)
+        passed = lax.ppermute(came, "groups", [(i, i ^ 1) for i in range(groups)])
+        full = jnp.where(
+            plane == 0, jnp.concatenate([came, passed], axis=1), jnp.concatenate([passed, came], axis=1))
+        return arranged(held, full, links), other[rows:]
+
     held0, second_wide = grow_with(held0, turns[1])
-    held1, first_wide = grow_with(held1, turns[0])
+    held1, first_wide = grow_split(held1, turns[0])
     around = [first_wide, second_wide, exchange(normed, 1), exchange(high, 2)]
     held0, held1, around = together(held0, held1, around)
 

time: 128 us -> 132 us (1.031)
  starting transfers between devices: 30.2 us -> 32.9 us
  waiting for transfers between devices: 56 us -> 57.6 us
    ppermute x0 -> x1, waiting for transfers between devices: none -> 4 us  [grow_split(): passed = lax.ppermute(came, 'groups', [(i, i ^ 1) for i in range(groups)])]
    ppermute x19, waiting for transfers between devices: 56 us -> 53.6 us  [swap(): return lax.ppermute(value, ('tm', 'site'), pairs)]
    ppermute x0 -> x1, starting transfers between devices: none -> 1.56 us  [grow_split(): passed = lax.ppermute(came, 'groups', [(i, i ^ 1) for i in range(groups)])]
  transfers between devices with their start and end apart: 21 -> 22, of which waited for: 14 -> 14; matrix products, arithmetic and copies ran while one was open for 3% -> 2% of each run, Pallas kernels for 15% -> 14%
where the time goes in v13:
time: 132 us; the launch traced here: 131 us
  waiting for transfers between devices  57.6 us (44%)
  Pallas kernels  34.5 us (26%)
  starting transfers between devices  32.9 us (25%)
  other arithmetic  3.88 us (3%)
  between operations  1.6 us (1%)
    ppermute x19, waiting for transfers between devices, swap(): return lax.ppermute(value, ('tm', 'site'), pairs)  53.6 us
    pallas_call x18, Pallas kernels, call(): pl.pallas_call(kernel, out_shape=[jax.ShapeDtypeStruct(s, d) for s, d in...  34.5 us
    ppermute x19, starting transfers between devices, swap(): return lax.ppermute(value, ('tm', 'site'), pairs)  29.9 us
    ppermute x1, waiting for transfers between devices, grow_split(): passed = lax.ppermute(came, 'groups', [(i, i ^ 1) for i in range(groups)])  4 us
    select_n x9, other arithmetic, arranged(): jnp.where(my_bit(links) == 0, jnp.concatenate([held, other]), jnp.concate...  3.12 us
  transfers between devices with their start and end apart: 22, of which 14 were waited for; matrix products, arithmetic and copies ran while one was open for 2% of the time, Pallas kernels for 14%

profile of v13, /device:TPU:0, one launch (start us, length us, event | category | flops | bytes accessed | tf_op | source)
XLA Modules:
  0.0 131.3 jit_solution(5738510033402572582)
XLA Ops:
  0.6 2.7 %shard_map.119 = (f32[512,128]{1,0:T(8,128)}, f32[512,128]{1,0:T(8,128)}, f32[512,128]{1,0:T(8,128)}, f32[3,128]{1,0:T(4,128)}, bf16[176,512]{1,0:T(8,128)(2,1)}, /*index=5*/bf16[160,512]{1,0:T(8,128)(2,1)}) custom-call(f32[512,128]{1,0:T(8,128)} %bitcast.76, f32[512,128]{1,0:T(8,128)} %bitcast.85, bf16[2,64,1024]{2,1,0:T(8,128)(2,1)} %conv_ref.1, ...), custom_call_target="tpu_custom_call" | custom-call | flops 2000000000 | bytes 2000384 | tf_op jit(solution)/shard_map/pallas_call | solution.py:38
  3.3 3.0 %collective-permute-start.1 = (f32[1,3,128]{2,1,0:T(4,128)}, f32[1,3,128]{2,1,0:T(4,128)S(1)}, u32[]{:S(2)}, u32[]{:S(2)}) collective-permute-start(f32[1,3,128]{2,1,0:T(4,128)} %bitcast.83), channel_id=1, source_target_pairs={{0,2},{1,3},{2,0},{3,1},{4,6},{5,7},{6,4},{7,5},{8,10},{9,11},{10,... | collective-permute-start | bytes 4616 | tf_op jit(solution)/shard_map/ppermute | solution.py:400
  6.4 2.6 %collective-permute-start = (bf16[1,176,512]{2,1,0:T(8,128)(2,1)}, bf16[1,176,512]{2,1,0:T(8,128)(2,1)S(1)}, u32[]{:S(2)}, u32[]{:S(2)}) collective-permute-start(bf16[1,176,512]{2,1,0:T(8,128)(2,1)} %bitcast.78), channel_id=1, source_target_pairs={{0,8},{1,9},{2,10},{3,11},{4,12},{5,13},{6,14},{7,15},{8,0},{9,1},... | collective-permute-start | bytes 540680 | tf_op jit(solution)/shard_map/ppermute | solution.py:400
  9.0 0.8 maximum_select_fusion.9
  9.7 1.6 %collective-permute-start.2 = (f32[2,3,128]{2,1,0:T(4,128)S(1)}, f32[2,3,128]{2,1,0:T(4,128)S(1)}, u32[]{:S(2)}, u32[]{:S(2)}) collective-permute-start(f32[2,3,128]{2,1,0:T(4,128)S(1)} %maximum_select_fusion.9), channel_id=1, source_target_pairs={{0,4},{1,5},{2,6},{3,7},{4,0},{5,1},{6,2},{7,3},{8,12},{9,13},{10,... | collective-permute-start | bytes 9224 | tf_op jit(solution)/shard_map/ppermute | solution.py:400
  11.3 2.0 %collective-permute-done.2 = f32[2,3,128]{2,1,0:T(4,128)S(1)} collective-permute-done((f32[2,3,128]{2,1,0:T(4,128)S(1)}, f32[2,3,128]{2,1,0:T(4,128)S(1)}, u32[]{:S(2)}, u32[]{:S(2)}) %collective-permute-start.2) | collective-permute-done | bytes 3104 | tf_op jit(solution)/shard_map/ppermute | solution.py:400
  13.3 4.0 %collective-permute-done = bf16[1,176,512]{2,1,0:T(8,128)(2,1)S(1)} collective-permute-done((bf16[1,176,512]{2,1,0:T(8,128)(2,1)}, bf16[1,176,512]{2,1,0:T(8,128)(2,1)S(1)}, u32[]{:S(2)}, u32[]{:S(2)}) %collective-permute-start) | collective-permute-done | bytes 180256 | tf_op jit(solution)/shard_map/ppermute | solution.py:400
  17.4 1.1 maximum_select_fusion.4
  18.4 0.5 collective-permute-start.3
  19.6 0.1 collective-permute-start.4
  19.7 2.9 %collective-permute-start.5 = (bf16[1,160,512]{2,1,0:T(8,128)(2,1)}, bf16[1,160,512]{2,1,0:T(8,128)(2,1)S(1)}, u32[]{:S(2)}, u32[]{:S(2)}) collective-permute-start(bf16[1,160,512]{2,1,0:T(8,128)(2,1)} %bitcast.80), channel_id=1, source_target_pairs={{0,8},{1,9},{2,10},{3,11},{4,12},{5,13},{6,14},{7,15},{8,0},{9,1},... | collective-permute-start | bytes 491528 | tf_op jit(solution)/shard_map/ppermute | solution.py:400
  22.6 0.6 pad_add_fusion.scalar_ref
  23.2 1.0 collective-permute-done.4
  24.2 0.6 maximum_select_fusion.7.carry_ref
  24.8 2.2 %shard_map.120 = (bf16[528,128]{1,0:T(8,128)(2,1)}, bf16[136,512]{1,0:T(8,128)(2,1)}, bf16[272,128]{1,0:T(8,128)(2,1)}) custom-call(s32[3]{0:T(128)} %pad_add_fusion.scalar_ref, f32[512,128]{1,0:T(8,128)} %bitcast.77, f32[512,128]{1,0:T(8,128)} %get-tuple-element.64.keep_ref, f32[512,128]{1,0:T(8,128)} %get-tuple-element.65.mass_ref, ...), custom_call_target="tpu_custom_call" | custom-call | flops 100000000 | bytes 1406988 | tf_op jit(solution)/shard_map/pallas_call | solution.py:38
  27.0 0.1 collective-permute-done.5
  27.1 0.1 maximum_select_fusion.2
  27.3 0.7 copy-done.2
  28.0 3.4 %collective-permute-start.6 = (bf16[840,512]{1,0:T(8,128)(2,1)S(1)}, bf16[840,512]{1,0:T(8,128)(2,1)S(1)}, u32[]{:S(2)}, u32[]{:S(2)}) collective-permute-start(bf16[840,512]{1,0:T(8,128)(2,1)S(1)} %pad_maximum_fusion), channel_id=1, source_target_pairs={{0,4},{1,3},{2,6},{3,1},{4,0},{5,7},{6,2},{7,5},{8,12},{9,11},{10,... | collective-permute-start | bytes 2580488 | tf_op jit(solution)/shard_map/ppermute | solution.py:400
  31.4 1.4 %collective-permute-start.7 = (bf16[296,512]{1,0:T(8,128)(2,1)S(1)}, bf16[296,512]{1,0:T(8,128)(2,1)S(1)}, u32[]{:S(2)}, u32[]{:S(2)}) collective-permute-start(bf16[296,512]{1,0:T(8,128)(2,1)S(1)} %pad_maximum_fusion.1), channel_id=1, source_target_pairs={{0,2},{1,5},{2,0},{3,7},{4,6},{5,1},{6,4},{7,3},{8,10},{9,13},{10,... | collective-permute-start | bytes 909320 | tf_op jit(solution)/shard_map/ppermute | solution.py:400
  32.8 8.7 %collective-permute-done.7 = bf16[296,512]{1,0:T(8,128)(2,1)S(1)} collective-permute-done((bf16[296,512]{1,0:T(8,128)(2,1)S(1)}, bf16[296,512]{1,0:T(8,128)(2,1)S(1)}, u32[]{:S(2)}, u32[]{:S(2)}) %collective-permute-start.7) | collective-permute-done | bytes 303136 | tf_op jit(solution)/shard_map/ppermute | solution.py:400
  41.5 1.6 %collective-permute-start.8 = (bf16[2,80,512]{2,1,0:T(8,128)(2,1)S(1)}, bf16[2,80,512]{2,1,0:T(8,128)(2,1)S(1)}, u32[]{:S(2)}, u32[]{:S(2)}) collective-permute-start(bf16[2,80,512]{2,1,0:T(8,128)(2,1)S(1)} %bitcast.73), channel_id=1, source_target_pairs={{0,16},{16,0},{1,17},{17,1},{2,18},{18,2},{3,19},{19,3},{4,20},{20... | collective-permute-start | bytes 491528 | tf_op jit(solution)/shard_map/ppermute | solution.py:522
  43.1 0.7 collective-permute-start.10
  43.7 0.8 collective-permute-start.9
  44.6 4.0 %collective-permute-done.8 = bf16[2,80,512]{2,1,0:T(8,128)(2,1)S(1)} collective-permute-done((bf16[2,80,512]{2,1,0:T(8,128)(2,1)S(1)}, bf16[2,80,512]{2,1,0:T(8,128)(2,1)S(1)}, u32[]{:S(2)}, u32[]{:S(2)}) %collective-permute-start.8) | collective-permute-done | bytes 163872 | tf_op jit(solution)/shard_map/ppermute | solution.py:522
  48.6 0.1 maximum_select_fusion.6
  48.7 0.1 maximum_select_fusion.3
  48.9 0.2 maximum_select_fusion.here_ref
  49.2 0.1 collective-permute-start.12
  49.3 8.7 %collective-permute-start.11 = (bf16[4,160,512]{2,1,0:T(8,128)(2,1)S(1)}, bf16[4,160,512]{2,1,0:T(8,128)(2,1)S(1)}, u32[]{:S(2)}, u32[]{:S(2)}) collective-permute-start(bf16[4,160,512]{2,1,0:T(8,128)(2,1)S(1)} %maximum_select_fusion.3), channel_id=1, source_target_pairs={{0,4},{1,3},{2,6},{3,1},{4,0},{5,7},{6,2},{7,5},{8,12},{9,11},{10,... | collective-permute-start | bytes 1966088 | tf_op jit(solution)/shard_map/ppermute | solution.py:400
  58.0 6.6 %shard_map.121 = (bf16[1792,512]{1,0:T(8,128)(2,1)S(1)}, bf16[512,128]{1,0:T(8,128)(2,1)S(1)}, f32[10,128]{1,0:T(8,128)S(1)}, bf16[768,512]{1,0:T(8,128)(2,1)S(1...) custom-call(s32[3]{0:T(128)S(1)} %copy-done, ...), custom_call_target="tpu_custom_call" | custom-call | flops 5637144576 | bytes 10978316 | tf_op jit(solution)/shard_map/pallas_call | solution.py:38
  64.6 1.9 %collective-permute-done.11 = bf16[4,160,512]{2,1,0:T(8,128)(2,1)S(1)} collective-permute-done((bf16[4,160,512]{2,1,0:T(8,128)(2,1)S(1)}, bf16[4,160,512]{2,1,0:T(8,128)(2,1)S(1)}, u32[]{:S(2)}, u32[]{:S(2)}) %collective-permute-start.11) | collective-permute-done | bytes 655392 | tf_op jit(solution)/shard_map/ppermute | solution.py:400
  66.5 0.2 maximum_select_fusion.1.here_ref
  66.8 0.1 collective-permute-start.13
  66.8 3.0 %collective-permute-done.13.there_ref = bf16[8,160,512]{2,1,0:T(8,128)(2,1)S(1)} collective-permute-done((bf16[8,160,512]{2,1,0:T(8,128)(2,1)S(1)}, bf16[8,160,512]{2,1,0:T(8,128)(2,1)S(1)}, u32[]{:S(2)}, u32[]{:S(2)}) %collective-permute-start.13) | collective-permute-done | bytes 1310752 | tf_op jit(solution)/shard_map/ppermute | solution.py:400
  69.9 11.1 %shard_map.122 = (f32[4,128]{1,0:T(4,128)}, bf16[8,168,512]{2,1,0:T(8,128)(2,1)S(1)}, bf16[8,168,512]{2,1,0:T(8,128)(2,1)S(1)}, f32[512,512]{1,0:T(8,128)S(1)}, ...) custom-call(s32[3]{0:T(128)S(1)} %copy-done, bf16[1792,512]{1,0:T(8,128)(2,1)S(1)} %get-tuple-element.84.h1_ref, ...), custom_call_target="tpu_custom_call" | custom-call | flops 7381975040 | bytes 12590092 | tf_op jit(solution)/shard_map/pallas_call | solution.py:38
  80.9 0.2 collective-permute-start.14
  81.1 3.3 %shard_map.123 = (bf16[8,168,512]{2,1,0:T(8,128)(2,1)S(1)}, bf16[8,168,512]{2,1,0:T(8,128)(2,1)S(1)}) custom-call(s32[3]{0:T(128)S(1)} %copy-done, bf16[768,1024]{1,0:T(8,128)(2,1)S(1)} %get-tuple-element.93.back_ref, f32[512,512]{1,0:T(8,128)S(1)} %get-tuple-element.94.grad_ref, bf16[512,512]{1,0:T(8,128)(2,1)S(1)} %get-tuple-element.95.round_ref, ...), custom_call_target="tpu_custom_call" | custom-call | flops 2415919104 | bytes 9441292 | tf_op jit(solution)/shard_map/pallas_call | solution.py:38
  84.5 0.4 collective-permute-start.15
  84.9 0.7 shard_map.126
  85.6 0.6 collective-permute-start.16
  86.3 0.7 shard_map.125
  87.0 0.7 collective-permute-done.15
  87.7 0.7 shard_map.127
  88.4 8.2 %collective-permute-done.16 = bf16[1,2,2,168,512]{4,3,2,1,0:T(8,128)(2,1)S(1)} collective-permute-done((bf16[1,2,2,168,512]{4,3,2,1,0:T(8,128)(2,1)S(1)}, bf16[1,2,2,168,512]{4,3,2,1,0:T(8,128)(2,1)S(1)}, u32[]{:S(2)}, u32[]{:S(2)}) %collective-permute-start.16) | collective-permute-done | bytes 688160 | tf_op jit(solution)/shard_map/ppermute | solution.py:400
  96.6 0.6 shard_map.128
  97.3 0.6 collective-permute-start.17
  97.9 2.0 %collective-permute-start.18 = (bf16[1,1,2,168,512]{4,3,2,1,0:T(8,128)(2,1)S(1)}, bf16[1,1,2,168,512]{4,3,2,1,0:T(8,128)(2,1)S(1)}, u32[]{:S(2)}, u32[]{:S(2)}) collective-permute-start(bf16[1,1,2,168,512]{4,3,2,1,0:T(8,128)(2,1)S(1)} %bitcast.65), channel_id=1, source_target_pairs={{0,4},{1,3},{2,6},{3,1},{4,0},{5,7},{6,2},{7,5},{8,12},{9,11},{10,... | collective-permute-start | bytes 1032200 | tf_op jit(solution)/shard_map/ppermute | solution.py:400
  99.9 0.7 shard_map.124
  100.6 0.6 shard_map.130
  101.3 7.6 %collective-permute-done.18 = bf16[1,1,2,168,512]{4,3,2,1,0:T(8,128)(2,1)S(1)} collective-permute-done((bf16[1,1,2,168,512]{4,3,2,1,0:T(8,128)(2,1)S(1)}, bf16[1,1,2,168,512]{4,3,2,1,0:T(8,128)(2,1)S(1)}, u32[]{:S(2)}, u32[]{:S(2)}) %collective-permute-start.18) | collective-permute-done | bytes 344096 | tf_op jit(solution)/shard_map/ppermute | solution.py:400
  108.9 0.6 shard_map.131
  109.5 2.5 %collective-permute-done.17 = bf16[1,2,2,168,512]{4,3,2,1,0:T(8,128)(2,1)S(1)} collective-permute-done((bf16[1,2,2,168,512]{4,3,2,1,0:T(8,128)(2,1)S(1)}, bf16[1,2,2,168,512]{4,3,2,1,0:T(8,128)(2,1)S(1)}, u32[]{:S(2)}, u32[]{:S(2)}) %collective-permute-start.17) | collective-permute-done | bytes 688160 | tf_op jit(solution)/shard_map/ppermute | solution.py:400
  112.0 0.6 shard_map.132
  112.6 0.5 collective-permute-start.19
  113.1 1.1 collective-permute-start.21
  114.1 0.6 shard_map.129
  114.8 7.8 %collective-permute-done.19 = bf16[1,1,2,168,512]{4,3,2,1,0:T(8,128)(2,1)S(1)} collective-permute-done((bf16[1,1,2,168,512]{4,3,2,1,0:T(8,128)(2,1)S(1)}, bf16[1,1,2,168,512]{4,3,2,1,0:T(8,128)(2,1)S(1)}, u32[]{:S(2)}, u32[]{:S(2)}) %collective-permute-start.19) | collective-permute-done | bytes 344096 | tf_op jit(solution)/shard_map/ppermute | solution.py:400
  122.6 0.6 shard_map.134
  123.2 0.1 collective-permute-start.20
  123.3 0.6 shard_map.135
  123.9 0.6 shard_map.133
  124.5 5.9 %collective-permute-done.20 = bf16[1,1,1,168,512]{4,3,2,1,0:T(8,128)(2,1)S(1)} collective-permute-done((bf16[1,1,1,168,512]{4,3,2,1,0:T(8,128)(2,1)S(1)}, bf16[1,1,1,168,512]{4,3,2,1,0:T(8,128)(2,1)S(1)}, u32[]{:S(2)}, u32[]{:S(2)}) %collective-permute-start.20) | collective-permute-done | bytes 172064 | tf_op jit(solution)/shard_map/ppermute | solution.py:400
  130.4 0.9 shard_map.136
  (24 shorter events, 0.2 us)
Async XLA Ops:
  3.3 23.7 %copy-start.3 = (bf16[160,512]{1,0:T(8,128)(2,1)S(1)}, bf16[160,512]{1,0:T(8,128)(2,1)}, u32[]{:S(2)}) copy-start(bf16[160,512]{1,0:T(8,128)(2,1)} %get-tuple-element.62) | copy-start | bytes 491524
  3.3 5.6 %collective-permute-start.1 = (f32[1,3,128]{2,1,0:T(4,128)}, f32[1,3,128]{2,1,0:T(4,128)S(1)}, u32[]{:S(2)}, u32[]{:S(2)}) collective-permute-start(f32[1,3,128]{2,1,0:T(4,128)} %bitcast.83), channel_id=1, source_target_pairs={{0,2},{1,3},{2,0},{3,1},{4,6},{5,7},{6,4},{7,5},{8,10},{9,11},{10,... | collective-permute-start | bytes 4616 | tf_op jit(solution)/shard_map/ppermute | solution.py:400
  6.4 11.0 %collective-permute-start = (bf16[1,176,512]{2,1,0:T(8,128)(2,1)}, bf16[1,176,512]{2,1,0:T(8,128)(2,1)S(1)}, u32[]{:S(2)}, u32[]{:S(2)}) collective-permute-start(bf16[1,176,512]{2,1,0:T(8,128)(2,1)} %bitcast.78), channel_id=1, source_target_pairs={{0,8},{1,9},{2,10},{3,11},{4,12},{5,13},{6,14},{7,15},{8,0},{9,1},... | collective-permute-start | bytes 540680 | tf_op jit(solution)/shard_map/ppermute | solution.py:400
  9.7 3.6 %collective-permute-start.2 = (f32[2,3,128]{2,1,0:T(4,128)S(1)}, f32[2,3,128]{2,1,0:T(4,128)S(1)}, u32[]{:S(2)}, u32[]{:S(2)}) collective-permute-start(f32[2,3,128]{2,1,0:T(4,128)S(1)} %maximum_select_fusion.9), channel_id=1, source_target_pairs={{0,4},{1,5},{2,6},{3,7},{4,0},{5,1},{6,2},{7,3},{8,12},{9,13},{10,... | collective-permute-start | bytes 9224 | tf_op jit(solution)/shard_map/ppermute | solution.py:400
  18.4 8.7 %collective-permute-start.3 = (bf16[2,176,512]{2,1,0:T(8,128)(2,1)S(1)}, bf16[2,176,512]{2,1,0:T(8,128)(2,1)S(1)}, u32[]{:S(2)}, u32[]{:S(2)}) collective-permute-start(bf16[2,176,512]{2,1,0:T(8,128)(2,1)S(1)} %maximum_select_fusion.4), channel_id=1, source_target_pairs={{0,2},{1,5},{2,0},{3,7},{4,6},{5,1},{6,4},{7,3},{8,10},{9,13},{10,... | collective-permute-start | bytes 1081352 | tf_op jit(solution)/shard_map/ppermute | solution.py:400
  19.6 4.6 %collective-permute-start.4 = (f32[4,3,128]{2,1,0:T(4,128)S(1)}, f32[4,3,128]{2,1,0:T(4,128)S(1)}, u32[]{:S(2)}, u32[]{:S(2)}) collective-permute-start(f32[4,3,128]{2,1,0:T(4,128)S(1)} %maximum_select_fusion.8), channel_id=1, source_target_pairs={{0,8},{1,9},{2,10},{3,11},{4,12},{5,13},{6,14},{7,15},{8,0},{9,1},... | collective-permute-start | bytes 18440 | tf_op jit(solution)/shard_map/ppermute | solution.py:400
  19.7 7.4 %collective-permute-start.5 = (bf16[1,160,512]{2,1,0:T(8,128)(2,1)}, bf16[1,160,512]{2,1,0:T(8,128)(2,1)S(1)}, u32[]{:S(2)}, u32[]{:S(2)}) collective-permute-start(bf16[1,160,512]{2,1,0:T(8,128)(2,1)} %bitcast.80), channel_id=1, source_target_pairs={{0,8},{1,9},{2,10},{3,11},{4,12},{5,13},{6,14},{7,15},{8,0},{9,1},... | collective-permute-start | bytes 491528 | tf_op jit(solution)/shard_map/ppermute | solution.py:400
  27.0 0.9 copy-start.2
  27.9 15.8 %copy-start.1 = (bf16[528,128]{1,0:T(8,128)(2,1)S(1)}, bf16[528,128]{1,0:T(8,128)(2,1)}, u32[]{:S(2)}) copy-start(bf16[528,128]{1,0:T(8,128)(2,1)} %get-tuple-element.75.own_ref.norm_ref) | copy-start | bytes 405508
  28.0 20.8 %collective-permute-start.6 = (bf16[840,512]{1,0:T(8,128)(2,1)S(1)}, bf16[840,512]{1,0:T(8,128)(2,1)S(1)}, u32[]{:S(2)}, u32[]{:S(2)}) collective-permute-start(bf16[840,512]{1,0:T(8,128)(2,1)S(1)} %pad_maximum_fusion), channel_id=1, source_target_pairs={{0,4},{1,3},{2,6},{3,1},{4,0},{5,7},{6,2},{7,5},{8,12},{9,11},{10,... | collective-permute-start | bytes 2580488 | tf_op jit(solution)/shard_map/ppermute | solution.py:400
  31.4 10.1 %collective-permute-start.7 = (bf16[296,512]{1,0:T(8,128)(2,1)S(1)}, bf16[296,512]{1,0:T(8,128)(2,1)S(1)}, u32[]{:S(2)}, u32[]{:S(2)}) collective-permute-start(bf16[296,512]{1,0:T(8,128)(2,1)S(1)} %pad_maximum_fusion.1), channel_id=1, source_target_pairs={{0,2},{1,5},{2,0},{3,7},{4,6},{5,1},{6,4},{7,3},{8,10},{9,13},{10,... | collective-permute-start | bytes 909320 | tf_op jit(solution)/shard_map/ppermute | solution.py:400
  41.5 7.1 %collective-permute-start.8 = (bf16[2,80,512]{2,1,0:T(8,128)(2,1)S(1)}, bf16[2,80,512]{2,1,0:T(8,128)(2,1)S(1)}, u32[]{:S(2)}, u32[]{:S(2)}) collective-permute-start(bf16[2,80,512]{2,1,0:T(8,128)(2,1)S(1)} %bitcast.73), channel_id=1, source_target_pairs={{0,16},{16,0},{1,17},{17,1},{2,18},{18,2},{3,19},{19,3},{4,20},{20... | collective-permute-start | bytes 491528 | tf_op jit(solution)/shard_map/ppermute | solution.py:522
  43.1 6.1 %collective-permute-start.10 = (bf16[272,128]{1,0:T(8,128)(2,1)}, bf16[272,128]{1,0:T(8,128)(2,1)S(1)}, u32[]{:S(2)}, u32[]{:S(2)}) collective-permute-start(bf16[272,128]{1,0:T(8,128)(2,1)} %get-tuple-element.76), channel_id=1, source_target_pairs={{4,8},{8,4},{6,10},{10,6},{5,9},{9,5},{7,11},{11,7},{20,24},{24,20... | collective-permute-start | bytes 208904 | tf_op jit(solution)/shard_map/ppermute | solution.py:458
  43.7 5.4 %collective-permute-start.9 = (bf16[528,128]{1,0:T(8,128)(2,1)S(1)}, bf16[528,128]{1,0:T(8,128)(2,1)S(1)}, u32[]{:S(2)}, u32[]{:S(2)}) collective-permute-start(bf16[528,128]{1,0:T(8,128)(2,1)S(1)} %copy-done.1), channel_id=1, source_target_pairs={{2,4},{4,2},{6,8},{8,6},{10,12},{12,10},{3,5},{5,3},{7,9},{9,7},{1... | collective-permute-start | bytes 405512 | tf_op jit(solution)/shard_map/ppermute | solution.py:458
  48.9 9.1 %copy-start = (s32[3]{0:T(128)S(1)}, s32[3]{0:T(128)}, u32[]{:S(2)}) copy-start(s32[3]{0:T(128)} %pad_add_fusion.scalar_ref) | copy-start | bytes 40
  49.2 8.8 %collective-permute-start.12 = (bf16[8,176,512]{2,1,0:T(8,128)(2,1)S(1)}, bf16[8,176,512]{2,1,0:T(8,128)(2,1)S(1)}, u32[]{:S(2)}, u32[]{:S(2)}) collective-permute-start(bf16[8,176,512]{2,1,0:T(8,128)(2,1)S(1)} %maximum_select_fusion.here_ref), channel_id=1, source_target_pairs={{0,1},{1,0},{2,3},{3,2},{4,5},{5,4},{6,7},{7,6},{8,9},{9,8},{10,11... | collective-permute-start | bytes 4325384 | tf_op jit(solution)/shard_map/ppermute | solution.py:400
  49.3 17.2 %collective-permute-start.11 = (bf16[4,160,512]{2,1,0:T(8,128)(2,1)S(1)}, bf16[4,160,512]{2,1,0:T(8,128)(2,1)S(1)}, u32[]{:S(2)}, u32[]{:S(2)}) collective-permute-start(bf16[4,160,512]{2,1,0:T(8,128)(2,1)S(1)} %maximum_select_fusion.3), channel_id=1, source_target_pairs={{0,4},{1,3},{2,6},{3,1},{4,0},{5,7},{6,2},{7,5},{8,12},{9,11},{10,... | collective-permute-start | bytes 1966088 | tf_op jit(solution)/shard_map/ppermute | solution.py:400
  66.8 3.1 %collective-permute-start.13 = (bf16[8,160,512]{2,1,0:T(8,128)(2,1)S(1)}, bf16[8,160,512]{2,1,0:T(8,128)(2,1)S(1)}, u32[]{:S(2)}, u32[]{:S(2)}) collective-permute-start(bf16[8,160,512]{2,1,0:T(8,128)(2,1)S(1)} %maximum_select_fusion.1.here_ref), channel_id=1, source_target_pairs={{0,1},{1,0},{2,3},{3,2},{4,5},{5,4},{6,7},{7,6},{8,9},{9,8},{10,11... | collective-permute-start | bytes 3932168 | tf_op jit(solution)/shard_map/ppermute | solution.py:400
  80.9 3.6 %collective-permute-start.14 = (bf16[8,168,512]{2,1,0:T(8,128)(2,1)S(1)}, bf16[8,168,512]{2,1,0:T(8,128)(2,1)S(1)}, u32[]{:S(2)}, u32[]{:S(2)}) collective-permute-start(bf16[8,168,512]{2,1,0:T(8,128)(2,1)S(1)} %get-tuple-element.92), channel_id=1, source_target_pairs={{0,1},{1,0},{2,3},{3,2},{4,5},{5,4},{6,7},{7,6},{8,9},{9,8},{10,11... | collective-permute-start | bytes 4128776 | tf_op jit(solution)/shard_map/ppermute | solution.py:400
  84.5 3.2 %collective-permute-start.15 = (bf16[8,168,512]{2,1,0:T(8,128)(2,1)S(1)}, bf16[8,168,512]{2,1,0:T(8,128)(2,1)S(1)}, u32[]{:S(2)}, u32[]{:S(2)}) collective-permute-start(bf16[8,168,512]{2,1,0:T(8,128)(2,1)S(1)} %get-tuple-element.102), channel_id=1, source_target_pairs={{0,1},{1,0},{2,3},{3,2},{4,5},{5,4},{6,7},{7,6},{8,9},{9,8},{10,11... | collective-permute-start | bytes 4128776 | tf_op jit(solution)/shard_map/ppermute | solution.py:400
  85.6 11.0 %collective-permute-start.16 = (bf16[1,2,2,168,512]{4,3,2,1,0:T(8,128)(2,1)S(1)}, bf16[1,2,2,168,512]{4,3,2,1,0:T(8,128)(2,1)S(1)}, u32[]{:S(2)}, u32[]{:S(2)}) collective-permute-start(bf16[1,2,2,168,512]{4,3,2,1,0:T(8,128)(2,1)S(1)} %bitcast.62), channel_id=1, source_target_pairs={{0,2},{1,5},{2,0},{3,7},{4,6},{5,1},{6,4},{7,3},{8,10},{9,13},{10,... | collective-permute-start | bytes 2064392 | tf_op jit(solution)/shard_map/ppermute | solution.py:400
  97.3 14.7 %collective-permute-start.17 = (bf16[1,2,2,168,512]{4,3,2,1,0:T(8,128)(2,1)S(1)}, bf16[1,2,2,168,512]{4,3,2,1,0:T(8,128)(2,1)S(1)}, u32[]{:S(2)}, u32[]{:S(2)}) collective-permute-start(bf16[1,2,2,168,512]{4,3,2,1,0:T(8,128)(2,1)S(1)} %bitcast.61), channel_id=1, source_target_pairs={{0,2},{1,5},{2,0},{3,7},{4,6},{5,1},{6,4},{7,3},{8,10},{9,13},{10,... | collective-permute-start | bytes 2064392 | tf_op jit(solution)/shard_map/ppermute | solution.py:400
  97.9 11.0 %collective-permute-start.18 = (bf16[1,1,2,168,512]{4,3,2,1,0:T(8,128)(2,1)S(1)}, bf16[1,1,2,168,512]{4,3,2,1,0:T(8,128)(2,1)S(1)}, u32[]{:S(2)}, u32[]{:S(2)}) collective-permute-start(bf16[1,1,2,168,512]{4,3,2,1,0:T(8,128)(2,1)S(1)} %bitcast.65), channel_id=1, source_target_pairs={{0,4},{1,3},{2,6},{3,1},{4,0},{5,7},{6,2},{7,5},{8,12},{9,11},{10,... | collective-permute-start | bytes 1032200 | tf_op jit(solution)/shard_map/ppermute | solution.py:400
  112.6 10.0 %collective-permute-start.19 = (bf16[1,1,2,168,512]{4,3,2,1,0:T(8,128)(2,1)S(1)}, bf16[1,1,2,168,512]{4,3,2,1,0:T(8,128)(2,1)S(1)}, u32[]{:S(2)}, u32[]{:S(2)}) collective-permute-start(bf16[1,1,2,168,512]{4,3,2,1,0:T(8,128)(2,1)S(1)} %bitcast.66), channel_id=1, source_target_pairs={{0,4},{1,3},{2,6},{3,1},{4,0},{5,7},{6,2},{7,5},{8,12},{9,11},{10,... | collective-permute-start | bytes 1032200 | tf_op jit(solution)/shard_map/ppermute | solution.py:400
  113.1 11.4 %collective-permute-start.21 = (bf16[1,1,1,168,512]{4,3,2,1,0:T(8,128)(2,1)S(1)}, bf16[1,1,1,168,512]{4,3,2,1,0:T(8,128)(2,1)S(1)}, u32[]{:S(2)}, u32[]{:S(2)}) collective-permute-start(bf16[1,1,1,168,512]{4,3,2,1,0:T(8,128)(2,1)S(1)} %bitcast.67), channel_id=1, source_target_pairs={{0,8},{1,9},{2,10},{3,11},{4,12},{5,13},{6,14},{7,15},{8,0},{9,1},... | collective-permute-start | bytes 516104 | tf_op jit(solution)/shard_map/ppermute | solution.py:400
  123.2 7.2 %collective-permute-start.20 = (bf16[1,1,1,168,512]{4,3,2,1,0:T(8,128)(2,1)S(1)}, bf16[1,1,1,168,512]{4,3,2,1,0:T(8,128)(2,1)S(1)}, u32[]{:S(2)}, u32[]{:S(2)}) collective-permute-start(bf16[1,1,1,168,512]{4,3,2,1,0:T(8,128)(2,1)S(1)} %bitcast.70), channel_id=1, source_target_pairs={{0,8},{1,9},{2,10},{3,11},{4,12},{5,13},{6,14},{7,15},{8,0},{9,1},... | collective-permute-start | bytes 516104 | tf_op jit(solution)/shard_map/ppermute | solution.py:400

commit v14 on v12

--- a/solution.py
+++ b/solution.py
@@ -278,7 +278,7 @@
     lanes = label_ref.shape[1]
     class_row = lax.broadcasted_iota(jnp.int32, (classes, lanes), 0).astype(F32)
     unit = class_row == lax.broadcasted_iota(jnp.int32, (lanes, lanes), 1).astype(F32)
-    cuts = [0, steps, 2 * steps, rows]
+    cuts = [0, steps, rows]
     left = scalar_ref[2] - scalar_ref[1] * steps
 
     for start, end in zip(cuts, cuts[1:]):

time: 128 us -> 127 us (level)
  no operation moved by 1% of the time
where the time goes in v14:
time: 127 us
  waiting for transfers between devices  56 us (44%)
  Pallas kernels  34.1 us (27%)
  starting transfers between devices  30.2 us (24%)
  other arithmetic  4.56 us (4%)
  between operations  1.59 us (1%)
    ppermute x19, waiting for transfers between devices, swap(): return lax.ppermute(value, ('tm', 'site'), pairs)  56 us
    pallas_call x18, Pallas kernels, call(): pl.pallas_call(kernel, out_shape=[jax.ShapeDtypeStruct(s, d) for s, d in...  34.1 us
    ppermute x19, starting transfers between devices, swap(): return lax.ppermute(value, ('tm', 'site'), pairs)  28.7 us
    select_n x9, other arithmetic, arranged(): jnp.where(my_bit(links) == 0, jnp.concatenate([held, other]), jnp.concate...  3.12 us
  transfers between devices with their start and end apart: 21, of which 14 were waited for; matrix products, arithmetic and copies ran while one was open for 3% of the time, Pallas kernels for 15%

profile of v14, /device:TPU:0, one launch (start us, length us, event | category | flops | bytes accessed | tf_op | source)
XLA Modules:
  0.0 127.2 jit_solution(15632982574706961368)
XLA Ops:
  0.6 2.7 %shard_map.119 = (f32[512,128]{1,0:T(8,128)}, f32[512,128]{1,0:T(8,128)}, f32[512,128]{1,0:T(8,128)}, f32[3,128]{1,0:T(4,128)}, bf16[176,512]{1,0:T(8,128)(2,1)}, /*index=5*/bf16[160,512]{1,0:T(8,128)(2,1)}) custom-call(f32[512,128]{1,0:T(8,128)} %bitcast.75, f32[512,128]{1,0:T(8,128)} %bitcast.84, bf16[2,64,1024]{2,1,0:T(8,128)(2,1)} %conv_ref.1, ...), custom_call_target="tpu_custom_call" | custom-call | flops 2000000000 | bytes 2000384 | tf_op jit(solution)/shard_map/pallas_call | solution.py:38
  3.3 3.0 %collective-permute-start.1 = (f32[1,3,128]{2,1,0:T(4,128)}, f32[1,3,128]{2,1,0:T(4,128)S(1)}, u32[]{:S(2)}, u32[]{:S(2)}) collective-permute-start(f32[1,3,128]{2,1,0:T(4,128)} %bitcast.82), channel_id=1, source_target_pairs={{0,2},{1,3},{2,0},{3,1},{4,6},{5,7},{6,4},{7,5},{8,10},{9,11},{10,... | collective-permute-start | bytes 4616 | tf_op jit(solution)/shard_map/ppermute | solution.py:400
  6.4 2.6 %collective-permute-start = (bf16[1,176,512]{2,1,0:T(8,128)(2,1)}, bf16[1,176,512]{2,1,0:T(8,128)(2,1)S(1)}, u32[]{:S(2)}, u32[]{:S(2)}) collective-permute-start(bf16[1,176,512]{2,1,0:T(8,128)(2,1)} %bitcast.77), channel_id=1, source_target_pairs={{0,8},{1,9},{2,10},{3,11},{4,12},{5,13},{6,14},{7,15},{8,0},{9,1},... | collective-permute-start | bytes 540680 | tf_op jit(solution)/shard_map/ppermute | solution.py:400
  9.0 0.8 maximum_select_fusion.8
  9.7 1.6 %collective-permute-start.2 = (f32[2,3,128]{2,1,0:T(4,128)S(1)}, f32[2,3,128]{2,1,0:T(4,128)S(1)}, u32[]{:S(2)}, u32[]{:S(2)}) collective-permute-start(f32[2,3,128]{2,1,0:T(4,128)S(1)} %maximum_select_fusion.8), channel_id=1, source_target_pairs={{0,4},{1,5},{2,6},{3,7},{4,0},{5,1},{6,2},{7,3},{8,12},{9,13},{10,... | collective-permute-start | bytes 9224 | tf_op jit(solution)/shard_map/ppermute | solution.py:400
  11.3 2.0 %collective-permute-done.2 = f32[2,3,128]{2,1,0:T(4,128)S(1)} collective-permute-done((f32[2,3,128]{2,1,0:T(4,128)S(1)}, f32[2,3,128]{2,1,0:T(4,128)S(1)}, u32[]{:S(2)}, u32[]{:S(2)}) %collective-permute-start.2) | collective-permute-done | bytes 3104 | tf_op jit(solution)/shard_map/ppermute | solution.py:400
  13.3 4.0 %collective-permute-done = bf16[1,176,512]{2,1,0:T(8,128)(2,1)S(1)} collective-permute-done((bf16[1,176,512]{2,1,0:T(8,128)(2,1)}, bf16[1,176,512]{2,1,0:T(8,128)(2,1)S(1)}, u32[]{:S(2)}, u32[]{:S(2)}) %collective-permute-start) | collective-permute-done | bytes 180256 | tf_op jit(solution)/shard_map/ppermute | solution.py:400
  17.4 1.1 maximum_select_fusion.4
  18.4 0.5 collective-permute-start.3
  19.6 0.1 collective-permute-start.4
  19.7 2.9 %collective-permute-start.5 = (bf16[1,160,512]{2,1,0:T(8,128)(2,1)}, bf16[1,160,512]{2,1,0:T(8,128)(2,1)S(1)}, u32[]{:S(2)}, u32[]{:S(2)}) collective-permute-start(bf16[1,160,512]{2,1,0:T(8,128)(2,1)} %bitcast.79), channel_id=1, source_target_pairs={{0,8},{1,9},{2,10},{3,11},{4,12},{5,13},{6,14},{7,15},{8,0},{9,1},... | collective-permute-start | bytes 491528 | tf_op jit(solution)/shard_map/ppermute | solution.py:400
  22.6 0.6 pad_add_fusion.scalar_ref
  23.2 1.0 collective-permute-done.4
  24.2 0.6 maximum_select_fusion.6.carry_ref
  24.8 2.2 %shard_map.120 = (bf16[528,128]{1,0:T(8,128)(2,1)}, bf16[136,512]{1,0:T(8,128)(2,1)}, bf16[272,128]{1,0:T(8,128)(2,1)}) custom-call(s32[3]{0:T(128)} %pad_add_fusion.scalar_ref, f32[512,128]{1,0:T(8,128)} %bitcast.76, f32[512,128]{1,0:T(8,128)} %get-tuple-element.64.keep_ref, f32[512,128]{1,0:T(8,128)} %get-tuple-element.65.mass_ref, ...), custom_call_target="tpu_custom_call" | custom-call | flops 100000000 | bytes 1406988 | tf_op jit(solution)/shard_map/pallas_call | solution.py:38
  27.0 0.1 collective-permute-done.5
  27.1 0.1 maximum_select_fusion.2
  27.3 0.6 copy-done.2
  27.9 0.1 pad_maximum_fusion
  28.0 3.4 %collective-permute-start.6 = (bf16[840,512]{1,0:T(8,128)(2,1)S(1)}, bf16[840,512]{1,0:T(8,128)(2,1)S(1)}, u32[]{:S(2)}, u32[]{:S(2)}) collective-permute-start(bf16[840,512]{1,0:T(8,128)(2,1)S(1)} %pad_maximum_fusion), channel_id=1, source_target_pairs={{0,4},{1,3},{2,6},{3,1},{4,0},{5,7},{6,2},{7,5},{8,12},{9,11},{10,... | collective-permute-start | bytes 2580488 | tf_op jit(solution)/shard_map/ppermute | solution.py:400
  31.4 0.8 pad_maximum_fusion.1
  32.2 1.3 %collective-permute-start.7 = (bf16[456,512]{1,0:T(8,128)(2,1)}, bf16[456,512]{1,0:T(8,128)(2,1)S(1)}, u32[]{:S(2)}, u32[]{:S(2)}) collective-permute-start(bf16[456,512]{1,0:T(8,128)(2,1)} %pad_maximum_fusion.1), channel_id=1, source_target_pairs={{0,2},{1,5},{2,0},{3,7},{4,6},{5,1},{6,4},{7,3},{8,10},{9,13},{10,... | collective-permute-start | bytes 1400840 | tf_op jit(solution)/shard_map/ppermute | solution.py:400
  33.5 0.7 collective-permute-start.9
  34.2 0.8 collective-permute-start.8
  35.0 11.0 %collective-permute-done.7 = bf16[456,512]{1,0:T(8,128)(2,1)S(1)} collective-permute-done((bf16[456,512]{1,0:T(8,128)(2,1)}, bf16[456,512]{1,0:T(8,128)(2,1)S(1)}, u32[]{:S(2)}, u32[]{:S(2)}) %collective-permute-start.7) | collective-permute-done | bytes 466976 | tf_op jit(solution)/shard_map/ppermute | solution.py:400
  46.1 0.1 maximum_select_fusion.3
  46.2 1.4 %collective-permute-done.6 = bf16[840,512]{1,0:T(8,128)(2,1)S(1)} collective-permute-done((bf16[840,512]{1,0:T(8,128)(2,1)S(1)}, bf16[840,512]{1,0:T(8,128)(2,1)S(1)}, u32[]{:S(2)}, u32[]{:S(2)}) %collective-permute-start.6) | collective-permute-done | bytes 860192 | tf_op jit(solution)/shard_map/ppermute | solution.py:400
  47.6 0.0 copy-start
  47.6 0.2 maximum_select_fusion.here_ref
  47.9 3.2 %collective-permute-start.11 = (bf16[8,176,512]{2,1,0:T(8,128)(2,1)S(1)}, bf16[8,176,512]{2,1,0:T(8,128)(2,1)S(1)}, u32[]{:S(2)}, u32[]{:S(2)}) collective-permute-start(bf16[8,176,512]{2,1,0:T(8,128)(2,1)S(1)} %maximum_select_fusion.here_ref), channel_id=1, source_target_pairs={{0,1},{1,0},{2,3},{3,2},{4,5},{5,4},{6,7},{7,6},{8,9},{9,8},{10,11... | collective-permute-start | bytes 4325384 | tf_op jit(solution)/shard_map/ppermute | solution.py:400
  51.1 1.7 %collective-permute-start.10 = (bf16[4,160,512]{2,1,0:T(8,128)(2,1)S(1)}, bf16[4,160,512]{2,1,0:T(8,128)(2,1)S(1)}, u32[]{:S(2)}, u32[]{:S(2)}) collective-permute-start(bf16[4,160,512]{2,1,0:T(8,128)(2,1)S(1)} %maximum_select_fusion.3), channel_id=1, source_target_pairs={{0,4},{1,3},{2,6},{3,1},{4,0},{5,7},{6,2},{7,5},{8,12},{9,11},{10,... | collective-permute-start | bytes 1966088 | tf_op jit(solution)/shard_map/ppermute | solution.py:400
  52.8 1.1 collective-permute-done.11.there_ref
  53.9 6.6 %shard_map.121 = (bf16[1792,512]{1,0:T(8,128)(2,1)S(1)}, bf16[512,128]{1,0:T(8,128)(2,1)S(1)}, f32[10,128]{1,0:T(8,128)S(1)}, bf16[768,512]{1,0:T(8,128)(2,1)S(1...) custom-call(s32[3]{0:T(128)S(1)} %copy-done, ...), custom_call_target="tpu_custom_call" | custom-call | flops 5637144576 | bytes 10978316 | tf_op jit(solution)/shard_map/pallas_call | solution.py:38
  60.5 1.1 collective-permute-done.10
  61.7 0.2 maximum_select_fusion.1.here_ref
  61.9 0.1 collective-permute-start.12
  61.9 3.0 %collective-permute-done.12.there_ref = bf16[8,160,512]{2,1,0:T(8,128)(2,1)S(1)} collective-permute-done((bf16[8,160,512]{2,1,0:T(8,128)(2,1)S(1)}, bf16[8,160,512]{2,1,0:T(8,128)(2,1)S(1)}, u32[]{:S(2)}, u32[]{:S(2)}) %collective-permute-start.12) | collective-permute-done | bytes 1310752 | tf_op jit(solution)/shard_map/ppermute | solution.py:400
  65.0 10.7 %shard_map.122 = (f32[4,128]{1,0:T(4,128)}, bf16[8,168,512]{2,1,0:T(8,128)(2,1)S(1)}, bf16[8,168,512]{2,1,0:T(8,128)(2,1)S(1)}, f32[512,512]{1,0:T(8,128)S(1)}, ...) custom-call(s32[3]{0:T(128)S(1)} %copy-done, bf16[1792,512]{1,0:T(8,128)(2,1)S(1)} %get-tuple-element.84.h1_ref, ...), custom_call_target="tpu_custom_call" | custom-call | flops 7381975040 | bytes 12590092 | tf_op jit(solution)/shard_map/pallas_call | solution.py:38
  75.7 0.2 collective-permute-start.13
  75.9 3.3 %shard_map.123 = (bf16[8,168,512]{2,1,0:T(8,128)(2,1)S(1)}, bf16[8,168,512]{2,1,0:T(8,128)(2,1)S(1)}) custom-call(s32[3]{0:T(128)S(1)} %copy-done, bf16[768,1024]{1,0:T(8,128)(2,1)S(1)} %get-tuple-element.93.back_ref, f32[512,512]{1,0:T(8,128)S(1)} %get-tuple-element.94.grad_ref, bf16[512,512]{1,0:T(8,128)(2,1)S(1)} %get-tuple-element.95.round_ref, ...), custom_call_target="tpu_custom_call" | custom-call | flops 2415919104 | bytes 9441292 | tf_op jit(solution)/shard_map/pallas_call | solution.py:38
  79.3 0.4 collective-permute-start.14
  79.7 0.7 shard_map.126
  80.4 2.2 %collective-permute-start.15 = (bf16[1,2,2,168,512]{4,3,2,1,0:T(8,128)(2,1)S(1)}, bf16[1,2,2,168,512]{4,3,2,1,0:T(8,128)(2,1)S(1)}, u32[]{:S(2)}, u32[]{:S(2)}) collective-permute-start(bf16[1,2,2,168,512]{4,3,2,1,0:T(8,128)(2,1)S(1)} %bitcast.62), channel_id=1, source_target_pairs={{0,2},{1,5},{2,0},{3,7},{4,6},{5,1},{6,4},{7,3},{8,10},{9,13},{10,... | collective-permute-start | bytes 2064392 | tf_op jit(solution)/shard_map/ppermute | solution.py:400
  82.7 0.7 shard_map.125
  83.4 0.7 shard_map.127
  84.1 7.5 %collective-permute-done.15 = bf16[1,2,2,168,512]{4,3,2,1,0:T(8,128)(2,1)S(1)} collective-permute-done((bf16[1,2,2,168,512]{4,3,2,1,0:T(8,128)(2,1)S(1)}, bf16[1,2,2,168,512]{4,3,2,1,0:T(8,128)(2,1)S(1)}, u32[]{:S(2)}, u32[]{:S(2)}) %collective-permute-start.15) | collective-permute-done | bytes 688160 | tf_op jit(solution)/shard_map/ppermute | solution.py:400
  91.6 0.6 shard_map.128
  92.2 2.1 %collective-permute-start.16 = (bf16[1,2,2,168,512]{4,3,2,1,0:T(8,128)(2,1)S(1)}, bf16[1,2,2,168,512]{4,3,2,1,0:T(8,128)(2,1)S(1)}, u32[]{:S(2)}, u32[]{:S(2)}) collective-permute-start(bf16[1,2,2,168,512]{4,3,2,1,0:T(8,128)(2,1)S(1)} %bitcast.61), channel_id=1, source_target_pairs={{0,2},{1,5},{2,0},{3,7},{4,6},{5,1},{6,4},{7,3},{8,10},{9,13},{10,... | collective-permute-start | bytes 2064392 | tf_op jit(solution)/shard_map/ppermute | solution.py:400
  94.3 0.7 shard_map.124
  95.0 0.6 shard_map.130
  95.7 9.4 %collective-permute-done.17 = bf16[1,1,2,168,512]{4,3,2,1,0:T(8,128)(2,1)S(1)} collective-permute-done((bf16[1,1,2,168,512]{4,3,2,1,0:T(8,128)(2,1)S(1)}, bf16[1,1,2,168,512]{4,3,2,1,0:T(8,128)(2,1)S(1)}, u32[]{:S(2)}, u32[]{:S(2)}) %collective-permute-start.17) | collective-permute-done | bytes 344096 | tf_op jit(solution)/shard_map/ppermute | solution.py:400
  105.1 0.6 shard_map.131
  105.7 0.8 collective-permute-done.16
  106.5 0.6 shard_map.132
  107.1 0.8 collective-permute-start.18
  107.9 2.1 %collective-permute-start.20 = (bf16[1,1,1,168,512]{4,3,2,1,0:T(8,128)(2,1)S(1)}, bf16[1,1,1,168,512]{4,3,2,1,0:T(8,128)(2,1)S(1)}, u32[]{:S(2)}, u32[]{:S(2)}) collective-permute-start(bf16[1,1,1,168,512]{4,3,2,1,0:T(8,128)(2,1)S(1)} %bitcast.67), channel_id=1, source_target_pairs={{0,8},{1,9},{2,10},{3,11},{4,12},{5,13},{6,14},{7,15},{8,0},{9,1},... | collective-permute-start | bytes 516104 | tf_op jit(solution)/shard_map/ppermute | solution.py:400
  110.1 0.6 shard_map.129
  110.7 7.5 %collective-permute-done.18 = bf16[1,1,2,168,512]{4,3,2,1,0:T(8,128)(2,1)S(1)} collective-permute-done((bf16[1,1,2,168,512]{4,3,2,1,0:T(8,128)(2,1)S(1)}, bf16[1,1,2,168,512]{4,3,2,1,0:T(8,128)(2,1)S(1)}, u32[]{:S(2)}, u32[]{:S(2)}) %collective-permute-start.18) | collective-permute-done | bytes 344096 | tf_op jit(solution)/shard_map/ppermute | solution.py:400
  118.2 0.6 shard_map.134
  118.8 0.5 collective-permute-start.19
  119.2 0.6 shard_map.135
  119.8 0.6 shard_map.133
  120.4 5.9 %collective-permute-done.19 = bf16[1,1,1,168,512]{4,3,2,1,0:T(8,128)(2,1)S(1)} collective-permute-done((bf16[1,1,1,168,512]{4,3,2,1,0:T(8,128)(2,1)S(1)}, bf16[1,1,1,168,512]{4,3,2,1,0:T(8,128)(2,1)S(1)}, u32[]{:S(2)}, u32[]{:S(2)}) %collective-permute-start.19) | collective-permute-done | bytes 172064 | tf_op jit(solution)/shard_map/ppermute | solution.py:400
  126.4 0.9 shard_map.136
  (22 shorter events, 0.2 us)
Async XLA Ops:
  3.3 23.7 %copy-start.3 = (bf16[160,512]{1,0:T(8,128)(2,1)S(1)}, bf16[160,512]{1,0:T(8,128)(2,1)}, u32[]{:S(2)}) copy-start(bf16[160,512]{1,0:T(8,128)(2,1)} %get-tuple-element.62) | copy-start | bytes 491524
  3.3 5.6 %collective-permute-start.1 = (f32[1,3,128]{2,1,0:T(4,128)}, f32[1,3,128]{2,1,0:T(4,128)S(1)}, u32[]{:S(2)}, u32[]{:S(2)}) collective-permute-start(f32[1,3,128]{2,1,0:T(4,128)} %bitcast.82), channel_id=1, source_target_pairs={{0,2},{1,3},{2,0},{3,1},{4,6},{5,7},{6,4},{7,5},{8,10},{9,11},{10,... | collective-permute-start | bytes 4616 | tf_op jit(solution)/shard_map/ppermute | solution.py:400
  6.4 11.0 %collective-permute-start = (bf16[1,176,512]{2,1,0:T(8,128)(2,1)}, bf16[1,176,512]{2,1,0:T(8,128)(2,1)S(1)}, u32[]{:S(2)}, u32[]{:S(2)}) collective-permute-start(bf16[1,176,512]{2,1,0:T(8,128)(2,1)} %bitcast.77), channel_id=1, source_target_pairs={{0,8},{1,9},{2,10},{3,11},{4,12},{5,13},{6,14},{7,15},{8,0},{9,1},... | collective-permute-start | bytes 540680 | tf_op jit(solution)/shard_map/ppermute | solution.py:400
  9.7 3.6 %collective-permute-start.2 = (f32[2,3,128]{2,1,0:T(4,128)S(1)}, f32[2,3,128]{2,1,0:T(4,128)S(1)}, u32[]{:S(2)}, u32[]{:S(2)}) collective-permute-start(f32[2,3,128]{2,1,0:T(4,128)S(1)} %maximum_select_fusion.8), channel_id=1, source_target_pairs={{0,4},{1,5},{2,6},{3,7},{4,0},{5,1},{6,2},{7,3},{8,12},{9,13},{10,... | collective-permute-start | bytes 9224 | tf_op jit(solution)/shard_map/ppermute | solution.py:400
  18.4 8.7 %collective-permute-start.3 = (bf16[2,176,512]{2,1,0:T(8,128)(2,1)S(1)}, bf16[2,176,512]{2,1,0:T(8,128)(2,1)S(1)}, u32[]{:S(2)}, u32[]{:S(2)}) collective-permute-start(bf16[2,176,512]{2,1,0:T(8,128)(2,1)S(1)} %maximum_select_fusion.4), channel_id=1, source_target_pairs={{0,2},{1,5},{2,0},{3,7},{4,6},{5,1},{6,4},{7,3},{8,10},{9,13},{10,... | collective-permute-start | bytes 1081352 | tf_op jit(solution)/shard_map/ppermute | solution.py:400
  19.6 4.6 %collective-permute-start.4 = (f32[4,3,128]{2,1,0:T(4,128)S(1)}, f32[4,3,128]{2,1,0:T(4,128)S(1)}, u32[]{:S(2)}, u32[]{:S(2)}) collective-permute-start(f32[4,3,128]{2,1,0:T(4,128)S(1)} %maximum_select_fusion.7), channel_id=1, source_target_pairs={{0,8},{1,9},{2,10},{3,11},{4,12},{5,13},{6,14},{7,15},{8,0},{9,1},... | collective-permute-start | bytes 18440 | tf_op jit(solution)/shard_map/ppermute | solution.py:400
  19.7 7.4 %collective-permute-start.5 = (bf16[1,160,512]{2,1,0:T(8,128)(2,1)}, bf16[1,160,512]{2,1,0:T(8,128)(2,1)S(1)}, u32[]{:S(2)}, u32[]{:S(2)}) collective-permute-start(bf16[1,160,512]{2,1,0:T(8,128)(2,1)} %bitcast.79), channel_id=1, source_target_pairs={{0,8},{1,9},{2,10},{3,11},{4,12},{5,13},{6,14},{7,15},{8,0},{9,1},... | collective-permute-start | bytes 491528 | tf_op jit(solution)/shard_map/ppermute | solution.py:400
  27.0 0.9 copy-start.2
  27.3 6.2 %copy-start.4 = (bf16[272,128]{1,0:T(8,128)(2,1)S(1)}, bf16[272,128]{1,0:T(8,128)(2,1)}, u32[]{:S(2)}) copy-start(bf16[272,128]{1,0:T(8,128)(2,1)} %get-tuple-element.76) | copy-start | bytes 208900
  27.3 6.9 %copy-start.1 = (bf16[528,128]{1,0:T(8,128)(2,1)S(1)}, bf16[528,128]{1,0:T(8,128)(2,1)}, u32[]{:S(2)}) copy-start(bf16[528,128]{1,0:T(8,128)(2,1)} %get-tuple-element.75.own_ref.norm_ref) | copy-start | bytes 405508
  28.0 19.6 %collective-permute-start.6 = (bf16[840,512]{1,0:T(8,128)(2,1)S(1)}, bf16[840,512]{1,0:T(8,128)(2,1)S(1)}, u32[]{:S(2)}, u32[]{:S(2)}) collective-permute-start(bf16[840,512]{1,0:T(8,128)(2,1)S(1)} %pad_maximum_fusion), channel_id=1, source_target_pairs={{0,4},{1,3},{2,6},{3,1},{4,0},{5,7},{6,2},{7,5},{8,12},{9,11},{10,... | collective-permute-start | bytes 2580488 | tf_op jit(solution)/shard_map/ppermute | solution.py:400
  32.2 13.8 %collective-permute-start.7 = (bf16[456,512]{1,0:T(8,128)(2,1)}, bf16[456,512]{1,0:T(8,128)(2,1)S(1)}, u32[]{:S(2)}, u32[]{:S(2)}) collective-permute-start(bf16[456,512]{1,0:T(8,128)(2,1)} %pad_maximum_fusion.1), channel_id=1, source_target_pairs={{0,2},{1,5},{2,0},{3,7},{4,6},{5,1},{6,4},{7,3},{8,10},{9,13},{10,... | collective-permute-start | bytes 1400840 | tf_op jit(solution)/shard_map/ppermute | solution.py:400
  33.5 14.4 %collective-permute-start.9 = (bf16[272,128]{1,0:T(8,128)(2,1)S(1)}, bf16[272,128]{1,0:T(8,128)(2,1)S(1)}, u32[]{:S(2)}, u32[]{:S(2)}) collective-permute-start(bf16[272,128]{1,0:T(8,128)(2,1)S(1)} %copy-done.4), channel_id=1, source_target_pairs={{4,8},{8,4},{6,10},{10,6},{5,9},{9,5},{7,11},{11,7},{20,24},{24,20... | collective-permute-start | bytes 208904 | tf_op jit(solution)/shard_map/ppermute | solution.py:458
  34.2 13.7 %collective-permute-start.8 = (bf16[528,128]{1,0:T(8,128)(2,1)S(1)}, bf16[528,128]{1,0:T(8,128)(2,1)S(1)}, u32[]{:S(2)}, u32[]{:S(2)}) collective-permute-start(bf16[528,128]{1,0:T(8,128)(2,1)S(1)} %copy-done.1), channel_id=1, source_target_pairs={{2,4},{4,2},{6,8},{8,6},{10,12},{12,10},{3,5},{5,3},{7,9},{9,7},{1... | collective-permute-start | bytes 405512 | tf_op jit(solution)/shard_map/ppermute | solution.py:458
  47.6 6.3 %copy-start = (s32[3]{0:T(128)S(1)}, s32[3]{0:T(128)}, u32[]{:S(2)}) copy-start(s32[3]{0:T(128)} %pad_add_fusion.scalar_ref) | copy-start | bytes 40
  47.9 6.0 %collective-permute-start.11 = (bf16[8,176,512]{2,1,0:T(8,128)(2,1)S(1)}, bf16[8,176,512]{2,1,0:T(8,128)(2,1)S(1)}, u32[]{:S(2)}, u32[]{:S(2)}) collective-permute-start(bf16[8,176,512]{2,1,0:T(8,128)(2,1)S(1)} %maximum_select_fusion.here_ref), channel_id=1, source_target_pairs={{0,1},{1,0},{2,3},{3,2},{4,5},{5,4},{6,7},{7,6},{8,9},{9,8},{10,11... | collective-permute-start | bytes 4325384 | tf_op jit(solution)/shard_map/ppermute | solution.py:400
  51.1 10.6 %collective-permute-start.10 = (bf16[4,160,512]{2,1,0:T(8,128)(2,1)S(1)}, bf16[4,160,512]{2,1,0:T(8,128)(2,1)S(1)}, u32[]{:S(2)}, u32[]{:S(2)}) collective-permute-start(bf16[4,160,512]{2,1,0:T(8,128)(2,1)S(1)} %maximum_select_fusion.3), channel_id=1, source_target_pairs={{0,4},{1,3},{2,6},{3,1},{4,0},{5,7},{6,2},{7,5},{8,12},{9,11},{10,... | collective-permute-start | bytes 1966088 | tf_op jit(solution)/shard_map/ppermute | solution.py:400
  61.9 3.1 %collective-permute-start.12 = (bf16[8,160,512]{2,1,0:T(8,128)(2,1)S(1)}, bf16[8,160,512]{2,1,0:T(8,128)(2,1)S(1)}, u32[]{:S(2)}, u32[]{:S(2)}) collective-permute-start(bf16[8,160,512]{2,1,0:T(8,128)(2,1)S(1)} %maximum_select_fusion.1.here_ref), channel_id=1, source_target_pairs={{0,1},{1,0},{2,3},{3,2},{4,5},{5,4},{6,7},{7,6},{8,9},{9,8},{10,11... | collective-permute-start | bytes 3932168 | tf_op jit(solution)/shard_map/ppermute | solution.py:400
  75.7 3.6 %collective-permute-start.13 = (bf16[8,168,512]{2,1,0:T(8,128)(2,1)S(1)}, bf16[8,168,512]{2,1,0:T(8,128)(2,1)S(1)}, u32[]{:S(2)}, u32[]{:S(2)}) collective-permute-start(bf16[8,168,512]{2,1,0:T(8,128)(2,1)S(1)} %get-tuple-element.92), channel_id=1, source_target_pairs={{0,1},{1,0},{2,3},{3,2},{4,5},{5,4},{6,7},{7,6},{8,9},{9,8},{10,11... | collective-permute-start | bytes 4128776 | tf_op jit(solution)/shard_map/ppermute | solution.py:400
  79.3 4.1 %collective-permute-start.14 = (bf16[8,168,512]{2,1,0:T(8,128)(2,1)S(1)}, bf16[8,168,512]{2,1,0:T(8,128)(2,1)S(1)}, u32[]{:S(2)}, u32[]{:S(2)}) collective-permute-start(bf16[8,168,512]{2,1,0:T(8,128)(2,1)S(1)} %get-tuple-element.102), channel_id=1, source_target_pairs={{0,1},{1,0},{2,3},{3,2},{4,5},{5,4},{6,7},{7,6},{8,9},{9,8},{10,11... | collective-permute-start | bytes 4128776 | tf_op jit(solution)/shard_map/ppermute | solution.py:400
  80.4 11.2 %collective-permute-start.15 = (bf16[1,2,2,168,512]{4,3,2,1,0:T(8,128)(2,1)S(1)}, bf16[1,2,2,168,512]{4,3,2,1,0:T(8,128)(2,1)S(1)}, u32[]{:S(2)}, u32[]{:S(2)}) collective-permute-start(bf16[1,2,2,168,512]{4,3,2,1,0:T(8,128)(2,1)S(1)} %bitcast.62), channel_id=1, source_target_pairs={{0,2},{1,5},{2,0},{3,7},{4,6},{5,1},{6,4},{7,3},{8,10},{9,13},{10,... | collective-permute-start | bytes 2064392 | tf_op jit(solution)/shard_map/ppermute | solution.py:400
  92.2 14.3 %collective-permute-start.16 = (bf16[1,2,2,168,512]{4,3,2,1,0:T(8,128)(2,1)S(1)}, bf16[1,2,2,168,512]{4,3,2,1,0:T(8,128)(2,1)S(1)}, u32[]{:S(2)}, u32[]{:S(2)}) collective-permute-start(bf16[1,2,2,168,512]{4,3,2,1,0:T(8,128)(2,1)S(1)} %bitcast.61), channel_id=1, source_target_pairs={{0,2},{1,5},{2,0},{3,7},{4,6},{5,1},{6,4},{7,3},{8,10},{9,13},{10,... | collective-permute-start | bytes 2064392 | tf_op jit(solution)/shard_map/ppermute | solution.py:400
  94.3 10.8 %collective-permute-start.17 = (bf16[1,1,2,168,512]{4,3,2,1,0:T(8,128)(2,1)S(1)}, bf16[1,1,2,168,512]{4,3,2,1,0:T(8,128)(2,1)S(1)}, u32[]{:S(2)}, u32[]{:S(2)}) collective-permute-start(bf16[1,1,2,168,512]{4,3,2,1,0:T(8,128)(2,1)S(1)} %bitcast.65), channel_id=1, source_target_pairs={{0,4},{1,3},{2,6},{3,1},{4,0},{5,7},{6,2},{7,5},{8,12},{9,11},{10,... | collective-permute-start | bytes 1032200 | tf_op jit(solution)/shard_map/ppermute | solution.py:400
  107.1 11.1 %collective-permute-start.18 = (bf16[1,1,2,168,512]{4,3,2,1,0:T(8,128)(2,1)S(1)}, bf16[1,1,2,168,512]{4,3,2,1,0:T(8,128)(2,1)S(1)}, u32[]{:S(2)}, u32[]{:S(2)}) collective-permute-start(bf16[1,1,2,168,512]{4,3,2,1,0:T(8,128)(2,1)S(1)} %bitcast.66), channel_id=1, source_target_pairs={{0,4},{1,3},{2,6},{3,1},{4,0},{5,7},{6,2},{7,5},{8,12},{9,11},{10,... | collective-permute-start | bytes 1032200 | tf_op jit(solution)/shard_map/ppermute | solution.py:400
  107.9 12.5 %collective-permute-start.20 = (bf16[1,1,1,168,512]{4,3,2,1,0:T(8,128)(2,1)S(1)}, bf16[1,1,1,168,512]{4,3,2,1,0:T(8,128)(2,1)S(1)}, u32[]{:S(2)}, u32[]{:S(2)}) collective-permute-start(bf16[1,1,1,168,512]{4,3,2,1,0:T(8,128)(2,1)S(1)} %bitcast.67), channel_id=1, source_target_pairs={{0,8},{1,9},{2,10},{3,11},{4,12},{5,13},{6,14},{7,15},{8,0},{9,1},... | collective-permute-start | bytes 516104 | tf_op jit(solution)/shard_map/ppermute | solution.py:400
  118.8 7.6 %collective-permute-start.19 = (bf16[1,1,1,168,512]{4,3,2,1,0:T(8,128)(2,1)S(1)}, bf16[1,1,1,168,512]{4,3,2,1,0:T(8,128)(2,1)S(1)}, u32[]{:S(2)}, u32[]{:S(2)}) collective-permute-start(bf16[1,1,1,168,512]{4,3,2,1,0:T(8,128)(2,1)S(1)} %bitcast.70), channel_id=1, source_target_pairs={{0,8},{1,9},{2,10},{3,11},{4,12},{5,13},{6,14},{7,15},{8,0},{9,1},... | collective-permute-start | bytes 516104 | tf_op jit(solution)/shard_map/ppermute | solution.py:400
